TPU v7x, 32 devices: a whole 2x2x4 slice. The times are simulated.
32 devices in a mesh: groups: 2 (over x), tensor: 16 (over z, y, core).
Axes of the slice: x: 2, y: 2, z: 4, core: 2. Of those that a mesh axis runs over, the one named last changes fastest.
Arguments:
- activations: bfloat16 [512, 8192], P(('groups', 'tensor')), parts along dimension 0, may hold values from -6 to 6
- dhidden: bfloat16 [512, 28672], P('groups', 'tensor'), parts along dimension 0, may hold values from -6 to 6
- frozen: bfloat16 [2, 8192, 28672], P(None, None, 'tensor'), may hold values from -0.0625 to 0.0625
- adapter_down_factors: bfloat16 [24, 8192, 128], P(None, 'tensor'), may hold values from -0.0625 to 0.0625
- adapter_up_factors: bfloat16 [24, 128, 28672], P(None, None, 'tensor'), may hold values from -0.75 to 0.75
- segment_adapter_index: int32 [2, 8], P('groups'), parts along dimension 0, may hold values from 0 to 23
- segment_row_counts: int32 [2, 8], P('groups'), parts along dimension 0, may hold values from 1 to 96, 256 in all within a row
- ranks: int32 [24], replicated, may hold values from 16 to 64, as said below
Outputs:
- dinput: bfloat16 [512, 8192], P(('groups', 'tensor')), parts along dimension 0
- grad_a: float32 [48, 8192, 128], P('groups', 'tensor'), parts along dimension 0
- grad_b: float32 [48, 128, 28672], P('groups', None, 'tensor'), parts along dimension 0
There are 2 independent parts, one for each index of `groups`. A program takes and returns all parts, laid end to end along the dimension named above; an argument that names none is the same for every part. Nothing has to cross between parts.
Inputs may be any that keep to these rules, and one draw needn't show every extreme that they name: `ranks`: at least one adapter has rank 64. `segment_row_counts`: each micro-batch's rows sum to 256; in each micro-batch one segment has exactly 96 rows.
All inputs are finite; a program needn't handle non-finite values.
Results may differ from a plain program's by a relative error of at most 0.0053.
Values may be sent and summed in bfloat16 or wider, within the bound.
No kernel may reach another device: no remote copies, remote signals or barrier semaphores. Data moves between devices by JAX's collectives and lax.ppermute only.
A program may use at most 256 MiB of HBM per device.

v0:
```python
import functools

import jax
import jax.numpy as jnp
from jax import lax
from jax.experimental import pallas as pl
from jax.experimental.pallas import tpu as pltpu
from jax.sharding import PartitionSpec as P

CHUNKS = 4
MIB = 1024 * 1024
BF16 = jnp.bfloat16
F32 = jnp.float32


def dot(left, right, dims=((1,), (0,))):
    return lax.dot_general(left, right, (dims, ((), ())), preferred_element_type=F32)


def params(mib):
    return pltpu.CompilerParams(vmem_limit_bytes=mib * MIB)


def cost(flops, moved):
    return pl.CostEstimate(flops=int(flops), bytes_accessed=int(moved), transcendentals=0)


def tile_of(size, most):
    return most if size % most == 0 else size


class Torus:
    def __init__(self, size):
        core = 2 if size % 2 == 0 else 1
        chips = size // core
        inner = 1
        while inner * 2 * inner * 2 <= chips and chips % (inner * 2) == 0:
            inner *= 2
        self.size = size
        self.dims = (chips // inner, inner, core)
        self.strides = (inner * core, core, 1)

    def place(self, index):
        return [index // s % n for s, n in zip(self.strides, self.dims)]

    def shifted(self, index, dim, by):
        at = index // self.strides[dim] % self.dims[dim]
        return index + ((at + by) % self.dims[dim] - at) * self.strides[dim]

    def move(self, x, dim, by):
        pairs = [(i, self.shifted(i, dim, by)) for i in range(self.size)]
        return lax.ppermute(x, "tensor", pairs)

    def gather(self, x, dim):
        return jnp.stack([x] + [self.move(x, dim, -k) for k in range(1, self.dims[dim])])

    def scatter_sum(self, x, dim):
        total = x[0].astype(F32)
        for k in range(1, self.dims[dim]):
            total = total + self.move(x[k], dim, k).astype(F32)
        return total

    def slot_devices(self, index):
        outer, inner, core = self.place(index)
        a, b, c = self.dims
        cs = lax.broadcasted_iota(jnp.int32, (c, b, a), 0)
        bs = lax.broadcasted_iota(jnp.int32, (c, b, a), 1)
        zs = lax.broadcasted_iota(jnp.int32, (c, b, a), 2)
        return (((outer + zs) % a * b + (inner + bs) % b) * c + (core + cs) % c).reshape(-1)

    def slots_of(self, index):
        outer, inner, core = self.place(index)
        a, b, c = self.dims
        zs = lax.broadcasted_iota(jnp.int32, (a, b, c), 0)
        bs = lax.broadcasted_iota(jnp.int32, (a, b, c), 1)
        cs = lax.broadcasted_iota(jnp.int32, (a, b, c), 2)
        return (((cs - core) % c * b + (bs - inner) % b) * a + (zs - outer) % a).reshape(-1)


def forward_kernel(has_start, tile, near, far, w, *rest):
    out = rest[-1]
    x = jnp.concatenate([near[...], far[...]], axis=0)
    first = pl.program_id(0) == 0
    for i in range(2):
        for n in range(0, out.shape[2], tile):
            at = (i, slice(None), slice(n, n + tile))
            part = dot(x, w[i, :, n : n + tile])
            if has_start:
                before = jnp.where(first, rest[0][at], out[at])
            else:
                before = jnp.where(first, 0.0, out[at])
            out[at] = before + part


def forward_chunk(near, far, frozen, start, q):
    half, step = near.shape
    hidden = frozen.shape[2]
    depth = tile_of(step, 512)
    base = q * (step // depth)
    whole = pl.BlockSpec((2, 2 * half, hidden), lambda k: (0, 0, 0))
    operands = [near, far, frozen]
    specs = [
        pl.BlockSpec((half, depth), lambda k: (0, k)),
        pl.BlockSpec((half, depth), lambda k: (0, k)),
        pl.BlockSpec((2, depth, hidden), lambda k: (0, base + k, 0)),
    ]
    if start is not None:
        operands.append(start)
        specs.append(whole)
    return pl.pallas_call(
        functools.partial(forward_kernel, start is not None, tile_of(hidden, 256)),
        grid=(step // depth,),
        in_specs=specs,
        out_specs=whole,
        out_shape=jax.ShapeDtypeStruct((2, 2 * half, hidden), F32),
        compiler_params=params(32),
        cost_estimate=cost(8 * half * step * hidden, 4 * step * hidden),
    )(*operands)


def low_in_kernel(segments, rows, adapters, slots, columns, seg, *rest):
    out = rest[-1]
    total = jnp.zeros((columns.shape[0], out.shape[1]), F32)
    for s in range(segments):
        part = dot(columns[...], rest[s][0])
        total = total + jnp.where(seg[...] == s, part, 0.0)
    put_rows(out, total, slots, rows)


def put_rows(out, total, slots, rows):
    if rows % 8:
        out[...] = total
        return
    for s in range(total.shape[0] // rows):
        out[pl.ds(pl.multiple_of(slots[s] * rows, rows), rows), :] = total[s * rows : (s + 1) * rows]


def of_segment(shape, s):
    return pl.BlockSpec((1,) + shape[1:], lambda *a: (a[-2][s], 0, 0))


def low_in_partial(columns, seg, down, adapters, slots, rows):
    segments = adapters.shape[0]
    tokens = columns.shape[0]
    full = lambda shape: pl.BlockSpec(shape, lambda *a: (0,) * len(shape))
    return pl.pallas_call(
        functools.partial(low_in_kernel, segments, rows),
        grid_spec=pltpu.PrefetchScalarGridSpec(
            num_scalar_prefetch=2,
            grid=(1,),
            in_specs=[full(columns.shape), full(seg.shape)]
            + [of_segment(down.shape, s) for s in range(segments)],
            out_specs=full((tokens, down.shape[2])),
        ),
        out_shape=jax.ShapeDtypeStruct((tokens, down.shape[2]), F32),
        compiler_params=params(16),
        cost_estimate=cost(2 * tokens * down[0].size * segments, 2 * down[0].size * segments),
    )(adapters, slots, columns, seg, *([down] * segments))


def middle_kernel(segments, rows, adapters, slots, base, dhidden, order, low, seg, *rest):
    factors = rest[:segments]
    dgate, dup, out, left, back = rest[segments:]
    rank = low.shape[1] // 2
    tokens = order.shape[0]
    n = pl.program_id(0)
    lane = lax.broadcasted_iota(jnp.int32, (tokens, segments * rank), 1) // rank
    mask = lane == seg[...]

    @pl.when(n == 0)
    def _():
        mine = dot(order[...], low[...])
        for i in range(2):
            wide = jnp.concatenate([mine[:, i * rank : (i + 1) * rank]] * segments, axis=1)
            left[i] = jnp.where(mask, wide, 0.0).astype(BF16)
        back[...] = jnp.zeros_like(back)

    up_g = jnp.concatenate([f[0, :rank] for f in factors], axis=0)
    up_u = jnp.concatenate([f[0, rank:] for f in factors], axis=0)
    gate = base[0] + dot(left[0], up_g)
    up = base[1] + dot(left[1], up_u)
    grad = dot(order[...], dhidden[...])
    sigma = 1.0 / (1.0 + jnp.exp(-gate))
    g = (grad * up * sigma * (1.0 + gate * (1.0 - sigma))).astype(BF16)
    u = (grad * gate * sigma).astype(BF16)
    dgate[...] = g
    dup[...] = u
    back[0] += dot(g, up_g, ((1,), (1,)))
    back[1] += dot(u, up_u, ((1,), (1,)))

    @pl.when(n == pl.num_programs(0) - 1)
    def _():
        parts = []
        for i in range(2):
            kept = jnp.where(mask, back[i], 0.0)
            parts.append(sum(kept[:, s * rank : (s + 1) * rank] for s in range(segments)))
        put_rows(out, jnp.concatenate(parts, axis=1), slots, rows)


def middle(base, dhidden, order, low, seg, up, adapters, slots, rows):
    segments = adapters.shape[0]
    tokens, hidden = dhidden.shape
    wide = up.shape[1]
    tile = tile_of(hidden, 256)
    full = lambda shape: pl.BlockSpec(shape, lambda *a: (0,) * len(shape))
    across = lambda lead: pl.BlockSpec(lead + (tokens, tile), lambda n, *a: (0,) * len(lead) + (0, n))

    def factor(s):
        return pl.BlockSpec((1, wide, tile), lambda n, adapters, slots: (adapters[s], 0, n))

    return pl.pallas_call(
        functools.partial(middle_kernel, segments, rows),
        grid_spec=pltpu.PrefetchScalarGridSpec(
            num_scalar_prefetch=2,
            grid=(hidden // tile,),
            in_specs=[across((2,)), across(()), full(order.shape), full(low.shape), full(seg.shape)]
            + [factor(s) for s in range(segments)],
            out_specs=[across(()), across(()), full((tokens, wide))],
            scratch_shapes=[
                pltpu.VMEM((2, tokens, segments * wide // 2), BF16),
                pltpu.VMEM((2, tokens, segments * wide // 2), F32),
            ],
        ),
        out_shape=[
            jax.ShapeDtypeStruct((tokens, hidden), BF16),
            jax.ShapeDtypeStruct((tokens, hidden), BF16),
            jax.ShapeDtypeStruct((tokens, wide), F32),
        ],
        compiler_params=params(32),
        cost_estimate=cost(
            4 * tokens * hidden * segments * wide, hidden * (tokens * 14 + segments * wide * 2)
        ),
    )(adapters, slots, base, dhidden, order, low, seg, *([up] * segments))


def grad_b_kernel(dgate, dup, order, low, adapter, out, left):
    adapters, wide, tile = out.shape
    rank = wide // 2

    @pl.when(pl.program_id(0) == 0)
    def _():
        turned = dot(order[...], low[...]).T
        for a in range(adapters):
            kept = jnp.where(adapter[...] == a, turned, 0.0).astype(BF16)
            left[0, a * rank : (a + 1) * rank] = kept[:rank]
            left[1, a * rank : (a + 1) * rank] = kept[rank:]

    for i, grad in enumerate((dgate, dup)):
        part = dot(left[i], grad[...])
        out[:, i * rank : (i + 1) * rank, :] = part.reshape(adapters, rank, tile)


def grad_b_of(dgate, dup, order, low, adapter_row, adapters):
    tokens, hidden = dgate.shape
    wide = low.shape[1]
    tile = tile_of(hidden, 256)
    full = lambda shape: pl.BlockSpec(shape, lambda n: (0,) * len(shape))
    across = pl.BlockSpec((tokens, tile), lambda n: (0, n))
    return pl.pallas_call(
        grad_b_kernel,
        grid=(hidden // tile,),
        in_specs=[across, across, full(order.shape), full(low.shape), full(adapter_row.shape)],
        out_specs=pl.BlockSpec((adapters, wide, tile), lambda n: (0, 0, n)),
        out_shape=jax.ShapeDtypeStruct((adapters, wide, hidden), F32),
        scratch_shapes=[pltpu.VMEM((2, adapters * wide // 2, tokens), BF16)],
        compiler_params=params(32),
        cost_estimate=cost(2 * tokens * hidden * adapters * wide, 4 * hidden * adapters * wide),
    )(dgate, dup, order, low, adapter_row)


def grad_a_kernel(per, columns, order, low, adapter, out, turned, mine):
    @pl.when(pl.program_id(0) == 0)
    def _():
        turned[...] = columns[...].astype(F32).T.astype(BF16)
        mine[...] = dot(order[...], low[...])

    for j in range(per):
        a = pl.program_id(0) * per + j
        kept = jnp.where(adapter[...] == a, mine[...], 0.0).astype(BF16)
        out[j] = dot(turned[...], kept)


def grad_a_of(columns, order, low, adapter, adapters):
    tokens, shard = columns.shape
    wide = low.shape[1]
    per = 4 if adapters % 4 == 0 else 1
    full = lambda shape: pl.BlockSpec(shape, lambda n: (0,) * len(shape))
    return pl.pallas_call(
        functools.partial(grad_a_kernel, per),
        grid=(adapters // per,),
        in_specs=[full(columns.shape), full(order.shape), full(low.shape), full(adapter.shape)],
        out_specs=pl.BlockSpec((per, shard, wide), lambda n: (n, 0, 0)),
        out_shape=jax.ShapeDtypeStruct((adapters, shard, wide), F32),
        scratch_shapes=[pltpu.VMEM((shard, tokens), BF16), pltpu.VMEM((tokens, wide), F32)],
        compiler_params=params(16),
        cost_estimate=cost(2 * tokens * shard * adapters * wide, 4 * shard * adapters * wide),
    )(columns, order, low, adapter)


def side_kernel(segments, adapters, slots, order, low, seg, *rest):
    out = rest[-1]
    turned = dot(order[...], low[...]).T
    total = jnp.zeros(out.shape, F32)
    for s in range(segments):
        kept = jnp.where(seg[...] == s, turned, 0.0).astype(BF16)
        total = total + dot(rest[s][0], kept)
    out[...] = total


def side_of(order, low, seg_row, down, adapters, slots):
    segments = adapters.shape[0]
    tokens = order.shape[0]
    shard = down.shape[1]
    full = lambda shape: pl.BlockSpec(shape, lambda *a: (0,) * len(shape))
    return pl.pallas_call(
        functools.partial(side_kernel, segments),
        grid_spec=pltpu.PrefetchScalarGridSpec(
            num_scalar_prefetch=2,
            grid=(1,),
            in_specs=[full(order.shape), full(low.shape), full(seg_row.shape)]
            + [of_segment(down.shape, s) for s in range(segments)],
            out_specs=full((shard, tokens)),
        ),
        out_shape=jax.ShapeDtypeStruct((shard, tokens), F32),
        compiler_params=params(16),
        cost_estimate=cost(2 * tokens * down[0].size * segments, 2 * down[0].size * segments),
    )(adapters, slots, order, low, seg_row, *([down] * segments))


def backward_kernel(base, at, w, dgate, dup, side, out, total):
    block, tokens = total.shape
    shard = side.shape[0]
    total[...] = dot(w[0], dgate[...], ((1,), (1,))) + dot(w[1], dup[...], ((1,), (1,)))
    first = at[0] * shard

    @pl.when(first // block == base + pl.program_id(0))
    def _():
        here = pl.ds(pl.multiple_of(first % block, shard), shard)
        total[here, :] += side[...]

    out[...] = total[...].T.astype(BF16)


def backward_chunk(frozen, dgate, dup, side, at, q, step):
    tokens, hidden = dgate.shape
    block = tile_of(step, 512)
    base = q * (step // block)
    full = lambda shape: pl.BlockSpec(shape, lambda *a: (0,) * len(shape))
    return pl.pallas_call(
        functools.partial(backward_kernel, base),
        grid_spec=pltpu.PrefetchScalarGridSpec(
            num_scalar_prefetch=1,
            grid=(step // block,),
            in_specs=[
                pl.BlockSpec((2, block, hidden), lambda k, at: (0, base + k, 0)),
                full(dgate.shape),
                full(dup.shape),
                full(side.shape),
            ],
            out_specs=pl.BlockSpec((tokens, block), lambda k, at: (0, k)),
            scratch_shapes=[pltpu.VMEM((block, tokens), F32)],
        ),
        out_shape=jax.ShapeDtypeStruct((tokens, step), BF16),
        compiler_params=params(32),
        cost_estimate=cost(4 * tokens * step * hidden, 4 * step * hidden),
    )(at, frozen, dgate, dup, side)


def local(
    activations,
    dhidden,
    frozen,
    adapter_down_factors,
    adapter_up_factors,
    segment_adapter_index,
    segment_row_counts,
    ranks,
):
    adapter_list, shard_width, gate_and_up = adapter_down_factors.shape
    rank = gate_and_up // 2
    width = frozen.shape[1]
    rows = activations.shape[0]
    torus = Torus(width // shard_width)
    tokens = rows * torus.size
    a, b, c = torus.dims
    index = lax.axis_index("tensor")
    slots = torus.slot_devices(index)
    token = (slots[:, None] * rows + jnp.arange(rows, dtype=jnp.int32)[None, :]).reshape(-1)

    ends = jnp.cumsum(segment_row_counts[0])
    seg_adapter = segment_adapter_index[0]
    count = ends.shape[0]

    def segment_of(place):
        return jnp.sum((place[:, None] >= ends[None, :]).astype(jnp.int32), axis=1)

    def adapter_of(segment):
        match = segment[:, None] == jnp.arange(count, dtype=jnp.int32)[None, :]
        return jnp.sum(jnp.where(match, seg_adapter[None, :], 0), axis=1)

    column = jnp.arange(gate_and_up, dtype=jnp.int32) % rank
    mine = index * rows + jnp.arange(rows, dtype=jnp.int32)
    my_adapter = adapter_of(segment_of(mine))
    hit = my_adapter[:, None] == jnp.arange(adapter_list, dtype=jnp.int32)[None, :]
    my_rank = jnp.sum(jnp.where(hit, ranks[None, :], 0), axis=1)[:, None]
    factor = jnp.where(column[None, :] < my_rank, 16.0 / my_rank.astype(F32), 0.0)

    segment = segment_of(token)
    adapter = adapter_of(segment)
    order = (token[:, None] == jnp.arange(tokens, dtype=jnp.int32)[None, :]).astype(BF16)

    def whole_sum(partial):
        if rows % 8:
            partial = jnp.take(
                partial.reshape(torus.size, rows, -1), torus.slots_of(index), axis=0
            )
        parts = lax.all_to_all(partial.reshape(torus.size, rows, gate_and_up), "tensor", 0, 0)
        low = (jnp.sum(parts, axis=0) * factor).astype(BF16)
        spread = jnp.broadcast_to(low[None], (torus.size, rows, gate_and_up))
        return lax.all_to_all(spread, "tensor", 0, 0).reshape(tokens, gate_and_up)

    step = width // CHUNKS
    pieces = []
    columns = None
    for q in range(CHUNKS):
        x = torus.gather(activations[:, q * step : (q + 1) * step], 0)
        x = torus.gather(x, 1).reshape(tokens // c, step)
        y = torus.move(x, 2, -1)
        pieces.append((x, y))
        first = index * shard_width - q * step
        at = jnp.clip(first, 0, step - shard_width)
        cut = jnp.concatenate(
            [lax.dynamic_slice_in_dim(v, at, shard_width, 1) for v in (x, y)], axis=0
        )
        inside = (first >= 0) & (first < step)
        columns = cut if columns is None else jnp.where(inside, cut, columns)

    base = None
    for q, (x, y) in enumerate(pieces):
        base = forward_chunk(x, y, frozen, base, q)

    partial_in = low_in_partial(
        columns, segment[:, None], adapter_down_factors, seg_adapter, slots, rows
    )
    low_in = whole_sum(partial_in)
    dgate, dup, partial_out = middle(
        base, dhidden, order, low_in, segment[:, None], adapter_up_factors, seg_adapter, slots, rows
    )
    low_out = whole_sum(partial_out)
    grad_b = grad_b_of(dgate, dup, order, low_in, adapter[None, :], adapter_list)
    side = side_of(order, low_out, segment[None, :], adapter_down_factors, seg_adapter, slots)
    blocks = []
    for q in range(CHUNKS):
        term = backward_chunk(frozen, dgate, dup, side, index[None], q, step)
        term = term.reshape(c, b, a, rows, step)
        term = torus.scatter_sum(term, 2).astype(BF16)
        term = torus.scatter_sum(term, 1).astype(BF16)
        blocks.append(torus.scatter_sum(term, 0).astype(BF16))
    dinput = jnp.concatenate(blocks, axis=1)
    grad_a = grad_a_of(columns, order, low_out, adapter[:, None], adapter_list)
    return (dinput, grad_a, grad_b)


def solution(mesh):
    placed = (
        P(("groups", "tensor"), None),
        P("groups", "tensor"),
        P(None, None, "tensor"),
        P(None, "tensor", None),
        P(None, None, "tensor"),
        P("groups", None),
        P("groups", None),
        P(),
    )
    return jax.shard_map(
        local,
        mesh=mesh,
        in_specs=placed,
        out_specs=(
            P(("groups", "tensor"), None),
            P("groups", "tensor", None),
            P("groups", None, "tensor"),
        ),
        check_vma=False,
    )
```

profile of v0, /device:TPU:0, one launch (start us, length us, event | category | flops | bytes accessed | tf_op | source)
XLA Modules:
  0.0 249.7 jit_solution(1787950276471274525)
XLA Ops:
  1.6 4.1 %collective-permute-start.6 = (bf16[16,2048]{1,0:T(8,128)(2,1)S(1)}, bf16[16,2048]{1,0:T(8,128)(2,1)S(1)}, u32[]{:S(2)}, u32[]{:S(2)}) collective-permute-start(bf16[16,2048]{1,0:T(8,128)(2,1)S(1)} %get-tuple-element.37), channel_id=1, source_target_pairs={{0,8},{1,9},{2,10},{3,11},{4,12},{5,13},{6,14},{7,15},{8,0},{9,1},... | collective-permute-start | bytes 196616 | tf_op jit(solution)/shard_map/ppermute | solution.py:52
  7.1 1.7 collective-permute-start.11
  16.0 3.4 %collective-permute-start.1 = (bf16[16,2048]{1,0:T(8,128)(2,1)S(1)}, bf16[16,2048]{1,0:T(8,128)(2,1)S(1)}, u32[]{:S(2)}, u32[]{:S(2)}) collective-permute-start(bf16[16,2048]{1,0:T(8,128)(2,1)S(1)} %get-tuple-element.38), channel_id=1, source_target_pairs={{0,8},{1,9},{2,10},{3,11},{4,12},{5,13},{6,14},{7,15},{8,0},{9,1},... | collective-permute-start | bytes 196616 | tf_op jit(solution)/shard_map/ppermute | solution.py:52
  21.1 2.8 %collective-permute-start.15 = (bf16[16,2048]{1,0:T(8,128)(2,1)S(1)}, bf16[16,2048]{1,0:T(8,128)(2,1)S(1)}, u32[]{:S(2)}, u32[]{:S(2)}) collective-permute-start(bf16[16,2048]{1,0:T(8,128)(2,1)S(1)} %get-tuple-element.39), channel_id=1, source_target_pairs={{0,12},{1,13},{2,14},{3,15},{4,0},{5,1},{6,2},{7,3},{8,4},{9,5},{1... | collective-permute-start | bytes 196616 | tf_op jit(solution)/shard_map/ppermute | solution.py:52
  23.9 4.4 %collective-permute-done.16 = bf16[16,2048]{1,0:T(8,128)(2,1)S(1)} collective-permute-done((bf16[16,2048]{1,0:T(8,128)(2,1)S(1)}, bf16[16,2048]{1,0:T(8,128)(2,1)S(1)}, u32[]{:S(2)}, u32[]{:S(2)}) %collective-permute-start.16) | collective-permute-done | bytes 65568 | tf_op jit(solution)/shard_map/ppermute | solution.py:52
  32.2 2.1 collective-permute-done.2
  34.4 1.6 collective-permute-start.3
  36.0 7.3 %collective-permute-done.13 = bf16[4,16,2048]{2,1,0:T(8,128)(2,1)S(1)} collective-permute-done((bf16[4,16,2048]{2,1,0:T(8,128)(2,1)S(1)}, bf16[4,16,2048]{2,1,0:T(8,128)(2,1)S(1)}, u32[]{:S(2)}, u32[]{:S(2)}) %collective-permute-start.13) | collective-permute-done | bytes 262176 | tf_op jit(solution)/shard_map/ppermute | solution.py:52
  43.4 5.5 %collective-permute-done.18 = bf16[4,16,2048]{2,1,0:T(8,128)(2,1)S(1)} collective-permute-done((bf16[4,16,2048]{2,1,0:T(8,128)(2,1)S(1)}, bf16[4,16,2048]{2,1,0:T(8,128)(2,1)S(1)}, u32[]{:S(2)}, u32[]{:S(2)}) %collective-permute-start.18) | collective-permute-done | bytes 262176 | tf_op jit(solution)/shard_map/ppermute | solution.py:52
  49.0 4.0 %collective-permute-done.3 = bf16[4,16,2048]{2,1,0:T(8,128)(2,1)S(1)} collective-permute-done((bf16[4,16,2048]{2,1,0:T(8,128)(2,1)S(1)}, bf16[4,16,2048]{2,1,0:T(8,128)(2,1)S(1)}, u32[]{:S(2)}, u32[]{:S(2)}) %collective-permute-start.3) | collective-permute-done | bytes 262176 | tf_op jit(solution)/shard_map/ppermute | solution.py:52
  56.9 1.9 shard_map.107
  58.9 5.9 %all-to-all-start = ((f32[16,16,128]{2,1,0:T(8,128)}), f32[16,16,128]{2,1,0:T(8,128)}, u32[]{:S(2)}, u32[]{:S(2)}) async-start(f32[16,16,128]{2,1,0:T(8,128)} %bitcast.33), calls=%async_computation | async-start | bytes 262144 | tf_op jit(solution)/shard_map/all_to_all | solution.py:417
  66.8 7.9 %shard_map.103.rest_0_ = f32[2,256,1792]{2,1,0:T(8,128)S(1)} custom-call(bf16[128,2048]{1,0:T(8,128)(2,1)S(1)} %bitcast.140, bf16[128,2048]{1,0:T(8,128)(2,1)S(1)} %copy-done.28, bf16[2,8192,1792]{2,1,0:T(8,128)(2,1)} %w.15), custom_call_target="tpu_custom_call" | custom-call | flops 3758096384 | bytes 14680064 | tf_op jit(solution)/shard_map/pallas_call | solution.py:110
  74.8 7.9 %shard_map.104.rest_0_ = f32[2,256,1792]{2,1,0:T(8,128)S(1)} custom-call(bf16[128,2048]{1,0:T(8,128)(2,1)S(1)} %bitcast.134, bf16[128,2048]{1,0:T(8,128)(2,1)S(1)} %copy-done.24, bf16[2,8192,1792]{2,1,0:T(8,128)(2,1)} %w.15, f32[2,256,1792]{2,1,0:T(8,128)S(1)} %shard_map.103.rest_0_), custom_call_target="tpu_custom_call" | custom-call | flops 3758096384 | bytes 14680064 | tf_op jit(solution)/shard_map/pallas_call | solution.py:110
  82.7 7.8 %shard_map.105.rest_0_ = f32[2,256,1792]{2,1,0:T(8,128)S(1)} custom-call(bf16[128,2048]{1,0:T(8,128)(2,1)S(1)} %bitcast.143, bf16[128,2048]{1,0:T(8,128)(2,1)S(1)} %copy-done.30, bf16[2,8192,1792]{2,1,0:T(8,128)(2,1)} %w.15, f32[2,256,1792]{2,1,0:T(8,128)S(1)} %shard_map.104.rest_0_), custom_call_target="tpu_custom_call" | custom-call | flops 3758096384 | bytes 14680064 | tf_op jit(solution)/shard_map/pallas_call | solution.py:110
  90.5 1.8 copy-done.8
  94.0 6.0 %all-to-all-start.1 = ((bf16[16,16,128]{2,1,0:T(8,128)(2,1)}), bf16[16,16,128]{2,1,0:T(8,128)(2,1)S(1)}, u32[]{:S(2)}, u32[]{:S(2)}) async-start(bf16[16,16,128]{2,1,0:T(8,128)(2,1)} %broadcast_in_dim.101), calls=%async_computation.1 | async-start | bytes 131072 | tf_op jit(solution)/shard_map/all_to_all | solution.py:420
  100.0 2.0 copy-done.9
  104.1 7.8 %shard_map.106.base = f32[2,256,1792]{2,1,0:T(8,128)S(1)} custom-call(bf16[128,2048]{1,0:T(8,128)(2,1)S(1)} %bitcast.137, bf16[128,2048]{1,0:T(8,128)(2,1)S(1)} %copy-done.26, bf16[2,8192,1792]{2,1,0:T(8,128)(2,1)} %w.15, f32[2,256,1792]{2,1,0:T(8,128)S(1)} %copy-done.9), custom_call_target="tpu_custom_call" | custom-call | flops 3758096384 | bytes 14680064 | tf_op jit(solution)/shard_map/pallas_call | solution.py:110
  111.9 1.8 copy-done.10
  113.8 4.1 %copy-done.1 = bf16[24,128,1792]{2,1,0:T(8,128)(2,1)S(1)} copy-done((bf16[24,128,1792]{2,1,0:T(8,128)(2,1)S(1)}, bf16[24,128,1792]{2,1,0:T(8,128)(2,1)}, u32[]{:S(2)}) %copy-start.1) | copy-done | bytes 11010072
  117.9 2.0 copy-done.11
  121.1 7.6 %shard_map.108 = (bf16[256,1792]{1,0:T(8,128)(2,1)S(1)}, bf16[256,1792]{1,0:T(8,128)(2,1)S(1)}, f32[256,128]{1,0:T(8,128)S(1)}) custom-call(s32[8]{0:T(128)S(1)} %bitcast.155, s32[16]{0:T(128)S(1)} %get-tuple-element.10.slots, f32[2,256,1792]{2,1,0:T(8,128)S(1)} %copy-done.11, bf16[256,1792]{1,0:T(8,128)(2,1)S(1)} %copy-done.22, ...), custom_call_target="tpu_custom_call" | custom-call | flops 1879048192 | bytes 10092544 | tf_op jit(solution)/shard_map/pallas_call | solution.py:211
  131.2 6.0 %all-to-all-start.2 = ((f32[16,16,128]{2,1,0:T(8,128)}), f32[16,16,128]{2,1,0:T(8,128)}, u32[]{:S(2)}, u32[]{:S(2)}) async-start(f32[16,16,128]{2,1,0:T(8,128)} %bitcast.148), calls=%async_computation.2 | async-start | bytes 262144 | tf_op jit(solution)/shard_map/all_to_all | solution.py:417
  138.2 7.1 %all-to-all-done.2 = f32[16,16,128]{2,1,0:T(8,128)} async-done(((f32[16,16,128]{2,1,0:T(8,128)}), f32[16,16,128]{2,1,0:T(8,128)}, u32[]{:S(2)}, u32[]{:S(2)}) %all-to-all-start.2) | async-done | bytes 131104 | tf_op jit(solution)/shard_map/all_to_all | solution.py:417
  146.9 3.7 %all-to-all-start.3 = ((bf16[16,16,128]{2,1,0:T(8,128)(2,1)}), bf16[16,16,128]{2,1,0:T(8,128)(2,1)S(1)}, u32[]{:S(2)}, u32[]{:S(2)}) async-start(bf16[16,16,128]{2,1,0:T(8,128)(2,1)} %broadcast_in_dim.102), calls=%async_computation.3 | async-start | bytes 131072 | tf_op jit(solution)/shard_map/all_to_all | solution.py:420
  152.9 9.5 %shard_map.115 = f32[24,128,1792]{2,1,0:T(8,128)} custom-call(bf16[256,1792]{1,0:T(8,128)(2,1)S(1)} %copy-done.3, bf16[256,1792]{1,0:T(8,128)(2,1)S(1)} %copy-done.6, bf16[256,256]{1,0:T(8,128)(2,1)S(1)} %fusion.8.order, bf16[256,128]{1,0:T(8,128)(2,1)S(1)} %bitcast.147, s32[1,256]{1,0:T(1,128)S(1)} %bitcast.152), custom_call_target="tpu_custom_call" | custom-call | flops 2818572288 | bytes 22020096 | tf_op jit(solution)/shard_map/pallas_call | solution.py:259
  164.0 8.2 %shard_map.113 = bf16[256,2048]{1,0:T(8,128)(2,1)S(1)} custom-call(s32[1]{0:T(128)} %bitcast.at, bf16[2,8192,1792]{2,1,0:T(8,128)(2,1)} %w.15, bf16[256,1792]{1,0:T(8,128)(2,1)S(1)} %copy-done.4, bf16[256,1792]{1,0:T(8,128)(2,1)S(1)} %copy-done.7, f32[512,256]{1,0:T(8,128)S(1)} %shard_map.109.side), custom_call_target="tpu_custom_call" | custom-call | flops 3758096384 | bytes 14680064 | tf_op jit(solution)/shard_map/pallas_call | solution.py:349
  172.3 8.2 %shard_map.112 = bf16[256,2048]{1,0:T(8,128)(2,1)S(1)} custom-call(s32[1]{0:T(128)} %bitcast.at, bf16[2,8192,1792]{2,1,0:T(8,128)(2,1)} %w.15, bf16[256,1792]{1,0:T(8,128)(2,1)S(1)} %copy-done.4, bf16[256,1792]{1,0:T(8,128)(2,1)S(1)} %copy-done.7, f32[512,256]{1,0:T(8,128)S(1)} %shard_map.109.side), custom_call_target="tpu_custom_call" | custom-call | flops 3758096384 | bytes 14680064 | tf_op jit(solution)/shard_map/pallas_call | solution.py:349
  180.5 8.2 %shard_map.111 = bf16[256,2048]{1,0:T(8,128)(2,1)S(1)} custom-call(s32[1]{0:T(128)} %bitcast.at, bf16[2,8192,1792]{2,1,0:T(8,128)(2,1)} %w.15, bf16[256,1792]{1,0:T(8,128)(2,1)S(1)} %copy-done.4, bf16[256,1792]{1,0:T(8,128)(2,1)S(1)} %copy-done.7, f32[512,256]{1,0:T(8,128)S(1)} %shard_map.109.side), custom_call_target="tpu_custom_call" | custom-call | flops 3758096384 | bytes 14680064 | tf_op jit(solution)/shard_map/pallas_call | solution.py:349
  188.7 8.2 %shard_map.110 = bf16[256,2048]{1,0:T(8,128)(2,1)S(1)} custom-call(s32[1]{0:T(128)} %bitcast.at, bf16[2,8192,1792]{2,1,0:T(8,128)(2,1)} %w.15, bf16[256,1792]{1,0:T(8,128)(2,1)S(1)} %copy-done.4, bf16[256,1792]{1,0:T(8,128)(2,1)S(1)} %copy-done.7, f32[512,256]{1,0:T(8,128)S(1)} %shard_map.109.side), custom_call_target="tpu_custom_call" | custom-call | flops 3758096384 | bytes 14680064 | tf_op jit(solution)/shard_map/pallas_call | solution.py:349
  198.7 5.3 %shard_map.114 = f32[24,512,128]{2,1,0:T(8,128)} custom-call(bf16[256,512]{1,0:T(8,128)(2,1)S(1)} %copy-done.21, bf16[256,256]{1,0:T(8,128)(2,1)S(1)} %fusion.8.order, bf16[256,128]{1,0:T(8,128)(2,1)S(1)} %bitcast.145, s32[256,1]{1,0:T(8,128)S(1)} %copy-done.31), custom_call_target="tpu_custom_call" | custom-call | flops 805306368 | bytes 6291456 | tf_op jit(solution)/shard_map/pallas_call | solution.py:288
  204.2 1.6 collective-permute-start.36
  206.7 1.6 collective-permute-start.21
  209.0 4.4 %collective-permute-done.36 = bf16[4,16,2048]{2,1,0:T(8,128)(2,1)S(1)} collective-permute-done((bf16[4,16,2048]{2,1,0:T(8,128)(2,1)S(1)}, bf16[4,16,2048]{2,1,0:T(8,128)(2,1)S(1)}, u32[]{:S(2)}, u32[]{:S(2)}) %collective-permute-start.36) | collective-permute-done | bytes 262176 | tf_op jit(solution)/shard_map/ppermute | solution.py:52
  213.5 1.7 collective-permute-start.37
  215.2 2.2 collective-permute-start.39
  217.4 1.6 collective-permute-done.31
  219.0 2.6 %collective-permute-start.38 = (bf16[16,2048]{1,0:T(8,128)(2,1)S(1)}, bf16[16,2048]{1,0:T(8,128)(2,1)S(1)}, u32[]{:S(2)}, u32[]{:S(2)}) collective-permute-start(bf16[16,2048]{1,0:T(8,128)(2,1)S(1)} %get-tuple-element.30), channel_id=1, source_target_pairs={{0,8},{1,9},{2,10},{3,11},{4,12},{5,13},{6,14},{7,15},{8,0},{9,1},... | collective-permute-start | bytes 196616 | tf_op jit(solution)/shard_map/ppermute | solution.py:52
  221.7 3.0 %collective-permute-done.21 = bf16[4,16,2048]{2,1,0:T(8,128)(2,1)S(1)} collective-permute-done((bf16[4,16,2048]{2,1,0:T(8,128)(2,1)S(1)}, bf16[4,16,2048]{2,1,0:T(8,128)(2,1)S(1)}, u32[]{:S(2)}, u32[]{:S(2)}) %collective-permute-start.21) | collective-permute-done | bytes 262176 | tf_op jit(solution)/shard_map/ppermute | solution.py:52
  224.6 1.6 collective-permute-start.32
  226.4 3.0 %collective-permute-done.26 = bf16[4,16,2048]{2,1,0:T(8,128)(2,1)S(1)} collective-permute-done((bf16[4,16,2048]{2,1,0:T(8,128)(2,1)S(1)}, bf16[4,16,2048]{2,1,0:T(8,128)(2,1)S(1)}, u32[]{:S(2)}, u32[]{:S(2)}) %collective-permute-start.26) | collective-permute-done | bytes 262176 | tf_op jit(solution)/shard_map/ppermute | solution.py:52
  229.4 3.5 %collective-permute-start.34 = (bf16[16,2048]{1,0:T(8,128)(2,1)S(1)}, bf16[16,2048]{1,0:T(8,128)(2,1)S(1)}, u32[]{:S(2)}, u32[]{:S(2)}) collective-permute-start(bf16[16,2048]{1,0:T(8,128)(2,1)S(1)} %get-tuple-element.26), channel_id=1, source_target_pairs={{0,12},{1,13},{2,14},{3,15},{4,0},{5,1},{6,2},{7,3},{8,4},{9,5},{1... | collective-permute-start | bytes 196616 | tf_op jit(solution)/shard_map/ppermute | solution.py:52
  234.2 2.8 %collective-permute-start.24 = (bf16[16,2048]{1,0:T(8,128)(2,1)S(1)}, bf16[16,2048]{1,0:T(8,128)(2,1)S(1)}, u32[]{:S(2)}, u32[]{:S(2)}) collective-permute-start(bf16[16,2048]{1,0:T(8,128)(2,1)S(1)} %get-tuple-element.20), channel_id=1, source_target_pairs={{0,12},{1,13},{2,14},{3,15},{4,0},{5,1},{6,2},{7,3},{8,4},{9,5},{1... | collective-permute-start | bytes 196616 | tf_op jit(solution)/shard_map/ppermute | solution.py:52
  238.2 2.2 collective-permute-done.33
  240.4 1.9 collective-permute-start.29
  242.4 2.6 %collective-permute-start.28 = (bf16[16,2048]{1,0:T(8,128)(2,1)S(1)}, bf16[16,2048]{1,0:T(8,128)(2,1)S(1)}, u32[]{:S(2)}, u32[]{:S(2)}) collective-permute-start(bf16[16,2048]{1,0:T(8,128)(2,1)S(1)} %get-tuple-element.24), channel_id=1, source_target_pairs={{0,8},{1,9},{2,10},{3,11},{4,12},{5,13},{6,14},{7,15},{8,0},{9,1},... | collective-permute-start | bytes 196616 | tf_op jit(solution)/shard_map/ppermute | solution.py:52
  246.1 2.9 %collective-permute-done.28 = bf16[16,2048]{1,0:T(8,128)(2,1)S(1)} collective-permute-done((bf16[16,2048]{1,0:T(8,128)(2,1)S(1)}, bf16[16,2048]{1,0:T(8,128)(2,1)S(1)}, u32[]{:S(2)}, u32[]{:S(2)}) %collective-permute-start.28) | collective-permute-done | bytes 65568 | tf_op jit(solution)/shard_map/ppermute | solution.py:52
  (192 shorter events, 42.9 us)
Async XLA Ops:
  1.6 17.8 %collective-permute-start.6 = (bf16[16,2048]{1,0:T(8,128)(2,1)S(1)}, bf16[16,2048]{1,0:T(8,128)(2,1)S(1)}, u32[]{:S(2)}, u32[]{:S(2)}) collective-permute-start(bf16[16,2048]{1,0:T(8,128)(2,1)S(1)} %get-tuple-element.37), channel_id=1, source_target_pairs={{0,8},{1,9},{2,10},{3,11},{4,12},{5,13},{6,14},{7,15},{8,0},{9,1},... | collective-permute-start | bytes 196616 | tf_op jit(solution)/shard_map/ppermute | solution.py:52
  5.7 15.3 %collective-permute-start.5 = (bf16[16,2048]{1,0:T(8,128)(2,1)S(1)}, bf16[16,2048]{1,0:T(8,128)(2,1)S(1)}, u32[]{:S(2)}, u32[]{:S(2)}) collective-permute-start(bf16[16,2048]{1,0:T(8,128)(2,1)S(1)} %get-tuple-element.37), channel_id=1, source_target_pairs={{0,12},{1,13},{2,14},{3,15},{4,0},{5,1},{6,2},{7,3},{8,4},{9,5},{1... | collective-permute-start | bytes 196616 | tf_op jit(solution)/shard_map/ppermute | solution.py:52
  7.1 8.0 %collective-permute-start.11 = (bf16[16,2048]{1,0:T(8,128)(2,1)S(1)}, bf16[16,2048]{1,0:T(8,128)(2,1)S(1)}, u32[]{:S(2)}, u32[]{:S(2)}) collective-permute-start(bf16[16,2048]{1,0:T(8,128)(2,1)S(1)} %get-tuple-element.40), channel_id=1, source_target_pairs={{0,8},{1,9},{2,10},{3,11},{4,12},{5,13},{6,14},{7,15},{8,0},{9,1},... | collective-permute-start | bytes 196616 | tf_op jit(solution)/shard_map/ppermute | solution.py:52
  8.8 7.2 %collective-permute-start.10 = (bf16[16,2048]{1,0:T(8,128)(2,1)S(1)}, bf16[16,2048]{1,0:T(8,128)(2,1)S(1)}, u32[]{:S(2)}, u32[]{:S(2)}) collective-permute-start(bf16[16,2048]{1,0:T(8,128)(2,1)S(1)} %get-tuple-element.40), channel_id=1, source_target_pairs={{0,12},{1,13},{2,14},{3,15},{4,0},{5,1},{6,2},{7,3},{8,4},{9,5},{1... | collective-permute-start | bytes 196616 | tf_op jit(solution)/shard_map/ppermute | solution.py:52
  10.1 9.2 %collective-permute-start.12 = (bf16[16,2048]{1,0:T(8,128)(2,1)S(1)}, bf16[16,2048]{1,0:T(8,128)(2,1)S(1)}, u32[]{:S(2)}, u32[]{:S(2)}) collective-permute-start(bf16[16,2048]{1,0:T(8,128)(2,1)S(1)} %get-tuple-element.40), channel_id=1, source_target_pairs={{0,4},{1,5},{2,6},{3,7},{4,8},{5,9},{6,10},{7,11},{8,12},{9,13},{1... | collective-permute-start | bytes 196616 | tf_op jit(solution)/shard_map/ppermute | solution.py:52
  15.1 8.8 %collective-permute-start.7 = (bf16[16,2048]{1,0:T(8,128)(2,1)S(1)}, bf16[16,2048]{1,0:T(8,128)(2,1)S(1)}, u32[]{:S(2)}, u32[]{:S(2)}) collective-permute-start(bf16[16,2048]{1,0:T(8,128)(2,1)S(1)} %get-tuple-element.37), channel_id=1, source_target_pairs={{0,4},{1,5},{2,6},{3,7},{4,8},{5,9},{6,10},{7,11},{8,12},{9,13},{1... | collective-permute-start | bytes 196616 | tf_op jit(solution)/shard_map/ppermute | solution.py:52
  16.0 15.7 %collective-permute-start.1 = (bf16[16,2048]{1,0:T(8,128)(2,1)S(1)}, bf16[16,2048]{1,0:T(8,128)(2,1)S(1)}, u32[]{:S(2)}, u32[]{:S(2)}) collective-permute-start(bf16[16,2048]{1,0:T(8,128)(2,1)S(1)} %get-tuple-element.38), channel_id=1, source_target_pairs={{0,8},{1,9},{2,10},{3,11},{4,12},{5,13},{6,14},{7,15},{8,0},{9,1},... | collective-permute-start | bytes 196616 | tf_op jit(solution)/shard_map/ppermute | solution.py:52
  19.4 12.8 %collective-permute-start = (bf16[16,2048]{1,0:T(8,128)(2,1)S(1)}, bf16[16,2048]{1,0:T(8,128)(2,1)S(1)}, u32[]{:S(2)}, u32[]{:S(2)}) collective-permute-start(bf16[16,2048]{1,0:T(8,128)(2,1)S(1)} %get-tuple-element.38), channel_id=1, source_target_pairs={{0,12},{1,13},{2,14},{3,15},{4,0},{5,1},{6,2},{7,3},{8,4},{9,5},{1... | collective-permute-start | bytes 196616 | tf_op jit(solution)/shard_map/ppermute | solution.py:52
  19.5 8.8 %collective-permute-start.16 = (bf16[16,2048]{1,0:T(8,128)(2,1)S(1)}, bf16[16,2048]{1,0:T(8,128)(2,1)S(1)}, u32[]{:S(2)}, u32[]{:S(2)}) collective-permute-start(bf16[16,2048]{1,0:T(8,128)(2,1)S(1)} %get-tuple-element.39), channel_id=1, source_target_pairs={{0,8},{1,9},{2,10},{3,11},{4,12},{5,13},{6,14},{7,15},{8,0},{9,1},... | collective-permute-start | bytes 196616 | tf_op jit(solution)/shard_map/ppermute | solution.py:52
  21.1 7.4 %collective-permute-start.15 = (bf16[16,2048]{1,0:T(8,128)(2,1)S(1)}, bf16[16,2048]{1,0:T(8,128)(2,1)S(1)}, u32[]{:S(2)}, u32[]{:S(2)}) collective-permute-start(bf16[16,2048]{1,0:T(8,128)(2,1)S(1)} %get-tuple-element.39), channel_id=1, source_target_pairs={{0,12},{1,13},{2,14},{3,15},{4,0},{5,1},{6,2},{7,3},{8,4},{9,5},{1... | collective-permute-start | bytes 196616 | tf_op jit(solution)/shard_map/ppermute | solution.py:52
  23.9 6.2 %collective-permute-start.17 = (bf16[16,2048]{1,0:T(8,128)(2,1)S(1)}, bf16[16,2048]{1,0:T(8,128)(2,1)S(1)}, u32[]{:S(2)}, u32[]{:S(2)}) collective-permute-start(bf16[16,2048]{1,0:T(8,128)(2,1)S(1)} %get-tuple-element.39), channel_id=1, source_target_pairs={{0,4},{1,5},{2,6},{3,7},{4,8},{5,9},{6,10},{7,11},{8,12},{9,13},{1... | collective-permute-start | bytes 196616 | tf_op jit(solution)/shard_map/ppermute | solution.py:52
  28.3 6.1 %collective-permute-start.2 = (bf16[16,2048]{1,0:T(8,128)(2,1)S(1)}, bf16[16,2048]{1,0:T(8,128)(2,1)S(1)}, u32[]{:S(2)}, u32[]{:S(2)}) collective-permute-start(bf16[16,2048]{1,0:T(8,128)(2,1)S(1)} %get-tuple-element.38), channel_id=1, source_target_pairs={{0,4},{1,5},{2,6},{3,7},{4,8},{5,9},{6,10},{7,11},{8,12},{9,13},{1... | collective-permute-start | bytes 196616 | tf_op jit(solution)/shard_map/ppermute | solution.py:52
  28.4 24.8 %collective-permute-start.8 = (bf16[4,16,2048]{2,1,0:T(8,128)(2,1)S(1)}, bf16[4,16,2048]{2,1,0:T(8,128)(2,1)S(1)}, u32[]{:S(2)}, u32[]{:S(2)}) collective-permute-start(bf16[4,16,2048]{2,1,0:T(8,128)(2,1)S(1)} %get-tuple-element.44), channel_id=1, source_target_pairs={{0,2},{1,3},{2,0},{3,1},{4,6},{5,7},{6,4},{7,5},{8,10},{9,11},{10,... | collective-permute-start | bytes 786440 | tf_op jit(solution)/shard_map/ppermute | solution.py:52
  30.0 13.2 %collective-permute-start.13 = (bf16[4,16,2048]{2,1,0:T(8,128)(2,1)S(1)}, bf16[4,16,2048]{2,1,0:T(8,128)(2,1)S(1)}, u32[]{:S(2)}, u32[]{:S(2)}) collective-permute-start(bf16[4,16,2048]{2,1,0:T(8,128)(2,1)S(1)} %get-tuple-element.42), channel_id=1, source_target_pairs={{0,2},{1,3},{2,0},{3,1},{4,6},{5,7},{6,4},{7,5},{8,10},{9,11},{10,... | collective-permute-start | bytes 786440 | tf_op jit(solution)/shard_map/ppermute | solution.py:52
  31.6 17.3 %collective-permute-start.18 = (bf16[4,16,2048]{2,1,0:T(8,128)(2,1)S(1)}, bf16[4,16,2048]{2,1,0:T(8,128)(2,1)S(1)}, u32[]{:S(2)}, u32[]{:S(2)}) collective-permute-start(bf16[4,16,2048]{2,1,0:T(8,128)(2,1)S(1)} %get-tuple-element.32), channel_id=1, source_target_pairs={{0,2},{1,3},{2,0},{3,1},{4,6},{5,7},{6,4},{7,5},{8,10},{9,11},{10,... | collective-permute-start | bytes 786440 | tf_op jit(solution)/shard_map/ppermute | solution.py:52
  34.4 18.7 %collective-permute-start.3 = (bf16[4,16,2048]{2,1,0:T(8,128)(2,1)S(1)}, bf16[4,16,2048]{2,1,0:T(8,128)(2,1)S(1)}, u32[]{:S(2)}, u32[]{:S(2)}) collective-permute-start(bf16[4,16,2048]{2,1,0:T(8,128)(2,1)S(1)} %get-tuple-element.46), channel_id=1, source_target_pairs={{0,2},{1,3},{2,0},{3,1},{4,6},{5,7},{6,4},{7,5},{8,10},{9,11},{10,... | collective-permute-start | bytes 786440 | tf_op jit(solution)/shard_map/ppermute | solution.py:52
  43.3 13.6 %copy-start = (bf16[24,512,128]{2,1,0:T(8,128)(2,1)S(1)}, bf16[24,512,128]{2,1,0:T(8,128)(2,1)}, u32[]{:S(2)}) copy-start(bf16[24,512,128]{2,1,0:T(8,128)(2,1)} %rest_7_.5) | copy-start | bytes 9437188
  43.3 13.6 %copy-start.33 = (s32[1,8]{1,0:T(1,128)S(1)}, s32[1,8]{1,0:T(1,128)}, u32[]{:S(2)}) copy-start(s32[1,8]{1,0:T(1,128)} %param.13) | copy-start | bytes 100
  43.3 10.7 %copy-start.12 = (bf16[2,4,16,2048]{3,2,1,0:T(8,128)(2,1)}, bf16[2,4,16,2048]{3,2,1,0:T(8,128)(2,1)S(1)}, u32[]{:S(2)}) copy-start(bf16[2,4,16,2048]{3,2,1,0:T(8,128)(2,1)S(1)} %pad_maximum_fusion.2) | copy-start | bytes 1572868
  43.4 10.8 %collective-permute-start.14 = (bf16[128,2048]{1,0:T(8,128)(2,1)S(1)}, bf16[128,2048]{1,0:T(8,128)(2,1)S(1)}, u32[]{:S(2)}, u32[]{:S(2)}) collective-permute-start(bf16[128,2048]{1,0:T(8,128)(2,1)S(1)} %bitcast.132), channel_id=1, source_target_pairs={{0,1},{1,0},{2,3},{3,2},{4,5},{5,4},{6,7},{7,6},{8,9},{9,8},{10,11... | collective-permute-start | bytes 1572872 | tf_op jit(solution)/shard_map/ppermute | solution.py:52
  49.0 5.4 %collective-permute-start.19 = (bf16[128,2048]{1,0:T(8,128)(2,1)S(1)}, bf16[128,2048]{1,0:T(8,128)(2,1)S(1)}, u32[]{:S(2)}, u32[]{:S(2)}) collective-permute-start(bf16[128,2048]{1,0:T(8,128)(2,1)S(1)} %bitcast.138), channel_id=1, source_target_pairs={{0,1},{1,0},{2,3},{3,2},{4,5},{5,4},{6,7},{7,6},{8,9},{9,8},{10,11... | collective-permute-start | bytes 1572872 | tf_op jit(solution)/shard_map/ppermute | solution.py:52
  53.1 2.1 collective-permute-start.4
  53.3 2.6 %collective-permute-start.9 = (bf16[128,2048]{1,0:T(8,128)(2,1)S(1)}, bf16[128,2048]{1,0:T(8,128)(2,1)S(1)}, u32[]{:S(2)}, u32[]{:S(2)}) collective-permute-start(bf16[128,2048]{1,0:T(8,128)(2,1)S(1)} %bitcast.141), channel_id=1, source_target_pairs={{0,1},{1,0},{2,3},{3,2},{4,5},{5,4},{6,7},{7,6},{8,9},{9,8},{10,11... | collective-permute-start | bytes 1572872 | tf_op jit(solution)/shard_map/ppermute | solution.py:52
  58.9 33.5 %all-to-all-start = ((f32[16,16,128]{2,1,0:T(8,128)}), f32[16,16,128]{2,1,0:T(8,128)}, u32[]{:S(2)}, u32[]{:S(2)}) async-start(f32[16,16,128]{2,1,0:T(8,128)} %bitcast.33), calls=%async_computation | async-start | bytes 262144 | tf_op jit(solution)/shard_map/all_to_all | solution.py:417
  74.7 7.9 %copy-start.19 = (bf16[2,4,16,2048]{3,2,1,0:T(8,128)(2,1)S(1)}, bf16[2,4,16,2048]{3,2,1,0:T(8,128)(2,1)}, u32[]{:S(2)}) copy-start(bf16[2,4,16,2048]{3,2,1,0:T(8,128)(2,1)} %copy-done.18) | copy-start | bytes 1572868
  94.0 19.8 %all-to-all-start.1 = ((bf16[16,16,128]{2,1,0:T(8,128)(2,1)}), bf16[16,16,128]{2,1,0:T(8,128)(2,1)S(1)}, u32[]{:S(2)}, u32[]{:S(2)}) async-start(bf16[16,16,128]{2,1,0:T(8,128)(2,1)} %broadcast_in_dim.101), calls=%async_computation.1 | async-start | bytes 131072 | tf_op jit(solution)/shard_map/all_to_all | solution.py:420
  131.2 14.0 %all-to-all-start.2 = ((f32[16,16,128]{2,1,0:T(8,128)}), f32[16,16,128]{2,1,0:T(8,128)}, u32[]{:S(2)}, u32[]{:S(2)}) async-start(f32[16,16,128]{2,1,0:T(8,128)} %bitcast.148), calls=%async_computation.2 | async-start | bytes 262144 | tf_op jit(solution)/shard_map/all_to_all | solution.py:417
  146.9 15.6 %all-to-all-start.3 = ((bf16[16,16,128]{2,1,0:T(8,128)(2,1)}), bf16[16,16,128]{2,1,0:T(8,128)(2,1)S(1)}, u32[]{:S(2)}, u32[]{:S(2)}) async-start(bf16[16,16,128]{2,1,0:T(8,128)(2,1)} %broadcast_in_dim.102), calls=%async_computation.3 | async-start | bytes 131072 | tf_op jit(solution)/shard_map/all_to_all | solution.py:420
  197.1 6.9 %collective-permute-start.35 = (bf16[2,4,16,2048]{3,2,1,0:T(8,128)(2,1)S(1)}, bf16[2,4,16,2048]{3,2,1,0:T(8,128)(2,1)S(1)}, u32[]{:S(2)}, u32[]{:S(2)}) collective-permute-start(bf16[2,4,16,2048]{3,2,1,0:T(8,128)(2,1)S(1)} %bitcast.165), channel_id=1, source_target_pairs={{0,1},{1,0},{2,3},{3,2},{4,5},{5,4},{6,7},{7,6},{8,9},{9,8},{10,11... | collective-permute-start | bytes 1572872 | tf_op jit(solution)/shard_map/ppermute | solution.py:52
  197.4 8.5 %collective-permute-start.30 = (bf16[2,4,16,2048]{3,2,1,0:T(8,128)(2,1)S(1)}, bf16[2,4,16,2048]{3,2,1,0:T(8,128)(2,1)S(1)}, u32[]{:S(2)}, u32[]{:S(2)}) collective-permute-start(bf16[2,4,16,2048]{3,2,1,0:T(8,128)(2,1)S(1)} %bitcast.164), channel_id=1, source_target_pairs={{0,1},{1,0},{2,3},{3,2},{4,5},{5,4},{6,7},{7,6},{8,9},{9,8},{10,11... | collective-permute-start | bytes 1572872 | tf_op jit(solution)/shard_map/ppermute | solution.py:52
  197.9 8.5 %collective-permute-start.20 = (bf16[2,4,16,2048]{3,2,1,0:T(8,128)(2,1)S(1)}, bf16[2,4,16,2048]{3,2,1,0:T(8,128)(2,1)S(1)}, u32[]{:S(2)}, u32[]{:S(2)}) collective-permute-start(bf16[2,4,16,2048]{3,2,1,0:T(8,128)(2,1)S(1)} %bitcast.163), channel_id=1, source_target_pairs={{0,1},{1,0},{2,3},{3,2},{4,5},{5,4},{6,7},{7,6},{8,9},{9,8},{10,11... | collective-permute-start | bytes 1572872 | tf_op jit(solution)/shard_map/ppermute | solution.py:52
  198.2 10.1 %collective-permute-start.25 = (bf16[2,4,16,2048]{3,2,1,0:T(8,128)(2,1)S(1)}, bf16[2,4,16,2048]{3,2,1,0:T(8,128)(2,1)S(1)}, u32[]{:S(2)}, u32[]{:S(2)}) collective-permute-start(bf16[2,4,16,2048]{3,2,1,0:T(8,128)(2,1)S(1)} %bitcast.162), channel_id=1, source_target_pairs={{0,1},{1,0},{2,3},{3,2},{4,5},{5,4},{6,7},{7,6},{8,9},{9,8},{10,11... | collective-permute-start | bytes 1572872 | tf_op jit(solution)/shard_map/ppermute | solution.py:52
  204.2 9.2 %collective-permute-start.36 = (bf16[4,16,2048]{2,1,0:T(8,128)(2,1)S(1)}, bf16[4,16,2048]{2,1,0:T(8,128)(2,1)S(1)}, u32[]{:S(2)}, u32[]{:S(2)}) collective-permute-start(bf16[4,16,2048]{2,1,0:T(8,128)(2,1)S(1)} %slice_bitcast_fusion), channel_id=1, source_target_pairs={{0,2},{1,3},{2,0},{3,1},{4,6},{5,7},{6,4},{7,5},{8,10},{9,11},{10,... | collective-permute-start | bytes 786440 | tf_op jit(solution)/shard_map/ppermute | solution.py:52
  206.0 13.0 %collective-permute-start.31 = (bf16[4,16,2048]{2,1,0:T(8,128)(2,1)S(1)}, bf16[4,16,2048]{2,1,0:T(8,128)(2,1)S(1)}, u32[]{:S(2)}, u32[]{:S(2)}) collective-permute-start(bf16[4,16,2048]{2,1,0:T(8,128)(2,1)S(1)} %slice_bitcast_fusion.2), channel_id=1, source_target_pairs={{0,2},{1,3},{2,0},{3,1},{4,6},{5,7},{6,4},{7,5},{8,10},{9,11},{10,... | collective-permute-start | bytes 786440 | tf_op jit(solution)/shard_map/ppermute | solution.py:52
  206.7 18.0 %collective-permute-start.21 = (bf16[4,16,2048]{2,1,0:T(8,128)(2,1)S(1)}, bf16[4,16,2048]{2,1,0:T(8,128)(2,1)S(1)}, u32[]{:S(2)}, u32[]{:S(2)}) collective-permute-start(bf16[4,16,2048]{2,1,0:T(8,128)(2,1)S(1)} %slice_bitcast_fusion.6), channel_id=1, source_target_pairs={{0,2},{1,3},{2,0},{3,1},{4,6},{5,7},{6,4},{7,5},{8,10},{9,11},{10,... | collective-permute-start | bytes 786440 | tf_op jit(solution)/shard_map/ppermute | solution.py:52
  208.5 20.9 %collective-permute-start.26 = (bf16[4,16,2048]{2,1,0:T(8,128)(2,1)S(1)}, bf16[4,16,2048]{2,1,0:T(8,128)(2,1)S(1)}, u32[]{:S(2)}, u32[]{:S(2)}) collective-permute-start(bf16[4,16,2048]{2,1,0:T(8,128)(2,1)S(1)} %slice_bitcast_fusion.4), channel_id=1, source_target_pairs={{0,2},{1,3},{2,0},{3,1},{4,6},{5,7},{6,4},{7,5},{8,10},{9,11},{10,... | collective-permute-start | bytes 786440 | tf_op jit(solution)/shard_map/ppermute | solution.py:52
  213.5 19.5 %collective-permute-start.37 = (bf16[16,2048]{1,0:T(8,128)(2,1)S(1)}, bf16[16,2048]{1,0:T(8,128)(2,1)S(1)}, u32[]{:S(2)}, u32[]{:S(2)}) collective-permute-start(bf16[16,2048]{1,0:T(8,128)(2,1)S(1)} %get-tuple-element.28), channel_id=1, source_target_pairs={{0,4},{1,5},{2,6},{3,7},{4,8},{5,9},{6,10},{7,11},{8,12},{9,13},{1... | collective-permute-start | bytes 196616 | tf_op jit(solution)/shard_map/ppermute | solution.py:52
  215.2 17.9 %collective-permute-start.39 = (bf16[16,2048]{1,0:T(8,128)(2,1)S(1)}, bf16[16,2048]{1,0:T(8,128)(2,1)S(1)}, u32[]{:S(2)}, u32[]{:S(2)}) collective-permute-start(bf16[16,2048]{1,0:T(8,128)(2,1)S(1)} %get-tuple-element.29), channel_id=1, source_target_pairs={{0,12},{1,13},{2,14},{3,15},{4,0},{5,1},{6,2},{7,3},{8,4},{9,5},{1... | collective-permute-start | bytes 196616 | tf_op jit(solution)/shard_map/ppermute | solution.py:52
  219.0 15.2 %collective-permute-start.38 = (bf16[16,2048]{1,0:T(8,128)(2,1)S(1)}, bf16[16,2048]{1,0:T(8,128)(2,1)S(1)}, u32[]{:S(2)}, u32[]{:S(2)}) collective-permute-start(bf16[16,2048]{1,0:T(8,128)(2,1)S(1)} %get-tuple-element.30), channel_id=1, source_target_pairs={{0,8},{1,9},{2,10},{3,11},{4,12},{5,13},{6,14},{7,15},{8,0},{9,1},... | collective-permute-start | bytes 196616 | tf_op jit(solution)/shard_map/ppermute | solution.py:52
  224.6 12.4 %collective-permute-start.32 = (bf16[16,2048]{1,0:T(8,128)(2,1)S(1)}, bf16[16,2048]{1,0:T(8,128)(2,1)S(1)}, u32[]{:S(2)}, u32[]{:S(2)}) collective-permute-start(bf16[16,2048]{1,0:T(8,128)(2,1)S(1)} %get-tuple-element.25), channel_id=1, source_target_pairs={{0,4},{1,5},{2,6},{3,7},{4,8},{5,9},{6,10},{7,11},{8,12},{9,13},{1... | collective-permute-start | bytes 196616 | tf_op jit(solution)/shard_map/ppermute | solution.py:52
  229.4 8.8 %collective-permute-start.34 = (bf16[16,2048]{1,0:T(8,128)(2,1)S(1)}, bf16[16,2048]{1,0:T(8,128)(2,1)S(1)}, u32[]{:S(2)}, u32[]{:S(2)}) collective-permute-start(bf16[16,2048]{1,0:T(8,128)(2,1)S(1)} %get-tuple-element.26), channel_id=1, source_target_pairs={{0,12},{1,13},{2,14},{3,15},{4,0},{5,1},{6,2},{7,3},{8,4},{9,5},{1... | collective-permute-start | bytes 196616 | tf_op jit(solution)/shard_map/ppermute | solution.py:52
  233.0 7.4 %collective-permute-start.33 = (bf16[16,2048]{1,0:T(8,128)(2,1)S(1)}, bf16[16,2048]{1,0:T(8,128)(2,1)S(1)}, u32[]{:S(2)}, u32[]{:S(2)}) collective-permute-start(bf16[16,2048]{1,0:T(8,128)(2,1)S(1)} %get-tuple-element.27), channel_id=1, source_target_pairs={{0,8},{1,9},{2,10},{3,11},{4,12},{5,13},{6,14},{7,15},{8,0},{9,1},... | collective-permute-start | bytes 196616 | tf_op jit(solution)/shard_map/ppermute | solution.py:52
  233.1 9.3 %collective-permute-start.22 = (bf16[16,2048]{1,0:T(8,128)(2,1)S(1)}, bf16[16,2048]{1,0:T(8,128)(2,1)S(1)}, u32[]{:S(2)}, u32[]{:S(2)}) collective-permute-start(bf16[16,2048]{1,0:T(8,128)(2,1)S(1)} %get-tuple-element.19), channel_id=1, source_target_pairs={{0,4},{1,5},{2,6},{3,7},{4,8},{5,9},{6,10},{7,11},{8,12},{9,13},{1... | collective-permute-start | bytes 196616 | tf_op jit(solution)/shard_map/ppermute | solution.py:52
  234.2 10.8 %collective-permute-start.24 = (bf16[16,2048]{1,0:T(8,128)(2,1)S(1)}, bf16[16,2048]{1,0:T(8,128)(2,1)S(1)}, u32[]{:S(2)}, u32[]{:S(2)}) collective-permute-start(bf16[16,2048]{1,0:T(8,128)(2,1)S(1)} %get-tuple-element.20), channel_id=1, source_target_pairs={{0,12},{1,13},{2,14},{3,15},{4,0},{5,1},{6,2},{7,3},{8,4},{9,5},{1... | collective-permute-start | bytes 196616 | tf_op jit(solution)/shard_map/ppermute | solution.py:52
  237.0 9.0 %collective-permute-start.23 = (bf16[16,2048]{1,0:T(8,128)(2,1)S(1)}, bf16[16,2048]{1,0:T(8,128)(2,1)S(1)}, u32[]{:S(2)}, u32[]{:S(2)}) collective-permute-start(bf16[16,2048]{1,0:T(8,128)(2,1)S(1)} %get-tuple-element.21), channel_id=1, source_target_pairs={{0,8},{1,9},{2,10},{3,11},{4,12},{5,13},{6,14},{7,15},{8,0},{9,1},... | collective-permute-start | bytes 196616 | tf_op jit(solution)/shard_map/ppermute | solution.py:52
  238.2 7.9 %collective-permute-start.27 = (bf16[16,2048]{1,0:T(8,128)(2,1)S(1)}, bf16[16,2048]{1,0:T(8,128)(2,1)S(1)}, u32[]{:S(2)}, u32[]{:S(2)}) collective-permute-start(bf16[16,2048]{1,0:T(8,128)(2,1)S(1)} %get-tuple-element.22), channel_id=1, source_target_pairs={{0,4},{1,5},{2,6},{3,7},{4,8},{5,9},{6,10},{7,11},{8,12},{9,13},{1... | collective-permute-start | bytes 196616 | tf_op jit(solution)/shard_map/ppermute | solution.py:52
  240.4 5.7 %collective-permute-start.29 = (bf16[16,2048]{1,0:T(8,128)(2,1)S(1)}, bf16[16,2048]{1,0:T(8,128)(2,1)S(1)}, u32[]{:S(2)}, u32[]{:S(2)}) collective-permute-start(bf16[16,2048]{1,0:T(8,128)(2,1)S(1)} %get-tuple-element.23), channel_id=1, source_target_pairs={{0,12},{1,13},{2,14},{3,15},{4,0},{5,1},{6,2},{7,3},{8,4},{9,5},{1... | collective-permute-start | bytes 196616 | tf_op jit(solution)/shard_map/ppermute | solution.py:52
  242.4 6.5 %collective-permute-start.28 = (bf16[16,2048]{1,0:T(8,128)(2,1)S(1)}, bf16[16,2048]{1,0:T(8,128)(2,1)S(1)}, u32[]{:S(2)}, u32[]{:S(2)}) collective-permute-start(bf16[16,2048]{1,0:T(8,128)(2,1)S(1)} %get-tuple-element.24), channel_id=1, source_target_pairs={{0,8},{1,9},{2,10},{3,11},{4,12},{5,13},{6,14},{7,15},{8,0},{9,1},... | collective-permute-start | bytes 196616 | tf_op jit(solution)/shard_map/ppermute | solution.py:52
  (30 other events, 69.3 us)
where the time goes:
time: 251 us; the launch traced here: 250 us
  Pallas kernels  90.2 us (36%)
  starting transfers between devices  72.4 us (29%)
  waiting for transfers between devices  50 us (20%)
  local copies, waits for them, and re-layouts  28.7 us (11%)
  other arithmetic  7.03 us (3%)
    ppermute x40, starting transfers between devices, move(): return lax.ppermute(x, 'tensor', pairs)  50.9 us
    ppermute x40, waiting for transfers between devices, move(): return lax.ppermute(x, 'tensor', pairs)  42.8 us
    pallas_call x4, Pallas kernels, backward_chunk(): pl.pallas_call(functools.partial(backward_kernel, base), grid_spec=pltpu....  32.9 us
    pallas_call x4, Pallas kernels, forward_chunk(): pl.pallas_call(functools.partial(forward_kernel, start is not None, tile_...  31.4 us
    unnamed x68, local copies, waits for them, and re-layouts  23.8 us
    all_to_all x2, starting transfers between devices, whole_sum(): lax.all_to_all(partial.reshape(torus.size, rows, gate_and_up), 'tensor',...  11.9 us
    all_to_all x2, starting transfers between devices, whole_sum(): return lax.all_to_all(spread, 'tensor', 0, 0).reshape(tokens, gate_and_up)  9.63 us
    pallas_call x1, Pallas kernels, grad_b_of(): pl.pallas_call(grad_b_kernel, grid=(hidden // tile,), in_specs=[across, a...  9.54 us
  transfers between devices with their start and end apart: 44, of which 16 were waited for; matrix products, arithmetic and copies ran while one was open for 3% of the time, Pallas kernels for 19%

commit v1 on v0

--- a/solution.py
+++ b/solution.py
@@ -7,7 +7,8 @@
 from jax.experimental.pallas import tpu as pltpu
 from jax.sharding import PartitionSpec as P
 
-CHUNKS = 4
+GATHER_CHUNKS = 2
+SUM_SHARES = (3, 3, 2)
 MIB = 1024 * 1024
 BF16 = jnp.bfloat16
 F32 = jnp.float32
@@ -27,6 +28,16 @@
 
 def tile_of(size, most):
     return most if size % most == 0 else size
+
+
+def parts_of(count, parts):
+    parts = min(parts, count)
+    ends = [count * k // parts for k in range(parts + 1)]
+    return list(zip(ends[:-1], ends[1:]))
+
+
+def after(x, other):
+    return lax.optimization_barrier((x, other))[0]
 
 
 class Torus:
@@ -68,6 +79,17 @@
         zs = lax.broadcasted_iota(jnp.int32, (c, b, a), 2)
         return (((outer + zs) % a * b + (inner + bs) % b) * c + (core + cs) % c).reshape(-1)
 
+    def exchange_sum(self, x, dim):
+        k = 1
+        while k < self.dims[dim]:
+            pairs = [
+                (i, i + ((i // self.strides[dim] ^ k) - i // self.strides[dim]) * self.strides[dim])
+                for i in range(self.size)
+            ]
+            x = x + lax.ppermute(x, "tensor", pairs)
+            k *= 2
+        return x
+
     def slots_of(self, index):
         outer, inner, core = self.place(index)
         a, b, c = self.dims
@@ -77,69 +99,64 @@
         return (((cs - core) % c * b + (bs - inner) % b) * a + (zs - outer) % a).reshape(-1)
 
 
-def forward_kernel(has_start, tile, near, far, w, *rest):
+def forward_kernel(near, far, w, *rest):
     out = rest[-1]
     x = jnp.concatenate([near[...], far[...]], axis=0)
-    first = pl.program_id(0) == 0
     for i in range(2):
-        for n in range(0, out.shape[2], tile):
-            at = (i, slice(None), slice(n, n + tile))
-            part = dot(x, w[i, :, n : n + tile])
-            if has_start:
-                before = jnp.where(first, rest[0][at], out[at])
-            else:
-                before = jnp.where(first, 0.0, out[at])
-            out[at] = before + part
-
-
-def forward_chunk(near, far, frozen, start, q):
+        part = dot(x, w[i])
+        out[i] = part if len(rest) == 1 else rest[0][i] + part
+
+
+def forward_chunk(near, far, frozen, start, first, tiles):
     half, step = near.shape
     hidden = frozen.shape[2]
-    depth = tile_of(step, 512)
-    base = q * (step // depth)
-    whole = pl.BlockSpec((2, 2 * half, hidden), lambda k: (0, 0, 0))
+    tile = tile_of(hidden, 256)
+    low, high = tiles
+    across = pl.BlockSpec((2, 2 * half, tile), lambda n: (0, 0, low + n))
     operands = [near, far, frozen]
     specs = [
-        pl.BlockSpec((half, depth), lambda k: (0, k)),
-        pl.BlockSpec((half, depth), lambda k: (0, k)),
-        pl.BlockSpec((2, depth, hidden), lambda k: (0, base + k, 0)),
+        pl.BlockSpec((half, step), lambda n: (0, 0)),
+        pl.BlockSpec((half, step), lambda n: (0, 0)),
+        pl.BlockSpec((2, step, tile), lambda n: (0, first // step, low + n)),
     ]
     if start is not None:
         operands.append(start)
-        specs.append(whole)
-    return pl.pallas_call(
-        functools.partial(forward_kernel, start is not None, tile_of(hidden, 256)),
-        grid=(step // depth,),
+        specs.append(across)
+    count = high - low
+    return pl.pallas_call(
+        forward_kernel,
+        grid=(count,),
         in_specs=specs,
-        out_specs=whole,
+        out_specs=across,
         out_shape=jax.ShapeDtypeStruct((2, 2 * half, hidden), F32),
+        input_output_aliases={} if start is None else {3: 0},
         compiler_params=params(32),
-        cost_estimate=cost(8 * half * step * hidden, 4 * step * hidden),
+        cost_estimate=cost(8 * half * step * tile * count, 4 * step * tile * count),
     )(*operands)
 
 
-def low_in_kernel(segments, rows, adapters, slots, columns, seg, *rest):
+def low_in_kernel(segments, rows, adapters, places, columns, seg, *rest):
     out = rest[-1]
     total = jnp.zeros((columns.shape[0], out.shape[1]), F32)
     for s in range(segments):
         part = dot(columns[...], rest[s][0])
         total = total + jnp.where(seg[...] == s, part, 0.0)
-    put_rows(out, total, slots, rows)
-
-
-def put_rows(out, total, slots, rows):
+    put_rows(out, total, places, rows)
+
+
+def put_rows(out, total, places, rows):
     if rows % 8:
         out[...] = total
         return
     for s in range(total.shape[0] // rows):
-        out[pl.ds(pl.multiple_of(slots[s] * rows, rows), rows), :] = total[s * rows : (s + 1) * rows]
+        out[pl.ds(pl.multiple_of(places[s] * rows, rows), rows), :] = total[s * rows : (s + 1) * rows]
 
 
 def of_segment(shape, s):
     return pl.BlockSpec((1,) + shape[1:], lambda *a: (a[-2][s], 0, 0))
 
 
-def low_in_partial(columns, seg, down, adapters, slots, rows):
+def low_in_partial(columns, seg, down, adapters, places, rows):
     segments = adapters.shape[0]
     tokens = columns.shape[0]
     full = lambda shape: pl.BlockSpec(shape, lambda *a: (0,) * len(shape))
@@ -155,10 +172,10 @@
         out_shape=jax.ShapeDtypeStruct((tokens, down.shape[2]), F32),
         compiler_params=params(16),
         cost_estimate=cost(2 * tokens * down[0].size * segments, 2 * down[0].size * segments),
-    )(adapters, slots, columns, seg, *([down] * segments))
-
-
-def middle_kernel(segments, rows, adapters, slots, base, dhidden, order, low, seg, *rest):
+    )(adapters, places, columns, seg, *([down] * segments))
+
+
+def middle_kernel(segments, rows, adapters, places, base, dhidden, token_order, order, low, seg, *rest):
     factors = rest[:segments]
     dgate, dup, out, left, back = rest[segments:]
     rank = low.shape[1] // 2
@@ -179,7 +196,7 @@
     up_u = jnp.concatenate([f[0, rank:] for f in factors], axis=0)
     gate = base[0] + dot(left[0], up_g)
     up = base[1] + dot(left[1], up_u)
-    grad = dot(order[...], dhidden[...])
+    grad = dot(token_order[...], dhidden[...])
     sigma = 1.0 / (1.0 + jnp.exp(-gate))
     g = (grad * up * sigma * (1.0 + gate * (1.0 - sigma))).astype(BF16)
     u = (grad * gate * sigma).astype(BF16)
@@ -194,10 +211,10 @@
         for i in range(2):
             kept = jnp.where(mask, back[i], 0.0)
             parts.append(sum(kept[:, s * rank : (s + 1) * rank] for s in range(segments)))
-        put_rows(out, jnp.concatenate(parts, axis=1), slots, rows)
-
-
-def middle(base, dhidden, order, low, seg, up, adapters, slots, rows):
+        put_rows(out, jnp.concatenate(parts, axis=1), places, rows)
+
+
+def middle(base, dhidden, token_order, order, low, seg, up, adapters, places, rows):
     segments = adapters.shape[0]
     tokens, hidden = dhidden.shape
     wide = up.shape[1]
@@ -206,14 +223,15 @@
     across = lambda lead: pl.BlockSpec(lead + (tokens, tile), lambda n, *a: (0,) * len(lead) + (0, n))
 
     def factor(s):
-        return pl.BlockSpec((1, wide, tile), lambda n, adapters, slots: (adapters[s], 0, n))
+        return pl.BlockSpec((1, wide, tile), lambda n, adapters, places: (adapters[s], 0, n))
 
     return pl.pallas_call(
         functools.partial(middle_kernel, segments, rows),
         grid_spec=pltpu.PrefetchScalarGridSpec(
             num_scalar_prefetch=2,
             grid=(hidden // tile,),
-            in_specs=[across((2,)), across(()), full(order.shape), full(low.shape), full(seg.shape)]
+            in_specs=[across((2,)), across(())]
+            + [full(v.shape) for v in (token_order, order, low, seg)]
             + [factor(s) for s in range(segments)],
             out_specs=[across(()), across(()), full((tokens, wide))],
             scratch_shapes=[
@@ -230,10 +248,11 @@
         cost_estimate=cost(
             4 * tokens * hidden * segments * wide, hidden * (tokens * 14 + segments * wide * 2)
         ),
-    )(adapters, slots, base, dhidden, order, low, seg, *([up] * segments))
-
-
-def grad_b_kernel(dgate, dup, order, low, adapter, out, left):
+    )(adapters, places, base, dhidden, token_order, order, low, seg, *([up] * segments))
+
+
+def grad_b_kernel(dgate, dup, order, low, adapter, *rest):
+    out, left = rest[-2:]
     adapters, wide, tile = out.shape
     rank = wide // 2
 
@@ -250,22 +269,30 @@
         out[:, i * rank : (i + 1) * rank, :] = part.reshape(adapters, rank, tile)
 
 
-def grad_b_of(dgate, dup, order, low, adapter_row, adapters):
+def grad_b_of(dgate, dup, order, low, adapter_row, adapters, start, tiles):
     tokens, hidden = dgate.shape
     wide = low.shape[1]
     tile = tile_of(hidden, 256)
+    first, last = tiles
     full = lambda shape: pl.BlockSpec(shape, lambda n: (0,) * len(shape))
-    across = pl.BlockSpec((tokens, tile), lambda n: (0, n))
+    across = pl.BlockSpec((tokens, tile), lambda n: (0, first + n))
+    operands = [dgate, dup, order, low, adapter_row]
+    specs = [across, across, full(order.shape), full(low.shape), full(adapter_row.shape)]
+    if start is not None:
+        operands.append(start)
+        specs.append(pl.BlockSpec(memory_space=pl.ANY))
+    part = tile * (last - first) * adapters * wide
     return pl.pallas_call(
         grad_b_kernel,
-        grid=(hidden // tile,),
-        in_specs=[across, across, full(order.shape), full(low.shape), full(adapter_row.shape)],
-        out_specs=pl.BlockSpec((adapters, wide, tile), lambda n: (0, 0, n)),
+        grid=(last - first,),
+        in_specs=specs,
+        out_specs=pl.BlockSpec((adapters, wide, tile), lambda n: (0, 0, first + n)),
         out_shape=jax.ShapeDtypeStruct((adapters, wide, hidden), F32),
         scratch_shapes=[pltpu.VMEM((2, adapters * wide // 2, tokens), BF16)],
+        input_output_aliases={} if start is None else {5: 0},
         compiler_params=params(32),
-        cost_estimate=cost(2 * tokens * hidden * adapters * wide, 4 * hidden * adapters * wide),
-    )(dgate, dup, order, low, adapter_row)
+        cost_estimate=cost(2 * tokens * part, 4 * part),
+    )(*operands)
 
 
 def grad_a_kernel(per, columns, order, low, adapter, out, turned, mine):
@@ -297,7 +324,7 @@
     )(columns, order, low, adapter)
 
 
-def side_kernel(segments, adapters, slots, order, low, seg, *rest):
+def side_kernel(segments, adapters, places, order, low, seg, *rest):
     out = rest[-1]
     turned = dot(order[...], low[...]).T
     total = jnp.zeros(out.shape, F32)
@@ -307,7 +334,7 @@
     out[...] = total
 
 
-def side_of(order, low, seg_row, down, adapters, slots):
+def side_of(order, low, seg_row, down, adapters, places):
     segments = adapters.shape[0]
     tokens = order.shape[0]
     shard = down.shape[1]
@@ -324,27 +351,42 @@
         out_shape=jax.ShapeDtypeStruct((shard, tokens), F32),
         compiler_params=params(16),
         cost_estimate=cost(2 * tokens * down[0].size * segments, 2 * down[0].size * segments),
-    )(adapters, slots, order, low, seg_row, *([down] * segments))
+    )(adapters, places, order, low, seg_row, *([down] * segments))
 
 
 def backward_kernel(base, at, w, dgate, dup, side, out, total):
     block, tokens = total.shape
     shard = side.shape[0]
-    total[...] = dot(w[0], dgate[...], ((1,), (1,))) + dot(w[1], dup[...], ((1,), (1,)))
+    part = tile_of(block, 256)
     first = at[0] * shard
-
-    @pl.when(first // block == base + pl.program_id(0))
+    own = first // block == base + pl.program_id(0)
+
+    def product(rows):
+        return dot(w[0, rows], dgate[...], ((1,), (1,))) + dot(w[1, rows], dup[...], ((1,), (1,)))
+
+    @pl.when(jnp.logical_not(own))
     def _():
-        here = pl.ds(pl.multiple_of(first % block, shard), shard)
-        total[here, :] += side[...]
-
-    out[...] = total[...].T.astype(BF16)
-
-
-def backward_chunk(frozen, dgate, dup, side, at, q, step):
+        for n in range(0, block, part):
+            rows = slice(n, n + part)
+            out[:, rows] = product(rows).T.astype(BF16)
+
+    @pl.when(own)
+    def _():
+        if shard == block:
+            for n in range(0, block, part):
+                rows = slice(n, n + part)
+                out[:, rows] = (product(rows) + side[rows]).T.astype(BF16)
+        else:
+            total[...] = product(slice(None))
+            here = pl.ds(pl.multiple_of(first % block, shard), shard)
+            total[here, :] += side[...]
+            out[...] = total[...].T.astype(BF16)
+
+
+def backward_chunk(frozen, dgate, dup, side, at, first, step):
     tokens, hidden = dgate.shape
     block = tile_of(step, 512)
-    base = q * (step // block)
+    base = first // block
     full = lambda shape: pl.BlockSpec(shape, lambda *a: (0,) * len(shape))
     return pl.pallas_call(
         functools.partial(backward_kernel, base),
@@ -399,34 +441,52 @@
         return jnp.sum(jnp.where(match, seg_adapter[None, :], 0), axis=1)
 
     column = jnp.arange(gate_and_up, dtype=jnp.int32) % rank
-    mine = index * rows + jnp.arange(rows, dtype=jnp.int32)
+    chips = a * b
+    core = index % c
+    mine = (jnp.arange(chips, dtype=jnp.int32)[:, None] * c + core) * rows
+    mine = (mine + jnp.arange(rows, dtype=jnp.int32)[None, :]).reshape(-1)
     my_adapter = adapter_of(segment_of(mine))
     hit = my_adapter[:, None] == jnp.arange(adapter_list, dtype=jnp.int32)[None, :]
     my_rank = jnp.sum(jnp.where(hit, ranks[None, :], 0), axis=1)[:, None]
     factor = jnp.where(column[None, :] < my_rank, 16.0 / my_rank.astype(F32), 0.0)
 
+    places = (slots % c - core) % c * chips + slots // c
+    spot = (places[:, None] * rows + jnp.arange(rows, dtype=jnp.int32)[None, :]).reshape(-1)
+    count_up = jnp.arange(tokens, dtype=jnp.int32)[None, :]
+    token_order = (token[:, None] == count_up).astype(BF16)
+    order = (spot[:, None] == count_up).astype(BF16)
+
     segment = segment_of(token)
     adapter = adapter_of(segment)
-    order = (token[:, None] == jnp.arange(tokens, dtype=jnp.int32)[None, :]).astype(BF16)
 
     def whole_sum(partial):
         if rows % 8:
+            at = jnp.arange(torus.size, dtype=jnp.int32)
+            device = at % chips * c + (core + at // chips) % c
             partial = jnp.take(
-                partial.reshape(torus.size, rows, -1), torus.slots_of(index), axis=0
+                partial.reshape(torus.size, rows, -1),
+                jnp.take(torus.slots_of(index), device),
+                axis=0,
             )
-        parts = lax.all_to_all(partial.reshape(torus.size, rows, gate_and_up), "tensor", 0, 0)
-        low = (jnp.sum(parts, axis=0) * factor).astype(BF16)
-        spread = jnp.broadcast_to(low[None], (torus.size, rows, gate_and_up))
-        return lax.all_to_all(spread, "tensor", 0, 0).reshape(tokens, gate_and_up)
-
-    step = width // CHUNKS
-    pieces = []
+        x = torus.scatter_sum(partial.reshape(c, chips * rows, gate_and_up), 2)
+        x = torus.exchange_sum(torus.exchange_sum(x, 1), 0)
+        return torus.gather((x * factor).astype(BF16), 2).reshape(tokens, gate_and_up)
+
+    hidden = frozen.shape[2]
+    tiles = hidden // tile_of(hidden, 256)
+    step = width // GATHER_CHUNKS
     columns = None
-    for q in range(CHUNKS):
-        x = torus.gather(activations[:, q * step : (q + 1) * step], 0)
-        x = torus.gather(x, 1).reshape(tokens // c, step)
+    behind = None
+    base = None
+    for q in range(GATHER_CHUNKS):
+        x = activations[:, q * step : (q + 1) * step]
+        if q:
+            x = after(x, behind)
+        behind = torus.gather(x, 0)
+        x = torus.gather(behind, 1).reshape(tokens // c, step)
+        if q:
+            x = after(x, base)
         y = torus.move(x, 2, -1)
-        pieces.append((x, y))
         first = index * shard_width - q * step
         at = jnp.clip(first, 0, step - shard_width)
         cut = jnp.concatenate(
@@ -434,28 +494,39 @@
         )
         inside = (first >= 0) & (first < step)
         columns = cut if columns is None else jnp.where(inside, cut, columns)
-
-    base = None
-    for q, (x, y) in enumerate(pieces):
-        base = forward_chunk(x, y, frozen, base, q)
+        for cut in parts_of(tiles, 3) if q == GATHER_CHUNKS - 1 else [(0, tiles)]:
+            base = forward_chunk(x, y, frozen, base, q * step, cut)
 
     partial_in = low_in_partial(
-        columns, segment[:, None], adapter_down_factors, seg_adapter, slots, rows
+        columns, segment[:, None], adapter_down_factors, seg_adapter, places, rows
     )
     low_in = whole_sum(partial_in)
     dgate, dup, partial_out = middle(
-        base, dhidden, order, low_in, segment[:, None], adapter_up_factors, seg_adapter, slots, rows
+        base, dhidden, token_order, order, low_in, segment[:, None], adapter_up_factors,
+        seg_adapter, places, rows,
     )
     low_out = whole_sum(partial_out)
-    grad_b = grad_b_of(dgate, dup, order, low_in, adapter[None, :], adapter_list)
-    side = side_of(order, low_out, segment[None, :], adapter_down_factors, seg_adapter, slots)
+    grad_b = None
+    for cut in parts_of(tiles, 2):
+        grad_b = grad_b_of(
+            dgate, dup, order, low_in, adapter[None, :], adapter_list, grad_b, cut
+        )
+    side = side_of(order, low_out, segment[None, :], adapter_down_factors, seg_adapter, places)
     blocks = []
-    for q in range(CHUNKS):
-        term = backward_chunk(frozen, dgate, dup, side, index[None], q, step)
-        term = term.reshape(c, b, a, rows, step)
-        term = torus.scatter_sum(term, 2).astype(BF16)
-        term = torus.scatter_sum(term, 1).astype(BF16)
-        blocks.append(torus.scatter_sum(term, 0).astype(BF16))
+    first = 0
+    cores, inners = [], []
+    for q, share in enumerate(SUM_SHARES):
+        step = width * share // sum(SUM_SHARES)
+        ready = index[None]
+        if q:
+            ready = after(ready, cores[q - 1])
+        if q > 1:
+            ready = after(ready, inners[q - 2])
+        term = backward_chunk(frozen, dgate, dup, side, ready, first, step)
+        cores.append(torus.scatter_sum(term.reshape(c, b, a, rows, step), 2).astype(BF16))
+        inners.append(torus.scatter_sum(cores[q], 1).astype(BF16))
+        blocks.append(torus.scatter_sum(inners[q], 0).astype(BF16))
+        first += step
     dinput = jnp.concatenate(blocks, axis=1)
     grad_a = grad_a_of(columns, order, low_out, adapter[:, None], adapter_list)
     return (dinput, grad_a, grad_b)

time: 251 us -> 206 us (0.82)
  starting transfers between devices: 72.4 us -> 39.6 us
  local copies, waits for them, and re-layouts: 28.7 us -> 10.3 us
  waiting for transfers between devices: 50 us -> 54.9 us
    all_to_all x4 -> x0, starting transfers between devices: 21.6 us -> none  [the longest x2 11.9 us: whole_sum(): lax.all_to_all(partial.reshape(torus.size, rows, gate_and_up), 'tensor',...]
    unnamed x68 -> x48, local copies, waits for them, and re-layouts: 23.8 us -> 3.15 us
    ppermute x40 -> x29, starting transfers between devices: 50.9 us -> 30.9 us  [move(): return lax.ppermute(x, 'tensor', pairs)]
    ppermute x0 -> x6, waiting for transfers between devices: none -> 13.6 us  [exchange_sum(): x = x + lax.ppermute(x, 'tensor', pairs)]
    ppermute x0 -> x6, starting transfers between devices: none -> 8.69 us  [exchange_sum(): x = x + lax.ppermute(x, 'tensor', pairs)]
    all_to_all x4 -> x0, waiting for transfers between devices: 7.12 us -> none  [the longest x2 7.11 us: whole_sum(): lax.all_to_all(partial.reshape(torus.size, rows, gate_and_up), 'tensor',...]
    pallas_call x5 -> x6, Pallas kernels: 41 us -> 45.2 us  [the longest x4 34.1 us: forward_chunk(): pl.pallas_call(forward_kernel, grid=(count,), in_specs=specs, out_specs=a...]
    ppermute x40 -> x29, waiting for transfers between devices: 42.8 us -> 41.3 us  [move(): return lax.ppermute(x, 'tensor', pairs)]
  transfers between devices with their start and end apart: 44 -> 35, of which waited for: 16 -> 17; matrix products, arithmetic and copies ran while one was open for 3% -> 4% of each run, Pallas kernels for 19% -> 27%
where the time goes in v1:
time: 206 us; the launch traced here: 205 us
  Pallas kernels  92.3 us (45%)
  waiting for transfers between devices  54.9 us (27%)
  starting transfers between devices  39.6 us (19%)
  local copies, waits for them, and re-layouts  10.3 us (5%)
  other arithmetic  6.72 us (3%)
    ppermute x29, waiting for transfers between devices, move(): return lax.ppermute(x, 'tensor', pairs)  41.3 us
    pallas_call x4, Pallas kernels, forward_chunk(): pl.pallas_call(forward_kernel, grid=(count,), in_specs=specs, out_specs=a...  34.1 us
    pallas_call x3, Pallas kernels, backward_chunk(): pl.pallas_call(functools.partial(backward_kernel, base), grid_spec=pltpu....  31.5 us
    ppermute x29, starting transfers between devices, move(): return lax.ppermute(x, 'tensor', pairs)  30.9 us
    ppermute x6, waiting for transfers between devices, exchange_sum(): x = x + lax.ppermute(x, 'tensor', pairs)  13.6 us
    pallas_call x2, Pallas kernels, grad_b_of(): pl.pallas_call(grad_b_kernel, grid=(last - first,), in_specs=specs, out_s...  11.1 us
    ppermute x6, starting transfers between devices, exchange_sum(): x = x + lax.ppermute(x, 'tensor', pairs)  8.69 us
    pallas_call x1, Pallas kernels, middle(): pl.pallas_call(functools.partial(middle_kernel, segments, rows), grid_spe...  7.57 us
  transfers between devices with their start and end apart: 35, of which 17 were waited for; matrix products, arithmetic and copies ran while one was open for 4% of the time, Pallas kernels for 27%

profile of v1, /device:TPU:0, one launch (start us, length us, event | category | flops | bytes accessed | tf_op | source)
XLA Modules:
  0.0 205.2 jit_solution(1913337097313550860)
XLA Ops:
  1.6 5.1 %collective-permute-start = (bf16[16,4096]{1,0:T(8,128)(2,1)S(1)}, bf16[16,4096]{1,0:T(8,128)(2,1)S(1)}, u32[]{:S(2)}, u32[]{:S(2)}) collective-permute-start(bf16[16,4096]{1,0:T(8,128)(2,1)S(1)} %get-tuple-element.42), channel_id=1, source_target_pairs={{0,12},{1,13},{2,14},{3,15},{4,0},{5,1},{6,2},{7,3},{8,4},{9,5},{1... | collective-permute-start | bytes 393224 | tf_op jit(solution)/shard_map/ppermute | solution.py:63
  8.2 2.5 %collective-permute-done = bf16[16,4096]{1,0:T(8,128)(2,1)S(1)} collective-permute-done((bf16[16,4096]{1,0:T(8,128)(2,1)S(1)}, bf16[16,4096]{1,0:T(8,128)(2,1)S(1)}, u32[]{:S(2)}, u32[]{:S(2)}) %collective-permute-start) | collective-permute-done | bytes 131104 | tf_op jit(solution)/shard_map/ppermute | solution.py:63
  10.6 7.3 %collective-permute-done.1 = bf16[16,4096]{1,0:T(8,128)(2,1)S(1)} collective-permute-done((bf16[16,4096]{1,0:T(8,128)(2,1)S(1)}, bf16[16,4096]{1,0:T(8,128)(2,1)S(1)}, u32[]{:S(2)}, u32[]{:S(2)}) %collective-permute-start.1) | collective-permute-done | bytes 131104 | tf_op jit(solution)/shard_map/ppermute | solution.py:63
  18.0 1.6 collective-permute-start.7
  19.8 1.3 reduce-window.8
  21.2 1.6 collective-permute-start.3
  22.8 1.0 collective-permute-start.4
  23.8 2.0 collective-permute-start.5
  25.8 5.5 %collective-permute-done.7 = bf16[4,16,4096]{2,1,0:T(8,128)(2,1)S(1)} collective-permute-done((bf16[4,16,4096]{2,1,0:T(8,128)(2,1)S(1)}, bf16[4,16,4096]{2,1,0:T(8,128)(2,1)S(1)}, u32[]{:S(2)}, u32[]{:S(2)}) %collective-permute-start.7) | collective-permute-done | bytes 524320 | tf_op jit(solution)/shard_map/ppermute | solution.py:63
  31.5 3.3 %collective-permute-done.4 = bf16[16,4096]{1,0:T(8,128)(2,1)S(1)} collective-permute-done((bf16[16,4096]{1,0:T(8,128)(2,1)S(1)}, bf16[16,4096]{1,0:T(8,128)(2,1)S(1)}, u32[]{:S(2)}, u32[]{:S(2)}) %collective-permute-start.4) | collective-permute-done | bytes 131104 | tf_op jit(solution)/shard_map/ppermute | solution.py:63
  35.6 10.3 %collective-permute-done.6 = bf16[4,16,4096]{2,1,0:T(8,128)(2,1)S(1)} collective-permute-done((bf16[4,16,4096]{2,1,0:T(8,128)(2,1)S(1)}, bf16[4,16,4096]{2,1,0:T(8,128)(2,1)S(1)}, u32[]{:S(2)}, u32[]{:S(2)}) %collective-permute-start.6) | collective-permute-done | bytes 524320 | tf_op jit(solution)/shard_map/ppermute | solution.py:63
  46.0 1.1 pad_maximum_fusion
  47.1 14.6 %shard_map.103.rest_0_ = f32[2,256,1792]{2,1,0:T(8,128)S(1)} custom-call(bf16[128,4096]{1,0:T(8,128)(2,1)S(1)} %bitcast.97, bf16[128,4096]{1,0:T(8,128)(2,1)S(1)} %collective-permute-done.8.far, bf16[2,8192,1792]{2,1,0:T(8,128)(2,1)} %w.13), custom_call_target="tpu_custom_call" | custom-call | flops 7516192768 | bytes 29360128 | tf_op jit(solution)/shard_map/pallas_call | solution.py:126
  61.7 1.8 copy-done.1
  66.1 1.1 constant_dynamic-slice_fusion
  69.3 1.2 shard_map.107
  72.0 1.6 collective-permute-start.11
  73.6 2.8 %collective-permute-done.11 = f32[128,128]{1,0:T(8,128)S(1)} collective-permute-done((f32[128,128]{1,0:T(8,128)S(1)}, f32[128,128]{1,0:T(8,128)S(1)}, u32[]{:S(2)}, u32[]{:S(2)}) %collective-permute-start.11) | collective-permute-done | bytes 65568 | tf_op jit(solution)/shard_map/ppermute | solution.py:89
  76.5 1.9 collective-permute-start.12
  78.4 5.4 %shard_map.104.rest_0_ = f32[2,256,1792]{2,1,0:T(8,128)S(1)} custom-call(bf16[128,4096]{1,0:T(8,128)(2,1)} %bitcast.12.near, bf16[128,4096]{1,0:T(8,128)(2,1)} %collective-permute-done.9.far, bf16[2,8192,1792]{2,1,0:T(8,128)(2,1)} %w.13, f32[2,256,1792]{2,1,0:T(8,128)S(1)} %copy-done.2), custom_call_target="tpu_custom_call", output_to_operand_aliasing={{}: (3, {})} | custom-call | flops 2147483648 | bytes 8388608 | tf_op jit(solution)/shard_map/pallas_call | solution.py:126
  83.9 2.0 collective-permute-start.13
  85.9 5.4 %shard_map.105.rest_0_ = f32[2,256,1792]{2,1,0:T(8,128)S(1)} custom-call(bf16[128,4096]{1,0:T(8,128)(2,1)} %bitcast.12.near, bf16[128,4096]{1,0:T(8,128)(2,1)} %collective-permute-done.9.far, bf16[2,8192,1792]{2,1,0:T(8,128)(2,1)} %w.13, f32[2,256,1792]{2,1,0:T(8,128)S(1)} %shard_map.104.rest_0_), custom_call_target="tpu_custom_call", output_to_operand_aliasing={{}: (3, {})} | custom-call | flops 2147483648 | bytes 8388608 | tf_op jit(solution)/shard_map/pallas_call | solution.py:126
  91.6 8.6 %shard_map.106.base = f32[2,256,1792]{2,1,0:T(8,128)S(1)} custom-call(bf16[128,4096]{1,0:T(8,128)(2,1)} %bitcast.12.near, bf16[128,4096]{1,0:T(8,128)(2,1)} %collective-permute-done.9.far, bf16[2,8192,1792]{2,1,0:T(8,128)(2,1)} %w.13, f32[2,256,1792]{2,1,0:T(8,128)S(1)} %shard_map.105.rest_0_), custom_call_target="tpu_custom_call", output_to_operand_aliasing={{}: (3, {})} | custom-call | flops 3221225472 | bytes 12582912 | tf_op jit(solution)/shard_map/pallas_call | solution.py:126
  100.3 7.6 %shard_map.108 = (bf16[256,1792]{1,0:T(8,128)(2,1)S(1)}, bf16[256,1792]{1,0:T(8,128)(2,1)S(1)}, f32[256,128]{1,0:T(8,128)S(1)}) custom-call(s32[8]{0:T(128)S(1)} %bitcast.111, s32[16]{0:T(128)S(1)} %get-tuple-element.20.places, f32[2,256,1792]{2,1,0:T(8,128)S(1)} %shard_map.106.base, bf16[256,1792]{1,0:T(8,128)(2,1)S(1)} %copy-done.15, ...), custom_call_target="tpu_custom_call" | custom-call | flops 1879048192 | bytes 10092544 | tf_op jit(solution)/shard_map/pallas_call | solution.py:228
  110.0 3.8 %collective-permute-done.16 = f32[128,128]{1,0:T(8,128)S(1)} collective-permute-done((f32[128,128]{1,0:T(8,128)S(1)}, f32[128,128]{1,0:T(8,128)S(1)}, u32[]{:S(2)}, u32[]{:S(2)}) %collective-permute-start.16) | collective-permute-done | bytes 65568 | tf_op jit(solution)/shard_map/ppermute | solution.py:89
  113.9 1.8 collective-permute-start.17
  115.7 2.5 %collective-permute-done.17 = f32[128,128]{1,0:T(8,128)S(1)} collective-permute-done((f32[128,128]{1,0:T(8,128)S(1)}, f32[128,128]{1,0:T(8,128)S(1)}, u32[]{:S(2)}, u32[]{:S(2)}) %collective-permute-start.17) | collective-permute-done | bytes 65568 | tf_op jit(solution)/shard_map/ppermute | solution.py:89
  119.0 4.4 %collective-permute-done.18 = f32[128,128]{1,0:T(8,128)S(1)} collective-permute-done((f32[128,128]{1,0:T(8,128)S(1)}, f32[128,128]{1,0:T(8,128)S(1)}, u32[]{:S(2)}, u32[]{:S(2)}) %collective-permute-start.18) | collective-permute-done | bytes 65568 | tf_op jit(solution)/shard_map/ppermute | solution.py:89
  123.6 1.2 collective-permute-done.19
  124.8 1.5 shard_map.109.side
  126.4 11.8 %shard_map.110 = bf16[256,3072]{1,0:T(8,128)(2,1)S(1)} custom-call(s32[1]{0:T(128)} %bitcast.at, bf16[2,8192,1792]{2,1,0:T(8,128)(2,1)} %w.13, bf16[256,1792]{1,0:T(8,128)(2,1)S(1)} %get-tuple-element.13.dgate, bf16[256,1792]{1,0:T(8,128)(2,1)S(1)} %get-tuple-element.14.dup, f32[512,256]{1,0:T(8,128)S(1)} %shard_map.109.side), custom_call_target="tpu_custom_call" | custom-call | flops 5637144576 | bytes 22020096 | tf_op jit(solution)/shard_map/pallas_call | solution.py:391
  139.9 5.0 %shard_map.114.rest_0_ = f32[24,128,1792]{2,1,0:T(8,128)} custom-call(bf16[256,1792]{1,0:T(8,128)(2,1)S(1)} %copy-done.4, bf16[256,1792]{1,0:T(8,128)(2,1)S(1)} %copy-done.6, bf16[256,256]{1,0:T(8,128)(2,1)S(1)} %fusion.7.order, bf16[256,128]{1,0:T(8,128)(2,1)S(1)} %bitcast.100, s32[1,256]{1,0:T(1,128)S(1)} %bitcast.105), custom_call_target="tpu_custom_call" | custom-call | flops 1207959552 | bytes 9437184 | tf_op jit(solution)/shard_map/pallas_call | solution.py:285
  145.0 1.4 fusion.1
  147.0 11.6 %shard_map.111 = bf16[256,3072]{1,0:T(8,128)(2,1)S(1)} custom-call(s32[1]{0:T(128)} %bitcast.at, bf16[2,8192,1792]{2,1,0:T(8,128)(2,1)} %w.13, bf16[256,1792]{1,0:T(8,128)(2,1)S(1)} %copy-done.4, bf16[256,1792]{1,0:T(8,128)(2,1)S(1)} %copy-done.6, f32[512,256]{1,0:T(8,128)S(1)} %copy-done.8), custom_call_target="tpu_custom_call" | custom-call | flops 5637144576 | bytes 22020096 | tf_op jit(solution)/shard_map/pallas_call | solution.py:391
  158.9 1.8 collective-permute-start.22
  161.7 1.4 collective-permute-start.24
  163.1 6.1 %shard_map.115 = f32[24,128,1792]{2,1,0:T(8,128)} custom-call(bf16[256,1792]{1,0:T(8,128)(2,1)S(1)} %copy-done.4, bf16[256,1792]{1,0:T(8,128)(2,1)S(1)} %copy-done.6, bf16[256,256]{1,0:T(8,128)(2,1)S(1)} %fusion.7.order, bf16[256,128]{1,0:T(8,128)(2,1)S(1)} %bitcast.101, s32[1,256]{1,0:T(1,128)S(1)} %bitcast.106, ...), custom_call_target="tpu_custom_call", output_to_operand_aliasing={{}: (5, {})} | custom-call | flops 1610612736 | bytes 12582912 | tf_op jit(solution)/shard_map/pallas_call | solution.py:285
  169.2 5.3 %shard_map.113 = f32[24,512,128]{2,1,0:T(8,128)} custom-call(bf16[256,512]{1,0:T(8,128)(2,1)S(1)} %maximum_select_fusion.columns, bf16[256,256]{1,0:T(8,128)(2,1)S(1)} %fusion.7.order, bf16[256,128]{1,0:T(8,128)(2,1)S(1)} %bitcast.103, s32[256,1]{1,0:T(8,128)S(1)} %copy.20.adapter), custom_call_target="tpu_custom_call" | custom-call | flops 805306368 | bytes 6291456 | tf_op jit(solution)/shard_map/pallas_call | solution.py:315
  174.8 1.6 collective-permute-start.26
  176.4 8.1 %shard_map.112 = bf16[256,2048]{1,0:T(8,128)(2,1)S(1)} custom-call(s32[1]{0:T(128)} %bitcast.at, bf16[2,8192,1792]{2,1,0:T(8,128)(2,1)} %w.13, bf16[256,1792]{1,0:T(8,128)(2,1)S(1)} %copy-done.4, bf16[256,1792]{1,0:T(8,128)(2,1)S(1)} %copy-done.6, f32[512,256]{1,0:T(8,128)S(1)} %copy-done.8), custom_call_target="tpu_custom_call" | custom-call | flops 3758096384 | bytes 14680064 | tf_op jit(solution)/shard_map/pallas_call | solution.py:391
  184.7 1.1 collective-permute-done.26
  188.1 1.9 collective-permute-start.28
  190.0 2.1 %collective-permute-start.29 = (bf16[16,3072]{1,0:T(8,128)(2,1)S(1)}, bf16[16,3072]{1,0:T(8,128)(2,1)S(1)}, u32[]{:S(2)}, u32[]{:S(2)}) collective-permute-start(bf16[16,3072]{1,0:T(8,128)(2,1)S(1)} %get-tuple-element.36), channel_id=1, source_target_pairs={{0,12},{1,13},{2,14},{3,15},{4,0},{5,1},{6,2},{7,3},{8,4},{9,5},{1... | collective-permute-start | bytes 294920 | tf_op jit(solution)/shard_map/ppermute | solution.py:63
  192.1 3.1 %collective-permute-done.31 = bf16[4,16,2048]{2,1,0:T(8,128)(2,1)S(1)} collective-permute-done((bf16[4,16,2048]{2,1,0:T(8,128)(2,1)S(1)}, bf16[4,16,2048]{2,1,0:T(8,128)(2,1)S(1)}, u32[]{:S(2)}, u32[]{:S(2)}) %collective-permute-start.31) | collective-permute-done | bytes 262176 | tf_op jit(solution)/shard_map/ppermute | solution.py:63
  195.9 1.9 collective-permute-start.33
  197.9 2.1 %collective-permute-start.34 = (bf16[16,2048]{1,0:T(8,128)(2,1)S(1)}, bf16[16,2048]{1,0:T(8,128)(2,1)S(1)}, u32[]{:S(2)}, u32[]{:S(2)}) collective-permute-start(bf16[16,2048]{1,0:T(8,128)(2,1)S(1)} %get-tuple-element.39), channel_id=1, source_target_pairs={{0,12},{1,13},{2,14},{3,15},{4,0},{5,1},{6,2},{7,3},{8,4},{9,5},{1... | collective-permute-start | bytes 196616 | tf_op jit(solution)/shard_map/ppermute | solution.py:63
  200.0 1.9 collective-permute-done.32
  201.9 2.5 %collective-permute-done.33 = bf16[16,2048]{1,0:T(8,128)(2,1)S(1)} collective-permute-done((bf16[16,2048]{1,0:T(8,128)(2,1)S(1)}, bf16[16,2048]{1,0:T(8,128)(2,1)S(1)}, u32[]{:S(2)}, u32[]{:S(2)}) %collective-permute-start.33) | collective-permute-done | bytes 65568 | tf_op jit(solution)/shard_map/ppermute | solution.py:63
  (154 shorter events, 20.9 us)
Async XLA Ops:
  1.6 9.0 %collective-permute-start = (bf16[16,4096]{1,0:T(8,128)(2,1)S(1)}, bf16[16,4096]{1,0:T(8,128)(2,1)S(1)}, u32[]{:S(2)}, u32[]{:S(2)}) collective-permute-start(bf16[16,4096]{1,0:T(8,128)(2,1)S(1)} %get-tuple-element.42), channel_id=1, source_target_pairs={{0,12},{1,13},{2,14},{3,15},{4,0},{5,1},{6,2},{7,3},{8,4},{9,5},{1... | collective-permute-start | bytes 393224 | tf_op jit(solution)/shard_map/ppermute | solution.py:63
  6.7 11.2 %collective-permute-start.1 = (bf16[16,4096]{1,0:T(8,128)(2,1)S(1)}, bf16[16,4096]{1,0:T(8,128)(2,1)S(1)}, u32[]{:S(2)}, u32[]{:S(2)}) collective-permute-start(bf16[16,4096]{1,0:T(8,128)(2,1)S(1)} %get-tuple-element.42), channel_id=1, source_target_pairs={{0,8},{1,9},{2,10},{3,11},{4,12},{5,13},{6,14},{7,15},{8,0},{9,1},... | collective-permute-start | bytes 393224 | tf_op jit(solution)/shard_map/ppermute | solution.py:63
  6.7 11.2 %collective-permute-start.2 = (bf16[16,4096]{1,0:T(8,128)(2,1)S(1)}, bf16[16,4096]{1,0:T(8,128)(2,1)S(1)}, u32[]{:S(2)}, u32[]{:S(2)}) collective-permute-start(bf16[16,4096]{1,0:T(8,128)(2,1)S(1)} %get-tuple-element.42), channel_id=1, source_target_pairs={{0,4},{1,5},{2,6},{3,7},{4,8},{5,9},{6,10},{7,11},{8,12},{9,13},{1... | collective-permute-start | bytes 393224 | tf_op jit(solution)/shard_map/ppermute | solution.py:63
  18.0 13.2 %collective-permute-start.7 = (bf16[4,16,4096]{2,1,0:T(8,128)(2,1)S(1)}, bf16[4,16,4096]{2,1,0:T(8,128)(2,1)S(1)}, u32[]{:S(2)}, u32[]{:S(2)}) collective-permute-start(bf16[4,16,4096]{2,1,0:T(8,128)(2,1)S(1)} %get-tuple-element.29), channel_id=1, source_target_pairs={{0,2},{1,3},{2,0},{3,1},{4,6},{5,7},{6,4},{7,5},{8,10},{9,11},{10,... | collective-permute-start | bytes 1572872 | tf_op jit(solution)/shard_map/ppermute | solution.py:63
  21.2 10.3 %collective-permute-start.3 = (bf16[16,4096]{1,0:T(8,128)(2,1)S(1)}, bf16[16,4096]{1,0:T(8,128)(2,1)S(1)}, u32[]{:S(2)}, u32[]{:S(2)}) collective-permute-start(bf16[16,4096]{1,0:T(8,128)(2,1)S(1)} %get-tuple-element.11), channel_id=1, source_target_pairs={{0,12},{1,13},{2,14},{3,15},{4,0},{5,1},{6,2},{7,3},{8,4},{9,5},{1... | collective-permute-start | bytes 393224 | tf_op jit(solution)/shard_map/ppermute | solution.py:63
  22.8 12.1 %collective-permute-start.4 = (bf16[16,4096]{1,0:T(8,128)(2,1)S(1)}, bf16[16,4096]{1,0:T(8,128)(2,1)S(1)}, u32[]{:S(2)}, u32[]{:S(2)}) collective-permute-start(bf16[16,4096]{1,0:T(8,128)(2,1)S(1)} %get-tuple-element.11), channel_id=1, source_target_pairs={{0,8},{1,9},{2,10},{3,11},{4,12},{5,13},{6,14},{7,15},{8,0},{9,1},... | collective-permute-start | bytes 393224 | tf_op jit(solution)/shard_map/ppermute | solution.py:63
  23.8 11.0 %collective-permute-start.5 = (bf16[16,4096]{1,0:T(8,128)(2,1)S(1)}, bf16[16,4096]{1,0:T(8,128)(2,1)S(1)}, u32[]{:S(2)}, u32[]{:S(2)}) collective-permute-start(bf16[16,4096]{1,0:T(8,128)(2,1)S(1)} %get-tuple-element.11), channel_id=1, source_target_pairs={{0,4},{1,5},{2,6},{3,7},{4,8},{5,9},{6,10},{7,11},{8,12},{9,13},{1... | collective-permute-start | bytes 393224 | tf_op jit(solution)/shard_map/ppermute | solution.py:63
  31.4 30.3 %copy-start.9 = (bf16[2,4,16,4096]{3,2,1,0:T(8,128)(2,1)}, bf16[2,4,16,4096]{3,2,1,0:T(8,128)(2,1)S(1)}, u32[]{:S(2)}) copy-start(bf16[2,4,16,4096]{3,2,1,0:T(8,128)(2,1)S(1)} %pad_maximum_fusion.1) | copy-start | bytes 3145732
  31.4 15.7 %collective-permute-start.8 = (bf16[128,4096]{1,0:T(8,128)(2,1)S(1)}, bf16[128,4096]{1,0:T(8,128)(2,1)S(1)}, u32[]{:S(2)}, u32[]{:S(2)}) collective-permute-start(bf16[128,4096]{1,0:T(8,128)(2,1)S(1)} %bitcast.96), channel_id=1, source_target_pairs={{0,1},{1,0},{2,3},{3,2},{4,5},{5,4},{6,7},{7,6},{8,9},{9,8},{10,11... | collective-permute-start | bytes 3145736 | tf_op jit(solution)/shard_map/ppermute | solution.py:63
  34.9 11.1 %collective-permute-start.6 = (bf16[4,16,4096]{2,1,0:T(8,128)(2,1)S(1)}, bf16[4,16,4096]{2,1,0:T(8,128)(2,1)S(1)}, u32[]{:S(2)}, u32[]{:S(2)}) collective-permute-start(bf16[4,16,4096]{2,1,0:T(8,128)(2,1)S(1)} %get-tuple-element.31), channel_id=1, source_target_pairs={{0,2},{1,3},{2,0},{3,1},{4,6},{5,7},{6,4},{7,5},{8,10},{9,11},{10,... | collective-permute-start | bytes 1572872 | tf_op jit(solution)/shard_map/ppermute | solution.py:63
  47.0 16.5 %copy-start.19 = (s32[8,1]{0,1:T(1,128)S(1)}, s32[8,1]{0,1:T(1,128)}, u32[]{:S(2)}) copy-start(s32[8,1]{0,1:T(1,128)} %reduce-window.8) | copy-start | bytes 100
  47.0 17.6 %copy-start.18 = (s32[1,8]{1,0:T(1,128)S(1)}, s32[1,8]{1,0:T(1,128)}, u32[]{:S(2)}) copy-start(s32[1,8]{1,0:T(1,128)} %param.13) | copy-start | bytes 100
  47.0 17.7 %copy-start.20 = (s32[24]{0:T(128)S(1)}, s32[24]{0:T(128)}, u32[]{:S(2)}) copy-start(s32[24]{0:T(128)} %param.15) | copy-start | bytes 292
  47.0 14.6 %copy-start.10 = (bf16[128,4096]{1,0:T(8,128)(2,1)}, bf16[128,4096]{1,0:T(8,128)(2,1)S(1)}, u32[]{:S(2)}) copy-start(bf16[128,4096]{1,0:T(8,128)(2,1)S(1)} %collective-permute-done.8.far) | copy-start | bytes 3145732
  47.1 21.3 %copy-start = (bf16[24,512,128]{2,1,0:T(8,128)(2,1)S(1)}, bf16[24,512,128]{2,1,0:T(8,128)(2,1)}, u32[]{:S(2)}) copy-start(bf16[24,512,128]{2,1,0:T(8,128)(2,1)} %rest_7_.5) | copy-start | bytes 9437188
  63.5 3.7 %collective-permute-start.9 = (bf16[128,4096]{1,0:T(8,128)(2,1)}, bf16[128,4096]{1,0:T(8,128)(2,1)}, u32[]{:S(2)}, u32[]{:S(2)}) collective-permute-start(bf16[128,4096]{1,0:T(8,128)(2,1)} %bitcast.12.near), channel_id=1, source_target_pairs={{0,1},{1,0},{2,3},{3,2},{4,5},{5,4},{6,7},{7,6},{8,9},{9,8},{10,11... | collective-permute-start | bytes 3145736 | tf_op jit(solution)/shard_map/ppermute | solution.py:63
  69.3 9.1 %copy-start.2 = (f32[2,256,1792]{2,1,0:T(8,128)S(1)}, f32[2,256,1792]{2,1,0:T(8,128)}, u32[]{:S(2)}) copy-start(f32[2,256,1792]{2,1,0:T(8,128)} %copy-done.1) | copy-start | bytes 11010052
  70.6 1.5 collective-permute-start.10
  72.0 4.4 %collective-permute-start.11 = (f32[128,128]{1,0:T(8,128)S(1)}, f32[128,128]{1,0:T(8,128)S(1)}, u32[]{:S(2)}, u32[]{:S(2)}) collective-permute-start(f32[128,128]{1,0:T(8,128)S(1)} %slice_add_fusion), channel_id=1, source_target_pairs={{0,2},{1,3},{2,0},{3,1},{4,6},{5,7},{6,4},{7,5},{8,10},{9,11},{10,... | collective-permute-start | bytes 196616 | tf_op jit(solution)/shard_map/ppermute | solution.py:89
  76.5 7.4 %collective-permute-start.12 = (f32[128,128]{1,0:T(8,128)S(1)}, f32[128,128]{1,0:T(8,128)S(1)}, u32[]{:S(2)}, u32[]{:S(2)}) collective-permute-start(f32[128,128]{1,0:T(8,128)S(1)} %add.307), channel_id=1, source_target_pairs={{0,4},{1,5},{2,6},{3,7},{4,0},{5,1},{6,2},{7,3},{8,12},{9,13},{10,... | collective-permute-start | bytes 196616 | tf_op jit(solution)/shard_map/ppermute | solution.py:89
  83.9 7.4 %collective-permute-start.13 = (f32[128,128]{1,0:T(8,128)S(1)}, f32[128,128]{1,0:T(8,128)S(1)}, u32[]{:S(2)}, u32[]{:S(2)}) collective-permute-start(f32[128,128]{1,0:T(8,128)S(1)} %add.308), channel_id=1, source_target_pairs={{0,8},{1,9},{2,10},{3,11},{4,12},{5,13},{6,14},{7,15},{8,0},{9,1},... | collective-permute-start | bytes 196616 | tf_op jit(solution)/shard_map/ppermute | solution.py:89
  91.3 8.9 %slice-start = ((s8[11010048]{0:T(1024)(128)(4,1)}), s8[4194304]{0:T(1024)(128)(4,1)S(1)}, s32[]{:S(2)}) async-start(s8[11010048]{0:T(1024)(128)(4,1)} %bitcast.94), calls=%async_computation | async-start | bytes 8388608
  91.4 8.8 %slice-start.1 = ((s8[11010048]{0:T(1024)(128)(4,1)}), s8[4194304]{0:T(1024)(128)(4,1)S(1)}, s32[]{:S(2)}) async-start(s8[11010048]{0:T(1024)(128)(4,1)} %bitcast.94), calls=%async_computation.1 | async-start | bytes 8388608
  91.5 8.8 %slice-start.2 = ((s8[11010048]{0:T(1024)(128)(4,1)}), s8[2621440]{0:T(1024)(128)(4,1)S(1)}, s32[]{:S(2)}) async-start(s8[11010048]{0:T(1024)(128)(4,1)} %bitcast.94), calls=%async_computation.2 | async-start | bytes 5242880
  91.5 8.7 %collective-permute-start.14 = (bf16[128,128]{1,0:T(8,128)(2,1)S(1)}, bf16[128,128]{1,0:T(8,128)(2,1)S(1)}, u32[]{:S(2)}, u32[]{:S(2)}) collective-permute-start(bf16[128,128]{1,0:T(8,128)(2,1)S(1)} %fusion.17), channel_id=1, source_target_pairs={{0,1},{1,0},{2,3},{3,2},{4,5},{5,4},{6,7},{7,6},{8,9},{9,8},{10,11... | collective-permute-start | bytes 98312 | tf_op jit(solution)/shard_map/ppermute | solution.py:63
  107.9 18.5 %copy-start.3 = (bf16[256,1792]{1,0:T(8,128)(2,1)}, bf16[256,1792]{1,0:T(8,128)(2,1)S(1)}, u32[]{:S(2)}) copy-start(bf16[256,1792]{1,0:T(8,128)(2,1)S(1)} %get-tuple-element.13.dgate) | copy-start | bytes 2752516
  107.9 18.5 %copy-start.5 = (bf16[256,1792]{1,0:T(8,128)(2,1)}, bf16[256,1792]{1,0:T(8,128)(2,1)S(1)}, u32[]{:S(2)}) copy-start(bf16[256,1792]{1,0:T(8,128)(2,1)S(1)} %get-tuple-element.14.dup) | copy-start | bytes 2752516
  107.9 1.5 collective-permute-start.15
  109.4 4.4 %collective-permute-start.16 = (f32[128,128]{1,0:T(8,128)S(1)}, f32[128,128]{1,0:T(8,128)S(1)}, u32[]{:S(2)}, u32[]{:S(2)}) collective-permute-start(f32[128,128]{1,0:T(8,128)S(1)} %slice_add_fusion.1), channel_id=1, source_target_pairs={{0,2},{1,3},{2,0},{3,1},{4,6},{5,7},{6,4},{7,5},{8,10},{9,11},{10,... | collective-permute-start | bytes 196616 | tf_op jit(solution)/shard_map/ppermute | solution.py:89
  113.9 4.3 %collective-permute-start.17 = (f32[128,128]{1,0:T(8,128)S(1)}, f32[128,128]{1,0:T(8,128)S(1)}, u32[]{:S(2)}, u32[]{:S(2)}) collective-permute-start(f32[128,128]{1,0:T(8,128)S(1)} %add.318), channel_id=1, source_target_pairs={{0,4},{1,5},{2,6},{3,7},{4,0},{5,1},{6,2},{7,3},{8,12},{9,13},{10,... | collective-permute-start | bytes 196616 | tf_op jit(solution)/shard_map/ppermute | solution.py:89
  118.2 5.2 %collective-permute-start.18 = (f32[128,128]{1,0:T(8,128)S(1)}, f32[128,128]{1,0:T(8,128)S(1)}, u32[]{:S(2)}, u32[]{:S(2)}) collective-permute-start(f32[128,128]{1,0:T(8,128)S(1)} %add.319), channel_id=1, source_target_pairs={{0,8},{1,9},{2,10},{3,11},{4,12},{5,13},{6,14},{7,15},{8,0},{9,1},... | collective-permute-start | bytes 196616 | tf_op jit(solution)/shard_map/ppermute | solution.py:89
  123.5 1.3 collective-permute-start.19
  126.4 11.8 %copy-start.7 = (f32[512,256]{1,0:T(8,128)}, f32[512,256]{1,0:T(8,128)S(1)}, u32[]{:S(2)}) copy-start(f32[512,256]{1,0:T(8,128)S(1)} %shard_map.109.side) | copy-start | bytes 1572868
  139.2 5.7 %collective-permute-start.20 = (bf16[2,4,16,3072]{3,2,1,0:T(8,128)(2,1)}, bf16[2,4,16,3072]{3,2,1,0:T(8,128)(2,1)}, u32[]{:S(2)}, u32[]{:S(2)}) collective-permute-start(bf16[2,4,16,3072]{3,2,1,0:T(8,128)(2,1)} %bitcast.27), channel_id=1, source_target_pairs={{0,1},{1,0},{2,3},{3,2},{4,5},{5,4},{6,7},{7,6},{8,9},{9,8},{10,11... | collective-permute-start | bytes 2359304 | tf_op jit(solution)/shard_map/ppermute | solution.py:63
  146.4 12.4 %collective-permute-start.21 = (bf16[4,16,3072]{2,1,0:T(8,128)(2,1)S(1)}, bf16[4,16,3072]{2,1,0:T(8,128)(2,1)S(1)}, u32[]{:S(2)}, u32[]{:S(2)}) collective-permute-start(bf16[4,16,3072]{2,1,0:T(8,128)(2,1)S(1)} %slice_bitcast_fusion.2), channel_id=1, source_target_pairs={{0,2},{1,3},{2,0},{3,1},{4,6},{5,7},{6,4},{7,5},{8,10},{9,11},{10,... | collective-permute-start | bytes 1179656 | tf_op jit(solution)/shard_map/ppermute | solution.py:63
  158.7 15.9 %collective-permute-start.25 = (bf16[2,4,16,3072]{3,2,1,0:T(8,128)(2,1)S(1)}, bf16[2,4,16,3072]{3,2,1,0:T(8,128)(2,1)S(1)}, u32[]{:S(2)}, u32[]{:S(2)}) collective-permute-start(bf16[2,4,16,3072]{3,2,1,0:T(8,128)(2,1)S(1)} %bitcast.117), channel_id=1, source_target_pairs={{0,1},{1,0},{2,3},{3,2},{4,5},{5,4},{6,7},{7,6},{8,9},{9,8},{10,11... | collective-permute-start | bytes 2359304 | tf_op jit(solution)/shard_map/ppermute | solution.py:63
  158.9 15.6 %collective-permute-start.22 = (bf16[16,3072]{1,0:T(8,128)(2,1)S(1)}, bf16[16,3072]{1,0:T(8,128)(2,1)S(1)}, u32[]{:S(2)}, u32[]{:S(2)}) collective-permute-start(bf16[16,3072]{1,0:T(8,128)(2,1)S(1)} %get-tuple-element.32), channel_id=1, source_target_pairs={{0,4},{1,5},{2,6},{3,7},{4,8},{5,9},{6,10},{7,11},{8,12},{9,13},{1... | collective-permute-start | bytes 294920 | tf_op jit(solution)/shard_map/ppermute | solution.py:63
  160.7 13.8 %collective-permute-start.23 = (bf16[16,3072]{1,0:T(8,128)(2,1)S(1)}, bf16[16,3072]{1,0:T(8,128)(2,1)S(1)}, u32[]{:S(2)}, u32[]{:S(2)}) collective-permute-start(bf16[16,3072]{1,0:T(8,128)(2,1)S(1)} %get-tuple-element.34), channel_id=1, source_target_pairs={{0,8},{1,9},{2,10},{3,11},{4,12},{5,13},{6,14},{7,15},{8,0},{9,1},... | collective-permute-start | bytes 294920 | tf_op jit(solution)/shard_map/ppermute | solution.py:63
  161.7 12.8 %collective-permute-start.24 = (bf16[16,3072]{1,0:T(8,128)(2,1)S(1)}, bf16[16,3072]{1,0:T(8,128)(2,1)S(1)}, u32[]{:S(2)}, u32[]{:S(2)}) collective-permute-start(bf16[16,3072]{1,0:T(8,128)(2,1)S(1)} %get-tuple-element.33), channel_id=1, source_target_pairs={{0,12},{1,13},{2,14},{3,15},{4,0},{5,1},{6,2},{7,3},{8,4},{9,5},{1... | collective-permute-start | bytes 294920 | tf_op jit(solution)/shard_map/ppermute | solution.py:63
  174.8 11.0 %collective-permute-start.26 = (bf16[4,16,3072]{2,1,0:T(8,128)(2,1)S(1)}, bf16[4,16,3072]{2,1,0:T(8,128)(2,1)S(1)}, u32[]{:S(2)}, u32[]{:S(2)}) collective-permute-start(bf16[4,16,3072]{2,1,0:T(8,128)(2,1)S(1)} %slice_bitcast_fusion), channel_id=1, source_target_pairs={{0,2},{1,3},{2,0},{3,1},{4,6},{5,7},{6,4},{7,5},{8,10},{9,11},{10,... | collective-permute-start | bytes 1179656 | tf_op jit(solution)/shard_map/ppermute | solution.py:63
  184.7 2.0 collective-permute-start.30
  186.8 8.4 %collective-permute-start.31 = (bf16[4,16,2048]{2,1,0:T(8,128)(2,1)S(1)}, bf16[4,16,2048]{2,1,0:T(8,128)(2,1)S(1)}, u32[]{:S(2)}, u32[]{:S(2)}) collective-permute-start(bf16[4,16,2048]{2,1,0:T(8,128)(2,1)S(1)} %slice_bitcast_fusion.4), channel_id=1, source_target_pairs={{0,2},{1,3},{2,0},{3,1},{4,6},{5,7},{6,4},{7,5},{8,10},{9,11},{10,... | collective-permute-start | bytes 786440 | tf_op jit(solution)/shard_map/ppermute | solution.py:63
  187.7 10.2 %collective-permute-start.27 = (bf16[16,3072]{1,0:T(8,128)(2,1)S(1)}, bf16[16,3072]{1,0:T(8,128)(2,1)S(1)}, u32[]{:S(2)}, u32[]{:S(2)}) collective-permute-start(bf16[16,3072]{1,0:T(8,128)(2,1)S(1)} %get-tuple-element.35), channel_id=1, source_target_pairs={{0,4},{1,5},{2,6},{3,7},{4,8},{5,9},{6,10},{7,11},{8,12},{9,13},{1... | collective-permute-start | bytes 294920 | tf_op jit(solution)/shard_map/ppermute | solution.py:63
  188.1 11.9 %collective-permute-start.28 = (bf16[16,3072]{1,0:T(8,128)(2,1)S(1)}, bf16[16,3072]{1,0:T(8,128)(2,1)S(1)}, u32[]{:S(2)}, u32[]{:S(2)}) collective-permute-start(bf16[16,3072]{1,0:T(8,128)(2,1)S(1)} %get-tuple-element.37), channel_id=1, source_target_pairs={{0,8},{1,9},{2,10},{3,11},{4,12},{5,13},{6,14},{7,15},{8,0},{9,1},... | collective-permute-start | bytes 294920 | tf_op jit(solution)/shard_map/ppermute | solution.py:63
  190.0 10.0 %collective-permute-start.29 = (bf16[16,3072]{1,0:T(8,128)(2,1)S(1)}, bf16[16,3072]{1,0:T(8,128)(2,1)S(1)}, u32[]{:S(2)}, u32[]{:S(2)}) collective-permute-start(bf16[16,3072]{1,0:T(8,128)(2,1)S(1)} %get-tuple-element.36), channel_id=1, source_target_pairs={{0,12},{1,13},{2,14},{3,15},{4,0},{5,1},{6,2},{7,3},{8,4},{9,5},{1... | collective-permute-start | bytes 294920 | tf_op jit(solution)/shard_map/ppermute | solution.py:63
  195.3 6.6 %collective-permute-start.32 = (bf16[16,2048]{1,0:T(8,128)(2,1)S(1)}, bf16[16,2048]{1,0:T(8,128)(2,1)S(1)}, u32[]{:S(2)}, u32[]{:S(2)}) collective-permute-start(bf16[16,2048]{1,0:T(8,128)(2,1)S(1)} %get-tuple-element.38), channel_id=1, source_target_pairs={{0,4},{1,5},{2,6},{3,7},{4,8},{5,9},{6,10},{7,11},{8,12},{9,13},{1... | collective-permute-start | bytes 196616 | tf_op jit(solution)/shard_map/ppermute | solution.py:63
  195.9 8.5 %collective-permute-start.33 = (bf16[16,2048]{1,0:T(8,128)(2,1)S(1)}, bf16[16,2048]{1,0:T(8,128)(2,1)S(1)}, u32[]{:S(2)}, u32[]{:S(2)}) collective-permute-start(bf16[16,2048]{1,0:T(8,128)(2,1)S(1)} %get-tuple-element.40), channel_id=1, source_target_pairs={{0,8},{1,9},{2,10},{3,11},{4,12},{5,13},{6,14},{7,15},{8,0},{9,1},... | collective-permute-start | bytes 196616 | tf_op jit(solution)/shard_map/ppermute | solution.py:63
  197.9 6.6 %collective-permute-start.34 = (bf16[16,2048]{1,0:T(8,128)(2,1)S(1)}, bf16[16,2048]{1,0:T(8,128)(2,1)S(1)}, u32[]{:S(2)}, u32[]{:S(2)}) collective-permute-start(bf16[16,2048]{1,0:T(8,128)(2,1)S(1)} %get-tuple-element.39), channel_id=1, source_target_pairs={{0,12},{1,13},{2,14},{3,15},{4,0},{5,1},{6,2},{7,3},{8,4},{9,5},{1... | collective-permute-start | bytes 196616 | tf_op jit(solution)/shard_map/ppermute | solution.py:63
  (11 other events, 43.9 us)

commit v2 on v1

--- a/solution.py
+++ b/solution.py
@@ -79,15 +79,17 @@
         zs = lax.broadcasted_iota(jnp.int32, (c, b, a), 2)
         return (((outer + zs) % a * b + (inner + bs) % b) * c + (core + cs) % c).reshape(-1)
 
-    def exchange_sum(self, x, dim):
-        k = 1
-        while k < self.dims[dim]:
-            pairs = [
-                (i, i + ((i // self.strides[dim] ^ k) - i // self.strides[dim]) * self.strides[dim])
-                for i in range(self.size)
-            ]
-            x = x + lax.ppermute(x, "tensor", pairs)
-            k *= 2
+    def exchange_sum(self, x, dims, beside):
+        beside = list(beside)
+        for dim in dims:
+            k = 1
+            while k < self.dims[dim]:
+                stride = self.strides[dim]
+                pairs = [(i, i + ((i // stride ^ k) - i // stride) * stride) for i in range(self.size)]
+                x = x + lax.ppermute(x, "tensor", pairs)
+                if beside:
+                    x = after(x, beside.pop(0))
+                k *= 2
         return x
 
     def slots_of(self, index):
@@ -99,26 +101,29 @@
         return (((cs - core) % c * b + (bs - inner) % b) * a + (zs - outer) % a).reshape(-1)
 
 
-def forward_kernel(near, far, w, *rest):
+def forward_kernel(near, far, *rest):
     out = rest[-1]
     x = jnp.concatenate([near[...], far[...]], axis=0)
+    depth = x.shape[1] // 2
     for i in range(2):
-        part = dot(x, w[i])
-        out[i] = part if len(rest) == 1 else rest[0][i] + part
+        part = dot(x[:, :depth], rest[2 * i][0]) + dot(x[:, depth:], rest[2 * i + 1][0])
+        out[i] = part if len(rest) == 5 else rest[4][i] + part
 
 
 def forward_chunk(near, far, frozen, start, first, tiles):
     half, step = near.shape
     hidden = frozen.shape[2]
     tile = tile_of(hidden, 256)
+    depth = step // 2
     low, high = tiles
     across = pl.BlockSpec((2, 2 * half, tile), lambda n: (0, 0, low + n))
-    operands = [near, far, frozen]
-    specs = [
-        pl.BlockSpec((half, step), lambda n: (0, 0)),
-        pl.BlockSpec((half, step), lambda n: (0, 0)),
-        pl.BlockSpec((2, step, tile), lambda n: (0, first // step, low + n)),
-    ]
+
+    def weight(i, h):
+        return pl.BlockSpec((1, depth, tile), lambda n: (i, first // depth + h, low + n))
+
+    operands = [near, far] + [frozen] * 4
+    specs = [pl.BlockSpec((half, step), lambda n: (0, 0))] * 2
+    specs += [weight(i, h) for i in range(2) for h in range(2)]
     if start is not None:
         operands.append(start)
         specs.append(across)
@@ -129,17 +134,26 @@
         in_specs=specs,
         out_specs=across,
         out_shape=jax.ShapeDtypeStruct((2, 2 * half, hidden), F32),
-        input_output_aliases={} if start is None else {3: 0},
+        input_output_aliases={} if start is None else {6: 0},
         compiler_params=params(32),
         cost_estimate=cost(8 * half * step * tile * count, 4 * step * tile * count),
     )(*operands)
 
 
-def low_in_kernel(segments, rows, adapters, places, columns, seg, *rest):
-    out = rest[-1]
-    total = jnp.zeros((columns.shape[0], out.shape[1]), F32)
+def low_in_kernel(segments, rows, adapters, places, which, seg, *rest):
+    factors, rest = rest[:segments], rest[segments:]
+    pairs, (columns, out) = rest[:-2], rest[-2:]
+    half = columns.shape[0] // 2
+    for q in range(len(pairs) // 2):
+
+        @pl.when(which[0] == q)
+        def _():
+            columns[:half] = pairs[2 * q][...]
+            columns[half:] = pairs[2 * q + 1][...]
+
+    total = jnp.zeros(out.shape, F32)
     for s in range(segments):
-        part = dot(columns[...], rest[s][0])
+        part = dot(columns[...], factors[s][0])
         total = total + jnp.where(seg[...] == s, part, 0.0)
     put_rows(out, total, places, rows)
 
@@ -156,23 +170,40 @@
     return pl.BlockSpec((1,) + shape[1:], lambda *a: (a[-2][s], 0, 0))
 
 
-def low_in_partial(columns, seg, down, adapters, places, rows):
+def low_in_partial(pairs, seg, down, adapters, places, index, rows):
     segments = adapters.shape[0]
-    tokens = columns.shape[0]
+    shard, wide = down.shape[1:]
+    half, step = pairs[0][0].shape
+    per = step // shard
+    if shard % 128:
+        joined = [jnp.concatenate(side, axis=1) for side in zip(*pairs)]
+        pairs = [[lax.dynamic_slice_in_dim(v, index * shard, shard, 1) for v in joined]]
+        which = jnp.zeros((1,), jnp.int32)
+        cuts = [pl.BlockSpec((half, shard), lambda *a: (0, 0))] * 2
+    else:
+        which = jnp.stack(
+            [index // per] + [jnp.clip(index - q * per, 0, per - 1) for q in range(len(pairs))]
+        ).astype(jnp.int32)
+        cuts = []
+        for q in range(len(pairs)):
+            cuts += [pl.BlockSpec((half, shard), lambda i, a, p, w, q=q: (0, w[1 + q]))] * 2
     full = lambda shape: pl.BlockSpec(shape, lambda *a: (0,) * len(shape))
+    factor = lambda s: pl.BlockSpec((1, shard, wide), lambda i, a, p, w: (a[s], 0, 0))
     return pl.pallas_call(
         functools.partial(low_in_kernel, segments, rows),
         grid_spec=pltpu.PrefetchScalarGridSpec(
-            num_scalar_prefetch=2,
+            num_scalar_prefetch=3,
             grid=(1,),
-            in_specs=[full(columns.shape), full(seg.shape)]
-            + [of_segment(down.shape, s) for s in range(segments)],
-            out_specs=full((tokens, down.shape[2])),
+            in_specs=[full(seg.shape)] + [factor(s) for s in range(segments)] + cuts,
+            out_specs=[full((2 * half, shard)), full((2 * half, wide))],
         ),
-        out_shape=jax.ShapeDtypeStruct((tokens, down.shape[2]), F32),
+        out_shape=[
+            jax.ShapeDtypeStruct((2 * half, shard), BF16),
+            jax.ShapeDtypeStruct((2 * half, wide), F32),
+        ],
         compiler_params=params(16),
-        cost_estimate=cost(2 * tokens * down[0].size * segments, 2 * down[0].size * segments),
-    )(adapters, places, columns, seg, *([down] * segments))
+        cost_estimate=cost(4 * half * down[0].size * segments, 2 * down[0].size * segments),
+    )(adapters, places, which, seg, *([down] * segments), *[v for pair in pairs for v in pair])
 
 
 def middle_kernel(segments, rows, adapters, places, base, dhidden, token_order, order, low, seg, *rest):
@@ -354,30 +385,31 @@
     )(adapters, places, order, low, seg_row, *([down] * segments))
 
 
-def backward_kernel(base, at, w, dgate, dup, side, out, total):
+def backward_kernel(base, at, g0, g1, u0, u1, dgate, dup, side, out, total):
     block, tokens = total.shape
     shard = side.shape[0]
-    part = tile_of(block, 256)
+    part = block // 2
     first = at[0] * shard
     own = first // block == base + pl.program_id(0)
 
-    def product(rows):
-        return dot(w[0, rows], dgate[...], ((1,), (1,))) + dot(w[1, rows], dup[...], ((1,), (1,)))
+    def product(h):
+        gate, up = ((g0, u0), (g1, u1))[h]
+        return dot(gate[0], dgate[...], ((1,), (1,))) + dot(up[0], dup[...], ((1,), (1,)))
 
     @pl.when(jnp.logical_not(own))
     def _():
-        for n in range(0, block, part):
-            rows = slice(n, n + part)
-            out[:, rows] = product(rows).T.astype(BF16)
+        for h in range(2):
+            out[:, h * part : (h + 1) * part] = product(h).T.astype(BF16)
 
     @pl.when(own)
     def _():
         if shard == block:
-            for n in range(0, block, part):
-                rows = slice(n, n + part)
-                out[:, rows] = (product(rows) + side[rows]).T.astype(BF16)
+            for h in range(2):
+                rows = slice(h * part, (h + 1) * part)
+                out[:, rows] = (product(h) + side[rows]).T.astype(BF16)
         else:
-            total[...] = product(slice(None))
+            for h in range(2):
+                total[h * part : (h + 1) * part] = product(h)
             here = pl.ds(pl.multiple_of(first % block, shard), shard)
             total[here, :] += side[...]
             out[...] = total[...].T.astype(BF16)
@@ -388,24 +420,24 @@
     block = tile_of(step, 512)
     base = first // block
     full = lambda shape: pl.BlockSpec(shape, lambda *a: (0,) * len(shape))
+
+    def weight(i, h):
+        return pl.BlockSpec((1, block // 2, hidden), lambda k, at: (i, 2 * (base + k) + h, 0))
+
     return pl.pallas_call(
         functools.partial(backward_kernel, base),
         grid_spec=pltpu.PrefetchScalarGridSpec(
             num_scalar_prefetch=1,
             grid=(step // block,),
-            in_specs=[
-                pl.BlockSpec((2, block, hidden), lambda k, at: (0, base + k, 0)),
-                full(dgate.shape),
-                full(dup.shape),
-                full(side.shape),
-            ],
+            in_specs=[weight(i, h) for i in range(2) for h in range(2)]
+            + [full(dgate.shape), full(dup.shape), full(side.shape)],
             out_specs=pl.BlockSpec((tokens, block), lambda k, at: (0, k)),
             scratch_shapes=[pltpu.VMEM((block, tokens), F32)],
         ),
         out_shape=jax.ShapeDtypeStruct((tokens, step), BF16),
         compiler_params=params(32),
         cost_estimate=cost(4 * tokens * step * hidden, 4 * step * hidden),
-    )(at, frozen, dgate, dup, side)
+    )(at, *([frozen] * 4), dgate, dup, side)
 
 
 def local(
@@ -459,7 +491,7 @@
     segment = segment_of(token)
     adapter = adapter_of(segment)
 
-    def whole_sum(partial):
+    def whole_sum(partial, beside=()):
         if rows % 8:
             at = jnp.arange(torus.size, dtype=jnp.int32)
             device = at % chips * c + (core + at // chips) % c
@@ -469,48 +501,47 @@
                 axis=0,
             )
         x = torus.scatter_sum(partial.reshape(c, chips * rows, gate_and_up), 2)
-        x = torus.exchange_sum(torus.exchange_sum(x, 1), 0)
+        x = torus.exchange_sum(x, (1, 0), beside)
         return torus.gather((x * factor).astype(BF16), 2).reshape(tokens, gate_and_up)
 
     hidden = frozen.shape[2]
     tiles = hidden // tile_of(hidden, 256)
     step = width // GATHER_CHUNKS
-    columns = None
     behind = None
     base = None
+    pairs = []
     for q in range(GATHER_CHUNKS):
         x = activations[:, q * step : (q + 1) * step]
         if q:
             x = after(x, behind)
         behind = torus.gather(x, 0)
-        x = torus.gather(behind, 1).reshape(tokens // c, step)
+        parts = [behind] + [torus.move(behind, 1, -k) for k in range(1, b)]
         if q:
-            x = after(x, base)
+            parts = list(lax.optimization_barrier((*parts, base))[:-1])
+        x = jnp.stack(parts).reshape(tokens // c, step)
         y = torus.move(x, 2, -1)
-        first = index * shard_width - q * step
-        at = jnp.clip(first, 0, step - shard_width)
-        cut = jnp.concatenate(
-            [lax.dynamic_slice_in_dim(v, at, shard_width, 1) for v in (x, y)], axis=0
-        )
-        inside = (first >= 0) & (first < step)
-        columns = cut if columns is None else jnp.where(inside, cut, columns)
+        pairs.append((x, y))
         for cut in parts_of(tiles, 3) if q == GATHER_CHUNKS - 1 else [(0, tiles)]:
             base = forward_chunk(x, y, frozen, base, q * step, cut)
 
-    partial_in = low_in_partial(
-        columns, segment[:, None], adapter_down_factors, seg_adapter, places, rows
+    columns, partial_in = low_in_partial(
+        pairs, segment[:, None], adapter_down_factors, seg_adapter, places, index, rows
     )
     low_in = whole_sum(partial_in)
     dgate, dup, partial_out = middle(
         base, dhidden, token_order, order, low_in, segment[:, None], adapter_up_factors,
         seg_adapter, places, rows,
     )
-    low_out = whole_sum(partial_out)
-    grad_b = None
-    for cut in parts_of(tiles, 2):
-        grad_b = grad_b_of(
-            dgate, dup, order, low_in, adapter[None, :], adapter_list, grad_b, cut
+    grad_b = []
+    for cut in parts_of(tiles, 3):
+        grad_b.append(
+            grad_b_of(
+                dgate, dup, order, low_in, adapter[None, :], adapter_list,
+                grad_b[-1] if grad_b else None, cut,
+            )
         )
+    low_out = whole_sum(partial_out, grad_b)
+    grad_b = grad_b[-1]
     side = side_of(order, low_out, segment[None, :], adapter_down_factors, seg_adapter, places)
     blocks = []
     first = 0
@@ -528,7 +559,7 @@
         blocks.append(torus.scatter_sum(inners[q], 0).astype(BF16))
         first += step
     dinput = jnp.concatenate(blocks, axis=1)
-    grad_a = grad_a_of(columns, order, low_out, adapter[:, None], adapter_list)
+    grad_a = grad_a_of(columns, order, after(low_out, term), adapter[:, None], adapter_list)
     return (dinput, grad_a, grad_b)
 
 

time: 206 us -> 221 us (1.073)
  waiting for transfers between devices: 54.9 us -> 63.2 us
  starting transfers between devices: 39.6 us -> 42.5 us
  Pallas kernels: 92.3 us -> 95.1 us
    ppermute x29, waiting for transfers between devices: 41.3 us -> 58.7 us  [move(): return lax.ppermute(x, 'tensor', pairs)]
    ppermute x6, waiting for transfers between devices: 13.6 us -> 4.57 us  [exchange_sum(): x = x + lax.ppermute(x, 'tensor', pairs)]
    unnamed x48 -> x58, local copies, waits for them, and re-layouts: 3.15 us -> 7.81 us
    ppermute x29, starting transfers between devices: 30.9 us -> 34.6 us  [move(): return lax.ppermute(x, 'tensor', pairs)]
    dynamic_slice x3 -> x0, local copies, waits for them, and re-layouts: 3.2 us -> none  [local(): lax.dynamic_slice_in_dim(v, at, shard_width, 1)]
    pallas_call x2 -> x3, Pallas kernels: 11.1 us -> 12.7 us  [grad_b_of(): pl.pallas_call(grad_b_kernel, grid=(last - first,), in_specs=specs, out_s...]
  transfers between devices with their start and end apart: 35 -> 35, of which waited for: 17 -> 20; matrix products, arithmetic and copies ran while one was open for 4% -> 2% of each run, Pallas kernels for 27% -> 24%
where the time goes in v2:
time: 221 us; the launch traced here: 220 us
  Pallas kernels  95.1 us (43%)
  waiting for transfers between devices  63.2 us (29%)
  starting transfers between devices  42.5 us (19%)
  local copies, waits for them, and re-layouts  11.3 us (5%)
  other arithmetic  6.74 us (3%)
    ppermute x29, waiting for transfers between devices, move(): return lax.ppermute(x, 'tensor', pairs)  58.7 us
    ppermute x29, starting transfers between devices, move(): return lax.ppermute(x, 'tensor', pairs)  34.6 us
    pallas_call x4, Pallas kernels, forward_chunk(): pl.pallas_call(forward_kernel, grid=(count,), in_specs=specs, out_specs=a...  34 us
    pallas_call x3, Pallas kernels, backward_chunk(): pl.pallas_call(functools.partial(backward_kernel, base), grid_spec=pltpu....  31.4 us
    pallas_call x3, Pallas kernels, grad_b_of(): pl.pallas_call(grad_b_kernel, grid=(last - first,), in_specs=specs, out_s...  12.7 us
    ppermute x6, starting transfers between devices, exchange_sum(): x = x + lax.ppermute(x, 'tensor', pairs)  7.86 us
    unnamed x58, local copies, waits for them, and re-layouts  7.81 us
    pallas_call x1, Pallas kernels, middle(): pl.pallas_call(functools.partial(middle_kernel, segments, rows), grid_spe...  7.57 us
  transfers between devices with their start and end apart: 35, of which 20 were waited for; matrix products, arithmetic and copies ran while one was open for 2% of the time, Pallas kernels for 24%

profile of v2, /device:TPU:0, one launch (start us, length us, event | category | flops | bytes accessed | tf_op | source)
XLA Modules:
  0.0 220.2 jit_solution(3673978992792675344)
XLA Ops:
  1.6 3.1 %collective-permute-start.2 = (bf16[16,4096]{1,0:T(8,128)(2,1)S(1)}, bf16[16,4096]{1,0:T(8,128)(2,1)S(1)}, u32[]{:S(2)}, u32[]{:S(2)}) collective-permute-start(bf16[16,4096]{1,0:T(8,128)(2,1)S(1)} %get-tuple-element.54), channel_id=1, source_target_pairs={{0,4},{1,5},{2,6},{3,7},{4,8},{5,9},{6,10},{7,11},{8,12},{9,13},{1... | collective-permute-start | bytes 393224 | tf_op jit(solution)/shard_map/ppermute | solution.py:63
  4.7 2.6 %collective-permute-start.1 = (bf16[16,4096]{1,0:T(8,128)(2,1)S(1)}, bf16[16,4096]{1,0:T(8,128)(2,1)S(1)}, u32[]{:S(2)}, u32[]{:S(2)}) collective-permute-start(bf16[16,4096]{1,0:T(8,128)(2,1)S(1)} %get-tuple-element.54), channel_id=1, source_target_pairs={{0,8},{1,9},{2,10},{3,11},{4,12},{5,13},{6,14},{7,15},{8,0},{9,1},... | collective-permute-start | bytes 393224 | tf_op jit(solution)/shard_map/ppermute | solution.py:63
  7.3 1.3 collective-permute-start
  9.0 2.2 collective-permute-done.2
  11.2 4.8 %collective-permute-done.1 = bf16[16,4096]{1,0:T(8,128)(2,1)S(1)} collective-permute-done((bf16[16,4096]{1,0:T(8,128)(2,1)S(1)}, bf16[16,4096]{1,0:T(8,128)(2,1)S(1)}, u32[]{:S(2)}, u32[]{:S(2)}) %collective-permute-start.1) | collective-permute-done | bytes 131104 | tf_op jit(solution)/shard_map/ppermute | solution.py:63
  16.0 1.6 collective-permute-start.7
  17.8 12.1 %collective-permute-done.7 = bf16[4,16,4096]{2,1,0:T(8,128)(2,1)S(1)} collective-permute-done((bf16[4,16,4096]{2,1,0:T(8,128)(2,1)S(1)}, bf16[4,16,4096]{2,1,0:T(8,128)(2,1)S(1)}, u32[]{:S(2)}, u32[]{:S(2)}) %collective-permute-start.7) | collective-permute-done | bytes 524320 | tf_op jit(solution)/shard_map/ppermute | solution.py:63
  30.5 3.4 %collective-permute-start.5 = (bf16[16,4096]{1,0:T(8,128)(2,1)S(1)}, bf16[16,4096]{1,0:T(8,128)(2,1)S(1)}, u32[]{:S(2)}, u32[]{:S(2)}) collective-permute-start(bf16[16,4096]{1,0:T(8,128)(2,1)S(1)} %get-tuple-element.18), channel_id=1, source_target_pairs={{0,4},{1,5},{2,6},{3,7},{4,8},{5,9},{6,10},{7,11},{8,12},{9,13},{1... | collective-permute-start | bytes 393224 | tf_op jit(solution)/shard_map/ppermute | solution.py:63
  34.4 1.8 collective-permute-start.3
  36.6 2.1 collective-permute-done.5
  38.7 5.2 %collective-permute-done.4 = bf16[16,4096]{1,0:T(8,128)(2,1)S(1)} collective-permute-done((bf16[16,4096]{1,0:T(8,128)(2,1)S(1)}, bf16[16,4096]{1,0:T(8,128)(2,1)S(1)}, u32[]{:S(2)}, u32[]{:S(2)}) %collective-permute-start.4) | collective-permute-done | bytes 131104 | tf_op jit(solution)/shard_map/ppermute | solution.py:63
  43.9 1.6 collective-permute-start.6
  49.0 14.3 %shard_map.103.rest_4_ = f32[2,256,1792]{2,1,0:T(8,128)S(1)} custom-call(bf16[128,4096]{1,0:T(8,128)(2,1)S(1)} %bitcast.100, bf16[128,4096]{1,0:T(8,128)(2,1)S(1)} %copy-done.15, bf16[2,8192,1792]{2,1,0:T(8,128)(2,1)} %u1_.5, bf16[2,8192,1792]{2,1,0:T(8,128)(2,1)} %u1_.5, bf16[2,8192,1792]{2,1,0:T(8,128)(2,1)} %u1_.5, bf16[2,8192,1792]{2,1,0:T(8,128)(2,1)} %u1_.5), custom_call_target="tpu_custom_call" | custom-call | flops 7516192768 | bytes 29360128 | tf_op jit(solution)/shard_map/pallas_call | solution.py:131
  63.3 1.8 copy-done.1
  66.9 2.3 %collective-permute-done.9.far.rest_11_ = bf16[128,4096]{1,0:T(8,128)(2,1)} collective-permute-done((bf16[128,4096]{1,0:T(8,128)(2,1)}, bf16[128,4096]{1,0:T(8,128)(2,1)}, u32[]{:S(2)}, u32[]{:S(2)}) %collective-permute-start.9) | collective-permute-done | bytes 1048608 | tf_op jit(solution)/shard_map/ppermute | solution.py:63
  71.6 2.6 %shard_map.107 = (bf16[256,512]{1,0:T(8,128)(2,1)S(1)}, f32[256,128]{1,0:T(8,128)S(1)}) custom-call(s32[8]{0:T(128)S(1)} %bitcast.115, s32[16]{0:T(128)S(1)} %get-tuple-element.34.places, s32[3]{0:T(128)S(1)} %pad_add_fusion.which, s32[256,1]{1,0:T(8,128)S(1)} %copy.19.seg, bf16[24,512,128]{2,1,0:T(8,128)(2,1)S(1)} %copy-done, ...), custom_call_target="tpu_custom_call" | custom-call | flops 268435456 | bytes 1048576 | tf_op jit(solution)/shard_map/pallas_call | solution.py:192
  76.2 3.8 %collective-permute-done.11 = f32[128,128]{1,0:T(8,128)S(1)} collective-permute-done((f32[128,128]{1,0:T(8,128)S(1)}, f32[128,128]{1,0:T(8,128)S(1)}, u32[]{:S(2)}, u32[]{:S(2)}) %collective-permute-start.11) | collective-permute-done | bytes 65568 | tf_op jit(solution)/shard_map/ppermute | solution.py:89
  79.9 3.4 %collective-permute-start.12 = (f32[128,128]{1,0:T(8,128)S(1)}, f32[128,128]{1,0:T(8,128)S(1)}, u32[]{:S(2)}, u32[]{:S(2)}) collective-permute-start(f32[128,128]{1,0:T(8,128)S(1)} %add.304), channel_id=1, source_target_pairs={{0,4},{1,5},{2,6},{3,7},{4,0},{5,1},{6,2},{7,3},{8,12},{9,13},{10,... | collective-permute-start | bytes 196616 | tf_op jit(solution)/shard_map/ppermute | solution.py:89
  83.3 5.5 %shard_map.104.rest_4_ = f32[2,256,1792]{2,1,0:T(8,128)S(1)} custom-call(bf16[128,4096]{1,0:T(8,128)(2,1)} %bitcast.15.near.rest_10_, bf16[128,4096]{1,0:T(8,128)(2,1)} %collective-permute-done.9.far.rest_11_, bf16[2,8192,1792]{2,1,0:T(8,128)(2,1)} %u1_.5, bf16[2,8192,1792]{2,1,0:T(8,128)(2,1)} %u1_.5, ...), custom_call_target="tpu_custom_call", output_to_operand_aliasing={{}: (6, {})} | custom-call | flops 2147483648 | bytes 8388608 | tf_op jit(solution)/shard_map/pallas_call | solution.py:131
  88.8 2.3 %collective-permute-start.13 = (f32[128,128]{1,0:T(8,128)S(1)}, f32[128,128]{1,0:T(8,128)S(1)}, u32[]{:S(2)}, u32[]{:S(2)}) collective-permute-start(f32[128,128]{1,0:T(8,128)S(1)} %add.305), channel_id=1, source_target_pairs={{0,8},{1,9},{2,10},{3,11},{4,12},{5,13},{6,14},{7,15},{8,0},{9,1},... | collective-permute-start | bytes 196616 | tf_op jit(solution)/shard_map/ppermute | solution.py:89
  91.1 5.5 %shard_map.105.rest_4_ = f32[2,256,1792]{2,1,0:T(8,128)S(1)} custom-call(bf16[128,4096]{1,0:T(8,128)(2,1)} %bitcast.15.near.rest_10_, bf16[128,4096]{1,0:T(8,128)(2,1)} %collective-permute-done.9.far.rest_11_, bf16[2,8192,1792]{2,1,0:T(8,128)(2,1)} %u1_.5, bf16[2,8192,1792]{2,1,0:T(8,128)(2,1)} %u1_.5, ...), custom_call_target="tpu_custom_call", output_to_operand_aliasing={{}: (6, {})} | custom-call | flops 2147483648 | bytes 8388608 | tf_op jit(solution)/shard_map/pallas_call | solution.py:131
  96.8 8.7 %shard_map.106.base = f32[2,256,1792]{2,1,0:T(8,128)S(1)} custom-call(bf16[128,4096]{1,0:T(8,128)(2,1)} %bitcast.15.near.rest_10_, bf16[128,4096]{1,0:T(8,128)(2,1)} %collective-permute-done.9.far.rest_11_, bf16[2,8192,1792]{2,1,0:T(8,128)(2,1)} %u1_.5, bf16[2,8192,1792]{2,1,0:T(8,128)(2,1)} %u1_.5, ...), custom_call_target="tpu_custom_call", output_to_operand_aliasing={{}: (6, {})} | custom-call | flops 3221225472 | bytes 12582912 | tf_op jit(solution)/shard_map/pallas_call | solution.py:131
  105.6 7.6 %shard_map.108 = (bf16[256,1792]{1,0:T(8,128)(2,1)S(1)}, bf16[256,1792]{1,0:T(8,128)(2,1)S(1)}, f32[256,128]{1,0:T(8,128)S(1)}) custom-call(s32[8]{0:T(128)S(1)} %bitcast.116, s32[16]{0:T(128)S(1)} %get-tuple-element.34.places, f32[2,256,1792]{2,1,0:T(8,128)S(1)} %shard_map.106.base, bf16[256,1792]{1,0:T(8,128)(2,1)S(1)} %copy-done.17, ...), custom_call_target="tpu_custom_call" | custom-call | flops 1879048192 | bytes 10092544 | tf_op jit(solution)/shard_map/pallas_call | solution.py:259
  115.1 3.8 %shard_map.109.rest_0_ = f32[24,128,1792]{2,1,0:T(8,128)} custom-call(bf16[256,1792]{1,0:T(8,128)(2,1)S(1)} %get-tuple-element.22.dgate, bf16[256,1792]{1,0:T(8,128)(2,1)S(1)} %get-tuple-element.23.dup, bf16[256,256]{1,0:T(8,128)(2,1)S(1)} %fusion.7.order, bf16[256,128]{1,0:T(8,128)(2,1)S(1)} %bitcast.103, s32[1,256]{1,0:T(1,128)S(1)} %bitcast.108), custom_call_target="tpu_custom_call" | custom-call | flops 805306368 | bytes 6291456 | tf_op jit(solution)/shard_map/pallas_call | solution.py:316
  119.3 3.8 %shard_map.110.rest_0_ = f32[24,128,1792]{2,1,0:T(8,128)} custom-call(bf16[256,1792]{1,0:T(8,128)(2,1)S(1)} %get-tuple-element.22.dgate, bf16[256,1792]{1,0:T(8,128)(2,1)S(1)} %get-tuple-element.23.dup, bf16[256,256]{1,0:T(8,128)(2,1)S(1)} %fusion.7.order, bf16[256,128]{1,0:T(8,128)(2,1)S(1)} %bitcast.104, ...), custom_call_target="tpu_custom_call", output_to_operand_aliasing={{}: (5, {})} | custom-call | flops 805306368 | bytes 6291456 | tf_op jit(solution)/shard_map/pallas_call | solution.py:316
  124.1 5.0 %shard_map.111 = f32[24,128,1792]{2,1,0:T(8,128)} custom-call(bf16[256,1792]{1,0:T(8,128)(2,1)S(1)} %get-tuple-element.22.dgate, bf16[256,1792]{1,0:T(8,128)(2,1)S(1)} %get-tuple-element.23.dup, bf16[256,256]{1,0:T(8,128)(2,1)S(1)} %fusion.7.order, bf16[256,128]{1,0:T(8,128)(2,1)S(1)} %bitcast.105, ...), custom_call_target="tpu_custom_call", output_to_operand_aliasing={{}: (5, {})} | custom-call | flops 1207959552 | bytes 9437184 | tf_op jit(solution)/shard_map/pallas_call | solution.py:316
  131.2 1.5 shard_map.112.side
  132.7 11.7 %shard_map.113 = bf16[256,3072]{1,0:T(8,128)(2,1)S(1)} custom-call(s32[1]{0:T(128)} %bitcast.at, bf16[2,8192,1792]{2,1,0:T(8,128)(2,1)} %u1_.5, bf16[2,8192,1792]{2,1,0:T(8,128)(2,1)} %u1_.5, bf16[2,8192,1792]{2,1,0:T(8,128)(2,1)} %u1_.5, bf16[2,8192,1792]{2,1,0:T(8,128)(2,1)} %u1_.5, bf16[256,1792]{1,0:T(8,128)(2,1)S(1)} %get-tuple-element.22.dgate, ...), custom_call_target="tpu_custom_call" | custom-call | flops 5637144576 | bytes 22020096 | tf_op jit(solution)/shard_map/pallas_call | solution.py:427
  144.8 2.1 collective-permute-done.20
  147.2 11.5 %shard_map.114 = bf16[256,3072]{1,0:T(8,128)(2,1)S(1)} custom-call(s32[1]{0:T(128)} %bitcast.at, bf16[2,8192,1792]{2,1,0:T(8,128)(2,1)} %u1_.5, bf16[2,8192,1792]{2,1,0:T(8,128)(2,1)} %u1_.5, bf16[2,8192,1792]{2,1,0:T(8,128)(2,1)} %u1_.5, bf16[2,8192,1792]{2,1,0:T(8,128)(2,1)} %u1_.5, bf16[256,1792]{1,0:T(8,128)(2,1)S(1)} %get-tuple-element.22.dgate, ...), custom_call_target="tpu_custom_call" | custom-call | flops 5637144576 | bytes 22020096 | tf_op jit(solution)/shard_map/pallas_call | solution.py:427
  158.7 1.6 collective-permute-start.21
  160.3 1.2 fusion.32
  161.6 8.4 %collective-permute-done.21 = bf16[4,16,3072]{2,1,0:T(8,128)(2,1)S(1)} collective-permute-done((bf16[4,16,3072]{2,1,0:T(8,128)(2,1)S(1)}, bf16[4,16,3072]{2,1,0:T(8,128)(2,1)S(1)}, u32[]{:S(2)}, u32[]{:S(2)}) %collective-permute-start.21) | collective-permute-done | bytes 393248 | tf_op jit(solution)/shard_map/ppermute | solution.py:63
  170.1 2.7 %collective-permute-start.24 = (bf16[16,3072]{1,0:T(8,128)(2,1)S(1)}, bf16[16,3072]{1,0:T(8,128)(2,1)S(1)}, u32[]{:S(2)}, u32[]{:S(2)}) collective-permute-start(bf16[16,3072]{1,0:T(8,128)(2,1)S(1)} %get-tuple-element.45), channel_id=1, source_target_pairs={{0,12},{1,13},{2,14},{3,15},{4,0},{5,1},{6,2},{7,3},{8,4},{9,5},{1... | collective-permute-start | bytes 294920 | tf_op jit(solution)/shard_map/ppermute | solution.py:63
  173.9 2.1 collective-permute-done.24
  176.0 5.5 %collective-permute-done.23 = bf16[16,3072]{1,0:T(8,128)(2,1)S(1)} collective-permute-done((bf16[16,3072]{1,0:T(8,128)(2,1)S(1)}, bf16[16,3072]{1,0:T(8,128)(2,1)S(1)}, u32[]{:S(2)}, u32[]{:S(2)}) %collective-permute-start.23) | collective-permute-done | bytes 98336 | tf_op jit(solution)/shard_map/ppermute | solution.py:63
  182.5 1.6 fusion
  184.1 8.2 %shard_map.115 = bf16[256,2048]{1,0:T(8,128)(2,1)S(1)} custom-call(s32[1]{0:T(128)} %bitcast.at, bf16[2,8192,1792]{2,1,0:T(8,128)(2,1)} %u1_.5, bf16[2,8192,1792]{2,1,0:T(8,128)(2,1)} %u1_.5, bf16[2,8192,1792]{2,1,0:T(8,128)(2,1)} %u1_.5, bf16[2,8192,1792]{2,1,0:T(8,128)(2,1)} %u1_.5, bf16[256,1792]{1,0:T(8,128)(2,1)S(1)} %copy-done.4, ...), custom_call_target="tpu_custom_call" | custom-call | flops 3758096384 | bytes 14680064 | tf_op jit(solution)/shard_map/pallas_call | solution.py:427
  192.3 1.6 collective-permute-start.26
  194.1 5.3 %shard_map.116 = f32[24,512,128]{2,1,0:T(8,128)} custom-call(bf16[256,512]{1,0:T(8,128)(2,1)S(1)} %get-tuple-element.31.columns, bf16[256,256]{1,0:T(8,128)(2,1)S(1)} %copy-done.13, bf16[256,128]{1,0:T(8,128)(2,1)S(1)} %bitcast.107, s32[256,1]{1,0:T(8,128)S(1)} %copy.21.adapter), custom_call_target="tpu_custom_call" | custom-call | flops 805306368 | bytes 6291456 | tf_op jit(solution)/shard_map/pallas_call | solution.py:346
  199.4 3.3 %collective-permute-done.26 = bf16[4,16,3072]{2,1,0:T(8,128)(2,1)S(1)} collective-permute-done((bf16[4,16,3072]{2,1,0:T(8,128)(2,1)S(1)}, bf16[4,16,3072]{2,1,0:T(8,128)(2,1)S(1)}, u32[]{:S(2)}, u32[]{:S(2)}) %collective-permute-start.26) | collective-permute-done | bytes 393248 | tf_op jit(solution)/shard_map/ppermute | solution.py:63
  203.0 1.6 collective-permute-start.31
  204.7 1.8 collective-permute-start.28
  206.4 1.9 collective-permute-start.27
  208.4 1.3 collective-permute-done.31
  211.6 3.6 %collective-permute-start.32 = (bf16[16,2048]{1,0:T(8,128)(2,1)S(1)}, bf16[16,2048]{1,0:T(8,128)(2,1)S(1)}, u32[]{:S(2)}, u32[]{:S(2)}) collective-permute-start(bf16[16,2048]{1,0:T(8,128)(2,1)S(1)} %get-tuple-element.50), channel_id=1, source_target_pairs={{0,4},{1,5},{2,6},{3,7},{4,8},{5,9},{6,10},{7,11},{8,12},{9,13},{1... | collective-permute-start | bytes 196616 | tf_op jit(solution)/shard_map/ppermute | solution.py:63
  215.2 2.8 %collective-permute-done.28 = bf16[16,3072]{1,0:T(8,128)(2,1)S(1)} collective-permute-done((bf16[16,3072]{1,0:T(8,128)(2,1)S(1)}, bf16[16,3072]{1,0:T(8,128)(2,1)S(1)}, u32[]{:S(2)}, u32[]{:S(2)}) %collective-permute-start.28) | collective-permute-done | bytes 98336 | tf_op jit(solution)/shard_map/ppermute | solution.py:63
  218.1 1.3 collective-permute-done.33
  (164 shorter events, 24.0 us)
Async XLA Ops:
  0.6 29.6 %copy-start.24 = (s32[1,8]{1,0:T(1,128)S(1)}, s32[1,8]{1,0:T(1,128)}, u32[]{:S(2)}) copy-start(s32[1,8]{1,0:T(1,128)} %param.14) | copy-start | bytes 100
  1.6 9.5 %collective-permute-start.2 = (bf16[16,4096]{1,0:T(8,128)(2,1)S(1)}, bf16[16,4096]{1,0:T(8,128)(2,1)S(1)}, u32[]{:S(2)}, u32[]{:S(2)}) collective-permute-start(bf16[16,4096]{1,0:T(8,128)(2,1)S(1)} %get-tuple-element.54), channel_id=1, source_target_pairs={{0,4},{1,5},{2,6},{3,7},{4,8},{5,9},{6,10},{7,11},{8,12},{9,13},{1... | collective-permute-start | bytes 393224 | tf_op jit(solution)/shard_map/ppermute | solution.py:63
  4.7 11.2 %collective-permute-start.1 = (bf16[16,4096]{1,0:T(8,128)(2,1)S(1)}, bf16[16,4096]{1,0:T(8,128)(2,1)S(1)}, u32[]{:S(2)}, u32[]{:S(2)}) collective-permute-start(bf16[16,4096]{1,0:T(8,128)(2,1)S(1)} %get-tuple-element.54), channel_id=1, source_target_pairs={{0,8},{1,9},{2,10},{3,11},{4,12},{5,13},{6,14},{7,15},{8,0},{9,1},... | collective-permute-start | bytes 393224 | tf_op jit(solution)/shard_map/ppermute | solution.py:63
  7.3 8.6 %collective-permute-start = (bf16[16,4096]{1,0:T(8,128)(2,1)S(1)}, bf16[16,4096]{1,0:T(8,128)(2,1)S(1)}, u32[]{:S(2)}, u32[]{:S(2)}) collective-permute-start(bf16[16,4096]{1,0:T(8,128)(2,1)S(1)} %get-tuple-element.54), channel_id=1, source_target_pairs={{0,12},{1,13},{2,14},{3,15},{4,0},{5,1},{6,2},{7,3},{8,4},{9,5},{1... | collective-permute-start | bytes 393224 | tf_op jit(solution)/shard_map/ppermute | solution.py:63
  16.0 13.8 %collective-permute-start.7 = (bf16[4,16,4096]{2,1,0:T(8,128)(2,1)S(1)}, bf16[4,16,4096]{2,1,0:T(8,128)(2,1)S(1)}, u32[]{:S(2)}, u32[]{:S(2)}) collective-permute-start(bf16[4,16,4096]{2,1,0:T(8,128)(2,1)S(1)} %get-tuple-element.43), channel_id=1, source_target_pairs={{0,2},{1,3},{2,0},{3,1},{4,6},{5,7},{6,4},{7,5},{8,10},{9,11},{10,... | collective-permute-start | bytes 1572872 | tf_op jit(solution)/shard_map/ppermute | solution.py:63
  30.0 15.6 %copy-start.7 = (bf16[2,4,16,4096]{3,2,1,0:T(8,128)(2,1)}, bf16[2,4,16,4096]{3,2,1,0:T(8,128)(2,1)S(1)}, u32[]{:S(2)}) copy-start(bf16[2,4,16,4096]{3,2,1,0:T(8,128)(2,1)S(1)} %pad_maximum_fusion) | copy-start | bytes 3145732
  30.0 15.6 %collective-permute-start.8 = (bf16[128,4096]{1,0:T(8,128)(2,1)S(1)}, bf16[128,4096]{1,0:T(8,128)(2,1)S(1)}, u32[]{:S(2)}, u32[]{:S(2)}) collective-permute-start(bf16[128,4096]{1,0:T(8,128)(2,1)S(1)} %bitcast.99), channel_id=1, source_target_pairs={{0,1},{1,0},{2,3},{3,2},{4,5},{5,4},{6,7},{7,6},{8,9},{9,8},{10,11... | collective-permute-start | bytes 3145736 | tf_op jit(solution)/shard_map/ppermute | solution.py:63
  30.5 8.2 %collective-permute-start.5 = (bf16[16,4096]{1,0:T(8,128)(2,1)S(1)}, bf16[16,4096]{1,0:T(8,128)(2,1)S(1)}, u32[]{:S(2)}, u32[]{:S(2)}) collective-permute-start(bf16[16,4096]{1,0:T(8,128)(2,1)S(1)} %get-tuple-element.18), channel_id=1, source_target_pairs={{0,4},{1,5},{2,6},{3,7},{4,8},{5,9},{6,10},{7,11},{8,12},{9,13},{1... | collective-permute-start | bytes 393224 | tf_op jit(solution)/shard_map/ppermute | solution.py:63
  33.8 10.0 %collective-permute-start.4 = (bf16[16,4096]{1,0:T(8,128)(2,1)S(1)}, bf16[16,4096]{1,0:T(8,128)(2,1)S(1)}, u32[]{:S(2)}, u32[]{:S(2)}) collective-permute-start(bf16[16,4096]{1,0:T(8,128)(2,1)S(1)} %get-tuple-element.18), channel_id=1, source_target_pairs={{0,8},{1,9},{2,10},{3,11},{4,12},{5,13},{6,14},{7,15},{8,0},{9,1},... | collective-permute-start | bytes 393224 | tf_op jit(solution)/shard_map/ppermute | solution.py:63
  34.4 9.4 %collective-permute-start.3 = (bf16[16,4096]{1,0:T(8,128)(2,1)S(1)}, bf16[16,4096]{1,0:T(8,128)(2,1)S(1)}, u32[]{:S(2)}, u32[]{:S(2)}) collective-permute-start(bf16[16,4096]{1,0:T(8,128)(2,1)S(1)} %get-tuple-element.18), channel_id=1, source_target_pairs={{0,12},{1,13},{2,14},{3,15},{4,0},{5,1},{6,2},{7,3},{8,4},{9,5},{1... | collective-permute-start | bytes 393224 | tf_op jit(solution)/shard_map/ppermute | solution.py:63
  43.9 22.7 %copy-start.22 = (s32[1,8]{1,0:T(1,128)S(1)}, s32[1,8]{1,0:T(1,128)}, u32[]{:S(2)}) copy-start(s32[1,8]{1,0:T(1,128)} %param.13) | copy-start | bytes 100
  43.9 22.7 %copy-start.25 = (s32[24]{0:T(128)S(1)}, s32[24]{0:T(128)}, u32[]{:S(2)}) copy-start(s32[24]{0:T(128)} %param.15) | copy-start | bytes 292
  43.9 21.2 %collective-permute-start.6 = (bf16[4,16,4096]{2,1,0:T(8,128)(2,1)S(1)}, bf16[4,16,4096]{2,1,0:T(8,128)(2,1)S(1)}, u32[]{:S(2)}, u32[]{:S(2)}) collective-permute-start(bf16[4,16,4096]{2,1,0:T(8,128)(2,1)S(1)} %pad_maximum_fusion.3), channel_id=1, source_target_pairs={{0,2},{1,3},{2,0},{3,1},{4,6},{5,7},{6,4},{7,5},{8,10},{9,11},{10,... | collective-permute-start | bytes 1572872 | tf_op jit(solution)/shard_map/ppermute | solution.py:63
  49.0 20.2 %copy-start = (bf16[24,512,128]{2,1,0:T(8,128)(2,1)S(1)}, bf16[24,512,128]{2,1,0:T(8,128)(2,1)}, u32[]{:S(2)}) copy-start(bf16[24,512,128]{2,1,0:T(8,128)(2,1)} %rest_7_.5) | copy-start | bytes 9437188
  66.2 3.0 %collective-permute-start.9 = (bf16[128,4096]{1,0:T(8,128)(2,1)}, bf16[128,4096]{1,0:T(8,128)(2,1)}, u32[]{:S(2)}, u32[]{:S(2)}) collective-permute-start(bf16[128,4096]{1,0:T(8,128)(2,1)} %bitcast.15.near.rest_10_), channel_id=1, source_target_pairs={{0,1},{1,0},{2,3},{3,2},{4,5},{5,4},{6,7},{7,6},{8,9},{9,8},{10,11... | collective-permute-start | bytes 3145736 | tf_op jit(solution)/shard_map/ppermute | solution.py:63
  66.9 64.3 %copy-start.12 = (bf16[256,256]{1,0:T(8,128)(2,1)}, bf16[256,256]{1,0:T(8,128)(2,1)S(1)}, u32[]{:S(2)}) copy-start(bf16[256,256]{1,0:T(8,128)(2,1)S(1)} %fusion.7.order) | copy-start | bytes 393220
  71.6 11.7 %copy-start.2 = (f32[2,256,1792]{2,1,0:T(8,128)S(1)}, f32[2,256,1792]{2,1,0:T(8,128)}, u32[]{:S(2)}) copy-start(f32[2,256,1792]{2,1,0:T(8,128)} %copy-done.1) | copy-start | bytes 11010052
  74.3 1.3 collective-permute-start.10
  75.6 4.3 %collective-permute-start.11 = (f32[128,128]{1,0:T(8,128)S(1)}, f32[128,128]{1,0:T(8,128)S(1)}, u32[]{:S(2)}, u32[]{:S(2)}) collective-permute-start(f32[128,128]{1,0:T(8,128)S(1)} %slice_add_fusion.1), channel_id=1, source_target_pairs={{0,2},{1,3},{2,0},{3,1},{4,6},{5,7},{6,4},{7,5},{8,10},{9,11},{10,... | collective-permute-start | bytes 196616 | tf_op jit(solution)/shard_map/ppermute | solution.py:89
  79.9 8.9 %collective-permute-start.12 = (f32[128,128]{1,0:T(8,128)S(1)}, f32[128,128]{1,0:T(8,128)S(1)}, u32[]{:S(2)}, u32[]{:S(2)}) collective-permute-start(f32[128,128]{1,0:T(8,128)S(1)} %add.304), channel_id=1, source_target_pairs={{0,4},{1,5},{2,6},{3,7},{4,0},{5,1},{6,2},{7,3},{8,12},{9,13},{10,... | collective-permute-start | bytes 196616 | tf_op jit(solution)/shard_map/ppermute | solution.py:89
  88.8 7.8 %collective-permute-start.13 = (f32[128,128]{1,0:T(8,128)S(1)}, f32[128,128]{1,0:T(8,128)S(1)}, u32[]{:S(2)}, u32[]{:S(2)}) collective-permute-start(f32[128,128]{1,0:T(8,128)S(1)} %add.305), channel_id=1, source_target_pairs={{0,8},{1,9},{2,10},{3,11},{4,12},{5,13},{6,14},{7,15},{8,0},{9,1},... | collective-permute-start | bytes 196616 | tf_op jit(solution)/shard_map/ppermute | solution.py:89
  96.8 8.8 %collective-permute-start.14 = (bf16[128,128]{1,0:T(8,128)(2,1)S(1)}, bf16[128,128]{1,0:T(8,128)(2,1)S(1)}, u32[]{:S(2)}, u32[]{:S(2)}) collective-permute-start(bf16[128,128]{1,0:T(8,128)(2,1)S(1)} %fusion.17), channel_id=1, source_target_pairs={{0,1},{1,0},{2,3},{3,2},{4,5},{5,4},{6,7},{7,6},{8,9},{9,8},{10,11... | collective-permute-start | bytes 98312 | tf_op jit(solution)/shard_map/ppermute | solution.py:63
  113.2 34.0 %copy-start.3 = (bf16[256,1792]{1,0:T(8,128)(2,1)}, bf16[256,1792]{1,0:T(8,128)(2,1)S(1)}, u32[]{:S(2)}) copy-start(bf16[256,1792]{1,0:T(8,128)(2,1)S(1)} %get-tuple-element.22.dgate) | copy-start | bytes 2752516
  113.2 33.9 %copy-start.5 = (bf16[256,1792]{1,0:T(8,128)(2,1)}, bf16[256,1792]{1,0:T(8,128)(2,1)S(1)}, u32[]{:S(2)}) copy-start(bf16[256,1792]{1,0:T(8,128)(2,1)S(1)} %get-tuple-element.23.dup) | copy-start | bytes 2752516
  113.2 1.3 collective-permute-start.15
  114.6 4.4 %collective-permute-start.16 = (f32[128,128]{1,0:T(8,128)S(1)}, f32[128,128]{1,0:T(8,128)S(1)}, u32[]{:S(2)}, u32[]{:S(2)}) collective-permute-start(f32[128,128]{1,0:T(8,128)S(1)} %slice_add_fusion), channel_id=1, source_target_pairs={{0,2},{1,3},{2,0},{3,1},{4,6},{5,7},{6,4},{7,5},{8,10},{9,11},{10,... | collective-permute-start | bytes 196616 | tf_op jit(solution)/shard_map/ppermute | solution.py:89
  119.0 4.3 %collective-permute-start.17 = (f32[128,128]{1,0:T(8,128)S(1)}, f32[128,128]{1,0:T(8,128)S(1)}, u32[]{:S(2)}, u32[]{:S(2)}) collective-permute-start(f32[128,128]{1,0:T(8,128)S(1)} %add.315), channel_id=1, source_target_pairs={{0,4},{1,5},{2,6},{3,7},{4,0},{5,1},{6,2},{7,3},{8,12},{9,13},{10,... | collective-permute-start | bytes 196616 | tf_op jit(solution)/shard_map/ppermute | solution.py:89
  123.3 6.4 %collective-permute-start.18 = (f32[128,128]{1,0:T(8,128)S(1)}, f32[128,128]{1,0:T(8,128)S(1)}, u32[]{:S(2)}, u32[]{:S(2)}) collective-permute-start(f32[128,128]{1,0:T(8,128)S(1)} %add.316), channel_id=1, source_target_pairs={{0,8},{1,9},{2,10},{3,11},{4,12},{5,13},{6,14},{7,15},{8,0},{9,1},... | collective-permute-start | bytes 196616 | tf_op jit(solution)/shard_map/ppermute | solution.py:89
  129.9 1.3 collective-permute-start.19
  132.7 14.4 %copy-start.10 = (f32[512,256]{1,0:T(8,128)}, f32[512,256]{1,0:T(8,128)S(1)}, u32[]{:S(2)}) copy-start(f32[512,256]{1,0:T(8,128)S(1)} %shard_map.112.side) | copy-start | bytes 1572868
  144.6 2.4 %collective-permute-start.20 = (bf16[2,4,16,3072]{3,2,1,0:T(8,128)(2,1)S(1)}, bf16[2,4,16,3072]{3,2,1,0:T(8,128)(2,1)S(1)}, u32[]{:S(2)}, u32[]{:S(2)}) collective-permute-start(bf16[2,4,16,3072]{3,2,1,0:T(8,128)(2,1)S(1)} %bitcast.123), channel_id=1, source_target_pairs={{0,1},{1,0},{2,3},{3,2},{4,5},{5,4},{6,7},{7,6},{8,9},{9,8},{10,11... | collective-permute-start | bytes 2359304 | tf_op jit(solution)/shard_map/ppermute | solution.py:63
  158.7 11.2 %collective-permute-start.21 = (bf16[4,16,3072]{2,1,0:T(8,128)(2,1)S(1)}, bf16[4,16,3072]{2,1,0:T(8,128)(2,1)S(1)}, u32[]{:S(2)}, u32[]{:S(2)}) collective-permute-start(bf16[4,16,3072]{2,1,0:T(8,128)(2,1)S(1)} %slice_bitcast_fusion.2), channel_id=1, source_target_pairs={{0,2},{1,3},{2,0},{3,1},{4,6},{5,7},{6,4},{7,5},{8,10},{9,11},{10,... | collective-permute-start | bytes 1179656 | tf_op jit(solution)/shard_map/ppermute | solution.py:63
  161.5 22.5 %copy-start.4 = (bf16[256,1792]{1,0:T(8,128)(2,1)S(1)}, bf16[256,1792]{1,0:T(8,128)(2,1)}, u32[]{:S(2)}) copy-start(bf16[256,1792]{1,0:T(8,128)(2,1)} %copy-done.3) | copy-start | bytes 2752516
  161.5 22.6 %copy-start.6 = (bf16[256,1792]{1,0:T(8,128)(2,1)S(1)}, bf16[256,1792]{1,0:T(8,128)(2,1)}, u32[]{:S(2)}) copy-start(bf16[256,1792]{1,0:T(8,128)(2,1)} %copy-done.5) | copy-start | bytes 2752516
  161.5 22.6 %copy-start.11 = (f32[512,256]{1,0:T(8,128)S(1)}, f32[512,256]{1,0:T(8,128)}, u32[]{:S(2)}) copy-start(f32[512,256]{1,0:T(8,128)} %copy-done.10) | copy-start | bytes 1572868
  161.5 20.9 %collective-permute-start.25 = (bf16[2,4,16,3072]{3,2,1,0:T(8,128)(2,1)}, bf16[2,4,16,3072]{3,2,1,0:T(8,128)(2,1)}, u32[]{:S(2)}, u32[]{:S(2)}) collective-permute-start(bf16[2,4,16,3072]{3,2,1,0:T(8,128)(2,1)} %bitcast.39), channel_id=1, source_target_pairs={{0,1},{1,0},{2,3},{3,2},{4,5},{5,4},{6,7},{7,6},{8,9},{9,8},{10,11... | collective-permute-start | bytes 2359304 | tf_op jit(solution)/shard_map/ppermute | solution.py:63
  170.1 5.9 %collective-permute-start.24 = (bf16[16,3072]{1,0:T(8,128)(2,1)S(1)}, bf16[16,3072]{1,0:T(8,128)(2,1)S(1)}, u32[]{:S(2)}, u32[]{:S(2)}) collective-permute-start(bf16[16,3072]{1,0:T(8,128)(2,1)S(1)} %get-tuple-element.45), channel_id=1, source_target_pairs={{0,12},{1,13},{2,14},{3,15},{4,0},{5,1},{6,2},{7,3},{8,4},{9,5},{1... | collective-permute-start | bytes 294920 | tf_op jit(solution)/shard_map/ppermute | solution.py:63
  172.8 8.7 %collective-permute-start.23 = (bf16[16,3072]{1,0:T(8,128)(2,1)S(1)}, bf16[16,3072]{1,0:T(8,128)(2,1)S(1)}, u32[]{:S(2)}, u32[]{:S(2)}) collective-permute-start(bf16[16,3072]{1,0:T(8,128)(2,1)S(1)} %get-tuple-element.46), channel_id=1, source_target_pairs={{0,8},{1,9},{2,10},{3,11},{4,12},{5,13},{6,14},{7,15},{8,0},{9,1},... | collective-permute-start | bytes 294920 | tf_op jit(solution)/shard_map/ppermute | solution.py:63
  172.8 8.7 %collective-permute-start.22 = (bf16[16,3072]{1,0:T(8,128)(2,1)S(1)}, bf16[16,3072]{1,0:T(8,128)(2,1)S(1)}, u32[]{:S(2)}, u32[]{:S(2)}) collective-permute-start(bf16[16,3072]{1,0:T(8,128)(2,1)S(1)} %get-tuple-element.44), channel_id=1, source_target_pairs={{0,4},{1,5},{2,6},{3,7},{4,8},{5,9},{6,10},{7,11},{8,12},{9,13},{1... | collective-permute-start | bytes 294920 | tf_op jit(solution)/shard_map/ppermute | solution.py:63
  192.3 10.4 %collective-permute-start.26 = (bf16[4,16,3072]{2,1,0:T(8,128)(2,1)S(1)}, bf16[4,16,3072]{2,1,0:T(8,128)(2,1)S(1)}, u32[]{:S(2)}, u32[]{:S(2)}) collective-permute-start(bf16[4,16,3072]{2,1,0:T(8,128)(2,1)S(1)} %slice_bitcast_fusion), channel_id=1, source_target_pairs={{0,2},{1,3},{2,0},{3,1},{4,6},{5,7},{6,4},{7,5},{8,10},{9,11},{10,... | collective-permute-start | bytes 1179656 | tf_op jit(solution)/shard_map/ppermute | solution.py:63
  194.0 8.9 %collective-permute-start.30 = (bf16[2,4,16,2048]{3,2,1,0:T(8,128)(2,1)S(1)}, bf16[2,4,16,2048]{3,2,1,0:T(8,128)(2,1)S(1)}, u32[]{:S(2)}, u32[]{:S(2)}) collective-permute-start(bf16[2,4,16,2048]{3,2,1,0:T(8,128)(2,1)S(1)} %bitcast.125), channel_id=1, source_target_pairs={{0,1},{1,0},{2,3},{3,2},{4,5},{5,4},{6,7},{7,6},{8,9},{9,8},{10,11... | collective-permute-start | bytes 1572872 | tf_op jit(solution)/shard_map/ppermute | solution.py:63
  203.0 6.7 %collective-permute-start.31 = (bf16[4,16,2048]{2,1,0:T(8,128)(2,1)S(1)}, bf16[4,16,2048]{2,1,0:T(8,128)(2,1)S(1)}, u32[]{:S(2)}, u32[]{:S(2)}) collective-permute-start(bf16[4,16,2048]{2,1,0:T(8,128)(2,1)S(1)} %slice_bitcast_fusion.4), channel_id=1, source_target_pairs={{0,2},{1,3},{2,0},{3,1},{4,6},{5,7},{6,4},{7,5},{8,10},{9,11},{10,... | collective-permute-start | bytes 786440 | tf_op jit(solution)/shard_map/ppermute | solution.py:63
  204.6 7.0 %collective-permute-start.29 = (bf16[16,3072]{1,0:T(8,128)(2,1)S(1)}, bf16[16,3072]{1,0:T(8,128)(2,1)S(1)}, u32[]{:S(2)}, u32[]{:S(2)}) collective-permute-start(bf16[16,3072]{1,0:T(8,128)(2,1)S(1)} %get-tuple-element.48), channel_id=1, source_target_pairs={{0,12},{1,13},{2,14},{3,15},{4,0},{5,1},{6,2},{7,3},{8,4},{9,5},{1... | collective-permute-start | bytes 294920 | tf_op jit(solution)/shard_map/ppermute | solution.py:63
  204.7 13.4 %collective-permute-start.28 = (bf16[16,3072]{1,0:T(8,128)(2,1)S(1)}, bf16[16,3072]{1,0:T(8,128)(2,1)S(1)}, u32[]{:S(2)}, u32[]{:S(2)}) collective-permute-start(bf16[16,3072]{1,0:T(8,128)(2,1)S(1)} %get-tuple-element.49), channel_id=1, source_target_pairs={{0,8},{1,9},{2,10},{3,11},{4,12},{5,13},{6,14},{7,15},{8,0},{9,1},... | collective-permute-start | bytes 294920 | tf_op jit(solution)/shard_map/ppermute | solution.py:63
  206.4 11.6 %collective-permute-start.27 = (bf16[16,3072]{1,0:T(8,128)(2,1)S(1)}, bf16[16,3072]{1,0:T(8,128)(2,1)S(1)}, u32[]{:S(2)}, u32[]{:S(2)}) collective-permute-start(bf16[16,3072]{1,0:T(8,128)(2,1)S(1)} %get-tuple-element.47), channel_id=1, source_target_pairs={{0,4},{1,5},{2,6},{3,7},{4,8},{5,9},{6,10},{7,11},{8,12},{9,13},{1... | collective-permute-start | bytes 294920 | tf_op jit(solution)/shard_map/ppermute | solution.py:63
  209.8 8.3 %collective-permute-start.34 = (bf16[16,2048]{1,0:T(8,128)(2,1)S(1)}, bf16[16,2048]{1,0:T(8,128)(2,1)S(1)}, u32[]{:S(2)}, u32[]{:S(2)}) collective-permute-start(bf16[16,2048]{1,0:T(8,128)(2,1)S(1)} %get-tuple-element.51), channel_id=1, source_target_pairs={{0,12},{1,13},{2,14},{3,15},{4,0},{5,1},{6,2},{7,3},{8,4},{9,5},{1... | collective-permute-start | bytes 196616 | tf_op jit(solution)/shard_map/ppermute | solution.py:63
  210.4 9.0 %collective-permute-start.33 = (bf16[16,2048]{1,0:T(8,128)(2,1)S(1)}, bf16[16,2048]{1,0:T(8,128)(2,1)S(1)}, u32[]{:S(2)}, u32[]{:S(2)}) collective-permute-start(bf16[16,2048]{1,0:T(8,128)(2,1)S(1)} %get-tuple-element.52), channel_id=1, source_target_pairs={{0,8},{1,9},{2,10},{3,11},{4,12},{5,13},{6,14},{7,15},{8,0},{9,1},... | collective-permute-start | bytes 196616 | tf_op jit(solution)/shard_map/ppermute | solution.py:63
  211.6 7.9 %collective-permute-start.32 = (bf16[16,2048]{1,0:T(8,128)(2,1)S(1)}, bf16[16,2048]{1,0:T(8,128)(2,1)S(1)}, u32[]{:S(2)}, u32[]{:S(2)}) collective-permute-start(bf16[16,2048]{1,0:T(8,128)(2,1)S(1)} %get-tuple-element.50), channel_id=1, source_target_pairs={{0,4},{1,5},{2,6},{3,7},{4,8},{5,9},{6,10},{7,11},{8,12},{9,13},{1... | collective-permute-start | bytes 196616 | tf_op jit(solution)/shard_map/ppermute | solution.py:63
  (16 other events, 85.4 us)

commit v3 on v2

--- a/solution.py
+++ b/solution.py
@@ -8,7 +8,7 @@
 from jax.sharding import PartitionSpec as P
 
 GATHER_CHUNKS = 2
-SUM_SHARES = (3, 3, 2)
+SUM_SHARES = (4, 2, 2)
 MIB = 1024 * 1024
 BF16 = jnp.bfloat16
 F32 = jnp.float32
@@ -385,59 +385,53 @@
     )(adapters, places, order, low, seg_row, *([down] * segments))
 
 
-def backward_kernel(base, at, g0, g1, u0, u1, dgate, dup, side, out, total):
-    block, tokens = total.shape
+def backward_kernel(base, at, gate, up, dgate, dup, side, out, total):
+    block, tokens = total.shape[1:]
     shard = side.shape[0]
-    part = block // 2
+    k = pl.program_id(0)
     first = at[0] * shard
-    own = first // block == base + pl.program_id(0)
-
-    def product(h):
-        gate, up = ((g0, u0), (g1, u1))[h]
-        return dot(gate[0], dgate[...], ((1,), (1,))) + dot(up[0], dup[...], ((1,), (1,)))
-
-    @pl.when(jnp.logical_not(own))
-    def _():
-        for h in range(2):
-            out[:, h * part : (h + 1) * part] = product(h).T.astype(BF16)
-
-    @pl.when(own)
-    def _():
-        if shard == block:
-            for h in range(2):
-                rows = slice(h * part, (h + 1) * part)
-                out[:, rows] = (product(h) + side[rows]).T.astype(BF16)
-        else:
-            for h in range(2):
-                total[h * part : (h + 1) * part] = product(h)
-            here = pl.ds(pl.multiple_of(first % block, shard), shard)
-            total[here, :] += side[...]
-            out[...] = total[...].T.astype(BF16)
+    now, before = k % 2, (k + 1) % 2
+
+    @pl.when(k < pl.num_programs(0) - 1)
+    def _():
+        out[...] = total[before].T.astype(BF16)
+        total[now] = dot(gate[0], dgate[...], ((1,), (1,))) + dot(up[0], dup[...], ((1,), (1,)))
+
+    @pl.when(jnp.logical_and(first // block == base + k, k < pl.num_programs(0) - 1))
+    def _():
+        here = pl.ds(pl.multiple_of(first % block, shard), shard)
+        total[now, here, :] += side[...]
+
+    @pl.when(k == pl.num_programs(0) - 1)
+    def _():
+        out[...] = total[before].T.astype(BF16)
 
 
 def backward_chunk(frozen, dgate, dup, side, at, first, step):
     tokens, hidden = dgate.shape
     block = tile_of(step, 512)
     base = first // block
+    count = step // block
     full = lambda shape: pl.BlockSpec(shape, lambda *a: (0,) * len(shape))
 
-    def weight(i, h):
-        return pl.BlockSpec((1, block // 2, hidden), lambda k, at: (i, 2 * (base + k) + h, 0))
+    def weight(i):
+        return pl.BlockSpec(
+            (1, block, hidden), lambda k, at: (i, base + jnp.minimum(k, count - 1), 0)
+        )
 
     return pl.pallas_call(
         functools.partial(backward_kernel, base),
         grid_spec=pltpu.PrefetchScalarGridSpec(
             num_scalar_prefetch=1,
-            grid=(step // block,),
-            in_specs=[weight(i, h) for i in range(2) for h in range(2)]
-            + [full(dgate.shape), full(dup.shape), full(side.shape)],
-            out_specs=pl.BlockSpec((tokens, block), lambda k, at: (0, k)),
-            scratch_shapes=[pltpu.VMEM((block, tokens), F32)],
+            grid=(count + 1,),
+            in_specs=[weight(0), weight(1), full(dgate.shape), full(dup.shape), full(side.shape)],
+            out_specs=pl.BlockSpec((tokens, block), lambda k, at: (0, jnp.maximum(k - 1, 0))),
+            scratch_shapes=[pltpu.VMEM((2, block, tokens), F32)],
         ),
         out_shape=jax.ShapeDtypeStruct((tokens, step), BF16),
         compiler_params=params(32),
         cost_estimate=cost(4 * tokens * step * hidden, 4 * step * hidden),
-    )(at, *([frozen] * 4), dgate, dup, side)
+    )(at, frozen, frozen, dgate, dup, side)
 
 
 def local(
@@ -507,21 +501,20 @@
     hidden = frozen.shape[2]
     tiles = hidden // tile_of(hidden, 256)
     step = width // GATHER_CHUNKS
-    behind = None
+    outer = []
+    for q in range(GATHER_CHUNKS):
+        x = activations[:, q * step : (q + 1) * step]
+        outer.append(torus.gather(after(x, outer[-1]) if q else x, 0))
     base = None
     pairs = []
     for q in range(GATHER_CHUNKS):
-        x = activations[:, q * step : (q + 1) * step]
-        if q:
-            x = after(x, behind)
-        behind = torus.gather(x, 0)
-        parts = [behind] + [torus.move(behind, 1, -k) for k in range(1, b)]
-        if q:
-            parts = list(lax.optimization_barrier((*parts, base))[:-1])
+        parts = [outer[q]] + [torus.move(outer[q], 1, -k) for k in range(1, b)]
+        ahead = base if q else outer[-1]
+        parts = lax.optimization_barrier((*parts, ahead))[:-1]
         x = jnp.stack(parts).reshape(tokens // c, step)
         y = torus.move(x, 2, -1)
         pairs.append((x, y))
-        for cut in parts_of(tiles, 3) if q == GATHER_CHUNKS - 1 else [(0, tiles)]:
+        for cut in parts_of(tiles, 4) if q == GATHER_CHUNKS - 1 else [(0, tiles)]:
             base = forward_chunk(x, y, frozen, base, q * step, cut)
 
     columns, partial_in = low_in_partial(
@@ -549,8 +542,8 @@
     for q, share in enumerate(SUM_SHARES):
         step = width * share // sum(SUM_SHARES)
         ready = index[None]
-        if q:
-            ready = after(ready, cores[q - 1])
+        if q == 1:
+            ready = after(ready, cores[0])
         if q > 1:
             ready = after(ready, inners[q - 2])
         term = backward_chunk(frozen, dgate, dup, side, ready, first, step)

time: 221 us -> 200 us (0.905)
  waiting for transfers between devices: 63.2 us -> 41.3 us
  starting transfers between devices: 42.5 us -> 37.5 us
  local copies, waits for them, and re-layouts: 11.3 us -> 14.3 us
    ppermute x29, waiting for transfers between devices: 58.7 us -> 41.2 us  [move(): return lax.ppermute(x, 'tensor', pairs)]
    ppermute x6, waiting for transfers between devices: 4.57 us -> 0.16 us  [exchange_sum(): x = x + lax.ppermute(x, 'tensor', pairs)]
    ppermute x29, starting transfers between devices: 34.6 us -> 30.5 us  [move(): return lax.ppermute(x, 'tensor', pairs)]
    unnamed x58 -> x60, local copies, waits for them, and re-layouts: 7.81 us -> 10.5 us
    pallas_call x4 -> x5, Pallas kernels: 34 us -> 35.3 us  [forward_chunk(): pl.pallas_call(forward_kernel, grid=(count,), in_specs=specs, out_specs=a...]
  transfers between devices with their start and end apart: 35 -> 35, of which waited for: 20 -> 17; matrix products, arithmetic and copies ran while one was open for 2% -> 2% of each run, Pallas kernels for 24% -> 35%
where the time goes in v3:
time: 200 us
  Pallas kernels  96.5 us (48%)
  waiting for transfers between devices  41.3 us (21%)
  starting transfers between devices  37.5 us (19%)
  local copies, waits for them, and re-layouts  14.3 us (7%)
  other arithmetic  8.91 us (4%)
    ppermute x29, waiting for transfers between devices, move(): return lax.ppermute(x, 'tensor', pairs)  41.2 us
    pallas_call x5, Pallas kernels, forward_chunk(): pl.pallas_call(forward_kernel, grid=(count,), in_specs=specs, out_specs=a...  35.3 us
    pallas_call x3, Pallas kernels, backward_chunk(): pl.pallas_call(functools.partial(backward_kernel, base), grid_spec=pltpu....  31.6 us
    ppermute x29, starting transfers between devices, move(): return lax.ppermute(x, 'tensor', pairs)  30.5 us
    pallas_call x3, Pallas kernels, grad_b_of(): pl.pallas_call(grad_b_kernel, grid=(last - first,), in_specs=specs, out_s...  12.7 us
    unnamed x60, local copies, waits for them, and re-layouts  10.5 us
    pallas_call x1, Pallas kernels, middle(): pl.pallas_call(functools.partial(middle_kernel, segments, rows), grid_spe...  7.55 us
    ppermute x6, starting transfers between devices, exchange_sum(): x = x + lax.ppermute(x, 'tensor', pairs)  7.02 us
  transfers between devices with their start and end apart: 35, of which 17 were waited for; matrix products, arithmetic and copies ran while one was open for 2% of the time, Pallas kernels for 35%

profile of v3, /device:TPU:0, one launch (start us, length us, event | category | flops | bytes accessed | tf_op | source)
XLA Modules:
  0.0 199.9 jit_solution(18192009527450041727)
XLA Ops:
  1.6 3.1 %collective-permute-start.2 = (bf16[16,4096]{1,0:T(8,128)(2,1)S(1)}, bf16[16,4096]{1,0:T(8,128)(2,1)S(1)}, u32[]{:S(2)}, u32[]{:S(2)}) collective-permute-start(bf16[16,4096]{1,0:T(8,128)(2,1)S(1)} %get-tuple-element.54), channel_id=1, source_target_pairs={{0,4},{1,5},{2,6},{3,7},{4,8},{5,9},{6,10},{7,11},{8,12},{9,13},{1... | collective-permute-start | bytes 393224 | tf_op jit(solution)/shard_map/ppermute | solution.py:63
  4.7 2.6 %collective-permute-start.1 = (bf16[16,4096]{1,0:T(8,128)(2,1)S(1)}, bf16[16,4096]{1,0:T(8,128)(2,1)S(1)}, u32[]{:S(2)}, u32[]{:S(2)}) collective-permute-start(bf16[16,4096]{1,0:T(8,128)(2,1)S(1)} %get-tuple-element.54), channel_id=1, source_target_pairs={{0,8},{1,9},{2,10},{3,11},{4,12},{5,13},{6,14},{7,15},{8,0},{9,1},... | collective-permute-start | bytes 393224 | tf_op jit(solution)/shard_map/ppermute | solution.py:63
  7.3 1.3 collective-permute-start
  9.1 2.1 %collective-permute-done.2 = bf16[16,4096]{1,0:T(8,128)(2,1)S(1)} collective-permute-done((bf16[16,4096]{1,0:T(8,128)(2,1)S(1)}, bf16[16,4096]{1,0:T(8,128)(2,1)S(1)}, u32[]{:S(2)}, u32[]{:S(2)}) %collective-permute-start.2) | collective-permute-done | bytes 131104 | tf_op jit(solution)/shard_map/ppermute | solution.py:63
  11.2 4.8 %collective-permute-done.1 = bf16[16,4096]{1,0:T(8,128)(2,1)S(1)} collective-permute-done((bf16[16,4096]{1,0:T(8,128)(2,1)S(1)}, bf16[16,4096]{1,0:T(8,128)(2,1)S(1)}, u32[]{:S(2)}, u32[]{:S(2)}) %collective-permute-start.1) | collective-permute-done | bytes 131104 | tf_op jit(solution)/shard_map/ppermute | solution.py:63
  16.0 3.3 %collective-permute-start.5 = (bf16[16,4096]{1,0:T(8,128)(2,1)S(1)}, bf16[16,4096]{1,0:T(8,128)(2,1)S(1)}, u32[]{:S(2)}, u32[]{:S(2)}) collective-permute-start(bf16[16,4096]{1,0:T(8,128)(2,1)S(1)} %get-tuple-element.19), channel_id=1, source_target_pairs={{0,4},{1,5},{2,6},{3,7},{4,8},{5,9},{6,10},{7,11},{8,12},{9,13},{1... | collective-permute-start | bytes 393224 | tf_op jit(solution)/shard_map/ppermute | solution.py:63
  19.4 1.6 collective-permute-start.4
  21.8 1.5 collective-permute-start.7
  24.5 4.5 %collective-permute-done.4 = bf16[16,4096]{1,0:T(8,128)(2,1)S(1)} collective-permute-done((bf16[16,4096]{1,0:T(8,128)(2,1)S(1)}, bf16[16,4096]{1,0:T(8,128)(2,1)S(1)}, u32[]{:S(2)}, u32[]{:S(2)}) %collective-permute-start.4) | collective-permute-done | bytes 131104 | tf_op jit(solution)/shard_map/ppermute | solution.py:63
  30.0 5.1 %collective-permute-done.7 = bf16[4,16,4096]{2,1,0:T(8,128)(2,1)S(1)} collective-permute-done((bf16[4,16,4096]{2,1,0:T(8,128)(2,1)S(1)}, bf16[4,16,4096]{2,1,0:T(8,128)(2,1)S(1)}, u32[]{:S(2)}, u32[]{:S(2)}) %collective-permute-start.7) | collective-permute-done | bytes 524320 | tf_op jit(solution)/shard_map/ppermute | solution.py:63
  36.8 1.5 collective-permute-start.6
  39.3 1.2 copy-done.8
  40.6 1.2 copy-done.13
  41.8 14.3 %shard_map.103.rest_4_ = f32[2,256,1792]{2,1,0:T(8,128)S(1)} custom-call(bf16[128,4096]{1,0:T(8,128)(2,1)S(1)} %bitcast.99, bf16[128,4096]{1,0:T(8,128)(2,1)S(1)} %copy-done.13, bf16[2,8192,1792]{2,1,0:T(8,128)(2,1)} %up.5, bf16[2,8192,1792]{2,1,0:T(8,128)(2,1)} %up.5, bf16[2,8192,1792]{2,1,0:T(8,128)(2,1)} %up.5, bf16[2,8192,1792]{2,1,0:T(8,128)(2,1)} %up.5), custom_call_target="tpu_custom_call" | custom-call | flops 7516192768 | bytes 29360128 | tf_op jit(solution)/shard_map/pallas_call | solution.py:131
  56.1 1.8 copy-done.1
  58.0 2.1 %pad_maximum_fusion.1 = bf16[2,4,16,4096]{3,2,1,0:T(8,128)(2,1)} fusion(bf16[1,4,16,4096]{3,2,1,0:T(8,128)(2,1)S(1)} %bitcast.125, bf16[1,4,16,4096]{3,2,1,0:T(8,128)(2,1)} %bitcast.13), kind=kLoop, calls=%fused_computation.3 | loop fusion | flops 524288 | bytes 2097152 | tf_op jit(solution)/shard_map/stack | solution.py:514
  61.7 1.3 collective-permute-done.9.far.rest_11_
  63.1 1.2 copy-done.9
  64.3 1.2 copy-done.14
  65.5 2.5 %shard_map.108 = (bf16[256,512]{1,0:T(8,128)(2,1)S(1)}, f32[256,128]{1,0:T(8,128)S(1)}) custom-call(s32[8]{0:T(128)S(1)} %bitcast.114, s32[16]{0:T(128)S(1)} %get-tuple-element.36.places, s32[3]{0:T(128)S(1)} %pad_add_fusion.which, s32[256,1]{1,0:T(8,128)S(1)} %copy.20.seg, bf16[24,512,128]{2,1,0:T(8,128)(2,1)S(1)} %copy-done, ...), custom_call_target="tpu_custom_call" | custom-call | flops 268435456 | bytes 1048576 | tf_op jit(solution)/shard_map/pallas_call | solution.py:192
  70.6 4.1 %shard_map.104.rest_4_ = f32[2,256,1792]{2,1,0:T(8,128)S(1)} custom-call(bf16[128,4096]{1,0:T(8,128)(2,1)} %bitcast.15.near.rest_10_, bf16[128,4096]{1,0:T(8,128)(2,1)} %collective-permute-done.9.far.rest_11_, bf16[2,8192,1792]{2,1,0:T(8,128)(2,1)} %up.5, bf16[2,8192,1792]{2,1,0:T(8,128)(2,1)} %up.5, ...), custom_call_target="tpu_custom_call", output_to_operand_aliasing={{}: (6, {})} | custom-call | flops 1073741824 | bytes 4194304 | tf_op jit(solution)/shard_map/pallas_call | solution.py:131
  74.8 5.7 %shard_map.105.rest_4_ = f32[2,256,1792]{2,1,0:T(8,128)S(1)} custom-call(bf16[128,4096]{1,0:T(8,128)(2,1)} %bitcast.15.near.rest_10_, bf16[128,4096]{1,0:T(8,128)(2,1)} %collective-permute-done.9.far.rest_11_, bf16[2,8192,1792]{2,1,0:T(8,128)(2,1)} %up.5, bf16[2,8192,1792]{2,1,0:T(8,128)(2,1)} %up.5, ...), custom_call_target="tpu_custom_call", output_to_operand_aliasing={{}: (6, {})} | custom-call | flops 2147483648 | bytes 8388608 | tf_op jit(solution)/shard_map/pallas_call | solution.py:131
  80.6 2.1 %collective-permute-start.13 = (f32[128,128]{1,0:T(8,128)S(1)}, f32[128,128]{1,0:T(8,128)S(1)}, u32[]{:S(2)}, u32[]{:S(2)}) collective-permute-start(f32[128,128]{1,0:T(8,128)S(1)} %add.305), channel_id=1, source_target_pairs={{0,8},{1,9},{2,10},{3,11},{4,12},{5,13},{6,14},{7,15},{8,0},{9,1},... | collective-permute-start | bytes 196616 | tf_op jit(solution)/shard_map/ppermute | solution.py:89
  82.6 5.5 %shard_map.106.rest_4_ = f32[2,256,1792]{2,1,0:T(8,128)S(1)} custom-call(bf16[128,4096]{1,0:T(8,128)(2,1)} %bitcast.15.near.rest_10_, bf16[128,4096]{1,0:T(8,128)(2,1)} %collective-permute-done.9.far.rest_11_, bf16[2,8192,1792]{2,1,0:T(8,128)(2,1)} %up.5, bf16[2,8192,1792]{2,1,0:T(8,128)(2,1)} %up.5, ...), custom_call_target="tpu_custom_call", output_to_operand_aliasing={{}: (6, {})} | custom-call | flops 2147483648 | bytes 8388608 | tf_op jit(solution)/shard_map/pallas_call | solution.py:131
  88.4 5.7 %shard_map.107.base = f32[2,256,1792]{2,1,0:T(8,128)S(1)} custom-call(bf16[128,4096]{1,0:T(8,128)(2,1)} %bitcast.15.near.rest_10_, bf16[128,4096]{1,0:T(8,128)(2,1)} %collective-permute-done.9.far.rest_11_, bf16[2,8192,1792]{2,1,0:T(8,128)(2,1)} %up.5, bf16[2,8192,1792]{2,1,0:T(8,128)(2,1)} %up.5, ...), custom_call_target="tpu_custom_call", output_to_operand_aliasing={{}: (6, {})} | custom-call | flops 2147483648 | bytes 8388608 | tf_op jit(solution)/shard_map/pallas_call | solution.py:131
  95.8 7.6 %shard_map.109 = (bf16[256,1792]{1,0:T(8,128)(2,1)S(1)}, bf16[256,1792]{1,0:T(8,128)(2,1)S(1)}, f32[256,128]{1,0:T(8,128)S(1)}) custom-call(s32[8]{0:T(128)S(1)} %bitcast.115, s32[16]{0:T(128)S(1)} %get-tuple-element.36.places, f32[2,256,1792]{2,1,0:T(8,128)S(1)} %shard_map.107.base, bf16[256,1792]{1,0:T(8,128)(2,1)S(1)} %copy-done.15, ...), custom_call_target="tpu_custom_call" | custom-call | flops 1879048192 | bytes 10092544 | tf_op jit(solution)/shard_map/pallas_call | solution.py:259
  105.8 3.8 %shard_map.110.rest_0_ = f32[24,128,1792]{2,1,0:T(8,128)} custom-call(bf16[256,1792]{1,0:T(8,128)(2,1)S(1)} %get-tuple-element.25.dgate, bf16[256,1792]{1,0:T(8,128)(2,1)S(1)} %get-tuple-element.26.dup, bf16[256,256]{1,0:T(8,128)(2,1)S(1)} %fusion.10.order, bf16[256,128]{1,0:T(8,128)(2,1)S(1)} %bitcast.102, s32[1,256]{1,0:T(1,128)S(1)} %bitcast.107), custom_call_target="tpu_custom_call" | custom-call | flops 805306368 | bytes 6291456 | tf_op jit(solution)/shard_map/pallas_call | solution.py:316
  110.0 3.8 %shard_map.111.rest_0_ = f32[24,128,1792]{2,1,0:T(8,128)} custom-call(bf16[256,1792]{1,0:T(8,128)(2,1)S(1)} %get-tuple-element.25.dgate, bf16[256,1792]{1,0:T(8,128)(2,1)S(1)} %get-tuple-element.26.dup, bf16[256,256]{1,0:T(8,128)(2,1)S(1)} %fusion.10.order, bf16[256,128]{1,0:T(8,128)(2,1)S(1)} %bitcast.103, ...), custom_call_target="tpu_custom_call", output_to_operand_aliasing={{}: (5, {})} | custom-call | flops 805306368 | bytes 6291456 | tf_op jit(solution)/shard_map/pallas_call | solution.py:316
  113.9 2.4 %collective-permute-start.18 = (f32[128,128]{1,0:T(8,128)S(1)}, f32[128,128]{1,0:T(8,128)S(1)}, u32[]{:S(2)}, u32[]{:S(2)}) collective-permute-start(f32[128,128]{1,0:T(8,128)S(1)} %add.316), channel_id=1, source_target_pairs={{0,8},{1,9},{2,10},{3,11},{4,12},{5,13},{6,14},{7,15},{8,0},{9,1},... | collective-permute-start | bytes 196616 | tf_op jit(solution)/shard_map/ppermute | solution.py:89
  116.3 5.0 %shard_map.112 = f32[24,128,1792]{2,1,0:T(8,128)} custom-call(bf16[256,1792]{1,0:T(8,128)(2,1)S(1)} %get-tuple-element.25.dgate, bf16[256,1792]{1,0:T(8,128)(2,1)S(1)} %get-tuple-element.26.dup, bf16[256,256]{1,0:T(8,128)(2,1)S(1)} %fusion.10.order, bf16[256,128]{1,0:T(8,128)(2,1)S(1)} %bitcast.104, ...), custom_call_target="tpu_custom_call", output_to_operand_aliasing={{}: (5, {})} | custom-call | flops 1207959552 | bytes 9437184 | tf_op jit(solution)/shard_map/pallas_call | solution.py:316
  122.7 1.5 shard_map.113.side
  124.3 15.1 %shard_map.114 = bf16[256,4096]{1,0:T(8,128)(2,1)S(1)} custom-call(s32[1]{0:T(128)} %bitcast.at, bf16[2,8192,1792]{2,1,0:T(8,128)(2,1)} %up.5, bf16[2,8192,1792]{2,1,0:T(8,128)(2,1)} %up.5, bf16[256,1792]{1,0:T(8,128)(2,1)S(1)} %get-tuple-element.25.dgate, bf16[256,1792]{1,0:T(8,128)(2,1)S(1)} %get-tuple-element.26.dup, f32[512,256]{1,0:T(8,128)S(1)} %shard_map.113.side), custom_call_target="tpu_custom_call" | custom-call | flops 7516192768 | bytes 29360128 | tf_op jit(solution)/shard_map/pallas_call | solution.py:422
  139.5 1.6 fusion.31
  141.3 2.7 %collective-permute-done.20 = bf16[2,4,16,4096]{3,2,1,0:T(8,128)(2,1)} collective-permute-done((bf16[2,4,16,4096]{3,2,1,0:T(8,128)(2,1)}, bf16[2,4,16,4096]{3,2,1,0:T(8,128)(2,1)}, u32[]{:S(2)}, u32[]{:S(2)}) %collective-permute-start.20) | collective-permute-done | bytes 1048608 | tf_op jit(solution)/shard_map/ppermute | solution.py:63
  144.1 1.8 fusion
  147.0 8.1 %shard_map.115 = bf16[256,2048]{1,0:T(8,128)(2,1)S(1)} custom-call(s32[1]{0:T(128)} %bitcast.at, bf16[2,8192,1792]{2,1,0:T(8,128)(2,1)} %up.5, bf16[2,8192,1792]{2,1,0:T(8,128)(2,1)} %up.5, bf16[256,1792]{1,0:T(8,128)(2,1)S(1)} %copy-done.4, bf16[256,1792]{1,0:T(8,128)(2,1)S(1)} %copy-done.6, f32[512,256]{1,0:T(8,128)S(1)} %copy-done.11), custom_call_target="tpu_custom_call" | custom-call | flops 3758096384 | bytes 14680064 | tf_op jit(solution)/shard_map/pallas_call | solution.py:422
  155.3 4.6 %collective-permute-done.21 = bf16[4,16,4096]{2,1,0:T(8,128)(2,1)S(1)} collective-permute-done((bf16[4,16,4096]{2,1,0:T(8,128)(2,1)S(1)}, bf16[4,16,4096]{2,1,0:T(8,128)(2,1)S(1)}, u32[]{:S(2)}, u32[]{:S(2)}) %collective-permute-start.21) | collective-permute-done | bytes 524320 | tf_op jit(solution)/shard_map/ppermute | solution.py:63
  160.1 8.4 %shard_map.116 = bf16[256,2048]{1,0:T(8,128)(2,1)S(1)} custom-call(s32[1]{0:T(128)} %bitcast.at, bf16[2,8192,1792]{2,1,0:T(8,128)(2,1)} %up.5, bf16[2,8192,1792]{2,1,0:T(8,128)(2,1)} %up.5, bf16[256,1792]{1,0:T(8,128)(2,1)S(1)} %copy-done.4, bf16[256,1792]{1,0:T(8,128)(2,1)S(1)} %copy-done.6, f32[512,256]{1,0:T(8,128)S(1)} %copy-done.11), custom_call_target="tpu_custom_call" | custom-call | flops 3758096384 | bytes 14680064 | tf_op jit(solution)/shard_map/pallas_call | solution.py:422
  168.6 1.7 collective-permute-start.24
  172.6 5.3 %shard_map.117 = f32[24,512,128]{2,1,0:T(8,128)} custom-call(bf16[256,512]{1,0:T(8,128)(2,1)S(1)} %copy-done.17, bf16[256,256]{1,0:T(8,128)(2,1)S(1)} %fusion.10.order, bf16[256,128]{1,0:T(8,128)(2,1)S(1)} %bitcast.106, s32[256,1]{1,0:T(8,128)S(1)} %copy.22.adapter), custom_call_target="tpu_custom_call" | custom-call | flops 805306368 | bytes 6291456 | tf_op jit(solution)/shard_map/pallas_call | solution.py:346
  177.9 5.0 %collective-permute-done.23 = bf16[16,4096]{1,0:T(8,128)(2,1)S(1)} collective-permute-done((bf16[16,4096]{1,0:T(8,128)(2,1)S(1)}, bf16[16,4096]{1,0:T(8,128)(2,1)S(1)}, u32[]{:S(2)}, u32[]{:S(2)}) %collective-permute-start.23) | collective-permute-done | bytes 131104 | tf_op jit(solution)/shard_map/ppermute | solution.py:63
  185.2 1.3 collective-permute-start.28
  186.4 1.9 collective-permute-start.27
  188.4 2.9 %collective-permute-done.31 = bf16[4,16,2048]{2,1,0:T(8,128)(2,1)S(1)} collective-permute-done((bf16[4,16,2048]{2,1,0:T(8,128)(2,1)S(1)}, bf16[4,16,2048]{2,1,0:T(8,128)(2,1)S(1)}, u32[]{:S(2)}, u32[]{:S(2)}) %collective-permute-start.31) | collective-permute-done | bytes 262176 | tf_op jit(solution)/shard_map/ppermute | solution.py:63
  191.5 1.6 collective-permute-start.33
  193.0 1.9 collective-permute-start.32
  195.7 1.7 collective-permute-done.33
  197.4 1.7 collective-permute-done.32
  (167 shorter events, 25.4 us)
Async XLA Ops:
  0.6 35.8 %copy-start.25 = (s32[1,8]{1,0:T(1,128)S(1)}, s32[1,8]{1,0:T(1,128)}, u32[]{:S(2)}) copy-start(s32[1,8]{1,0:T(1,128)} %param.14) | copy-start | bytes 100
  1.6 9.5 %collective-permute-start.2 = (bf16[16,4096]{1,0:T(8,128)(2,1)S(1)}, bf16[16,4096]{1,0:T(8,128)(2,1)S(1)}, u32[]{:S(2)}, u32[]{:S(2)}) collective-permute-start(bf16[16,4096]{1,0:T(8,128)(2,1)S(1)} %get-tuple-element.54), channel_id=1, source_target_pairs={{0,4},{1,5},{2,6},{3,7},{4,8},{5,9},{6,10},{7,11},{8,12},{9,13},{1... | collective-permute-start | bytes 393224 | tf_op jit(solution)/shard_map/ppermute | solution.py:63
  4.7 11.2 %collective-permute-start.1 = (bf16[16,4096]{1,0:T(8,128)(2,1)S(1)}, bf16[16,4096]{1,0:T(8,128)(2,1)S(1)}, u32[]{:S(2)}, u32[]{:S(2)}) collective-permute-start(bf16[16,4096]{1,0:T(8,128)(2,1)S(1)} %get-tuple-element.54), channel_id=1, source_target_pairs={{0,8},{1,9},{2,10},{3,11},{4,12},{5,13},{6,14},{7,15},{8,0},{9,1},... | collective-permute-start | bytes 393224 | tf_op jit(solution)/shard_map/ppermute | solution.py:63
  7.3 8.6 %collective-permute-start = (bf16[16,4096]{1,0:T(8,128)(2,1)S(1)}, bf16[16,4096]{1,0:T(8,128)(2,1)S(1)}, u32[]{:S(2)}, u32[]{:S(2)}) collective-permute-start(bf16[16,4096]{1,0:T(8,128)(2,1)S(1)} %get-tuple-element.54), channel_id=1, source_target_pairs={{0,12},{1,13},{2,14},{3,15},{4,0},{5,1},{6,2},{7,3},{8,4},{9,5},{1... | collective-permute-start | bytes 393224 | tf_op jit(solution)/shard_map/ppermute | solution.py:63
  16.0 8.5 %collective-permute-start.5 = (bf16[16,4096]{1,0:T(8,128)(2,1)S(1)}, bf16[16,4096]{1,0:T(8,128)(2,1)S(1)}, u32[]{:S(2)}, u32[]{:S(2)}) collective-permute-start(bf16[16,4096]{1,0:T(8,128)(2,1)S(1)} %get-tuple-element.19), channel_id=1, source_target_pairs={{0,4},{1,5},{2,6},{3,7},{4,8},{5,9},{6,10},{7,11},{8,12},{9,13},{1... | collective-permute-start | bytes 393224 | tf_op jit(solution)/shard_map/ppermute | solution.py:63
  19.4 9.7 %collective-permute-start.4 = (bf16[16,4096]{1,0:T(8,128)(2,1)S(1)}, bf16[16,4096]{1,0:T(8,128)(2,1)S(1)}, u32[]{:S(2)}, u32[]{:S(2)}) collective-permute-start(bf16[16,4096]{1,0:T(8,128)(2,1)S(1)} %get-tuple-element.19), channel_id=1, source_target_pairs={{0,8},{1,9},{2,10},{3,11},{4,12},{5,13},{6,14},{7,15},{8,0},{9,1},... | collective-permute-start | bytes 393224 | tf_op jit(solution)/shard_map/ppermute | solution.py:63
  21.0 8.1 %collective-permute-start.3 = (bf16[16,4096]{1,0:T(8,128)(2,1)S(1)}, bf16[16,4096]{1,0:T(8,128)(2,1)S(1)}, u32[]{:S(2)}, u32[]{:S(2)}) collective-permute-start(bf16[16,4096]{1,0:T(8,128)(2,1)S(1)} %get-tuple-element.19), channel_id=1, source_target_pairs={{0,12},{1,13},{2,14},{3,15},{4,0},{5,1},{6,2},{7,3},{8,4},{9,5},{1... | collective-permute-start | bytes 393224 | tf_op jit(solution)/shard_map/ppermute | solution.py:63
  21.8 13.3 %collective-permute-start.7 = (bf16[4,16,4096]{2,1,0:T(8,128)(2,1)S(1)}, bf16[4,16,4096]{2,1,0:T(8,128)(2,1)S(1)}, u32[]{:S(2)}, u32[]{:S(2)}) collective-permute-start(bf16[4,16,4096]{2,1,0:T(8,128)(2,1)S(1)} %pad_maximum_fusion.2), channel_id=1, source_target_pairs={{0,2},{1,3},{2,0},{3,1},{4,6},{5,7},{6,4},{7,5},{8,10},{9,11},{10,... | collective-permute-start | bytes 1572872 | tf_op jit(solution)/shard_map/ppermute | solution.py:63
  35.2 3.2 %collective-permute-start.8 = (bf16[128,4096]{1,0:T(8,128)(2,1)S(1)}, bf16[128,4096]{1,0:T(8,128)(2,1)S(1)}, u32[]{:S(2)}, u32[]{:S(2)}) collective-permute-start(bf16[128,4096]{1,0:T(8,128)(2,1)S(1)} %bitcast.98), channel_id=1, source_target_pairs={{0,1},{1,0},{2,3},{3,2},{4,5},{5,4},{6,7},{7,6},{8,9},{9,8},{10,11... | collective-permute-start | bytes 3145736 | tf_op jit(solution)/shard_map/ppermute | solution.py:63
  36.7 23.8 %copy-start.18 = (s32[256]{0:T(256)}, s32[256]{0:T(256)S(1)}, u32[]{:S(2)}) copy-start(s32[256]{0:T(256)S(1)} %convert_reduce_fusion) | copy-start | bytes 3076
  36.8 24.0 %copy-start.20 = (s32[1,8]{1,0:T(1,128)S(1)}, s32[1,8]{1,0:T(1,128)}, u32[]{:S(2)}) copy-start(s32[1,8]{1,0:T(1,128)} %param.13) | copy-start | bytes 100
  36.8 24.1 %copy-start.26 = (s32[24]{0:T(128)S(1)}, s32[24]{0:T(128)}, u32[]{:S(2)}) copy-start(s32[24]{0:T(128)} %param.15) | copy-start | bytes 292
  36.8 21.1 %collective-permute-start.6 = (bf16[4,16,4096]{2,1,0:T(8,128)(2,1)}, bf16[4,16,4096]{2,1,0:T(8,128)(2,1)S(1)}, u32[]{:S(2)}, u32[]{:S(2)}) collective-permute-start(bf16[4,16,4096]{2,1,0:T(8,128)(2,1)} %pad_maximum_fusion.3), channel_id=1, source_target_pairs={{0,2},{1,3},{2,0},{3,1},{4,6},{5,7},{6,4},{7,5},{8,10},{9,11},{10,... | collective-permute-start | bytes 1572872 | tf_op jit(solution)/shard_map/ppermute | solution.py:63
  41.8 21.3 %copy-start = (bf16[24,512,128]{2,1,0:T(8,128)(2,1)S(1)}, bf16[24,512,128]{2,1,0:T(8,128)(2,1)}, u32[]{:S(2)}) copy-start(bf16[24,512,128]{2,1,0:T(8,128)(2,1)} %rest_7_.5) | copy-start | bytes 9437188
  60.1 3.0 %collective-permute-start.9 = (bf16[128,4096]{1,0:T(8,128)(2,1)}, bf16[128,4096]{1,0:T(8,128)(2,1)}, u32[]{:S(2)}, u32[]{:S(2)}) collective-permute-start(bf16[128,4096]{1,0:T(8,128)(2,1)} %bitcast.15.near.rest_10_), channel_id=1, source_target_pairs={{0,1},{1,0},{2,3},{3,2},{4,5},{5,4},{6,7},{7,6},{8,9},{9,8},{10,11... | collective-permute-start | bytes 3145736 | tf_op jit(solution)/shard_map/ppermute | solution.py:63
  68.1 1.3 collective-permute-start.10
  69.4 5.3 %collective-permute-start.11 = (f32[128,128]{1,0:T(8,128)S(1)}, f32[128,128]{1,0:T(8,128)S(1)}, u32[]{:S(2)}, u32[]{:S(2)}) collective-permute-start(f32[128,128]{1,0:T(8,128)S(1)} %slice_add_fusion.1), channel_id=1, source_target_pairs={{0,2},{1,3},{2,0},{3,1},{4,6},{5,7},{6,4},{7,5},{8,10},{9,11},{10,... | collective-permute-start | bytes 196616 | tf_op jit(solution)/shard_map/ppermute | solution.py:89
  74.7 5.8 %collective-permute-start.12 = (f32[128,128]{1,0:T(8,128)S(1)}, f32[128,128]{1,0:T(8,128)S(1)}, u32[]{:S(2)}, u32[]{:S(2)}) collective-permute-start(f32[128,128]{1,0:T(8,128)S(1)} %add.304), channel_id=1, source_target_pairs={{0,4},{1,5},{2,6},{3,7},{4,0},{5,1},{6,2},{7,3},{8,12},{9,13},{10,... | collective-permute-start | bytes 196616 | tf_op jit(solution)/shard_map/ppermute | solution.py:89
  80.5 7.6 %copy-start.22 = (s32[128]{0:T(128)S(1)}, s32[128]{0:T(128)}, u32[]{:S(2)}) copy-start(s32[128]{0:T(128)} %copy-done.21) | copy-start | bytes 1540
  80.5 7.6 %copy-start.23 = (f32[128]{0:T(128)S(1)}, f32[128]{0:T(128)}, u32[]{:S(2)}) copy-start(f32[128]{0:T(128)} %convert_divide_fusion) | copy-start | bytes 1540
  80.6 7.6 %copy-start.24 = (s32[128]{0:T(128)S(1)}, s32[128]{0:T(128)}, u32[]{:S(2)}) copy-start(s32[128]{0:T(128)} %and_select_fusion) | copy-start | bytes 1540
  80.6 7.6 %collective-permute-start.13 = (f32[128,128]{1,0:T(8,128)S(1)}, f32[128,128]{1,0:T(8,128)S(1)}, u32[]{:S(2)}, u32[]{:S(2)}) collective-permute-start(f32[128,128]{1,0:T(8,128)S(1)} %add.305), channel_id=1, source_target_pairs={{0,8},{1,9},{2,10},{3,11},{4,12},{5,13},{6,14},{7,15},{8,0},{9,1},... | collective-permute-start | bytes 196616 | tf_op jit(solution)/shard_map/ppermute | solution.py:89
  88.3 5.7 %collective-permute-start.14 = (bf16[128,128]{1,0:T(8,128)(2,1)S(1)}, bf16[128,128]{1,0:T(8,128)(2,1)S(1)}, u32[]{:S(2)}, u32[]{:S(2)}) collective-permute-start(bf16[128,128]{1,0:T(8,128)(2,1)S(1)} %fusion.17), channel_id=1, source_target_pairs={{0,1},{1,0},{2,3},{3,2},{4,5},{5,4},{6,7},{7,6},{8,9},{9,8},{10,11... | collective-permute-start | bytes 98312 | tf_op jit(solution)/shard_map/ppermute | solution.py:63
  95.8 7.7 %copy-start.19 = (s32[256]{0:T(256)S(1)}, s32[256]{0:T(256)}, u32[]{:S(2)}) copy-start(s32[256]{0:T(256)} %copy-done.18) | copy-start | bytes 3076
  103.4 20.9 %copy-start.3 = (bf16[256,1792]{1,0:T(8,128)(2,1)}, bf16[256,1792]{1,0:T(8,128)(2,1)S(1)}, u32[]{:S(2)}) copy-start(bf16[256,1792]{1,0:T(8,128)(2,1)S(1)} %get-tuple-element.25.dgate) | copy-start | bytes 2752516
  103.4 20.9 %copy-start.5 = (bf16[256,1792]{1,0:T(8,128)(2,1)}, bf16[256,1792]{1,0:T(8,128)(2,1)S(1)}, u32[]{:S(2)}) copy-start(bf16[256,1792]{1,0:T(8,128)(2,1)S(1)} %get-tuple-element.26.dup) | copy-start | bytes 2752516
  103.4 1.3 collective-permute-start.15
  104.7 4.9 %collective-permute-start.16 = (f32[128,128]{1,0:T(8,128)S(1)}, f32[128,128]{1,0:T(8,128)S(1)}, u32[]{:S(2)}, u32[]{:S(2)}) collective-permute-start(f32[128,128]{1,0:T(8,128)S(1)} %slice_add_fusion), channel_id=1, source_target_pairs={{0,2},{1,3},{2,0},{3,1},{4,6},{5,7},{6,4},{7,5},{8,10},{9,11},{10,... | collective-permute-start | bytes 196616 | tf_op jit(solution)/shard_map/ppermute | solution.py:89
  109.6 4.3 %collective-permute-start.17 = (f32[128,128]{1,0:T(8,128)S(1)}, f32[128,128]{1,0:T(8,128)S(1)}, u32[]{:S(2)}, u32[]{:S(2)}) collective-permute-start(f32[128,128]{1,0:T(8,128)S(1)} %add.315), channel_id=1, source_target_pairs={{0,4},{1,5},{2,6},{3,7},{4,0},{5,1},{6,2},{7,3},{8,12},{9,13},{10,... | collective-permute-start | bytes 196616 | tf_op jit(solution)/shard_map/ppermute | solution.py:89
  113.9 7.4 %collective-permute-start.18 = (f32[128,128]{1,0:T(8,128)S(1)}, f32[128,128]{1,0:T(8,128)S(1)}, u32[]{:S(2)}, u32[]{:S(2)}) collective-permute-start(f32[128,128]{1,0:T(8,128)S(1)} %add.316), channel_id=1, source_target_pairs={{0,8},{1,9},{2,10},{3,11},{4,12},{5,13},{6,14},{7,15},{8,0},{9,1},... | collective-permute-start | bytes 196616 | tf_op jit(solution)/shard_map/ppermute | solution.py:89
  121.5 1.3 collective-permute-start.19
  124.3 15.2 %copy-start.10 = (f32[512,256]{1,0:T(8,128)}, f32[512,256]{1,0:T(8,128)S(1)}, u32[]{:S(2)}) copy-start(f32[512,256]{1,0:T(8,128)S(1)} %shard_map.113.side) | copy-start | bytes 1572868
  139.5 7.5 %copy-start.4 = (bf16[256,1792]{1,0:T(8,128)(2,1)S(1)}, bf16[256,1792]{1,0:T(8,128)(2,1)}, u32[]{:S(2)}) copy-start(bf16[256,1792]{1,0:T(8,128)(2,1)} %copy-done.3) | copy-start | bytes 2752516
  141.1 3.0 %collective-permute-start.20 = (bf16[2,4,16,4096]{3,2,1,0:T(8,128)(2,1)}, bf16[2,4,16,4096]{3,2,1,0:T(8,128)(2,1)}, u32[]{:S(2)}, u32[]{:S(2)}) collective-permute-start(bf16[2,4,16,4096]{3,2,1,0:T(8,128)(2,1)} %bitcast.31), channel_id=1, source_target_pairs={{0,1},{1,0},{2,3},{3,2},{4,5},{5,4},{6,7},{7,6},{8,9},{9,8},{10,11... | collective-permute-start | bytes 3145736 | tf_op jit(solution)/shard_map/ppermute | solution.py:63
  145.9 14.0 %collective-permute-start.21 = (bf16[4,16,4096]{2,1,0:T(8,128)(2,1)S(1)}, bf16[4,16,4096]{2,1,0:T(8,128)(2,1)S(1)}, u32[]{:S(2)}, u32[]{:S(2)}) collective-permute-start(bf16[4,16,4096]{2,1,0:T(8,128)(2,1)S(1)} %slice_bitcast_fusion), channel_id=1, source_target_pairs={{0,2},{1,3},{2,0},{3,1},{4,6},{5,7},{6,4},{7,5},{8,10},{9,11},{10,... | collective-permute-start | bytes 1572872 | tf_op jit(solution)/shard_map/ppermute | solution.py:63
  155.3 16.0 %collective-permute-start.25 = (bf16[2,4,16,2048]{3,2,1,0:T(8,128)(2,1)S(1)}, bf16[2,4,16,2048]{3,2,1,0:T(8,128)(2,1)S(1)}, u32[]{:S(2)}, u32[]{:S(2)}) collective-permute-start(bf16[2,4,16,2048]{3,2,1,0:T(8,128)(2,1)S(1)} %bitcast.123), channel_id=1, source_target_pairs={{0,1},{1,0},{2,3},{3,2},{4,5},{5,4},{6,7},{7,6},{8,9},{9,8},{10,11... | collective-permute-start | bytes 1572872 | tf_op jit(solution)/shard_map/ppermute | solution.py:63
  168.5 14.5 %collective-permute-start.30 = (bf16[2,4,16,2048]{3,2,1,0:T(8,128)(2,1)S(1)}, bf16[2,4,16,2048]{3,2,1,0:T(8,128)(2,1)S(1)}, u32[]{:S(2)}, u32[]{:S(2)}) collective-permute-start(bf16[2,4,16,2048]{3,2,1,0:T(8,128)(2,1)S(1)} %bitcast.122), channel_id=1, source_target_pairs={{0,1},{1,0},{2,3},{3,2},{4,5},{5,4},{6,7},{7,6},{8,9},{9,8},{10,11... | collective-permute-start | bytes 1572872 | tf_op jit(solution)/shard_map/ppermute | solution.py:63
  168.6 9.3 %collective-permute-start.24 = (bf16[16,4096]{1,0:T(8,128)(2,1)S(1)}, bf16[16,4096]{1,0:T(8,128)(2,1)S(1)}, u32[]{:S(2)}, u32[]{:S(2)}) collective-permute-start(bf16[16,4096]{1,0:T(8,128)(2,1)S(1)} %get-tuple-element.45), channel_id=1, source_target_pairs={{0,12},{1,13},{2,14},{3,15},{4,0},{5,1},{6,2},{7,3},{8,4},{9,5},{1... | collective-permute-start | bytes 393224 | tf_op jit(solution)/shard_map/ppermute | solution.py:63
  170.4 12.5 %collective-permute-start.23 = (bf16[16,4096]{1,0:T(8,128)(2,1)S(1)}, bf16[16,4096]{1,0:T(8,128)(2,1)S(1)}, u32[]{:S(2)}, u32[]{:S(2)}) collective-permute-start(bf16[16,4096]{1,0:T(8,128)(2,1)S(1)} %get-tuple-element.46), channel_id=1, source_target_pairs={{0,8},{1,9},{2,10},{3,11},{4,12},{5,13},{6,14},{7,15},{8,0},{9,1},... | collective-permute-start | bytes 393224 | tf_op jit(solution)/shard_map/ppermute | solution.py:63
  170.6 12.3 %collective-permute-start.22 = (bf16[16,4096]{1,0:T(8,128)(2,1)S(1)}, bf16[16,4096]{1,0:T(8,128)(2,1)S(1)}, u32[]{:S(2)}, u32[]{:S(2)}) collective-permute-start(bf16[16,4096]{1,0:T(8,128)(2,1)S(1)} %get-tuple-element.44), channel_id=1, source_target_pairs={{0,4},{1,5},{2,6},{3,7},{4,8},{5,9},{6,10},{7,11},{8,12},{9,13},{1... | collective-permute-start | bytes 393224 | tf_op jit(solution)/shard_map/ppermute | solution.py:63
  171.5 11.5 %collective-permute-start.26 = (bf16[4,16,2048]{2,1,0:T(8,128)(2,1)S(1)}, bf16[4,16,2048]{2,1,0:T(8,128)(2,1)S(1)}, u32[]{:S(2)}, u32[]{:S(2)}) collective-permute-start(bf16[4,16,2048]{2,1,0:T(8,128)(2,1)S(1)} %slice_bitcast_fusion.4), channel_id=1, source_target_pairs={{0,2},{1,3},{2,0},{3,1},{4,6},{5,7},{6,4},{7,5},{8,10},{9,11},{10,... | collective-permute-start | bytes 786440 | tf_op jit(solution)/shard_map/ppermute | solution.py:63
  183.2 8.1 %collective-permute-start.31 = (bf16[4,16,2048]{2,1,0:T(8,128)(2,1)S(1)}, bf16[4,16,2048]{2,1,0:T(8,128)(2,1)S(1)}, u32[]{:S(2)}, u32[]{:S(2)}) collective-permute-start(bf16[4,16,2048]{2,1,0:T(8,128)(2,1)S(1)} %slice_bitcast_fusion.2), channel_id=1, source_target_pairs={{0,2},{1,3},{2,0},{3,1},{4,6},{5,7},{6,4},{7,5},{8,10},{9,11},{10,... | collective-permute-start | bytes 786440 | tf_op jit(solution)/shard_map/ppermute | solution.py:63
  184.4 8.7 %collective-permute-start.29 = (bf16[16,2048]{1,0:T(8,128)(2,1)S(1)}, bf16[16,2048]{1,0:T(8,128)(2,1)S(1)}, u32[]{:S(2)}, u32[]{:S(2)}) collective-permute-start(bf16[16,2048]{1,0:T(8,128)(2,1)S(1)} %get-tuple-element.48), channel_id=1, source_target_pairs={{0,12},{1,13},{2,14},{3,15},{4,0},{5,1},{6,2},{7,3},{8,4},{9,5},{1... | collective-permute-start | bytes 196616 | tf_op jit(solution)/shard_map/ppermute | solution.py:63
  185.2 9.8 %collective-permute-start.28 = (bf16[16,2048]{1,0:T(8,128)(2,1)S(1)}, bf16[16,2048]{1,0:T(8,128)(2,1)S(1)}, u32[]{:S(2)}, u32[]{:S(2)}) collective-permute-start(bf16[16,2048]{1,0:T(8,128)(2,1)S(1)} %get-tuple-element.49), channel_id=1, source_target_pairs={{0,8},{1,9},{2,10},{3,11},{4,12},{5,13},{6,14},{7,15},{8,0},{9,1},... | collective-permute-start | bytes 196616 | tf_op jit(solution)/shard_map/ppermute | solution.py:63
  186.4 8.6 %collective-permute-start.27 = (bf16[16,2048]{1,0:T(8,128)(2,1)S(1)}, bf16[16,2048]{1,0:T(8,128)(2,1)S(1)}, u32[]{:S(2)}, u32[]{:S(2)}) collective-permute-start(bf16[16,2048]{1,0:T(8,128)(2,1)S(1)} %get-tuple-element.47), channel_id=1, source_target_pairs={{0,4},{1,5},{2,6},{3,7},{4,8},{5,9},{6,10},{7,11},{8,12},{9,13},{1... | collective-permute-start | bytes 196616 | tf_op jit(solution)/shard_map/ppermute | solution.py:63
  191.4 4.3 %collective-permute-start.34 = (bf16[16,2048]{1,0:T(8,128)(2,1)S(1)}, bf16[16,2048]{1,0:T(8,128)(2,1)S(1)}, u32[]{:S(2)}, u32[]{:S(2)}) collective-permute-start(bf16[16,2048]{1,0:T(8,128)(2,1)S(1)} %get-tuple-element.51), channel_id=1, source_target_pairs={{0,12},{1,13},{2,14},{3,15},{4,0},{5,1},{6,2},{7,3},{8,4},{9,5},{1... | collective-permute-start | bytes 196616 | tf_op jit(solution)/shard_map/ppermute | solution.py:63
  191.5 6.0 %collective-permute-start.33 = (bf16[16,2048]{1,0:T(8,128)(2,1)S(1)}, bf16[16,2048]{1,0:T(8,128)(2,1)S(1)}, u32[]{:S(2)}, u32[]{:S(2)}) collective-permute-start(bf16[16,2048]{1,0:T(8,128)(2,1)S(1)} %get-tuple-element.52), channel_id=1, source_target_pairs={{0,8},{1,9},{2,10},{3,11},{4,12},{5,13},{6,14},{7,15},{8,0},{9,1},... | collective-permute-start | bytes 196616 | tf_op jit(solution)/shard_map/ppermute | solution.py:63
  193.0 6.1 %collective-permute-start.32 = (bf16[16,2048]{1,0:T(8,128)(2,1)S(1)}, bf16[16,2048]{1,0:T(8,128)(2,1)S(1)}, u32[]{:S(2)}, u32[]{:S(2)}) collective-permute-start(bf16[16,2048]{1,0:T(8,128)(2,1)S(1)} %get-tuple-element.50), channel_id=1, source_target_pairs={{0,4},{1,5},{2,6},{3,7},{4,8},{5,9},{6,10},{7,11},{8,12},{9,13},{1... | collective-permute-start | bytes 196616 | tf_op jit(solution)/shard_map/ppermute | solution.py:63
  (17 other events, 65.9 us)

commit v4 on v3

--- a/solution.py
+++ b/solution.py
@@ -1,4 +1,5 @@
 import functools
+import math
 
 import jax
 import jax.numpy as jnp
@@ -7,8 +8,8 @@
 from jax.experimental.pallas import tpu as pltpu
 from jax.sharding import PartitionSpec as P
 
-GATHER_CHUNKS = 2
-SUM_SHARES = (4, 2, 2)
+GATHER_SHARES = (3, 5)
+SUM_SHARES = (3, 3, 2)
 MIB = 1024 * 1024
 BF16 = jnp.bfloat16
 F32 = jnp.float32
@@ -101,55 +102,64 @@
         return (((cs - core) % c * b + (bs - inner) % b) * a + (zs - outer) % a).reshape(-1)
 
 
-def forward_kernel(near, far, *rest):
+def forward_kernel(pieces, blocks, *rest):
+    x = jnp.concatenate([v[...] for v in rest[:pieces]], axis=0)
+    weights = rest[pieces : pieces + 2 * blocks]
+    rest = rest[pieces + 2 * blocks :]
     out = rest[-1]
-    x = jnp.concatenate([near[...], far[...]], axis=0)
-    depth = x.shape[1] // 2
+    depth = weights[0].shape[1]
     for i in range(2):
-        part = dot(x[:, :depth], rest[2 * i][0]) + dot(x[:, depth:], rest[2 * i + 1][0])
-        out[i] = part if len(rest) == 5 else rest[4][i] + part
-
-
-def forward_chunk(near, far, frozen, start, first, tiles):
-    half, step = near.shape
+        part = sum(
+            dot(x[:, h * depth : (h + 1) * depth], weights[i * blocks + h][0])
+            for h in range(blocks)
+        )
+        out[i] = part if len(rest) == 1 else rest[0][i] + part
+
+
+def forward_chunk(pieces, frozen, start, first, tiles):
+    step = pieces[0].shape[1]
+    tokens = sum(v.shape[0] for v in pieces)
     hidden = frozen.shape[2]
     tile = tile_of(hidden, 256)
-    depth = step // 2
+    depth = math.gcd(first, step)
+    blocks = step // depth
     low, high = tiles
-    across = pl.BlockSpec((2, 2 * half, tile), lambda n: (0, 0, low + n))
+    across = pl.BlockSpec((2, tokens, tile), lambda n: (0, 0, low + n))
 
     def weight(i, h):
         return pl.BlockSpec((1, depth, tile), lambda n: (i, first // depth + h, low + n))
 
-    operands = [near, far] + [frozen] * 4
-    specs = [pl.BlockSpec((half, step), lambda n: (0, 0))] * 2
-    specs += [weight(i, h) for i in range(2) for h in range(2)]
+    operands = [*pieces] + [frozen] * (2 * blocks)
+    specs = [pl.BlockSpec(v.shape, lambda n: (0, 0)) for v in pieces]
+    specs += [weight(i, h) for i in range(2) for h in range(blocks)]
     if start is not None:
         operands.append(start)
         specs.append(across)
     count = high - low
     return pl.pallas_call(
-        forward_kernel,
+        functools.partial(forward_kernel, len(pieces), blocks),
         grid=(count,),
         in_specs=specs,
         out_specs=across,
-        out_shape=jax.ShapeDtypeStruct((2, 2 * half, hidden), F32),
-        input_output_aliases={} if start is None else {6: 0},
-        compiler_params=params(32),
-        cost_estimate=cost(8 * half * step * tile * count, 4 * step * tile * count),
+        out_shape=jax.ShapeDtypeStruct((2, tokens, hidden), F32),
+        input_output_aliases={} if start is None else {len(operands) - 1: 0},
+        compiler_params=params(24),
+        cost_estimate=cost(4 * tokens * step * tile * count, 4 * step * tile * count),
     )(*operands)
 
 
-def low_in_kernel(segments, rows, adapters, places, which, seg, *rest):
+def low_in_kernel(segments, chunks, rows, adapters, places, which, seg, *rest):
     factors, rest = rest[:segments], rest[segments:]
-    pairs, (columns, out) = rest[:-2], rest[-2:]
-    half = columns.shape[0] // 2
-    for q in range(len(pairs) // 2):
+    cuts, (columns, out) = rest[:-2], rest[-2:]
+    pieces = len(cuts) // chunks
+    for q in range(chunks):
 
         @pl.when(which[0] == q)
         def _():
-            columns[:half] = pairs[2 * q][...]
-            columns[half:] = pairs[2 * q + 1][...]
+            first = 0
+            for v in cuts[q * pieces : (q + 1) * pieces]:
+                columns[first : first + v.shape[0]] = v[...]
+                first += v.shape[0]
 
     total = jnp.zeros(out.shape, F32)
     for s in range(segments):
@@ -170,40 +180,43 @@
     return pl.BlockSpec((1,) + shape[1:], lambda *a: (a[-2][s], 0, 0))
 
 
-def low_in_partial(pairs, seg, down, adapters, places, index, rows):
+def low_in_partial(chunks, seg, down, adapters, places, index, rows):
     segments = adapters.shape[0]
     shard, wide = down.shape[1:]
-    half, step = pairs[0][0].shape
-    per = step // shard
+    tokens = seg.shape[0]
     if shard % 128:
-        joined = [jnp.concatenate(side, axis=1) for side in zip(*pairs)]
-        pairs = [[lax.dynamic_slice_in_dim(v, index * shard, shard, 1) for v in joined]]
+        joined = [jnp.concatenate(piece, axis=1) for piece in zip(*chunks)]
+        chunks = [[lax.dynamic_slice_in_dim(v, index * shard, shard, 1) for v in joined]]
         which = jnp.zeros((1,), jnp.int32)
-        cuts = [pl.BlockSpec((half, shard), lambda *a: (0, 0))] * 2
+        cuts = [pl.BlockSpec(v.shape, lambda *a: (0, 0)) for v in chunks[0]]
     else:
-        which = jnp.stack(
-            [index // per] + [jnp.clip(index - q * per, 0, per - 1) for q in range(len(pairs))]
-        ).astype(jnp.int32)
-        cuts = []
-        for q in range(len(pairs)):
-            cuts += [pl.BlockSpec((half, shard), lambda i, a, p, w, q=q: (0, w[1 + q]))] * 2
+        inside, at, cuts, first = [], [], [], 0
+        for q, pieces in enumerate(chunks):
+            per = pieces[0].shape[1] // shard
+            inside.append(index >= first)
+            at.append(jnp.clip(index - first, 0, per - 1))
+            cuts += [
+                pl.BlockSpec((v.shape[0], shard), lambda i, a, p, w, q=q: (0, w[1 + q])) for v in pieces
+            ]
+            first += per
+        which = jnp.stack([sum(v.astype(jnp.int32) for v in inside) - 1] + at).astype(jnp.int32)
     full = lambda shape: pl.BlockSpec(shape, lambda *a: (0,) * len(shape))
     factor = lambda s: pl.BlockSpec((1, shard, wide), lambda i, a, p, w: (a[s], 0, 0))
     return pl.pallas_call(
-        functools.partial(low_in_kernel, segments, rows),
+        functools.partial(low_in_kernel, segments, len(chunks), rows),
         grid_spec=pltpu.PrefetchScalarGridSpec(
             num_scalar_prefetch=3,
             grid=(1,),
             in_specs=[full(seg.shape)] + [factor(s) for s in range(segments)] + cuts,
-            out_specs=[full((2 * half, shard)), full((2 * half, wide))],
+            out_specs=[full((tokens, shard)), full((tokens, wide))],
         ),
         out_shape=[
-            jax.ShapeDtypeStruct((2 * half, shard), BF16),
-            jax.ShapeDtypeStruct((2 * half, wide), F32),
+            jax.ShapeDtypeStruct((tokens, shard), BF16),
+            jax.ShapeDtypeStruct((tokens, wide), F32),
         ],
         compiler_params=params(16),
-        cost_estimate=cost(4 * half * down[0].size * segments, 2 * down[0].size * segments),
-    )(adapters, places, which, seg, *([down] * segments), *[v for pair in pairs for v in pair])
+        cost_estimate=cost(2 * tokens * down[0].size * segments, 2 * down[0].size * segments),
+    )(adapters, places, which, seg, *([down] * segments), *[v for pieces in chunks for v in pieces])
 
 
 def middle_kernel(segments, rows, adapters, places, base, dhidden, token_order, order, low, seg, *rest):
@@ -275,7 +288,7 @@
             jax.ShapeDtypeStruct((tokens, hidden), BF16),
             jax.ShapeDtypeStruct((tokens, wide), F32),
         ],
-        compiler_params=params(32),
+        compiler_params=params(20),
         cost_estimate=cost(
             4 * tokens * hidden * segments * wide, hidden * (tokens * 14 + segments * wide * 2)
         ),
@@ -321,7 +334,7 @@
         out_shape=jax.ShapeDtypeStruct((adapters, wide, hidden), F32),
         scratch_shapes=[pltpu.VMEM((2, adapters * wide // 2, tokens), BF16)],
         input_output_aliases={} if start is None else {5: 0},
-        compiler_params=params(32),
+        compiler_params=params(20),
         cost_estimate=cost(2 * tokens * part, 4 * part),
     )(*operands)
 
@@ -356,16 +369,18 @@
 
 
 def side_kernel(segments, adapters, places, order, low, seg, *rest):
-    out = rest[-1]
-    turned = dot(order[...], low[...]).T
-    total = jnp.zeros(out.shape, F32)
+    near, far = rest[-2:]
+    half = near.shape[0]
+    mine = dot(order[...], low[...])
+    total = jnp.zeros((2 * half, near.shape[1]), F32)
     for s in range(segments):
-        kept = jnp.where(seg[...] == s, turned, 0.0).astype(BF16)
-        total = total + dot(rest[s][0], kept)
-    out[...] = total
-
-
-def side_of(order, low, seg_row, down, adapters, places):
+        kept = jnp.where(seg[...] == s, mine, 0.0).astype(BF16)
+        total = total + dot(kept, rest[s][0], ((1,), (1,)))
+    near[...] = total[:half]
+    far[...] = total[half:]
+
+
+def side_of(order, low, seg, down, adapters, places):
     segments = adapters.shape[0]
     tokens = order.shape[0]
     shard = down.shape[1]
@@ -375,63 +390,98 @@
         grid_spec=pltpu.PrefetchScalarGridSpec(
             num_scalar_prefetch=2,
             grid=(1,),
-            in_specs=[full(order.shape), full(low.shape), full(seg_row.shape)]
+            in_specs=[full(order.shape), full(low.shape), full(seg.shape)]
             + [of_segment(down.shape, s) for s in range(segments)],
-            out_specs=full((shard, tokens)),
+            out_specs=[full((tokens // 2, shard))] * 2,
         ),
-        out_shape=jax.ShapeDtypeStruct((shard, tokens), F32),
+        out_shape=[jax.ShapeDtypeStruct((tokens // 2, shard), F32)] * 2,
         compiler_params=params(16),
         cost_estimate=cost(2 * tokens * down[0].size * segments, 2 * down[0].size * segments),
-    )(adapters, places, order, low, seg_row, *([down] * segments))
-
-
-def backward_kernel(base, at, gate, up, dgate, dup, side, out, total):
-    block, tokens = total.shape[1:]
-    shard = side.shape[0]
+    )(adapters, places, order, low, seg, *([down] * segments))
+
+
+def backward_kernel(gate, up, dgate, dup, near, far, total):
     k = pl.program_id(0)
-    first = at[0] * shard
     now, before = k % 2, (k + 1) % 2
+    half = near.shape[0]
+
+    def store():
+        block = total[before].T.astype(BF16)
+        near[...] = block[:half]
+        far[...] = block[half:]
 
     @pl.when(k < pl.num_programs(0) - 1)
     def _():
-        out[...] = total[before].T.astype(BF16)
+        store()
         total[now] = dot(gate[0], dgate[...], ((1,), (1,))) + dot(up[0], dup[...], ((1,), (1,)))
 
-    @pl.when(jnp.logical_and(first // block == base + k, k < pl.num_programs(0) - 1))
-    def _():
-        here = pl.ds(pl.multiple_of(first % block, shard), shard)
-        total[now, here, :] += side[...]
-
     @pl.when(k == pl.num_programs(0) - 1)
     def _():
-        out[...] = total[before].T.astype(BF16)
-
-
-def backward_chunk(frozen, dgate, dup, side, at, first, step):
+        store()
+
+
+def backward_chunk(frozen, dgate, dup, first, step):
     tokens, hidden = dgate.shape
     block = tile_of(step, 512)
     base = first // block
     count = step // block
     full = lambda shape: pl.BlockSpec(shape, lambda *a: (0,) * len(shape))
+    out = pl.BlockSpec((tokens // 2, block), lambda k: (0, jnp.maximum(k - 1, 0)))
 
     def weight(i):
-        return pl.BlockSpec(
-            (1, block, hidden), lambda k, at: (i, base + jnp.minimum(k, count - 1), 0)
-        )
-
-    return pl.pallas_call(
-        functools.partial(backward_kernel, base),
+        return pl.BlockSpec((1, block, hidden), lambda k: (i, base + jnp.minimum(k, count - 1), 0))
+
+    return pl.pallas_call(
+        backward_kernel,
+        grid=(count + 1,),
+        in_specs=[weight(0), weight(1), full(dgate.shape), full(dup.shape)],
+        out_specs=[out, out],
+        out_shape=[jax.ShapeDtypeStruct((tokens // 2, step), BF16)] * 2,
+        scratch_shapes=[pltpu.VMEM((2, block, tokens), F32)],
+        compiler_params=params(20),
+        cost_estimate=cost(4 * tokens * step * hidden, 4 * step * hidden),
+    )(frozen, frozen, dgate, dup)
+
+
+def core_sum_kernel(base, at, near, far, side, side_far, *outs):
+    total = near[...].astype(F32) + far[...].astype(F32)
+    rows = outs[0].shape[0]
+    own = at[0] == base + pl.program_id(0)
+
+    def store(total):
+        for s, out in enumerate(outs):
+            out[...] = total[s * rows : (s + 1) * rows].astype(BF16)
+
+    @pl.when(jnp.logical_not(own))
+    def _():
+        store(total)
+
+    @pl.when(jnp.logical_and(own, at[1] == 0))
+    def _():
+        store(total + jnp.concatenate([side[...], side_far[...]], axis=1))
+
+    @pl.when(jnp.logical_and(own, at[1] != 0))
+    def _():
+        store(total + jnp.concatenate([side_far[...], side[...]], axis=1))
+
+
+def core_sum(near, far, side, side_far, at, first, slots):
+    half, step = near.shape
+    block = 2 * side.shape[1]
+    full = lambda shape: pl.BlockSpec(shape, lambda *a: (0,) * len(shape))
+    across = lambda rows: pl.BlockSpec((rows, block), lambda k, at: (0, k))
+    return pl.pallas_call(
+        functools.partial(core_sum_kernel, first // block),
         grid_spec=pltpu.PrefetchScalarGridSpec(
             num_scalar_prefetch=1,
-            grid=(count + 1,),
-            in_specs=[weight(0), weight(1), full(dgate.shape), full(dup.shape), full(side.shape)],
-            out_specs=pl.BlockSpec((tokens, block), lambda k, at: (0, jnp.maximum(k - 1, 0))),
-            scratch_shapes=[pltpu.VMEM((2, block, tokens), F32)],
+            grid=(step // block,),
+            in_specs=[across(half), across(half), full(side.shape), full(side_far.shape)],
+            out_specs=[across(half // slots)] * slots,
         ),
-        out_shape=jax.ShapeDtypeStruct((tokens, step), BF16),
-        compiler_params=params(32),
-        cost_estimate=cost(4 * tokens * step * hidden, 4 * step * hidden),
-    )(at, frozen, frozen, dgate, dup, side)
+        out_shape=[jax.ShapeDtypeStruct((half // slots, step), BF16)] * slots,
+        compiler_params=params(16),
+        cost_estimate=cost(2 * half * step, 6 * half * step),
+    )(at, near, far, side, side_far)
 
 
 def local(
@@ -500,25 +550,27 @@
 
     hidden = frozen.shape[2]
     tiles = hidden // tile_of(hidden, 256)
-    step = width // GATHER_CHUNKS
+    chunks = []
+    for share in GATHER_SHARES:
+        first = sum(v.shape[1] for v in chunks)
+        chunks.append(activations[:, first : first + width * share // sum(GATHER_SHARES)])
     outer = []
-    for q in range(GATHER_CHUNKS):
-        x = activations[:, q * step : (q + 1) * step]
-        outer.append(torus.gather(after(x, outer[-1]) if q else x, 0))
+    for x in chunks:
+        x = torus.gather(after(x, outer[-1]) if outer else x, 0)
+        outer.append(x.reshape(a * rows, -1))
     base = None
-    pairs = []
-    for q in range(GATHER_CHUNKS):
-        parts = [outer[q]] + [torus.move(outer[q], 1, -k) for k in range(1, b)]
-        ahead = base if q else outer[-1]
-        parts = lax.optimization_barrier((*parts, ahead))[:-1]
-        x = jnp.stack(parts).reshape(tokens // c, step)
-        y = torus.move(x, 2, -1)
-        pairs.append((x, y))
-        for cut in parts_of(tiles, 4) if q == GATHER_CHUNKS - 1 else [(0, tiles)]:
-            base = forward_chunk(x, y, frozen, base, q * step, cut)
+    gathered = []
+    for q, x in enumerate(outer):
+        near = [x] + [torus.move(x, 1, -k) for k in range(1, b)]
+        near[1:] = lax.optimization_barrier((*near[1:], base if q else outer[-1]))[:-1]
+        far = [torus.move(v, 2, -1) for v in near]
+        gathered.append([*near, *far])
+        first = sum(v.shape[1] for v in chunks[:q])
+        for cut in parts_of(tiles, 4 if q else 1):
+            base = forward_chunk(gathered[q], frozen, base, first, cut)
 
     columns, partial_in = low_in_partial(
-        pairs, segment[:, None], adapter_down_factors, seg_adapter, places, index, rows
+        gathered, segment[:, None], adapter_down_factors, seg_adapter, places, index, rows
     )
     low_in = whole_sum(partial_in)
     dgate, dup, partial_out = middle(
@@ -526,33 +578,50 @@
         seg_adapter, places, rows,
     )
     grad_b = []
-    for cut in parts_of(tiles, 3):
+    thirds = parts_of(tiles, 3)
+    for cut in thirds[:-1]:
         grad_b.append(
             grad_b_of(
                 dgate, dup, order, low_in, adapter[None, :], adapter_list,
                 grad_b[-1] if grad_b else None, cut,
             )
         )
-    low_out = whole_sum(partial_out, grad_b)
-    grad_b = grad_b[-1]
-    side = side_of(order, low_out, segment[None, :], adapter_down_factors, seg_adapter, places)
-    blocks = []
-    first = 0
-    cores, inners = [], []
-    for q, share in enumerate(SUM_SHARES):
-        step = width * share // sum(SUM_SHARES)
-        ready = index[None]
-        if q == 1:
-            ready = after(ready, cores[0])
-        if q > 1:
-            ready = after(ready, inners[q - 2])
-        term = backward_chunk(frozen, dgate, dup, side, ready, first, step)
-        cores.append(torus.scatter_sum(term.reshape(c, b, a, rows, step), 2).astype(BF16))
-        inners.append(torus.scatter_sum(cores[q], 1).astype(BF16))
-        blocks.append(torus.scatter_sum(inners[q], 0).astype(BF16))
-        first += step
+    cuts = []
+    for share in SUM_SHARES:
+        cuts.append((sum(v[1] for v in cuts), width * share // sum(SUM_SHARES)))
+    near, far = backward_chunk(frozen, dgate, dup, *cuts[0])
+    low_out = whole_sum(partial_out, [*grad_b, near])
+    side, side_far = side_of(
+        order, low_out, segment[:, None], adapter_down_factors, seg_adapter, places
+    )
+    side_far = torus.move(side_far, 2, 1)
+    at = jnp.stack([index // c, core]).astype(jnp.int32)
+    blocks, sums = [], []
+    for q, (first, step) in enumerate(cuts):
+        if q:
+            ready = after(dgate, sums[0][0] if q > 1 else near)
+            near, far = backward_chunk(frozen, ready, dup, first, step)
+        sent = core_sum(near, torus.move(far, 2, 1), side, side_far, at, first, b)
+        sums.append(sent)
+    for q, (first, step) in enumerate(cuts):
+        hold = lambda v, wait: after(v, sums[-1][0]) if wait else v
+        last = q == len(cuts) - 1
+        total = sums[q][0].astype(F32)
+        for k in range(1, b):
+            total = total + hold(torus.move(sums[q][k], 1, k), q and not last).astype(F32)
+        inner = total.astype(BF16).reshape(a, rows, step)
+        total = inner[0].astype(F32)
+        for k in range(1, a):
+            total = total + hold(torus.move(inner[k], 0, k), not last).astype(F32)
+        blocks.append(total.astype(BF16))
     dinput = jnp.concatenate(blocks, axis=1)
-    grad_a = grad_a_of(columns, order, after(low_out, term), adapter[:, None], adapter_list)
+    grad_b = grad_b_of(
+        dgate, dup, order, after(low_in, near), adapter[None, :], adapter_list,
+        grad_b[-1] if grad_b else None, thirds[-1],
+    )
+    grad_a = grad_a_of(
+        columns, order, after(low_out, sent[0]), adapter[:, None], adapter_list
+    )
     return (dinput, grad_a, grad_b)
 
 

time: 200 us -> 190 us (0.950)
  waiting for transfers between devices: 41.3 us -> 26.8 us
  local copies, waits for them, and re-layouts: 14.3 us -> 7.76 us
  other arithmetic: 8.91 us -> 13.4 us
  Pallas kernels: 96.5 us -> 99.6 us
  starting transfers between devices: 37.5 us -> 40.4 us
    ppermute x29 -> x32, waiting for transfers between devices: 41.2 us -> 26.3 us  [move(): return lax.ppermute(x, 'tensor', pairs)]
    unnamed x60 -> x42, local copies, waits for them, and re-layouts: 10.5 us -> 4.95 us
    pallas_call x9 -> x12, Pallas kernels: 69.5 us -> 72.6 us  [the longest x5 33.3 us: forward_chunk(): pl.pallas_call(functools.partial(forward_kernel, len(pieces), blocks), gr...]
    ppermute x29 -> x32, starting transfers between devices: 30.5 us -> 33.6 us  [move(): return lax.ppermute(x, 'tensor', pairs)]
    add x5, other arithmetic: 0.05 us -> 3.05 us  [exchange_sum(): x = x + lax.ppermute(x, 'tensor', pairs)]
  transfers between devices with their start and end apart: 35 -> 38, of which waited for: 17 -> 15; matrix products, arithmetic and copies ran while one was open for 2% -> 4% of each run, Pallas kernels for 35% -> 48%
where the time goes in v4:
time: 190 us; the launch traced here: 189 us
  Pallas kernels  99.6 us (52%)
  starting transfers between devices  40.4 us (21%)
  waiting for transfers between devices  26.8 us (14%)
  other arithmetic  13.4 us (7%)
  local copies, waits for them, and re-layouts  7.76 us (4%)
    ppermute x32, starting transfers between devices, move(): return lax.ppermute(x, 'tensor', pairs)  33.6 us
    pallas_call x5, Pallas kernels, forward_chunk(): pl.pallas_call(functools.partial(forward_kernel, len(pieces), blocks), gr...  33.3 us
    pallas_call x3, Pallas kernels, backward_chunk(): pl.pallas_call(backward_kernel, grid=(count + 1,), in_specs=[weight(0), w...  31.8 us
    ppermute x32, waiting for transfers between devices, move(): return lax.ppermute(x, 'tensor', pairs)  26.3 us
    pallas_call x3, Pallas kernels, grad_b_of(): pl.pallas_call(grad_b_kernel, grid=(last - first,), in_specs=specs, out_s...  12.7 us
    pallas_call x1, Pallas kernels, middle(): pl.pallas_call(functools.partial(middle_kernel, segments, rows), grid_spe...  7.55 us
    ppermute x6, starting transfers between devices, exchange_sum(): x = x + lax.ppermute(x, 'tensor', pairs)  6.83 us
    pallas_call x3, Pallas kernels, core_sum(): pl.pallas_call(functools.partial(core_sum_kernel, first // block), grid_s...  6.08 us
  transfers between devices with their start and end apart: 38, of which 15 were waited for; matrix products, arithmetic and copies ran while one was open for 4% of the time, Pallas kernels for 48%

profile of v4, /device:TPU:0, one launch (start us, length us, event | category | flops | bytes accessed | tf_op | source)
XLA Modules:
  0.0 189.1 jit_solution(16425603465085900208)
XLA Ops:
  1.5 5.1 %collective-permute-start = (bf16[16,3072]{1,0:T(8,128)(2,1)S(1)}, bf16[16,3072]{1,0:T(8,128)(2,1)S(1)}, u32[]{:S(2)}, u32[]{:S(2)}) collective-permute-start(bf16[16,3072]{1,0:T(8,128)(2,1)S(1)} %get-tuple-element.88), channel_id=1, source_target_pairs={{0,12},{1,13},{2,14},{3,15},{4,0},{5,1},{6,2},{7,3},{8,4},{9,5},{1... | collective-permute-start | bytes 294920 | tf_op jit(solution)/shard_map/ppermute | solution.py:64
  10.2 5.2 %collective-permute-done.1 = bf16[16,3072]{1,0:T(8,128)(2,1)S(1)} collective-permute-done((bf16[16,3072]{1,0:T(8,128)(2,1)S(1)}, bf16[16,3072]{1,0:T(8,128)(2,1)S(1)}, u32[]{:S(2)}, u32[]{:S(2)}) %collective-permute-start.1) | collective-permute-done | bytes 98336 | tf_op jit(solution)/shard_map/ppermute | solution.py:64
  15.4 2.3 %collective-permute-start.4 = (bf16[16,5120]{1,0:T(8,128)(2,1)S(1)}, bf16[16,5120]{1,0:T(8,128)(2,1)S(1)}, u32[]{:S(2)}, u32[]{:S(2)}) collective-permute-start(bf16[16,5120]{1,0:T(8,128)(2,1)S(1)} %slice.70), channel_id=1, source_target_pairs={{0,8},{1,9},{2,10},{3,11},{4,12},{5,13},{6,14},{7,15},{8,0},{9,1},... | collective-permute-start | bytes 491528 | tf_op jit(solution)/shard_map/ppermute | solution.py:64
  18.0 3.6 %collective-permute-start.3 = (bf16[16,5120]{1,0:T(8,128)(2,1)S(1)}, bf16[16,5120]{1,0:T(8,128)(2,1)S(1)}, u32[]{:S(2)}, u32[]{:S(2)}) collective-permute-start(bf16[16,5120]{1,0:T(8,128)(2,1)S(1)} %slice.70), channel_id=1, source_target_pairs={{0,12},{1,13},{2,14},{3,15},{4,0},{5,1},{6,2},{7,3},{8,4},{9,5},{1... | collective-permute-start | bytes 491528 | tf_op jit(solution)/shard_map/ppermute | solution.py:64
  22.4 1.5 collective-permute-start.7
  24.0 4.7 %collective-permute-done.4 = bf16[16,5120]{1,0:T(8,128)(2,1)S(1)} collective-permute-done((bf16[16,5120]{1,0:T(8,128)(2,1)S(1)}, bf16[16,5120]{1,0:T(8,128)(2,1)S(1)}, u32[]{:S(2)}, u32[]{:S(2)}) %collective-permute-start.4) | collective-permute-done | bytes 163872 | tf_op jit(solution)/shard_map/ppermute | solution.py:64
  28.7 1.4 collective-permute-done.3
  30.2 1.7 collective-permute-done.7.rest_1_.rest_9_
  32.8 1.5 collective-permute-start.6
  35.6 11.9 %shard_map.103.rest_14_ = f32[2,256,1792]{2,1,0:T(8,128)S(1)} custom-call(bf16[64,3072]{1,0:T(8,128)(2,1)S(1)} %bitcast.38, bf16[64,3072]{1,0:T(8,128)(2,1)S(1)} %collective-permute-done.7.rest_1_.rest_9_, bf16[64,3072]{1,0:T(8,128)(2,1)S(1)} %collective-permute-done.8.rest_2_.rest_10_, bf16[64,3072]{1,0:T(8,128)(2,1)S(1)} %collective-permute-done.9.rest_3_.rest_11_, ...), custom_call_target="tpu_custom_call" | custom-call | flops 5637144576 | bytes 22020096 | tf_op jit(solution)/shard_map/pallas_call | solution.py:139
  47.6 2.3 %collective-permute-done.6.rest_1_.rest_13_ = bf16[64,5120]{1,0:T(8,128)(2,1)S(1)} collective-permute-done((bf16[64,5120]{1,0:T(8,128)(2,1)S(1)}, bf16[64,5120]{1,0:T(8,128)(2,1)S(1)}, u32[]{:S(2)}, u32[]{:S(2)}) %collective-permute-start.6) | collective-permute-done | bytes 655392 | tf_op jit(solution)/shard_map/ppermute | solution.py:64
  50.6 1.4 collective-permute-done.11.rest_3_.rest_15_
  52.0 1.4 shard_map.108
  55.4 1.5 collective-permute-start.13
  56.9 4.1 %shard_map.104.rest_14_ = f32[2,256,1792]{2,1,0:T(8,128)S(1)} custom-call(bf16[64,5120]{1,0:T(8,128)(2,1)S(1)} %bitcast.32, bf16[64,5120]{1,0:T(8,128)(2,1)S(1)} %collective-permute-done.6.rest_1_.rest_13_, bf16[64,5120]{1,0:T(8,128)(2,1)S(1)} %collective-permute-done.10.rest_2_.rest_14_, ...), custom_call_target="tpu_custom_call", output_to_operand_aliasing={{}: (14, {})} | custom-call | flops 1342177280 | bytes 5242880 | tf_op jit(solution)/shard_map/pallas_call | solution.py:139
  61.0 1.5 add.299
  63.5 5.7 %shard_map.105.rest_14_ = f32[2,256,1792]{2,1,0:T(8,128)S(1)} custom-call(bf16[64,5120]{1,0:T(8,128)(2,1)S(1)} %bitcast.33, bf16[64,5120]{1,0:T(8,128)(2,1)S(1)} %collective-permute-done.6.rest_1_.rest_13_, bf16[64,5120]{1,0:T(8,128)(2,1)S(1)} %collective-permute-done.10.rest_2_.rest_14_, ...), custom_call_target="tpu_custom_call", output_to_operand_aliasing={{}: (14, {})} | custom-call | flops 2684354560 | bytes 10485760 | tf_op jit(solution)/shard_map/pallas_call | solution.py:139
  69.2 1.5 add.300
  70.8 5.7 %shard_map.106.rest_14_ = f32[2,256,1792]{2,1,0:T(8,128)S(1)} custom-call(bf16[64,5120]{1,0:T(8,128)(2,1)S(1)} %bitcast.34, bf16[64,5120]{1,0:T(8,128)(2,1)S(1)} %collective-permute-done.6.rest_1_.rest_13_, bf16[64,5120]{1,0:T(8,128)(2,1)S(1)} %collective-permute-done.10.rest_2_.rest_14_, ...), custom_call_target="tpu_custom_call", output_to_operand_aliasing={{}: (14, {})} | custom-call | flops 2684354560 | bytes 10485760 | tf_op jit(solution)/shard_map/pallas_call | solution.py:139
  77.0 1.6 fusion.2
  78.6 5.9 %shard_map.107.base = f32[2,256,1792]{2,1,0:T(8,128)S(1)} custom-call(bf16[64,5120]{1,0:T(8,128)(2,1)S(1)} %bitcast.35, bf16[64,5120]{1,0:T(8,128)(2,1)S(1)} %collective-permute-done.6.rest_1_.rest_13_, bf16[64,5120]{1,0:T(8,128)(2,1)S(1)} %collective-permute-done.10.rest_2_.rest_14_, ...), custom_call_target="tpu_custom_call", output_to_operand_aliasing={{}: (14, {})} | custom-call | flops 2684354560 | bytes 10485760 | tf_op jit(solution)/shard_map/pallas_call | solution.py:139
  85.3 4.1 %copy-done.2 = bf16[24,128,1792]{2,1,0:T(8,128)(2,1)S(1)} copy-done((bf16[24,128,1792]{2,1,0:T(8,128)(2,1)S(1)}, bf16[24,128,1792]{2,1,0:T(8,128)(2,1)}, u32[]{:S(2)}) %copy-start.2) | copy-done | bytes 11010072
  89.4 7.5 %shard_map.109 = (bf16[256,1792]{1,0:T(8,128)(2,1)S(1)}, bf16[256,1792]{1,0:T(8,128)(2,1)S(1)}, f32[256,128]{1,0:T(8,128)S(1)}) custom-call(s32[8]{0:T(128)S(1)} %bitcast.53, s32[16]{0:T(128)S(1)} %get-tuple-element.76.places, f32[2,256,1792]{2,1,0:T(8,128)S(1)} %shard_map.107.base, bf16[256,1792]{1,0:T(8,128)(2,1)S(1)} %copy-done.5, ...), custom_call_target="tpu_custom_call" | custom-call | flops 1879048192 | bytes 10092544 | tf_op jit(solution)/shard_map/pallas_call | solution.py:272
  97.5 11.5 %shard_map.110 = (bf16[128,3072]{1,0:T(8,128)(2,1)S(1)}, bf16[128,3072]{1,0:T(8,128)(2,1)S(1)}) custom-call(bf16[2,8192,1792]{2,1,0:T(8,128)(2,1)} %up.5, bf16[2,8192,1792]{2,1,0:T(8,128)(2,1)} %up.5, bf16[256,1792]{1,0:T(8,128)(2,1)S(1)} %get-tuple-element.62.dgate, bf16[256,1792]{1,0:T(8,128)(2,1)S(1)} %get-tuple-element.44.dup), custom_call_target="tpu_custom_call" | custom-call | flops 5637144576 | bytes 22020096 | tf_op jit(solution)/shard_map/pallas_call | solution.py:434
  109.7 3.8 %shard_map.111.rest_0_ = f32[24,128,1792]{2,1,0:T(8,128)} custom-call(bf16[256,1792]{1,0:T(8,128)(2,1)S(1)} %get-tuple-element.62.dgate, bf16[256,1792]{1,0:T(8,128)(2,1)S(1)} %get-tuple-element.44.dup, bf16[256,256]{1,0:T(8,128)(2,1)S(1)} %fusion.1.order, bf16[256,128]{1,0:T(8,128)(2,1)S(1)} %bitcast.41, s32[1,256]{1,0:T(1,128)S(1)} %bitcast.46), custom_call_target="tpu_custom_call" | custom-call | flops 805306368 | bytes 6291456 | tf_op jit(solution)/shard_map/pallas_call | solution.py:329
  113.7 1.5 collective-permute-start.20
  115.2 3.8 %shard_map.112.rest_0_ = f32[24,128,1792]{2,1,0:T(8,128)} custom-call(bf16[256,1792]{1,0:T(8,128)(2,1)S(1)} %get-tuple-element.62.dgate, bf16[256,1792]{1,0:T(8,128)(2,1)S(1)} %get-tuple-element.44.dup, bf16[256,256]{1,0:T(8,128)(2,1)S(1)} %fusion.1.order, bf16[256,128]{1,0:T(8,128)(2,1)S(1)} %bitcast.42, ...), custom_call_target="tpu_custom_call", output_to_operand_aliasing={{}: (5, {})} | custom-call | flops 805306368 | bytes 6291456 | tf_op jit(solution)/shard_map/pallas_call | solution.py:329
  119.2 2.1 %collective-permute-start.21 = (f32[128,128]{1,0:T(8,128)S(1)}, f32[128,128]{1,0:T(8,128)S(1)}, u32[]{:S(2)}, u32[]{:S(2)}) collective-permute-start(f32[128,128]{1,0:T(8,128)S(1)} %add.311), channel_id=1, source_target_pairs={{0,8},{1,9},{2,10},{3,11},{4,12},{5,13},{6,14},{7,15},{8,0},{9,1},... | collective-permute-start | bytes 196616 | tf_op jit(solution)/shard_map/ppermute | solution.py:90
  121.3 12.2 %shard_map.117 = (bf16[128,3072]{1,0:T(8,128)(2,1)S(1)}, bf16[128,3072]{1,0:T(8,128)(2,1)}) custom-call(bf16[2,8192,1792]{2,1,0:T(8,128)(2,1)} %up.5, bf16[2,8192,1792]{2,1,0:T(8,128)(2,1)} %up.5, bf16[256,1792]{1,0:T(8,128)(2,1)S(1)} %get-tuple-element.62.dgate, bf16[256,1792]{1,0:T(8,128)(2,1)S(1)} %get-tuple-element.44.dup), custom_call_target="tpu_custom_call" | custom-call | flops 5637144576 | bytes 22020096 | tf_op jit(solution)/shard_map/pallas_call | solution.py:434
  134.3 1.5 collective-permute-done.22
  135.8 1.4 shard_map.113
  137.5 1.3 collective-permute-done.23.side_far
  138.8 2.3 %shard_map.114 = (bf16[64,3072]{1,0:T(8,128)(2,1)S(1)}, bf16[64,3072]{1,0:T(8,128)(2,1)}) custom-call(s32[2]{0:T(128)S(1)} %pad_add_fusion.at, bf16[128,3072]{1,0:T(8,128)(2,1)S(1)} %get-tuple-element.45.near, bf16[128,3072]{1,0:T(8,128)(2,1)S(1)} %collective-permute-done.17.far, f32[128,512]{1,0:T(8,128)S(1)} %get-tuple-element.51.side, ...), custom_call_target="tpu_custom_call" | custom-call | flops 786432 | bytes 2359296 | tf_op jit(solution)/shard_map/pallas_call | solution.py:473
  141.8 1.4 collective-permute-start.24
  143.4 8.2 %shard_map.115 = (bf16[128,2048]{1,0:T(8,128)(2,1)S(1)}, bf16[128,2048]{1,0:T(8,128)(2,1)S(1)}) custom-call(bf16[2,8192,1792]{2,1,0:T(8,128)(2,1)} %up.5, bf16[2,8192,1792]{2,1,0:T(8,128)(2,1)} %up.5, bf16[256,1792]{1,0:T(8,128)(2,1)S(1)} %get-tuple-element.62.dgate, bf16[256,1792]{1,0:T(8,128)(2,1)S(1)} %get-tuple-element.44.dup), custom_call_target="tpu_custom_call" | custom-call | flops 3758096384 | bytes 14680064 | tf_op jit(solution)/shard_map/pallas_call | solution.py:434
  151.6 2.8 %shard_map.118 = (bf16[64,3072]{1,0:T(8,128)(2,1)S(1)}, bf16[64,3072]{1,0:T(8,128)(2,1)S(1)}) custom-call(s32[2]{0:T(128)S(1)} %pad_add_fusion.at, bf16[128,3072]{1,0:T(8,128)(2,1)S(1)} %get-tuple-element.63.near, bf16[128,3072]{1,0:T(8,128)(2,1)} %collective-permute-done.29.far, f32[128,512]{1,0:T(8,128)S(1)} %get-tuple-element.51.side, ...), custom_call_target="tpu_custom_call" | custom-call | flops 786432 | bytes 2359296 | tf_op jit(solution)/shard_map/pallas_call | solution.py:473
  156.3 1.3 collective-permute-start.25
  158.2 2.2 %collective-permute-start.28 = (bf16[16,3072]{1,0:T(8,128)(2,1)S(1)}, bf16[16,3072]{1,0:T(8,128)(2,1)S(1)}, u32[]{:S(2)}, u32[]{:S(2)}) collective-permute-start(bf16[16,3072]{1,0:T(8,128)(2,1)S(1)} %get-tuple-element.79), channel_id=1, source_target_pairs={{0,12},{1,13},{2,14},{3,15},{4,0},{5,1},{6,2},{7,3},{8,4},{9,5},{1... | collective-permute-start | bytes 294920 | tf_op jit(solution)/shard_map/ppermute | solution.py:64
  160.4 5.0 %shard_map.120 = f32[24,128,1792]{2,1,0:T(8,128)} custom-call(bf16[256,1792]{1,0:T(8,128)(2,1)S(1)} %get-tuple-element.62.dgate, bf16[256,1792]{1,0:T(8,128)(2,1)S(1)} %get-tuple-element.44.dup, bf16[256,256]{1,0:T(8,128)(2,1)S(1)} %fusion.1.order, bf16[256,128]{1,0:T(8,128)(2,1)S(1)} %bitcast.43, ...), custom_call_target="tpu_custom_call", output_to_operand_aliasing={{}: (5, {})} | custom-call | flops 1207959552 | bytes 9437184 | tf_op jit(solution)/shard_map/pallas_call | solution.py:329
  166.4 1.2 collective-permute-done.27
  167.7 2.5 %collective-permute-start.31 = (bf16[16,3072]{1,0:T(8,128)(2,1)S(1)}, bf16[16,3072]{1,0:T(8,128)(2,1)S(1)}, u32[]{:S(2)}, u32[]{:S(2)}) collective-permute-start(bf16[16,3072]{1,0:T(8,128)(2,1)S(1)} %get-tuple-element.81), channel_id=1, source_target_pairs={{0,4},{1,5},{2,6},{3,7},{4,8},{5,9},{6,10},{7,11},{8,12},{9,13},{1... | collective-permute-start | bytes 294920 | tf_op jit(solution)/shard_map/ppermute | solution.py:64
  170.8 1.9 collective-permute-start.33
  172.6 1.3 collective-permute-start.34
  174.0 5.3 %shard_map.119 = f32[24,512,128]{2,1,0:T(8,128)} custom-call(bf16[256,512]{1,0:T(8,128)(2,1)S(1)} %copy-done.9, bf16[256,256]{1,0:T(8,128)(2,1)S(1)} %fusion.1.order, bf16[256,128]{1,0:T(8,128)(2,1)S(1)} %bitcast.45, s32[256,1]{1,0:T(8,128)S(1)} %copy.24.adapter), custom_call_target="tpu_custom_call" | custom-call | flops 805306368 | bytes 6291456 | tf_op jit(solution)/shard_map/pallas_call | solution.py:359
  181.1 1.4 collective-permute-start.36
  182.5 1.6 collective-permute-start.37
  184.1 2.9 %collective-permute-done.35 = bf16[16,2048]{1,0:T(8,128)(2,1)S(1)} collective-permute-done((bf16[16,2048]{1,0:T(8,128)(2,1)S(1)}, bf16[16,2048]{1,0:T(8,128)(2,1)S(1)}, u32[]{:S(2)}, u32[]{:S(2)}) %collective-permute-start.35) | collective-permute-done | bytes 65568 | tf_op jit(solution)/shard_map/ppermute | solution.py:64
  187.0 1.3 collective-permute-done.36
  (148 shorter events, 23.1 us)
Async XLA Ops:
  1.5 8.7 %collective-permute-start = (bf16[16,3072]{1,0:T(8,128)(2,1)S(1)}, bf16[16,3072]{1,0:T(8,128)(2,1)S(1)}, u32[]{:S(2)}, u32[]{:S(2)}) collective-permute-start(bf16[16,3072]{1,0:T(8,128)(2,1)S(1)} %get-tuple-element.88), channel_id=1, source_target_pairs={{0,12},{1,13},{2,14},{3,15},{4,0},{5,1},{6,2},{7,3},{8,4},{9,5},{1... | collective-permute-start | bytes 294920 | tf_op jit(solution)/shard_map/ppermute | solution.py:64
  6.6 8.7 %collective-permute-start.1 = (bf16[16,3072]{1,0:T(8,128)(2,1)S(1)}, bf16[16,3072]{1,0:T(8,128)(2,1)S(1)}, u32[]{:S(2)}, u32[]{:S(2)}) collective-permute-start(bf16[16,3072]{1,0:T(8,128)(2,1)S(1)} %get-tuple-element.88), channel_id=1, source_target_pairs={{0,8},{1,9},{2,10},{3,11},{4,12},{5,13},{6,14},{7,15},{8,0},{9,1},... | collective-permute-start | bytes 294920 | tf_op jit(solution)/shard_map/ppermute | solution.py:64
  6.6 8.7 %collective-permute-start.2 = (bf16[16,3072]{1,0:T(8,128)(2,1)S(1)}, bf16[16,3072]{1,0:T(8,128)(2,1)S(1)}, u32[]{:S(2)}, u32[]{:S(2)}) collective-permute-start(bf16[16,3072]{1,0:T(8,128)(2,1)S(1)} %get-tuple-element.88), channel_id=1, source_target_pairs={{0,4},{1,5},{2,6},{3,7},{4,8},{5,9},{6,10},{7,11},{8,12},{9,13},{1... | collective-permute-start | bytes 294920 | tf_op jit(solution)/shard_map/ppermute | solution.py:64
  8.1 77.1 %copy-start.12 = (s32[16]{0:T(128)}, s32[16]{0:T(128)S(1)}, u32[]{:S(2)}) copy-start(s32[16]{0:T(128)S(1)} %get-tuple-element.76.places) | copy-start | bytes 196
  15.4 13.3 %collective-permute-start.4 = (bf16[16,5120]{1,0:T(8,128)(2,1)S(1)}, bf16[16,5120]{1,0:T(8,128)(2,1)S(1)}, u32[]{:S(2)}, u32[]{:S(2)}) collective-permute-start(bf16[16,5120]{1,0:T(8,128)(2,1)S(1)} %slice.70), channel_id=1, source_target_pairs={{0,8},{1,9},{2,10},{3,11},{4,12},{5,13},{6,14},{7,15},{8,0},{9,1},... | collective-permute-start | bytes 491528 | tf_op jit(solution)/shard_map/ppermute | solution.py:64
  17.8 10.9 %collective-permute-start.5 = (bf16[16,5120]{1,0:T(8,128)(2,1)S(1)}, bf16[16,5120]{1,0:T(8,128)(2,1)S(1)}, u32[]{:S(2)}, u32[]{:S(2)}) collective-permute-start(bf16[16,5120]{1,0:T(8,128)(2,1)S(1)} %slice.70), channel_id=1, source_target_pairs={{0,4},{1,5},{2,6},{3,7},{4,8},{5,9},{6,10},{7,11},{8,12},{9,13},{1... | collective-permute-start | bytes 491528 | tf_op jit(solution)/shard_map/ppermute | solution.py:64
  18.0 12.1 %collective-permute-start.3 = (bf16[16,5120]{1,0:T(8,128)(2,1)S(1)}, bf16[16,5120]{1,0:T(8,128)(2,1)S(1)}, u32[]{:S(2)}, u32[]{:S(2)}) collective-permute-start(bf16[16,5120]{1,0:T(8,128)(2,1)S(1)} %slice.70), channel_id=1, source_target_pairs={{0,12},{1,13},{2,14},{3,15},{4,0},{5,1},{6,2},{7,3},{8,4},{9,5},{1... | collective-permute-start | bytes 491528 | tf_op jit(solution)/shard_map/ppermute | solution.py:64
  22.4 9.4 %collective-permute-start.7 = (bf16[64,3072]{1,0:T(8,128)(2,1)S(1)}, bf16[64,3072]{1,0:T(8,128)(2,1)S(1)}, u32[]{:S(2)}, u32[]{:S(2)}) collective-permute-start(bf16[64,3072]{1,0:T(8,128)(2,1)S(1)} %bitcast.36), channel_id=1, source_target_pairs={{0,2},{1,3},{2,0},{3,1},{4,6},{5,7},{6,4},{7,5},{8,10},{9,11},{10,... | collective-permute-start | bytes 1179656 | tf_op jit(solution)/shard_map/ppermute | solution.py:64
  24.0 11.7 %collective-permute-start.8 = (bf16[64,3072]{1,0:T(8,128)(2,1)S(1)}, bf16[64,3072]{1,0:T(8,128)(2,1)S(1)}, u32[]{:S(2)}, u32[]{:S(2)}) collective-permute-start(bf16[64,3072]{1,0:T(8,128)(2,1)S(1)} %bitcast.37), channel_id=1, source_target_pairs={{0,1},{1,0},{2,3},{3,2},{4,5},{5,4},{6,7},{7,6},{8,9},{9,8},{10,11... | collective-permute-start | bytes 1179656 | tf_op jit(solution)/shard_map/ppermute | solution.py:64
  31.8 3.8 %collective-permute-start.9 = (bf16[64,3072]{1,0:T(8,128)(2,1)S(1)}, bf16[64,3072]{1,0:T(8,128)(2,1)S(1)}, u32[]{:S(2)}, u32[]{:S(2)}) collective-permute-start(bf16[64,3072]{1,0:T(8,128)(2,1)S(1)} %collective-permute-done.7.rest_1_.rest_9_), channel_id=1, source_target_pairs={{0,1},{1,0},{2,3},{3,2},{4,5},{5,4},{6,7},{7,6},{8,9},{9,8},{10,11... | collective-permute-start | bytes 1179656 | tf_op jit(solution)/shard_map/ppermute | solution.py:64
  32.6 17.3 %copy-start.14 = (s32[128]{0:T(128)}, s32[128]{0:T(128)S(1)}, u32[]{:S(2)}) copy-start(s32[128]{0:T(128)S(1)} %select_reduce_fusion) | copy-start | bytes 1540
  32.8 17.1 %collective-permute-start.6 = (bf16[64,5120]{1,0:T(8,128)(2,1)S(1)}, bf16[64,5120]{1,0:T(8,128)(2,1)S(1)}, u32[]{:S(2)}, u32[]{:S(2)}) collective-permute-start(bf16[64,5120]{1,0:T(8,128)(2,1)S(1)} %bitcast.29), channel_id=1, source_target_pairs={{0,2},{1,3},{2,0},{3,1},{4,6},{5,7},{6,4},{7,5},{8,10},{9,11},{10,... | collective-permute-start | bytes 1966088 | tf_op jit(solution)/shard_map/ppermute | solution.py:64
  34.5 17.5 %copy-start.3 = (s32[256,1]{1,0:T(8,128)}, s32[256,1]{1,0:T(8,128)S(1)}, u32[]{:S(2)}) copy-start(s32[256,1]{1,0:T(8,128)S(1)} %copy.21.seg) | copy-start | bytes 3076
  35.3 16.7 %copy-start = (bf16[24,512,128]{2,1,0:T(8,128)(2,1)S(1)}, bf16[24,512,128]{2,1,0:T(8,128)(2,1)}, u32[]{:S(2)}) copy-start(bf16[24,512,128]{2,1,0:T(8,128)(2,1)} %rest_7_.13) | copy-start | bytes 9437188
  35.3 16.7 %copy-start.10 = (s32[1,8]{1,0:T(1,128)S(1)}, s32[1,8]{1,0:T(1,128)}, u32[]{:S(2)}) copy-start(s32[1,8]{1,0:T(1,128)} %param.13) | copy-start | bytes 100
  35.3 15.3 %collective-permute-start.10 = (bf16[64,5120]{1,0:T(8,128)(2,1)S(1)}, bf16[64,5120]{1,0:T(8,128)(2,1)S(1)}, u32[]{:S(2)}, u32[]{:S(2)}) collective-permute-start(bf16[64,5120]{1,0:T(8,128)(2,1)S(1)} %bitcast.30), channel_id=1, source_target_pairs={{0,1},{1,0},{2,3},{3,2},{4,5},{5,4},{6,7},{7,6},{8,9},{9,8},{10,11... | collective-permute-start | bytes 1966088 | tf_op jit(solution)/shard_map/ppermute | solution.py:64
  49.9 2.1 %collective-permute-start.11 = (bf16[64,5120]{1,0:T(8,128)(2,1)S(1)}, bf16[64,5120]{1,0:T(8,128)(2,1)S(1)}, u32[]{:S(2)}, u32[]{:S(2)}) collective-permute-start(bf16[64,5120]{1,0:T(8,128)(2,1)S(1)} %collective-permute-done.6.rest_1_.rest_13_), channel_id=1, source_target_pairs={{0,1},{1,0},{2,3},{3,2},{4,5},{5,4},{6,7},{7,6},{8,9},{9,8},{10,11... | collective-permute-start | bytes 1966088 | tf_op jit(solution)/shard_map/ppermute | solution.py:64
  53.4 1.3 collective-permute-start.12
  55.4 5.6 %collective-permute-start.13 = (f32[128,128]{1,0:T(8,128)}, f32[128,128]{1,0:T(8,128)}, u32[]{:S(2)}, u32[]{:S(2)}) collective-permute-start(f32[128,128]{1,0:T(8,128)} %slice_add_fusion.1), channel_id=1, source_target_pairs={{0,2},{1,3},{2,0},{3,1},{4,6},{5,7},{6,4},{7,5},{8,10},{9,11},{10,... | collective-permute-start | bytes 196616 | tf_op jit(solution)/shard_map/ppermute | solution.py:90
  62.5 6.7 %collective-permute-start.14 = (f32[128,128]{1,0:T(8,128)}, f32[128,128]{1,0:T(8,128)}, u32[]{:S(2)}, u32[]{:S(2)}) collective-permute-start(f32[128,128]{1,0:T(8,128)} %add.299), channel_id=1, source_target_pairs={{0,4},{1,5},{2,6},{3,7},{4,0},{5,1},{6,2},{7,3},{8,12},{9,13},{10,... | collective-permute-start | bytes 196616 | tf_op jit(solution)/shard_map/ppermute | solution.py:90
  70.7 6.2 %collective-permute-start.15 = (f32[128,128]{1,0:T(8,128)}, f32[128,128]{1,0:T(8,128)}, u32[]{:S(2)}, u32[]{:S(2)}) collective-permute-start(f32[128,128]{1,0:T(8,128)} %add.300), channel_id=1, source_target_pairs={{0,8},{1,9},{2,10},{3,11},{4,12},{5,13},{6,14},{7,15},{8,0},{9,1},... | collective-permute-start | bytes 196616 | tf_op jit(solution)/shard_map/ppermute | solution.py:90
  78.6 5.9 %collective-permute-start.16 = (bf16[128,128]{1,0:T(8,128)(2,1)}, bf16[128,128]{1,0:T(8,128)(2,1)}, u32[]{:S(2)}, u32[]{:S(2)}) collective-permute-start(bf16[128,128]{1,0:T(8,128)(2,1)} %fusion.2), channel_id=1, source_target_pairs={{0,1},{1,0},{2,3},{3,2},{4,5},{5,4},{6,7},{7,6},{8,9},{9,8},{10,11... | collective-permute-start | bytes 98312 | tf_op jit(solution)/shard_map/ppermute | solution.py:64
  97.0 12.1 %collective-permute-start.18 = (f32[128,128]{1,0:T(8,128)S(1)}, f32[128,128]{1,0:T(8,128)S(1)}, u32[]{:S(2)}, u32[]{:S(2)}) collective-permute-start(f32[128,128]{1,0:T(8,128)S(1)} %slice.75), channel_id=1, source_target_pairs={{0,1},{1,0},{2,3},{3,2},{4,5},{5,4},{6,7},{7,6},{8,9},{9,8},{10,11... | collective-permute-start | bytes 196616 | tf_op jit(solution)/shard_map/ppermute | solution.py:64
  109.0 29.8 %collective-permute-start.17 = (bf16[128,3072]{1,0:T(8,128)(2,1)S(1)}, bf16[128,3072]{1,0:T(8,128)(2,1)S(1)}, u32[]{:S(2)}, u32[]{:S(2)}) collective-permute-start(bf16[128,3072]{1,0:T(8,128)(2,1)S(1)} %get-tuple-element.46), channel_id=1, source_target_pairs={{0,1},{1,0},{2,3},{3,2},{4,5},{5,4},{6,7},{7,6},{8,9},{9,8},{10,11... | collective-permute-start | bytes 2359304 | tf_op jit(solution)/shard_map/ppermute | solution.py:64
  109.1 4.5 %collective-permute-start.19 = (f32[128,128]{1,0:T(8,128)S(1)}, f32[128,128]{1,0:T(8,128)S(1)}, u32[]{:S(2)}, u32[]{:S(2)}) collective-permute-start(f32[128,128]{1,0:T(8,128)S(1)} %slice_add_fusion), channel_id=1, source_target_pairs={{0,2},{1,3},{2,0},{3,1},{4,6},{5,7},{6,4},{7,5},{8,10},{9,11},{10,... | collective-permute-start | bytes 196616 | tf_op jit(solution)/shard_map/ppermute | solution.py:90
  113.7 5.4 %collective-permute-start.20 = (f32[128,128]{1,0:T(8,128)S(1)}, f32[128,128]{1,0:T(8,128)S(1)}, u32[]{:S(2)}, u32[]{:S(2)}) collective-permute-start(f32[128,128]{1,0:T(8,128)S(1)} %add.310), channel_id=1, source_target_pairs={{0,4},{1,5},{2,6},{3,7},{4,0},{5,1},{6,2},{7,3},{8,12},{9,13},{10,... | collective-permute-start | bytes 196616 | tf_op jit(solution)/shard_map/ppermute | solution.py:90
  119.1 14.4 %copy-start.16 = (s32[128]{0:T(128)S(1)}, s32[128]{0:T(128)}, u32[]{:S(2)}) copy-start(s32[128]{0:T(128)} %copy-done.14) | copy-start | bytes 1540
  119.1 16.7 %copy-start.1 = (bf16[24,512,128]{2,1,0:T(8,128)(2,1)S(1)}, bf16[24,512,128]{2,1,0:T(8,128)(2,1)}, u32[]{:S(2)}) copy-start(bf16[24,512,128]{2,1,0:T(8,128)(2,1)} %rest_7_.13) | copy-start | bytes 9437188
  119.1 16.7 %copy-start.11 = (s32[1,8]{1,0:T(1,128)S(1)}, s32[1,8]{1,0:T(1,128)}, u32[]{:S(2)}) copy-start(s32[1,8]{1,0:T(1,128)} %param.13) | copy-start | bytes 100
  119.1 16.7 %copy-start.13 = (s32[16]{0:T(128)S(1)}, s32[16]{0:T(128)}, u32[]{:S(2)}) copy-start(s32[16]{0:T(128)} %copy-done.12) | copy-start | bytes 196
  119.2 14.3 %collective-permute-start.21 = (f32[128,128]{1,0:T(8,128)S(1)}, f32[128,128]{1,0:T(8,128)S(1)}, u32[]{:S(2)}, u32[]{:S(2)}) collective-permute-start(f32[128,128]{1,0:T(8,128)S(1)} %add.311), channel_id=1, source_target_pairs={{0,8},{1,9},{2,10},{3,11},{4,12},{5,13},{6,14},{7,15},{8,0},{9,1},... | collective-permute-start | bytes 196616 | tf_op jit(solution)/shard_map/ppermute | solution.py:90
  133.4 18.2 %collective-permute-start.29 = (bf16[128,3072]{1,0:T(8,128)(2,1)}, bf16[128,3072]{1,0:T(8,128)(2,1)}, u32[]{:S(2)}, u32[]{:S(2)}) collective-permute-start(bf16[128,3072]{1,0:T(8,128)(2,1)} %get-tuple-element.64), channel_id=1, source_target_pairs={{0,1},{1,0},{2,3},{3,2},{4,5},{5,4},{6,7},{7,6},{8,9},{9,8},{10,11... | collective-permute-start | bytes 2359304 | tf_op jit(solution)/shard_map/ppermute | solution.py:64
  133.6 2.2 %collective-permute-start.22 = (bf16[128,128]{1,0:T(8,128)(2,1)S(1)}, bf16[128,128]{1,0:T(8,128)(2,1)S(1)}, u32[]{:S(2)}, u32[]{:S(2)}) collective-permute-start(bf16[128,128]{1,0:T(8,128)(2,1)S(1)} %fusion.3), channel_id=1, source_target_pairs={{0,1},{1,0},{2,3},{3,2},{4,5},{5,4},{6,7},{7,6},{8,9},{9,8},{10,11... | collective-permute-start | bytes 98312 | tf_op jit(solution)/shard_map/ppermute | solution.py:64
  137.2 1.6 collective-permute-start.23
  141.8 13.3 %collective-permute-start.24 = (bf16[64,3072]{1,0:T(8,128)(2,1)}, bf16[64,3072]{1,0:T(8,128)(2,1)}, u32[]{:S(2)}, u32[]{:S(2)}) collective-permute-start(bf16[64,3072]{1,0:T(8,128)(2,1)} %get-tuple-element.54), channel_id=1, source_target_pairs={{0,2},{1,3},{2,0},{3,1},{4,6},{5,7},{6,4},{7,5},{8,10},{9,11},{10,... | collective-permute-start | bytes 1179656 | tf_op jit(solution)/shard_map/ppermute | solution.py:64
  151.5 13.9 %collective-permute-start.26 = (bf16[128,2048]{1,0:T(8,128)(2,1)S(1)}, bf16[128,2048]{1,0:T(8,128)(2,1)S(1)}, u32[]{:S(2)}, u32[]{:S(2)}) collective-permute-start(bf16[128,2048]{1,0:T(8,128)(2,1)S(1)} %get-tuple-element.57), channel_id=1, source_target_pairs={{0,1},{1,0},{2,3},{3,2},{4,5},{5,4},{6,7},{7,6},{8,9},{9,8},{10,11... | collective-permute-start | bytes 1572872 | tf_op jit(solution)/shard_map/ppermute | solution.py:64
  154.4 13.1 %collective-permute-start.30 = (bf16[64,3072]{1,0:T(8,128)(2,1)S(1)}, bf16[64,3072]{1,0:T(8,128)(2,1)S(1)}, u32[]{:S(2)}, u32[]{:S(2)}) collective-permute-start(bf16[64,3072]{1,0:T(8,128)(2,1)S(1)} %get-tuple-element.66), channel_id=1, source_target_pairs={{0,2},{1,3},{2,0},{3,1},{4,6},{5,7},{6,4},{7,5},{8,10},{9,11},{10,... | collective-permute-start | bytes 1179656 | tf_op jit(solution)/shard_map/ppermute | solution.py:64
  156.3 10.1 %collective-permute-start.25 = (bf16[16,3072]{1,0:T(8,128)(2,1)S(1)}, bf16[16,3072]{1,0:T(8,128)(2,1)S(1)}, u32[]{:S(2)}, u32[]{:S(2)}) collective-permute-start(bf16[16,3072]{1,0:T(8,128)(2,1)S(1)} %get-tuple-element.78), channel_id=1, source_target_pairs={{0,4},{1,5},{2,6},{3,7},{4,8},{5,9},{6,10},{7,11},{8,12},{9,13},{1... | collective-permute-start | bytes 294920 | tf_op jit(solution)/shard_map/ppermute | solution.py:64
  157.6 10.0 %collective-permute-start.27 = (bf16[16,3072]{1,0:T(8,128)(2,1)S(1)}, bf16[16,3072]{1,0:T(8,128)(2,1)S(1)}, u32[]{:S(2)}, u32[]{:S(2)}) collective-permute-start(bf16[16,3072]{1,0:T(8,128)(2,1)S(1)} %get-tuple-element.80), channel_id=1, source_target_pairs={{0,8},{1,9},{2,10},{3,11},{4,12},{5,13},{6,14},{7,15},{8,0},{9,1},... | collective-permute-start | bytes 294920 | tf_op jit(solution)/shard_map/ppermute | solution.py:64
  158.2 15.8 %copy-start.9 = (bf16[256,512]{1,0:T(8,128)(2,1)S(1)}, bf16[256,512]{1,0:T(8,128)(2,1)}, u32[]{:S(2)}) copy-start(bf16[256,512]{1,0:T(8,128)(2,1)} %copy-done.8) | copy-start | bytes 786436
  158.2 9.3 %collective-permute-start.28 = (bf16[16,3072]{1,0:T(8,128)(2,1)S(1)}, bf16[16,3072]{1,0:T(8,128)(2,1)S(1)}, u32[]{:S(2)}, u32[]{:S(2)}) collective-permute-start(bf16[16,3072]{1,0:T(8,128)(2,1)S(1)} %get-tuple-element.79), channel_id=1, source_target_pairs={{0,12},{1,13},{2,14},{3,15},{4,0},{5,1},{6,2},{7,3},{8,4},{9,5},{1... | collective-permute-start | bytes 294920 | tf_op jit(solution)/shard_map/ppermute | solution.py:64
  167.7 11.6 %collective-permute-start.31 = (bf16[16,3072]{1,0:T(8,128)(2,1)S(1)}, bf16[16,3072]{1,0:T(8,128)(2,1)S(1)}, u32[]{:S(2)}, u32[]{:S(2)}) collective-permute-start(bf16[16,3072]{1,0:T(8,128)(2,1)S(1)} %get-tuple-element.81), channel_id=1, source_target_pairs={{0,4},{1,5},{2,6},{3,7},{4,8},{5,9},{6,10},{7,11},{8,12},{9,13},{1... | collective-permute-start | bytes 294920 | tf_op jit(solution)/shard_map/ppermute | solution.py:64
  170.2 9.2 %collective-permute-start.32 = (bf16[16,3072]{1,0:T(8,128)(2,1)S(1)}, bf16[16,3072]{1,0:T(8,128)(2,1)S(1)}, u32[]{:S(2)}, u32[]{:S(2)}) collective-permute-start(bf16[16,3072]{1,0:T(8,128)(2,1)S(1)} %get-tuple-element.83), channel_id=1, source_target_pairs={{0,8},{1,9},{2,10},{3,11},{4,12},{5,13},{6,14},{7,15},{8,0},{9,1},... | collective-permute-start | bytes 294920 | tf_op jit(solution)/shard_map/ppermute | solution.py:64
  170.8 8.6 %collective-permute-start.33 = (bf16[16,3072]{1,0:T(8,128)(2,1)S(1)}, bf16[16,3072]{1,0:T(8,128)(2,1)S(1)}, u32[]{:S(2)}, u32[]{:S(2)}) collective-permute-start(bf16[16,3072]{1,0:T(8,128)(2,1)S(1)} %get-tuple-element.82), channel_id=1, source_target_pairs={{0,12},{1,13},{2,14},{3,15},{4,0},{5,1},{6,2},{7,3},{8,4},{9,5},{1... | collective-permute-start | bytes 294920 | tf_op jit(solution)/shard_map/ppermute | solution.py:64
  172.6 7.5 %collective-permute-start.34 = (bf16[64,2048]{1,0:T(8,128)(2,1)S(1)}, bf16[64,2048]{1,0:T(8,128)(2,1)S(1)}, u32[]{:S(2)}, u32[]{:S(2)}) collective-permute-start(bf16[64,2048]{1,0:T(8,128)(2,1)S(1)} %get-tuple-element.71), channel_id=1, source_target_pairs={{0,2},{1,3},{2,0},{3,1},{4,6},{5,7},{6,4},{7,5},{8,10},{9,11},{10,... | collective-permute-start | bytes 786440 | tf_op jit(solution)/shard_map/ppermute | solution.py:64
  180.2 6.8 %collective-permute-start.35 = (bf16[16,2048]{1,0:T(8,128)(2,1)S(1)}, bf16[16,2048]{1,0:T(8,128)(2,1)S(1)}, u32[]{:S(2)}, u32[]{:S(2)}) collective-permute-start(bf16[16,2048]{1,0:T(8,128)(2,1)S(1)} %get-tuple-element.84), channel_id=1, source_target_pairs={{0,4},{1,5},{2,6},{3,7},{4,8},{5,9},{6,10},{7,11},{8,12},{9,13},{1... | collective-permute-start | bytes 196616 | tf_op jit(solution)/shard_map/ppermute | solution.py:64
  181.1 7.2 %collective-permute-start.36 = (bf16[16,2048]{1,0:T(8,128)(2,1)S(1)}, bf16[16,2048]{1,0:T(8,128)(2,1)S(1)}, u32[]{:S(2)}, u32[]{:S(2)}) collective-permute-start(bf16[16,2048]{1,0:T(8,128)(2,1)S(1)} %get-tuple-element.86), channel_id=1, source_target_pairs={{0,8},{1,9},{2,10},{3,11},{4,12},{5,13},{6,14},{7,15},{8,0},{9,1},... | collective-permute-start | bytes 196616 | tf_op jit(solution)/shard_map/ppermute | solution.py:64
  182.5 5.9 %collective-permute-start.37 = (bf16[16,2048]{1,0:T(8,128)(2,1)S(1)}, bf16[16,2048]{1,0:T(8,128)(2,1)S(1)}, u32[]{:S(2)}, u32[]{:S(2)}) collective-permute-start(bf16[16,2048]{1,0:T(8,128)(2,1)S(1)} %get-tuple-element.85), channel_id=1, source_target_pairs={{0,12},{1,13},{2,14},{3,15},{4,0},{5,1},{6,2},{7,3},{8,4},{9,5},{1... | collective-permute-start | bytes 196616 | tf_op jit(solution)/shard_map/ppermute | solution.py:64
  (11 other events, 79.2 us)

commit v5 on v4

--- a/solution.py
+++ b/solution.py
@@ -8,7 +8,7 @@
 from jax.experimental.pallas import tpu as pltpu
 from jax.sharding import PartitionSpec as P
 
-GATHER_SHARES = (3, 5)
+GATHER_SHARES = (2, 3, 3)
 SUM_SHARES = (3, 3, 2)
 MIB = 1024 * 1024
 BF16 = jnp.bfloat16
@@ -108,12 +108,17 @@
     rest = rest[pieces + 2 * blocks :]
     out = rest[-1]
     depth = weights[0].shape[1]
+    tile = out.shape[2]
+    part = sum(
+        dot(
+            x[:, h * depth : (h + 1) * depth],
+            jnp.concatenate([weights[h][0], weights[blocks + h][0]], axis=1),
+        )
+        for h in range(blocks)
+    )
     for i in range(2):
-        part = sum(
-            dot(x[:, h * depth : (h + 1) * depth], weights[i * blocks + h][0])
-            for h in range(blocks)
-        )
-        out[i] = part if len(rest) == 1 else rest[0][i] + part
+        now = part[:, i * tile : (i + 1) * tile]
+        out[i] = now if len(rest) == 1 else rest[0][i] + now
 
 
 def forward_chunk(pieces, frozen, start, first, tiles):
@@ -288,7 +293,7 @@
             jax.ShapeDtypeStruct((tokens, hidden), BF16),
             jax.ShapeDtypeStruct((tokens, wide), F32),
         ],
-        compiler_params=params(20),
+        compiler_params=params(44),
         cost_estimate=cost(
             4 * tokens * hidden * segments * wide, hidden * (tokens * 14 + segments * wide * 2)
         ),
@@ -400,44 +405,29 @@
     )(adapters, places, order, low, seg, *([down] * segments))
 
 
-def backward_kernel(gate, up, dgate, dup, near, far, total):
-    k = pl.program_id(0)
-    now, before = k % 2, (k + 1) % 2
+def backward_kernel(gate, up, dgate, dup, near, far):
     half = near.shape[0]
-
-    def store():
-        block = total[before].T.astype(BF16)
-        near[...] = block[:half]
-        far[...] = block[half:]
-
-    @pl.when(k < pl.num_programs(0) - 1)
-    def _():
-        store()
-        total[now] = dot(gate[0], dgate[...], ((1,), (1,))) + dot(up[0], dup[...], ((1,), (1,)))
-
-    @pl.when(k == pl.num_programs(0) - 1)
-    def _():
-        store()
+    term = dot(dgate[...], gate[0], ((1,), (1,))) + dot(dup[...], up[0], ((1,), (1,)))
+    near[...] = term[:half].astype(BF16)
+    far[...] = term[half:].astype(BF16)
 
 
 def backward_chunk(frozen, dgate, dup, first, step):
     tokens, hidden = dgate.shape
     block = tile_of(step, 512)
     base = first // block
-    count = step // block
     full = lambda shape: pl.BlockSpec(shape, lambda *a: (0,) * len(shape))
-    out = pl.BlockSpec((tokens // 2, block), lambda k: (0, jnp.maximum(k - 1, 0)))
+    out = pl.BlockSpec((tokens // 2, block), lambda k: (0, k))
 
     def weight(i):
-        return pl.BlockSpec((1, block, hidden), lambda k: (i, base + jnp.minimum(k, count - 1), 0))
+        return pl.BlockSpec((1, block, hidden), lambda k: (i, base + k, 0))
 
     return pl.pallas_call(
         backward_kernel,
-        grid=(count + 1,),
+        grid=(step // block,),
         in_specs=[weight(0), weight(1), full(dgate.shape), full(dup.shape)],
         out_specs=[out, out],
         out_shape=[jax.ShapeDtypeStruct((tokens // 2, step), BF16)] * 2,
-        scratch_shapes=[pltpu.VMEM((2, block, tokens), F32)],
         compiler_params=params(20),
         cost_estimate=cost(4 * tokens * step * hidden, 4 * step * hidden),
     )(frozen, frozen, dgate, dup)
@@ -550,24 +540,24 @@
 
     hidden = frozen.shape[2]
     tiles = hidden // tile_of(hidden, 256)
-    chunks = []
-    for share in GATHER_SHARES:
-        first = sum(v.shape[1] for v in chunks)
-        chunks.append(activations[:, first : first + width * share // sum(GATHER_SHARES)])
-    outer = []
-    for x in chunks:
-        x = torus.gather(after(x, outer[-1]) if outer else x, 0)
-        outer.append(x.reshape(a * rows, -1))
+    outer = torus.gather(activations, 0).reshape(a * rows, width)
     base = None
     gathered = []
-    for q, x in enumerate(outer):
-        near = [x] + [torus.move(x, 1, -k) for k in range(1, b)]
-        near[1:] = lax.optimization_barrier((*near[1:], base if q else outer[-1]))[:-1]
-        far = [torus.move(v, 2, -1) for v in near]
-        gathered.append([*near, *far])
-        first = sum(v.shape[1] for v in chunks[:q])
-        for cut in parts_of(tiles, 4 if q else 1):
-            base = forward_chunk(gathered[q], frozen, base, first, cut)
+    first = 0
+    for share in GATHER_SHARES:
+        step = width * share // sum(GATHER_SHARES)
+        x = outer[:, first : first + step]
+        if gathered:
+            x = after(x, gathered[-1][1])
+        inner = [torus.move(x, 1, -k) for k in range(1, b)]
+        if gathered:
+            inner = list(lax.optimization_barrier((*inner, base))[:-1])
+        near = [x, *inner]
+        gathered.append([*near, *[torus.move(v, 2, -1) for v in near]])
+        last = len(gathered) == len(GATHER_SHARES)
+        for cut in parts_of(tiles, 3 if last else 1):
+            base = forward_chunk(gathered[-1], frozen, base, first, cut)
+        first += step
 
     columns, partial_in = low_in_partial(
         gathered, segment[:, None], adapter_down_factors, seg_adapter, places, index, rows
@@ -596,31 +586,33 @@
     )
     side_far = torus.move(side_far, 2, 1)
     at = jnp.stack([index // c, core]).astype(jnp.int32)
-    blocks, sums = [], []
+    sums, inners, inner_moves, outer_moves, blocks = [], [], [], [], []
     for q, (first, step) in enumerate(cuts):
         if q:
-            ready = after(dgate, sums[0][0] if q > 1 else near)
-            near, far = backward_chunk(frozen, ready, dup, first, step)
-        sent = core_sum(near, torus.move(far, 2, 1), side, side_far, at, first, b)
-        sums.append(sent)
-    for q, (first, step) in enumerate(cuts):
-        hold = lambda v, wait: after(v, sums[-1][0]) if wait else v
-        last = q == len(cuts) - 1
+            near, far = backward_chunk(frozen, after(dgate, sums[-1][0]), dup, first, step)
+            ahead = inner_moves[q - 1] + (outer_moves[q - 2] if q > 1 else [])
+            far = lax.optimization_barrier((far, *ahead))[0]
+        far = torus.move(far, 2, 1)
+        sums.append(core_sum(near, far, side, side_far, at, first, b))
+        inner_moves.append([torus.move(sums[q][k], 1, k) for k in range(1, b)])
         total = sums[q][0].astype(F32)
-        for k in range(1, b):
-            total = total + hold(torus.move(sums[q][k], 1, k), q and not last).astype(F32)
-        inner = total.astype(BF16).reshape(a, rows, step)
+        for v in inner_moves[q]:
+            total = total + v.astype(F32)
+        inners.append(total.astype(BF16).reshape(a, rows, step))
+        outer_moves.append([torus.move(inners[q][k], 0, k) for k in range(1, a)])
+    for q, inner in enumerate(inners):
         total = inner[0].astype(F32)
-        for k in range(1, a):
-            total = total + hold(torus.move(inner[k], 0, k), not last).astype(F32)
+        for v in outer_moves[q]:
+            v = lax.optimization_barrier((v, *inner_moves[-1]))[0] if q < len(cuts) - 1 else v
+            total = total + v.astype(F32)
         blocks.append(total.astype(BF16))
     dinput = jnp.concatenate(blocks, axis=1)
     grad_b = grad_b_of(
-        dgate, dup, order, after(low_in, near), adapter[None, :], adapter_list,
+        dgate, dup, order, after(low_in, sums[-1][0]), adapter[None, :], adapter_list,
         grad_b[-1] if grad_b else None, thirds[-1],
     )
     grad_a = grad_a_of(
-        columns, order, after(low_out, sent[0]), adapter[:, None], adapter_list
+        columns, order, after(low_out, sums[-1][0]), adapter[:, None], adapter_list
     )
     return (dinput, grad_a, grad_b)
 

time: 190 us -> 206 us (1.084)
  waiting for transfers between devices: 26.8 us -> 38.6 us
  local copies, waits for them, and re-layouts: 7.76 us -> 16.3 us
  other arithmetic: 13.4 us -> 7.89 us
  Pallas kernels: 99.6 us -> 102 us
  starting transfers between devices: 40.4 us -> 38.2 us
    ppermute x32, waiting for transfers between devices: 26.3 us -> 36.3 us  [move(): return lax.ppermute(x, 'tensor', pairs)]
    unnamed x42 -> x76, local copies, waits for them, and re-layouts: 4.95 us -> 13.2 us
    ppermute x32, starting transfers between devices: 33.6 us -> 29 us  [move(): return lax.ppermute(x, 'tensor', pairs)]
    pallas_call x5, Pallas kernels: 33.3 us -> 36.8 us  [forward_chunk(): pl.pallas_call(functools.partial(forward_kernel, len(pieces), blocks), gr...]
    add x5, other arithmetic: 3.05 us -> 0.05 us  [exchange_sum(): x = x + lax.ppermute(x, 'tensor', pairs)]
    pallas_call x3, Pallas kernels: 6.08 us -> 3.37 us  [core_sum(): pl.pallas_call(functools.partial(core_sum_kernel, first // block), grid_s...]
    ppermute x6, starting transfers between devices: 6.83 us -> 9.2 us  [exchange_sum(): x = x + lax.ppermute(x, 'tensor', pairs)]
  transfers between devices with their start and end apart: 38 -> 38, of which waited for: 15 -> 12; matrix products, arithmetic and copies ran while one was open for 4% -> 4% of each run, Pallas kernels for 48% -> 43%
where the time goes in v5:
time: 206 us; the launch traced here: 205 us
  Pallas kernels  102 us (50%)
  waiting for transfers between devices  38.6 us (19%)
  starting transfers between devices  38.2 us (19%)
  local copies, waits for them, and re-layouts  16.3 us (8%)
  other arithmetic  7.89 us (4%)
    pallas_call x5, Pallas kernels, forward_chunk(): pl.pallas_call(functools.partial(forward_kernel, len(pieces), blocks), gr...  36.8 us
    ppermute x32, waiting for transfers between devices, move(): return lax.ppermute(x, 'tensor', pairs)  36.3 us
    pallas_call x3, Pallas kernels, backward_chunk(): pl.pallas_call(backward_kernel, grid=(step // block,), in_specs=[weight(0...  31 us
    ppermute x32, starting transfers between devices, move(): return lax.ppermute(x, 'tensor', pairs)  29 us
    unnamed x76, local copies, waits for them, and re-layouts  13.2 us
    pallas_call x3, Pallas kernels, grad_b_of(): pl.pallas_call(grad_b_kernel, grid=(last - first,), in_specs=specs, out_s...  12.7 us
    ppermute x6, starting transfers between devices, exchange_sum(): x = x + lax.ppermute(x, 'tensor', pairs)  9.2 us
    pallas_call x1, Pallas kernels, middle(): pl.pallas_call(functools.partial(middle_kernel, segments, rows), grid_spe...  8.9 us
  transfers between devices with their start and end apart: 38, of which 12 were waited for; matrix products, arithmetic and copies ran while one was open for 4% of the time, Pallas kernels for 43%

profile of v5, /device:TPU:0, one launch (start us, length us, event | category | flops | bytes accessed | tf_op | source)
XLA Modules:
  0.0 204.7 jit_solution(12887008739181016507)
XLA Ops:
  0.6 5.1 %collective-permute-start = (bf16[16,8192]{1,0:T(8,128)(2,1)}, bf16[16,8192]{1,0:T(8,128)(2,1)S(1)}, u32[]{:S(2)}, u32[]{:S(2)}) collective-permute-start(bf16[16,8192]{1,0:T(8,128)(2,1)} %param.8), channel_id=1, source_target_pairs={{0,12},{1,13},{2,14},{3,15},{4,0},{5,1},{6,2},{7,3},{8,4},{9,5},{1... | collective-permute-start | bytes 786440 | tf_op jit(solution)/shard_map/ppermute | solution.py:64
  5.7 1.0 collective-permute-start.2
  7.3 5.5 %collective-permute-done = bf16[16,8192]{1,0:T(8,128)(2,1)S(1)} collective-permute-done((bf16[16,8192]{1,0:T(8,128)(2,1)}, bf16[16,8192]{1,0:T(8,128)(2,1)S(1)}, u32[]{:S(2)}, u32[]{:S(2)}) %collective-permute-start) | collective-permute-done | bytes 262176 | tf_op jit(solution)/shard_map/ppermute | solution.py:64
  12.8 15.4 %collective-permute-done.1 = bf16[16,8192]{1,0:T(8,128)(2,1)S(1)} collective-permute-done((bf16[16,8192]{1,0:T(8,128)(2,1)}, bf16[16,8192]{1,0:T(8,128)(2,1)S(1)}, u32[]{:S(2)}, u32[]{:S(2)}) %collective-permute-start.1) | collective-permute-done | bytes 262176 | tf_op jit(solution)/shard_map/ppermute | solution.py:64
  28.3 1.1 pad_maximum_fusion
  29.4 1.6 collective-permute-start.3
  32.6 4.0 %collective-permute-done.3.rest_1_.rest_9_ = bf16[64,2048]{1,0:T(8,128)(2,1)S(1)} collective-permute-done((bf16[64,2048]{1,0:T(8,128)(2,1)S(1)}, bf16[64,2048]{1,0:T(8,128)(2,1)S(1)}, u32[]{:S(2)}, u32[]{:S(2)}) %collective-permute-start.3) | collective-permute-done | bytes 262176 | tf_op jit(solution)/shard_map/ppermute | solution.py:64
  37.5 1.5 collective-permute-start.4
  39.3 9.5 %shard_map.103.rest_10_ = f32[2,256,1792]{2,1,0:T(8,128)S(1)} custom-call(bf16[64,2048]{1,0:T(8,128)(2,1)S(1)} %slice.94.rest_0_.rest_8_, bf16[64,2048]{1,0:T(8,128)(2,1)S(1)} %collective-permute-done.3.rest_1_.rest_9_, bf16[64,2048]{1,0:T(8,128)(2,1)S(1)} %collective-permute-done.5.rest_2_.rest_10_, ...), custom_call_target="tpu_custom_call" | custom-call | flops 3758096384 | bytes 14680064 | tf_op jit(solution)/shard_map/pallas_call | solution.py:144
  48.9 1.8 copy-done.1
  53.1 2.3 %copy-done.2 = f32[2,256,1792]{2,1,0:T(8,128)S(1)} copy-done((f32[2,256,1792]{2,1,0:T(8,128)S(1)}, f32[2,256,1792]{2,1,0:T(8,128)}, u32[]{:S(2)}) %copy-start.2) | copy-done | bytes 3670040
  55.4 12.3 %shard_map.104.rest_10_ = f32[2,256,1792]{2,1,0:T(8,128)S(1)} custom-call(bf16[64,3072]{1,0:T(8,128)(2,1)} %get-tuple-element.41.rest_0_.rest_12_, bf16[64,3072]{1,0:T(8,128)(2,1)} %collective-permute-done.4.rest_1_.rest_13_, bf16[64,3072]{1,0:T(8,128)(2,1)} %collective-permute-done.8.rest_2_.rest_14_, ...), custom_call_target="tpu_custom_call", output_to_operand_aliasing={{}: (10, {})} | custom-call | flops 5637144576 | bytes 22020096 | tf_op jit(solution)/shard_map/pallas_call | solution.py:144
  67.7 1.8 copy-done.3
  77.2 2.8 %shard_map.108 = (bf16[256,512]{1,0:T(8,128)(2,1)S(1)}, f32[256,128]{1,0:T(8,128)S(1)}) custom-call(s32[8]{0:T(128)S(1)} %bitcast.35, s32[16]{0:T(128)S(1)} %get-tuple-element.80.places, s32[4]{0:T(128)S(1)} %pad_add_fusion.1.which, s32[256,1]{1,0:T(8,128)S(1)} %copy-done.15, bf16[24,512,128]{2,1,0:T(8,128)(2,1)S(1)} %copy-done, ...), custom_call_target="tpu_custom_call" | custom-call | flops 268435456 | bytes 1048576 | tf_op jit(solution)/shard_map/pallas_call | solution.py:210
  81.3 1.5 collective-permute-start.13
  83.3 2.3 %collective-permute-done.13 = f32[128,128]{1,0:T(8,128)S(1)} collective-permute-done((f32[128,128]{1,0:T(8,128)S(1)}, f32[128,128]{1,0:T(8,128)S(1)}, u32[]{:S(2)}, u32[]{:S(2)}) %collective-permute-start.13) | collective-permute-done | bytes 65568 | tf_op jit(solution)/shard_map/ppermute | solution.py:90
  85.7 1.3 collective-permute-start.14
  87.0 4.3 %shard_map.105.rest_10_ = f32[2,256,1792]{2,1,0:T(8,128)S(1)} custom-call(bf16[64,3072]{1,0:T(8,128)(2,1)S(1)} %get-tuple-element.43.rest_0_.rest_16_, bf16[64,3072]{1,0:T(8,128)(2,1)} %collective-permute-done.7.rest_1_.rest_17_, bf16[64,3072]{1,0:T(8,128)(2,1)} %collective-permute-done.10.rest_2_.rest_18_, ...), custom_call_target="tpu_custom_call", output_to_operand_aliasing={{}: (10, {})} | custom-call | flops 1610612736 | bytes 6291456 | tf_op jit(solution)/shard_map/pallas_call | solution.py:144
  91.4 1.9 collective-permute-start.15
  93.3 4.4 %shard_map.106.rest_10_ = f32[2,256,1792]{2,1,0:T(8,128)S(1)} custom-call(bf16[64,3072]{1,0:T(8,128)(2,1)S(1)} %get-tuple-element.43.rest_0_.rest_16_, bf16[64,3072]{1,0:T(8,128)(2,1)} %collective-permute-done.7.rest_1_.rest_17_, bf16[64,3072]{1,0:T(8,128)(2,1)} %collective-permute-done.10.rest_2_.rest_18_, ...), custom_call_target="tpu_custom_call", output_to_operand_aliasing={{}: (10, {})} | custom-call | flops 1610612736 | bytes 6291456 | tf_op jit(solution)/shard_map/pallas_call | solution.py:144
  97.9 6.3 %shard_map.107.base = f32[2,256,1792]{2,1,0:T(8,128)S(1)} custom-call(bf16[64,3072]{1,0:T(8,128)(2,1)S(1)} %get-tuple-element.43.rest_0_.rest_16_, bf16[64,3072]{1,0:T(8,128)(2,1)} %collective-permute-done.7.rest_1_.rest_17_, bf16[64,3072]{1,0:T(8,128)(2,1)} %collective-permute-done.10.rest_2_.rest_18_, ...), custom_call_target="tpu_custom_call", output_to_operand_aliasing={{}: (10, {})} | custom-call | flops 2415919104 | bytes 9437184 | tf_op jit(solution)/shard_map/pallas_call | solution.py:144
  104.3 8.9 %shard_map.109 = (bf16[256,1792]{1,0:T(8,128)(2,1)S(1)}, bf16[256,1792]{1,0:T(8,128)(2,1)S(1)}, f32[256,128]{1,0:T(8,128)S(1)}) custom-call(s32[8]{0:T(128)S(1)} %bitcast.36, s32[16]{0:T(128)S(1)} %get-tuple-element.80.places, f32[2,256,1792]{2,1,0:T(8,128)S(1)} %shard_map.107.base, bf16[256,1792]{1,0:T(8,128)(2,1)S(1)} %copy-done.23, ...), custom_call_target="tpu_custom_call" | custom-call | flops 1879048192 | bytes 10092544 | tf_op jit(solution)/shard_map/pallas_call | solution.py:277
  114.6 1.5 collective-permute-start.19
  116.1 3.8 %shard_map.111.rest_0_ = f32[24,128,1792]{2,1,0:T(8,128)} custom-call(bf16[256,1792]{1,0:T(8,128)(2,1)S(1)} %get-tuple-element.63.dgate, bf16[256,1792]{1,0:T(8,128)(2,1)S(1)} %get-tuple-element.47.dup, bf16[256,256]{1,0:T(8,128)(2,1)S(1)} %fusion.1.order, bf16[256,128]{1,0:T(8,128)(2,1)S(1)} %bitcast.25, s32[1,256]{1,0:T(1,128)S(1)} %bitcast.30), custom_call_target="tpu_custom_call" | custom-call | flops 805306368 | bytes 6291456 | tf_op jit(solution)/shard_map/pallas_call | solution.py:334
  120.0 2.1 %collective-permute-start.20 = (f32[128,128]{1,0:T(8,128)S(1)}, f32[128,128]{1,0:T(8,128)S(1)}, u32[]{:S(2)}, u32[]{:S(2)}) collective-permute-start(f32[128,128]{1,0:T(8,128)S(1)} %add.315), channel_id=1, source_target_pairs={{0,4},{1,5},{2,6},{3,7},{4,0},{5,1},{6,2},{7,3},{8,12},{9,13},{10,... | collective-permute-start | bytes 196616 | tf_op jit(solution)/shard_map/ppermute | solution.py:90
  122.0 3.8 %shard_map.112.rest_0_ = f32[24,128,1792]{2,1,0:T(8,128)} custom-call(bf16[256,1792]{1,0:T(8,128)(2,1)S(1)} %get-tuple-element.63.dgate, bf16[256,1792]{1,0:T(8,128)(2,1)S(1)} %get-tuple-element.47.dup, bf16[256,256]{1,0:T(8,128)(2,1)S(1)} %fusion.1.order, bf16[256,128]{1,0:T(8,128)(2,1)S(1)} %bitcast.26, ...), custom_call_target="tpu_custom_call", output_to_operand_aliasing={{}: (5, {})} | custom-call | flops 805306368 | bytes 6291456 | tf_op jit(solution)/shard_map/pallas_call | solution.py:334
  126.9 11.2 %shard_map.110 = (bf16[128,3072]{1,0:T(8,128)(2,1)S(1)}, bf16[128,3072]{1,0:T(8,128)(2,1)S(1)}) custom-call(bf16[2,8192,1792]{2,1,0:T(8,128)(2,1)} %up.5, bf16[2,8192,1792]{2,1,0:T(8,128)(2,1)} %up.5, bf16[256,1792]{1,0:T(8,128)(2,1)S(1)} %get-tuple-element.63.dgate, bf16[256,1792]{1,0:T(8,128)(2,1)S(1)} %get-tuple-element.47.dup), custom_call_target="tpu_custom_call" | custom-call | flops 5637144576 | bytes 22020096 | tf_op jit(solution)/shard_map/pallas_call | solution.py:425
  139.0 1.5 collective-permute-done.22
  140.5 1.4 shard_map.113
  142.1 1.3 collective-permute-done.23.side_far
  143.5 1.2 shard_map.114
  145.4 11.9 %shard_map.115 = (bf16[128,3072]{1,0:T(8,128)(2,1)S(1)}, bf16[128,3072]{1,0:T(8,128)(2,1)}) custom-call(bf16[2,8192,1792]{2,1,0:T(8,128)(2,1)} %up.5, bf16[2,8192,1792]{2,1,0:T(8,128)(2,1)} %up.5, bf16[256,1792]{1,0:T(8,128)(2,1)S(1)} %get-tuple-element.63.dgate, bf16[256,1792]{1,0:T(8,128)(2,1)S(1)} %get-tuple-element.47.dup), custom_call_target="tpu_custom_call" | custom-call | flops 5637144576 | bytes 22020096 | tf_op jit(solution)/shard_map/pallas_call | solution.py:425
  157.6 2.2 %collective-permute-done.26.far = bf16[128,3072]{1,0:T(8,128)(2,1)S(1)} collective-permute-done((bf16[128,3072]{1,0:T(8,128)(2,1)}, bf16[128,3072]{1,0:T(8,128)(2,1)S(1)}, u32[]{:S(2)}, u32[]{:S(2)}) %collective-permute-start.26) | collective-permute-done | bytes 786464 | tf_op jit(solution)/shard_map/ppermute | solution.py:64
  159.8 1.2 shard_map.116
  161.0 1.5 collective-permute-start.27
  163.0 2.0 collective-permute-start.28
  165.0 2.5 %collective-permute-start.29 = (bf16[16,3072]{1,0:T(8,128)(2,1)S(1)}, bf16[16,3072]{1,0:T(8,128)(2,1)S(1)}, u32[]{:S(2)}, u32[]{:S(2)}) collective-permute-start(bf16[16,3072]{1,0:T(8,128)(2,1)S(1)} %get-tuple-element.87), channel_id=1, source_target_pairs={{0,12},{1,13},{2,14},{3,15},{4,0},{5,1},{6,2},{7,3},{8,4},{9,5},{1... | collective-permute-start | bytes 294920 | tf_op jit(solution)/shard_map/ppermute | solution.py:64
  167.5 1.2 copy-done.6
  168.7 1.2 copy-done.9
  169.9 7.9 %shard_map.117 = (bf16[128,2048]{1,0:T(8,128)(2,1)S(1)}, bf16[128,2048]{1,0:T(8,128)(2,1)S(1)}) custom-call(bf16[2,8192,1792]{2,1,0:T(8,128)(2,1)} %up.5, bf16[2,8192,1792]{2,1,0:T(8,128)(2,1)} %up.5, bf16[256,1792]{1,0:T(8,128)(2,1)S(1)} %copy-done.6, bf16[256,1792]{1,0:T(8,128)(2,1)S(1)} %copy-done.9), custom_call_target="tpu_custom_call" | custom-call | flops 3758096384 | bytes 14680064 | tf_op jit(solution)/shard_map/pallas_call | solution.py:425
  178.0 1.8 collective-permute-done.30.far
  182.5 2.8 %collective-permute-start.34 = (bf16[16,3072]{1,0:T(8,128)(2,1)S(1)}, bf16[16,3072]{1,0:T(8,128)(2,1)S(1)}, u32[]{:S(2)}, u32[]{:S(2)}) collective-permute-start(bf16[16,3072]{1,0:T(8,128)(2,1)S(1)} %get-tuple-element.85), channel_id=1, source_target_pairs={{0,12},{1,13},{2,14},{3,15},{4,0},{5,1},{6,2},{7,3},{8,4},{9,5},{1... | collective-permute-start | bytes 294920 | tf_op jit(solution)/shard_map/ppermute | solution.py:64
  185.4 5.3 %shard_map.119 = f32[24,512,128]{2,1,0:T(8,128)} custom-call(bf16[256,512]{1,0:T(8,128)(2,1)S(1)} %copy-done.26, bf16[256,256]{1,0:T(8,128)(2,1)S(1)} %copy-done.12, bf16[256,128]{1,0:T(8,128)(2,1)S(1)} %bitcast.29, s32[256,1]{1,0:T(8,128)S(1)} %copy.24.adapter), custom_call_target="tpu_custom_call" | custom-call | flops 805306368 | bytes 6291456 | tf_op jit(solution)/shard_map/pallas_call | solution.py:364
  190.7 5.0 %shard_map.120 = f32[24,128,1792]{2,1,0:T(8,128)} custom-call(bf16[256,1792]{1,0:T(8,128)(2,1)S(1)} %copy-done.7, bf16[256,1792]{1,0:T(8,128)(2,1)S(1)} %copy-done.10, bf16[256,256]{1,0:T(8,128)(2,1)S(1)} %copy-done.12, bf16[256,128]{1,0:T(8,128)(2,1)S(1)} %bitcast.27, s32[1,256]{1,0:T(1,128)S(1)} %bitcast.33, ...), custom_call_target="tpu_custom_call", output_to_operand_aliasing={{}: (5, {})} | custom-call | flops 1207959552 | bytes 9437184 | tf_op jit(solution)/shard_map/pallas_call | solution.py:334
  196.5 1.5 collective-permute-start.36
  198.0 2.8 %collective-permute-start.37 = (bf16[16,2048]{1,0:T(8,128)(2,1)S(1)}, bf16[16,2048]{1,0:T(8,128)(2,1)S(1)}, u32[]{:S(2)}, u32[]{:S(2)}) collective-permute-start(bf16[16,2048]{1,0:T(8,128)(2,1)S(1)} %get-tuple-element.91), channel_id=1, source_target_pairs={{0,12},{1,13},{2,14},{3,15},{4,0},{5,1},{6,2},{7,3},{8,4},{9,5},{1... | collective-permute-start | bytes 196616 | tf_op jit(solution)/shard_map/ppermute | solution.py:64
  200.9 1.5 collective-permute-done.35
  202.5 1.4 collective-permute-done.36
  (180 shorter events, 24.9 us)
Async XLA Ops:
  0.6 12.2 %collective-permute-start = (bf16[16,8192]{1,0:T(8,128)(2,1)}, bf16[16,8192]{1,0:T(8,128)(2,1)S(1)}, u32[]{:S(2)}, u32[]{:S(2)}) collective-permute-start(bf16[16,8192]{1,0:T(8,128)(2,1)} %param.8), channel_id=1, source_target_pairs={{0,12},{1,13},{2,14},{3,15},{4,0},{5,1},{6,2},{7,3},{8,4},{9,5},{1... | collective-permute-start | bytes 786440 | tf_op jit(solution)/shard_map/ppermute | solution.py:64
  5.7 22.5 %collective-permute-start.1 = (bf16[16,8192]{1,0:T(8,128)(2,1)}, bf16[16,8192]{1,0:T(8,128)(2,1)S(1)}, u32[]{:S(2)}, u32[]{:S(2)}) collective-permute-start(bf16[16,8192]{1,0:T(8,128)(2,1)} %param.8), channel_id=1, source_target_pairs={{0,8},{1,9},{2,10},{3,11},{4,12},{5,13},{6,14},{7,15},{8,0},{9,1},... | collective-permute-start | bytes 786440 | tf_op jit(solution)/shard_map/ppermute | solution.py:64
  5.7 22.5 %collective-permute-start.2 = (bf16[16,8192]{1,0:T(8,128)(2,1)}, bf16[16,8192]{1,0:T(8,128)(2,1)S(1)}, u32[]{:S(2)}, u32[]{:S(2)}) collective-permute-start(bf16[16,8192]{1,0:T(8,128)(2,1)} %param.8), channel_id=1, source_target_pairs={{0,4},{1,5},{2,6},{3,7},{4,8},{5,9},{6,10},{7,11},{8,12},{9,13},{1... | collective-permute-start | bytes 786440 | tf_op jit(solution)/shard_map/ppermute | solution.py:64
  29.4 19.5 %copy-start.13 = (bf16[64,2048]{1,0:T(8,128)(2,1)}, bf16[64,2048]{1,0:T(8,128)(2,1)S(1)}, u32[]{:S(2)}) copy-start(bf16[64,2048]{1,0:T(8,128)(2,1)S(1)} %slice.94.rest_0_.rest_8_) | copy-start | bytes 786436
  29.4 7.2 %collective-permute-start.3 = (bf16[64,2048]{1,0:T(8,128)(2,1)S(1)}, bf16[64,2048]{1,0:T(8,128)(2,1)S(1)}, u32[]{:S(2)}, u32[]{:S(2)}) collective-permute-start(bf16[64,2048]{1,0:T(8,128)(2,1)S(1)} %slice.94.rest_0_.rest_8_), channel_id=1, source_target_pairs={{0,2},{1,3},{2,0},{3,1},{4,6},{5,7},{6,4},{7,5},{8,10},{9,11},{10,... | collective-permute-start | bytes 786440 | tf_op jit(solution)/shard_map/ppermute | solution.py:64
  32.6 6.7 %collective-permute-start.5 = (bf16[64,2048]{1,0:T(8,128)(2,1)S(1)}, bf16[64,2048]{1,0:T(8,128)(2,1)S(1)}, u32[]{:S(2)}, u32[]{:S(2)}) collective-permute-start(bf16[64,2048]{1,0:T(8,128)(2,1)S(1)} %slice.94.rest_0_.rest_8_), channel_id=1, source_target_pairs={{0,1},{1,0},{2,3},{3,2},{4,5},{5,4},{6,7},{7,6},{8,9},{9,8},{10,11... | collective-permute-start | bytes 786440 | tf_op jit(solution)/shard_map/ppermute | solution.py:64
  36.6 2.7 %collective-permute-start.6 = (bf16[64,2048]{1,0:T(8,128)(2,1)S(1)}, bf16[64,2048]{1,0:T(8,128)(2,1)S(1)}, u32[]{:S(2)}, u32[]{:S(2)}) collective-permute-start(bf16[64,2048]{1,0:T(8,128)(2,1)S(1)} %collective-permute-done.3.rest_1_.rest_9_), channel_id=1, source_target_pairs={{0,1},{1,0},{2,3},{3,2},{4,5},{5,4},{6,7},{7,6},{8,9},{9,8},{10,11... | collective-permute-start | bytes 786440 | tf_op jit(solution)/shard_map/ppermute | solution.py:64
  37.5 13.2 %collective-permute-start.4 = (bf16[64,3072]{1,0:T(8,128)(2,1)}, bf16[64,3072]{1,0:T(8,128)(2,1)}, u32[]{:S(2)}, u32[]{:S(2)}) collective-permute-start(bf16[64,3072]{1,0:T(8,128)(2,1)} %get-tuple-element.41.rest_0_.rest_12_), channel_id=1, source_target_pairs={{0,2},{1,3},{2,0},{3,1},{4,6},{5,7},{6,4},{7,5},{8,10},{9,11},{10,... | collective-permute-start | bytes 1179656 | tf_op jit(solution)/shard_map/ppermute | solution.py:64
  39.1 14.0 %collective-permute-start.8 = (bf16[64,3072]{1,0:T(8,128)(2,1)}, bf16[64,3072]{1,0:T(8,128)(2,1)}, u32[]{:S(2)}, u32[]{:S(2)}) collective-permute-start(bf16[64,3072]{1,0:T(8,128)(2,1)} %get-tuple-element.41.rest_0_.rest_12_), channel_id=1, source_target_pairs={{0,1},{1,0},{2,3},{3,2},{4,5},{5,4},{6,7},{7,6},{8,9},{9,8},{10,11... | collective-permute-start | bytes 1179656 | tf_op jit(solution)/shard_map/ppermute | solution.py:64
  50.7 2.4 %collective-permute-start.9 = (bf16[64,3072]{1,0:T(8,128)(2,1)}, bf16[64,3072]{1,0:T(8,128)(2,1)}, u32[]{:S(2)}, u32[]{:S(2)}) collective-permute-start(bf16[64,3072]{1,0:T(8,128)(2,1)} %collective-permute-done.4.rest_1_.rest_13_), channel_id=1, source_target_pairs={{0,1},{1,0},{2,3},{3,2},{4,5},{5,4},{6,7},{7,6},{8,9},{9,8},{10,11... | collective-permute-start | bytes 1179656 | tf_op jit(solution)/shard_map/ppermute | solution.py:64
  51.8 18.2 %copy-start.29 = (s32[256]{0:T(256)}, s32[256]{0:T(256)S(1)}, u32[]{:S(2)}) copy-start(s32[256]{0:T(256)S(1)} %convert_reduce_fusion) | copy-start | bytes 3076
  52.5 19.9 %copy-start = (bf16[24,512,128]{2,1,0:T(8,128)(2,1)S(1)}, bf16[24,512,128]{2,1,0:T(8,128)(2,1)}, u32[]{:S(2)}) copy-start(bf16[24,512,128]{2,1,0:T(8,128)(2,1)} %rest_7_.13) | copy-start | bytes 9437188
  52.5 17.0 %collective-permute-start.7 = (bf16[64,3072]{1,0:T(8,128)(2,1)S(1)}, bf16[64,3072]{1,0:T(8,128)(2,1)}, u32[]{:S(2)}, u32[]{:S(2)}) collective-permute-start(bf16[64,3072]{1,0:T(8,128)(2,1)S(1)} %get-tuple-element.43.rest_0_.rest_16_), channel_id=1, source_target_pairs={{0,2},{1,3},{2,0},{3,1},{4,6},{5,7},{6,4},{7,5},{8,10},{9,11},{10,... | collective-permute-start | bytes 1179656 | tf_op jit(solution)/shard_map/ppermute | solution.py:64
  53.0 19.4 %collective-permute-start.10 = (bf16[64,3072]{1,0:T(8,128)(2,1)S(1)}, bf16[64,3072]{1,0:T(8,128)(2,1)}, u32[]{:S(2)}, u32[]{:S(2)}) collective-permute-start(bf16[64,3072]{1,0:T(8,128)(2,1)S(1)} %get-tuple-element.43.rest_0_.rest_16_), channel_id=1, source_target_pairs={{0,1},{1,0},{2,3},{3,2},{4,5},{5,4},{6,7},{7,6},{8,9},{9,8},{10,11... | collective-permute-start | bytes 1179656 | tf_op jit(solution)/shard_map/ppermute | solution.py:64
  69.5 2.9 %collective-permute-start.11 = (bf16[64,3072]{1,0:T(8,128)(2,1)}, bf16[64,3072]{1,0:T(8,128)(2,1)}, u32[]{:S(2)}, u32[]{:S(2)}) collective-permute-start(bf16[64,3072]{1,0:T(8,128)(2,1)} %collective-permute-done.7.rest_1_.rest_17_), channel_id=1, source_target_pairs={{0,1},{1,0},{2,3},{3,2},{4,5},{5,4},{6,7},{7,6},{8,9},{9,8},{10,11... | collective-permute-start | bytes 1179656 | tf_op jit(solution)/shard_map/ppermute | solution.py:64
  72.4 68.1 %copy-start.11 = (bf16[256,256]{1,0:T(8,128)(2,1)}, bf16[256,256]{1,0:T(8,128)(2,1)S(1)}, u32[]{:S(2)}) copy-start(bf16[256,256]{1,0:T(8,128)(2,1)S(1)} %fusion.1.order) | copy-start | bytes 393220
  80.0 1.3 collective-permute-start.12
  81.3 4.3 %collective-permute-start.13 = (f32[128,128]{1,0:T(8,128)S(1)}, f32[128,128]{1,0:T(8,128)S(1)}, u32[]{:S(2)}, u32[]{:S(2)}) collective-permute-start(f32[128,128]{1,0:T(8,128)S(1)} %slice_add_fusion.1), channel_id=1, source_target_pairs={{0,2},{1,3},{2,0},{3,1},{4,6},{5,7},{6,4},{7,5},{8,10},{9,11},{10,... | collective-permute-start | bytes 196616 | tf_op jit(solution)/shard_map/ppermute | solution.py:90
  85.7 5.7 %collective-permute-start.14 = (f32[128,128]{1,0:T(8,128)S(1)}, f32[128,128]{1,0:T(8,128)S(1)}, u32[]{:S(2)}, u32[]{:S(2)}) collective-permute-start(f32[128,128]{1,0:T(8,128)S(1)} %add.304), channel_id=1, source_target_pairs={{0,4},{1,5},{2,6},{3,7},{4,0},{5,1},{6,2},{7,3},{8,12},{9,13},{10,... | collective-permute-start | bytes 196616 | tf_op jit(solution)/shard_map/ppermute | solution.py:90
  91.4 6.3 %collective-permute-start.15 = (f32[128,128]{1,0:T(8,128)S(1)}, f32[128,128]{1,0:T(8,128)S(1)}, u32[]{:S(2)}, u32[]{:S(2)}) collective-permute-start(f32[128,128]{1,0:T(8,128)S(1)} %add.305), channel_id=1, source_target_pairs={{0,8},{1,9},{2,10},{3,11},{4,12},{5,13},{6,14},{7,15},{8,0},{9,1},... | collective-permute-start | bytes 196616 | tf_op jit(solution)/shard_map/ppermute | solution.py:90
  97.9 6.4 %collective-permute-start.16 = (bf16[128,128]{1,0:T(8,128)(2,1)S(1)}, bf16[128,128]{1,0:T(8,128)(2,1)S(1)}, u32[]{:S(2)}, u32[]{:S(2)}) collective-permute-start(bf16[128,128]{1,0:T(8,128)(2,1)S(1)} %fusion.2), channel_id=1, source_target_pairs={{0,1},{1,0},{2,3},{3,2},{4,5},{5,4},{6,7},{7,6},{8,9},{9,8},{10,11... | collective-permute-start | bytes 98312 | tf_op jit(solution)/shard_map/ppermute | solution.py:64
  113.2 32.1 %copy-start.5 = (bf16[256,1792]{1,0:T(8,128)(2,1)}, bf16[256,1792]{1,0:T(8,128)(2,1)S(1)}, u32[]{:S(2)}) copy-start(bf16[256,1792]{1,0:T(8,128)(2,1)S(1)} %get-tuple-element.63.dgate) | copy-start | bytes 2752516
  113.2 32.1 %copy-start.8 = (bf16[256,1792]{1,0:T(8,128)(2,1)}, bf16[256,1792]{1,0:T(8,128)(2,1)S(1)}, u32[]{:S(2)}) copy-start(bf16[256,1792]{1,0:T(8,128)(2,1)S(1)} %get-tuple-element.47.dup) | copy-start | bytes 2752516
  113.3 1.4 collective-permute-start.18
  114.6 5.3 %collective-permute-start.19 = (f32[128,128]{1,0:T(8,128)S(1)}, f32[128,128]{1,0:T(8,128)S(1)}, u32[]{:S(2)}, u32[]{:S(2)}) collective-permute-start(f32[128,128]{1,0:T(8,128)S(1)} %slice_add_fusion), channel_id=1, source_target_pairs={{0,2},{1,3},{2,0},{3,1},{4,6},{5,7},{6,4},{7,5},{8,10},{9,11},{10,... | collective-permute-start | bytes 196616 | tf_op jit(solution)/shard_map/ppermute | solution.py:90
  120.0 5.9 %collective-permute-start.20 = (f32[128,128]{1,0:T(8,128)S(1)}, f32[128,128]{1,0:T(8,128)S(1)}, u32[]{:S(2)}, u32[]{:S(2)}) collective-permute-start(f32[128,128]{1,0:T(8,128)S(1)} %add.315), channel_id=1, source_target_pairs={{0,4},{1,5},{2,6},{3,7},{4,0},{5,1},{6,2},{7,3},{8,12},{9,13},{10,... | collective-permute-start | bytes 196616 | tf_op jit(solution)/shard_map/ppermute | solution.py:90
  125.9 12.3 %collective-permute-start.21 = (f32[128,128]{1,0:T(8,128)S(1)}, f32[128,128]{1,0:T(8,128)S(1)}, u32[]{:S(2)}, u32[]{:S(2)}) collective-permute-start(f32[128,128]{1,0:T(8,128)S(1)} %add.316), channel_id=1, source_target_pairs={{0,8},{1,9},{2,10},{3,11},{4,12},{5,13},{6,14},{7,15},{8,0},{9,1},... | collective-permute-start | bytes 196616 | tf_op jit(solution)/shard_map/ppermute | solution.py:90
  138.1 5.4 %collective-permute-start.17 = (bf16[128,3072]{1,0:T(8,128)(2,1)S(1)}, bf16[128,3072]{1,0:T(8,128)(2,1)S(1)}, u32[]{:S(2)}, u32[]{:S(2)}) collective-permute-start(bf16[128,3072]{1,0:T(8,128)(2,1)S(1)} %get-tuple-element.49), channel_id=1, source_target_pairs={{0,1},{1,0},{2,3},{3,2},{4,5},{5,4},{6,7},{7,6},{8,9},{9,8},{10,11... | collective-permute-start | bytes 2359304 | tf_op jit(solution)/shard_map/ppermute | solution.py:64
  138.3 2.2 %collective-permute-start.22 = (bf16[128,128]{1,0:T(8,128)(2,1)S(1)}, bf16[128,128]{1,0:T(8,128)(2,1)S(1)}, u32[]{:S(2)}, u32[]{:S(2)}) collective-permute-start(bf16[128,128]{1,0:T(8,128)(2,1)S(1)} %fusion.3), channel_id=1, source_target_pairs={{0,1},{1,0},{2,3},{3,2},{4,5},{5,4},{6,7},{7,6},{8,9},{9,8},{10,11... | collective-permute-start | bytes 98312 | tf_op jit(solution)/shard_map/ppermute | solution.py:64
  141.9 1.6 collective-permute-start.23
  144.7 12.6 %collective-permute-start.24 = (bf16[64,3072]{1,0:T(8,128)(2,1)S(1)}, bf16[64,3072]{1,0:T(8,128)(2,1)S(1)}, u32[]{:S(2)}, u32[]{:S(2)}) collective-permute-start(bf16[64,3072]{1,0:T(8,128)(2,1)S(1)} %get-tuple-element.57), channel_id=1, source_target_pairs={{0,2},{1,3},{2,0},{3,1},{4,6},{5,7},{6,4},{7,5},{8,10},{9,11},{10,... | collective-permute-start | bytes 1179656 | tf_op jit(solution)/shard_map/ppermute | solution.py:64
  157.3 2.5 %collective-permute-start.26 = (bf16[128,3072]{1,0:T(8,128)(2,1)}, bf16[128,3072]{1,0:T(8,128)(2,1)S(1)}, u32[]{:S(2)}, u32[]{:S(2)}) collective-permute-start(bf16[128,3072]{1,0:T(8,128)(2,1)} %get-tuple-element.61), channel_id=1, source_target_pairs={{0,1},{1,0},{2,3},{3,2},{4,5},{5,4},{6,7},{7,6},{8,9},{9,8},{10,11... | collective-permute-start | bytes 2359304 | tf_op jit(solution)/shard_map/ppermute | solution.py:64
  161.0 16.8 %collective-permute-start.27 = (bf16[64,3072]{1,0:T(8,128)(2,1)S(1)}, bf16[64,3072]{1,0:T(8,128)(2,1)S(1)}, u32[]{:S(2)}, u32[]{:S(2)}) collective-permute-start(bf16[64,3072]{1,0:T(8,128)(2,1)S(1)} %get-tuple-element.66), channel_id=1, source_target_pairs={{0,2},{1,3},{2,0},{3,1},{4,6},{5,7},{6,4},{7,5},{8,10},{9,11},{10,... | collective-permute-start | bytes 1179656 | tf_op jit(solution)/shard_map/ppermute | solution.py:64
  162.5 15.3 %collective-permute-start.25 = (bf16[16,3072]{1,0:T(8,128)(2,1)S(1)}, bf16[16,3072]{1,0:T(8,128)(2,1)S(1)}, u32[]{:S(2)}, u32[]{:S(2)}) collective-permute-start(bf16[16,3072]{1,0:T(8,128)(2,1)S(1)} %get-tuple-element.89), channel_id=1, source_target_pairs={{0,4},{1,5},{2,6},{3,7},{4,8},{5,9},{6,10},{7,11},{8,12},{9,13},{1... | collective-permute-start | bytes 294920 | tf_op jit(solution)/shard_map/ppermute | solution.py:64
  163.0 14.8 %collective-permute-start.28 = (bf16[16,3072]{1,0:T(8,128)(2,1)S(1)}, bf16[16,3072]{1,0:T(8,128)(2,1)S(1)}, u32[]{:S(2)}, u32[]{:S(2)}) collective-permute-start(bf16[16,3072]{1,0:T(8,128)(2,1)S(1)} %get-tuple-element.88), channel_id=1, source_target_pairs={{0,8},{1,9},{2,10},{3,11},{4,12},{5,13},{6,14},{7,15},{8,0},{9,1},... | collective-permute-start | bytes 294920 | tf_op jit(solution)/shard_map/ppermute | solution.py:64
  165.0 12.8 %collective-permute-start.29 = (bf16[16,3072]{1,0:T(8,128)(2,1)S(1)}, bf16[16,3072]{1,0:T(8,128)(2,1)S(1)}, u32[]{:S(2)}, u32[]{:S(2)}) collective-permute-start(bf16[16,3072]{1,0:T(8,128)(2,1)S(1)} %get-tuple-element.87), channel_id=1, source_target_pairs={{0,12},{1,13},{2,14},{3,15},{4,0},{5,1},{6,2},{7,3},{8,4},{9,5},{1... | collective-permute-start | bytes 294920 | tf_op jit(solution)/shard_map/ppermute | solution.py:64
  169.9 15.5 %copy-start.12 = (bf16[256,256]{1,0:T(8,128)(2,1)S(1)}, bf16[256,256]{1,0:T(8,128)(2,1)}, u32[]{:S(2)}) copy-start(bf16[256,256]{1,0:T(8,128)(2,1)} %copy-done.11) | copy-start | bytes 393220
  169.9 15.5 %copy-start.26 = (bf16[256,512]{1,0:T(8,128)(2,1)S(1)}, bf16[256,512]{1,0:T(8,128)(2,1)}, u32[]{:S(2)}) copy-start(bf16[256,512]{1,0:T(8,128)(2,1)} %copy-done.25) | copy-start | bytes 786436
  177.7 12.9 %copy-start.7 = (bf16[256,1792]{1,0:T(8,128)(2,1)S(1)}, bf16[256,1792]{1,0:T(8,128)(2,1)}, u32[]{:S(2)}) copy-start(bf16[256,1792]{1,0:T(8,128)(2,1)} %copy-done.5) | copy-start | bytes 2752516
  177.8 12.9 %copy-start.10 = (bf16[256,1792]{1,0:T(8,128)(2,1)S(1)}, bf16[256,1792]{1,0:T(8,128)(2,1)}, u32[]{:S(2)}) copy-start(bf16[256,1792]{1,0:T(8,128)(2,1)} %copy-done.8) | copy-start | bytes 2752516
  177.8 2.0 collective-permute-start.30
  180.8 15.0 %collective-permute-start.31 = (bf16[64,2048]{1,0:T(8,128)(2,1)S(1)}, bf16[64,2048]{1,0:T(8,128)(2,1)S(1)}, u32[]{:S(2)}, u32[]{:S(2)}) collective-permute-start(bf16[64,2048]{1,0:T(8,128)(2,1)S(1)} %get-tuple-element.68), channel_id=1, source_target_pairs={{0,2},{1,3},{2,0},{3,1},{4,6},{5,7},{6,4},{7,5},{8,10},{9,11},{10,... | collective-permute-start | bytes 786440 | tf_op jit(solution)/shard_map/ppermute | solution.py:64
  181.5 14.2 %collective-permute-start.32 = (bf16[16,3072]{1,0:T(8,128)(2,1)S(1)}, bf16[16,3072]{1,0:T(8,128)(2,1)S(1)}, u32[]{:S(2)}, u32[]{:S(2)}) collective-permute-start(bf16[16,3072]{1,0:T(8,128)(2,1)S(1)} %get-tuple-element.84), channel_id=1, source_target_pairs={{0,4},{1,5},{2,6},{3,7},{4,8},{5,9},{6,10},{7,11},{8,12},{9,13},{1... | collective-permute-start | bytes 294920 | tf_op jit(solution)/shard_map/ppermute | solution.py:64
  181.5 14.2 %collective-permute-start.33 = (bf16[16,3072]{1,0:T(8,128)(2,1)S(1)}, bf16[16,3072]{1,0:T(8,128)(2,1)S(1)}, u32[]{:S(2)}, u32[]{:S(2)}) collective-permute-start(bf16[16,3072]{1,0:T(8,128)(2,1)S(1)} %get-tuple-element.86), channel_id=1, source_target_pairs={{0,8},{1,9},{2,10},{3,11},{4,12},{5,13},{6,14},{7,15},{8,0},{9,1},... | collective-permute-start | bytes 294920 | tf_op jit(solution)/shard_map/ppermute | solution.py:64
  182.5 13.2 %collective-permute-start.34 = (bf16[16,3072]{1,0:T(8,128)(2,1)S(1)}, bf16[16,3072]{1,0:T(8,128)(2,1)S(1)}, u32[]{:S(2)}, u32[]{:S(2)}) collective-permute-start(bf16[16,3072]{1,0:T(8,128)(2,1)S(1)} %get-tuple-element.85), channel_id=1, source_target_pairs={{0,12},{1,13},{2,14},{3,15},{4,0},{5,1},{6,2},{7,3},{8,4},{9,5},{1... | collective-permute-start | bytes 294920 | tf_op jit(solution)/shard_map/ppermute | solution.py:64
  195.8 6.6 %collective-permute-start.35 = (bf16[16,2048]{1,0:T(8,128)(2,1)S(1)}, bf16[16,2048]{1,0:T(8,128)(2,1)S(1)}, u32[]{:S(2)}, u32[]{:S(2)}) collective-permute-start(bf16[16,2048]{1,0:T(8,128)(2,1)S(1)} %get-tuple-element.90), channel_id=1, source_target_pairs={{0,4},{1,5},{2,6},{3,7},{4,8},{5,9},{6,10},{7,11},{8,12},{9,13},{1... | collective-permute-start | bytes 196616 | tf_op jit(solution)/shard_map/ppermute | solution.py:64
  196.5 7.4 %collective-permute-start.36 = (bf16[16,2048]{1,0:T(8,128)(2,1)S(1)}, bf16[16,2048]{1,0:T(8,128)(2,1)S(1)}, u32[]{:S(2)}, u32[]{:S(2)}) collective-permute-start(bf16[16,2048]{1,0:T(8,128)(2,1)S(1)} %get-tuple-element.92), channel_id=1, source_target_pairs={{0,8},{1,9},{2,10},{3,11},{4,12},{5,13},{6,14},{7,15},{8,0},{9,1},... | collective-permute-start | bytes 196616 | tf_op jit(solution)/shard_map/ppermute | solution.py:64
  198.0 5.9 %collective-permute-start.37 = (bf16[16,2048]{1,0:T(8,128)(2,1)S(1)}, bf16[16,2048]{1,0:T(8,128)(2,1)S(1)}, u32[]{:S(2)}, u32[]{:S(2)}) collective-permute-start(bf16[16,2048]{1,0:T(8,128)(2,1)S(1)} %get-tuple-element.91), channel_id=1, source_target_pairs={{0,12},{1,13},{2,14},{3,15},{4,0},{5,1},{6,2},{7,3},{8,4},{9,5},{1... | collective-permute-start | bytes 196616 | tf_op jit(solution)/shard_map/ppermute | solution.py:64
  (28 other events, 173.9 us)

commit v6 on v5

--- a/solution.py
+++ b/solution.py
@@ -1,5 +1,4 @@
 import functools
-import math
 
 import jax
 import jax.numpy as jnp
@@ -8,10 +7,12 @@
 from jax.experimental.pallas import tpu as pltpu
 from jax.sharding import PartitionSpec as P
 
-GATHER_SHARES = (2, 3, 3)
+GATHER_SHARES = (3, 5)
 SUM_SHARES = (3, 3, 2)
 MIB = 1024 * 1024
 BF16 = jnp.bfloat16
+DEPTH = 3
+ONCE = pl.Buffered(1)
 F32 = jnp.float32
 
 
@@ -102,23 +103,49 @@
         return (((cs - core) % c * b + (bs - inner) % b) * a + (zs - outer) % a).reshape(-1)
 
 
-def forward_kernel(pieces, blocks, *rest):
-    x = jnp.concatenate([v[...] for v in rest[:pieces]], axis=0)
-    weights = rest[pieces : pieces + 2 * blocks]
-    rest = rest[pieces + 2 * blocks :]
-    out = rest[-1]
-    depth = weights[0].shape[1]
-    tile = out.shape[2]
-    part = sum(
-        dot(
-            x[:, h * depth : (h + 1) * depth],
-            jnp.concatenate([weights[h][0], weights[blocks + h][0]], axis=1),
-        )
-        for h in range(blocks)
-    )
+def tile_at(ref, n, tile):
+    if ref.shape[1] == tile:
+        return ref
+    return ref.at[:, pl.ds(pl.multiple_of(n * tile, tile), tile)]
+
+
+def ring(fetch, k, count):
+    @pl.when(k == 0)
+    def _():
+        for j in range(min(DEPTH - 1, count)):
+            for copy in fetch(j, j):
+                copy.start()
+
+    @pl.when(k + DEPTH - 1 < count)
+    def _():
+        for copy in fetch(k + DEPTH - 1, (k + DEPTH - 1) % DEPTH):
+            copy.start()
+
+    for copy in fetch(k, k % DEPTH):
+        copy.wait()
+    return k % DEPTH
+
+
+def forward_kernel(pieces, low, count, first, *rest):
+    parts, frozen, rest = rest[:pieces], rest[pieces], rest[pieces + 1 :]
+    out, held, arrived = rest[-3:]
+    step, tile = held.shape[2:]
+
+    def fetch(n, slot):
+        return [
+            pltpu.make_async_copy(
+                tile_at(frozen.at[i, pl.ds(first, step)], low + n, tile),
+                held.at[slot, i],
+                arrived.at[slot, i],
+            )
+            for i in range(2)
+        ]
+
+    slot = ring(fetch, pl.program_id(0), count)
+    x = jnp.concatenate([v[...] for v in parts], axis=0)
     for i in range(2):
-        now = part[:, i * tile : (i + 1) * tile]
-        out[i] = now if len(rest) == 1 else rest[0][i] + now
+        part = dot(x, held[slot, i])
+        out[i] = part if len(rest) == 3 else rest[0][i] + part
 
 
 def forward_chunk(pieces, frozen, start, first, tiles):
@@ -126,27 +153,25 @@
     tokens = sum(v.shape[0] for v in pieces)
     hidden = frozen.shape[2]
     tile = tile_of(hidden, 256)
-    depth = math.gcd(first, step)
-    blocks = step // depth
     low, high = tiles
     across = pl.BlockSpec((2, tokens, tile), lambda n: (0, 0, low + n))
-
-    def weight(i, h):
-        return pl.BlockSpec((1, depth, tile), lambda n: (i, first // depth + h, low + n))
-
-    operands = [*pieces] + [frozen] * (2 * blocks)
-    specs = [pl.BlockSpec(v.shape, lambda n: (0, 0)) for v in pieces]
-    specs += [weight(i, h) for i in range(2) for h in range(blocks)]
+    operands = [*pieces, frozen]
+    specs = [pl.BlockSpec(v.shape, lambda n: (0, 0), pipeline_mode=ONCE) for v in pieces]
+    specs.append(pl.BlockSpec(memory_space=pltpu.HBM))
     if start is not None:
         operands.append(start)
         specs.append(across)
     count = high - low
     return pl.pallas_call(
-        functools.partial(forward_kernel, len(pieces), blocks),
+        functools.partial(forward_kernel, len(pieces), low, count, first),
         grid=(count,),
         in_specs=specs,
         out_specs=across,
         out_shape=jax.ShapeDtypeStruct((2, tokens, hidden), F32),
+        scratch_shapes=[
+            pltpu.VMEM((DEPTH, 2, step, tile), BF16),
+            pltpu.SemaphoreType.DMA((DEPTH, 2)),
+        ],
         input_output_aliases={} if start is None else {len(operands) - 1: 0},
         compiler_params=params(24),
         cost_estimate=cost(4 * tokens * step * tile * count, 4 * step * tile * count),
@@ -224,30 +249,45 @@
     )(adapters, places, which, seg, *([down] * segments), *[v for pieces in chunks for v in pieces])
 
 
-def middle_kernel(segments, rows, adapters, places, base, dhidden, token_order, order, low, seg, *rest):
-    factors = rest[:segments]
-    dgate, dup, out, left, back = rest[segments:]
-    rank = low.shape[1] // 2
+def middle_kernel(rows, adapters, places, base, dhidden, token_order, order, low, seg, up, *rest):
+    dgate, dup, out, left, back, factors, arrived = rest
+    segments, wide, tile = factors.shape[1:]
+    rank = wide // 2
     tokens = order.shape[0]
     n = pl.program_id(0)
+    slot = n % 2
     lane = lax.broadcasted_iota(jnp.int32, (tokens, segments * rank), 1) // rank
     mask = lane == seg[...]
 
+    def fetch(n, slot, s):
+        return pltpu.make_async_copy(
+            tile_at(up.at[adapters[s]], n, tile), factors.at[slot, s], arrived.at[slot, s]
+        )
+
     @pl.when(n == 0)
     def _():
+        for s in range(segments):
+            fetch(0, 0, s).start()
         mine = dot(order[...], low[...])
         for i in range(2):
-            wide = jnp.concatenate([mine[:, i * rank : (i + 1) * rank]] * segments, axis=1)
-            left[i] = jnp.where(mask, wide, 0.0).astype(BF16)
+            block = jnp.concatenate([mine[:, i * rank : (i + 1) * rank]] * segments, axis=1)
+            left[i] = jnp.where(mask, block, 0.0).astype(BF16)
         back[...] = jnp.zeros_like(back)
 
-    up_g = jnp.concatenate([f[0, :rank] for f in factors], axis=0)
-    up_u = jnp.concatenate([f[0, rank:] for f in factors], axis=0)
+    @pl.when(n + 1 < pl.num_programs(0))
+    def _():
+        for s in range(segments):
+            fetch(n + 1, 1 - slot, s).start()
+
+    for s in range(segments):
+        fetch(n, slot, s).wait()
+    up_g = jnp.concatenate([factors[slot, s, :rank] for s in range(segments)], axis=0)
+    up_u = jnp.concatenate([factors[slot, s, rank:] for s in range(segments)], axis=0)
     gate = base[0] + dot(left[0], up_g)
-    up = base[1] + dot(left[1], up_u)
+    up_sum = base[1] + dot(left[1], up_u)
     grad = dot(token_order[...], dhidden[...])
     sigma = 1.0 / (1.0 + jnp.exp(-gate))
-    g = (grad * up * sigma * (1.0 + gate * (1.0 - sigma))).astype(BF16)
+    g = (grad * up_sum * sigma * (1.0 + gate * (1.0 - sigma))).astype(BF16)
     u = (grad * gate * sigma).astype(BF16)
     dgate[...] = g
     dup[...] = u
@@ -270,22 +310,20 @@
     tile = tile_of(hidden, 256)
     full = lambda shape: pl.BlockSpec(shape, lambda *a: (0,) * len(shape))
     across = lambda lead: pl.BlockSpec(lead + (tokens, tile), lambda n, *a: (0,) * len(lead) + (0, n))
-
-    def factor(s):
-        return pl.BlockSpec((1, wide, tile), lambda n, adapters, places: (adapters[s], 0, n))
-
-    return pl.pallas_call(
-        functools.partial(middle_kernel, segments, rows),
+    return pl.pallas_call(
+        functools.partial(middle_kernel, rows),
         grid_spec=pltpu.PrefetchScalarGridSpec(
             num_scalar_prefetch=2,
             grid=(hidden // tile,),
             in_specs=[across((2,)), across(())]
             + [full(v.shape) for v in (token_order, order, low, seg)]
-            + [factor(s) for s in range(segments)],
+            + [pl.BlockSpec(memory_space=pltpu.HBM)],
             out_specs=[across(()), across(()), full((tokens, wide))],
             scratch_shapes=[
                 pltpu.VMEM((2, tokens, segments * wide // 2), BF16),
                 pltpu.VMEM((2, tokens, segments * wide // 2), F32),
+                pltpu.VMEM((2, segments, wide, tile), BF16),
+                pltpu.SemaphoreType.DMA((2, segments)),
             ],
         ),
         out_shape=[
@@ -293,11 +331,11 @@
             jax.ShapeDtypeStruct((tokens, hidden), BF16),
             jax.ShapeDtypeStruct((tokens, wide), F32),
         ],
-        compiler_params=params(44),
+        compiler_params=params(20),
         cost_estimate=cost(
             4 * tokens * hidden * segments * wide, hidden * (tokens * 14 + segments * wide * 2)
         ),
-    )(adapters, places, base, dhidden, token_order, order, low, seg, *([up] * segments))
+    )(adapters, places, base, dhidden, token_order, order, low, seg, up)
 
 
 def grad_b_kernel(dgate, dup, order, low, adapter, *rest):
@@ -405,9 +443,19 @@
     )(adapters, places, order, low, seg, *([down] * segments))
 
 
-def backward_kernel(gate, up, dgate, dup, near, far):
+def backward_kernel(count, first, frozen, dgate, dup, near, far, held, arrived):
     half = near.shape[0]
-    term = dot(dgate[...], gate[0], ((1,), (1,))) + dot(dup[...], up[0], ((1,), (1,)))
+    block = held.shape[2]
+
+    def fetch(k, slot):
+        rows = pl.ds(pl.multiple_of(first + k * block, block), block)
+        return [
+            pltpu.make_async_copy(frozen.at[i, rows, :], held.at[slot, i], arrived.at[slot, i])
+            for i in range(2)
+        ]
+
+    slot = ring(fetch, pl.program_id(0), count)
+    term = dot(dgate[...], held[slot, 0], ((1,), (1,))) + dot(dup[...], held[slot, 1], ((1,), (1,)))
     near[...] = term[:half].astype(BF16)
     far[...] = term[half:].astype(BF16)
 
@@ -415,22 +463,22 @@
 def backward_chunk(frozen, dgate, dup, first, step):
     tokens, hidden = dgate.shape
     block = tile_of(step, 512)
-    base = first // block
-    full = lambda shape: pl.BlockSpec(shape, lambda *a: (0,) * len(shape))
+    count = step // block
+    full = lambda shape: pl.BlockSpec(shape, lambda k: (0, 0), pipeline_mode=ONCE)
     out = pl.BlockSpec((tokens // 2, block), lambda k: (0, k))
-
-    def weight(i):
-        return pl.BlockSpec((1, block, hidden), lambda k: (i, base + k, 0))
-
-    return pl.pallas_call(
-        backward_kernel,
-        grid=(step // block,),
-        in_specs=[weight(0), weight(1), full(dgate.shape), full(dup.shape)],
+    return pl.pallas_call(
+        functools.partial(backward_kernel, count, first),
+        grid=(count,),
+        in_specs=[pl.BlockSpec(memory_space=pltpu.HBM), full(dgate.shape), full(dup.shape)],
         out_specs=[out, out],
         out_shape=[jax.ShapeDtypeStruct((tokens // 2, step), BF16)] * 2,
+        scratch_shapes=[
+            pltpu.VMEM((DEPTH, 2, block, hidden), BF16),
+            pltpu.SemaphoreType.DMA((DEPTH, 2)),
+        ],
         compiler_params=params(20),
         cost_estimate=cost(4 * tokens * step * hidden, 4 * step * hidden),
-    )(frozen, frozen, dgate, dup)
+    )(frozen, dgate, dup)
 
 
 def core_sum_kernel(base, at, near, far, side, side_far, *outs):
@@ -540,24 +588,24 @@
 
     hidden = frozen.shape[2]
     tiles = hidden // tile_of(hidden, 256)
-    outer = torus.gather(activations, 0).reshape(a * rows, width)
+    chunks = []
+    for share in GATHER_SHARES:
+        first = sum(v.shape[1] for v in chunks)
+        chunks.append(activations[:, first : first + width * share // sum(GATHER_SHARES)])
+    outer = []
+    for x in chunks:
+        x = torus.gather(after(x, outer[-1]) if outer else x, 0)
+        outer.append(x.reshape(a * rows, -1))
     base = None
     gathered = []
-    first = 0
-    for share in GATHER_SHARES:
-        step = width * share // sum(GATHER_SHARES)
-        x = outer[:, first : first + step]
-        if gathered:
-            x = after(x, gathered[-1][1])
-        inner = [torus.move(x, 1, -k) for k in range(1, b)]
-        if gathered:
-            inner = list(lax.optimization_barrier((*inner, base))[:-1])
-        near = [x, *inner]
-        gathered.append([*near, *[torus.move(v, 2, -1) for v in near]])
-        last = len(gathered) == len(GATHER_SHARES)
-        for cut in parts_of(tiles, 3 if last else 1):
-            base = forward_chunk(gathered[-1], frozen, base, first, cut)
-        first += step
+    for q, x in enumerate(outer):
+        near = [x] + [torus.move(x, 1, -k) for k in range(1, b)]
+        near[1:] = lax.optimization_barrier((*near[1:], base if q else outer[-1]))[:-1]
+        far = [torus.move(v, 2, -1) for v in near]
+        gathered.append([*near, *far])
+        first = sum(v.shape[1] for v in chunks[:q])
+        for cut in parts_of(tiles, 4 if q else 1):
+            base = forward_chunk(gathered[q], frozen, base, first, cut)
 
     columns, partial_in = low_in_partial(
         gathered, segment[:, None], adapter_down_factors, seg_adapter, places, index, rows

time: 206 us -> 176 us (0.85)
  local copies, waits for them, and re-layouts: 16.3 us -> 4.86 us
  Pallas kernels: 102 us -> 90.6 us
  waiting for transfers between devices: 38.6 us -> 32.1 us
  starting transfers between devices: 38.2 us -> 40.7 us
    pallas_call x9, Pallas kernels: 76.7 us -> 65 us  [the longest x5 31.7 us: forward_chunk(): pl.pallas_call(functools.partial(forward_kernel, len(pieces), low, count,...]
    unnamed x76 -> x18, local copies, waits for them, and re-layouts: 13.2 us -> 2.05 us
    ppermute x32, starting transfers between devices: 29 us -> 33.3 us  [move(): return lax.ppermute(x, 'tensor', pairs)]
    ppermute x32, waiting for transfers between devices: 36.3 us -> 32.1 us  [move(): return lax.ppermute(x, 'tensor', pairs)]
    ppermute x6, waiting for transfers between devices: 2.35 us -> 0.02 us  [exchange_sum(): x = x + lax.ppermute(x, 'tensor', pairs)]
  transfers between devices with their start and end apart: 38 -> 38, of which waited for: 12 -> 15; matrix products, arithmetic and copies ran while one was open for 4% -> 4% of each run, Pallas kernels for 43% -> 44%
where the time goes in v6:
time: 176 us; the launch traced here: 175 us
  Pallas kernels  90.6 us (51%)
  starting transfers between devices  40.7 us (23%)
  waiting for transfers between devices  32.1 us (18%)
  other arithmetic  5.95 us (3%)
  local copies, waits for them, and re-layouts  4.86 us (3%)
    ppermute x32, starting transfers between devices, move(): return lax.ppermute(x, 'tensor', pairs)  33.3 us
    ppermute x32, waiting for transfers between devices, move(): return lax.ppermute(x, 'tensor', pairs)  32.1 us
    pallas_call x5, Pallas kernels, forward_chunk(): pl.pallas_call(functools.partial(forward_kernel, len(pieces), low, count,...  31.7 us
    pallas_call x3, Pallas kernels, backward_chunk(): pl.pallas_call(functools.partial(backward_kernel, count, first), grid=(co...  25.8 us
    pallas_call x3, Pallas kernels, grad_b_of(): pl.pallas_call(grad_b_kernel, grid=(last - first,), in_specs=specs, out_s...  12.7 us
    pallas_call x1, Pallas kernels, middle(): pl.pallas_call(functools.partial(middle_kernel, rows), grid_spec=pltpu.Pr...  7.47 us
    ppermute x6, starting transfers between devices, exchange_sum(): x = x + lax.ppermute(x, 'tensor', pairs)  7.37 us
    pallas_call x1, Pallas kernels, grad_a_of(): pl.pallas_call(functools.partial(grad_a_kernel, per), grid=(adapters // p...  5.31 us
  transfers between devices with their start and end apart: 38, of which 15 were waited for; matrix products, arithmetic and copies ran while one was open for 4% of the time, Pallas kernels for 44%

profile of v6, /device:TPU:0, one launch (start us, length us, event | category | flops | bytes accessed | tf_op | source)
XLA Modules:
  0.0 175.5 jit_solution(2924681175330423316)
XLA Ops:
  1.5 5.1 %collective-permute-start = (bf16[16,3072]{1,0:T(8,128)(2,1)S(1)}, bf16[16,3072]{1,0:T(8,128)(2,1)S(1)}, u32[]{:S(2)}, u32[]{:S(2)}) collective-permute-start(bf16[16,3072]{1,0:T(8,128)(2,1)S(1)} %get-tuple-element.90), channel_id=1, source_target_pairs={{0,12},{1,13},{2,14},{3,15},{4,0},{5,1},{6,2},{7,3},{8,4},{9,5},{1... | collective-permute-start | bytes 294920 | tf_op jit(solution)/shard_map/ppermute | solution.py:65
  6.6 1.0 collective-permute-start.2
  9.8 5.5 %collective-permute-done.1 = bf16[16,3072]{1,0:T(8,128)(2,1)S(1)} collective-permute-done((bf16[16,3072]{1,0:T(8,128)(2,1)S(1)}, bf16[16,3072]{1,0:T(8,128)(2,1)S(1)}, u32[]{:S(2)}, u32[]{:S(2)}) %collective-permute-start.1) | collective-permute-done | bytes 98336 | tf_op jit(solution)/shard_map/ppermute | solution.py:65
  15.4 2.3 %collective-permute-start.4 = (bf16[16,5120]{1,0:T(8,128)(2,1)S(1)}, bf16[16,5120]{1,0:T(8,128)(2,1)S(1)}, u32[]{:S(2)}, u32[]{:S(2)}) collective-permute-start(bf16[16,5120]{1,0:T(8,128)(2,1)S(1)} %slice.70), channel_id=1, source_target_pairs={{0,8},{1,9},{2,10},{3,11},{4,12},{5,13},{6,14},{7,15},{8,0},{9,1},... | collective-permute-start | bytes 491528 | tf_op jit(solution)/shard_map/ppermute | solution.py:65
  18.0 3.6 %collective-permute-start.3 = (bf16[16,5120]{1,0:T(8,128)(2,1)S(1)}, bf16[16,5120]{1,0:T(8,128)(2,1)S(1)}, u32[]{:S(2)}, u32[]{:S(2)}) collective-permute-start(bf16[16,5120]{1,0:T(8,128)(2,1)S(1)} %slice.70), channel_id=1, source_target_pairs={{0,12},{1,13},{2,14},{3,15},{4,0},{5,1},{6,2},{7,3},{8,4},{9,5},{1... | collective-permute-start | bytes 491528 | tf_op jit(solution)/shard_map/ppermute | solution.py:65
  22.7 1.5 collective-permute-start.7
  24.2 4.5 %collective-permute-done.4 = bf16[16,5120]{1,0:T(8,128)(2,1)S(1)} collective-permute-done((bf16[16,5120]{1,0:T(8,128)(2,1)S(1)}, bf16[16,5120]{1,0:T(8,128)(2,1)S(1)}, u32[]{:S(2)}, u32[]{:S(2)}) %collective-permute-start.4) | collective-permute-done | bytes 163872 | tf_op jit(solution)/shard_map/ppermute | solution.py:65
  28.7 1.4 collective-permute-done.3
  30.2 1.9 %collective-permute-done.7.rest_1_.rest_9_ = bf16[64,3072]{1,0:T(8,128)(2,1)S(1)} collective-permute-done((bf16[64,3072]{1,0:T(8,128)(2,1)S(1)}, bf16[64,3072]{1,0:T(8,128)(2,1)S(1)}, u32[]{:S(2)}, u32[]{:S(2)}) %collective-permute-start.7) | collective-permute-done | bytes 393248 | tf_op jit(solution)/shard_map/ppermute | solution.py:65
  33.0 1.5 collective-permute-start.6
  35.9 9.8 %shard_map.103.rest_5_ = f32[2,256,1792]{2,1,0:T(8,128)S(1)} custom-call(bf16[64,3072]{1,0:T(8,128)(2,1)S(1)} %bitcast.40, bf16[64,3072]{1,0:T(8,128)(2,1)S(1)} %collective-permute-done.7.rest_1_.rest_9_, bf16[64,3072]{1,0:T(8,128)(2,1)S(1)} %collective-permute-done.8.rest_2_.rest_10_, bf16[64,3072]{1,0:T(8,128)(2,1)S(1)} %collective-permute-done.9.rest_3_.rest_11_, ...), custom_call_target="tpu_custom_call" | custom-call | flops 5637144576 | bytes 22020096 | tf_op jit(solution)/shard_map/pallas_call | solution.py:165
  45.7 4.4 %collective-permute-done.6.rest_1_.rest_13_ = bf16[64,5120]{1,0:T(8,128)(2,1)S(1)} collective-permute-done((bf16[64,5120]{1,0:T(8,128)(2,1)S(1)}, bf16[64,5120]{1,0:T(8,128)(2,1)S(1)}, u32[]{:S(2)}, u32[]{:S(2)}) %collective-permute-start.6) | collective-permute-done | bytes 655392 | tf_op jit(solution)/shard_map/ppermute | solution.py:65
  50.4 1.9 %collective-permute-done.11.rest_3_.rest_15_ = bf16[64,5120]{1,0:T(8,128)(2,1)S(1)} collective-permute-done((bf16[64,5120]{1,0:T(8,128)(2,1)S(1)}, bf16[64,5120]{1,0:T(8,128)(2,1)S(1)}, u32[]{:S(2)}, u32[]{:S(2)}) %collective-permute-start.11) | collective-permute-done | bytes 655392 | tf_op jit(solution)/shard_map/ppermute | solution.py:65
  52.3 1.3 shard_map.108
  53.8 1.1 collective-permute-done.12
  54.9 1.6 collective-permute-start.13
  56.5 4.1 %shard_map.104.rest_5_ = f32[2,256,1792]{2,1,0:T(8,128)S(1)} custom-call(bf16[64,5120]{1,0:T(8,128)(2,1)S(1)} %bitcast.32, bf16[64,5120]{1,0:T(8,128)(2,1)S(1)} %collective-permute-done.6.rest_1_.rest_13_, bf16[64,5120]{1,0:T(8,128)(2,1)S(1)} %collective-permute-done.10.rest_2_.rest_14_, ...), custom_call_target="tpu_custom_call", output_to_operand_aliasing={{}: (5, {})} | custom-call | flops 1342177280 | bytes 5242880 | tf_op jit(solution)/shard_map/pallas_call | solution.py:165
  61.5 5.8 %shard_map.105.rest_5_ = f32[2,256,1792]{2,1,0:T(8,128)S(1)} custom-call(bf16[64,5120]{1,0:T(8,128)(2,1)S(1)} %bitcast.33, bf16[64,5120]{1,0:T(8,128)(2,1)S(1)} %collective-permute-done.6.rest_1_.rest_13_, bf16[64,5120]{1,0:T(8,128)(2,1)S(1)} %collective-permute-done.10.rest_2_.rest_14_, ...), custom_call_target="tpu_custom_call", output_to_operand_aliasing={{}: (5, {})} | custom-call | flops 2684354560 | bytes 10485760 | tf_op jit(solution)/shard_map/pallas_call | solution.py:165
  67.6 5.8 %shard_map.106.rest_5_ = f32[2,256,1792]{2,1,0:T(8,128)S(1)} custom-call(bf16[64,5120]{1,0:T(8,128)(2,1)S(1)} %bitcast.34, bf16[64,5120]{1,0:T(8,128)(2,1)S(1)} %collective-permute-done.6.rest_1_.rest_13_, bf16[64,5120]{1,0:T(8,128)(2,1)S(1)} %collective-permute-done.10.rest_2_.rest_14_, ...), custom_call_target="tpu_custom_call", output_to_operand_aliasing={{}: (5, {})} | custom-call | flops 2684354560 | bytes 10485760 | tf_op jit(solution)/shard_map/pallas_call | solution.py:165
  73.6 6.0 %shard_map.107.base = f32[2,256,1792]{2,1,0:T(8,128)S(1)} custom-call(bf16[64,5120]{1,0:T(8,128)(2,1)S(1)} %bitcast.35, bf16[64,5120]{1,0:T(8,128)(2,1)S(1)} %collective-permute-done.6.rest_1_.rest_13_, bf16[64,5120]{1,0:T(8,128)(2,1)S(1)} %collective-permute-done.10.rest_2_.rest_14_, ...), custom_call_target="tpu_custom_call", output_to_operand_aliasing={{}: (5, {})} | custom-call | flops 2684354560 | bytes 10485760 | tf_op jit(solution)/shard_map/pallas_call | solution.py:165
  81.0 7.5 %shard_map.109 = (bf16[256,1792]{1,0:T(8,128)(2,1)S(1)}, bf16[256,1792]{1,0:T(8,128)(2,1)S(1)}, f32[256,128]{1,0:T(8,128)S(1)}) custom-call(s32[8]{0:T(128)S(1)} %bitcast.54, s32[16]{0:T(128)S(1)} %get-tuple-element.78.places, f32[2,256,1792]{2,1,0:T(8,128)S(1)} %shard_map.107.base, bf16[256,1792]{1,0:T(8,128)(2,1)S(1)} %copy-done.1, ...), custom_call_target="tpu_custom_call" | custom-call | flops 1879048192 | bytes 10092544 | tf_op jit(solution)/shard_map/pallas_call | solution.py:313
  88.6 1.2 collective-permute-done.18
  90.4 3.8 %shard_map.111.rest_0_ = f32[24,128,1792]{2,1,0:T(8,128)} custom-call(bf16[256,1792]{1,0:T(8,128)(2,1)S(1)} %get-tuple-element.61.dgate, bf16[256,1792]{1,0:T(8,128)(2,1)S(1)} %get-tuple-element.45.dup, bf16[256,256]{1,0:T(8,128)(2,1)S(1)} %fusion.1.order, bf16[256,128]{1,0:T(8,128)(2,1)S(1)} %bitcast.43, s32[1,256]{1,0:T(1,128)S(1)} %bitcast.48), custom_call_target="tpu_custom_call" | custom-call | flops 805306368 | bytes 6291456 | tf_op jit(solution)/shard_map/pallas_call | solution.py:372
  94.2 1.9 %collective-permute-start.20 = (f32[128,128]{1,0:T(8,128)S(1)}, f32[128,128]{1,0:T(8,128)S(1)}, u32[]{:S(2)}, u32[]{:S(2)}) collective-permute-start(f32[128,128]{1,0:T(8,128)S(1)} %add.310), channel_id=1, source_target_pairs={{0,4},{1,5},{2,6},{3,7},{4,0},{5,1},{6,2},{7,3},{8,12},{9,13},{10,... | collective-permute-start | bytes 196616 | tf_op jit(solution)/shard_map/ppermute | solution.py:91
  96.1 3.8 %shard_map.112.rest_0_ = f32[24,128,1792]{2,1,0:T(8,128)} custom-call(bf16[256,1792]{1,0:T(8,128)(2,1)S(1)} %get-tuple-element.61.dgate, bf16[256,1792]{1,0:T(8,128)(2,1)S(1)} %get-tuple-element.45.dup, bf16[256,256]{1,0:T(8,128)(2,1)S(1)} %fusion.1.order, bf16[256,128]{1,0:T(8,128)(2,1)S(1)} %bitcast.44, ...), custom_call_target="tpu_custom_call", output_to_operand_aliasing={{}: (5, {})} | custom-call | flops 805306368 | bytes 6291456 | tf_op jit(solution)/shard_map/pallas_call | solution.py:372
  99.9 2.4 %collective-permute-start.21 = (f32[128,128]{1,0:T(8,128)S(1)}, f32[128,128]{1,0:T(8,128)S(1)}, u32[]{:S(2)}, u32[]{:S(2)}) collective-permute-start(f32[128,128]{1,0:T(8,128)S(1)} %add.311), channel_id=1, source_target_pairs={{0,8},{1,9},{2,10},{3,11},{4,12},{5,13},{6,14},{7,15},{8,0},{9,1},... | collective-permute-start | bytes 196616 | tf_op jit(solution)/shard_map/ppermute | solution.py:91
  102.3 9.2 %shard_map.110 = (bf16[128,3072]{1,0:T(8,128)(2,1)S(1)}, bf16[128,3072]{1,0:T(8,128)(2,1)S(1)}) custom-call(bf16[2,8192,1792]{2,1,0:T(8,128)(2,1)} %frozen.5, bf16[256,1792]{1,0:T(8,128)(2,1)S(1)} %get-tuple-element.61.dgate, bf16[256,1792]{1,0:T(8,128)(2,1)S(1)} %get-tuple-element.45.dup), custom_call_target="tpu_custom_call" | custom-call | flops 5637144576 | bytes 22020096 | tf_op jit(solution)/shard_map/pallas_call | solution.py:469
  112.3 1.5 collective-permute-done.22
  113.9 1.4 shard_map.113
  115.5 1.3 collective-permute-done.23.side_far
  116.9 1.2 shard_map.114
  118.8 1.5 collective-permute-start.24
  120.4 9.8 %shard_map.115 = (bf16[128,3072]{1,0:T(8,128)(2,1)S(1)}, bf16[128,3072]{1,0:T(8,128)(2,1)}) custom-call(bf16[2,8192,1792]{2,1,0:T(8,128)(2,1)} %frozen.5, bf16[256,1792]{1,0:T(8,128)(2,1)S(1)} %get-tuple-element.61.dgate, bf16[256,1792]{1,0:T(8,128)(2,1)S(1)} %get-tuple-element.45.dup), custom_call_target="tpu_custom_call" | custom-call | flops 5637144576 | bytes 22020096 | tf_op jit(solution)/shard_map/pallas_call | solution.py:469
  130.4 1.2 add_convert_fusion.1
  131.6 1.3 collective-permute-done.26.far
  132.9 2.8 %shard_map.116 = (bf16[64,3072]{1,0:T(8,128)(2,1)S(1)}, bf16[64,3072]{1,0:T(8,128)(2,1)S(1)}) custom-call(s32[2]{0:T(128)S(1)} %pad_add_fusion.at, bf16[128,3072]{1,0:T(8,128)(2,1)S(1)} %get-tuple-element.57.near, bf16[128,3072]{1,0:T(8,128)(2,1)} %collective-permute-done.26.far, f32[128,512]{1,0:T(8,128)S(1)} %get-tuple-element.52.side, ...), custom_call_target="tpu_custom_call" | custom-call | flops 786432 | bytes 2359296 | tf_op jit(solution)/shard_map/pallas_call | solution.py:511
  135.7 1.4 collective-permute-start.27
  138.3 2.8 %collective-permute-start.29 = (bf16[16,3072]{1,0:T(8,128)(2,1)S(1)}, bf16[16,3072]{1,0:T(8,128)(2,1)S(1)}, u32[]{:S(2)}, u32[]{:S(2)}) collective-permute-start(bf16[16,3072]{1,0:T(8,128)(2,1)S(1)} %get-tuple-element.83), channel_id=1, source_target_pairs={{0,12},{1,13},{2,14},{3,15},{4,0},{5,1},{6,2},{7,3},{8,4},{9,5},{1... | collective-permute-start | bytes 294920 | tf_op jit(solution)/shard_map/ppermute | solution.py:65
  141.0 6.9 %shard_map.117 = (bf16[128,2048]{1,0:T(8,128)(2,1)S(1)}, bf16[128,2048]{1,0:T(8,128)(2,1)S(1)}) custom-call(bf16[2,8192,1792]{2,1,0:T(8,128)(2,1)} %frozen.5, bf16[256,1792]{1,0:T(8,128)(2,1)S(1)} %get-tuple-element.61.dgate, bf16[256,1792]{1,0:T(8,128)(2,1)S(1)} %get-tuple-element.45.dup), custom_call_target="tpu_custom_call" | custom-call | flops 3758096384 | bytes 14680064 | tf_op jit(solution)/shard_map/pallas_call | solution.py:469
  148.1 1.8 %collective-permute-done.30.far = bf16[128,2048]{1,0:T(8,128)(2,1)S(1)} collective-permute-done((bf16[128,2048]{1,0:T(8,128)(2,1)S(1)}, bf16[128,2048]{1,0:T(8,128)(2,1)S(1)}, u32[]{:S(2)}, u32[]{:S(2)}) %collective-permute-start.30) | collective-permute-done | bytes 524320 | tf_op jit(solution)/shard_map/ppermute | solution.py:65
  151.6 2.0 %collective-permute-start.32 = (bf16[16,3072]{1,0:T(8,128)(2,1)S(1)}, bf16[16,3072]{1,0:T(8,128)(2,1)S(1)}, u32[]{:S(2)}, u32[]{:S(2)}) collective-permute-start(bf16[16,3072]{1,0:T(8,128)(2,1)S(1)} %get-tuple-element.80), channel_id=1, source_target_pairs={{0,4},{1,5},{2,6},{3,7},{4,8},{5,9},{6,10},{7,11},{8,12},{9,13},{1... | collective-permute-start | bytes 294920 | tf_op jit(solution)/shard_map/ppermute | solution.py:65
  154.2 2.4 %collective-permute-start.34 = (bf16[16,3072]{1,0:T(8,128)(2,1)S(1)}, bf16[16,3072]{1,0:T(8,128)(2,1)S(1)}, u32[]{:S(2)}, u32[]{:S(2)}) collective-permute-start(bf16[16,3072]{1,0:T(8,128)(2,1)S(1)} %get-tuple-element.81), channel_id=1, source_target_pairs={{0,12},{1,13},{2,14},{3,15},{4,0},{5,1},{6,2},{7,3},{8,4},{9,5},{1... | collective-permute-start | bytes 294920 | tf_op jit(solution)/shard_map/ppermute | solution.py:65
  156.6 5.3 %shard_map.119 = f32[24,512,128]{2,1,0:T(8,128)} custom-call(bf16[256,512]{1,0:T(8,128)(2,1)S(1)} %copy-done.4, bf16[256,256]{1,0:T(8,128)(2,1)S(1)} %fusion.1.order, bf16[256,128]{1,0:T(8,128)(2,1)S(1)} %bitcast.47, s32[256,1]{1,0:T(8,128)S(1)} %copy.24.adapter), custom_call_target="tpu_custom_call" | custom-call | flops 805306368 | bytes 6291456 | tf_op jit(solution)/shard_map/pallas_call | solution.py:402
  161.9 5.0 %shard_map.120 = f32[24,128,1792]{2,1,0:T(8,128)} custom-call(bf16[256,1792]{1,0:T(8,128)(2,1)S(1)} %get-tuple-element.61.dgate, bf16[256,1792]{1,0:T(8,128)(2,1)S(1)} %get-tuple-element.45.dup, bf16[256,256]{1,0:T(8,128)(2,1)S(1)} %fusion.1.order, bf16[256,128]{1,0:T(8,128)(2,1)S(1)} %bitcast.45, ...), custom_call_target="tpu_custom_call", output_to_operand_aliasing={{}: (5, {})} | custom-call | flops 1207959552 | bytes 9437184 | tf_op jit(solution)/shard_map/pallas_call | solution.py:372
  167.2 2.0 %collective-permute-start.36 = (bf16[16,2048]{1,0:T(8,128)(2,1)S(1)}, bf16[16,2048]{1,0:T(8,128)(2,1)S(1)}, u32[]{:S(2)}, u32[]{:S(2)}) collective-permute-start(bf16[16,2048]{1,0:T(8,128)(2,1)S(1)} %get-tuple-element.88), channel_id=1, source_target_pairs={{0,8},{1,9},{2,10},{3,11},{4,12},{5,13},{6,14},{7,15},{8,0},{9,1},... | collective-permute-start | bytes 196616 | tf_op jit(solution)/shard_map/ppermute | solution.py:65
  169.1 1.8 %collective-permute-start.37 = (bf16[16,2048]{1,0:T(8,128)(2,1)S(1)}, bf16[16,2048]{1,0:T(8,128)(2,1)S(1)}, u32[]{:S(2)}, u32[]{:S(2)}) collective-permute-start(bf16[16,2048]{1,0:T(8,128)(2,1)S(1)} %get-tuple-element.87), channel_id=1, source_target_pairs={{0,12},{1,13},{2,14},{3,15},{4,0},{5,1},{6,2},{7,3},{8,4},{9,5},{1... | collective-permute-start | bytes 196616 | tf_op jit(solution)/shard_map/ppermute | solution.py:65
  171.1 2.4 %collective-permute-done.35 = bf16[16,2048]{1,0:T(8,128)(2,1)S(1)} collective-permute-done((bf16[16,2048]{1,0:T(8,128)(2,1)S(1)}, bf16[16,2048]{1,0:T(8,128)(2,1)S(1)}, u32[]{:S(2)}, u32[]{:S(2)}) %collective-permute-start.35) | collective-permute-done | bytes 65568 | tf_op jit(solution)/shard_map/ppermute | solution.py:65
  173.5 1.2 collective-permute-done.36
  (124 shorter events, 17.1 us)
Async XLA Ops:
  1.5 8.3 %collective-permute-start = (bf16[16,3072]{1,0:T(8,128)(2,1)S(1)}, bf16[16,3072]{1,0:T(8,128)(2,1)S(1)}, u32[]{:S(2)}, u32[]{:S(2)}) collective-permute-start(bf16[16,3072]{1,0:T(8,128)(2,1)S(1)} %get-tuple-element.90), channel_id=1, source_target_pairs={{0,12},{1,13},{2,14},{3,15},{4,0},{5,1},{6,2},{7,3},{8,4},{9,5},{1... | collective-permute-start | bytes 294920 | tf_op jit(solution)/shard_map/ppermute | solution.py:65
  6.6 8.7 %collective-permute-start.1 = (bf16[16,3072]{1,0:T(8,128)(2,1)S(1)}, bf16[16,3072]{1,0:T(8,128)(2,1)S(1)}, u32[]{:S(2)}, u32[]{:S(2)}) collective-permute-start(bf16[16,3072]{1,0:T(8,128)(2,1)S(1)} %get-tuple-element.90), channel_id=1, source_target_pairs={{0,8},{1,9},{2,10},{3,11},{4,12},{5,13},{6,14},{7,15},{8,0},{9,1},... | collective-permute-start | bytes 294920 | tf_op jit(solution)/shard_map/ppermute | solution.py:65
  6.6 8.7 %collective-permute-start.2 = (bf16[16,3072]{1,0:T(8,128)(2,1)S(1)}, bf16[16,3072]{1,0:T(8,128)(2,1)S(1)}, u32[]{:S(2)}, u32[]{:S(2)}) collective-permute-start(bf16[16,3072]{1,0:T(8,128)(2,1)S(1)} %get-tuple-element.90), channel_id=1, source_target_pairs={{0,4},{1,5},{2,6},{3,7},{4,8},{5,9},{6,10},{7,11},{8,12},{9,13},{1... | collective-permute-start | bytes 294920 | tf_op jit(solution)/shard_map/ppermute | solution.py:65
  15.4 13.3 %collective-permute-start.4 = (bf16[16,5120]{1,0:T(8,128)(2,1)S(1)}, bf16[16,5120]{1,0:T(8,128)(2,1)S(1)}, u32[]{:S(2)}, u32[]{:S(2)}) collective-permute-start(bf16[16,5120]{1,0:T(8,128)(2,1)S(1)} %slice.70), channel_id=1, source_target_pairs={{0,8},{1,9},{2,10},{3,11},{4,12},{5,13},{6,14},{7,15},{8,0},{9,1},... | collective-permute-start | bytes 491528 | tf_op jit(solution)/shard_map/ppermute | solution.py:65
  17.8 10.9 %collective-permute-start.5 = (bf16[16,5120]{1,0:T(8,128)(2,1)S(1)}, bf16[16,5120]{1,0:T(8,128)(2,1)S(1)}, u32[]{:S(2)}, u32[]{:S(2)}) collective-permute-start(bf16[16,5120]{1,0:T(8,128)(2,1)S(1)} %slice.70), channel_id=1, source_target_pairs={{0,4},{1,5},{2,6},{3,7},{4,8},{5,9},{6,10},{7,11},{8,12},{9,13},{1... | collective-permute-start | bytes 491528 | tf_op jit(solution)/shard_map/ppermute | solution.py:65
  18.0 12.1 %collective-permute-start.3 = (bf16[16,5120]{1,0:T(8,128)(2,1)S(1)}, bf16[16,5120]{1,0:T(8,128)(2,1)S(1)}, u32[]{:S(2)}, u32[]{:S(2)}) collective-permute-start(bf16[16,5120]{1,0:T(8,128)(2,1)S(1)} %slice.70), channel_id=1, source_target_pairs={{0,12},{1,13},{2,14},{3,15},{4,0},{5,1},{6,2},{7,3},{8,4},{9,5},{1... | collective-permute-start | bytes 491528 | tf_op jit(solution)/shard_map/ppermute | solution.py:65
  22.7 9.4 %collective-permute-start.7 = (bf16[64,3072]{1,0:T(8,128)(2,1)S(1)}, bf16[64,3072]{1,0:T(8,128)(2,1)S(1)}, u32[]{:S(2)}, u32[]{:S(2)}) collective-permute-start(bf16[64,3072]{1,0:T(8,128)(2,1)S(1)} %bitcast.38), channel_id=1, source_target_pairs={{0,2},{1,3},{2,0},{3,1},{4,6},{5,7},{6,4},{7,5},{8,10},{9,11},{10,... | collective-permute-start | bytes 1179656 | tf_op jit(solution)/shard_map/ppermute | solution.py:65
  24.2 11.7 %collective-permute-start.8 = (bf16[64,3072]{1,0:T(8,128)(2,1)S(1)}, bf16[64,3072]{1,0:T(8,128)(2,1)S(1)}, u32[]{:S(2)}, u32[]{:S(2)}) collective-permute-start(bf16[64,3072]{1,0:T(8,128)(2,1)S(1)} %bitcast.39), channel_id=1, source_target_pairs={{0,1},{1,0},{2,3},{3,2},{4,5},{5,4},{6,7},{7,6},{8,9},{9,8},{10,11... | collective-permute-start | bytes 1179656 | tf_op jit(solution)/shard_map/ppermute | solution.py:65
  32.1 3.8 %collective-permute-start.9 = (bf16[64,3072]{1,0:T(8,128)(2,1)S(1)}, bf16[64,3072]{1,0:T(8,128)(2,1)S(1)}, u32[]{:S(2)}, u32[]{:S(2)}) collective-permute-start(bf16[64,3072]{1,0:T(8,128)(2,1)S(1)} %collective-permute-done.7.rest_1_.rest_9_), channel_id=1, source_target_pairs={{0,1},{1,0},{2,3},{3,2},{4,5},{5,4},{6,7},{7,6},{8,9},{9,8},{10,11... | collective-permute-start | bytes 1179656 | tf_op jit(solution)/shard_map/ppermute | solution.py:65
  33.0 17.1 %collective-permute-start.6 = (bf16[64,5120]{1,0:T(8,128)(2,1)S(1)}, bf16[64,5120]{1,0:T(8,128)(2,1)S(1)}, u32[]{:S(2)}, u32[]{:S(2)}) collective-permute-start(bf16[64,5120]{1,0:T(8,128)(2,1)S(1)} %bitcast.29), channel_id=1, source_target_pairs={{0,2},{1,3},{2,0},{3,1},{4,6},{5,7},{6,4},{7,5},{8,10},{9,11},{10,... | collective-permute-start | bytes 1966088 | tf_op jit(solution)/shard_map/ppermute | solution.py:65
  35.6 16.7 %copy-start = (bf16[24,512,128]{2,1,0:T(8,128)(2,1)S(1)}, bf16[24,512,128]{2,1,0:T(8,128)(2,1)}, u32[]{:S(2)}) copy-start(bf16[24,512,128]{2,1,0:T(8,128)(2,1)} %rest_7_.3) | copy-start | bytes 9437188
  35.6 16.7 %copy-start.5 = (s32[1,8]{1,0:T(1,128)S(1)}, s32[1,8]{1,0:T(1,128)}, u32[]{:S(2)}) copy-start(s32[1,8]{1,0:T(1,128)} %param.13) | copy-start | bytes 100
  35.6 14.8 %collective-permute-start.10 = (bf16[64,5120]{1,0:T(8,128)(2,1)S(1)}, bf16[64,5120]{1,0:T(8,128)(2,1)S(1)}, u32[]{:S(2)}, u32[]{:S(2)}) collective-permute-start(bf16[64,5120]{1,0:T(8,128)(2,1)S(1)} %bitcast.30), channel_id=1, source_target_pairs={{0,1},{1,0},{2,3},{3,2},{4,5},{5,4},{6,7},{7,6},{8,9},{9,8},{10,11... | collective-permute-start | bytes 1966088 | tf_op jit(solution)/shard_map/ppermute | solution.py:65
  50.2 2.1 %collective-permute-start.11 = (bf16[64,5120]{1,0:T(8,128)(2,1)S(1)}, bf16[64,5120]{1,0:T(8,128)(2,1)S(1)}, u32[]{:S(2)}, u32[]{:S(2)}) collective-permute-start(bf16[64,5120]{1,0:T(8,128)(2,1)S(1)} %collective-permute-done.6.rest_1_.rest_13_), channel_id=1, source_target_pairs={{0,1},{1,0},{2,3},{3,2},{4,5},{5,4},{6,7},{7,6},{8,9},{9,8},{10,11... | collective-permute-start | bytes 1966088 | tf_op jit(solution)/shard_map/ppermute | solution.py:65
  53.6 1.4 copy-start.3
  53.6 1.3 collective-permute-start.12
  54.9 5.7 %collective-permute-start.13 = (f32[128,128]{1,0:T(8,128)S(1)}, f32[128,128]{1,0:T(8,128)S(1)}, u32[]{:S(2)}, u32[]{:S(2)}) collective-permute-start(f32[128,128]{1,0:T(8,128)S(1)} %slice_add_fusion.1), channel_id=1, source_target_pairs={{0,2},{1,3},{2,0},{3,1},{4,6},{5,7},{6,4},{7,5},{8,10},{9,11},{10,... | collective-permute-start | bytes 196616 | tf_op jit(solution)/shard_map/ppermute | solution.py:91
  60.7 6.7 %collective-permute-start.14 = (f32[128,128]{1,0:T(8,128)S(1)}, f32[128,128]{1,0:T(8,128)S(1)}, u32[]{:S(2)}, u32[]{:S(2)}) collective-permute-start(f32[128,128]{1,0:T(8,128)S(1)} %add.299), channel_id=1, source_target_pairs={{0,4},{1,5},{2,6},{3,7},{4,0},{5,1},{6,2},{7,3},{8,12},{9,13},{10,... | collective-permute-start | bytes 196616 | tf_op jit(solution)/shard_map/ppermute | solution.py:91
  67.4 6.0 %collective-permute-start.15 = (f32[128,128]{1,0:T(8,128)S(1)}, f32[128,128]{1,0:T(8,128)S(1)}, u32[]{:S(2)}, u32[]{:S(2)}) collective-permute-start(f32[128,128]{1,0:T(8,128)S(1)} %add.300), channel_id=1, source_target_pairs={{0,8},{1,9},{2,10},{3,11},{4,12},{5,13},{6,14},{7,15},{8,0},{9,1},... | collective-permute-start | bytes 196616 | tf_op jit(solution)/shard_map/ppermute | solution.py:91
  73.4 6.3 %slice-start = ((s8[11010048]{0:T(1024)(128)(4,1)}), s8[4194304]{0:T(1024)(128)(4,1)S(1)}, s32[]{:S(2)}) async-start(s8[11010048]{0:T(1024)(128)(4,1)} %bitcast.36), calls=%async_computation | async-start | bytes 8388608
  73.5 6.5 %slice-start.1 = ((s8[11010048]{0:T(1024)(128)(4,1)}), s8[4194304]{0:T(1024)(128)(4,1)S(1)}, s32[]{:S(2)}) async-start(s8[11010048]{0:T(1024)(128)(4,1)} %bitcast.36), calls=%async_computation.1 | async-start | bytes 8388608
  73.5 7.2 %slice-start.2 = ((s8[11010048]{0:T(1024)(128)(4,1)}), s8[2621440]{0:T(1024)(128)(4,1)S(1)}, s32[]{:S(2)}) async-start(s8[11010048]{0:T(1024)(128)(4,1)} %bitcast.36), calls=%async_computation.2 | async-start | bytes 5242880
  73.6 7.4 %copy-start.1 = (bf16[256,1792]{1,0:T(8,128)(2,1)S(1)}, bf16[256,1792]{1,0:T(8,128)(2,1)}, u32[]{:S(2)}) copy-start(bf16[256,1792]{1,0:T(8,128)(2,1)} %dhidden.1) | copy-start | bytes 2752516
  73.6 6.1 %collective-permute-start.16 = (bf16[128,128]{1,0:T(8,128)(2,1)S(1)}, bf16[128,128]{1,0:T(8,128)(2,1)S(1)}, u32[]{:S(2)}, u32[]{:S(2)}) collective-permute-start(bf16[128,128]{1,0:T(8,128)(2,1)S(1)} %fusion.2), channel_id=1, source_target_pairs={{0,1},{1,0},{2,3},{3,2},{4,5},{5,4},{6,7},{7,6},{8,9},{9,8},{10,11... | collective-permute-start | bytes 98312 | tf_op jit(solution)/shard_map/ppermute | solution.py:65
  88.4 1.3 collective-permute-start.18
  89.8 4.4 %collective-permute-start.19 = (f32[128,128]{1,0:T(8,128)S(1)}, f32[128,128]{1,0:T(8,128)S(1)}, u32[]{:S(2)}, u32[]{:S(2)}) collective-permute-start(f32[128,128]{1,0:T(8,128)S(1)} %slice_add_fusion), channel_id=1, source_target_pairs={{0,2},{1,3},{2,0},{3,1},{4,6},{5,7},{6,4},{7,5},{8,10},{9,11},{10,... | collective-permute-start | bytes 196616 | tf_op jit(solution)/shard_map/ppermute | solution.py:91
  94.2 5.7 %collective-permute-start.20 = (f32[128,128]{1,0:T(8,128)S(1)}, f32[128,128]{1,0:T(8,128)S(1)}, u32[]{:S(2)}, u32[]{:S(2)}) collective-permute-start(f32[128,128]{1,0:T(8,128)S(1)} %add.310), channel_id=1, source_target_pairs={{0,4},{1,5},{2,6},{3,7},{4,0},{5,1},{6,2},{7,3},{8,12},{9,13},{10,... | collective-permute-start | bytes 196616 | tf_op jit(solution)/shard_map/ppermute | solution.py:91
  99.9 11.6 %collective-permute-start.21 = (f32[128,128]{1,0:T(8,128)S(1)}, f32[128,128]{1,0:T(8,128)S(1)}, u32[]{:S(2)}, u32[]{:S(2)}) collective-permute-start(f32[128,128]{1,0:T(8,128)S(1)} %add.311), channel_id=1, source_target_pairs={{0,8},{1,9},{2,10},{3,11},{4,12},{5,13},{6,14},{7,15},{8,0},{9,1},... | collective-permute-start | bytes 196616 | tf_op jit(solution)/shard_map/ppermute | solution.py:91
  111.5 5.4 %collective-permute-start.17 = (bf16[128,3072]{1,0:T(8,128)(2,1)S(1)}, bf16[128,3072]{1,0:T(8,128)(2,1)S(1)}, u32[]{:S(2)}, u32[]{:S(2)}) collective-permute-start(bf16[128,3072]{1,0:T(8,128)(2,1)S(1)} %get-tuple-element.47), channel_id=1, source_target_pairs={{0,1},{1,0},{2,3},{3,2},{4,5},{5,4},{6,7},{7,6},{8,9},{9,8},{10,11... | collective-permute-start | bytes 2359304 | tf_op jit(solution)/shard_map/ppermute | solution.py:65
  111.7 2.2 %collective-permute-start.22 = (bf16[128,128]{1,0:T(8,128)(2,1)S(1)}, bf16[128,128]{1,0:T(8,128)(2,1)S(1)}, u32[]{:S(2)}, u32[]{:S(2)}) collective-permute-start(bf16[128,128]{1,0:T(8,128)(2,1)S(1)} %fusion.3), channel_id=1, source_target_pairs={{0,1},{1,0},{2,3},{3,2},{4,5},{5,4},{6,7},{7,6},{8,9},{9,8},{10,11... | collective-permute-start | bytes 98312 | tf_op jit(solution)/shard_map/ppermute | solution.py:65
  115.2 1.6 collective-permute-start.23
  118.1 0.8 copy-start.2
  118.8 11.3 %collective-permute-start.24 = (bf16[64,3072]{1,0:T(8,128)(2,1)S(1)}, bf16[64,3072]{1,0:T(8,128)(2,1)}, u32[]{:S(2)}, u32[]{:S(2)}) collective-permute-start(bf16[64,3072]{1,0:T(8,128)(2,1)S(1)} %get-tuple-element.55), channel_id=1, source_target_pairs={{0,2},{1,3},{2,0},{3,1},{4,6},{5,7},{6,4},{7,5},{8,10},{9,11},{10,... | collective-permute-start | bytes 1179656 | tf_op jit(solution)/shard_map/ppermute | solution.py:65
  130.2 2.7 %collective-permute-start.26 = (bf16[128,3072]{1,0:T(8,128)(2,1)}, bf16[128,3072]{1,0:T(8,128)(2,1)}, u32[]{:S(2)}, u32[]{:S(2)}) collective-permute-start(bf16[128,3072]{1,0:T(8,128)(2,1)} %get-tuple-element.59), channel_id=1, source_target_pairs={{0,1},{1,0},{2,3},{3,2},{4,5},{5,4},{6,7},{7,6},{8,9},{9,8},{10,11... | collective-permute-start | bytes 2359304 | tf_op jit(solution)/shard_map/ppermute | solution.py:65
  135.7 12.2 %collective-permute-start.27 = (bf16[64,3072]{1,0:T(8,128)(2,1)S(1)}, bf16[64,3072]{1,0:T(8,128)(2,1)S(1)}, u32[]{:S(2)}, u32[]{:S(2)}) collective-permute-start(bf16[64,3072]{1,0:T(8,128)(2,1)S(1)} %get-tuple-element.64), channel_id=1, source_target_pairs={{0,2},{1,3},{2,0},{3,1},{4,6},{5,7},{6,4},{7,5},{8,10},{9,11},{10,... | collective-permute-start | bytes 1179656 | tf_op jit(solution)/shard_map/ppermute | solution.py:65
  137.1 10.7 %collective-permute-start.25 = (bf16[16,3072]{1,0:T(8,128)(2,1)S(1)}, bf16[16,3072]{1,0:T(8,128)(2,1)S(1)}, u32[]{:S(2)}, u32[]{:S(2)}) collective-permute-start(bf16[16,3072]{1,0:T(8,128)(2,1)S(1)} %get-tuple-element.85), channel_id=1, source_target_pairs={{0,4},{1,5},{2,6},{3,7},{4,8},{5,9},{6,10},{7,11},{8,12},{9,13},{1... | collective-permute-start | bytes 294920 | tf_op jit(solution)/shard_map/ppermute | solution.py:65
  138.0 10.0 %collective-permute-start.28 = (bf16[16,3072]{1,0:T(8,128)(2,1)S(1)}, bf16[16,3072]{1,0:T(8,128)(2,1)S(1)}, u32[]{:S(2)}, u32[]{:S(2)}) collective-permute-start(bf16[16,3072]{1,0:T(8,128)(2,1)S(1)} %get-tuple-element.84), channel_id=1, source_target_pairs={{0,8},{1,9},{2,10},{3,11},{4,12},{5,13},{6,14},{7,15},{8,0},{9,1},... | collective-permute-start | bytes 294920 | tf_op jit(solution)/shard_map/ppermute | solution.py:65
  138.3 9.7 %collective-permute-start.29 = (bf16[16,3072]{1,0:T(8,128)(2,1)S(1)}, bf16[16,3072]{1,0:T(8,128)(2,1)S(1)}, u32[]{:S(2)}, u32[]{:S(2)}) collective-permute-start(bf16[16,3072]{1,0:T(8,128)(2,1)S(1)} %get-tuple-element.83), channel_id=1, source_target_pairs={{0,12},{1,13},{2,14},{3,15},{4,0},{5,1},{6,2},{7,3},{8,4},{9,5},{1... | collective-permute-start | bytes 294920 | tf_op jit(solution)/shard_map/ppermute | solution.py:65
  141.0 15.6 %copy-start.4 = (bf16[256,512]{1,0:T(8,128)(2,1)S(1)}, bf16[256,512]{1,0:T(8,128)(2,1)}, u32[]{:S(2)}) copy-start(bf16[256,512]{1,0:T(8,128)(2,1)} %copy-done.3) | copy-start | bytes 786436
  147.9 2.0 %collective-permute-start.30 = (bf16[128,2048]{1,0:T(8,128)(2,1)S(1)}, bf16[128,2048]{1,0:T(8,128)(2,1)S(1)}, u32[]{:S(2)}, u32[]{:S(2)}) collective-permute-start(bf16[128,2048]{1,0:T(8,128)(2,1)S(1)} %get-tuple-element.65), channel_id=1, source_target_pairs={{0,1},{1,0},{2,3},{3,2},{4,5},{5,4},{6,7},{7,6},{8,9},{9,8},{10,11... | collective-permute-start | bytes 1572872 | tf_op jit(solution)/shard_map/ppermute | solution.py:65
  150.9 16.1 %collective-permute-start.31 = (bf16[64,2048]{1,0:T(8,128)(2,1)S(1)}, bf16[64,2048]{1,0:T(8,128)(2,1)S(1)}, u32[]{:S(2)}, u32[]{:S(2)}) collective-permute-start(bf16[64,2048]{1,0:T(8,128)(2,1)S(1)} %get-tuple-element.66), channel_id=1, source_target_pairs={{0,2},{1,3},{2,0},{3,1},{4,6},{5,7},{6,4},{7,5},{8,10},{9,11},{10,... | collective-permute-start | bytes 786440 | tf_op jit(solution)/shard_map/ppermute | solution.py:65
  151.6 15.3 %collective-permute-start.32 = (bf16[16,3072]{1,0:T(8,128)(2,1)S(1)}, bf16[16,3072]{1,0:T(8,128)(2,1)S(1)}, u32[]{:S(2)}, u32[]{:S(2)}) collective-permute-start(bf16[16,3072]{1,0:T(8,128)(2,1)S(1)} %get-tuple-element.80), channel_id=1, source_target_pairs={{0,4},{1,5},{2,6},{3,7},{4,8},{5,9},{6,10},{7,11},{8,12},{9,13},{1... | collective-permute-start | bytes 294920 | tf_op jit(solution)/shard_map/ppermute | solution.py:65
  153.7 13.3 %collective-permute-start.33 = (bf16[16,3072]{1,0:T(8,128)(2,1)S(1)}, bf16[16,3072]{1,0:T(8,128)(2,1)S(1)}, u32[]{:S(2)}, u32[]{:S(2)}) collective-permute-start(bf16[16,3072]{1,0:T(8,128)(2,1)S(1)} %get-tuple-element.82), channel_id=1, source_target_pairs={{0,8},{1,9},{2,10},{3,11},{4,12},{5,13},{6,14},{7,15},{8,0},{9,1},... | collective-permute-start | bytes 294920 | tf_op jit(solution)/shard_map/ppermute | solution.py:65
  154.2 12.8 %collective-permute-start.34 = (bf16[16,3072]{1,0:T(8,128)(2,1)S(1)}, bf16[16,3072]{1,0:T(8,128)(2,1)S(1)}, u32[]{:S(2)}, u32[]{:S(2)}) collective-permute-start(bf16[16,3072]{1,0:T(8,128)(2,1)S(1)} %get-tuple-element.81), channel_id=1, source_target_pairs={{0,12},{1,13},{2,14},{3,15},{4,0},{5,1},{6,2},{7,3},{8,4},{9,5},{1... | collective-permute-start | bytes 294920 | tf_op jit(solution)/shard_map/ppermute | solution.py:65
  167.1 6.4 %collective-permute-start.35 = (bf16[16,2048]{1,0:T(8,128)(2,1)S(1)}, bf16[16,2048]{1,0:T(8,128)(2,1)S(1)}, u32[]{:S(2)}, u32[]{:S(2)}) collective-permute-start(bf16[16,2048]{1,0:T(8,128)(2,1)S(1)} %get-tuple-element.86), channel_id=1, source_target_pairs={{0,4},{1,5},{2,6},{3,7},{4,8},{5,9},{6,10},{7,11},{8,12},{9,13},{1... | collective-permute-start | bytes 196616 | tf_op jit(solution)/shard_map/ppermute | solution.py:65
  167.2 7.5 %collective-permute-start.36 = (bf16[16,2048]{1,0:T(8,128)(2,1)S(1)}, bf16[16,2048]{1,0:T(8,128)(2,1)S(1)}, u32[]{:S(2)}, u32[]{:S(2)}) collective-permute-start(bf16[16,2048]{1,0:T(8,128)(2,1)S(1)} %get-tuple-element.88), channel_id=1, source_target_pairs={{0,8},{1,9},{2,10},{3,11},{4,12},{5,13},{6,14},{7,15},{8,0},{9,1},... | collective-permute-start | bytes 196616 | tf_op jit(solution)/shard_map/ppermute | solution.py:65
  169.1 5.6 %collective-permute-start.37 = (bf16[16,2048]{1,0:T(8,128)(2,1)S(1)}, bf16[16,2048]{1,0:T(8,128)(2,1)S(1)}, u32[]{:S(2)}, u32[]{:S(2)}) collective-permute-start(bf16[16,2048]{1,0:T(8,128)(2,1)S(1)} %get-tuple-element.87), channel_id=1, source_target_pairs={{0,12},{1,13},{2,14},{3,15},{4,0},{5,1},{6,2},{7,3},{8,4},{9,5},{1... | collective-permute-start | bytes 196616 | tf_op jit(solution)/shard_map/ppermute | solution.py:65

commit v7 on v6

--- a/solution.py
+++ b/solution.py
@@ -7,11 +7,13 @@
 from jax.experimental.pallas import tpu as pltpu
 from jax.sharding import PartitionSpec as P
 
-GATHER_SHARES = (3, 5)
-SUM_SHARES = (3, 3, 2)
+OUTER_SHARES = (3, 5)
+INNER_CUTS = (1, 2)
+SUM_SHARES = (5, 3)
 MIB = 1024 * 1024
 BF16 = jnp.bfloat16
 DEPTH = 3
+SLOTS = 4
 ONCE = pl.Buffered(1)
 F32 = jnp.float32
 
@@ -88,9 +90,9 @@
             while k < self.dims[dim]:
                 stride = self.strides[dim]
                 pairs = [(i, i + ((i // stride ^ k) - i // stride) * stride) for i in range(self.size)]
+                done = beside.pop(0)(x) if beside else None
                 x = x + lax.ppermute(x, "tensor", pairs)
-                if beside:
-                    x = after(x, beside.pop(0))
+                x = x if done is None else after(x, done)
                 k *= 2
         return x
 
@@ -121,9 +123,21 @@
         for copy in fetch(k + DEPTH - 1, (k + DEPTH - 1) % DEPTH):
             copy.start()
 
-    for copy in fetch(k, k % DEPTH):
-        copy.wait()
-    return k % DEPTH
+    return k % DEPTH, fetch(k, k % DEPTH)
+
+
+def send(copy_of, k, count, fill):
+    @pl.when(k >= SLOTS)
+    def _():
+        copy_of(k - SLOTS).wait()
+
+    fill(k % SLOTS)
+    copy_of(k).start()
+
+    @pl.when(k == count - 1)
+    def _():
+        for j in range(min(SLOTS, count)):
+            copy_of(k - j).wait()
 
 
 def forward_kernel(pieces, low, count, first, *rest):
@@ -131,21 +145,28 @@
     out, held, arrived = rest[-3:]
     step, tile = held.shape[2:]
 
+    depth = step // 2
+
     def fetch(n, slot):
         return [
             pltpu.make_async_copy(
-                tile_at(frozen.at[i, pl.ds(first, step)], low + n, tile),
-                held.at[slot, i],
-                arrived.at[slot, i],
+                tile_at(frozen.at[i, pl.ds(first + h * depth, depth)], low + n, tile),
+                held.at[slot, i, pl.ds(h * depth, depth)],
+                arrived.at[slot, i, h],
             )
             for i in range(2)
+            for h in range(2)
         ]
 
-    slot = ring(fetch, pl.program_id(0), count)
+    slot, copies = ring(fetch, pl.program_id(0), count)
     x = jnp.concatenate([v[...] for v in parts], axis=0)
     for i in range(2):
-        part = dot(x, held[slot, i])
-        out[i] = part if len(rest) == 3 else rest[0][i] + part
+        part = 0.0 if len(rest) == 3 else rest[0][i]
+        for h in range(2):
+            rows = slice(h * depth, (h + 1) * depth)
+            copies[2 * i + h].wait()
+            part = part + dot(x[:, rows], held[slot, i, rows])
+        out[i] = part
 
 
 def forward_chunk(pieces, frozen, start, first, tiles):
@@ -170,7 +191,7 @@
         out_shape=jax.ShapeDtypeStruct((2, tokens, hidden), F32),
         scratch_shapes=[
             pltpu.VMEM((DEPTH, 2, step, tile), BF16),
-            pltpu.SemaphoreType.DMA((DEPTH, 2)),
+            pltpu.SemaphoreType.DMA((DEPTH, 2, 2)),
         ],
         input_output_aliases={} if start is None else {len(operands) - 1: 0},
         compiler_params=params(24),
@@ -338,22 +359,36 @@
     )(adapters, places, base, dhidden, token_order, order, low, seg, up)
 
 
-def grad_b_kernel(dgate, dup, order, low, adapter, *rest):
-    out, left = rest[-2:]
-    adapters, wide, tile = out.shape
+def grad_b_kernel(first, count, dgate, dup, order, low, adapter, *rest):
+    out, left, staged, sent = rest[-4:]
+    group, wide, tile = staged.shape[1:]
+    groups = left.shape[1]
     rank = wide // 2
-
-    @pl.when(pl.program_id(0) == 0)
+    g = pl.program_id(1)
+    k = pl.program_id(0) * groups + g
+
+    @pl.when(k == 0)
     def _():
         turned = dot(order[...], low[...]).T
-        for a in range(adapters):
+        for a in range(groups * group):
             kept = jnp.where(adapter[...] == a, turned, 0.0).astype(BF16)
-            left[0, a * rank : (a + 1) * rank] = kept[:rank]
-            left[1, a * rank : (a + 1) * rank] = kept[rank:]
-
-    for i, grad in enumerate((dgate, dup)):
-        part = dot(left[i], grad[...])
-        out[:, i * rank : (i + 1) * rank, :] = part.reshape(adapters, rank, tile)
+            at = (a // group, slice(a % group * rank, (a % group + 1) * rank))
+            left[(0, *at)] = kept[:rank]
+            left[(1, *at)] = kept[rank:]
+
+    def copy_of(k):
+        block = out.at[pl.ds(k % groups * group, group)]
+        if out.shape[2] != tile:
+            at = pl.multiple_of((first + k // groups) * tile, tile)
+            block = block.at[:, :, pl.ds(at, tile)]
+        return pltpu.make_async_copy(staged.at[k % SLOTS], block, sent.at[k % SLOTS])
+
+    def fill(slot):
+        for i, grad in enumerate((dgate, dup)):
+            part = dot(left[i, g], grad[...])
+            staged[slot, :, i * rank : (i + 1) * rank, :] = part.reshape(group, rank, tile)
+
+    send(copy_of, k, count * groups, fill)
 
 
 def grad_b_of(dgate, dup, order, low, adapter_row, adapters, start, tiles):
@@ -361,37 +396,53 @@
     wide = low.shape[1]
     tile = tile_of(hidden, 256)
     first, last = tiles
-    full = lambda shape: pl.BlockSpec(shape, lambda n: (0,) * len(shape))
-    across = pl.BlockSpec((tokens, tile), lambda n: (0, first + n))
+    groups = 2 if adapters % 2 == 0 else 1
+    group = adapters // groups
+    full = lambda shape: pl.BlockSpec(shape, lambda n, g: (0,) * len(shape))
+    across = pl.BlockSpec((tokens, tile), lambda n, g: (0, first + n))
     operands = [dgate, dup, order, low, adapter_row]
     specs = [across, across, full(order.shape), full(low.shape), full(adapter_row.shape)]
     if start is not None:
         operands.append(start)
-        specs.append(pl.BlockSpec(memory_space=pl.ANY))
+        specs.append(pl.BlockSpec(memory_space=pltpu.HBM))
     part = tile * (last - first) * adapters * wide
     return pl.pallas_call(
-        grad_b_kernel,
-        grid=(last - first,),
+        functools.partial(grad_b_kernel, first, last - first),
+        grid=(last - first, groups),
         in_specs=specs,
-        out_specs=pl.BlockSpec((adapters, wide, tile), lambda n: (0, 0, first + n)),
+        out_specs=pl.BlockSpec(memory_space=pltpu.HBM),
         out_shape=jax.ShapeDtypeStruct((adapters, wide, hidden), F32),
-        scratch_shapes=[pltpu.VMEM((2, adapters * wide // 2, tokens), BF16)],
+        scratch_shapes=[
+            pltpu.VMEM((2, groups, group * wide // 2, tokens), BF16),
+            pltpu.VMEM((SLOTS, group, wide, tile), F32),
+            pltpu.SemaphoreType.DMA((SLOTS,)),
+        ],
         input_output_aliases={} if start is None else {5: 0},
         compiler_params=params(20),
         cost_estimate=cost(2 * tokens * part, 4 * part),
     )(*operands)
 
 
-def grad_a_kernel(per, columns, order, low, adapter, out, turned, mine):
-    @pl.when(pl.program_id(0) == 0)
+def grad_a_kernel(columns, order, low, adapter, out, turned, mine, staged, sent):
+    per = staged.shape[1]
+    k = pl.program_id(0)
+
+    @pl.when(k == 0)
     def _():
         turned[...] = columns[...].astype(F32).T.astype(BF16)
         mine[...] = dot(order[...], low[...])
 
-    for j in range(per):
-        a = pl.program_id(0) * per + j
-        kept = jnp.where(adapter[...] == a, mine[...], 0.0).astype(BF16)
-        out[j] = dot(turned[...], kept)
+    def copy_of(k):
+        return pltpu.make_async_copy(
+            staged.at[k % SLOTS], out.at[pl.ds(k * per, per)], sent.at[k % SLOTS]
+        )
+
+    def fill(slot):
+        for j in range(per):
+            kept = jnp.where(adapter[...] == k * per + j, mine[...], 0.0).astype(BF16)
+            staged[slot, j] = dot(turned[...], kept)
+
+    send(copy_of, k, out.shape[0] // per, fill)
 
 
 def grad_a_of(columns, order, low, adapter, adapters):
@@ -400,12 +451,17 @@
     per = 4 if adapters % 4 == 0 else 1
     full = lambda shape: pl.BlockSpec(shape, lambda n: (0,) * len(shape))
     return pl.pallas_call(
-        functools.partial(grad_a_kernel, per),
+        grad_a_kernel,
         grid=(adapters // per,),
         in_specs=[full(columns.shape), full(order.shape), full(low.shape), full(adapter.shape)],
-        out_specs=pl.BlockSpec((per, shard, wide), lambda n: (n, 0, 0)),
+        out_specs=pl.BlockSpec(memory_space=pltpu.HBM),
         out_shape=jax.ShapeDtypeStruct((adapters, shard, wide), F32),
-        scratch_shapes=[pltpu.VMEM((shard, tokens), BF16), pltpu.VMEM((tokens, wide), F32)],
+        scratch_shapes=[
+            pltpu.VMEM((shard, tokens), BF16),
+            pltpu.VMEM((tokens, wide), F32),
+            pltpu.VMEM((SLOTS, per, shard, wide), F32),
+            pltpu.SemaphoreType.DMA((SLOTS,)),
+        ],
         compiler_params=params(16),
         cost_estimate=cost(2 * tokens * shard * adapters * wide, 4 * shard * adapters * wide),
     )(columns, order, low, adapter)
@@ -447,17 +503,29 @@
     half = near.shape[0]
     block = held.shape[2]
 
+    part = block // 2
+
     def fetch(k, slot):
-        rows = pl.ds(pl.multiple_of(first + k * block, block), block)
+        at = pl.multiple_of(first + k * block, block)
         return [
-            pltpu.make_async_copy(frozen.at[i, rows, :], held.at[slot, i], arrived.at[slot, i])
+            pltpu.make_async_copy(
+                frozen.at[i, pl.ds(at + h * part, part)],
+                held.at[slot, i, pl.ds(h * part, part)],
+                arrived.at[slot, i, h],
+            )
+            for h in range(2)
             for i in range(2)
         ]
 
-    slot = ring(fetch, pl.program_id(0), count)
-    term = dot(dgate[...], held[slot, 0], ((1,), (1,))) + dot(dup[...], held[slot, 1], ((1,), (1,)))
-    near[...] = term[:half].astype(BF16)
-    far[...] = term[half:].astype(BF16)
+    slot, copies = ring(fetch, pl.program_id(0), count)
+    for h in range(2):
+        rows = slice(h * part, (h + 1) * part)
+        copies[2 * h].wait()
+        term = dot(dgate[...], held[slot, 0, rows], ((1,), (1,)))
+        copies[2 * h + 1].wait()
+        term = term + dot(dup[...], held[slot, 1, rows], ((1,), (1,)))
+        near[:, rows] = term[:half].astype(BF16)
+        far[:, rows] = term[half:].astype(BF16)
 
 
 def backward_chunk(frozen, dgate, dup, first, step):
@@ -474,7 +542,7 @@
         out_shape=[jax.ShapeDtypeStruct((tokens // 2, step), BF16)] * 2,
         scratch_shapes=[
             pltpu.VMEM((DEPTH, 2, block, hidden), BF16),
-            pltpu.SemaphoreType.DMA((DEPTH, 2)),
+            pltpu.SemaphoreType.DMA((DEPTH, 2, 2)),
         ],
         compiler_params=params(20),
         cost_estimate=cost(4 * tokens * step * hidden, 4 * step * hidden),
@@ -589,23 +657,28 @@
     hidden = frozen.shape[2]
     tiles = hidden // tile_of(hidden, 256)
     chunks = []
-    for share in GATHER_SHARES:
+    for share in OUTER_SHARES:
         first = sum(v.shape[1] for v in chunks)
-        chunks.append(activations[:, first : first + width * share // sum(GATHER_SHARES)])
+        chunks.append(activations[:, first : first + width * share // sum(OUTER_SHARES)])
     outer = []
     for x in chunks:
         x = torus.gather(after(x, outer[-1]) if outer else x, 0)
         outer.append(x.reshape(a * rows, -1))
+    parts = []
+    for x, cuts in zip(outer, INNER_CUTS):
+        step = x.shape[1] // cuts
+        parts += [x[:, j * step : (j + 1) * step] for j in range(cuts)]
     base = None
     gathered = []
-    for q, x in enumerate(outer):
+    first = 0
+    for q, x in enumerate(parts):
         near = [x] + [torus.move(x, 1, -k) for k in range(1, b)]
         near[1:] = lax.optimization_barrier((*near[1:], base if q else outer[-1]))[:-1]
         far = [torus.move(v, 2, -1) for v in near]
         gathered.append([*near, *far])
-        first = sum(v.shape[1] for v in chunks[:q])
-        for cut in parts_of(tiles, 4 if q else 1):
+        for cut in parts_of(tiles, 4 if q == len(parts) - 1 else 1):
             base = forward_chunk(gathered[q], frozen, base, first, cut)
+        first += x.shape[1]
 
     columns, partial_in = low_in_partial(
         gathered, segment[:, None], adapter_down_factors, seg_adapter, places, index, rows
@@ -615,20 +688,29 @@
         base, dhidden, token_order, order, low_in, segment[:, None], adapter_up_factors,
         seg_adapter, places, rows,
     )
+    thirds = parts_of(tiles, 3)
     grad_b = []
-    thirds = parts_of(tiles, 3)
-    for cut in thirds[:-1]:
+
+    def grad_b_part(token):
         grad_b.append(
             grad_b_of(
-                dgate, dup, order, low_in, adapter[None, :], adapter_list,
-                grad_b[-1] if grad_b else None, cut,
+                dgate, dup, order, after(low_in, token), adapter[None, :], adapter_list,
+                grad_b[-1] if grad_b else None, thirds[len(grad_b)],
             )
         )
+        return grad_b[-1]
+
     cuts = []
     for share in SUM_SHARES:
         cuts.append((sum(v[1] for v in cuts), width * share // sum(SUM_SHARES)))
-    near, far = backward_chunk(frozen, dgate, dup, *cuts[0])
-    low_out = whole_sum(partial_out, [*grad_b, near])
+    terms = []
+
+    def first_term(token):
+        terms.append(backward_chunk(frozen, after(dgate, token), dup, *cuts[0]))
+        return terms[0][0]
+
+    low_out = whole_sum(partial_out, [grad_b_part] * (len(thirds) - 1) + [first_term])
+    near, far = terms[0][0], after(terms[0][1], low_out)
     side, side_far = side_of(
         order, low_out, segment[:, None], adapter_down_factors, seg_adapter, places
     )
@@ -648,17 +730,15 @@
             total = total + v.astype(F32)
         inners.append(total.astype(BF16).reshape(a, rows, step))
         outer_moves.append([torus.move(inners[q][k], 0, k) for k in range(1, a)])
+    grad_b = grad_b_part(inner_moves[-1][0])
     for q, inner in enumerate(inners):
         total = inner[0].astype(F32)
         for v in outer_moves[q]:
-            v = lax.optimization_barrier((v, *inner_moves[-1]))[0] if q < len(cuts) - 1 else v
+            behind = (v, *inner_moves[-1], grad_b)
+            v = lax.optimization_barrier(behind)[0] if q < len(cuts) - 1 else v
             total = total + v.astype(F32)
         blocks.append(total.astype(BF16))
     dinput = jnp.concatenate(blocks, axis=1)
-    grad_b = grad_b_of(
-        dgate, dup, order, after(low_in, sums[-1][0]), adapter[None, :], adapter_list,
-        grad_b[-1] if grad_b else None, thirds[-1],
-    )
     grad_a = grad_a_of(
         columns, order, after(low_out, sums[-1][0]), adapter[:, None], adapter_list
     )

time: 176 us -> 198 us (1.12)
  Pallas kernels: 90.6 us -> 123 us
  waiting for transfers between devices: 32.1 us -> 27.7 us
  starting transfers between devices: 40.7 us -> 36.6 us
    pallas_call x3 -> x2, Pallas kernels: 25.8 us -> 43.2 us  [backward_chunk(): pl.pallas_call(functools.partial(backward_kernel, count, first), grid=(co...]
    pallas_call x5 -> x6, Pallas kernels: 31.7 us -> 48.9 us  [forward_chunk(): pl.pallas_call(functools.partial(forward_kernel, len(pieces), low, count,...]
    ppermute x32 -> x30, waiting for transfers between devices: 32.1 us -> 26.9 us  [move(): return lax.ppermute(x, 'tensor', pairs)]
    ppermute x32 -> x30, starting transfers between devices: 33.3 us -> 28.6 us  [move(): return lax.ppermute(x, 'tensor', pairs)]
    pallas_call x3 -> x2, Pallas kernels: 4.99 us -> 4.27 us  [core_sum(): pl.pallas_call(functools.partial(core_sum_kernel, first // block), grid_s...]
  transfers between devices with their start and end apart: 38 -> 36, of which waited for: 15 -> 15; matrix products, arithmetic and copies ran while one was open for 4% -> 3% of each run, Pallas kernels for 44% -> 56%
where the time goes in v7:
time: 198 us; the launch traced here: 197 us
  Pallas kernels  123 us (62%)
  starting transfers between devices  36.6 us (18%)
  waiting for transfers between devices  27.7 us (14%)
  other arithmetic  5.25 us (3%)
  local copies, waits for them, and re-layouts  3.57 us (2%)
    pallas_call x6, Pallas kernels, forward_chunk(): pl.pallas_call(functools.partial(forward_kernel, len(pieces), low, count,...  48.9 us
    pallas_call x2, Pallas kernels, backward_chunk(): pl.pallas_call(functools.partial(backward_kernel, count, first), grid=(co...  43.2 us
    ppermute x30, starting transfers between devices, move(): return lax.ppermute(x, 'tensor', pairs)  28.6 us
    ppermute x30, waiting for transfers between devices, move(): return lax.ppermute(x, 'tensor', pairs)  26.9 us
    pallas_call x3, Pallas kernels, grad_b_of(): pl.pallas_call(functools.partial(grad_b_kernel, first, last - first), gri...  11.9 us
    ppermute x6, starting transfers between devices, exchange_sum(): x = x + lax.ppermute(x, 'tensor', pairs)  7.99 us
    pallas_call x1, Pallas kernels, middle(): pl.pallas_call(functools.partial(middle_kernel, rows), grid_spec=pltpu.Pr...  7.47 us
    pallas_call x1, Pallas kernels, grad_a_of(): pl.pallas_call(grad_a_kernel, grid=(adapters // per,), in_specs=[full(col...  4.66 us
  transfers between devices with their start and end apart: 36, of which 15 were waited for; matrix products, arithmetic and copies ran while one was open for 3% of the time, Pallas kernels for 56%

profile of v7, /device:TPU:0, one launch (start us, length us, event | category | flops | bytes accessed | tf_op | source)
XLA Modules:
  0.0 197.5 jit_solution(3997686106201111417)
XLA Ops:
  0.6 0.9 slice_bitcast_fusion
  1.5 3.1 %collective-permute-start.2 = (bf16[16,3072]{1,0:T(8,128)(2,1)S(1)}, bf16[16,3072]{1,0:T(8,128)(2,1)S(1)}, u32[]{:S(2)}, u32[]{:S(2)}) collective-permute-start(bf16[16,3072]{1,0:T(8,128)(2,1)S(1)} %get-tuple-element.81), channel_id=1, source_target_pairs={{0,4},{1,5},{2,6},{3,7},{4,8},{5,9},{6,10},{7,11},{8,12},{9,13},{1... | collective-permute-start | bytes 294920 | tf_op jit(solution)/shard_map/ppermute | solution.py:67
  4.6 2.6 %collective-permute-start.1 = (bf16[16,3072]{1,0:T(8,128)(2,1)S(1)}, bf16[16,3072]{1,0:T(8,128)(2,1)S(1)}, u32[]{:S(2)}, u32[]{:S(2)}) collective-permute-start(bf16[16,3072]{1,0:T(8,128)(2,1)S(1)} %get-tuple-element.81), channel_id=1, source_target_pairs={{0,8},{1,9},{2,10},{3,11},{4,12},{5,13},{6,14},{7,15},{8,0},{9,1},... | collective-permute-start | bytes 294920 | tf_op jit(solution)/shard_map/ppermute | solution.py:67
  7.2 1.3 collective-permute-start
  8.6 0.9 slice.60
  11.3 2.5 %collective-permute-done.1 = bf16[16,3072]{1,0:T(8,128)(2,1)S(1)} collective-permute-done((bf16[16,3072]{1,0:T(8,128)(2,1)S(1)}, bf16[16,3072]{1,0:T(8,128)(2,1)S(1)}, u32[]{:S(2)}, u32[]{:S(2)}) %collective-permute-start.1) | collective-permute-done | bytes 98336 | tf_op jit(solution)/shard_map/ppermute | solution.py:67
  13.9 2.6 %collective-permute-start.5 = (bf16[16,5120]{1,0:T(8,128)(2,1)S(1)}, bf16[16,5120]{1,0:T(8,128)(2,1)S(1)}, u32[]{:S(2)}, u32[]{:S(2)}) collective-permute-start(bf16[16,5120]{1,0:T(8,128)(2,1)S(1)} %slice.60), channel_id=1, source_target_pairs={{0,4},{1,5},{2,6},{3,7},{4,8},{5,9},{6,10},{7,11},{8,12},{9,13},{1... | collective-permute-start | bytes 491528 | tf_op jit(solution)/shard_map/ppermute | solution.py:67
  16.5 1.6 collective-permute-start.4
  20.0 1.5 collective-permute-start.8
  21.5 1.5 collective-permute-done.5
  23.0 5.9 %collective-permute-done.4 = bf16[16,5120]{1,0:T(8,128)(2,1)S(1)} collective-permute-done((bf16[16,5120]{1,0:T(8,128)(2,1)S(1)}, bf16[16,5120]{1,0:T(8,128)(2,1)S(1)}, u32[]{:S(2)}, u32[]{:S(2)}) %collective-permute-start.4) | collective-permute-done | bytes 163872 | tf_op jit(solution)/shard_map/ppermute | solution.py:67
  29.0 1.5 collective-permute-done.8.rest_1_.rest_9_
  30.5 1.6 collective-permute-start.7
  32.3 16.5 %shard_map.103.rest_5_ = f32[2,256,1792]{2,1,0:T(8,128)S(1)} custom-call(bf16[64,3072]{1,0:T(8,128)(2,1)S(1)} %bitcast.34, bf16[64,3072]{1,0:T(8,128)(2,1)S(1)} %collective-permute-done.8.rest_1_.rest_9_, bf16[64,3072]{1,0:T(8,128)(2,1)S(1)} %collective-permute-done.9.rest_2_.rest_10_, bf16[64,3072]{1,0:T(8,128)(2,1)S(1)} %collective-permute-done.10.rest_3_.rest_11_, ...), custom_call_target="tpu_custom_call" | custom-call | flops 5637144576 | bytes 22020096 | tf_op jit(solution)/shard_map/pallas_call | solution.py:186
  49.4 1.3 collective-permute-start.6
  50.7 14.5 %shard_map.104.rest_5_ = f32[2,256,1792]{2,1,0:T(8,128)S(1)} custom-call(bf16[64,2560]{1,0:T(8,128)(2,1)S(1)} %get-tuple-element.75.rest_0_.rest_12_, bf16[64,2560]{1,0:T(8,128)(2,1)S(1)} %collective-permute-done.7.rest_1_.rest_13_, bf16[64,2560]{1,0:T(8,128)(2,1)S(1)} %collective-permute-done.11.rest_2_.rest_14_, ...), custom_call_target="tpu_custom_call", output_to_operand_aliasing={{}: (5, {})} | custom-call | flops 4697620480 | bytes 18350080 | tf_op jit(solution)/shard_map/pallas_call | solution.py:186
  66.0 1.1 collective-permute-done.14.rest_3_.rest_19_
  67.0 1.4 shard_map.109
  69.8 1.1 collective-permute-start.16
  70.9 3.0 %shard_map.105.rest_5_ = f32[2,256,1792]{2,1,0:T(8,128)S(1)} custom-call(bf16[64,2560]{1,0:T(8,128)(2,1)S(1)} %get-tuple-element.76.rest_0_.rest_16_, bf16[64,2560]{1,0:T(8,128)(2,1)S(1)} %collective-permute-done.6.rest_1_.rest_17_, bf16[64,2560]{1,0:T(8,128)(2,1)S(1)} %collective-permute-done.13.rest_2_.rest_18_, ...), custom_call_target="tpu_custom_call", output_to_operand_aliasing={{}: (5, {})} | custom-call | flops 671088640 | bytes 2621440 | tf_op jit(solution)/shard_map/pallas_call | solution.py:186
  74.2 2.7 %collective-permute-start.17 = (f32[128,128]{1,0:T(8,128)S(1)}, f32[128,128]{1,0:T(8,128)S(1)}, u32[]{:S(2)}, u32[]{:S(2)}) collective-permute-start(f32[128,128]{1,0:T(8,128)S(1)} %add.292), channel_id=1, source_target_pairs={{0,4},{1,5},{2,6},{3,7},{4,0},{5,1},{6,2},{7,3},{8,12},{9,13},{10,... | collective-permute-start | bytes 196616 | tf_op jit(solution)/shard_map/ppermute | solution.py:94
  76.9 4.9 %shard_map.106.rest_5_ = f32[2,256,1792]{2,1,0:T(8,128)S(1)} custom-call(bf16[64,2560]{1,0:T(8,128)(2,1)S(1)} %get-tuple-element.76.rest_0_.rest_16_, bf16[64,2560]{1,0:T(8,128)(2,1)S(1)} %collective-permute-done.6.rest_1_.rest_17_, bf16[64,2560]{1,0:T(8,128)(2,1)S(1)} %collective-permute-done.13.rest_2_.rest_18_, ...), custom_call_target="tpu_custom_call", output_to_operand_aliasing={{}: (5, {})} | custom-call | flops 1342177280 | bytes 5242880 | tf_op jit(solution)/shard_map/pallas_call | solution.py:186
  81.8 1.5 collective-permute-start.18
  83.3 4.9 %shard_map.107.rest_5_ = f32[2,256,1792]{2,1,0:T(8,128)S(1)} custom-call(bf16[64,2560]{1,0:T(8,128)(2,1)S(1)} %get-tuple-element.76.rest_0_.rest_16_, bf16[64,2560]{1,0:T(8,128)(2,1)S(1)} %collective-permute-done.6.rest_1_.rest_17_, bf16[64,2560]{1,0:T(8,128)(2,1)S(1)} %collective-permute-done.13.rest_2_.rest_18_, ...), custom_call_target="tpu_custom_call", output_to_operand_aliasing={{}: (5, {})} | custom-call | flops 1342177280 | bytes 5242880 | tf_op jit(solution)/shard_map/pallas_call | solution.py:186
  88.5 5.1 %shard_map.108.base = f32[2,256,1792]{2,1,0:T(8,128)S(1)} custom-call(bf16[64,2560]{1,0:T(8,128)(2,1)S(1)} %get-tuple-element.76.rest_0_.rest_16_, bf16[64,2560]{1,0:T(8,128)(2,1)S(1)} %collective-permute-done.6.rest_1_.rest_17_, bf16[64,2560]{1,0:T(8,128)(2,1)S(1)} %collective-permute-done.13.rest_2_.rest_18_, ...), custom_call_target="tpu_custom_call", output_to_operand_aliasing={{}: (5, {})} | custom-call | flops 1342177280 | bytes 5242880 | tf_op jit(solution)/shard_map/pallas_call | solution.py:186
  94.4 7.5 %shard_map.110 = (bf16[256,1792]{1,0:T(8,128)(2,1)S(1)}, bf16[256,1792]{1,0:T(8,128)(2,1)S(1)}, f32[256,128]{1,0:T(8,128)S(1)}) custom-call(s32[8]{0:T(128)S(1)} %bitcast.48, s32[16]{0:T(128)S(1)} %get-tuple-element.70.places, f32[2,256,1792]{2,1,0:T(8,128)S(1)} %shard_map.108.base, bf16[256,1792]{1,0:T(8,128)(2,1)S(1)} %copy-done.1, ...), custom_call_target="tpu_custom_call" | custom-call | flops 1879048192 | bytes 10092544 | tf_op jit(solution)/shard_map/pallas_call | solution.py:334
  103.3 0.9 collective-permute-start.21
  104.2 3.6 %shard_map.111.rest_0_ = f32[24,128,1792]{2,1,0:T(8,128)} custom-call(bf16[256,1792]{1,0:T(8,128)(2,1)S(1)} %get-tuple-element.57.dgate, bf16[256,1792]{1,0:T(8,128)(2,1)S(1)} %get-tuple-element.43.dup, bf16[256,256]{1,0:T(8,128)(2,1)S(1)} %fusion.1.order, bf16[256,128]{1,0:T(8,128)(2,1)S(1)} %bitcast.37, s32[1,256]{1,0:T(1,128)S(1)} %bitcast.42), custom_call_target="tpu_custom_call" | custom-call | flops 805306368 | bytes 6291456 | tf_op jit(solution)/shard_map/pallas_call | solution.py:409
  108.2 3.6 %shard_map.112.rest_0_ = f32[24,128,1792]{2,1,0:T(8,128)} custom-call(bf16[256,1792]{1,0:T(8,128)(2,1)S(1)} %get-tuple-element.57.dgate, bf16[256,1792]{1,0:T(8,128)(2,1)S(1)} %get-tuple-element.43.dup, bf16[256,256]{1,0:T(8,128)(2,1)S(1)} %fusion.1.order, bf16[256,128]{1,0:T(8,128)(2,1)S(1)} %bitcast.38, ...), custom_call_target="tpu_custom_call", output_to_operand_aliasing={{}: (5, {})} | custom-call | flops 805306368 | bytes 6291456 | tf_op jit(solution)/shard_map/pallas_call | solution.py:409
  112.3 1.5 collective-permute-start.23
  113.8 26.6 %shard_map.113 = (bf16[128,5120]{1,0:T(8,128)(2,1)S(1)}, bf16[128,5120]{1,0:T(8,128)(2,1)S(1)}) custom-call(bf16[2,8192,1792]{2,1,0:T(8,128)(2,1)} %frozen.3, bf16[256,1792]{1,0:T(8,128)(2,1)S(1)} %get-tuple-element.57.dgate, bf16[256,1792]{1,0:T(8,128)(2,1)S(1)} %get-tuple-element.43.dup), custom_call_target="tpu_custom_call" | custom-call | flops 9395240960 | bytes 36700160 | tf_op jit(solution)/shard_map/pallas_call | solution.py:537
  140.8 1.1 collective-permute-done.24
  142.1 1.4 shard_map.114
  144.0 1.4 collective-permute-done.26.side_far
  145.4 3.1 %shard_map.115 = (bf16[64,5120]{1,0:T(8,128)(2,1)S(1)}, bf16[64,5120]{1,0:T(8,128)(2,1)}) custom-call(s32[2]{0:T(128)S(1)} %pad_add_fusion.at, bf16[128,5120]{1,0:T(8,128)(2,1)S(1)} %get-tuple-element.49.near, bf16[128,5120]{1,0:T(8,128)(2,1)S(1)} %collective-permute-done.25.far, f32[128,512]{1,0:T(8,128)S(1)} %get-tuple-element.53.side, ...), custom_call_target="tpu_custom_call" | custom-call | flops 1310720 | bytes 3932160 | tf_op jit(solution)/shard_map/pallas_call | solution.py:579
  148.4 1.1 collective-permute-start.27
  149.7 16.6 %shard_map.116 = (bf16[128,3072]{1,0:T(8,128)(2,1)S(1)}, bf16[128,3072]{1,0:T(8,128)(2,1)S(1)}) custom-call(bf16[2,8192,1792]{2,1,0:T(8,128)(2,1)} %frozen.3, bf16[256,1792]{1,0:T(8,128)(2,1)S(1)} %get-tuple-element.57.dgate, bf16[256,1792]{1,0:T(8,128)(2,1)S(1)} %get-tuple-element.43.dup), custom_call_target="tpu_custom_call" | custom-call | flops 5637144576 | bytes 22020096 | tf_op jit(solution)/shard_map/pallas_call | solution.py:537
  166.4 1.2 add_convert_fusion
  167.6 1.0 collective-permute-done.29.far
  168.7 1.2 shard_map.117
  169.9 1.0 collective-permute-start.30
  170.9 2.4 %collective-permute-start.32 = (bf16[16,5120]{1,0:T(8,128)(2,1)S(1)}, bf16[16,5120]{1,0:T(8,128)(2,1)S(1)}, u32[]{:S(2)}, u32[]{:S(2)}) collective-permute-start(bf16[16,5120]{1,0:T(8,128)(2,1)S(1)} %get-tuple-element.73), channel_id=1, source_target_pairs={{0,12},{1,13},{2,14},{3,15},{4,0},{5,1},{6,2},{7,3},{8,4},{9,5},{1... | collective-permute-start | bytes 491528 | tf_op jit(solution)/shard_map/ppermute | solution.py:67
  174.4 4.7 %shard_map.119 = f32[24,512,128]{2,1,0:T(8,128)} custom-call(bf16[256,512]{1,0:T(8,128)(2,1)S(1)} %copy-done.3, bf16[256,256]{1,0:T(8,128)(2,1)S(1)} %fusion.1.order, bf16[256,128]{1,0:T(8,128)(2,1)S(1)} %bitcast.41, s32[256,1]{1,0:T(8,128)S(1)} %copy.25.adapter), custom_call_target="tpu_custom_call" | custom-call | flops 805306368 | bytes 6291456 | tf_op jit(solution)/shard_map/pallas_call | solution.py:453
  179.1 2.0 %collective-permute-done.30 = bf16[64,3072]{1,0:T(8,128)(2,1)S(1)} collective-permute-done((bf16[64,3072]{1,0:T(8,128)(2,1)S(1)}, bf16[64,3072]{1,0:T(8,128)(2,1)S(1)}, u32[]{:S(2)}, u32[]{:S(2)}) %collective-permute-start.30) | collective-permute-done | bytes 393248 | tf_op jit(solution)/shard_map/ppermute | solution.py:67
  181.2 2.4 %collective-permute-start.35 = (bf16[16,3072]{1,0:T(8,128)(2,1)S(1)}, bf16[16,3072]{1,0:T(8,128)(2,1)S(1)}, u32[]{:S(2)}, u32[]{:S(2)}) collective-permute-start(bf16[16,3072]{1,0:T(8,128)(2,1)S(1)} %get-tuple-element.78), channel_id=1, source_target_pairs={{0,12},{1,13},{2,14},{3,15},{4,0},{5,1},{6,2},{7,3},{8,4},{9,5},{1... | collective-permute-start | bytes 294920 | tf_op jit(solution)/shard_map/ppermute | solution.py:67
  184.2 4.6 %shard_map.118 = f32[24,128,1792]{2,1,0:T(8,128)} custom-call(bf16[256,1792]{1,0:T(8,128)(2,1)S(1)} %get-tuple-element.57.dgate, bf16[256,1792]{1,0:T(8,128)(2,1)S(1)} %get-tuple-element.43.dup, bf16[256,256]{1,0:T(8,128)(2,1)S(1)} %fusion.1.order, bf16[256,128]{1,0:T(8,128)(2,1)S(1)} %bitcast.39, ...), custom_call_target="tpu_custom_call", output_to_operand_aliasing={{}: (5, {})} | custom-call | flops 1207959552 | bytes 9437184 | tf_op jit(solution)/shard_map/pallas_call | solution.py:409
  189.4 2.1 %collective-permute-done.31 = bf16[16,5120]{1,0:T(8,128)(2,1)S(1)} collective-permute-done((bf16[16,5120]{1,0:T(8,128)(2,1)S(1)}, bf16[16,5120]{1,0:T(8,128)(2,1)S(1)}, u32[]{:S(2)}, u32[]{:S(2)}) %collective-permute-start.31) | collective-permute-done | bytes 163872 | tf_op jit(solution)/shard_map/ppermute | solution.py:67
  191.6 5.1 %collective-permute-done.34 = bf16[16,3072]{1,0:T(8,128)(2,1)S(1)} collective-permute-done((bf16[16,3072]{1,0:T(8,128)(2,1)S(1)}, bf16[16,3072]{1,0:T(8,128)(2,1)S(1)}, u32[]{:S(2)}, u32[]{:S(2)}) %collective-permute-start.34) | collective-permute-done | bytes 98336 | tf_op jit(solution)/shard_map/ppermute | solution.py:67
  (118 shorter events, 14.8 us)
Async XLA Ops:
  1.5 9.7 %collective-permute-start.2 = (bf16[16,3072]{1,0:T(8,128)(2,1)S(1)}, bf16[16,3072]{1,0:T(8,128)(2,1)S(1)}, u32[]{:S(2)}, u32[]{:S(2)}) collective-permute-start(bf16[16,3072]{1,0:T(8,128)(2,1)S(1)} %get-tuple-element.81), channel_id=1, source_target_pairs={{0,4},{1,5},{2,6},{3,7},{4,8},{5,9},{6,10},{7,11},{8,12},{9,13},{1... | collective-permute-start | bytes 294920 | tf_op jit(solution)/shard_map/ppermute | solution.py:67
  4.6 9.2 %collective-permute-start.1 = (bf16[16,3072]{1,0:T(8,128)(2,1)S(1)}, bf16[16,3072]{1,0:T(8,128)(2,1)S(1)}, u32[]{:S(2)}, u32[]{:S(2)}) collective-permute-start(bf16[16,3072]{1,0:T(8,128)(2,1)S(1)} %get-tuple-element.81), channel_id=1, source_target_pairs={{0,8},{1,9},{2,10},{3,11},{4,12},{5,13},{6,14},{7,15},{8,0},{9,1},... | collective-permute-start | bytes 294920 | tf_op jit(solution)/shard_map/ppermute | solution.py:67
  7.2 6.6 %collective-permute-start = (bf16[16,3072]{1,0:T(8,128)(2,1)S(1)}, bf16[16,3072]{1,0:T(8,128)(2,1)S(1)}, u32[]{:S(2)}, u32[]{:S(2)}) collective-permute-start(bf16[16,3072]{1,0:T(8,128)(2,1)S(1)} %get-tuple-element.81), channel_id=1, source_target_pairs={{0,12},{1,13},{2,14},{3,15},{4,0},{5,1},{6,2},{7,3},{8,4},{9,5},{1... | collective-permute-start | bytes 294920 | tf_op jit(solution)/shard_map/ppermute | solution.py:67
  13.9 9.1 %collective-permute-start.5 = (bf16[16,5120]{1,0:T(8,128)(2,1)S(1)}, bf16[16,5120]{1,0:T(8,128)(2,1)S(1)}, u32[]{:S(2)}, u32[]{:S(2)}) collective-permute-start(bf16[16,5120]{1,0:T(8,128)(2,1)S(1)} %slice.60), channel_id=1, source_target_pairs={{0,4},{1,5},{2,6},{3,7},{4,8},{5,9},{6,10},{7,11},{8,12},{9,13},{1... | collective-permute-start | bytes 491528 | tf_op jit(solution)/shard_map/ppermute | solution.py:67
  16.5 12.4 %collective-permute-start.4 = (bf16[16,5120]{1,0:T(8,128)(2,1)S(1)}, bf16[16,5120]{1,0:T(8,128)(2,1)S(1)}, u32[]{:S(2)}, u32[]{:S(2)}) collective-permute-start(bf16[16,5120]{1,0:T(8,128)(2,1)S(1)} %slice.60), channel_id=1, source_target_pairs={{0,8},{1,9},{2,10},{3,11},{4,12},{5,13},{6,14},{7,15},{8,0},{9,1},... | collective-permute-start | bytes 491528 | tf_op jit(solution)/shard_map/ppermute | solution.py:67
  18.1 10.8 %collective-permute-start.3 = (bf16[16,5120]{1,0:T(8,128)(2,1)S(1)}, bf16[16,5120]{1,0:T(8,128)(2,1)S(1)}, u32[]{:S(2)}, u32[]{:S(2)}) collective-permute-start(bf16[16,5120]{1,0:T(8,128)(2,1)S(1)} %slice.60), channel_id=1, source_target_pairs={{0,12},{1,13},{2,14},{3,15},{4,0},{5,1},{6,2},{7,3},{8,4},{9,5},{1... | collective-permute-start | bytes 491528 | tf_op jit(solution)/shard_map/ppermute | solution.py:67
  20.0 10.5 %collective-permute-start.8 = (bf16[64,3072]{1,0:T(8,128)(2,1)S(1)}, bf16[64,3072]{1,0:T(8,128)(2,1)S(1)}, u32[]{:S(2)}, u32[]{:S(2)}) collective-permute-start(bf16[64,3072]{1,0:T(8,128)(2,1)S(1)} %bitcast.32), channel_id=1, source_target_pairs={{0,2},{1,3},{2,0},{3,1},{4,6},{5,7},{6,4},{7,5},{8,10},{9,11},{10,... | collective-permute-start | bytes 1179656 | tf_op jit(solution)/shard_map/ppermute | solution.py:67
  21.5 10.8 %collective-permute-start.9 = (bf16[64,3072]{1,0:T(8,128)(2,1)S(1)}, bf16[64,3072]{1,0:T(8,128)(2,1)S(1)}, u32[]{:S(2)}, u32[]{:S(2)}) collective-permute-start(bf16[64,3072]{1,0:T(8,128)(2,1)S(1)} %bitcast.33), channel_id=1, source_target_pairs={{0,1},{1,0},{2,3},{3,2},{4,5},{5,4},{6,7},{7,6},{8,9},{9,8},{10,11... | collective-permute-start | bytes 1179656 | tf_op jit(solution)/shard_map/ppermute | solution.py:67
  30.4 1.9 collective-permute-start.10
  30.5 18.7 %copy-start.5 = (s32[24]{0:T(128)S(1)}, s32[24]{0:T(128)}, u32[]{:S(2)}) copy-start(s32[24]{0:T(128)} %param.15) | copy-start | bytes 292
  30.5 18.3 %collective-permute-start.7 = (bf16[64,2560]{1,0:T(8,128)(2,1)S(1)}, bf16[64,2560]{1,0:T(8,128)(2,1)S(1)}, u32[]{:S(2)}, u32[]{:S(2)}) collective-permute-start(bf16[64,2560]{1,0:T(8,128)(2,1)S(1)} %get-tuple-element.75.rest_0_.rest_12_), channel_id=1, source_target_pairs={{0,2},{1,3},{2,0},{3,1},{4,6},{5,7},{6,4},{7,5},{8,10},{9,11},{10,... | collective-permute-start | bytes 983048 | tf_op jit(solution)/shard_map/ppermute | solution.py:67
  32.1 18.7 %collective-permute-start.11 = (bf16[64,2560]{1,0:T(8,128)(2,1)S(1)}, bf16[64,2560]{1,0:T(8,128)(2,1)S(1)}, u32[]{:S(2)}, u32[]{:S(2)}) collective-permute-start(bf16[64,2560]{1,0:T(8,128)(2,1)S(1)} %get-tuple-element.75.rest_0_.rest_12_), channel_id=1, source_target_pairs={{0,1},{1,0},{2,3},{3,2},{4,5},{5,4},{6,7},{7,6},{8,9},{9,8},{10,11... | collective-permute-start | bytes 983048 | tf_op jit(solution)/shard_map/ppermute | solution.py:67
  48.8 2.0 collective-permute-start.12
  49.3 17.7 %copy-start = (bf16[24,512,128]{2,1,0:T(8,128)(2,1)S(1)}, bf16[24,512,128]{2,1,0:T(8,128)(2,1)}, u32[]{:S(2)}) copy-start(bf16[24,512,128]{2,1,0:T(8,128)(2,1)} %rest_7_.3) | copy-start | bytes 9437188
  49.4 17.7 %copy-start.4 = (s32[1,8]{1,0:T(1,128)S(1)}, s32[1,8]{1,0:T(1,128)}, u32[]{:S(2)}) copy-start(s32[1,8]{1,0:T(1,128)} %param.13) | copy-start | bytes 100
  49.4 15.9 %collective-permute-start.6 = (bf16[64,2560]{1,0:T(8,128)(2,1)S(1)}, bf16[64,2560]{1,0:T(8,128)(2,1)S(1)}, u32[]{:S(2)}, u32[]{:S(2)}) collective-permute-start(bf16[64,2560]{1,0:T(8,128)(2,1)S(1)} %get-tuple-element.76.rest_0_.rest_16_), channel_id=1, source_target_pairs={{0,2},{1,3},{2,0},{3,1},{4,6},{5,7},{6,4},{7,5},{8,10},{9,11},{10,... | collective-permute-start | bytes 983048 | tf_op jit(solution)/shard_map/ppermute | solution.py:67
  50.7 15.3 %collective-permute-start.13 = (bf16[64,2560]{1,0:T(8,128)(2,1)S(1)}, bf16[64,2560]{1,0:T(8,128)(2,1)S(1)}, u32[]{:S(2)}, u32[]{:S(2)}) collective-permute-start(bf16[64,2560]{1,0:T(8,128)(2,1)S(1)} %get-tuple-element.76.rest_0_.rest_16_), channel_id=1, source_target_pairs={{0,1},{1,0},{2,3},{3,2},{4,5},{5,4},{6,7},{7,6},{8,9},{9,8},{10,11... | collective-permute-start | bytes 983048 | tf_op jit(solution)/shard_map/ppermute | solution.py:67
  65.3 1.8 collective-permute-start.14
  68.4 2.5 %copy-start.2 = (bf16[256,512]{1,0:T(8,128)(2,1)}, bf16[256,512]{1,0:T(8,128)(2,1)S(1)}, u32[]{:S(2)}) copy-start(bf16[256,512]{1,0:T(8,128)(2,1)S(1)} %get-tuple-element.67.columns) | copy-start | bytes 786436
  68.4 1.3 collective-permute-start.15
  69.8 4.4 %collective-permute-start.16 = (f32[128,128]{1,0:T(8,128)S(1)}, f32[128,128]{1,0:T(8,128)S(1)}, u32[]{:S(2)}, u32[]{:S(2)}) collective-permute-start(f32[128,128]{1,0:T(8,128)S(1)} %slice_add_fusion.1), channel_id=1, source_target_pairs={{0,2},{1,3},{2,0},{3,1},{4,6},{5,7},{6,4},{7,5},{8,10},{9,11},{10,... | collective-permute-start | bytes 196616 | tf_op jit(solution)/shard_map/ppermute | solution.py:94
  74.2 7.6 %collective-permute-start.17 = (f32[128,128]{1,0:T(8,128)S(1)}, f32[128,128]{1,0:T(8,128)S(1)}, u32[]{:S(2)}, u32[]{:S(2)}) collective-permute-start(f32[128,128]{1,0:T(8,128)S(1)} %add.292), channel_id=1, source_target_pairs={{0,4},{1,5},{2,6},{3,7},{4,0},{5,1},{6,2},{7,3},{8,12},{9,13},{10,... | collective-permute-start | bytes 196616 | tf_op jit(solution)/shard_map/ppermute | solution.py:94
  81.8 6.5 %collective-permute-start.18 = (f32[128,128]{1,0:T(8,128)S(1)}, f32[128,128]{1,0:T(8,128)S(1)}, u32[]{:S(2)}, u32[]{:S(2)}) collective-permute-start(f32[128,128]{1,0:T(8,128)S(1)} %add.293), channel_id=1, source_target_pairs={{0,8},{1,9},{2,10},{3,11},{4,12},{5,13},{6,14},{7,15},{8,0},{9,1},... | collective-permute-start | bytes 196616 | tf_op jit(solution)/shard_map/ppermute | solution.py:94
  88.3 5.4 %slice-start = ((s8[11010048]{0:T(1024)(128)(4,1)}), s8[4194304]{0:T(1024)(128)(4,1)S(1)}, s32[]{:S(2)}) async-start(s8[11010048]{0:T(1024)(128)(4,1)} %bitcast.30), calls=%async_computation | async-start | bytes 8388608
  88.4 5.3 %slice-start.1 = ((s8[11010048]{0:T(1024)(128)(4,1)}), s8[4194304]{0:T(1024)(128)(4,1)S(1)}, s32[]{:S(2)}) async-start(s8[11010048]{0:T(1024)(128)(4,1)} %bitcast.30), calls=%async_computation.1 | async-start | bytes 8388608
  88.4 5.8 %slice-start.2 = ((s8[11010048]{0:T(1024)(128)(4,1)}), s8[2621440]{0:T(1024)(128)(4,1)S(1)}, s32[]{:S(2)}) async-start(s8[11010048]{0:T(1024)(128)(4,1)} %bitcast.30), calls=%async_computation.2 | async-start | bytes 5242880
  88.4 5.9 %copy-start.1 = (bf16[256,1792]{1,0:T(8,128)(2,1)S(1)}, bf16[256,1792]{1,0:T(8,128)(2,1)}, u32[]{:S(2)}) copy-start(bf16[256,1792]{1,0:T(8,128)(2,1)} %dhidden.1) | copy-start | bytes 2752516
  88.4 5.2 %collective-permute-start.19 = (bf16[128,128]{1,0:T(8,128)(2,1)S(1)}, bf16[128,128]{1,0:T(8,128)(2,1)S(1)}, u32[]{:S(2)}, u32[]{:S(2)}) collective-permute-start(bf16[128,128]{1,0:T(8,128)(2,1)S(1)} %fusion.2), channel_id=1, source_target_pairs={{0,1},{1,0},{2,3},{3,2},{4,5},{5,4},{6,7},{7,6},{8,9},{9,8},{10,11... | collective-permute-start | bytes 98312 | tf_op jit(solution)/shard_map/ppermute | solution.py:67
  101.9 1.4 collective-permute-start.20
  103.3 4.6 %collective-permute-start.21 = (f32[128,128]{1,0:T(8,128)S(1)}, f32[128,128]{1,0:T(8,128)S(1)}, u32[]{:S(2)}, u32[]{:S(2)}) collective-permute-start(f32[128,128]{1,0:T(8,128)S(1)} %slice_add_fusion), channel_id=1, source_target_pairs={{0,2},{1,3},{2,0},{3,1},{4,6},{5,7},{6,4},{7,5},{8,10},{9,11},{10,... | collective-permute-start | bytes 196616 | tf_op jit(solution)/shard_map/ppermute | solution.py:94
  107.9 4.3 %collective-permute-start.22 = (f32[128,128]{1,0:T(8,128)S(1)}, f32[128,128]{1,0:T(8,128)S(1)}, u32[]{:S(2)}, u32[]{:S(2)}) collective-permute-start(f32[128,128]{1,0:T(8,128)S(1)} %add.303), channel_id=1, source_target_pairs={{0,4},{1,5},{2,6},{3,7},{4,0},{5,1},{6,2},{7,3},{8,12},{9,13},{10,... | collective-permute-start | bytes 196616 | tf_op jit(solution)/shard_map/ppermute | solution.py:94
  112.3 28.2 %collective-permute-start.23 = (f32[128,128]{1,0:T(8,128)S(1)}, f32[128,128]{1,0:T(8,128)S(1)}, u32[]{:S(2)}, u32[]{:S(2)}) collective-permute-start(f32[128,128]{1,0:T(8,128)S(1)} %add.304), channel_id=1, source_target_pairs={{0,8},{1,9},{2,10},{3,11},{4,12},{5,13},{6,14},{7,15},{8,0},{9,1},... | collective-permute-start | bytes 196616 | tf_op jit(solution)/shard_map/ppermute | solution.py:94
  140.6 1.3 collective-permute-start.24
  141.9 3.5 %collective-permute-start.25 = (bf16[128,5120]{1,0:T(8,128)(2,1)S(1)}, bf16[128,5120]{1,0:T(8,128)(2,1)S(1)}, u32[]{:S(2)}, u32[]{:S(2)}) collective-permute-start(bf16[128,5120]{1,0:T(8,128)(2,1)S(1)} %get-tuple-element.52), channel_id=1, source_target_pairs={{0,1},{1,0},{2,3},{3,2},{4,5},{5,4},{6,7},{7,6},{8,9},{9,8},{10,11... | collective-permute-start | bytes 3932168 | tf_op jit(solution)/shard_map/ppermute | solution.py:67
  143.4 1.9 collective-permute-start.26
  148.4 17.9 %collective-permute-start.27 = (bf16[64,5120]{1,0:T(8,128)(2,1)}, bf16[64,5120]{1,0:T(8,128)(2,1)}, u32[]{:S(2)}, u32[]{:S(2)}) collective-permute-start(bf16[64,5120]{1,0:T(8,128)(2,1)} %get-tuple-element.56), channel_id=1, source_target_pairs={{0,2},{1,3},{2,0},{3,1},{4,6},{5,7},{6,4},{7,5},{8,10},{9,11},{10,... | collective-permute-start | bytes 1966088 | tf_op jit(solution)/shard_map/ppermute | solution.py:67
  166.3 8.1 %copy-start.3 = (bf16[256,512]{1,0:T(8,128)(2,1)S(1)}, bf16[256,512]{1,0:T(8,128)(2,1)}, u32[]{:S(2)}) copy-start(bf16[256,512]{1,0:T(8,128)(2,1)} %copy-done.2) | copy-start | bytes 786436
  166.3 2.4 %collective-permute-start.29 = (bf16[128,3072]{1,0:T(8,128)(2,1)S(1)}, bf16[128,3072]{1,0:T(8,128)(2,1)S(1)}, u32[]{:S(2)}, u32[]{:S(2)}) collective-permute-start(bf16[128,3072]{1,0:T(8,128)(2,1)S(1)} %get-tuple-element.60), channel_id=1, source_target_pairs={{0,1},{1,0},{2,3},{3,2},{4,5},{5,4},{6,7},{7,6},{8,9},{9,8},{10,11... | collective-permute-start | bytes 2359304 | tf_op jit(solution)/shard_map/ppermute | solution.py:67
  169.9 11.2 %collective-permute-start.30 = (bf16[64,3072]{1,0:T(8,128)(2,1)S(1)}, bf16[64,3072]{1,0:T(8,128)(2,1)S(1)}, u32[]{:S(2)}, u32[]{:S(2)}) collective-permute-start(bf16[64,3072]{1,0:T(8,128)(2,1)S(1)} %get-tuple-element.61), channel_id=1, source_target_pairs={{0,2},{1,3},{2,0},{3,1},{4,6},{5,7},{6,4},{7,5},{8,10},{9,11},{10,... | collective-permute-start | bytes 1179656 | tf_op jit(solution)/shard_map/ppermute | solution.py:67
  170.9 17.9 %collective-permute-start.32 = (bf16[16,5120]{1,0:T(8,128)(2,1)S(1)}, bf16[16,5120]{1,0:T(8,128)(2,1)S(1)}, u32[]{:S(2)}, u32[]{:S(2)}) collective-permute-start(bf16[16,5120]{1,0:T(8,128)(2,1)S(1)} %get-tuple-element.73), channel_id=1, source_target_pairs={{0,12},{1,13},{2,14},{3,15},{4,0},{5,1},{6,2},{7,3},{8,4},{9,5},{1... | collective-permute-start | bytes 491528 | tf_op jit(solution)/shard_map/ppermute | solution.py:67
  173.2 18.3 %collective-permute-start.31 = (bf16[16,5120]{1,0:T(8,128)(2,1)S(1)}, bf16[16,5120]{1,0:T(8,128)(2,1)S(1)}, u32[]{:S(2)}, u32[]{:S(2)}) collective-permute-start(bf16[16,5120]{1,0:T(8,128)(2,1)S(1)} %get-tuple-element.74), channel_id=1, source_target_pairs={{0,8},{1,9},{2,10},{3,11},{4,12},{5,13},{6,14},{7,15},{8,0},{9,1},... | collective-permute-start | bytes 491528 | tf_op jit(solution)/shard_map/ppermute | solution.py:67
  173.8 17.7 %collective-permute-start.28 = (bf16[16,5120]{1,0:T(8,128)(2,1)S(1)}, bf16[16,5120]{1,0:T(8,128)(2,1)S(1)}, u32[]{:S(2)}, u32[]{:S(2)}) collective-permute-start(bf16[16,5120]{1,0:T(8,128)(2,1)S(1)} %get-tuple-element.72), channel_id=1, source_target_pairs={{0,4},{1,5},{2,6},{3,7},{4,8},{5,9},{6,10},{7,11},{8,12},{9,13},{1... | collective-permute-start | bytes 491528 | tf_op jit(solution)/shard_map/ppermute | solution.py:67
  181.2 10.4 %collective-permute-start.35 = (bf16[16,3072]{1,0:T(8,128)(2,1)S(1)}, bf16[16,3072]{1,0:T(8,128)(2,1)S(1)}, u32[]{:S(2)}, u32[]{:S(2)}) collective-permute-start(bf16[16,3072]{1,0:T(8,128)(2,1)S(1)} %get-tuple-element.78), channel_id=1, source_target_pairs={{0,12},{1,13},{2,14},{3,15},{4,0},{5,1},{6,2},{7,3},{8,4},{9,5},{1... | collective-permute-start | bytes 294920 | tf_op jit(solution)/shard_map/ppermute | solution.py:67
  183.6 13.1 %collective-permute-start.34 = (bf16[16,3072]{1,0:T(8,128)(2,1)S(1)}, bf16[16,3072]{1,0:T(8,128)(2,1)S(1)}, u32[]{:S(2)}, u32[]{:S(2)}) collective-permute-start(bf16[16,3072]{1,0:T(8,128)(2,1)S(1)} %get-tuple-element.79), channel_id=1, source_target_pairs={{0,8},{1,9},{2,10},{3,11},{4,12},{5,13},{6,14},{7,15},{8,0},{9,1},... | collective-permute-start | bytes 294920 | tf_op jit(solution)/shard_map/ppermute | solution.py:67
  188.8 7.9 %collective-permute-start.33 = (bf16[16,3072]{1,0:T(8,128)(2,1)S(1)}, bf16[16,3072]{1,0:T(8,128)(2,1)S(1)}, u32[]{:S(2)}, u32[]{:S(2)}) collective-permute-start(bf16[16,3072]{1,0:T(8,128)(2,1)S(1)} %get-tuple-element.77), channel_id=1, source_target_pairs={{0,4},{1,5},{2,6},{3,7},{4,8},{5,9},{6,10},{7,11},{8,12},{9,13},{1... | collective-permute-start | bytes 294920 | tf_op jit(solution)/shard_map/ppermute | solution.py:67

commit v8 on v7

--- a/solution.py
+++ b/solution.py
@@ -9,7 +9,7 @@
 
 OUTER_SHARES = (3, 5)
 INNER_CUTS = (1, 2)
-SUM_SHARES = (5, 3)
+SUM_SHARES = (4, 4)
 MIB = 1024 * 1024
 BF16 = jnp.bfloat16
 DEPTH = 3
@@ -123,7 +123,9 @@
         for copy in fetch(k + DEPTH - 1, (k + DEPTH - 1) % DEPTH):
             copy.start()
 
-    return k % DEPTH, fetch(k, k % DEPTH)
+    for copy in fetch(k, k % DEPTH):
+        copy.wait()
+    return k % DEPTH
 
 
 def send(copy_of, k, count, fill):
@@ -145,28 +147,21 @@
     out, held, arrived = rest[-3:]
     step, tile = held.shape[2:]
 
-    depth = step // 2
-
     def fetch(n, slot):
         return [
             pltpu.make_async_copy(
-                tile_at(frozen.at[i, pl.ds(first + h * depth, depth)], low + n, tile),
-                held.at[slot, i, pl.ds(h * depth, depth)],
-                arrived.at[slot, i, h],
+                tile_at(frozen.at[i, pl.ds(first, step)], low + n, tile),
+                held.at[slot, i],
+                arrived.at[slot, i],
             )
             for i in range(2)
-            for h in range(2)
         ]
 
-    slot, copies = ring(fetch, pl.program_id(0), count)
+    slot = ring(fetch, pl.program_id(0), count)
     x = jnp.concatenate([v[...] for v in parts], axis=0)
     for i in range(2):
-        part = 0.0 if len(rest) == 3 else rest[0][i]
-        for h in range(2):
-            rows = slice(h * depth, (h + 1) * depth)
-            copies[2 * i + h].wait()
-            part = part + dot(x[:, rows], held[slot, i, rows])
-        out[i] = part
+        part = dot(x, held[slot, i])
+        out[i] = part if len(rest) == 3 else rest[0][i] + part
 
 
 def forward_chunk(pieces, frozen, start, first, tiles):
@@ -191,7 +186,7 @@
         out_shape=jax.ShapeDtypeStruct((2, tokens, hidden), F32),
         scratch_shapes=[
             pltpu.VMEM((DEPTH, 2, step, tile), BF16),
-            pltpu.SemaphoreType.DMA((DEPTH, 2, 2)),
+            pltpu.SemaphoreType.DMA((DEPTH, 2)),
         ],
         input_output_aliases={} if start is None else {len(operands) - 1: 0},
         compiler_params=params(24),
@@ -503,29 +498,17 @@
     half = near.shape[0]
     block = held.shape[2]
 
-    part = block // 2
-
     def fetch(k, slot):
-        at = pl.multiple_of(first + k * block, block)
+        rows = pl.ds(pl.multiple_of(first + k * block, block), block)
         return [
-            pltpu.make_async_copy(
-                frozen.at[i, pl.ds(at + h * part, part)],
-                held.at[slot, i, pl.ds(h * part, part)],
-                arrived.at[slot, i, h],
-            )
-            for h in range(2)
+            pltpu.make_async_copy(frozen.at[i, rows, :], held.at[slot, i], arrived.at[slot, i])
             for i in range(2)
         ]
 
-    slot, copies = ring(fetch, pl.program_id(0), count)
-    for h in range(2):
-        rows = slice(h * part, (h + 1) * part)
-        copies[2 * h].wait()
-        term = dot(dgate[...], held[slot, 0, rows], ((1,), (1,)))
-        copies[2 * h + 1].wait()
-        term = term + dot(dup[...], held[slot, 1, rows], ((1,), (1,)))
-        near[:, rows] = term[:half].astype(BF16)
-        far[:, rows] = term[half:].astype(BF16)
+    slot = ring(fetch, pl.program_id(0), count)
+    term = dot(dgate[...], held[slot, 0], ((1,), (1,))) + dot(dup[...], held[slot, 1], ((1,), (1,)))
+    near[...] = term[:half].astype(BF16)
+    far[...] = term[half:].astype(BF16)
 
 
 def backward_chunk(frozen, dgate, dup, first, step):
@@ -542,7 +525,7 @@
         out_shape=[jax.ShapeDtypeStruct((tokens // 2, step), BF16)] * 2,
         scratch_shapes=[
             pltpu.VMEM((DEPTH, 2, block, hidden), BF16),
-            pltpu.SemaphoreType.DMA((DEPTH, 2, 2)),
+            pltpu.SemaphoreType.DMA((DEPTH, 2)),
         ],
         compiler_params=params(20),
         cost_estimate=cost(4 * tokens * step * hidden, 4 * step * hidden),
@@ -676,7 +659,7 @@
         near[1:] = lax.optimization_barrier((*near[1:], base if q else outer[-1]))[:-1]
         far = [torus.move(v, 2, -1) for v in near]
         gathered.append([*near, *far])
-        for cut in parts_of(tiles, 4 if q == len(parts) - 1 else 1):
+        for cut in parts_of(tiles, 2 if q == len(parts) - 1 else 1):
             base = forward_chunk(gathered[q], frozen, base, first, cut)
         first += x.shape[1]
 
@@ -730,7 +713,7 @@
             total = total + v.astype(F32)
         inners.append(total.astype(BF16).reshape(a, rows, step))
         outer_moves.append([torus.move(inners[q][k], 0, k) for k in range(1, a)])
-    grad_b = grad_b_part(inner_moves[-1][0])
+    grad_b = grad_b_part(sums[-1][0])
     for q, inner in enumerate(inners):
         total = inner[0].astype(F32)
         for v in outer_moves[q]:

time: 198 us -> 173 us (0.87)
  Pallas kernels: 123 us -> 84 us
  waiting for transfers between devices: 27.7 us -> 40 us
  local copies, waits for them, and re-layouts: 3.57 us -> 7.17 us
    pallas_call x6 -> x4, Pallas kernels: 48.9 us -> 28.9 us  [forward_chunk(): pl.pallas_call(functools.partial(forward_kernel, len(pieces), low, count,...]
    pallas_call x2, Pallas kernels: 43.2 us -> 23.7 us  [backward_chunk(): pl.pallas_call(functools.partial(backward_kernel, count, first), grid=(co...]
    ppermute x6, waiting for transfers between devices: 0.79 us -> 7.38 us  [exchange_sum(): x = x + lax.ppermute(x, 'tensor', pairs)]
    ppermute x30, waiting for transfers between devices: 26.9 us -> 32.6 us  [move(): return lax.ppermute(x, 'tensor', pairs)]
    unnamed x18 -> x26, local copies, waits for them, and re-layouts: 0.72 us -> 4.32 us
  transfers between devices with their start and end apart: 36 -> 36, of which waited for: 15 -> 18; matrix products, arithmetic and copies ran while one was open for 3% -> 3% of each run, Pallas kernels for 56% -> 41%
where the time goes in v8:
time: 173 us
  Pallas kernels  84 us (49%)
  waiting for transfers between devices  40 us (23%)
  starting transfers between devices  35.9 us (21%)
  local copies, waits for them, and re-layouts  7.17 us (4%)
  other arithmetic  4.71 us (3%)
    ppermute x30, waiting for transfers between devices, move(): return lax.ppermute(x, 'tensor', pairs)  32.6 us
    ppermute x30, starting transfers between devices, move(): return lax.ppermute(x, 'tensor', pairs)  29.2 us
    pallas_call x4, Pallas kernels, forward_chunk(): pl.pallas_call(functools.partial(forward_kernel, len(pieces), low, count,...  28.9 us
    pallas_call x2, Pallas kernels, backward_chunk(): pl.pallas_call(functools.partial(backward_kernel, count, first), grid=(co...  23.7 us
    pallas_call x3, Pallas kernels, grad_b_of(): pl.pallas_call(functools.partial(grad_b_kernel, first, last - first), gri...  11.9 us
    pallas_call x1, Pallas kernels, middle(): pl.pallas_call(functools.partial(middle_kernel, rows), grid_spec=pltpu.Pr...  7.58 us
    ppermute x6, waiting for transfers between devices, exchange_sum(): x = x + lax.ppermute(x, 'tensor', pairs)  7.38 us
    ppermute x6, starting transfers between devices, exchange_sum(): x = x + lax.ppermute(x, 'tensor', pairs)  6.68 us
  transfers between devices with their start and end apart: 36, of which 18 were waited for; matrix products, arithmetic and copies ran while one was open for 3% of the time, Pallas kernels for 41%

profile of v8, /device:TPU:0, one launch (start us, length us, event | category | flops | bytes accessed | tf_op | source)
XLA Modules:
  0.0 173.0 jit_solution(6039731819322701868)
XLA Ops:
  1.5 4.1 %collective-permute-start.1 = (bf16[16,3072]{1,0:T(8,128)(2,1)S(1)}, bf16[16,3072]{1,0:T(8,128)(2,1)S(1)}, u32[]{:S(2)}, u32[]{:S(2)}) collective-permute-start(bf16[16,3072]{1,0:T(8,128)(2,1)S(1)} %get-tuple-element.81), channel_id=1, source_target_pairs={{0,8},{1,9},{2,10},{3,11},{4,12},{5,13},{6,14},{7,15},{8,0},{9,1},... | collective-permute-start | bytes 294920 | tf_op jit(solution)/shard_map/ppermute | solution.py:67
  5.6 1.3 collective-permute-start
  10.2 1.8 %collective-permute-done.1 = bf16[16,3072]{1,0:T(8,128)(2,1)S(1)} collective-permute-done((bf16[16,3072]{1,0:T(8,128)(2,1)S(1)}, bf16[16,3072]{1,0:T(8,128)(2,1)S(1)}, u32[]{:S(2)}, u32[]{:S(2)}) %collective-permute-start.1) | collective-permute-done | bytes 98336 | tf_op jit(solution)/shard_map/ppermute | solution.py:67
  12.0 1.8 %collective-permute-done.2 = bf16[16,3072]{1,0:T(8,128)(2,1)S(1)} collective-permute-done((bf16[16,3072]{1,0:T(8,128)(2,1)S(1)}, bf16[16,3072]{1,0:T(8,128)(2,1)S(1)}, u32[]{:S(2)}, u32[]{:S(2)}) %collective-permute-start.2) | collective-permute-done | bytes 98336 | tf_op jit(solution)/shard_map/ppermute | solution.py:67
  13.9 1.7 collective-permute-start.5
  15.6 2.0 %collective-permute-start.4 = (bf16[16,5120]{1,0:T(8,128)(2,1)S(1)}, bf16[16,5120]{1,0:T(8,128)(2,1)S(1)}, u32[]{:S(2)}, u32[]{:S(2)}) collective-permute-start(bf16[16,5120]{1,0:T(8,128)(2,1)S(1)} %slice.60), channel_id=1, source_target_pairs={{0,8},{1,9},{2,10},{3,11},{4,12},{5,13},{6,14},{7,15},{8,0},{9,1},... | collective-permute-start | bytes 491528 | tf_op jit(solution)/shard_map/ppermute | solution.py:67
  17.6 2.8 %collective-permute-start.3 = (bf16[16,5120]{1,0:T(8,128)(2,1)S(1)}, bf16[16,5120]{1,0:T(8,128)(2,1)S(1)}, u32[]{:S(2)}, u32[]{:S(2)}) collective-permute-start(bf16[16,5120]{1,0:T(8,128)(2,1)S(1)} %slice.60), channel_id=1, source_target_pairs={{0,12},{1,13},{2,14},{3,15},{4,0},{5,1},{6,2},{7,3},{8,4},{9,5},{1... | collective-permute-start | bytes 491528 | tf_op jit(solution)/shard_map/ppermute | solution.py:67
  20.9 1.6 collective-permute-start.8
  22.5 5.6 %collective-permute-done.4 = bf16[16,5120]{1,0:T(8,128)(2,1)S(1)} collective-permute-done((bf16[16,5120]{1,0:T(8,128)(2,1)S(1)}, bf16[16,5120]{1,0:T(8,128)(2,1)S(1)}, u32[]{:S(2)}, u32[]{:S(2)}) %collective-permute-start.4) | collective-permute-done | bytes 163872 | tf_op jit(solution)/shard_map/ppermute | solution.py:67
  28.2 4.3 %collective-permute-done.8.rest_1_.rest_9_ = bf16[64,3072]{1,0:T(8,128)(2,1)S(1)} collective-permute-done((bf16[64,3072]{1,0:T(8,128)(2,1)S(1)}, bf16[64,3072]{1,0:T(8,128)(2,1)S(1)}, u32[]{:S(2)}, u32[]{:S(2)}) %collective-permute-start.8) | collective-permute-done | bytes 393248 | tf_op jit(solution)/shard_map/ppermute | solution.py:67
  33.1 1.5 collective-permute-start.7
  34.6 9.3 %shard_map.103.rest_5_ = f32[2,256,1792]{2,1,0:T(8,128)S(1)} custom-call(bf16[64,3072]{1,0:T(8,128)(2,1)S(1)} %bitcast.34, bf16[64,3072]{1,0:T(8,128)(2,1)S(1)} %collective-permute-done.8.rest_1_.rest_9_, bf16[64,3072]{1,0:T(8,128)(2,1)S(1)} %collective-permute-done.9.rest_2_.rest_10_, bf16[64,3072]{1,0:T(8,128)(2,1)S(1)} %collective-permute-done.10.rest_3_.rest_11_, ...), custom_call_target="tpu_custom_call" | custom-call | flops 5637144576 | bytes 22020096 | tf_op jit(solution)/shard_map/pallas_call | solution.py:181
  44.7 1.1 collective-permute-start.6
  45.8 8.4 %shard_map.104.rest_5_ = f32[2,256,1792]{2,1,0:T(8,128)S(1)} custom-call(bf16[64,2560]{1,0:T(8,128)(2,1)S(1)} %get-tuple-element.72.rest_0_.rest_12_, bf16[64,2560]{1,0:T(8,128)(2,1)S(1)} %collective-permute-done.7.rest_1_.rest_13_, bf16[64,2560]{1,0:T(8,128)(2,1)S(1)} %collective-permute-done.11.rest_2_.rest_14_, ...), custom_call_target="tpu_custom_call", output_to_operand_aliasing={{}: (5, {})} | custom-call | flops 4697620480 | bytes 18350080 | tf_op jit(solution)/shard_map/pallas_call | solution.py:181
  54.6 1.4 collective-permute-done.14.rest_3_.rest_19_
  56.1 1.6 shard_map.107
  57.9 1.0 collective-permute-done.15
  59.0 1.2 collective-permute-start.16
  60.2 3.1 %collective-permute-done.16 = f32[128,128]{1,0:T(8,128)S(1)} collective-permute-done((f32[128,128]{1,0:T(8,128)S(1)}, f32[128,128]{1,0:T(8,128)S(1)}, u32[]{:S(2)}, u32[]{:S(2)}) %collective-permute-start.16) | collective-permute-done | bytes 65568 | tf_op jit(solution)/shard_map/ppermute | solution.py:94
  63.4 4.2 %collective-permute-done.17 = f32[128,128]{1,0:T(8,128)S(1)} collective-permute-done((f32[128,128]{1,0:T(8,128)S(1)}, f32[128,128]{1,0:T(8,128)S(1)}, u32[]{:S(2)}, u32[]{:S(2)}) %collective-permute-start.17) | collective-permute-done | bytes 65568 | tf_op jit(solution)/shard_map/ppermute | solution.py:94
  67.7 1.4 collective-permute-start.18
  69.1 4.6 %shard_map.105.rest_5_ = f32[2,256,1792]{2,1,0:T(8,128)S(1)} custom-call(bf16[64,2560]{1,0:T(8,128)(2,1)S(1)} %get-tuple-element.73.rest_0_.rest_16_, bf16[64,2560]{1,0:T(8,128)(2,1)S(1)} %collective-permute-done.6.rest_1_.rest_17_, bf16[64,2560]{1,0:T(8,128)(2,1)S(1)} %collective-permute-done.13.rest_2_.rest_18_, ...), custom_call_target="tpu_custom_call", output_to_operand_aliasing={{}: (5, {})} | custom-call | flops 2013265920 | bytes 7864320 | tf_op jit(solution)/shard_map/pallas_call | solution.py:181
  73.9 6.6 %shard_map.106.base = f32[2,256,1792]{2,1,0:T(8,128)S(1)} custom-call(bf16[64,2560]{1,0:T(8,128)(2,1)S(1)} %get-tuple-element.73.rest_0_.rest_16_, bf16[64,2560]{1,0:T(8,128)(2,1)S(1)} %collective-permute-done.6.rest_1_.rest_17_, bf16[64,2560]{1,0:T(8,128)(2,1)S(1)} %collective-permute-done.13.rest_2_.rest_18_, ...), custom_call_target="tpu_custom_call", output_to_operand_aliasing={{}: (5, {})} | custom-call | flops 2684354560 | bytes 10485760 | tf_op jit(solution)/shard_map/pallas_call | solution.py:181
  81.3 7.6 %shard_map.108 = (bf16[256,1792]{1,0:T(8,128)(2,1)S(1)}, bf16[256,1792]{1,0:T(8,128)(2,1)S(1)}, f32[256,128]{1,0:T(8,128)S(1)}) custom-call(s32[8]{0:T(128)S(1)} %bitcast.48, s32[16]{0:T(128)S(1)} %get-tuple-element.70.places, f32[2,256,1792]{2,1,0:T(8,128)S(1)} %shard_map.106.base, bf16[256,1792]{1,0:T(8,128)(2,1)S(1)} %copy-done.3, ...), custom_call_target="tpu_custom_call" | custom-call | flops 1879048192 | bytes 10092544 | tf_op jit(solution)/shard_map/pallas_call | solution.py:329
  89.1 1.2 collective-permute-done.20
  90.3 1.2 collective-permute-start.21
  91.5 3.6 %shard_map.109.rest_0_ = f32[24,128,1792]{2,1,0:T(8,128)} custom-call(bf16[256,1792]{1,0:T(8,128)(2,1)S(1)} %get-tuple-element.57.dgate, bf16[256,1792]{1,0:T(8,128)(2,1)S(1)} %get-tuple-element.43.dup, bf16[256,256]{1,0:T(8,128)(2,1)S(1)} %fusion.1.order, bf16[256,128]{1,0:T(8,128)(2,1)S(1)} %bitcast.37, s32[1,256]{1,0:T(1,128)S(1)} %bitcast.42), custom_call_target="tpu_custom_call" | custom-call | flops 805306368 | bytes 6291456 | tf_op jit(solution)/shard_map/pallas_call | solution.py:404
  95.2 2.1 %collective-permute-start.22 = (f32[128,128]{1,0:T(8,128)S(1)}, f32[128,128]{1,0:T(8,128)S(1)}, u32[]{:S(2)}, u32[]{:S(2)}) collective-permute-start(f32[128,128]{1,0:T(8,128)S(1)} %add.303), channel_id=1, source_target_pairs={{0,4},{1,5},{2,6},{3,7},{4,0},{5,1},{6,2},{7,3},{8,12},{9,13},{10,... | collective-permute-start | bytes 196616 | tf_op jit(solution)/shard_map/ppermute | solution.py:94
  97.2 3.6 %shard_map.110.rest_0_ = f32[24,128,1792]{2,1,0:T(8,128)} custom-call(bf16[256,1792]{1,0:T(8,128)(2,1)S(1)} %get-tuple-element.57.dgate, bf16[256,1792]{1,0:T(8,128)(2,1)S(1)} %get-tuple-element.43.dup, bf16[256,256]{1,0:T(8,128)(2,1)S(1)} %fusion.1.order, bf16[256,128]{1,0:T(8,128)(2,1)S(1)} %bitcast.38, ...), custom_call_target="tpu_custom_call", output_to_operand_aliasing={{}: (5, {})} | custom-call | flops 805306368 | bytes 6291456 | tf_op jit(solution)/shard_map/pallas_call | solution.py:404
  101.7 11.5 %shard_map.111 = (bf16[128,4096]{1,0:T(8,128)(2,1)S(1)}, bf16[128,4096]{1,0:T(8,128)(2,1)S(1)}) custom-call(bf16[2,8192,1792]{2,1,0:T(8,128)(2,1)} %frozen.3, bf16[256,1792]{1,0:T(8,128)(2,1)S(1)} %get-tuple-element.57.dgate, bf16[256,1792]{1,0:T(8,128)(2,1)S(1)} %get-tuple-element.43.dup), custom_call_target="tpu_custom_call" | custom-call | flops 7516192768 | bytes 29360128 | tf_op jit(solution)/shard_map/pallas_call | solution.py:520
  113.5 1.1 collective-permute-done.24
  114.8 1.4 shard_map.112
  116.7 1.1 collective-permute-done.26.side_far
  117.8 1.4 shard_map.113
  120.9 12.2 %shard_map.114 = (bf16[128,4096]{1,0:T(8,128)(2,1)S(1)}, bf16[128,4096]{1,0:T(8,128)(2,1)}) custom-call(bf16[2,8192,1792]{2,1,0:T(8,128)(2,1)} %frozen.3, bf16[256,1792]{1,0:T(8,128)(2,1)S(1)} %get-tuple-element.57.dgate, bf16[256,1792]{1,0:T(8,128)(2,1)S(1)} %get-tuple-element.43.dup), custom_call_target="tpu_custom_call" | custom-call | flops 7516192768 | bytes 29360128 | tf_op jit(solution)/shard_map/pallas_call | solution.py:520
  133.1 1.1 collective-permute-done.27
  135.2 1.3 add_convert_fusion.1
  137.2 0.9 copy-done.2
  138.2 3.0 %shard_map.115 = (bf16[64,4096]{1,0:T(8,128)(2,1)S(1)}, bf16[64,4096]{1,0:T(8,128)(2,1)S(1)}) custom-call(s32[2]{0:T(128)S(1)} %pad_add_fusion.at, bf16[128,4096]{1,0:T(8,128)(2,1)S(1)} %get-tuple-element.58.near, bf16[128,4096]{1,0:T(8,128)(2,1)} %collective-permute-done.29.far, f32[128,512]{1,0:T(8,128)S(1)} %get-tuple-element.53.side, ...), custom_call_target="tpu_custom_call" | custom-call | flops 1048576 | bytes 3145728 | tf_op jit(solution)/shard_map/pallas_call | solution.py:562
  141.2 1.0 collective-permute-start.30
  142.2 1.0 collective-permute-start.28
  143.2 2.9 %collective-permute-start.32 = (bf16[16,4096]{1,0:T(8,128)(2,1)S(1)}, bf16[16,4096]{1,0:T(8,128)(2,1)S(1)}, u32[]{:S(2)}, u32[]{:S(2)}) collective-permute-start(bf16[16,4096]{1,0:T(8,128)(2,1)S(1)} %get-tuple-element.75), channel_id=1, source_target_pairs={{0,12},{1,13},{2,14},{3,15},{4,0},{5,1},{6,2},{7,3},{8,4},{9,5},{1... | collective-permute-start | bytes 393224 | tf_op jit(solution)/shard_map/ppermute | solution.py:67
  147.5 4.7 %shard_map.117 = f32[24,512,128]{2,1,0:T(8,128)} custom-call(bf16[256,512]{1,0:T(8,128)(2,1)S(1)} %copy-done.6, bf16[256,256]{1,0:T(8,128)(2,1)S(1)} %fusion.1.order, bf16[256,128]{1,0:T(8,128)(2,1)S(1)} %bitcast.41, s32[256,1]{1,0:T(8,128)S(1)} %copy.23.adapter), custom_call_target="tpu_custom_call" | custom-call | flops 805306368 | bytes 6291456 | tf_op jit(solution)/shard_map/pallas_call | solution.py:448
  152.1 4.6 %shard_map.116 = f32[24,128,1792]{2,1,0:T(8,128)} custom-call(bf16[256,1792]{1,0:T(8,128)(2,1)S(1)} %get-tuple-element.57.dgate, bf16[256,1792]{1,0:T(8,128)(2,1)S(1)} %get-tuple-element.43.dup, bf16[256,256]{1,0:T(8,128)(2,1)S(1)} %fusion.1.order, bf16[256,128]{1,0:T(8,128)(2,1)S(1)} %bitcast.39, ...), custom_call_target="tpu_custom_call", output_to_operand_aliasing={{}: (5, {})} | custom-call | flops 1207959552 | bytes 9437184 | tf_op jit(solution)/shard_map/pallas_call | solution.py:404
  156.8 0.9 collective-permute-done.31
  158.0 3.8 %collective-permute-start.35 = (bf16[16,4096]{1,0:T(8,128)(2,1)S(1)}, bf16[16,4096]{1,0:T(8,128)(2,1)S(1)}, u32[]{:S(2)}, u32[]{:S(2)}) collective-permute-start(bf16[16,4096]{1,0:T(8,128)(2,1)S(1)} %get-tuple-element.78), channel_id=1, source_target_pairs={{0,12},{1,13},{2,14},{3,15},{4,0},{5,1},{6,2},{7,3},{8,4},{9,5},{1... | collective-permute-start | bytes 393224 | tf_op jit(solution)/shard_map/ppermute | solution.py:67
  161.8 4.3 %collective-permute-done.33 = bf16[16,4096]{1,0:T(8,128)(2,1)S(1)} collective-permute-done((bf16[16,4096]{1,0:T(8,128)(2,1)S(1)}, bf16[16,4096]{1,0:T(8,128)(2,1)S(1)}, u32[]{:S(2)}, u32[]{:S(2)}) %collective-permute-start.33) | collective-permute-done | bytes 131104 | tf_op jit(solution)/shard_map/ppermute | solution.py:67
  167.1 5.1 %collective-permute-done.34 = bf16[16,4096]{1,0:T(8,128)(2,1)S(1)} collective-permute-done((bf16[16,4096]{1,0:T(8,128)(2,1)S(1)}, bf16[16,4096]{1,0:T(8,128)(2,1)S(1)}, u32[]{:S(2)}, u32[]{:S(2)}) %collective-permute-start.34) | collective-permute-done | bytes 131104 | tf_op jit(solution)/shard_map/ppermute | solution.py:67
  (124 shorter events, 16.7 us)
Async XLA Ops:
  1.5 10.4 %collective-permute-start.1 = (bf16[16,3072]{1,0:T(8,128)(2,1)S(1)}, bf16[16,3072]{1,0:T(8,128)(2,1)S(1)}, u32[]{:S(2)}, u32[]{:S(2)}) collective-permute-start(bf16[16,3072]{1,0:T(8,128)(2,1)S(1)} %get-tuple-element.81), channel_id=1, source_target_pairs={{0,8},{1,9},{2,10},{3,11},{4,12},{5,13},{6,14},{7,15},{8,0},{9,1},... | collective-permute-start | bytes 294920 | tf_op jit(solution)/shard_map/ppermute | solution.py:67
  5.6 6.3 %collective-permute-start = (bf16[16,3072]{1,0:T(8,128)(2,1)S(1)}, bf16[16,3072]{1,0:T(8,128)(2,1)S(1)}, u32[]{:S(2)}, u32[]{:S(2)}) collective-permute-start(bf16[16,3072]{1,0:T(8,128)(2,1)S(1)} %get-tuple-element.81), channel_id=1, source_target_pairs={{0,12},{1,13},{2,14},{3,15},{4,0},{5,1},{6,2},{7,3},{8,4},{9,5},{1... | collective-permute-start | bytes 294920 | tf_op jit(solution)/shard_map/ppermute | solution.py:67
  7.0 6.8 %collective-permute-start.2 = (bf16[16,3072]{1,0:T(8,128)(2,1)S(1)}, bf16[16,3072]{1,0:T(8,128)(2,1)S(1)}, u32[]{:S(2)}, u32[]{:S(2)}) collective-permute-start(bf16[16,3072]{1,0:T(8,128)(2,1)S(1)} %get-tuple-element.81), channel_id=1, source_target_pairs={{0,4},{1,5},{2,6},{3,7},{4,8},{5,9},{6,10},{7,11},{8,12},{9,13},{1... | collective-permute-start | bytes 294920 | tf_op jit(solution)/shard_map/ppermute | solution.py:67
  13.9 8.6 %collective-permute-start.5 = (bf16[16,5120]{1,0:T(8,128)(2,1)S(1)}, bf16[16,5120]{1,0:T(8,128)(2,1)S(1)}, u32[]{:S(2)}, u32[]{:S(2)}) collective-permute-start(bf16[16,5120]{1,0:T(8,128)(2,1)S(1)} %slice.60), channel_id=1, source_target_pairs={{0,4},{1,5},{2,6},{3,7},{4,8},{5,9},{6,10},{7,11},{8,12},{9,13},{1... | collective-permute-start | bytes 491528 | tf_op jit(solution)/shard_map/ppermute | solution.py:67
  15.6 12.5 %collective-permute-start.4 = (bf16[16,5120]{1,0:T(8,128)(2,1)S(1)}, bf16[16,5120]{1,0:T(8,128)(2,1)S(1)}, u32[]{:S(2)}, u32[]{:S(2)}) collective-permute-start(bf16[16,5120]{1,0:T(8,128)(2,1)S(1)} %slice.60), channel_id=1, source_target_pairs={{0,8},{1,9},{2,10},{3,11},{4,12},{5,13},{6,14},{7,15},{8,0},{9,1},... | collective-permute-start | bytes 491528 | tf_op jit(solution)/shard_map/ppermute | solution.py:67
  17.6 10.5 %collective-permute-start.3 = (bf16[16,5120]{1,0:T(8,128)(2,1)S(1)}, bf16[16,5120]{1,0:T(8,128)(2,1)S(1)}, u32[]{:S(2)}, u32[]{:S(2)}) collective-permute-start(bf16[16,5120]{1,0:T(8,128)(2,1)S(1)} %slice.60), channel_id=1, source_target_pairs={{0,12},{1,13},{2,14},{3,15},{4,0},{5,1},{6,2},{7,3},{8,4},{9,5},{1... | collective-permute-start | bytes 491528 | tf_op jit(solution)/shard_map/ppermute | solution.py:67
  20.9 13.7 %collective-permute-start.9 = (bf16[64,3072]{1,0:T(8,128)(2,1)S(1)}, bf16[64,3072]{1,0:T(8,128)(2,1)S(1)}, u32[]{:S(2)}, u32[]{:S(2)}) collective-permute-start(bf16[64,3072]{1,0:T(8,128)(2,1)S(1)} %bitcast.32), channel_id=1, source_target_pairs={{0,1},{1,0},{2,3},{3,2},{4,5},{5,4},{6,7},{7,6},{8,9},{9,8},{10,11... | collective-permute-start | bytes 1179656 | tf_op jit(solution)/shard_map/ppermute | solution.py:67
  20.9 11.5 %collective-permute-start.8 = (bf16[64,3072]{1,0:T(8,128)(2,1)S(1)}, bf16[64,3072]{1,0:T(8,128)(2,1)S(1)}, u32[]{:S(2)}, u32[]{:S(2)}) collective-permute-start(bf16[64,3072]{1,0:T(8,128)(2,1)S(1)} %bitcast.33), channel_id=1, source_target_pairs={{0,2},{1,3},{2,0},{3,1},{4,6},{5,7},{6,4},{7,5},{8,10},{9,11},{10,... | collective-permute-start | bytes 1179656 | tf_op jit(solution)/shard_map/ppermute | solution.py:67
  32.5 2.2 %collective-permute-start.10 = (bf16[64,3072]{1,0:T(8,128)(2,1)S(1)}, bf16[64,3072]{1,0:T(8,128)(2,1)S(1)}, u32[]{:S(2)}, u32[]{:S(2)}) collective-permute-start(bf16[64,3072]{1,0:T(8,128)(2,1)S(1)} %collective-permute-done.8.rest_1_.rest_9_), channel_id=1, source_target_pairs={{0,1},{1,0},{2,3},{3,2},{4,5},{5,4},{6,7},{7,6},{8,9},{9,8},{10,11... | collective-permute-start | bytes 1179656 | tf_op jit(solution)/shard_map/ppermute | solution.py:67
  32.5 11.5 %copy-start.7 = (s32[1,8]{1,0:T(1,128)S(1)}, s32[1,8]{1,0:T(1,128)}, u32[]{:S(2)}) copy-start(s32[1,8]{1,0:T(1,128)} %param.13) | copy-start | bytes 100
  32.5 13.3 %collective-permute-start.11 = (bf16[64,2560]{1,0:T(8,128)(2,1)S(1)}, bf16[64,2560]{1,0:T(8,128)(2,1)S(1)}, u32[]{:S(2)}, u32[]{:S(2)}) collective-permute-start(bf16[64,2560]{1,0:T(8,128)(2,1)S(1)} %get-tuple-element.72.rest_0_.rest_12_), channel_id=1, source_target_pairs={{0,1},{1,0},{2,3},{3,2},{4,5},{5,4},{6,7},{7,6},{8,9},{9,8},{10,11... | collective-permute-start | bytes 983048 | tf_op jit(solution)/shard_map/ppermute | solution.py:67
  33.1 10.8 %collective-permute-start.7 = (bf16[64,2560]{1,0:T(8,128)(2,1)S(1)}, bf16[64,2560]{1,0:T(8,128)(2,1)S(1)}, u32[]{:S(2)}, u32[]{:S(2)}) collective-permute-start(bf16[64,2560]{1,0:T(8,128)(2,1)S(1)} %get-tuple-element.72.rest_0_.rest_12_), channel_id=1, source_target_pairs={{0,2},{1,3},{2,0},{3,1},{4,6},{5,7},{6,4},{7,5},{8,10},{9,11},{10,... | collective-permute-start | bytes 983048 | tf_op jit(solution)/shard_map/ppermute | solution.py:67
  43.9 1.9 %collective-permute-start.12 = (bf16[64,2560]{1,0:T(8,128)(2,1)S(1)}, bf16[64,2560]{1,0:T(8,128)(2,1)S(1)}, u32[]{:S(2)}, u32[]{:S(2)}) collective-permute-start(bf16[64,2560]{1,0:T(8,128)(2,1)S(1)} %collective-permute-done.7.rest_1_.rest_13_), channel_id=1, source_target_pairs={{0,1},{1,0},{2,3},{3,2},{4,5},{5,4},{6,7},{7,6},{8,9},{9,8},{10,11... | collective-permute-start | bytes 983048 | tf_op jit(solution)/shard_map/ppermute | solution.py:67
  44.2 11.9 %copy-start = (bf16[24,512,128]{2,1,0:T(8,128)(2,1)S(1)}, bf16[24,512,128]{2,1,0:T(8,128)(2,1)}, u32[]{:S(2)}) copy-start(bf16[24,512,128]{2,1,0:T(8,128)(2,1)} %rest_7_.3) | copy-start | bytes 9437188
  44.2 10.4 %collective-permute-start.13 = (bf16[64,2560]{1,0:T(8,128)(2,1)S(1)}, bf16[64,2560]{1,0:T(8,128)(2,1)S(1)}, u32[]{:S(2)}, u32[]{:S(2)}) collective-permute-start(bf16[64,2560]{1,0:T(8,128)(2,1)S(1)} %get-tuple-element.73.rest_0_.rest_16_), channel_id=1, source_target_pairs={{0,1},{1,0},{2,3},{3,2},{4,5},{5,4},{6,7},{7,6},{8,9},{9,8},{10,11... | collective-permute-start | bytes 983048 | tf_op jit(solution)/shard_map/ppermute | solution.py:67
  44.7 9.7 %collective-permute-start.6 = (bf16[64,2560]{1,0:T(8,128)(2,1)S(1)}, bf16[64,2560]{1,0:T(8,128)(2,1)S(1)}, u32[]{:S(2)}, u32[]{:S(2)}) collective-permute-start(bf16[64,2560]{1,0:T(8,128)(2,1)S(1)} %get-tuple-element.73.rest_0_.rest_16_), channel_id=1, source_target_pairs={{0,2},{1,3},{2,0},{3,1},{4,6},{5,7},{6,4},{7,5},{8,10},{9,11},{10,... | collective-permute-start | bytes 983048 | tf_op jit(solution)/shard_map/ppermute | solution.py:67
  54.4 1.6 collective-permute-start.14
  56.1 1.8 %copy-start.9 = (s32[24]{0:T(128)S(1)}, s32[24]{0:T(128)}, u32[]{:S(2)}) copy-start(s32[24]{0:T(128)} %param.15) | copy-start | bytes 292
  57.6 10.0 %copy-start.5 = (bf16[256,512]{1,0:T(8,128)(2,1)}, bf16[256,512]{1,0:T(8,128)(2,1)S(1)}, u32[]{:S(2)}) copy-start(bf16[256,512]{1,0:T(8,128)(2,1)S(1)} %get-tuple-element.67.columns) | copy-start | bytes 786436
  57.7 1.3 collective-permute-start.15
  59.0 4.3 %collective-permute-start.16 = (f32[128,128]{1,0:T(8,128)S(1)}, f32[128,128]{1,0:T(8,128)S(1)}, u32[]{:S(2)}, u32[]{:S(2)}) collective-permute-start(f32[128,128]{1,0:T(8,128)S(1)} %slice_add_fusion.1), channel_id=1, source_target_pairs={{0,2},{1,3},{2,0},{3,1},{4,6},{5,7},{6,4},{7,5},{8,10},{9,11},{10,... | collective-permute-start | bytes 196616 | tf_op jit(solution)/shard_map/ppermute | solution.py:94
  63.3 4.3 %collective-permute-start.17 = (f32[128,128]{1,0:T(8,128)S(1)}, f32[128,128]{1,0:T(8,128)S(1)}, u32[]{:S(2)}, u32[]{:S(2)}) collective-permute-start(f32[128,128]{1,0:T(8,128)S(1)} %add.292), channel_id=1, source_target_pairs={{0,4},{1,5},{2,6},{3,7},{4,0},{5,1},{6,2},{7,3},{8,12},{9,13},{10,... | collective-permute-start | bytes 196616 | tf_op jit(solution)/shard_map/ppermute | solution.py:94
  67.7 6.0 %collective-permute-start.18 = (f32[128,128]{1,0:T(8,128)S(1)}, f32[128,128]{1,0:T(8,128)S(1)}, u32[]{:S(2)}, u32[]{:S(2)}) collective-permute-start(f32[128,128]{1,0:T(8,128)S(1)} %add.293), channel_id=1, source_target_pairs={{0,8},{1,9},{2,10},{3,11},{4,12},{5,13},{6,14},{7,15},{8,0},{9,1},... | collective-permute-start | bytes 196616 | tf_op jit(solution)/shard_map/ppermute | solution.py:94
  73.7 6.8 %slice-start = ((s8[11010048]{0:T(1024)(128)(4,1)}), s8[4194304]{0:T(1024)(128)(4,1)S(1)}, s32[]{:S(2)}) async-start(s8[11010048]{0:T(1024)(128)(4,1)} %bitcast.30), calls=%async_computation | async-start | bytes 8388608
  73.8 6.7 %slice-start.1 = ((s8[11010048]{0:T(1024)(128)(4,1)}), s8[4194304]{0:T(1024)(128)(4,1)S(1)}, s32[]{:S(2)}) async-start(s8[11010048]{0:T(1024)(128)(4,1)} %bitcast.30), calls=%async_computation.1 | async-start | bytes 8388608
  73.8 7.3 %slice-start.2 = ((s8[11010048]{0:T(1024)(128)(4,1)}), s8[2621440]{0:T(1024)(128)(4,1)S(1)}, s32[]{:S(2)}) async-start(s8[11010048]{0:T(1024)(128)(4,1)} %bitcast.30), calls=%async_computation.2 | async-start | bytes 5242880
  73.8 7.5 %copy-start.3 = (bf16[256,1792]{1,0:T(8,128)(2,1)S(1)}, bf16[256,1792]{1,0:T(8,128)(2,1)}, u32[]{:S(2)}) copy-start(bf16[256,1792]{1,0:T(8,128)(2,1)} %dhidden.1) | copy-start | bytes 2752516
  73.8 6.7 %collective-permute-start.19 = (bf16[128,128]{1,0:T(8,128)(2,1)S(1)}, bf16[128,128]{1,0:T(8,128)(2,1)S(1)}, u32[]{:S(2)}, u32[]{:S(2)}) collective-permute-start(bf16[128,128]{1,0:T(8,128)(2,1)S(1)} %fusion.2), channel_id=1, source_target_pairs={{0,1},{1,0},{2,3},{3,2},{4,5},{5,4},{6,7},{7,6},{8,9},{9,8},{10,11... | collective-permute-start | bytes 98312 | tf_op jit(solution)/shard_map/ppermute | solution.py:67
  88.9 1.3 collective-permute-start.20
  90.3 4.9 %collective-permute-start.21 = (f32[128,128]{1,0:T(8,128)S(1)}, f32[128,128]{1,0:T(8,128)S(1)}, u32[]{:S(2)}, u32[]{:S(2)}) collective-permute-start(f32[128,128]{1,0:T(8,128)S(1)} %slice_add_fusion), channel_id=1, source_target_pairs={{0,2},{1,3},{2,0},{3,1},{4,6},{5,7},{6,4},{7,5},{8,10},{9,11},{10,... | collective-permute-start | bytes 196616 | tf_op jit(solution)/shard_map/ppermute | solution.py:94
  95.2 5.7 %collective-permute-start.22 = (f32[128,128]{1,0:T(8,128)S(1)}, f32[128,128]{1,0:T(8,128)S(1)}, u32[]{:S(2)}, u32[]{:S(2)}) collective-permute-start(f32[128,128]{1,0:T(8,128)S(1)} %add.303), channel_id=1, source_target_pairs={{0,4},{1,5},{2,6},{3,7},{4,0},{5,1},{6,2},{7,3},{8,12},{9,13},{10,... | collective-permute-start | bytes 196616 | tf_op jit(solution)/shard_map/ppermute | solution.py:94
  100.9 12.3 %collective-permute-start.23 = (f32[128,128]{1,0:T(8,128)S(1)}, f32[128,128]{1,0:T(8,128)S(1)}, u32[]{:S(2)}, u32[]{:S(2)}) collective-permute-start(f32[128,128]{1,0:T(8,128)S(1)} %add.304), channel_id=1, source_target_pairs={{0,8},{1,9},{2,10},{3,11},{4,12},{5,13},{6,14},{7,15},{8,0},{9,1},... | collective-permute-start | bytes 196616 | tf_op jit(solution)/shard_map/ppermute | solution.py:94
  113.3 1.3 collective-permute-start.24
  114.6 3.2 %collective-permute-start.25 = (bf16[128,4096]{1,0:T(8,128)(2,1)S(1)}, bf16[128,4096]{1,0:T(8,128)(2,1)S(1)}, u32[]{:S(2)}, u32[]{:S(2)}) collective-permute-start(bf16[128,4096]{1,0:T(8,128)(2,1)S(1)} %get-tuple-element.52), channel_id=1, source_target_pairs={{0,1},{1,0},{2,3},{3,2},{4,5},{5,4},{6,7},{7,6},{8,9},{9,8},{10,11... | collective-permute-start | bytes 3145736 | tf_op jit(solution)/shard_map/ppermute | solution.py:67
  116.2 1.6 collective-permute-start.26
  117.8 2.2 %copy-start.1 = (f32[128,512]{1,0:T(8,128)}, f32[128,512]{1,0:T(8,128)S(1)}, u32[]{:S(2)}) copy-start(f32[128,512]{1,0:T(8,128)S(1)} %collective-permute-done.26.side_far) | copy-start | bytes 786436
  119.2 0.8 copy-start.4
  120.0 14.2 %collective-permute-start.27 = (bf16[64,4096]{1,0:T(8,128)(2,1)S(1)}, bf16[64,4096]{1,0:T(8,128)(2,1)S(1)}, u32[]{:S(2)}, u32[]{:S(2)}) collective-permute-start(bf16[64,4096]{1,0:T(8,128)(2,1)S(1)} %get-tuple-element.56), channel_id=1, source_target_pairs={{0,2},{1,3},{2,0},{3,1},{4,6},{5,7},{6,4},{7,5},{8,10},{9,11},{10,... | collective-permute-start | bytes 1572872 | tf_op jit(solution)/shard_map/ppermute | solution.py:67
  134.2 3.0 %collective-permute-start.29 = (bf16[128,4096]{1,0:T(8,128)(2,1)}, bf16[128,4096]{1,0:T(8,128)(2,1)}, u32[]{:S(2)}, u32[]{:S(2)}) collective-permute-start(bf16[128,4096]{1,0:T(8,128)(2,1)} %get-tuple-element.60), channel_id=1, source_target_pairs={{0,1},{1,0},{2,3},{3,2},{4,5},{5,4},{6,7},{7,6},{8,9},{9,8},{10,11... | collective-permute-start | bytes 3145736 | tf_op jit(solution)/shard_map/ppermute | solution.py:67
  137.2 1.0 copy-start.2
  141.2 15.6 %collective-permute-start.30 = (bf16[64,4096]{1,0:T(8,128)(2,1)S(1)}, bf16[64,4096]{1,0:T(8,128)(2,1)S(1)}, u32[]{:S(2)}, u32[]{:S(2)}) collective-permute-start(bf16[64,4096]{1,0:T(8,128)(2,1)S(1)} %get-tuple-element.61), channel_id=1, source_target_pairs={{0,2},{1,3},{2,0},{3,1},{4,6},{5,7},{6,4},{7,5},{8,10},{9,11},{10,... | collective-permute-start | bytes 1572872 | tf_op jit(solution)/shard_map/ppermute | solution.py:67
  142.2 15.5 %collective-permute-start.28 = (bf16[16,4096]{1,0:T(8,128)(2,1)S(1)}, bf16[16,4096]{1,0:T(8,128)(2,1)S(1)}, u32[]{:S(2)}, u32[]{:S(2)}) collective-permute-start(bf16[16,4096]{1,0:T(8,128)(2,1)S(1)} %get-tuple-element.74), channel_id=1, source_target_pairs={{0,4},{1,5},{2,6},{3,7},{4,8},{5,9},{6,10},{7,11},{8,12},{9,13},{1... | collective-permute-start | bytes 393224 | tf_op jit(solution)/shard_map/ppermute | solution.py:67
  143.2 13.6 %collective-permute-start.32 = (bf16[16,4096]{1,0:T(8,128)(2,1)S(1)}, bf16[16,4096]{1,0:T(8,128)(2,1)S(1)}, u32[]{:S(2)}, u32[]{:S(2)}) collective-permute-start(bf16[16,4096]{1,0:T(8,128)(2,1)S(1)} %get-tuple-element.75), channel_id=1, source_target_pairs={{0,12},{1,13},{2,14},{3,15},{4,0},{5,1},{6,2},{7,3},{8,4},{9,5},{1... | collective-permute-start | bytes 393224 | tf_op jit(solution)/shard_map/ppermute | solution.py:67
  146.1 11.7 %collective-permute-start.31 = (bf16[16,4096]{1,0:T(8,128)(2,1)S(1)}, bf16[16,4096]{1,0:T(8,128)(2,1)S(1)}, u32[]{:S(2)}, u32[]{:S(2)}) collective-permute-start(bf16[16,4096]{1,0:T(8,128)(2,1)S(1)} %get-tuple-element.76), channel_id=1, source_target_pairs={{0,8},{1,9},{2,10},{3,11},{4,12},{5,13},{6,14},{7,15},{8,0},{9,1},... | collective-permute-start | bytes 393224 | tf_op jit(solution)/shard_map/ppermute | solution.py:67
  146.5 0.9 copy-start.6
  157.9 8.2 %collective-permute-start.33 = (bf16[16,4096]{1,0:T(8,128)(2,1)S(1)}, bf16[16,4096]{1,0:T(8,128)(2,1)S(1)}, u32[]{:S(2)}, u32[]{:S(2)}) collective-permute-start(bf16[16,4096]{1,0:T(8,128)(2,1)S(1)} %get-tuple-element.77), channel_id=1, source_target_pairs={{0,4},{1,5},{2,6},{3,7},{4,8},{5,9},{6,10},{7,11},{8,12},{9,13},{1... | collective-permute-start | bytes 393224 | tf_op jit(solution)/shard_map/ppermute | solution.py:67
  158.0 9.1 %collective-permute-start.35 = (bf16[16,4096]{1,0:T(8,128)(2,1)S(1)}, bf16[16,4096]{1,0:T(8,128)(2,1)S(1)}, u32[]{:S(2)}, u32[]{:S(2)}) collective-permute-start(bf16[16,4096]{1,0:T(8,128)(2,1)S(1)} %get-tuple-element.78), channel_id=1, source_target_pairs={{0,12},{1,13},{2,14},{3,15},{4,0},{5,1},{6,2},{7,3},{8,4},{9,5},{1... | collective-permute-start | bytes 393224 | tf_op jit(solution)/shard_map/ppermute | solution.py:67
  161.8 10.4 %collective-permute-start.34 = (bf16[16,4096]{1,0:T(8,128)(2,1)S(1)}, bf16[16,4096]{1,0:T(8,128)(2,1)S(1)}, u32[]{:S(2)}, u32[]{:S(2)}) collective-permute-start(bf16[16,4096]{1,0:T(8,128)(2,1)S(1)} %get-tuple-element.79), channel_id=1, source_target_pairs={{0,8},{1,9},{2,10},{3,11},{4,12},{5,13},{6,14},{7,15},{8,0},{9,1},... | collective-permute-start | bytes 393224 | tf_op jit(solution)/shard_map/ppermute | solution.py:67
  (1 other events, 0.8 us)

commit v9 on v8

--- a/solution.py
+++ b/solution.py
@@ -7,8 +7,6 @@
 from jax.experimental.pallas import tpu as pltpu
 from jax.sharding import PartitionSpec as P
 
-OUTER_SHARES = (3, 5)
-INNER_CUTS = (1, 2)
 SUM_SHARES = (4, 4)
 MIB = 1024 * 1024
 BF16 = jnp.bfloat16
@@ -164,7 +162,7 @@
         out[i] = part if len(rest) == 3 else rest[0][i] + part
 
 
-def forward_chunk(pieces, frozen, start, first, tiles):
+def forward_chunk(pieces, frozen, start, first, tiles, share=1):
     step = pieces[0].shape[1]
     tokens = sum(v.shape[0] for v in pieces)
     hidden = frozen.shape[2]
@@ -190,7 +188,7 @@
         ],
         input_output_aliases={} if start is None else {len(operands) - 1: 0},
         compiler_params=params(24),
-        cost_estimate=cost(4 * tokens * step * tile * count, 4 * step * tile * count),
+        cost_estimate=cost(4 * tokens * step * tile * count // share, 4 * step * tile * count // share),
     )(*operands)
 
 
@@ -639,34 +637,45 @@
 
     hidden = frozen.shape[2]
     tiles = hidden // tile_of(hidden, 256)
-    chunks = []
-    for share in OUTER_SHARES:
-        first = sum(v.shape[1] for v in chunks)
-        chunks.append(activations[:, first : first + width * share // sum(OUTER_SHARES)])
-    outer = []
-    for x in chunks:
-        x = torus.gather(after(x, outer[-1]) if outer else x, 0)
-        outer.append(x.reshape(a * rows, -1))
+    split = width * 3 // 8
+    last, main = activations[:, :split], activations[:, split:]
+    pair = [torus.move(last, 1, -k) for k in range(1, b)]
+    main = torus.gather(main, 0).reshape(a * rows, -1)
+    step = main.shape[1] // 2
     parts = []
-    for x, cuts in zip(outer, INNER_CUTS):
-        step = x.shape[1] // cuts
-        parts += [x[:, j * step : (j + 1) * step] for j in range(cuts)]
+    for j in range(2):
+        x = main[:, j * step : (j + 1) * step]
+        x = lax.optimization_barrier((x, *pair))[0] if j else x
+        parts.append((split + j * step, [x] + [torus.move(x, 1, -k) for k in range(1, b)]))
+    pair = after(jnp.stack([last, *pair]), main)
+    outer = [pair] + [torus.move(pair, 0, -k) for k in range(1, a)]
+
     base = None
     gathered = []
-    first = 0
-    for q, x in enumerate(parts):
-        near = [x] + [torus.move(x, 1, -k) for k in range(1, b)]
-        near[1:] = lax.optimization_barrier((*near[1:], base if q else outer[-1]))[:-1]
-        far = [torus.move(v, 2, -1) for v in near]
-        gathered.append([*near, *far])
-        for cut in parts_of(tiles, 2 if q == len(parts) - 1 else 1):
-            base = forward_chunk(gathered[q], frozen, base, first, cut)
-        first += x.shape[1]
+    for first, near in parts:
+        if gathered:
+            near[1:] = lax.optimization_barrier((*near[1:], base, *outer[1:]))[: b - 1]
+        gathered.append([*near, *[torus.move(v, 2, -1) for v in near]])
+        share = 64 if base is not None else 1
+        base = forward_chunk(gathered[-1], frozen, base, first, (0, tiles), share)
+    outer = lax.optimization_barrier((*outer, base))[:-1]
+    near = [jnp.stack([v[k] for v in outer]).reshape(a * rows, split) for k in range(b)]
+    gathered.insert(0, [*near, *[torus.move(v, 2, -1) for v in near]])
 
     columns, partial_in = low_in_partial(
         gathered, segment[:, None], adapter_down_factors, seg_adapter, places, index, rows
     )
-    low_in = whole_sum(partial_in)
+    ends_at = [cut[1] for cut in parts_of(tiles, 3)]
+    bases = [base]
+
+    def forward_part(token):
+        cut = (ends_at[len(bases) - 2] if len(bases) > 1 else 0, ends_at[len(bases) - 1])
+        pieces = [after(gathered[0][0], token), *gathered[0][1:]]
+        bases.append(forward_chunk(pieces, frozen, bases[-1], 0, cut))
+        return bases[-1]
+
+    low_in = whole_sum(partial_in, [forward_part] * len(ends_at))
+    base = bases[-1]
     dgate, dup, partial_out = middle(
         base, dhidden, token_order, order, low_in, segment[:, None], adapter_up_factors,
         seg_adapter, places, rows,
@@ -713,12 +722,11 @@
             total = total + v.astype(F32)
         inners.append(total.astype(BF16).reshape(a, rows, step))
         outer_moves.append([torus.move(inners[q][k], 0, k) for k in range(1, a)])
-    grad_b = grad_b_part(sums[-1][0])
+    grad_b = grad_b_part(outer_moves[-1][0])
     for q, inner in enumerate(inners):
         total = inner[0].astype(F32)
         for v in outer_moves[q]:
-            behind = (v, *inner_moves[-1], grad_b)
-            v = lax.optimization_barrier(behind)[0] if q < len(cuts) - 1 else v
+            v = lax.optimization_barrier((v, *inner_moves[-1]))[0] if q < len(cuts) - 1 else v
             total = total + v.astype(F32)
         blocks.append(total.astype(BF16))
     dinput = jnp.concatenate(blocks, axis=1)

time: 173 us -> 198 us (1.14)
  local copies, waits for them, and re-layouts: 7.17 us -> 19.3 us
  starting transfers between devices: 35.9 us -> 43.4 us
  waiting for transfers between devices: 40 us -> 32.5 us
  Pallas kernels: 84 us -> 90.3 us
  other arithmetic: 4.71 us -> 10.1 us
    unnamed x26 -> x100, local copies, waits for them, and re-layouts: 4.32 us -> 13.8 us
    ppermute x6, waiting for transfers between devices: 7.38 us -> 0.68 us  [exchange_sum(): x = x + lax.ppermute(x, 'tensor', pairs)]
    pallas_call x4 -> x5, Pallas kernels: 28.9 us -> 35.1 us  [forward_chunk(): pl.pallas_call(functools.partial(forward_kernel, len(pieces), low, count,...]
    ppermute x30, starting transfers between devices: 29.2 us -> 33.4 us  [move(): return lax.ppermute(x, 'tensor', pairs)]
    ppermute x6, starting transfers between devices: 6.68 us -> 10 us  [exchange_sum(): x = x + lax.ppermute(x, 'tensor', pairs)]
  transfers between devices with their start and end apart: 36 -> 36, of which waited for: 18 -> 16; matrix products, arithmetic and copies ran while one was open for 3% -> 6% of each run, Pallas kernels for 41% -> 34%
where the time goes in v9:
time: 198 us; the launch traced here: 197 us
  Pallas kernels  90.3 us (46%)
  starting transfers between devices  43.4 us (22%)
  waiting for transfers between devices  32.5 us (16%)
  local copies, waits for them, and re-layouts  19.3 us (10%)
  other arithmetic  10.1 us (5%)
    pallas_call x5, Pallas kernels, forward_chunk(): pl.pallas_call(functools.partial(forward_kernel, len(pieces), low, count,...  35.1 us
    ppermute x30, starting transfers between devices, move(): return lax.ppermute(x, 'tensor', pairs)  33.4 us
    ppermute x30, waiting for transfers between devices, move(): return lax.ppermute(x, 'tensor', pairs)  31.8 us
    pallas_call x2, Pallas kernels, backward_chunk(): pl.pallas_call(functools.partial(backward_kernel, count, first), grid=(co...  23.1 us
    unnamed x100, local copies, waits for them, and re-layouts  13.8 us
    pallas_call x3, Pallas kernels, grad_b_of(): pl.pallas_call(functools.partial(grad_b_kernel, first, last - first), gri...  11.9 us
    ppermute x6, starting transfers between devices, exchange_sum(): x = x + lax.ppermute(x, 'tensor', pairs)  10 us
    pallas_call x1, Pallas kernels, middle(): pl.pallas_call(functools.partial(middle_kernel, rows), grid_spec=pltpu.Pr...  7.56 us
  transfers between devices with their start and end apart: 36, of which 16 were waited for; matrix products, arithmetic and copies ran while one was open for 6% of the time, Pallas kernels for 34%

profile of v9, /device:TPU:0, one launch (start us, length us, event | category | flops | bytes accessed | tf_op | source)
XLA Modules:
  0.0 197.2 jit_solution(6727542695267449327)
XLA Ops:
  1.6 4.1 %collective-permute-start.2 = (bf16[16,5120]{1,0:T(8,128)(2,1)S(1)}, bf16[16,5120]{1,0:T(8,128)(2,1)S(1)}, u32[]{:S(2)}, u32[]{:S(2)}) collective-permute-start(bf16[16,5120]{1,0:T(8,128)(2,1)S(1)} %get-tuple-element.99), channel_id=1, source_target_pairs={{0,8},{1,9},{2,10},{3,11},{4,12},{5,13},{6,14},{7,15},{8,0},{9,1},... | collective-permute-start | bytes 491528 | tf_op jit(solution)/shard_map/ppermute | solution.py:65
  5.7 1.3 collective-permute-start.1
  8.6 1.6 collective-permute-start
  12.6 2.5 %collective-permute-done.2 = bf16[16,5120]{1,0:T(8,128)(2,1)S(1)} collective-permute-done((bf16[16,5120]{1,0:T(8,128)(2,1)S(1)}, bf16[16,5120]{1,0:T(8,128)(2,1)S(1)}, u32[]{:S(2)}, u32[]{:S(2)}) %collective-permute-start.2) | collective-permute-done | bytes 163872 | tf_op jit(solution)/shard_map/ppermute | solution.py:65
  15.0 3.1 %collective-permute-done.3 = bf16[16,5120]{1,0:T(8,128)(2,1)S(1)} collective-permute-done((bf16[16,5120]{1,0:T(8,128)(2,1)S(1)}, bf16[16,5120]{1,0:T(8,128)(2,1)S(1)}, u32[]{:S(2)}, u32[]{:S(2)}) %collective-permute-start.3) | collective-permute-done | bytes 163872 | tf_op jit(solution)/shard_map/ppermute | solution.py:65
  18.3 1.6 collective-permute-start.8
  20.7 6.2 %collective-permute-done.8.rest_1_.rest_13_ = bf16[64,2560]{1,0:T(8,128)(2,1)S(1)} collective-permute-done((bf16[64,2560]{1,0:T(8,128)(2,1)S(1)}, bf16[64,2560]{1,0:T(8,128)(2,1)S(1)}, u32[]{:S(2)}, u32[]{:S(2)}) %collective-permute-start.8) | collective-permute-done | bytes 327712 | tf_op jit(solution)/shard_map/ppermute | solution.py:65
  27.0 4.2 %collective-permute-start.6 = (bf16[2,16,3072]{2,1,0:T(8,128)(2,1)S(1)}, bf16[2,16,3072]{2,1,0:T(8,128)(2,1)S(1)}, u32[]{:S(2)}, u32[]{:S(2)}) collective-permute-start(bf16[2,16,3072]{2,1,0:T(8,128)(2,1)S(1)} %pad_maximum_fusion.4), channel_id=1, source_target_pairs={{0,4},{1,5},{2,6},{3,7},{4,8},{5,9},{6,10},{7,11},{8,12},{9,13},{1... | collective-permute-start | bytes 589832 | tf_op jit(solution)/shard_map/ppermute | solution.py:65
  31.1 2.0 %collective-permute-start.5 = (bf16[2,16,3072]{2,1,0:T(8,128)(2,1)S(1)}, bf16[2,16,3072]{2,1,0:T(8,128)(2,1)S(1)}, u32[]{:S(2)}, u32[]{:S(2)}) collective-permute-start(bf16[2,16,3072]{2,1,0:T(8,128)(2,1)S(1)} %pad_maximum_fusion.4), channel_id=1, source_target_pairs={{0,8},{1,9},{2,10},{3,11},{4,12},{5,13},{6,14},{7,15},{8,0},{9,1},... | collective-permute-start | bytes 589832 | tf_op jit(solution)/shard_map/ppermute | solution.py:65
  33.1 2.8 %collective-permute-start.4 = (bf16[2,16,3072]{2,1,0:T(8,128)(2,1)S(1)}, bf16[2,16,3072]{2,1,0:T(8,128)(2,1)S(1)}, u32[]{:S(2)}, u32[]{:S(2)}) collective-permute-start(bf16[2,16,3072]{2,1,0:T(8,128)(2,1)S(1)} %pad_maximum_fusion.4), channel_id=1, source_target_pairs={{0,12},{1,13},{2,14},{3,15},{4,0},{5,1},{6,2},{7,3},{8,4},{9,5},{1... | collective-permute-start | bytes 589832 | tf_op jit(solution)/shard_map/ppermute | solution.py:65
  36.0 1.6 collective-permute-start.7
  37.6 8.2 %shard_map.103.rest_5_ = f32[2,256,1792]{2,1,0:T(8,128)S(1)} custom-call(bf16[64,2560]{1,0:T(8,128)(2,1)S(1)} %get-tuple-element.90.rest_0_.rest_12_, bf16[64,2560]{1,0:T(8,128)(2,1)S(1)} %collective-permute-done.8.rest_1_.rest_13_, bf16[64,2560]{1,0:T(8,128)(2,1)S(1)} %collective-permute-done.9.rest_2_.rest_14_, ...), custom_call_target="tpu_custom_call" | custom-call | flops 4697620480 | bytes 18350080 | tf_op jit(solution)/shard_map/pallas_call | solution.py:179
  45.9 1.8 copy-done.1
  50.6 2.2 %copy-done.2 = f32[2,256,1792]{2,1,0:T(8,128)S(1)} copy-done((f32[2,256,1792]{2,1,0:T(8,128)S(1)}, f32[2,256,1792]{2,1,0:T(8,128)}, u32[]{:S(2)}) %copy-start.2) | copy-done | bytes 3670040
  52.8 9.7 %shard_map.104.rest_5_ = f32[2,256,1792]{2,1,0:T(8,128)S(1)} custom-call(bf16[64,2560]{1,0:T(8,128)(2,1)S(1)} %get-tuple-element.46.rest_0_.rest_16_, bf16[64,2560]{1,0:T(8,128)(2,1)} %collective-permute-done.7.rest_1_.rest_17_, bf16[64,2560]{1,0:T(8,128)(2,1)} %collective-permute-done.11.rest_2_.rest_18_, ...), custom_call_target="tpu_custom_call", output_to_operand_aliasing={{}: (5, {})} | custom-call | flops 73400320 | bytes 286720 | tf_op jit(solution)/shard_map/pallas_call | solution.py:179
  62.5 1.8 copy-done.3
  67.2 1.4 copy.21.seg
  75.3 2.8 %shard_map.105 = (bf16[256,512]{1,0:T(8,128)(2,1)S(1)}, f32[256,128]{1,0:T(8,128)S(1)}) custom-call(s32[8]{0:T(128)S(1)} %bitcast.49, s32[16]{0:T(128)S(1)} %get-tuple-element.88.places, s32[4]{0:T(128)S(1)} %pad_add_fusion.1.which, s32[256,1]{1,0:T(8,128)S(1)} %copy-done.15, bf16[24,512,128]{2,1,0:T(8,128)(2,1)S(1)} %copy-done, ...), custom_call_target="tpu_custom_call" | custom-call | flops 268435456 | bytes 1048576 | tf_op jit(solution)/shard_map/pallas_call | solution.py:249
  80.0 5.3 %shard_map.106.rest_5_ = f32[2,256,1792]{2,1,0:T(8,128)S(1)} custom-call(bf16[64,3072]{1,0:T(8,128)(2,1)S(1)} %bitcast.35, bf16[64,3072]{1,0:T(8,128)(2,1)} %bitcast.18.rest_9_.rest_1_, bf16[64,3072]{1,0:T(8,128)(2,1)} %collective-permute-done.13.rest_10_.rest_2_, ...), custom_call_target="tpu_custom_call", output_to_operand_aliasing={{}: (5, {})} | custom-call | flops 1610612736 | bytes 6291456 | tf_op jit(solution)/shard_map/pallas_call | solution.py:179
  85.4 4.3 %collective-permute-start.17 = (f32[128,128]{1,0:T(8,128)S(1)}, f32[128,128]{1,0:T(8,128)S(1)}, u32[]{:S(2)}, u32[]{:S(2)}) collective-permute-start(f32[128,128]{1,0:T(8,128)S(1)} %add.288), channel_id=1, source_target_pairs={{0,4},{1,5},{2,6},{3,7},{4,0},{5,1},{6,2},{7,3},{8,12},{9,13},{10,... | collective-permute-start | bytes 196616 | tf_op jit(solution)/shard_map/ppermute | solution.py:92
  89.7 5.3 %shard_map.107.rest_5_ = f32[2,256,1792]{2,1,0:T(8,128)S(1)} custom-call(bf16[64,3072]{1,0:T(8,128)(2,1)S(1)} %bitcast.36, bf16[64,3072]{1,0:T(8,128)(2,1)} %bitcast.18.rest_9_.rest_1_, bf16[64,3072]{1,0:T(8,128)(2,1)} %collective-permute-done.13.rest_10_.rest_2_, ...), custom_call_target="tpu_custom_call", output_to_operand_aliasing={{}: (5, {})} | custom-call | flops 1610612736 | bytes 6291456 | tf_op jit(solution)/shard_map/pallas_call | solution.py:179
  95.2 3.4 %collective-permute-start.18 = (f32[128,128]{1,0:T(8,128)S(1)}, f32[128,128]{1,0:T(8,128)S(1)}, u32[]{:S(2)}, u32[]{:S(2)}) collective-permute-start(f32[128,128]{1,0:T(8,128)S(1)} %add.289), channel_id=1, source_target_pairs={{0,8},{1,9},{2,10},{3,11},{4,12},{5,13},{6,14},{7,15},{8,0},{9,1},... | collective-permute-start | bytes 196616 | tf_op jit(solution)/shard_map/ppermute | solution.py:92
  98.6 6.4 %shard_map.108.base = f32[2,256,1792]{2,1,0:T(8,128)S(1)} custom-call(bf16[64,3072]{1,0:T(8,128)(2,1)S(1)} %bitcast.37, bf16[64,3072]{1,0:T(8,128)(2,1)} %bitcast.18.rest_9_.rest_1_, bf16[64,3072]{1,0:T(8,128)(2,1)} %collective-permute-done.13.rest_10_.rest_2_, ...), custom_call_target="tpu_custom_call", output_to_operand_aliasing={{}: (5, {})} | custom-call | flops 2415919104 | bytes 9437184 | tf_op jit(solution)/shard_map/pallas_call | solution.py:179
  105.4 1.1 collective-permute-done.19
  106.6 7.6 %shard_map.109 = (bf16[256,1792]{1,0:T(8,128)(2,1)S(1)}, bf16[256,1792]{1,0:T(8,128)(2,1)S(1)}, f32[256,128]{1,0:T(8,128)S(1)}) custom-call(s32[8]{0:T(128)S(1)} %bitcast.50, s32[16]{0:T(128)S(1)} %get-tuple-element.88.places, f32[2,256,1792]{2,1,0:T(8,128)S(1)} %shard_map.108.base, bf16[256,1792]{1,0:T(8,128)(2,1)S(1)} %copy-done.23, ...), custom_call_target="tpu_custom_call" | custom-call | flops 1879048192 | bytes 10092544 | tf_op jit(solution)/shard_map/pallas_call | solution.py:327
  116.1 3.6 %shard_map.110.rest_0_ = f32[24,128,1792]{2,1,0:T(8,128)} custom-call(bf16[256,1792]{1,0:T(8,128)(2,1)S(1)} %get-tuple-element.75.dgate, bf16[256,1792]{1,0:T(8,128)(2,1)S(1)} %get-tuple-element.61.dup, bf16[256,256]{1,0:T(8,128)(2,1)S(1)} %fusion.1.order, bf16[256,128]{1,0:T(8,128)(2,1)S(1)} %bitcast.39, s32[1,256]{1,0:T(1,128)S(1)} %bitcast.44), custom_call_target="tpu_custom_call" | custom-call | flops 805306368 | bytes 6291456 | tf_op jit(solution)/shard_map/pallas_call | solution.py:402
  120.0 3.6 %shard_map.111.rest_0_ = f32[24,128,1792]{2,1,0:T(8,128)} custom-call(bf16[256,1792]{1,0:T(8,128)(2,1)S(1)} %get-tuple-element.75.dgate, bf16[256,1792]{1,0:T(8,128)(2,1)S(1)} %get-tuple-element.61.dup, bf16[256,256]{1,0:T(8,128)(2,1)S(1)} %fusion.1.order, bf16[256,128]{1,0:T(8,128)(2,1)S(1)} %bitcast.40, ...), custom_call_target="tpu_custom_call", output_to_operand_aliasing={{}: (5, {})} | custom-call | flops 805306368 | bytes 6291456 | tf_op jit(solution)/shard_map/pallas_call | solution.py:402
  125.2 11.5 %shard_map.112 = (bf16[128,4096]{1,0:T(8,128)(2,1)S(1)}, bf16[128,4096]{1,0:T(8,128)(2,1)S(1)}) custom-call(bf16[2,8192,1792]{2,1,0:T(8,128)(2,1)} %frozen.3, bf16[256,1792]{1,0:T(8,128)(2,1)S(1)} %get-tuple-element.75.dgate, bf16[256,1792]{1,0:T(8,128)(2,1)S(1)} %get-tuple-element.61.dup), custom_call_target="tpu_custom_call" | custom-call | flops 7516192768 | bytes 29360128 | tf_op jit(solution)/shard_map/pallas_call | solution.py:518
  137.1 1.1 collective-permute-done.24
  138.4 1.4 shard_map.113
  140.3 1.1 collective-permute-done.26.side_far
  141.4 1.4 shard_map.114
  142.8 1.5 collective-permute-start.27
  144.3 11.5 %shard_map.115 = (bf16[128,4096]{1,0:T(8,128)(2,1)S(1)}, bf16[128,4096]{1,0:T(8,128)(2,1)S(1)}) custom-call(bf16[2,8192,1792]{2,1,0:T(8,128)(2,1)} %frozen.3, bf16[256,1792]{1,0:T(8,128)(2,1)S(1)} %get-tuple-element.75.dgate, bf16[256,1792]{1,0:T(8,128)(2,1)S(1)} %get-tuple-element.61.dup), custom_call_target="tpu_custom_call" | custom-call | flops 7516192768 | bytes 29360128 | tf_op jit(solution)/shard_map/pallas_call | solution.py:518
  155.9 1.2 collective-permute-done.27
  157.2 2.5 %collective-permute-done.29.far = bf16[128,4096]{1,0:T(8,128)(2,1)S(1)} collective-permute-done((bf16[128,4096]{1,0:T(8,128)(2,1)S(1)}, bf16[128,4096]{1,0:T(8,128)(2,1)S(1)}, u32[]{:S(2)}, u32[]{:S(2)}) %collective-permute-start.29) | collective-permute-done | bytes 1048608 | tf_op jit(solution)/shard_map/ppermute | solution.py:65
  159.8 2.4 %shard_map.116 = (bf16[64,4096]{1,0:T(8,128)(2,1)S(1)}, bf16[64,4096]{1,0:T(8,128)(2,1)}) custom-call(s32[2]{0:T(128)S(1)} %pad_add_fusion.at, bf16[128,4096]{1,0:T(8,128)(2,1)S(1)} %get-tuple-element.76.near, bf16[128,4096]{1,0:T(8,128)(2,1)S(1)} %collective-permute-done.29.far, f32[128,512]{1,0:T(8,128)S(1)} %get-tuple-element.71.side, ...), custom_call_target="tpu_custom_call" | custom-call | flops 1048576 | bytes 3145728 | tf_op jit(solution)/shard_map/pallas_call | solution.py:560
  163.0 1.4 collective-permute-start.30
  165.2 2.9 %collective-permute-start.32 = (bf16[16,4096]{1,0:T(8,128)(2,1)}, bf16[16,4096]{1,0:T(8,128)(2,1)S(1)}, u32[]{:S(2)}, u32[]{:S(2)}) collective-permute-start(bf16[16,4096]{1,0:T(8,128)(2,1)} %get-tuple-element.93), channel_id=1, source_target_pairs={{0,12},{1,13},{2,14},{3,15},{4,0},{5,1},{6,2},{7,3},{8,4},{9,5},{1... | collective-permute-start | bytes 393224 | tf_op jit(solution)/shard_map/ppermute | solution.py:65
  168.1 1.1 collective-permute-start.28
  169.3 4.7 %shard_map.117 = f32[24,512,128]{2,1,0:T(8,128)} custom-call(bf16[256,512]{1,0:T(8,128)(2,1)S(1)} %copy-done.28, bf16[256,256]{1,0:T(8,128)(2,1)S(1)} %copy-done.10, bf16[256,128]{1,0:T(8,128)(2,1)S(1)} %bitcast.43, s32[256,1]{1,0:T(8,128)S(1)} %copy.24.adapter), custom_call_target="tpu_custom_call" | custom-call | flops 805306368 | bytes 6291456 | tf_op jit(solution)/shard_map/pallas_call | solution.py:446
  174.0 3.3 %collective-permute-done.30 = bf16[64,4096]{1,0:T(8,128)(2,1)} collective-permute-done((bf16[64,4096]{1,0:T(8,128)(2,1)}, bf16[64,4096]{1,0:T(8,128)(2,1)}, u32[]{:S(2)}, u32[]{:S(2)}) %collective-permute-start.30) | collective-permute-done | bytes 524320 | tf_op jit(solution)/shard_map/ppermute | solution.py:65
  177.3 2.6 %collective-permute-done.31 = bf16[16,4096]{1,0:T(8,128)(2,1)S(1)} collective-permute-done((bf16[16,4096]{1,0:T(8,128)(2,1)}, bf16[16,4096]{1,0:T(8,128)(2,1)S(1)}, u32[]{:S(2)}, u32[]{:S(2)}) %collective-permute-start.31) | collective-permute-done | bytes 131104 | tf_op jit(solution)/shard_map/ppermute | solution.py:65
  179.9 1.2 add_convert_fusion
  181.6 3.4 %collective-permute-start.35 = (bf16[16,4096]{1,0:T(8,128)(2,1)S(1)}, bf16[16,4096]{1,0:T(8,128)(2,1)S(1)}, u32[]{:S(2)}, u32[]{:S(2)}) collective-permute-start(bf16[16,4096]{1,0:T(8,128)(2,1)S(1)} %get-tuple-element.96), channel_id=1, source_target_pairs={{0,12},{1,13},{2,14},{3,15},{4,0},{5,1},{6,2},{7,3},{8,4},{9,5},{1... | collective-permute-start | bytes 393224 | tf_op jit(solution)/shard_map/ppermute | solution.py:65
  186.5 2.9 %collective-permute-done.33 = bf16[16,4096]{1,0:T(8,128)(2,1)S(1)} collective-permute-done((bf16[16,4096]{1,0:T(8,128)(2,1)S(1)}, bf16[16,4096]{1,0:T(8,128)(2,1)S(1)}, u32[]{:S(2)}, u32[]{:S(2)}) %collective-permute-start.33) | collective-permute-done | bytes 131104 | tf_op jit(solution)/shard_map/ppermute | solution.py:65
  189.4 4.6 %shard_map.118 = f32[24,128,1792]{2,1,0:T(8,128)} custom-call(bf16[256,1792]{1,0:T(8,128)(2,1)S(1)} %copy-done.6, bf16[256,1792]{1,0:T(8,128)(2,1)S(1)} %copy-done.8, bf16[256,256]{1,0:T(8,128)(2,1)S(1)} %copy-done.10, bf16[256,128]{1,0:T(8,128)(2,1)S(1)} %bitcast.41, s32[1,256]{1,0:T(1,128)S(1)} %bitcast.47, ...), custom_call_target="tpu_custom_call", output_to_operand_aliasing={{}: (5, {})} | custom-call | flops 1207959552 | bytes 9437184 | tf_op jit(solution)/shard_map/pallas_call | solution.py:402
  194.0 2.4 %collective-permute-done.34 = bf16[16,4096]{1,0:T(8,128)(2,1)S(1)} collective-permute-done((bf16[16,4096]{1,0:T(8,128)(2,1)S(1)}, bf16[16,4096]{1,0:T(8,128)(2,1)S(1)}, u32[]{:S(2)}, u32[]{:S(2)}) %collective-permute-start.34) | collective-permute-done | bytes 131104 | tf_op jit(solution)/shard_map/ppermute | solution.py:65
  (205 shorter events, 29.8 us)
Async XLA Ops:
  1.6 13.5 %collective-permute-start.2 = (bf16[16,5120]{1,0:T(8,128)(2,1)S(1)}, bf16[16,5120]{1,0:T(8,128)(2,1)S(1)}, u32[]{:S(2)}, u32[]{:S(2)}) collective-permute-start(bf16[16,5120]{1,0:T(8,128)(2,1)S(1)} %get-tuple-element.99), channel_id=1, source_target_pairs={{0,8},{1,9},{2,10},{3,11},{4,12},{5,13},{6,14},{7,15},{8,0},{9,1},... | collective-permute-start | bytes 491528 | tf_op jit(solution)/shard_map/ppermute | solution.py:65
  5.7 9.4 %collective-permute-start.1 = (bf16[16,5120]{1,0:T(8,128)(2,1)S(1)}, bf16[16,5120]{1,0:T(8,128)(2,1)S(1)}, u32[]{:S(2)}, u32[]{:S(2)}) collective-permute-start(bf16[16,5120]{1,0:T(8,128)(2,1)S(1)} %get-tuple-element.99), channel_id=1, source_target_pairs={{0,12},{1,13},{2,14},{3,15},{4,0},{5,1},{6,2},{7,3},{8,4},{9,5},{1... | collective-permute-start | bytes 491528 | tf_op jit(solution)/shard_map/ppermute | solution.py:65
  7.0 11.1 %collective-permute-start.3 = (bf16[16,5120]{1,0:T(8,128)(2,1)S(1)}, bf16[16,5120]{1,0:T(8,128)(2,1)S(1)}, u32[]{:S(2)}, u32[]{:S(2)}) collective-permute-start(bf16[16,5120]{1,0:T(8,128)(2,1)S(1)} %get-tuple-element.99), channel_id=1, source_target_pairs={{0,4},{1,5},{2,6},{3,7},{4,8},{5,9},{6,10},{7,11},{8,12},{9,13},{1... | collective-permute-start | bytes 491528 | tf_op jit(solution)/shard_map/ppermute | solution.py:65
  8.6 18.3 %collective-permute-start = (bf16[16,3072]{1,0:T(8,128)(2,1)S(1)}, bf16[16,3072]{1,0:T(8,128)(2,1)S(1)}, u32[]{:S(2)}, u32[]{:S(2)}) collective-permute-start(bf16[16,3072]{1,0:T(8,128)(2,1)S(1)} %get-tuple-element.101), channel_id=1, source_target_pairs={{0,2},{1,3},{2,0},{3,1},{4,6},{5,7},{6,4},{7,5},{8,10},{9,11},{10,... | collective-permute-start | bytes 294920 | tf_op jit(solution)/shard_map/ppermute | solution.py:65
  18.3 27.6 %copy-start.11 = (bf16[64,2560]{1,0:T(8,128)(2,1)}, bf16[64,2560]{1,0:T(8,128)(2,1)S(1)}, u32[]{:S(2)}) copy-start(bf16[64,2560]{1,0:T(8,128)(2,1)S(1)} %get-tuple-element.90.rest_0_.rest_12_) | copy-start | bytes 983044
  18.3 32.3 %copy-start.13 = (bf16[64,2560]{1,0:T(8,128)(2,1)}, bf16[64,2560]{1,0:T(8,128)(2,1)S(1)}, u32[]{:S(2)}) copy-start(bf16[64,2560]{1,0:T(8,128)(2,1)S(1)} %get-tuple-element.46.rest_0_.rest_16_) | copy-start | bytes 983044
  18.3 8.6 %collective-permute-start.8 = (bf16[64,2560]{1,0:T(8,128)(2,1)S(1)}, bf16[64,2560]{1,0:T(8,128)(2,1)S(1)}, u32[]{:S(2)}, u32[]{:S(2)}) collective-permute-start(bf16[64,2560]{1,0:T(8,128)(2,1)S(1)} %get-tuple-element.90.rest_0_.rest_12_), channel_id=1, source_target_pairs={{0,2},{1,3},{2,0},{3,1},{4,6},{5,7},{6,4},{7,5},{8,10},{9,11},{10,... | collective-permute-start | bytes 983048 | tf_op jit(solution)/shard_map/ppermute | solution.py:65
  20.7 27.9 %copy-start.42 = (s32[128]{0:T(128)}, s32[128]{0:T(128)S(1)}, u32[]{:S(2)}) copy-start(s32[128]{0:T(128)S(1)} %select_reduce_fusion) | copy-start | bytes 1540
  20.7 15.3 %collective-permute-start.9 = (bf16[64,2560]{1,0:T(8,128)(2,1)S(1)}, bf16[64,2560]{1,0:T(8,128)(2,1)S(1)}, u32[]{:S(2)}, u32[]{:S(2)}) collective-permute-start(bf16[64,2560]{1,0:T(8,128)(2,1)S(1)} %get-tuple-element.90.rest_0_.rest_12_), channel_id=1, source_target_pairs={{0,1},{1,0},{2,3},{3,2},{4,5},{5,4},{6,7},{7,6},{8,9},{9,8},{10,11... | collective-permute-start | bytes 983048 | tf_op jit(solution)/shard_map/ppermute | solution.py:65
  26.9 19.0 %copy-start.17 = (bf16[64,2560]{1,0:T(8,128)(2,1)}, bf16[64,2560]{1,0:T(8,128)(2,1)S(1)}, u32[]{:S(2)}) copy-start(bf16[64,2560]{1,0:T(8,128)(2,1)S(1)} %collective-permute-done.8.rest_1_.rest_13_) | copy-start | bytes 983044
  26.9 9.1 %collective-permute-start.10 = (bf16[64,2560]{1,0:T(8,128)(2,1)S(1)}, bf16[64,2560]{1,0:T(8,128)(2,1)S(1)}, u32[]{:S(2)}, u32[]{:S(2)}) collective-permute-start(bf16[64,2560]{1,0:T(8,128)(2,1)S(1)} %collective-permute-done.8.rest_1_.rest_13_), channel_id=1, source_target_pairs={{0,1},{1,0},{2,3},{3,2},{4,5},{5,4},{6,7},{7,6},{8,9},{9,8},{10,11... | collective-permute-start | bytes 983048 | tf_op jit(solution)/shard_map/ppermute | solution.py:65
  27.0 20.8 %collective-permute-start.6 = (bf16[2,16,3072]{2,1,0:T(8,128)(2,1)S(1)}, bf16[2,16,3072]{2,1,0:T(8,128)(2,1)S(1)}, u32[]{:S(2)}, u32[]{:S(2)}) collective-permute-start(bf16[2,16,3072]{2,1,0:T(8,128)(2,1)S(1)} %pad_maximum_fusion.4), channel_id=1, source_target_pairs={{0,4},{1,5},{2,6},{3,7},{4,8},{5,9},{6,10},{7,11},{8,12},{9,13},{1... | collective-permute-start | bytes 589832 | tf_op jit(solution)/shard_map/ppermute | solution.py:65
  31.1 16.6 %collective-permute-start.5 = (bf16[2,16,3072]{2,1,0:T(8,128)(2,1)S(1)}, bf16[2,16,3072]{2,1,0:T(8,128)(2,1)S(1)}, u32[]{:S(2)}, u32[]{:S(2)}) collective-permute-start(bf16[2,16,3072]{2,1,0:T(8,128)(2,1)S(1)} %pad_maximum_fusion.4), channel_id=1, source_target_pairs={{0,8},{1,9},{2,10},{3,11},{4,12},{5,13},{6,14},{7,15},{8,0},{9,1},... | collective-permute-start | bytes 589832 | tf_op jit(solution)/shard_map/ppermute | solution.py:65
  33.1 14.6 %collective-permute-start.4 = (bf16[2,16,3072]{2,1,0:T(8,128)(2,1)S(1)}, bf16[2,16,3072]{2,1,0:T(8,128)(2,1)S(1)}, u32[]{:S(2)}, u32[]{:S(2)}) collective-permute-start(bf16[2,16,3072]{2,1,0:T(8,128)(2,1)S(1)} %pad_maximum_fusion.4), channel_id=1, source_target_pairs={{0,12},{1,13},{2,14},{3,15},{4,0},{5,1},{6,2},{7,3},{8,4},{9,5},{1... | collective-permute-start | bytes 589832 | tf_op jit(solution)/shard_map/ppermute | solution.py:65
  36.0 14.6 %collective-permute-start.11 = (bf16[64,2560]{1,0:T(8,128)(2,1)S(1)}, bf16[64,2560]{1,0:T(8,128)(2,1)}, u32[]{:S(2)}, u32[]{:S(2)}) collective-permute-start(bf16[64,2560]{1,0:T(8,128)(2,1)S(1)} %get-tuple-element.46.rest_0_.rest_16_), channel_id=1, source_target_pairs={{0,1},{1,0},{2,3},{3,2},{4,5},{5,4},{6,7},{7,6},{8,9},{9,8},{10,11... | collective-permute-start | bytes 983048 | tf_op jit(solution)/shard_map/ppermute | solution.py:65
  36.0 11.8 %collective-permute-start.7 = (bf16[64,2560]{1,0:T(8,128)(2,1)S(1)}, bf16[64,2560]{1,0:T(8,128)(2,1)}, u32[]{:S(2)}, u32[]{:S(2)}) collective-permute-start(bf16[64,2560]{1,0:T(8,128)(2,1)S(1)} %get-tuple-element.46.rest_0_.rest_16_), channel_id=1, source_target_pairs={{0,2},{1,3},{2,0},{3,1},{4,6},{5,7},{6,4},{7,5},{8,10},{9,11},{10,... | collective-permute-start | bytes 983048 | tf_op jit(solution)/shard_map/ppermute | solution.py:65
  48.4 2.1 %collective-permute-start.12 = (bf16[64,2560]{1,0:T(8,128)(2,1)}, bf16[64,2560]{1,0:T(8,128)(2,1)}, u32[]{:S(2)}, u32[]{:S(2)}) collective-permute-start(bf16[64,2560]{1,0:T(8,128)(2,1)} %collective-permute-done.7.rest_1_.rest_17_), channel_id=1, source_target_pairs={{0,1},{1,0},{2,3},{3,2},{4,5},{5,4},{6,7},{7,6},{8,9},{9,8},{10,11... | collective-permute-start | bytes 983048 | tf_op jit(solution)/shard_map/ppermute | solution.py:65
  49.8 19.7 %copy-start.29 = (s32[1,8]{1,0:T(1,128)S(1)}, s32[1,8]{1,0:T(1,128)}, u32[]{:S(2)}) copy-start(s32[1,8]{1,0:T(1,128)} %param.13) | copy-start | bytes 100
  64.5 5.0 %collective-permute-start.13 = (bf16[64,3072]{1,0:T(8,128)(2,1)S(1)}, bf16[64,3072]{1,0:T(8,128)(2,1)}, u32[]{:S(2)}, u32[]{:S(2)}) collective-permute-start(bf16[64,3072]{1,0:T(8,128)(2,1)S(1)} %bitcast.33), channel_id=1, source_target_pairs={{0,1},{1,0},{2,3},{3,2},{4,5},{5,4},{6,7},{7,6},{8,9},{9,8},{10,11... | collective-permute-start | bytes 1179656 | tf_op jit(solution)/shard_map/ppermute | solution.py:65
  65.7 3.8 %collective-permute-start.14 = (bf16[64,3072]{1,0:T(8,128)(2,1)}, bf16[64,3072]{1,0:T(8,128)(2,1)}, u32[]{:S(2)}, u32[]{:S(2)}) collective-permute-start(bf16[64,3072]{1,0:T(8,128)(2,1)} %bitcast.18.rest_9_.rest_1_), channel_id=1, source_target_pairs={{0,1},{1,0},{2,3},{3,2},{4,5},{5,4},{6,7},{7,6},{8,9},{9,8},{10,11... | collective-permute-start | bytes 1179656 | tf_op jit(solution)/shard_map/ppermute | solution.py:65
  69.5 68.9 %copy-start.9 = (bf16[256,256]{1,0:T(8,128)(2,1)}, bf16[256,256]{1,0:T(8,128)(2,1)S(1)}, u32[]{:S(2)}) copy-start(bf16[256,256]{1,0:T(8,128)(2,1)S(1)} %fusion.1.order) | copy-start | bytes 393220
  78.1 1.3 collective-permute-start.15
  79.4 5.9 %collective-permute-start.16 = (f32[128,128]{1,0:T(8,128)S(1)}, f32[128,128]{1,0:T(8,128)S(1)}, u32[]{:S(2)}, u32[]{:S(2)}) collective-permute-start(f32[128,128]{1,0:T(8,128)S(1)} %slice_add_fusion.1), channel_id=1, source_target_pairs={{0,2},{1,3},{2,0},{3,1},{4,6},{5,7},{6,4},{7,5},{8,10},{9,11},{10,... | collective-permute-start | bytes 196616 | tf_op jit(solution)/shard_map/ppermute | solution.py:92
  85.4 9.7 %collective-permute-start.17 = (f32[128,128]{1,0:T(8,128)S(1)}, f32[128,128]{1,0:T(8,128)S(1)}, u32[]{:S(2)}, u32[]{:S(2)}) collective-permute-start(f32[128,128]{1,0:T(8,128)S(1)} %add.288), channel_id=1, source_target_pairs={{0,4},{1,5},{2,6},{3,7},{4,0},{5,1},{6,2},{7,3},{8,12},{9,13},{10,... | collective-permute-start | bytes 196616 | tf_op jit(solution)/shard_map/ppermute | solution.py:92
  95.2 9.9 %collective-permute-start.18 = (f32[128,128]{1,0:T(8,128)S(1)}, f32[128,128]{1,0:T(8,128)S(1)}, u32[]{:S(2)}, u32[]{:S(2)}) collective-permute-start(f32[128,128]{1,0:T(8,128)S(1)} %add.289), channel_id=1, source_target_pairs={{0,8},{1,9},{2,10},{3,11},{4,12},{5,13},{6,14},{7,15},{8,0},{9,1},... | collective-permute-start | bytes 196616 | tf_op jit(solution)/shard_map/ppermute | solution.py:92
  105.2 1.3 collective-permute-start.19
  114.2 30.2 %copy-start.5 = (bf16[256,1792]{1,0:T(8,128)(2,1)}, bf16[256,1792]{1,0:T(8,128)(2,1)S(1)}, u32[]{:S(2)}) copy-start(bf16[256,1792]{1,0:T(8,128)(2,1)S(1)} %get-tuple-element.75.dgate) | copy-start | bytes 2752516
  114.2 30.1 %copy-start.7 = (bf16[256,1792]{1,0:T(8,128)(2,1)}, bf16[256,1792]{1,0:T(8,128)(2,1)S(1)}, u32[]{:S(2)}) copy-start(bf16[256,1792]{1,0:T(8,128)(2,1)S(1)} %get-tuple-element.61.dup) | copy-start | bytes 2752516
  114.2 1.3 collective-permute-start.20
  115.5 4.3 %collective-permute-start.21 = (f32[128,128]{1,0:T(8,128)S(1)}, f32[128,128]{1,0:T(8,128)S(1)}, u32[]{:S(2)}, u32[]{:S(2)}) collective-permute-start(f32[128,128]{1,0:T(8,128)S(1)} %slice_add_fusion), channel_id=1, source_target_pairs={{0,2},{1,3},{2,0},{3,1},{4,6},{5,7},{6,4},{7,5},{8,10},{9,11},{10,... | collective-permute-start | bytes 196616 | tf_op jit(solution)/shard_map/ppermute | solution.py:92
  119.9 4.3 %collective-permute-start.22 = (f32[128,128]{1,0:T(8,128)S(1)}, f32[128,128]{1,0:T(8,128)S(1)}, u32[]{:S(2)}, u32[]{:S(2)}) collective-permute-start(f32[128,128]{1,0:T(8,128)S(1)} %add.303), channel_id=1, source_target_pairs={{0,4},{1,5},{2,6},{3,7},{4,0},{5,1},{6,2},{7,3},{8,12},{9,13},{10,... | collective-permute-start | bytes 196616 | tf_op jit(solution)/shard_map/ppermute | solution.py:92
  124.2 12.6 %collective-permute-start.23 = (f32[128,128]{1,0:T(8,128)S(1)}, f32[128,128]{1,0:T(8,128)S(1)}, u32[]{:S(2)}, u32[]{:S(2)}) collective-permute-start(f32[128,128]{1,0:T(8,128)S(1)} %add.304), channel_id=1, source_target_pairs={{0,8},{1,9},{2,10},{3,11},{4,12},{5,13},{6,14},{7,15},{8,0},{9,1},... | collective-permute-start | bytes 196616 | tf_op jit(solution)/shard_map/ppermute | solution.py:92
  136.9 1.3 collective-permute-start.24
  138.2 3.2 %collective-permute-start.25 = (bf16[128,4096]{1,0:T(8,128)(2,1)S(1)}, bf16[128,4096]{1,0:T(8,128)(2,1)S(1)}, u32[]{:S(2)}, u32[]{:S(2)}) collective-permute-start(bf16[128,4096]{1,0:T(8,128)(2,1)S(1)} %get-tuple-element.70), channel_id=1, source_target_pairs={{0,1},{1,0},{2,3},{3,2},{4,5},{5,4},{6,7},{7,6},{8,9},{9,8},{10,11... | collective-permute-start | bytes 3145736 | tf_op jit(solution)/shard_map/ppermute | solution.py:65
  139.8 1.6 collective-permute-start.26
  142.8 26.5 %copy-start.10 = (bf16[256,256]{1,0:T(8,128)(2,1)S(1)}, bf16[256,256]{1,0:T(8,128)(2,1)}, u32[]{:S(2)}) copy-start(bf16[256,256]{1,0:T(8,128)(2,1)} %copy-done.9) | copy-start | bytes 393220
  142.8 26.5 %copy-start.28 = (bf16[256,512]{1,0:T(8,128)(2,1)S(1)}, bf16[256,512]{1,0:T(8,128)(2,1)}, u32[]{:S(2)}) copy-start(bf16[256,512]{1,0:T(8,128)(2,1)} %copy-done.27) | copy-start | bytes 786436
  142.8 14.3 %collective-permute-start.27 = (bf16[64,4096]{1,0:T(8,128)(2,1)S(1)}, bf16[64,4096]{1,0:T(8,128)(2,1)S(1)}, u32[]{:S(2)}, u32[]{:S(2)}) collective-permute-start(bf16[64,4096]{1,0:T(8,128)(2,1)S(1)} %get-tuple-element.74), channel_id=1, source_target_pairs={{0,2},{1,3},{2,0},{3,1},{4,6},{5,7},{6,4},{7,5},{8,10},{9,11},{10,... | collective-permute-start | bytes 1572872 | tf_op jit(solution)/shard_map/ppermute | solution.py:65
  157.1 2.7 %collective-permute-start.29 = (bf16[128,4096]{1,0:T(8,128)(2,1)S(1)}, bf16[128,4096]{1,0:T(8,128)(2,1)S(1)}, u32[]{:S(2)}, u32[]{:S(2)}) collective-permute-start(bf16[128,4096]{1,0:T(8,128)(2,1)S(1)} %get-tuple-element.78), channel_id=1, source_target_pairs={{0,1},{1,0},{2,3},{3,2},{4,5},{5,4},{6,7},{7,6},{8,9},{9,8},{10,11... | collective-permute-start | bytes 3145736 | tf_op jit(solution)/shard_map/ppermute | solution.py:65
  159.8 29.7 %copy-start.6 = (bf16[256,1792]{1,0:T(8,128)(2,1)S(1)}, bf16[256,1792]{1,0:T(8,128)(2,1)}, u32[]{:S(2)}) copy-start(bf16[256,1792]{1,0:T(8,128)(2,1)} %copy-done.5) | copy-start | bytes 2752516
  159.8 29.7 %copy-start.8 = (bf16[256,1792]{1,0:T(8,128)(2,1)S(1)}, bf16[256,1792]{1,0:T(8,128)(2,1)}, u32[]{:S(2)}) copy-start(bf16[256,1792]{1,0:T(8,128)(2,1)} %copy-done.7) | copy-start | bytes 2752516
  163.0 14.3 %collective-permute-start.30 = (bf16[64,4096]{1,0:T(8,128)(2,1)}, bf16[64,4096]{1,0:T(8,128)(2,1)}, u32[]{:S(2)}, u32[]{:S(2)}) collective-permute-start(bf16[64,4096]{1,0:T(8,128)(2,1)} %get-tuple-element.79), channel_id=1, source_target_pairs={{0,2},{1,3},{2,0},{3,1},{4,6},{5,7},{6,4},{7,5},{8,10},{9,11},{10,... | collective-permute-start | bytes 1572872 | tf_op jit(solution)/shard_map/ppermute | solution.py:65
  165.2 8.8 %collective-permute-start.32 = (bf16[16,4096]{1,0:T(8,128)(2,1)}, bf16[16,4096]{1,0:T(8,128)(2,1)S(1)}, u32[]{:S(2)}, u32[]{:S(2)}) collective-permute-start(bf16[16,4096]{1,0:T(8,128)(2,1)} %get-tuple-element.93), channel_id=1, source_target_pairs={{0,12},{1,13},{2,14},{3,15},{4,0},{5,1},{6,2},{7,3},{8,4},{9,5},{1... | collective-permute-start | bytes 393224 | tf_op jit(solution)/shard_map/ppermute | solution.py:65
  168.0 11.9 %collective-permute-start.31 = (bf16[16,4096]{1,0:T(8,128)(2,1)}, bf16[16,4096]{1,0:T(8,128)(2,1)S(1)}, u32[]{:S(2)}, u32[]{:S(2)}) collective-permute-start(bf16[16,4096]{1,0:T(8,128)(2,1)} %get-tuple-element.94), channel_id=1, source_target_pairs={{0,8},{1,9},{2,10},{3,11},{4,12},{5,13},{6,14},{7,15},{8,0},{9,1},... | collective-permute-start | bytes 393224 | tf_op jit(solution)/shard_map/ppermute | solution.py:65
  168.1 11.9 %collective-permute-start.28 = (bf16[16,4096]{1,0:T(8,128)(2,1)S(1)}, bf16[16,4096]{1,0:T(8,128)(2,1)S(1)}, u32[]{:S(2)}, u32[]{:S(2)}) collective-permute-start(bf16[16,4096]{1,0:T(8,128)(2,1)S(1)} %get-tuple-element.92), channel_id=1, source_target_pairs={{0,4},{1,5},{2,6},{3,7},{4,8},{5,9},{6,10},{7,11},{8,12},{9,13},{1... | collective-permute-start | bytes 393224 | tf_op jit(solution)/shard_map/ppermute | solution.py:65
  181.2 8.2 %collective-permute-start.33 = (bf16[16,4096]{1,0:T(8,128)(2,1)S(1)}, bf16[16,4096]{1,0:T(8,128)(2,1)S(1)}, u32[]{:S(2)}, u32[]{:S(2)}) collective-permute-start(bf16[16,4096]{1,0:T(8,128)(2,1)S(1)} %get-tuple-element.95), channel_id=1, source_target_pairs={{0,4},{1,5},{2,6},{3,7},{4,8},{5,9},{6,10},{7,11},{8,12},{9,13},{1... | collective-permute-start | bytes 393224 | tf_op jit(solution)/shard_map/ppermute | solution.py:65
  181.6 12.4 %collective-permute-start.35 = (bf16[16,4096]{1,0:T(8,128)(2,1)S(1)}, bf16[16,4096]{1,0:T(8,128)(2,1)S(1)}, u32[]{:S(2)}, u32[]{:S(2)}) collective-permute-start(bf16[16,4096]{1,0:T(8,128)(2,1)S(1)} %get-tuple-element.96), channel_id=1, source_target_pairs={{0,12},{1,13},{2,14},{3,15},{4,0},{5,1},{6,2},{7,3},{8,4},{9,5},{1... | collective-permute-start | bytes 393224 | tf_op jit(solution)/shard_map/ppermute | solution.py:65
  185.0 11.4 %collective-permute-start.34 = (bf16[16,4096]{1,0:T(8,128)(2,1)S(1)}, bf16[16,4096]{1,0:T(8,128)(2,1)S(1)}, u32[]{:S(2)}, u32[]{:S(2)}) collective-permute-start(bf16[16,4096]{1,0:T(8,128)(2,1)S(1)} %get-tuple-element.97), channel_id=1, source_target_pairs={{0,8},{1,9},{2,10},{3,11},{4,12},{5,13},{6,14},{7,15},{8,0},{9,1},... | collective-permute-start | bytes 393224 | tf_op jit(solution)/shard_map/ppermute | solution.py:65
  (38 other events, 286.9 us)

commit v10 on v8

--- a/solution.py
+++ b/solution.py
@@ -189,7 +189,7 @@
             pltpu.SemaphoreType.DMA((DEPTH, 2)),
         ],
         input_output_aliases={} if start is None else {len(operands) - 1: 0},
-        compiler_params=params(24),
+        compiler_params=params(16),
         cost_estimate=cost(4 * tokens * step * tile * count, 4 * step * tile * count),
     )(*operands)
 
@@ -347,7 +347,7 @@
             jax.ShapeDtypeStruct((tokens, hidden), BF16),
             jax.ShapeDtypeStruct((tokens, wide), F32),
         ],
-        compiler_params=params(20),
+        compiler_params=params(16),
         cost_estimate=cost(
             4 * tokens * hidden * segments * wide, hidden * (tokens * 14 + segments * wide * 2)
         ),
@@ -413,7 +413,7 @@
             pltpu.SemaphoreType.DMA((SLOTS,)),
         ],
         input_output_aliases={} if start is None else {5: 0},
-        compiler_params=params(20),
+        compiler_params=params(16),
         cost_estimate=cost(2 * tokens * part, 4 * part),
     )(*operands)
 
@@ -527,7 +527,7 @@
             pltpu.VMEM((DEPTH, 2, block, hidden), BF16),
             pltpu.SemaphoreType.DMA((DEPTH, 2)),
         ],
-        compiler_params=params(20),
+        compiler_params=params(16),
         cost_estimate=cost(4 * tokens * step * hidden, 4 * step * hidden),
     )(frozen, dgate, dup)
 
@@ -659,19 +659,27 @@
         near[1:] = lax.optimization_barrier((*near[1:], base if q else outer[-1]))[:-1]
         far = [torus.move(v, 2, -1) for v in near]
         gathered.append([*near, *far])
-        for cut in parts_of(tiles, 2 if q == len(parts) - 1 else 1):
-            base = forward_chunk(gathered[q], frozen, base, first, cut)
-        first += x.shape[1]
+        if q < len(parts) - 1:
+            base = forward_chunk(gathered[q], frozen, base, first, (0, tiles))
+            first += x.shape[1]
 
     columns, partial_in = low_in_partial(
         gathered, segment[:, None], adapter_down_factors, seg_adapter, places, index, rows
     )
-    low_in = whole_sum(partial_in)
+    thirds = parts_of(tiles, 3)
+    bases = [base]
+
+    def forward_part(token):
+        pieces = [after(gathered[-1][0], token), *gathered[-1][1:]]
+        bases.append(forward_chunk(pieces, frozen, bases[-1], first, thirds[len(bases) - 1]))
+        return bases[-1]
+
+    low_in = whole_sum(partial_in, [forward_part] * len(thirds))
+    base = bases[-1]
     dgate, dup, partial_out = middle(
         base, dhidden, token_order, order, low_in, segment[:, None], adapter_up_factors,
         seg_adapter, places, rows,
     )
-    thirds = parts_of(tiles, 3)
     grad_b = []
 
     def grad_b_part(token):
@@ -713,12 +721,11 @@
             total = total + v.astype(F32)
         inners.append(total.astype(BF16).reshape(a, rows, step))
         outer_moves.append([torus.move(inners[q][k], 0, k) for k in range(1, a)])
-    grad_b = grad_b_part(sums[-1][0])
+    grad_b = grad_b_part(outer_moves[-1][0])
     for q, inner in enumerate(inners):
         total = inner[0].astype(F32)
         for v in outer_moves[q]:
-            behind = (v, *inner_moves[-1], grad_b)
-            v = lax.optimization_barrier(behind)[0] if q < len(cuts) - 1 else v
+            v = lax.optimization_barrier((v, *inner_moves[-1]))[0] if q < len(cuts) - 1 else v
             total = total + v.astype(F32)
         blocks.append(total.astype(BF16))
     dinput = jnp.concatenate(blocks, axis=1)

time: 173 us -> 176 us (1.017)
  waiting for transfers between devices: 40 us -> 32.4 us
  local copies, waits for them, and re-layouts: 7.17 us -> 10.9 us
  starting transfers between devices: 35.9 us -> 38.4 us
  other arithmetic: 4.71 us -> 6.87 us
    ppermute x6, waiting for transfers between devices: 7.38 us -> 0.18 us  [exchange_sum(): x = x + lax.ppermute(x, 'tensor', pairs)]
    unnamed x26 -> x36, local copies, waits for them, and re-layouts: 4.32 us -> 6.74 us
    pallas_call x4 -> x5, Pallas kernels: 28.9 us -> 30.7 us  [forward_chunk(): pl.pallas_call(functools.partial(forward_kernel, len(pieces), low, count,...]
  transfers between devices with their start and end apart: 36 -> 36, of which waited for: 18 -> 16; matrix products, arithmetic and copies ran while one was open for 3% -> 4% of each run, Pallas kernels for 41% -> 41%
where the time goes in v10:
time: 176 us
  Pallas kernels  85.7 us (49%)
  starting transfers between devices  38.4 us (22%)
  waiting for transfers between devices  32.4 us (18%)
  local copies, waits for them, and re-layouts  10.9 us (6%)
  other arithmetic  6.87 us (4%)
    ppermute x30, waiting for transfers between devices, move(): return lax.ppermute(x, 'tensor', pairs)  32.2 us
    ppermute x30, starting transfers between devices, move(): return lax.ppermute(x, 'tensor', pairs)  30.8 us
    pallas_call x5, Pallas kernels, forward_chunk(): pl.pallas_call(functools.partial(forward_kernel, len(pieces), low, count,...  30.7 us
    pallas_call x2, Pallas kernels, backward_chunk(): pl.pallas_call(functools.partial(backward_kernel, count, first), grid=(co...  23.1 us
    pallas_call x3, Pallas kernels, grad_b_of(): pl.pallas_call(functools.partial(grad_b_kernel, first, last - first), gri...  11.9 us
    ppermute x6, starting transfers between devices, exchange_sum(): x = x + lax.ppermute(x, 'tensor', pairs)  7.58 us
    pallas_call x1, Pallas kernels, middle(): pl.pallas_call(functools.partial(middle_kernel, rows), grid_spec=pltpu.Pr...  7.48 us
    unnamed x36, local copies, waits for them, and re-layouts  6.74 us
  transfers between devices with their start and end apart: 36, of which 16 were waited for; matrix products, arithmetic and copies ran while one was open for 4% of the time, Pallas kernels for 41%

profile of v10, /device:TPU:0, one launch (start us, length us, event | category | flops | bytes accessed | tf_op | source)
XLA Modules:
  0.0 175.5 jit_solution(16704724880927485640)
XLA Ops:
  1.5 4.1 %collective-permute-start.1 = (bf16[16,3072]{1,0:T(8,128)(2,1)S(1)}, bf16[16,3072]{1,0:T(8,128)(2,1)S(1)}, u32[]{:S(2)}, u32[]{:S(2)}) collective-permute-start(bf16[16,3072]{1,0:T(8,128)(2,1)S(1)} %get-tuple-element.93), channel_id=1, source_target_pairs={{0,8},{1,9},{2,10},{3,11},{4,12},{5,13},{6,14},{7,15},{8,0},{9,1},... | collective-permute-start | bytes 294920 | tf_op jit(solution)/shard_map/ppermute | solution.py:67
  5.6 1.3 collective-permute-start
  12.6 1.3 collective-permute-done.2
  13.9 1.7 collective-permute-start.5
  15.6 2.0 %collective-permute-start.4 = (bf16[16,5120]{1,0:T(8,128)(2,1)S(1)}, bf16[16,5120]{1,0:T(8,128)(2,1)S(1)}, u32[]{:S(2)}, u32[]{:S(2)}) collective-permute-start(bf16[16,5120]{1,0:T(8,128)(2,1)S(1)} %slice.60), channel_id=1, source_target_pairs={{0,8},{1,9},{2,10},{3,11},{4,12},{5,13},{6,14},{7,15},{8,0},{9,1},... | collective-permute-start | bytes 491528 | tf_op jit(solution)/shard_map/ppermute | solution.py:67
  17.6 2.8 %collective-permute-start.3 = (bf16[16,5120]{1,0:T(8,128)(2,1)S(1)}, bf16[16,5120]{1,0:T(8,128)(2,1)S(1)}, u32[]{:S(2)}, u32[]{:S(2)}) collective-permute-start(bf16[16,5120]{1,0:T(8,128)(2,1)S(1)} %slice.60), channel_id=1, source_target_pairs={{0,12},{1,13},{2,14},{3,15},{4,0},{5,1},{6,2},{7,3},{8,4},{9,5},{1... | collective-permute-start | bytes 491528 | tf_op jit(solution)/shard_map/ppermute | solution.py:67
  20.4 1.5 collective-permute-start.6
  22.0 6.1 %collective-permute-done.4 = bf16[16,5120]{1,0:T(8,128)(2,1)S(1)} collective-permute-done((bf16[16,5120]{1,0:T(8,128)(2,1)S(1)}, bf16[16,5120]{1,0:T(8,128)(2,1)S(1)}, u32[]{:S(2)}, u32[]{:S(2)}) %collective-permute-start.4) | collective-permute-done | bytes 163872 | tf_op jit(solution)/shard_map/ppermute | solution.py:67
  28.2 3.8 %collective-permute-done.6.rest_1_.rest_9_ = bf16[64,3072]{1,0:T(8,128)(2,1)S(1)} collective-permute-done((bf16[64,3072]{1,0:T(8,128)(2,1)S(1)}, bf16[64,3072]{1,0:T(8,128)(2,1)S(1)}, u32[]{:S(2)}, u32[]{:S(2)}) %collective-permute-start.6) | collective-permute-done | bytes 393248 | tf_op jit(solution)/shard_map/ppermute | solution.py:67
  32.6 1.5 collective-permute-start.9
  34.1 9.4 %shard_map.103.rest_5_ = f32[2,256,1792]{2,1,0:T(8,128)S(1)} custom-call(bf16[64,3072]{1,0:T(8,128)(2,1)S(1)} %bitcast.35, bf16[64,3072]{1,0:T(8,128)(2,1)S(1)} %collective-permute-done.6.rest_1_.rest_9_, bf16[64,3072]{1,0:T(8,128)(2,1)S(1)} %collective-permute-done.7.rest_2_.rest_10_, bf16[64,3072]{1,0:T(8,128)(2,1)S(1)} %collective-permute-done.8.rest_3_.rest_11_, ...), custom_call_target="tpu_custom_call" | custom-call | flops 5637144576 | bytes 22020096 | tf_op jit(solution)/shard_map/pallas_call | solution.py:181
  43.5 1.8 %copy-done.1 = f32[2,256,1792]{2,1,0:T(8,128)} copy-done((f32[2,256,1792]{2,1,0:T(8,128)}, f32[2,256,1792]{2,1,0:T(8,128)S(1)}, u32[]{:S(2)}) %copy-start.1) | copy-done | bytes 3670040
  46.3 1.1 collective-permute-start.12
  47.4 2.0 %copy-done.2 = f32[2,256,1792]{2,1,0:T(8,128)S(1)} copy-done((f32[2,256,1792]{2,1,0:T(8,128)S(1)}, f32[2,256,1792]{2,1,0:T(8,128)}, u32[]{:S(2)}) %copy-start.2) | copy-done | bytes 3670040
  49.4 9.4 %shard_map.104.rest_5_ = f32[2,256,1792]{2,1,0:T(8,128)S(1)} custom-call(bf16[64,2560]{1,0:T(8,128)(2,1)S(1)} %get-tuple-element.84.rest_0_.rest_12_, bf16[64,2560]{1,0:T(8,128)(2,1)S(1)} %collective-permute-done.9.rest_1_.rest_13_, bf16[64,2560]{1,0:T(8,128)(2,1)S(1)} %collective-permute-done.10.rest_2_.rest_14_, ...), custom_call_target="tpu_custom_call", output_to_operand_aliasing={{}: (5, {})} | custom-call | flops 4697620480 | bytes 18350080 | tf_op jit(solution)/shard_map/pallas_call | solution.py:181
  58.9 1.8 %copy-done.3 = f32[2,256,1792]{2,1,0:T(8,128)} copy-done((f32[2,256,1792]{2,1,0:T(8,128)}, f32[2,256,1792]{2,1,0:T(8,128)S(1)}, u32[]{:S(2)}) %copy-start.3) | copy-done | bytes 3670040
  60.9 1.4 collective-permute-done.14.rest_19_.rest_3_
  63.3 2.7 %shard_map.105 = (bf16[256,512]{1,0:T(8,128)(2,1)S(1)}, f32[256,128]{1,0:T(8,128)S(1)}) custom-call(s32[8]{0:T(128)S(1)} %bitcast.48, s32[16]{0:T(128)S(1)} %get-tuple-element.82.places, s32[4]{0:T(128)S(1)} %pad_add_fusion.1.which, s32[256,1]{1,0:T(8,128)S(1)} %copy.21.seg, bf16[24,512,128]{2,1,0:T(8,128)(2,1)S(1)} %copy-done, ...), custom_call_target="tpu_custom_call" | custom-call | flops 268435456 | bytes 1048576 | tf_op jit(solution)/shard_map/pallas_call | solution.py:251
  66.2 1.1 collective-permute-done.15
  68.4 3.7 %shard_map.106.rest_5_ = f32[2,256,1792]{2,1,0:T(8,128)S(1)} custom-call(bf16[64,2560]{1,0:T(8,128)(2,1)S(1)} %get-tuple-element.51.rest_16_.rest_0_, bf16[64,2560]{1,0:T(8,128)(2,1)S(1)} %collective-permute-done.12.rest_17_.rest_1_, bf16[64,2560]{1,0:T(8,128)(2,1)S(1)} %collective-permute-done.13.rest_18_.rest_2_, ...), custom_call_target="tpu_custom_call", output_to_operand_aliasing={{}: (5, {})} | custom-call | flops 1342177280 | bytes 5242880 | tf_op jit(solution)/shard_map/pallas_call | solution.py:181
  72.6 3.7 %shard_map.107.rest_5_ = f32[2,256,1792]{2,1,0:T(8,128)S(1)} custom-call(bf16[64,2560]{1,0:T(8,128)(2,1)S(1)} %get-tuple-element.51.rest_16_.rest_0_, bf16[64,2560]{1,0:T(8,128)(2,1)S(1)} %collective-permute-done.12.rest_17_.rest_1_, bf16[64,2560]{1,0:T(8,128)(2,1)S(1)} %collective-permute-done.13.rest_18_.rest_2_, ...), custom_call_target="tpu_custom_call", output_to_operand_aliasing={{}: (5, {})} | custom-call | flops 1342177280 | bytes 5242880 | tf_op jit(solution)/shard_map/pallas_call | solution.py:181
  76.5 3.3 %collective-permute-start.18 = (f32[128,128]{1,0:T(8,128)S(1)}, f32[128,128]{1,0:T(8,128)S(1)}, u32[]{:S(2)}, u32[]{:S(2)}) collective-permute-start(f32[128,128]{1,0:T(8,128)S(1)} %add.289), channel_id=1, source_target_pairs={{0,8},{1,9},{2,10},{3,11},{4,12},{5,13},{6,14},{7,15},{8,0},{9,1},... | collective-permute-start | bytes 196616 | tf_op jit(solution)/shard_map/ppermute | solution.py:94
  79.8 4.6 %shard_map.108.base = f32[2,256,1792]{2,1,0:T(8,128)S(1)} custom-call(bf16[64,2560]{1,0:T(8,128)(2,1)S(1)} %get-tuple-element.51.rest_16_.rest_0_, bf16[64,2560]{1,0:T(8,128)(2,1)S(1)} %collective-permute-done.12.rest_17_.rest_1_, bf16[64,2560]{1,0:T(8,128)(2,1)S(1)} %collective-permute-done.13.rest_18_.rest_2_, ...), custom_call_target="tpu_custom_call", output_to_operand_aliasing={{}: (5, {})} | custom-call | flops 2013265920 | bytes 7864320 | tf_op jit(solution)/shard_map/pallas_call | solution.py:181
  84.7 1.1 collective-permute-done.19
  85.9 7.5 %shard_map.109 = (bf16[256,1792]{1,0:T(8,128)(2,1)S(1)}, bf16[256,1792]{1,0:T(8,128)(2,1)S(1)}, f32[256,128]{1,0:T(8,128)S(1)}) custom-call(s32[8]{0:T(128)S(1)} %bitcast.49, s32[16]{0:T(128)S(1)} %get-tuple-element.82.places, f32[2,256,1792]{2,1,0:T(8,128)S(1)} %shard_map.108.base, bf16[256,1792]{1,0:T(8,128)(2,1)S(1)} %copy-done.9, ...), custom_call_target="tpu_custom_call" | custom-call | flops 1879048192 | bytes 10092544 | tf_op jit(solution)/shard_map/pallas_call | solution.py:329
  94.7 1.1 collective-permute-start.21
  95.9 3.6 %shard_map.110.rest_0_ = f32[24,128,1792]{2,1,0:T(8,128)} custom-call(bf16[256,1792]{1,0:T(8,128)(2,1)S(1)} %get-tuple-element.69.dgate, bf16[256,1792]{1,0:T(8,128)(2,1)S(1)} %get-tuple-element.55.dup, bf16[256,256]{1,0:T(8,128)(2,1)S(1)} %fusion.1.order, bf16[256,128]{1,0:T(8,128)(2,1)S(1)} %bitcast.38, s32[1,256]{1,0:T(1,128)S(1)} %bitcast.43), custom_call_target="tpu_custom_call" | custom-call | flops 805306368 | bytes 6291456 | tf_op jit(solution)/shard_map/pallas_call | solution.py:404
  99.5 1.4 collective-permute-start.22
  100.9 3.6 %shard_map.111.rest_0_ = f32[24,128,1792]{2,1,0:T(8,128)} custom-call(bf16[256,1792]{1,0:T(8,128)(2,1)S(1)} %get-tuple-element.69.dgate, bf16[256,1792]{1,0:T(8,128)(2,1)S(1)} %get-tuple-element.55.dup, bf16[256,256]{1,0:T(8,128)(2,1)S(1)} %fusion.1.order, bf16[256,128]{1,0:T(8,128)(2,1)S(1)} %bitcast.39, ...), custom_call_target="tpu_custom_call", output_to_operand_aliasing={{}: (5, {})} | custom-call | flops 805306368 | bytes 6291456 | tf_op jit(solution)/shard_map/pallas_call | solution.py:404
  104.8 11.5 %shard_map.112 = (bf16[128,4096]{1,0:T(8,128)(2,1)S(1)}, bf16[128,4096]{1,0:T(8,128)(2,1)S(1)}) custom-call(bf16[2,8192,1792]{2,1,0:T(8,128)(2,1)} %frozen.3, bf16[256,1792]{1,0:T(8,128)(2,1)S(1)} %get-tuple-element.69.dgate, bf16[256,1792]{1,0:T(8,128)(2,1)S(1)} %get-tuple-element.55.dup), custom_call_target="tpu_custom_call" | custom-call | flops 7516192768 | bytes 29360128 | tf_op jit(solution)/shard_map/pallas_call | solution.py:520
  116.7 1.1 collective-permute-done.24
  118.0 1.4 shard_map.113
  119.9 1.1 collective-permute-done.26.side_far
  121.0 1.4 shard_map.114
  123.4 11.5 %shard_map.115 = (bf16[128,4096]{1,0:T(8,128)(2,1)S(1)}, bf16[128,4096]{1,0:T(8,128)(2,1)S(1)}) custom-call(bf16[2,8192,1792]{2,1,0:T(8,128)(2,1)} %frozen.3, bf16[256,1792]{1,0:T(8,128)(2,1)S(1)} %get-tuple-element.69.dgate, bf16[256,1792]{1,0:T(8,128)(2,1)S(1)} %get-tuple-element.55.dup), custom_call_target="tpu_custom_call" | custom-call | flops 7516192768 | bytes 29360128 | tf_op jit(solution)/shard_map/pallas_call | solution.py:520
  135.0 1.7 collective-permute-done.27
  136.8 2.5 %collective-permute-done.29.far = bf16[128,4096]{1,0:T(8,128)(2,1)S(1)} collective-permute-done((bf16[128,4096]{1,0:T(8,128)(2,1)S(1)}, bf16[128,4096]{1,0:T(8,128)(2,1)S(1)}, u32[]{:S(2)}, u32[]{:S(2)}) %collective-permute-start.29) | collective-permute-done | bytes 1048608 | tf_op jit(solution)/shard_map/ppermute | solution.py:67
  139.3 2.5 %shard_map.116 = (bf16[64,4096]{1,0:T(8,128)(2,1)S(1)}, bf16[64,4096]{1,0:T(8,128)(2,1)}) custom-call(s32[2]{0:T(128)S(1)} %pad_add_fusion.at, bf16[128,4096]{1,0:T(8,128)(2,1)S(1)} %get-tuple-element.70.near, bf16[128,4096]{1,0:T(8,128)(2,1)S(1)} %collective-permute-done.29.far, f32[128,512]{1,0:T(8,128)S(1)} %get-tuple-element.65.side, ...), custom_call_target="tpu_custom_call" | custom-call | flops 1048576 | bytes 3145728 | tf_op jit(solution)/shard_map/pallas_call | solution.py:562
  143.5 2.9 %collective-permute-start.32 = (bf16[16,4096]{1,0:T(8,128)(2,1)}, bf16[16,4096]{1,0:T(8,128)(2,1)S(1)}, u32[]{:S(2)}, u32[]{:S(2)}) collective-permute-start(bf16[16,4096]{1,0:T(8,128)(2,1)} %get-tuple-element.87), channel_id=1, source_target_pairs={{0,12},{1,13},{2,14},{3,15},{4,0},{5,1},{6,2},{7,3},{8,4},{9,5},{1... | collective-permute-start | bytes 393224 | tf_op jit(solution)/shard_map/ppermute | solution.py:67
  146.4 1.9 %collective-permute-start.28 = (bf16[16,4096]{1,0:T(8,128)(2,1)S(1)}, bf16[16,4096]{1,0:T(8,128)(2,1)S(1)}, u32[]{:S(2)}, u32[]{:S(2)}) collective-permute-start(bf16[16,4096]{1,0:T(8,128)(2,1)S(1)} %get-tuple-element.86), channel_id=1, source_target_pairs={{0,4},{1,5},{2,6},{3,7},{4,8},{5,9},{6,10},{7,11},{8,12},{9,13},{1... | collective-permute-start | bytes 393224 | tf_op jit(solution)/shard_map/ppermute | solution.py:67
  148.4 4.7 %shard_map.117 = f32[24,512,128]{2,1,0:T(8,128)} custom-call(bf16[256,512]{1,0:T(8,128)(2,1)S(1)} %copy-done.11, bf16[256,256]{1,0:T(8,128)(2,1)S(1)} %fusion.1.order, bf16[256,128]{1,0:T(8,128)(2,1)S(1)} %bitcast.42, s32[256,1]{1,0:T(8,128)S(1)} %copy.24.adapter), custom_call_target="tpu_custom_call" | custom-call | flops 805306368 | bytes 6291456 | tf_op jit(solution)/shard_map/pallas_call | solution.py:448
  153.1 3.0 %collective-permute-done.30 = bf16[64,4096]{1,0:T(8,128)(2,1)} collective-permute-done((bf16[64,4096]{1,0:T(8,128)(2,1)}, bf16[64,4096]{1,0:T(8,128)(2,1)}, u32[]{:S(2)}, u32[]{:S(2)}) %collective-permute-start.30) | collective-permute-done | bytes 524320 | tf_op jit(solution)/shard_map/ppermute | solution.py:67
  156.1 2.3 %collective-permute-done.31 = bf16[16,4096]{1,0:T(8,128)(2,1)S(1)} collective-permute-done((bf16[16,4096]{1,0:T(8,128)(2,1)}, bf16[16,4096]{1,0:T(8,128)(2,1)S(1)}, u32[]{:S(2)}, u32[]{:S(2)}) %collective-permute-start.31) | collective-permute-done | bytes 131104 | tf_op jit(solution)/shard_map/ppermute | solution.py:67
  158.4 1.2 add_convert_fusion
  160.5 2.9 %collective-permute-start.35 = (bf16[16,4096]{1,0:T(8,128)(2,1)S(1)}, bf16[16,4096]{1,0:T(8,128)(2,1)S(1)}, u32[]{:S(2)}, u32[]{:S(2)}) collective-permute-start(bf16[16,4096]{1,0:T(8,128)(2,1)S(1)} %get-tuple-element.90), channel_id=1, source_target_pairs={{0,12},{1,13},{2,14},{3,15},{4,0},{5,1},{6,2},{7,3},{8,4},{9,5},{1... | collective-permute-start | bytes 393224 | tf_op jit(solution)/shard_map/ppermute | solution.py:67
  165.4 2.4 %collective-permute-done.33 = bf16[16,4096]{1,0:T(8,128)(2,1)S(1)} collective-permute-done((bf16[16,4096]{1,0:T(8,128)(2,1)S(1)}, bf16[16,4096]{1,0:T(8,128)(2,1)S(1)}, u32[]{:S(2)}, u32[]{:S(2)}) %collective-permute-start.33) | collective-permute-done | bytes 131104 | tf_op jit(solution)/shard_map/ppermute | solution.py:67
  167.9 4.6 %shard_map.118 = f32[24,128,1792]{2,1,0:T(8,128)} custom-call(bf16[256,1792]{1,0:T(8,128)(2,1)S(1)} %get-tuple-element.69.dgate, bf16[256,1792]{1,0:T(8,128)(2,1)S(1)} %get-tuple-element.55.dup, bf16[256,256]{1,0:T(8,128)(2,1)S(1)} %fusion.1.order, bf16[256,128]{1,0:T(8,128)(2,1)S(1)} %bitcast.40, ...), custom_call_target="tpu_custom_call", output_to_operand_aliasing={{}: (5, {})} | custom-call | flops 1207959552 | bytes 9437184 | tf_op jit(solution)/shard_map/pallas_call | solution.py:404
  172.5 2.2 %collective-permute-done.34 = bf16[16,4096]{1,0:T(8,128)(2,1)S(1)} collective-permute-done((bf16[16,4096]{1,0:T(8,128)(2,1)S(1)}, bf16[16,4096]{1,0:T(8,128)(2,1)S(1)}, u32[]{:S(2)}, u32[]{:S(2)}) %collective-permute-start.34) | collective-permute-done | bytes 131104 | tf_op jit(solution)/shard_map/ppermute | solution.py:67
  (137 shorter events, 20.9 us)
Async XLA Ops:
  1.5 11.0 %collective-permute-start.1 = (bf16[16,3072]{1,0:T(8,128)(2,1)S(1)}, bf16[16,3072]{1,0:T(8,128)(2,1)S(1)}, u32[]{:S(2)}, u32[]{:S(2)}) collective-permute-start(bf16[16,3072]{1,0:T(8,128)(2,1)S(1)} %get-tuple-element.93), channel_id=1, source_target_pairs={{0,8},{1,9},{2,10},{3,11},{4,12},{5,13},{6,14},{7,15},{8,0},{9,1},... | collective-permute-start | bytes 294920 | tf_op jit(solution)/shard_map/ppermute | solution.py:67
  5.6 6.9 %collective-permute-start = (bf16[16,3072]{1,0:T(8,128)(2,1)S(1)}, bf16[16,3072]{1,0:T(8,128)(2,1)S(1)}, u32[]{:S(2)}, u32[]{:S(2)}) collective-permute-start(bf16[16,3072]{1,0:T(8,128)(2,1)S(1)} %get-tuple-element.93), channel_id=1, source_target_pairs={{0,12},{1,13},{2,14},{3,15},{4,0},{5,1},{6,2},{7,3},{8,4},{9,5},{1... | collective-permute-start | bytes 294920 | tf_op jit(solution)/shard_map/ppermute | solution.py:67
  7.0 6.8 %collective-permute-start.2 = (bf16[16,3072]{1,0:T(8,128)(2,1)S(1)}, bf16[16,3072]{1,0:T(8,128)(2,1)S(1)}, u32[]{:S(2)}, u32[]{:S(2)}) collective-permute-start(bf16[16,3072]{1,0:T(8,128)(2,1)S(1)} %get-tuple-element.93), channel_id=1, source_target_pairs={{0,4},{1,5},{2,6},{3,7},{4,8},{5,9},{6,10},{7,11},{8,12},{9,13},{1... | collective-permute-start | bytes 294920 | tf_op jit(solution)/shard_map/ppermute | solution.py:67
  13.9 8.1 %collective-permute-start.5 = (bf16[16,5120]{1,0:T(8,128)(2,1)S(1)}, bf16[16,5120]{1,0:T(8,128)(2,1)S(1)}, u32[]{:S(2)}, u32[]{:S(2)}) collective-permute-start(bf16[16,5120]{1,0:T(8,128)(2,1)S(1)} %slice.60), channel_id=1, source_target_pairs={{0,4},{1,5},{2,6},{3,7},{4,8},{5,9},{6,10},{7,11},{8,12},{9,13},{1... | collective-permute-start | bytes 491528 | tf_op jit(solution)/shard_map/ppermute | solution.py:67
  15.6 12.5 %collective-permute-start.4 = (bf16[16,5120]{1,0:T(8,128)(2,1)S(1)}, bf16[16,5120]{1,0:T(8,128)(2,1)S(1)}, u32[]{:S(2)}, u32[]{:S(2)}) collective-permute-start(bf16[16,5120]{1,0:T(8,128)(2,1)S(1)} %slice.60), channel_id=1, source_target_pairs={{0,8},{1,9},{2,10},{3,11},{4,12},{5,13},{6,14},{7,15},{8,0},{9,1},... | collective-permute-start | bytes 491528 | tf_op jit(solution)/shard_map/ppermute | solution.py:67
  17.6 10.5 %collective-permute-start.3 = (bf16[16,5120]{1,0:T(8,128)(2,1)S(1)}, bf16[16,5120]{1,0:T(8,128)(2,1)S(1)}, u32[]{:S(2)}, u32[]{:S(2)}) collective-permute-start(bf16[16,5120]{1,0:T(8,128)(2,1)S(1)} %slice.60), channel_id=1, source_target_pairs={{0,12},{1,13},{2,14},{3,15},{4,0},{5,1},{6,2},{7,3},{8,4},{9,5},{1... | collective-permute-start | bytes 491528 | tf_op jit(solution)/shard_map/ppermute | solution.py:67
  20.4 13.7 %collective-permute-start.7 = (bf16[64,3072]{1,0:T(8,128)(2,1)S(1)}, bf16[64,3072]{1,0:T(8,128)(2,1)S(1)}, u32[]{:S(2)}, u32[]{:S(2)}) collective-permute-start(bf16[64,3072]{1,0:T(8,128)(2,1)S(1)} %bitcast.33), channel_id=1, source_target_pairs={{0,1},{1,0},{2,3},{3,2},{4,5},{5,4},{6,7},{7,6},{8,9},{9,8},{10,11... | collective-permute-start | bytes 1179656 | tf_op jit(solution)/shard_map/ppermute | solution.py:67
  20.4 11.5 %collective-permute-start.6 = (bf16[64,3072]{1,0:T(8,128)(2,1)S(1)}, bf16[64,3072]{1,0:T(8,128)(2,1)S(1)}, u32[]{:S(2)}, u32[]{:S(2)}) collective-permute-start(bf16[64,3072]{1,0:T(8,128)(2,1)S(1)} %bitcast.34), channel_id=1, source_target_pairs={{0,2},{1,3},{2,0},{3,1},{4,6},{5,7},{6,4},{7,5},{8,10},{9,11},{10,... | collective-permute-start | bytes 1179656 | tf_op jit(solution)/shard_map/ppermute | solution.py:67
  32.0 2.1 %collective-permute-start.8 = (bf16[64,3072]{1,0:T(8,128)(2,1)S(1)}, bf16[64,3072]{1,0:T(8,128)(2,1)S(1)}, u32[]{:S(2)}, u32[]{:S(2)}) collective-permute-start(bf16[64,3072]{1,0:T(8,128)(2,1)S(1)} %collective-permute-done.6.rest_1_.rest_9_), channel_id=1, source_target_pairs={{0,1},{1,0},{2,3},{3,2},{4,5},{5,4},{6,7},{7,6},{8,9},{9,8},{10,11... | collective-permute-start | bytes 1179656 | tf_op jit(solution)/shard_map/ppermute | solution.py:67
  32.0 15.4 %collective-permute-start.10 = (bf16[64,2560]{1,0:T(8,128)(2,1)S(1)}, bf16[64,2560]{1,0:T(8,128)(2,1)S(1)}, u32[]{:S(2)}, u32[]{:S(2)}) collective-permute-start(bf16[64,2560]{1,0:T(8,128)(2,1)S(1)} %get-tuple-element.84.rest_0_.rest_12_), channel_id=1, source_target_pairs={{0,1},{1,0},{2,3},{3,2},{4,5},{5,4},{6,7},{7,6},{8,9},{9,8},{10,11... | collective-permute-start | bytes 983048 | tf_op jit(solution)/shard_map/ppermute | solution.py:67
  32.6 12.8 %collective-permute-start.9 = (bf16[64,2560]{1,0:T(8,128)(2,1)S(1)}, bf16[64,2560]{1,0:T(8,128)(2,1)S(1)}, u32[]{:S(2)}, u32[]{:S(2)}) collective-permute-start(bf16[64,2560]{1,0:T(8,128)(2,1)S(1)} %get-tuple-element.84.rest_0_.rest_12_), channel_id=1, source_target_pairs={{0,2},{1,3},{2,0},{3,1},{4,6},{5,7},{6,4},{7,5},{8,10},{9,11},{10,... | collective-permute-start | bytes 983048 | tf_op jit(solution)/shard_map/ppermute | solution.py:67
  34.1 9.4 %copy-start.5 = (bf16[64,3072]{1,0:T(8,128)(2,1)}, bf16[64,3072]{1,0:T(8,128)(2,1)S(1)}, u32[]{:S(2)}) copy-start(bf16[64,3072]{1,0:T(8,128)(2,1)S(1)} %collective-permute-done.8.rest_3_.rest_11_) | copy-start | bytes 1179652
  45.4 13.5 %copy-start.7 = (bf16[64,2560]{1,0:T(8,128)(2,1)}, bf16[64,2560]{1,0:T(8,128)(2,1)S(1)}, u32[]{:S(2)}) copy-start(bf16[64,2560]{1,0:T(8,128)(2,1)S(1)} %collective-permute-done.9.rest_1_.rest_13_) | copy-start | bytes 983044
  45.4 2.0 %collective-permute-start.11 = (bf16[64,2560]{1,0:T(8,128)(2,1)S(1)}, bf16[64,2560]{1,0:T(8,128)(2,1)}, u32[]{:S(2)}, u32[]{:S(2)}) collective-permute-start(bf16[64,2560]{1,0:T(8,128)(2,1)S(1)} %collective-permute-done.9.rest_1_.rest_13_), channel_id=1, source_target_pairs={{0,1},{1,0},{2,3},{3,2},{4,5},{5,4},{6,7},{7,6},{8,9},{9,8},{10,11... | collective-permute-start | bytes 983048 | tf_op jit(solution)/shard_map/ppermute | solution.py:67
  45.7 15.1 %copy-start.14 = (s32[256]{0:T(256)S(1)}, s32[256]{0:T(256)}, u32[]{:S(2)}) copy-start(s32[256]{0:T(256)} %add.293) | copy-start | bytes 3076
  45.7 16.6 %copy-start.12 = (s32[1,8]{1,0:T(1,128)S(1)}, s32[1,8]{1,0:T(1,128)}, u32[]{:S(2)}) copy-start(s32[1,8]{1,0:T(1,128)} %param.13) | copy-start | bytes 100
  45.7 16.6 %copy-start = (bf16[24,512,128]{2,1,0:T(8,128)(2,1)S(1)}, bf16[24,512,128]{2,1,0:T(8,128)(2,1)}, u32[]{:S(2)}) copy-start(bf16[24,512,128]{2,1,0:T(8,128)(2,1)} %rest_7_.3) | copy-start | bytes 9437188
  45.8 15.2 %collective-permute-start.13 = (bf16[64,2560]{1,0:T(8,128)(2,1)S(1)}, bf16[64,2560]{1,0:T(8,128)(2,1)S(1)}, u32[]{:S(2)}, u32[]{:S(2)}) collective-permute-start(bf16[64,2560]{1,0:T(8,128)(2,1)S(1)} %get-tuple-element.51.rest_16_.rest_0_), channel_id=1, source_target_pairs={{0,1},{1,0},{2,3},{3,2},{4,5},{5,4},{6,7},{7,6},{8,9},{9,8},{10,11... | collective-permute-start | bytes 983048 | tf_op jit(solution)/shard_map/ppermute | solution.py:67
  46.3 14.4 %collective-permute-start.12 = (bf16[64,2560]{1,0:T(8,128)(2,1)S(1)}, bf16[64,2560]{1,0:T(8,128)(2,1)S(1)}, u32[]{:S(2)}, u32[]{:S(2)}) collective-permute-start(bf16[64,2560]{1,0:T(8,128)(2,1)S(1)} %get-tuple-element.51.rest_16_.rest_0_), channel_id=1, source_target_pairs={{0,2},{1,3},{2,0},{3,1},{4,6},{5,7},{6,4},{7,5},{8,10},{9,11},{10,... | collective-permute-start | bytes 983048 | tf_op jit(solution)/shard_map/ppermute | solution.py:67
  49.4 12.9 %copy-start.6 = (bf16[64,3072]{1,0:T(8,128)(2,1)S(1)}, bf16[64,3072]{1,0:T(8,128)(2,1)}, u32[]{:S(2)}) copy-start(bf16[64,3072]{1,0:T(8,128)(2,1)} %copy-done.5) | copy-start | bytes 1179652
  60.7 1.6 collective-permute-start.14
  66.0 1.3 collective-permute-start.15
  67.3 4.7 %collective-permute-start.16 = (f32[128,128]{1,0:T(8,128)S(1)}, f32[128,128]{1,0:T(8,128)S(1)}, u32[]{:S(2)}, u32[]{:S(2)}) collective-permute-start(f32[128,128]{1,0:T(8,128)S(1)} %slice_add_fusion.1), channel_id=1, source_target_pairs={{0,2},{1,3},{2,0},{3,1},{4,6},{5,7},{6,4},{7,5},{8,10},{9,11},{10,... | collective-permute-start | bytes 196616 | tf_op jit(solution)/shard_map/ppermute | solution.py:94
  72.1 4.3 %collective-permute-start.17 = (f32[128,128]{1,0:T(8,128)S(1)}, f32[128,128]{1,0:T(8,128)S(1)}, u32[]{:S(2)}, u32[]{:S(2)}) collective-permute-start(f32[128,128]{1,0:T(8,128)S(1)} %add.288), channel_id=1, source_target_pairs={{0,4},{1,5},{2,6},{3,7},{4,0},{5,1},{6,2},{7,3},{8,12},{9,13},{10,... | collective-permute-start | bytes 196616 | tf_op jit(solution)/shard_map/ppermute | solution.py:94
  76.4 9.4 %slice-start = ((s8[11010048]{0:T(1024)(128)(4,1)}), s8[4194304]{0:T(1024)(128)(4,1)S(1)}, s32[]{:S(2)}) async-start(s8[11010048]{0:T(1024)(128)(4,1)} %bitcast.31), calls=%async_computation | async-start | bytes 8388608
  76.4 9.4 %slice-start.1 = ((s8[11010048]{0:T(1024)(128)(4,1)}), s8[4194304]{0:T(1024)(128)(4,1)S(1)}, s32[]{:S(2)}) async-start(s8[11010048]{0:T(1024)(128)(4,1)} %bitcast.31), calls=%async_computation.1 | async-start | bytes 8388608
  76.4 9.4 %slice-start.2 = ((s8[11010048]{0:T(1024)(128)(4,1)}), s8[2621440]{0:T(1024)(128)(4,1)S(1)}, s32[]{:S(2)}) async-start(s8[11010048]{0:T(1024)(128)(4,1)} %bitcast.31), calls=%async_computation.2 | async-start | bytes 5242880
  76.5 9.4 %copy-start.9 = (bf16[256,1792]{1,0:T(8,128)(2,1)S(1)}, bf16[256,1792]{1,0:T(8,128)(2,1)}, u32[]{:S(2)}) copy-start(bf16[256,1792]{1,0:T(8,128)(2,1)} %dhidden.1) | copy-start | bytes 2752516
  76.5 7.9 %collective-permute-start.18 = (f32[128,128]{1,0:T(8,128)S(1)}, f32[128,128]{1,0:T(8,128)S(1)}, u32[]{:S(2)}, u32[]{:S(2)}) collective-permute-start(f32[128,128]{1,0:T(8,128)S(1)} %add.289), channel_id=1, source_target_pairs={{0,8},{1,9},{2,10},{3,11},{4,12},{5,13},{6,14},{7,15},{8,0},{9,1},... | collective-permute-start | bytes 196616 | tf_op jit(solution)/shard_map/ppermute | solution.py:94
  84.5 1.3 collective-permute-start.19
  93.4 1.3 collective-permute-start.20
  94.7 4.8 %collective-permute-start.21 = (f32[128,128]{1,0:T(8,128)S(1)}, f32[128,128]{1,0:T(8,128)S(1)}, u32[]{:S(2)}, u32[]{:S(2)}) collective-permute-start(f32[128,128]{1,0:T(8,128)S(1)} %slice_add_fusion), channel_id=1, source_target_pairs={{0,2},{1,3},{2,0},{3,1},{4,6},{5,7},{6,4},{7,5},{8,10},{9,11},{10,... | collective-permute-start | bytes 196616 | tf_op jit(solution)/shard_map/ppermute | solution.py:94
  99.5 5.0 %collective-permute-start.22 = (f32[128,128]{1,0:T(8,128)S(1)}, f32[128,128]{1,0:T(8,128)S(1)}, u32[]{:S(2)}, u32[]{:S(2)}) collective-permute-start(f32[128,128]{1,0:T(8,128)S(1)} %add.303), channel_id=1, source_target_pairs={{0,4},{1,5},{2,6},{3,7},{4,0},{5,1},{6,2},{7,3},{8,12},{9,13},{10,... | collective-permute-start | bytes 196616 | tf_op jit(solution)/shard_map/ppermute | solution.py:94
  104.6 11.8 %collective-permute-start.23 = (f32[128,128]{1,0:T(8,128)S(1)}, f32[128,128]{1,0:T(8,128)S(1)}, u32[]{:S(2)}, u32[]{:S(2)}) collective-permute-start(f32[128,128]{1,0:T(8,128)S(1)} %add.304), channel_id=1, source_target_pairs={{0,8},{1,9},{2,10},{3,11},{4,12},{5,13},{6,14},{7,15},{8,0},{9,1},... | collective-permute-start | bytes 196616 | tf_op jit(solution)/shard_map/ppermute | solution.py:94
  116.5 1.3 collective-permute-start.24
  117.8 3.2 %collective-permute-start.25 = (bf16[128,4096]{1,0:T(8,128)(2,1)S(1)}, bf16[128,4096]{1,0:T(8,128)(2,1)S(1)}, u32[]{:S(2)}, u32[]{:S(2)}) collective-permute-start(bf16[128,4096]{1,0:T(8,128)(2,1)S(1)} %get-tuple-element.64), channel_id=1, source_target_pairs={{0,1},{1,0},{2,3},{3,2},{4,5},{5,4},{6,7},{7,6},{8,9},{9,8},{10,11... | collective-permute-start | bytes 3145736 | tf_op jit(solution)/shard_map/ppermute | solution.py:67
  119.3 1.6 collective-permute-start.26
  122.4 26.0 %copy-start.11 = (bf16[256,512]{1,0:T(8,128)(2,1)S(1)}, bf16[256,512]{1,0:T(8,128)(2,1)}, u32[]{:S(2)}) copy-start(bf16[256,512]{1,0:T(8,128)(2,1)} %copy-done.10) | copy-start | bytes 786436
  122.4 14.3 %collective-permute-start.27 = (bf16[64,4096]{1,0:T(8,128)(2,1)S(1)}, bf16[64,4096]{1,0:T(8,128)(2,1)S(1)}, u32[]{:S(2)}, u32[]{:S(2)}) collective-permute-start(bf16[64,4096]{1,0:T(8,128)(2,1)S(1)} %get-tuple-element.68), channel_id=1, source_target_pairs={{0,2},{1,3},{2,0},{3,1},{4,6},{5,7},{6,4},{7,5},{8,10},{9,11},{10,... | collective-permute-start | bytes 1572872 | tf_op jit(solution)/shard_map/ppermute | solution.py:67
  136.7 2.7 %collective-permute-start.29 = (bf16[128,4096]{1,0:T(8,128)(2,1)S(1)}, bf16[128,4096]{1,0:T(8,128)(2,1)S(1)}, u32[]{:S(2)}, u32[]{:S(2)}) collective-permute-start(bf16[128,4096]{1,0:T(8,128)(2,1)S(1)} %get-tuple-element.72), channel_id=1, source_target_pairs={{0,1},{1,0},{2,3},{3,2},{4,5},{5,4},{6,7},{7,6},{8,9},{9,8},{10,11... | collective-permute-start | bytes 3145736 | tf_op jit(solution)/shard_map/ppermute | solution.py:67
  136.8 11.4 %copy-start.13 = (bf16[64,4096]{1,0:T(8,128)(2,1)}, bf16[64,4096]{1,0:T(8,128)(2,1)S(1)}, u32[]{:S(2)}) copy-start(bf16[64,4096]{1,0:T(8,128)(2,1)S(1)} %add_convert_fusion.1) | copy-start | bytes 1572868
  141.8 14.3 %collective-permute-start.30 = (bf16[64,4096]{1,0:T(8,128)(2,1)}, bf16[64,4096]{1,0:T(8,128)(2,1)}, u32[]{:S(2)}, u32[]{:S(2)}) collective-permute-start(bf16[64,4096]{1,0:T(8,128)(2,1)} %get-tuple-element.73), channel_id=1, source_target_pairs={{0,2},{1,3},{2,0},{3,1},{4,6},{5,7},{6,4},{7,5},{8,10},{9,11},{10,... | collective-permute-start | bytes 1572872 | tf_op jit(solution)/shard_map/ppermute | solution.py:67
  143.5 9.6 %collective-permute-start.32 = (bf16[16,4096]{1,0:T(8,128)(2,1)}, bf16[16,4096]{1,0:T(8,128)(2,1)S(1)}, u32[]{:S(2)}, u32[]{:S(2)}) collective-permute-start(bf16[16,4096]{1,0:T(8,128)(2,1)} %get-tuple-element.87), channel_id=1, source_target_pairs={{0,12},{1,13},{2,14},{3,15},{4,0},{5,1},{6,2},{7,3},{8,4},{9,5},{1... | collective-permute-start | bytes 393224 | tf_op jit(solution)/shard_map/ppermute | solution.py:67
  146.4 12.0 %collective-permute-start.31 = (bf16[16,4096]{1,0:T(8,128)(2,1)}, bf16[16,4096]{1,0:T(8,128)(2,1)S(1)}, u32[]{:S(2)}, u32[]{:S(2)}) collective-permute-start(bf16[16,4096]{1,0:T(8,128)(2,1)} %get-tuple-element.88), channel_id=1, source_target_pairs={{0,8},{1,9},{2,10},{3,11},{4,12},{5,13},{6,14},{7,15},{8,0},{9,1},... | collective-permute-start | bytes 393224 | tf_op jit(solution)/shard_map/ppermute | solution.py:67
  146.4 12.0 %collective-permute-start.28 = (bf16[16,4096]{1,0:T(8,128)(2,1)S(1)}, bf16[16,4096]{1,0:T(8,128)(2,1)S(1)}, u32[]{:S(2)}, u32[]{:S(2)}) collective-permute-start(bf16[16,4096]{1,0:T(8,128)(2,1)S(1)} %get-tuple-element.86), channel_id=1, source_target_pairs={{0,4},{1,5},{2,6},{3,7},{4,8},{5,9},{6,10},{7,11},{8,12},{9,13},{1... | collective-permute-start | bytes 393224 | tf_op jit(solution)/shard_map/ppermute | solution.py:67
  159.6 8.3 %collective-permute-start.33 = (bf16[16,4096]{1,0:T(8,128)(2,1)S(1)}, bf16[16,4096]{1,0:T(8,128)(2,1)S(1)}, u32[]{:S(2)}, u32[]{:S(2)}) collective-permute-start(bf16[16,4096]{1,0:T(8,128)(2,1)S(1)} %get-tuple-element.89), channel_id=1, source_target_pairs={{0,4},{1,5},{2,6},{3,7},{4,8},{5,9},{6,10},{7,11},{8,12},{9,13},{1... | collective-permute-start | bytes 393224 | tf_op jit(solution)/shard_map/ppermute | solution.py:67
  160.5 12.0 %collective-permute-start.35 = (bf16[16,4096]{1,0:T(8,128)(2,1)S(1)}, bf16[16,4096]{1,0:T(8,128)(2,1)S(1)}, u32[]{:S(2)}, u32[]{:S(2)}) collective-permute-start(bf16[16,4096]{1,0:T(8,128)(2,1)S(1)} %get-tuple-element.90), channel_id=1, source_target_pairs={{0,12},{1,13},{2,14},{3,15},{4,0},{5,1},{6,2},{7,3},{8,4},{9,5},{1... | collective-permute-start | bytes 393224 | tf_op jit(solution)/shard_map/ppermute | solution.py:67
  163.4 11.3 %collective-permute-start.34 = (bf16[16,4096]{1,0:T(8,128)(2,1)S(1)}, bf16[16,4096]{1,0:T(8,128)(2,1)S(1)}, u32[]{:S(2)}, u32[]{:S(2)}) collective-permute-start(bf16[16,4096]{1,0:T(8,128)(2,1)S(1)} %get-tuple-element.91), channel_id=1, source_target_pairs={{0,8},{1,9},{2,10},{3,11},{4,12},{5,13},{6,14},{7,15},{8,0},{9,1},... | collective-permute-start | bytes 393224 | tf_op jit(solution)/shard_map/ppermute | solution.py:67
  (6 other events, 17.8 us)

commit v11 on v8

--- a/solution.py
+++ b/solution.py
@@ -659,7 +659,7 @@
         near[1:] = lax.optimization_barrier((*near[1:], base if q else outer[-1]))[:-1]
         far = [torus.move(v, 2, -1) for v in near]
         gathered.append([*near, *far])
-        for cut in parts_of(tiles, 2 if q == len(parts) - 1 else 1):
+        for cut in parts_of(tiles, 4 if q == len(parts) - 1 else 1):
             base = forward_chunk(gathered[q], frozen, base, first, cut)
         first += x.shape[1]
 
@@ -713,12 +713,11 @@
             total = total + v.astype(F32)
         inners.append(total.astype(BF16).reshape(a, rows, step))
         outer_moves.append([torus.move(inners[q][k], 0, k) for k in range(1, a)])
-    grad_b = grad_b_part(sums[-1][0])
+    grad_b = grad_b_part(outer_moves[-1][0])
     for q, inner in enumerate(inners):
         total = inner[0].astype(F32)
         for v in outer_moves[q]:
-            behind = (v, *inner_moves[-1], grad_b)
-            v = lax.optimization_barrier(behind)[0] if q < len(cuts) - 1 else v
+            v = lax.optimization_barrier((v, *inner_moves[-1]))[0] if q < len(cuts) - 1 else v
             total = total + v.astype(F32)
         blocks.append(total.astype(BF16))
     dinput = jnp.concatenate(blocks, axis=1)

time: 173 us -> 169 us (0.977)
  waiting for transfers between devices: 40 us -> 36.3 us
    ppermute x6, waiting for transfers between devices: 7.38 us -> 1.04 us  [exchange_sum(): x = x + lax.ppermute(x, 'tensor', pairs)]
    pallas_call x4 -> x6, Pallas kernels: 28.9 us -> 31.5 us  [forward_chunk(): pl.pallas_call(functools.partial(forward_kernel, len(pieces), low, count,...]
    ppermute x30, waiting for transfers between devices: 32.6 us -> 35.2 us  [move(): return lax.ppermute(x, 'tensor', pairs)]
    unnamed x26 -> x16, local copies, waits for them, and re-layouts: 4.32 us -> 1.97 us
  transfers between devices with their start and end apart: 36 -> 36, of which waited for: 18 -> 18; matrix products, arithmetic and copies ran while one was open for 3% -> 4% of each run, Pallas kernels for 41% -> 43%
where the time goes in v11:
time: 169 us
  Pallas kernels  84.2 us (50%)
  waiting for transfers between devices  36.3 us (21%)
  starting transfers between devices  35.6 us (21%)
  other arithmetic  6.3 us (4%)
  local copies, waits for them, and re-layouts  5.54 us (3%)
    ppermute x30, waiting for transfers between devices, move(): return lax.ppermute(x, 'tensor', pairs)  35.2 us
    pallas_call x6, Pallas kernels, forward_chunk(): pl.pallas_call(functools.partial(forward_kernel, len(pieces), low, count,...  31.5 us
    ppermute x30, starting transfers between devices, move(): return lax.ppermute(x, 'tensor', pairs)  28.5 us
    pallas_call x2, Pallas kernels, backward_chunk(): pl.pallas_call(functools.partial(backward_kernel, count, first), grid=(co...  23.1 us
    pallas_call x3, Pallas kernels, grad_b_of(): pl.pallas_call(functools.partial(grad_b_kernel, first, last - first), gri...  11.9 us
    pallas_call x1, Pallas kernels, middle(): pl.pallas_call(functools.partial(middle_kernel, rows), grid_spec=pltpu.Pr...  7.47 us
    ppermute x6, starting transfers between devices, exchange_sum(): x = x + lax.ppermute(x, 'tensor', pairs)  7.05 us
    pallas_call x1, Pallas kernels, grad_a_of(): pl.pallas_call(grad_a_kernel, grid=(adapters // per,), in_specs=[full(col...  4.68 us
  transfers between devices with their start and end apart: 36, of which 18 were waited for; matrix products, arithmetic and copies ran while one was open for 4% of the time, Pallas kernels for 43%

profile of v11, /device:TPU:0, one launch (start us, length us, event | category | flops | bytes accessed | tf_op | source)
XLA Modules:
  0.0 169.1 jit_solution(12729880437880524565)
XLA Ops:
  1.5 4.1 %collective-permute-start.1 = (bf16[16,3072]{1,0:T(8,128)(2,1)S(1)}, bf16[16,3072]{1,0:T(8,128)(2,1)S(1)}, u32[]{:S(2)}, u32[]{:S(2)}) collective-permute-start(bf16[16,3072]{1,0:T(8,128)(2,1)S(1)} %get-tuple-element.81), channel_id=1, source_target_pairs={{0,8},{1,9},{2,10},{3,11},{4,12},{5,13},{6,14},{7,15},{8,0},{9,1},... | collective-permute-start | bytes 294920 | tf_op jit(solution)/shard_map/ppermute | solution.py:67
  5.6 1.3 collective-permute-start
  10.4 1.6 collective-permute-done.1
  12.0 1.8 %collective-permute-done.2 = bf16[16,3072]{1,0:T(8,128)(2,1)S(1)} collective-permute-done((bf16[16,3072]{1,0:T(8,128)(2,1)S(1)}, bf16[16,3072]{1,0:T(8,128)(2,1)S(1)}, u32[]{:S(2)}, u32[]{:S(2)}) %collective-permute-start.2) | collective-permute-done | bytes 98336 | tf_op jit(solution)/shard_map/ppermute | solution.py:67
  13.9 1.7 %collective-permute-start.5 = (bf16[16,5120]{1,0:T(8,128)(2,1)S(1)}, bf16[16,5120]{1,0:T(8,128)(2,1)S(1)}, u32[]{:S(2)}, u32[]{:S(2)}) collective-permute-start(bf16[16,5120]{1,0:T(8,128)(2,1)S(1)} %slice.60), channel_id=1, source_target_pairs={{0,4},{1,5},{2,6},{3,7},{4,8},{5,9},{6,10},{7,11},{8,12},{9,13},{1... | collective-permute-start | bytes 491528 | tf_op jit(solution)/shard_map/ppermute | solution.py:67
  15.6 2.0 %collective-permute-start.4 = (bf16[16,5120]{1,0:T(8,128)(2,1)S(1)}, bf16[16,5120]{1,0:T(8,128)(2,1)S(1)}, u32[]{:S(2)}, u32[]{:S(2)}) collective-permute-start(bf16[16,5120]{1,0:T(8,128)(2,1)S(1)} %slice.60), channel_id=1, source_target_pairs={{0,8},{1,9},{2,10},{3,11},{4,12},{5,13},{6,14},{7,15},{8,0},{9,1},... | collective-permute-start | bytes 491528 | tf_op jit(solution)/shard_map/ppermute | solution.py:67
  17.6 2.8 %collective-permute-start.3 = (bf16[16,5120]{1,0:T(8,128)(2,1)S(1)}, bf16[16,5120]{1,0:T(8,128)(2,1)S(1)}, u32[]{:S(2)}, u32[]{:S(2)}) collective-permute-start(bf16[16,5120]{1,0:T(8,128)(2,1)S(1)} %slice.60), channel_id=1, source_target_pairs={{0,12},{1,13},{2,14},{3,15},{4,0},{5,1},{6,2},{7,3},{8,4},{9,5},{1... | collective-permute-start | bytes 491528 | tf_op jit(solution)/shard_map/ppermute | solution.py:67
  21.5 1.6 collective-permute-start.8
  23.1 5.0 %collective-permute-done.4 = bf16[16,5120]{1,0:T(8,128)(2,1)S(1)} collective-permute-done((bf16[16,5120]{1,0:T(8,128)(2,1)S(1)}, bf16[16,5120]{1,0:T(8,128)(2,1)S(1)}, u32[]{:S(2)}, u32[]{:S(2)}) %collective-permute-start.4) | collective-permute-done | bytes 163872 | tf_op jit(solution)/shard_map/ppermute | solution.py:67
  28.2 4.8 %collective-permute-done.8.rest_1_.rest_9_ = bf16[64,3072]{1,0:T(8,128)(2,1)S(1)} collective-permute-done((bf16[64,3072]{1,0:T(8,128)(2,1)S(1)}, bf16[64,3072]{1,0:T(8,128)(2,1)S(1)}, u32[]{:S(2)}, u32[]{:S(2)}) %collective-permute-start.8) | collective-permute-done | bytes 393248 | tf_op jit(solution)/shard_map/ppermute | solution.py:67
  33.6 1.5 collective-permute-start.7
  35.2 9.2 %shard_map.103.rest_5_ = f32[2,256,1792]{2,1,0:T(8,128)S(1)} custom-call(bf16[64,3072]{1,0:T(8,128)(2,1)S(1)} %bitcast.34, bf16[64,3072]{1,0:T(8,128)(2,1)S(1)} %collective-permute-done.8.rest_1_.rest_9_, bf16[64,3072]{1,0:T(8,128)(2,1)S(1)} %collective-permute-done.9.rest_2_.rest_10_, bf16[64,3072]{1,0:T(8,128)(2,1)S(1)} %collective-permute-done.10.rest_3_.rest_11_, ...), custom_call_target="tpu_custom_call" | custom-call | flops 5637144576 | bytes 22020096 | tf_op jit(solution)/shard_map/pallas_call | solution.py:181
  45.3 1.1 collective-permute-start.6
  46.4 8.4 %shard_map.104.rest_5_ = f32[2,256,1792]{2,1,0:T(8,128)S(1)} custom-call(bf16[64,2560]{1,0:T(8,128)(2,1)S(1)} %get-tuple-element.72.rest_0_.rest_12_, bf16[64,2560]{1,0:T(8,128)(2,1)S(1)} %collective-permute-done.7.rest_1_.rest_13_, bf16[64,2560]{1,0:T(8,128)(2,1)S(1)} %collective-permute-done.11.rest_2_.rest_14_, ...), custom_call_target="tpu_custom_call", output_to_operand_aliasing={{}: (5, {})} | custom-call | flops 4697620480 | bytes 18350080 | tf_op jit(solution)/shard_map/pallas_call | solution.py:181
  55.2 1.4 collective-permute-done.14.rest_3_.rest_19_
  56.6 1.5 shard_map.109
  58.4 1.1 collective-permute-done.15
  59.5 1.2 collective-permute-start.16
  60.7 2.6 %shard_map.105.rest_5_ = f32[2,256,1792]{2,1,0:T(8,128)S(1)} custom-call(bf16[64,2560]{1,0:T(8,128)(2,1)S(1)} %get-tuple-element.73.rest_0_.rest_16_, bf16[64,2560]{1,0:T(8,128)(2,1)S(1)} %collective-permute-done.6.rest_1_.rest_17_, bf16[64,2560]{1,0:T(8,128)(2,1)S(1)} %collective-permute-done.13.rest_2_.rest_18_, ...), custom_call_target="tpu_custom_call", output_to_operand_aliasing={{}: (5, {})} | custom-call | flops 671088640 | bytes 2621440 | tf_op jit(solution)/shard_map/pallas_call | solution.py:181
  63.9 3.7 %shard_map.106.rest_5_ = f32[2,256,1792]{2,1,0:T(8,128)S(1)} custom-call(bf16[64,2560]{1,0:T(8,128)(2,1)S(1)} %get-tuple-element.73.rest_0_.rest_16_, bf16[64,2560]{1,0:T(8,128)(2,1)S(1)} %collective-permute-done.6.rest_1_.rest_17_, bf16[64,2560]{1,0:T(8,128)(2,1)S(1)} %collective-permute-done.13.rest_2_.rest_18_, ...), custom_call_target="tpu_custom_call", output_to_operand_aliasing={{}: (5, {})} | custom-call | flops 1342177280 | bytes 5242880 | tf_op jit(solution)/shard_map/pallas_call | solution.py:181
  68.2 2.3 %collective-permute-start.18 = (f32[128,128]{1,0:T(8,128)S(1)}, f32[128,128]{1,0:T(8,128)S(1)}, u32[]{:S(2)}, u32[]{:S(2)}) collective-permute-start(f32[128,128]{1,0:T(8,128)S(1)} %add.293), channel_id=1, source_target_pairs={{0,8},{1,9},{2,10},{3,11},{4,12},{5,13},{6,14},{7,15},{8,0},{9,1},... | collective-permute-start | bytes 196616 | tf_op jit(solution)/shard_map/ppermute | solution.py:94
  70.4 3.7 %shard_map.107.rest_5_ = f32[2,256,1792]{2,1,0:T(8,128)S(1)} custom-call(bf16[64,2560]{1,0:T(8,128)(2,1)S(1)} %get-tuple-element.73.rest_0_.rest_16_, bf16[64,2560]{1,0:T(8,128)(2,1)S(1)} %collective-permute-done.6.rest_1_.rest_17_, bf16[64,2560]{1,0:T(8,128)(2,1)S(1)} %collective-permute-done.13.rest_2_.rest_18_, ...), custom_call_target="tpu_custom_call", output_to_operand_aliasing={{}: (5, {})} | custom-call | flops 1342177280 | bytes 5242880 | tf_op jit(solution)/shard_map/pallas_call | solution.py:181
  74.3 3.8 %shard_map.108.base = f32[2,256,1792]{2,1,0:T(8,128)S(1)} custom-call(bf16[64,2560]{1,0:T(8,128)(2,1)S(1)} %get-tuple-element.73.rest_0_.rest_16_, bf16[64,2560]{1,0:T(8,128)(2,1)S(1)} %collective-permute-done.6.rest_1_.rest_17_, bf16[64,2560]{1,0:T(8,128)(2,1)S(1)} %collective-permute-done.13.rest_2_.rest_18_, ...), custom_call_target="tpu_custom_call", output_to_operand_aliasing={{}: (5, {})} | custom-call | flops 1342177280 | bytes 5242880 | tf_op jit(solution)/shard_map/pallas_call | solution.py:181
  80.2 7.5 %shard_map.110 = (bf16[256,1792]{1,0:T(8,128)(2,1)S(1)}, bf16[256,1792]{1,0:T(8,128)(2,1)S(1)}, f32[256,128]{1,0:T(8,128)S(1)}) custom-call(s32[8]{0:T(128)S(1)} %bitcast.48, s32[16]{0:T(128)S(1)} %get-tuple-element.70.places, f32[2,256,1792]{2,1,0:T(8,128)S(1)} %shard_map.108.base, bf16[256,1792]{1,0:T(8,128)(2,1)S(1)} %copy-done.1, ...), custom_call_target="tpu_custom_call" | custom-call | flops 1879048192 | bytes 10092544 | tf_op jit(solution)/shard_map/pallas_call | solution.py:329
  87.8 1.2 collective-permute-done.20
  89.0 1.2 collective-permute-start.21
  90.2 3.6 %shard_map.111.rest_0_ = f32[24,128,1792]{2,1,0:T(8,128)} custom-call(bf16[256,1792]{1,0:T(8,128)(2,1)S(1)} %get-tuple-element.57.dgate, bf16[256,1792]{1,0:T(8,128)(2,1)S(1)} %get-tuple-element.43.dup, bf16[256,256]{1,0:T(8,128)(2,1)S(1)} %fusion.1.order, bf16[256,128]{1,0:T(8,128)(2,1)S(1)} %bitcast.37, s32[1,256]{1,0:T(1,128)S(1)} %bitcast.42), custom_call_target="tpu_custom_call" | custom-call | flops 805306368 | bytes 6291456 | tf_op jit(solution)/shard_map/pallas_call | solution.py:404
  94.7 3.6 %shard_map.112.rest_0_ = f32[24,128,1792]{2,1,0:T(8,128)} custom-call(bf16[256,1792]{1,0:T(8,128)(2,1)S(1)} %get-tuple-element.57.dgate, bf16[256,1792]{1,0:T(8,128)(2,1)S(1)} %get-tuple-element.43.dup, bf16[256,256]{1,0:T(8,128)(2,1)S(1)} %fusion.1.order, bf16[256,128]{1,0:T(8,128)(2,1)S(1)} %bitcast.38, ...), custom_call_target="tpu_custom_call", output_to_operand_aliasing={{}: (5, {})} | custom-call | flops 805306368 | bytes 6291456 | tf_op jit(solution)/shard_map/pallas_call | solution.py:404
  98.4 1.5 collective-permute-start.23
  99.9 11.5 %shard_map.113 = (bf16[128,4096]{1,0:T(8,128)(2,1)S(1)}, bf16[128,4096]{1,0:T(8,128)(2,1)S(1)}) custom-call(bf16[2,8192,1792]{2,1,0:T(8,128)(2,1)} %frozen.3, bf16[256,1792]{1,0:T(8,128)(2,1)S(1)} %get-tuple-element.57.dgate, bf16[256,1792]{1,0:T(8,128)(2,1)S(1)} %get-tuple-element.43.dup), custom_call_target="tpu_custom_call" | custom-call | flops 7516192768 | bytes 29360128 | tf_op jit(solution)/shard_map/pallas_call | solution.py:520
  111.7 1.1 collective-permute-done.24
  113.0 1.4 shard_map.114
  114.9 1.1 collective-permute-done.26.side_far
  116.0 1.4 shard_map.115
  118.4 11.5 %shard_map.116 = (bf16[128,4096]{1,0:T(8,128)(2,1)S(1)}, bf16[128,4096]{1,0:T(8,128)(2,1)S(1)}) custom-call(bf16[2,8192,1792]{2,1,0:T(8,128)(2,1)} %frozen.3, bf16[256,1792]{1,0:T(8,128)(2,1)S(1)} %get-tuple-element.57.dgate, bf16[256,1792]{1,0:T(8,128)(2,1)S(1)} %get-tuple-element.43.dup), custom_call_target="tpu_custom_call" | custom-call | flops 7516192768 | bytes 29360128 | tf_op jit(solution)/shard_map/pallas_call | solution.py:520
  129.9 1.8 %collective-permute-done.27 = bf16[64,4096]{1,0:T(8,128)(2,1)S(1)} collective-permute-done((bf16[64,4096]{1,0:T(8,128)(2,1)S(1)}, bf16[64,4096]{1,0:T(8,128)(2,1)S(1)}, u32[]{:S(2)}, u32[]{:S(2)}) %collective-permute-start.27) | collective-permute-done | bytes 524320 | tf_op jit(solution)/shard_map/ppermute | solution.py:67
  131.8 2.5 %collective-permute-done.29.far = bf16[128,4096]{1,0:T(8,128)(2,1)S(1)} collective-permute-done((bf16[128,4096]{1,0:T(8,128)(2,1)S(1)}, bf16[128,4096]{1,0:T(8,128)(2,1)S(1)}, u32[]{:S(2)}, u32[]{:S(2)}) %collective-permute-start.29) | collective-permute-done | bytes 1048608 | tf_op jit(solution)/shard_map/ppermute | solution.py:67
  134.3 1.4 shard_map.117
  137.4 2.2 %collective-permute-start.32 = (bf16[16,4096]{1,0:T(8,128)(2,1)}, bf16[16,4096]{1,0:T(8,128)(2,1)}, u32[]{:S(2)}, u32[]{:S(2)}) collective-permute-start(bf16[16,4096]{1,0:T(8,128)(2,1)} %get-tuple-element.75), channel_id=1, source_target_pairs={{0,12},{1,13},{2,14},{3,15},{4,0},{5,1},{6,2},{7,3},{8,4},{9,5},{1... | collective-permute-start | bytes 393224 | tf_op jit(solution)/shard_map/ppermute | solution.py:67
  141.1 4.7 %shard_map.118 = f32[24,512,128]{2,1,0:T(8,128)} custom-call(bf16[256,512]{1,0:T(8,128)(2,1)S(1)} %get-tuple-element.66.columns, bf16[256,256]{1,0:T(8,128)(2,1)S(1)} %fusion.1.order, bf16[256,128]{1,0:T(8,128)(2,1)S(1)} %bitcast.41, s32[256,1]{1,0:T(8,128)S(1)} %copy.25.adapter), custom_call_target="tpu_custom_call" | custom-call | flops 805306368 | bytes 6291456 | tf_op jit(solution)/shard_map/pallas_call | solution.py:448
  145.8 4.1 %collective-permute-done.30 = bf16[64,4096]{1,0:T(8,128)(2,1)} collective-permute-done((bf16[64,4096]{1,0:T(8,128)(2,1)S(1)}, bf16[64,4096]{1,0:T(8,128)(2,1)}, u32[]{:S(2)}, u32[]{:S(2)}) %collective-permute-start.30) | collective-permute-done | bytes 524320 | tf_op jit(solution)/shard_map/ppermute | solution.py:67
  149.9 2.3 %collective-permute-done.31 = bf16[16,4096]{1,0:T(8,128)(2,1)} collective-permute-done((bf16[16,4096]{1,0:T(8,128)(2,1)}, bf16[16,4096]{1,0:T(8,128)(2,1)}, u32[]{:S(2)}, u32[]{:S(2)}) %collective-permute-start.31) | collective-permute-done | bytes 131104 | tf_op jit(solution)/shard_map/ppermute | solution.py:67
  152.2 1.2 add_convert_fusion
  153.5 3.8 %collective-permute-start.35 = (bf16[16,4096]{1,0:T(8,128)(2,1)S(1)}, bf16[16,4096]{1,0:T(8,128)(2,1)S(1)}, u32[]{:S(2)}, u32[]{:S(2)}) collective-permute-start(bf16[16,4096]{1,0:T(8,128)(2,1)S(1)} %get-tuple-element.78), channel_id=1, source_target_pairs={{0,12},{1,13},{2,14},{3,15},{4,0},{5,1},{6,2},{7,3},{8,4},{9,5},{1... | collective-permute-start | bytes 393224 | tf_op jit(solution)/shard_map/ppermute | solution.py:67
  157.4 1.2 add_convert_fusion.3
  158.6 3.2 %collective-permute-done.33 = bf16[16,4096]{1,0:T(8,128)(2,1)S(1)} collective-permute-done((bf16[16,4096]{1,0:T(8,128)(2,1)S(1)}, bf16[16,4096]{1,0:T(8,128)(2,1)S(1)}, u32[]{:S(2)}, u32[]{:S(2)}) %collective-permute-start.33) | collective-permute-done | bytes 131104 | tf_op jit(solution)/shard_map/ppermute | solution.py:67
  161.7 4.6 %shard_map.119 = f32[24,128,1792]{2,1,0:T(8,128)} custom-call(bf16[256,1792]{1,0:T(8,128)(2,1)S(1)} %get-tuple-element.57.dgate, bf16[256,1792]{1,0:T(8,128)(2,1)S(1)} %get-tuple-element.43.dup, bf16[256,256]{1,0:T(8,128)(2,1)S(1)} %fusion.1.order, bf16[256,128]{1,0:T(8,128)(2,1)S(1)} %bitcast.39, ...), custom_call_target="tpu_custom_call", output_to_operand_aliasing={{}: (5, {})} | custom-call | flops 1207959552 | bytes 9437184 | tf_op jit(solution)/shard_map/pallas_call | solution.py:404
  166.4 2.0 %collective-permute-done.34 = bf16[16,4096]{1,0:T(8,128)(2,1)S(1)} collective-permute-done((bf16[16,4096]{1,0:T(8,128)(2,1)S(1)}, bf16[16,4096]{1,0:T(8,128)(2,1)S(1)}, u32[]{:S(2)}, u32[]{:S(2)}) %collective-permute-start.34) | collective-permute-done | bytes 131104 | tf_op jit(solution)/shard_map/ppermute | solution.py:67
  (116 shorter events, 18.0 us)
Async XLA Ops:
  1.5 10.4 %collective-permute-start.1 = (bf16[16,3072]{1,0:T(8,128)(2,1)S(1)}, bf16[16,3072]{1,0:T(8,128)(2,1)S(1)}, u32[]{:S(2)}, u32[]{:S(2)}) collective-permute-start(bf16[16,3072]{1,0:T(8,128)(2,1)S(1)} %get-tuple-element.81), channel_id=1, source_target_pairs={{0,8},{1,9},{2,10},{3,11},{4,12},{5,13},{6,14},{7,15},{8,0},{9,1},... | collective-permute-start | bytes 294920 | tf_op jit(solution)/shard_map/ppermute | solution.py:67
  5.6 6.3 %collective-permute-start = (bf16[16,3072]{1,0:T(8,128)(2,1)S(1)}, bf16[16,3072]{1,0:T(8,128)(2,1)S(1)}, u32[]{:S(2)}, u32[]{:S(2)}) collective-permute-start(bf16[16,3072]{1,0:T(8,128)(2,1)S(1)} %get-tuple-element.81), channel_id=1, source_target_pairs={{0,12},{1,13},{2,14},{3,15},{4,0},{5,1},{6,2},{7,3},{8,4},{9,5},{1... | collective-permute-start | bytes 294920 | tf_op jit(solution)/shard_map/ppermute | solution.py:67
  7.0 6.8 %collective-permute-start.2 = (bf16[16,3072]{1,0:T(8,128)(2,1)S(1)}, bf16[16,3072]{1,0:T(8,128)(2,1)S(1)}, u32[]{:S(2)}, u32[]{:S(2)}) collective-permute-start(bf16[16,3072]{1,0:T(8,128)(2,1)S(1)} %get-tuple-element.81), channel_id=1, source_target_pairs={{0,4},{1,5},{2,6},{3,7},{4,8},{5,9},{6,10},{7,11},{8,12},{9,13},{1... | collective-permute-start | bytes 294920 | tf_op jit(solution)/shard_map/ppermute | solution.py:67
  13.9 9.2 %collective-permute-start.5 = (bf16[16,5120]{1,0:T(8,128)(2,1)S(1)}, bf16[16,5120]{1,0:T(8,128)(2,1)S(1)}, u32[]{:S(2)}, u32[]{:S(2)}) collective-permute-start(bf16[16,5120]{1,0:T(8,128)(2,1)S(1)} %slice.60), channel_id=1, source_target_pairs={{0,4},{1,5},{2,6},{3,7},{4,8},{5,9},{6,10},{7,11},{8,12},{9,13},{1... | collective-permute-start | bytes 491528 | tf_op jit(solution)/shard_map/ppermute | solution.py:67
  15.6 12.5 %collective-permute-start.4 = (bf16[16,5120]{1,0:T(8,128)(2,1)S(1)}, bf16[16,5120]{1,0:T(8,128)(2,1)S(1)}, u32[]{:S(2)}, u32[]{:S(2)}) collective-permute-start(bf16[16,5120]{1,0:T(8,128)(2,1)S(1)} %slice.60), channel_id=1, source_target_pairs={{0,8},{1,9},{2,10},{3,11},{4,12},{5,13},{6,14},{7,15},{8,0},{9,1},... | collective-permute-start | bytes 491528 | tf_op jit(solution)/shard_map/ppermute | solution.py:67
  17.6 10.5 %collective-permute-start.3 = (bf16[16,5120]{1,0:T(8,128)(2,1)S(1)}, bf16[16,5120]{1,0:T(8,128)(2,1)S(1)}, u32[]{:S(2)}, u32[]{:S(2)}) collective-permute-start(bf16[16,5120]{1,0:T(8,128)(2,1)S(1)} %slice.60), channel_id=1, source_target_pairs={{0,12},{1,13},{2,14},{3,15},{4,0},{5,1},{6,2},{7,3},{8,4},{9,5},{1... | collective-permute-start | bytes 491528 | tf_op jit(solution)/shard_map/ppermute | solution.py:67
  21.5 13.7 %collective-permute-start.9 = (bf16[64,3072]{1,0:T(8,128)(2,1)S(1)}, bf16[64,3072]{1,0:T(8,128)(2,1)S(1)}, u32[]{:S(2)}, u32[]{:S(2)}) collective-permute-start(bf16[64,3072]{1,0:T(8,128)(2,1)S(1)} %bitcast.32), channel_id=1, source_target_pairs={{0,1},{1,0},{2,3},{3,2},{4,5},{5,4},{6,7},{7,6},{8,9},{9,8},{10,11... | collective-permute-start | bytes 1179656 | tf_op jit(solution)/shard_map/ppermute | solution.py:67
  21.5 11.5 %collective-permute-start.8 = (bf16[64,3072]{1,0:T(8,128)(2,1)S(1)}, bf16[64,3072]{1,0:T(8,128)(2,1)S(1)}, u32[]{:S(2)}, u32[]{:S(2)}) collective-permute-start(bf16[64,3072]{1,0:T(8,128)(2,1)S(1)} %bitcast.33), channel_id=1, source_target_pairs={{0,2},{1,3},{2,0},{3,1},{4,6},{5,7},{6,4},{7,5},{8,10},{9,11},{10,... | collective-permute-start | bytes 1179656 | tf_op jit(solution)/shard_map/ppermute | solution.py:67
  33.0 2.2 %collective-permute-start.10 = (bf16[64,3072]{1,0:T(8,128)(2,1)S(1)}, bf16[64,3072]{1,0:T(8,128)(2,1)S(1)}, u32[]{:S(2)}, u32[]{:S(2)}) collective-permute-start(bf16[64,3072]{1,0:T(8,128)(2,1)S(1)} %collective-permute-done.8.rest_1_.rest_9_), channel_id=1, source_target_pairs={{0,1},{1,0},{2,3},{3,2},{4,5},{5,4},{6,7},{7,6},{8,9},{9,8},{10,11... | collective-permute-start | bytes 1179656 | tf_op jit(solution)/shard_map/ppermute | solution.py:67
  33.1 11.4 %copy-start.4 = (s32[24]{0:T(128)S(1)}, s32[24]{0:T(128)}, u32[]{:S(2)}) copy-start(s32[24]{0:T(128)} %param.15) | copy-start | bytes 292
  33.1 13.3 %collective-permute-start.11 = (bf16[64,2560]{1,0:T(8,128)(2,1)S(1)}, bf16[64,2560]{1,0:T(8,128)(2,1)S(1)}, u32[]{:S(2)}, u32[]{:S(2)}) collective-permute-start(bf16[64,2560]{1,0:T(8,128)(2,1)S(1)} %get-tuple-element.72.rest_0_.rest_12_), channel_id=1, source_target_pairs={{0,1},{1,0},{2,3},{3,2},{4,5},{5,4},{6,7},{7,6},{8,9},{9,8},{10,11... | collective-permute-start | bytes 983048 | tf_op jit(solution)/shard_map/ppermute | solution.py:67
  33.6 10.8 %collective-permute-start.7 = (bf16[64,2560]{1,0:T(8,128)(2,1)S(1)}, bf16[64,2560]{1,0:T(8,128)(2,1)S(1)}, u32[]{:S(2)}, u32[]{:S(2)}) collective-permute-start(bf16[64,2560]{1,0:T(8,128)(2,1)S(1)} %get-tuple-element.72.rest_0_.rest_12_), channel_id=1, source_target_pairs={{0,2},{1,3},{2,0},{3,1},{4,6},{5,7},{6,4},{7,5},{8,10},{9,11},{10,... | collective-permute-start | bytes 983048 | tf_op jit(solution)/shard_map/ppermute | solution.py:67
  44.4 2.0 %collective-permute-start.12 = (bf16[64,2560]{1,0:T(8,128)(2,1)S(1)}, bf16[64,2560]{1,0:T(8,128)(2,1)S(1)}, u32[]{:S(2)}, u32[]{:S(2)}) collective-permute-start(bf16[64,2560]{1,0:T(8,128)(2,1)S(1)} %collective-permute-done.7.rest_1_.rest_13_), channel_id=1, source_target_pairs={{0,1},{1,0},{2,3},{3,2},{4,5},{5,4},{6,7},{7,6},{8,9},{9,8},{10,11... | collective-permute-start | bytes 983048 | tf_op jit(solution)/shard_map/ppermute | solution.py:67
  44.7 11.9 %copy-start = (bf16[24,512,128]{2,1,0:T(8,128)(2,1)S(1)}, bf16[24,512,128]{2,1,0:T(8,128)(2,1)}, u32[]{:S(2)}) copy-start(bf16[24,512,128]{2,1,0:T(8,128)(2,1)} %rest_7_.3) | copy-start | bytes 9437188
  44.7 11.9 %copy-start.2 = (s32[1,8]{1,0:T(1,128)S(1)}, s32[1,8]{1,0:T(1,128)}, u32[]{:S(2)}) copy-start(s32[1,8]{1,0:T(1,128)} %param.13) | copy-start | bytes 100
  44.7 10.4 %collective-permute-start.13 = (bf16[64,2560]{1,0:T(8,128)(2,1)S(1)}, bf16[64,2560]{1,0:T(8,128)(2,1)S(1)}, u32[]{:S(2)}, u32[]{:S(2)}) collective-permute-start(bf16[64,2560]{1,0:T(8,128)(2,1)S(1)} %get-tuple-element.73.rest_0_.rest_16_), channel_id=1, source_target_pairs={{0,1},{1,0},{2,3},{3,2},{4,5},{5,4},{6,7},{7,6},{8,9},{9,8},{10,11... | collective-permute-start | bytes 983048 | tf_op jit(solution)/shard_map/ppermute | solution.py:67
  45.3 9.7 %collective-permute-start.6 = (bf16[64,2560]{1,0:T(8,128)(2,1)S(1)}, bf16[64,2560]{1,0:T(8,128)(2,1)S(1)}, u32[]{:S(2)}, u32[]{:S(2)}) collective-permute-start(bf16[64,2560]{1,0:T(8,128)(2,1)S(1)} %get-tuple-element.73.rest_0_.rest_16_), channel_id=1, source_target_pairs={{0,2},{1,3},{2,0},{3,1},{4,6},{5,7},{6,4},{7,5},{8,10},{9,11},{10,... | collective-permute-start | bytes 983048 | tf_op jit(solution)/shard_map/ppermute | solution.py:67
  55.0 1.6 collective-permute-start.14
  58.2 1.3 collective-permute-start.15
  59.5 4.3 %collective-permute-start.16 = (f32[128,128]{1,0:T(8,128)S(1)}, f32[128,128]{1,0:T(8,128)S(1)}, u32[]{:S(2)}, u32[]{:S(2)}) collective-permute-start(f32[128,128]{1,0:T(8,128)S(1)} %slice_add_fusion.1), channel_id=1, source_target_pairs={{0,2},{1,3},{2,0},{3,1},{4,6},{5,7},{6,4},{7,5},{8,10},{9,11},{10,... | collective-permute-start | bytes 196616 | tf_op jit(solution)/shard_map/ppermute | solution.py:94
  63.8 4.3 %collective-permute-start.17 = (f32[128,128]{1,0:T(8,128)S(1)}, f32[128,128]{1,0:T(8,128)S(1)}, u32[]{:S(2)}, u32[]{:S(2)}) collective-permute-start(f32[128,128]{1,0:T(8,128)S(1)} %add.292), channel_id=1, source_target_pairs={{0,4},{1,5},{2,6},{3,7},{4,0},{5,1},{6,2},{7,3},{8,12},{9,13},{10,... | collective-permute-start | bytes 196616 | tf_op jit(solution)/shard_map/ppermute | solution.py:94
  68.2 5.9 %collective-permute-start.18 = (f32[128,128]{1,0:T(8,128)S(1)}, f32[128,128]{1,0:T(8,128)S(1)}, u32[]{:S(2)}, u32[]{:S(2)}) collective-permute-start(f32[128,128]{1,0:T(8,128)S(1)} %add.293), channel_id=1, source_target_pairs={{0,8},{1,9},{2,10},{3,11},{4,12},{5,13},{6,14},{7,15},{8,0},{9,1},... | collective-permute-start | bytes 196616 | tf_op jit(solution)/shard_map/ppermute | solution.py:94
  74.1 4.1 %slice-start = ((s8[11010048]{0:T(1024)(128)(4,1)}), s8[4194304]{0:T(1024)(128)(4,1)S(1)}, s32[]{:S(2)}) async-start(s8[11010048]{0:T(1024)(128)(4,1)} %bitcast.30), calls=%async_computation | async-start | bytes 8388608
  74.2 5.0 %slice-start.1 = ((s8[11010048]{0:T(1024)(128)(4,1)}), s8[4194304]{0:T(1024)(128)(4,1)S(1)}, s32[]{:S(2)}) async-start(s8[11010048]{0:T(1024)(128)(4,1)} %bitcast.30), calls=%async_computation.1 | async-start | bytes 8388608
  74.2 5.8 %slice-start.2 = ((s8[11010048]{0:T(1024)(128)(4,1)}), s8[2621440]{0:T(1024)(128)(4,1)S(1)}, s32[]{:S(2)}) async-start(s8[11010048]{0:T(1024)(128)(4,1)} %bitcast.30), calls=%async_computation.2 | async-start | bytes 5242880
  74.3 5.9 %copy-start.1 = (bf16[256,1792]{1,0:T(8,128)(2,1)S(1)}, bf16[256,1792]{1,0:T(8,128)(2,1)}, u32[]{:S(2)}) copy-start(bf16[256,1792]{1,0:T(8,128)(2,1)} %dhidden.1) | copy-start | bytes 2752516
  74.3 3.9 %collective-permute-start.19 = (bf16[128,128]{1,0:T(8,128)(2,1)S(1)}, bf16[128,128]{1,0:T(8,128)(2,1)S(1)}, u32[]{:S(2)}, u32[]{:S(2)}) collective-permute-start(bf16[128,128]{1,0:T(8,128)(2,1)S(1)} %fusion.2), channel_id=1, source_target_pairs={{0,1},{1,0},{2,3},{3,2},{4,5},{5,4},{6,7},{7,6},{8,9},{9,8},{10,11... | collective-permute-start | bytes 98312 | tf_op jit(solution)/shard_map/ppermute | solution.py:67
  87.7 1.3 collective-permute-start.20
  89.0 4.9 %collective-permute-start.21 = (f32[128,128]{1,0:T(8,128)S(1)}, f32[128,128]{1,0:T(8,128)S(1)}, u32[]{:S(2)}, u32[]{:S(2)}) collective-permute-start(f32[128,128]{1,0:T(8,128)S(1)} %slice_add_fusion), channel_id=1, source_target_pairs={{0,2},{1,3},{2,0},{3,1},{4,6},{5,7},{6,4},{7,5},{8,10},{9,11},{10,... | collective-permute-start | bytes 196616 | tf_op jit(solution)/shard_map/ppermute | solution.py:94
  93.9 4.5 %collective-permute-start.22 = (f32[128,128]{1,0:T(8,128)S(1)}, f32[128,128]{1,0:T(8,128)S(1)}, u32[]{:S(2)}, u32[]{:S(2)}) collective-permute-start(f32[128,128]{1,0:T(8,128)S(1)} %add.303), channel_id=1, source_target_pairs={{0,4},{1,5},{2,6},{3,7},{4,0},{5,1},{6,2},{7,3},{8,12},{9,13},{10,... | collective-permute-start | bytes 196616 | tf_op jit(solution)/shard_map/ppermute | solution.py:94
  98.4 13.0 %collective-permute-start.23 = (f32[128,128]{1,0:T(8,128)S(1)}, f32[128,128]{1,0:T(8,128)S(1)}, u32[]{:S(2)}, u32[]{:S(2)}) collective-permute-start(f32[128,128]{1,0:T(8,128)S(1)} %add.304), channel_id=1, source_target_pairs={{0,8},{1,9},{2,10},{3,11},{4,12},{5,13},{6,14},{7,15},{8,0},{9,1},... | collective-permute-start | bytes 196616 | tf_op jit(solution)/shard_map/ppermute | solution.py:94
  111.5 1.3 collective-permute-start.24
  112.8 3.2 %collective-permute-start.25 = (bf16[128,4096]{1,0:T(8,128)(2,1)S(1)}, bf16[128,4096]{1,0:T(8,128)(2,1)S(1)}, u32[]{:S(2)}, u32[]{:S(2)}) collective-permute-start(bf16[128,4096]{1,0:T(8,128)(2,1)S(1)} %get-tuple-element.52), channel_id=1, source_target_pairs={{0,1},{1,0},{2,3},{3,2},{4,5},{5,4},{6,7},{7,6},{8,9},{9,8},{10,11... | collective-permute-start | bytes 3145736 | tf_op jit(solution)/shard_map/ppermute | solution.py:67
  114.4 1.6 collective-permute-start.26
  117.4 14.3 %collective-permute-start.27 = (bf16[64,4096]{1,0:T(8,128)(2,1)S(1)}, bf16[64,4096]{1,0:T(8,128)(2,1)S(1)}, u32[]{:S(2)}, u32[]{:S(2)}) collective-permute-start(bf16[64,4096]{1,0:T(8,128)(2,1)S(1)} %get-tuple-element.56), channel_id=1, source_target_pairs={{0,2},{1,3},{2,0},{3,1},{4,6},{5,7},{6,4},{7,5},{8,10},{9,11},{10,... | collective-permute-start | bytes 1572872 | tf_op jit(solution)/shard_map/ppermute | solution.py:67
  131.7 2.7 %collective-permute-start.29 = (bf16[128,4096]{1,0:T(8,128)(2,1)S(1)}, bf16[128,4096]{1,0:T(8,128)(2,1)S(1)}, u32[]{:S(2)}, u32[]{:S(2)}) collective-permute-start(bf16[128,4096]{1,0:T(8,128)(2,1)S(1)} %get-tuple-element.60), channel_id=1, source_target_pairs={{0,1},{1,0},{2,3},{3,2},{4,5},{5,4},{6,7},{7,6},{8,9},{9,8},{10,11... | collective-permute-start | bytes 3145736 | tf_op jit(solution)/shard_map/ppermute | solution.py:67
  131.8 9.1 %copy-start.3 = (bf16[64,4096]{1,0:T(8,128)(2,1)}, bf16[64,4096]{1,0:T(8,128)(2,1)S(1)}, u32[]{:S(2)}) copy-start(bf16[64,4096]{1,0:T(8,128)(2,1)S(1)} %add_convert_fusion.1) | copy-start | bytes 1572868
  135.7 14.1 %collective-permute-start.30 = (bf16[64,4096]{1,0:T(8,128)(2,1)S(1)}, bf16[64,4096]{1,0:T(8,128)(2,1)}, u32[]{:S(2)}, u32[]{:S(2)}) collective-permute-start(bf16[64,4096]{1,0:T(8,128)(2,1)S(1)} %get-tuple-element.61), channel_id=1, source_target_pairs={{0,2},{1,3},{2,0},{3,1},{4,6},{5,7},{6,4},{7,5},{8,10},{9,11},{10,... | collective-permute-start | bytes 1572872 | tf_op jit(solution)/shard_map/ppermute | solution.py:67
  137.4 8.3 %collective-permute-start.32 = (bf16[16,4096]{1,0:T(8,128)(2,1)}, bf16[16,4096]{1,0:T(8,128)(2,1)}, u32[]{:S(2)}, u32[]{:S(2)}) collective-permute-start(bf16[16,4096]{1,0:T(8,128)(2,1)} %get-tuple-element.75), channel_id=1, source_target_pairs={{0,12},{1,13},{2,14},{3,15},{4,0},{5,1},{6,2},{7,3},{8,4},{9,5},{1... | collective-permute-start | bytes 393224 | tf_op jit(solution)/shard_map/ppermute | solution.py:67
  139.6 12.6 %collective-permute-start.31 = (bf16[16,4096]{1,0:T(8,128)(2,1)}, bf16[16,4096]{1,0:T(8,128)(2,1)}, u32[]{:S(2)}, u32[]{:S(2)}) collective-permute-start(bf16[16,4096]{1,0:T(8,128)(2,1)} %get-tuple-element.76), channel_id=1, source_target_pairs={{0,8},{1,9},{2,10},{3,11},{4,12},{5,13},{6,14},{7,15},{8,0},{9,1},... | collective-permute-start | bytes 393224 | tf_op jit(solution)/shard_map/ppermute | solution.py:67
  140.2 12.0 %collective-permute-start.28 = (bf16[16,4096]{1,0:T(8,128)(2,1)}, bf16[16,4096]{1,0:T(8,128)(2,1)}, u32[]{:S(2)}, u32[]{:S(2)}) collective-permute-start(bf16[16,4096]{1,0:T(8,128)(2,1)} %get-tuple-element.74), channel_id=1, source_target_pairs={{0,4},{1,5},{2,6},{3,7},{4,8},{5,9},{6,10},{7,11},{8,12},{9,13},{1... | collective-permute-start | bytes 393224 | tf_op jit(solution)/shard_map/ppermute | solution.py:67
  153.4 8.3 %collective-permute-start.33 = (bf16[16,4096]{1,0:T(8,128)(2,1)S(1)}, bf16[16,4096]{1,0:T(8,128)(2,1)S(1)}, u32[]{:S(2)}, u32[]{:S(2)}) collective-permute-start(bf16[16,4096]{1,0:T(8,128)(2,1)S(1)} %get-tuple-element.77), channel_id=1, source_target_pairs={{0,4},{1,5},{2,6},{3,7},{4,8},{5,9},{6,10},{7,11},{8,12},{9,13},{1... | collective-permute-start | bytes 393224 | tf_op jit(solution)/shard_map/ppermute | solution.py:67
  153.5 12.9 %collective-permute-start.35 = (bf16[16,4096]{1,0:T(8,128)(2,1)S(1)}, bf16[16,4096]{1,0:T(8,128)(2,1)S(1)}, u32[]{:S(2)}, u32[]{:S(2)}) collective-permute-start(bf16[16,4096]{1,0:T(8,128)(2,1)S(1)} %get-tuple-element.78), channel_id=1, source_target_pairs={{0,12},{1,13},{2,14},{3,15},{4,0},{5,1},{6,2},{7,3},{8,4},{9,5},{1... | collective-permute-start | bytes 393224 | tf_op jit(solution)/shard_map/ppermute | solution.py:67
  157.3 11.1 %collective-permute-start.34 = (bf16[16,4096]{1,0:T(8,128)(2,1)S(1)}, bf16[16,4096]{1,0:T(8,128)(2,1)S(1)}, u32[]{:S(2)}, u32[]{:S(2)}) collective-permute-start(bf16[16,4096]{1,0:T(8,128)(2,1)S(1)} %get-tuple-element.79), channel_id=1, source_target_pairs={{0,8},{1,9},{2,10},{3,11},{4,12},{5,13},{6,14},{7,15},{8,0},{9,1},... | collective-permute-start | bytes 393224 | tf_op jit(solution)/shard_map/ppermute | solution.py:67

commit v12 on v11

--- a/solution.py
+++ b/solution.py
@@ -9,7 +9,7 @@
 
 OUTER_SHARES = (3, 5)
 INNER_CUTS = (1, 2)
-SUM_SHARES = (4, 4)
+SUM_SHARES = (5, 3)
 MIB = 1024 * 1024
 BF16 = jnp.bfloat16
 DEPTH = 3
@@ -704,6 +704,11 @@
         if q:
             near, far = backward_chunk(frozen, after(dgate, sums[-1][0]), dup, first, step)
             ahead = inner_moves[q - 1] + (outer_moves[q - 2] if q > 1 else [])
+            if q == len(cuts) - 1:
+                grad_a = grad_a_of(
+                    columns, order, after(low_out, near), adapter[:, None], adapter_list
+                )
+                ahead = ahead + [grad_a]
             far = lax.optimization_barrier((far, *ahead))[0]
         far = torus.move(far, 2, 1)
         sums.append(core_sum(near, far, side, side_far, at, first, b))
@@ -713,7 +718,7 @@
             total = total + v.astype(F32)
         inners.append(total.astype(BF16).reshape(a, rows, step))
         outer_moves.append([torus.move(inners[q][k], 0, k) for k in range(1, a)])
-    grad_b = grad_b_part(outer_moves[-1][0])
+    grad_b = grad_b_part(sums[-1][0])
     for q, inner in enumerate(inners):
         total = inner[0].astype(F32)
         for v in outer_moves[q]:
@@ -721,9 +726,6 @@
             total = total + v.astype(F32)
         blocks.append(total.astype(BF16))
     dinput = jnp.concatenate(blocks, axis=1)
-    grad_a = grad_a_of(
-        columns, order, after(low_out, sums[-1][0]), adapter[:, None], adapter_list
-    )
     return (dinput, grad_a, grad_b)
 
 

time: 169 us -> 169 us (level)
  Pallas kernels: 84.2 us -> 85.9 us
  waiting for transfers between devices: 36.3 us -> 34.6 us
    ppermute x30, waiting for transfers between devices: 35.2 us -> 32.9 us  [move(): return lax.ppermute(x, 'tensor', pairs)]
where the time goes in v12:
time: 169 us; the launch traced here: 168 us
  Pallas kernels  85.9 us (51%)
  starting transfers between devices  36.7 us (22%)
  waiting for transfers between devices  34.6 us (20%)
  other arithmetic  5.25 us (3%)
  local copies, waits for them, and re-layouts  4.84 us (3%)
    ppermute x30, waiting for transfers between devices, move(): return lax.ppermute(x, 'tensor', pairs)  32.9 us
    pallas_call x6, Pallas kernels, forward_chunk(): pl.pallas_call(functools.partial(forward_kernel, len(pieces), low, count,...  31.5 us
    ppermute x30, starting transfers between devices, move(): return lax.ppermute(x, 'tensor', pairs)  29 us
    pallas_call x2, Pallas kernels, backward_chunk(): pl.pallas_call(functools.partial(backward_kernel, count, first), grid=(co...  23.1 us
    pallas_call x3, Pallas kernels, grad_b_of(): pl.pallas_call(functools.partial(grad_b_kernel, first, last - first), gri...  11.9 us
    ppermute x6, starting transfers between devices, exchange_sum(): x = x + lax.ppermute(x, 'tensor', pairs)  7.69 us
    pallas_call x1, Pallas kernels, middle(): pl.pallas_call(functools.partial(middle_kernel, rows), grid_spec=pltpu.Pr...  7.48 us
    pallas_call x1, Pallas kernels, grad_a_of(): pl.pallas_call(grad_a_kernel, grid=(adapters // per,), in_specs=[full(col...  4.67 us
  transfers between devices with their start and end apart: 36, of which 18 were waited for; matrix products, arithmetic and copies ran while one was open for 4% of the time, Pallas kernels for 43%

profile of v12, /device:TPU:0, one launch (start us, length us, event | category | flops | bytes accessed | tf_op | source)
XLA Modules:
  0.0 168.4 jit_solution(2467534021052695802)
XLA Ops:
  1.5 3.1 %collective-permute-start.2 = (bf16[16,3072]{1,0:T(8,128)(2,1)S(1)}, bf16[16,3072]{1,0:T(8,128)(2,1)S(1)}, u32[]{:S(2)}, u32[]{:S(2)}) collective-permute-start(bf16[16,3072]{1,0:T(8,128)(2,1)S(1)} %get-tuple-element.81), channel_id=1, source_target_pairs={{0,4},{1,5},{2,6},{3,7},{4,8},{5,9},{6,10},{7,11},{8,12},{9,13},{1... | collective-permute-start | bytes 294920 | tf_op jit(solution)/shard_map/ppermute | solution.py:67
  4.6 2.6 %collective-permute-start.1 = (bf16[16,3072]{1,0:T(8,128)(2,1)S(1)}, bf16[16,3072]{1,0:T(8,128)(2,1)S(1)}, u32[]{:S(2)}, u32[]{:S(2)}) collective-permute-start(bf16[16,3072]{1,0:T(8,128)(2,1)S(1)} %get-tuple-element.81), channel_id=1, source_target_pairs={{0,8},{1,9},{2,10},{3,11},{4,12},{5,13},{6,14},{7,15},{8,0},{9,1},... | collective-permute-start | bytes 294920 | tf_op jit(solution)/shard_map/ppermute | solution.py:67
  7.2 1.3 collective-permute-start
  11.3 2.5 %collective-permute-done.1 = bf16[16,3072]{1,0:T(8,128)(2,1)S(1)} collective-permute-done((bf16[16,3072]{1,0:T(8,128)(2,1)S(1)}, bf16[16,3072]{1,0:T(8,128)(2,1)S(1)}, u32[]{:S(2)}, u32[]{:S(2)}) %collective-permute-start.1) | collective-permute-done | bytes 98336 | tf_op jit(solution)/shard_map/ppermute | solution.py:67
  13.9 2.6 %collective-permute-start.5 = (bf16[16,5120]{1,0:T(8,128)(2,1)S(1)}, bf16[16,5120]{1,0:T(8,128)(2,1)S(1)}, u32[]{:S(2)}, u32[]{:S(2)}) collective-permute-start(bf16[16,5120]{1,0:T(8,128)(2,1)S(1)} %slice.60), channel_id=1, source_target_pairs={{0,4},{1,5},{2,6},{3,7},{4,8},{5,9},{6,10},{7,11},{8,12},{9,13},{1... | collective-permute-start | bytes 491528 | tf_op jit(solution)/shard_map/ppermute | solution.py:67
  16.5 1.6 collective-permute-start.4
  20.0 1.5 collective-permute-start.8
  21.5 1.5 collective-permute-done.5
  23.0 5.9 %collective-permute-done.4 = bf16[16,5120]{1,0:T(8,128)(2,1)S(1)} collective-permute-done((bf16[16,5120]{1,0:T(8,128)(2,1)S(1)}, bf16[16,5120]{1,0:T(8,128)(2,1)S(1)}, u32[]{:S(2)}, u32[]{:S(2)}) %collective-permute-start.4) | collective-permute-done | bytes 163872 | tf_op jit(solution)/shard_map/ppermute | solution.py:67
  29.0 1.5 collective-permute-done.8.rest_1_.rest_9_
  30.5 1.6 collective-permute-start.7
  32.3 9.2 %shard_map.103.rest_5_ = f32[2,256,1792]{2,1,0:T(8,128)S(1)} custom-call(bf16[64,3072]{1,0:T(8,128)(2,1)S(1)} %bitcast.34, bf16[64,3072]{1,0:T(8,128)(2,1)S(1)} %collective-permute-done.8.rest_1_.rest_9_, bf16[64,3072]{1,0:T(8,128)(2,1)S(1)} %collective-permute-done.9.rest_2_.rest_10_, bf16[64,3072]{1,0:T(8,128)(2,1)S(1)} %collective-permute-done.10.rest_3_.rest_11_, ...), custom_call_target="tpu_custom_call" | custom-call | flops 5637144576 | bytes 22020096 | tf_op jit(solution)/shard_map/pallas_call | solution.py:181
  42.1 1.3 collective-permute-start.6
  43.5 8.4 %shard_map.104.rest_5_ = f32[2,256,1792]{2,1,0:T(8,128)S(1)} custom-call(bf16[64,2560]{1,0:T(8,128)(2,1)S(1)} %get-tuple-element.75.rest_0_.rest_12_, bf16[64,2560]{1,0:T(8,128)(2,1)S(1)} %collective-permute-done.7.rest_1_.rest_13_, bf16[64,2560]{1,0:T(8,128)(2,1)S(1)} %collective-permute-done.11.rest_2_.rest_14_, ...), custom_call_target="tpu_custom_call", output_to_operand_aliasing={{}: (5, {})} | custom-call | flops 4697620480 | bytes 18350080 | tf_op jit(solution)/shard_map/pallas_call | solution.py:181
  52.7 1.1 collective-permute-done.14.rest_3_.rest_19_
  53.7 1.6 shard_map.109
  56.7 1.4 collective-permute-start.16
  58.0 2.7 %shard_map.105.rest_5_ = f32[2,256,1792]{2,1,0:T(8,128)S(1)} custom-call(bf16[64,2560]{1,0:T(8,128)(2,1)S(1)} %get-tuple-element.76.rest_0_.rest_16_, bf16[64,2560]{1,0:T(8,128)(2,1)S(1)} %collective-permute-done.6.rest_1_.rest_17_, bf16[64,2560]{1,0:T(8,128)(2,1)S(1)} %collective-permute-done.13.rest_2_.rest_18_, ...), custom_call_target="tpu_custom_call", output_to_operand_aliasing={{}: (5, {})} | custom-call | flops 671088640 | bytes 2621440 | tf_op jit(solution)/shard_map/pallas_call | solution.py:181
  61.1 2.6 %collective-permute-start.17 = (f32[128,128]{1,0:T(8,128)S(1)}, f32[128,128]{1,0:T(8,128)S(1)}, u32[]{:S(2)}, u32[]{:S(2)}) collective-permute-start(f32[128,128]{1,0:T(8,128)S(1)} %add.292), channel_id=1, source_target_pairs={{0,4},{1,5},{2,6},{3,7},{4,0},{5,1},{6,2},{7,3},{8,12},{9,13},{10,... | collective-permute-start | bytes 196616 | tf_op jit(solution)/shard_map/ppermute | solution.py:94
  63.7 3.7 %shard_map.106.rest_5_ = f32[2,256,1792]{2,1,0:T(8,128)S(1)} custom-call(bf16[64,2560]{1,0:T(8,128)(2,1)S(1)} %get-tuple-element.76.rest_0_.rest_16_, bf16[64,2560]{1,0:T(8,128)(2,1)S(1)} %collective-permute-done.6.rest_1_.rest_17_, bf16[64,2560]{1,0:T(8,128)(2,1)S(1)} %collective-permute-done.13.rest_2_.rest_18_, ...), custom_call_target="tpu_custom_call", output_to_operand_aliasing={{}: (5, {})} | custom-call | flops 1342177280 | bytes 5242880 | tf_op jit(solution)/shard_map/pallas_call | solution.py:181
  67.4 1.5 collective-permute-start.18
  69.0 3.7 %shard_map.107.rest_5_ = f32[2,256,1792]{2,1,0:T(8,128)S(1)} custom-call(bf16[64,2560]{1,0:T(8,128)(2,1)S(1)} %get-tuple-element.76.rest_0_.rest_16_, bf16[64,2560]{1,0:T(8,128)(2,1)S(1)} %collective-permute-done.6.rest_1_.rest_17_, bf16[64,2560]{1,0:T(8,128)(2,1)S(1)} %collective-permute-done.13.rest_2_.rest_18_, ...), custom_call_target="tpu_custom_call", output_to_operand_aliasing={{}: (5, {})} | custom-call | flops 1342177280 | bytes 5242880 | tf_op jit(solution)/shard_map/pallas_call | solution.py:181
  73.6 3.8 %shard_map.108.base = f32[2,256,1792]{2,1,0:T(8,128)S(1)} custom-call(bf16[64,2560]{1,0:T(8,128)(2,1)S(1)} %get-tuple-element.76.rest_0_.rest_16_, bf16[64,2560]{1,0:T(8,128)(2,1)S(1)} %collective-permute-done.6.rest_1_.rest_17_, bf16[64,2560]{1,0:T(8,128)(2,1)S(1)} %collective-permute-done.13.rest_2_.rest_18_, ...), custom_call_target="tpu_custom_call", output_to_operand_aliasing={{}: (5, {})} | custom-call | flops 1342177280 | bytes 5242880 | tf_op jit(solution)/shard_map/pallas_call | solution.py:181
  77.5 1.0 slice-done.1
  79.4 7.5 %shard_map.110 = (bf16[256,1792]{1,0:T(8,128)(2,1)S(1)}, bf16[256,1792]{1,0:T(8,128)(2,1)S(1)}, f32[256,128]{1,0:T(8,128)S(1)}) custom-call(s32[8]{0:T(128)S(1)} %bitcast.48, s32[16]{0:T(128)S(1)} %get-tuple-element.70.places, f32[2,256,1792]{2,1,0:T(8,128)S(1)} %shard_map.108.base, bf16[256,1792]{1,0:T(8,128)(2,1)S(1)} %copy-done.1, ...), custom_call_target="tpu_custom_call" | custom-call | flops 1879048192 | bytes 10092544 | tf_op jit(solution)/shard_map/pallas_call | solution.py:329
  87.1 1.2 collective-permute-done.20
  88.3 1.3 collective-permute-start.21
  89.5 3.6 %shard_map.111.rest_0_ = f32[24,128,1792]{2,1,0:T(8,128)} custom-call(bf16[256,1792]{1,0:T(8,128)(2,1)S(1)} %get-tuple-element.57.dgate, bf16[256,1792]{1,0:T(8,128)(2,1)S(1)} %get-tuple-element.43.dup, bf16[256,256]{1,0:T(8,128)(2,1)S(1)} %fusion.1.order, bf16[256,128]{1,0:T(8,128)(2,1)S(1)} %bitcast.37, s32[1,256]{1,0:T(1,128)S(1)} %bitcast.42), custom_call_target="tpu_custom_call" | custom-call | flops 805306368 | bytes 6291456 | tf_op jit(solution)/shard_map/pallas_call | solution.py:404
  93.3 3.7 %shard_map.112.rest_0_ = f32[24,128,1792]{2,1,0:T(8,128)} custom-call(bf16[256,1792]{1,0:T(8,128)(2,1)S(1)} %get-tuple-element.57.dgate, bf16[256,1792]{1,0:T(8,128)(2,1)S(1)} %get-tuple-element.43.dup, bf16[256,256]{1,0:T(8,128)(2,1)S(1)} %fusion.1.order, bf16[256,128]{1,0:T(8,128)(2,1)S(1)} %bitcast.38, ...), custom_call_target="tpu_custom_call", output_to_operand_aliasing={{}: (5, {})} | custom-call | flops 805306368 | bytes 6291456 | tf_op jit(solution)/shard_map/pallas_call | solution.py:404
  98.4 13.9 %shard_map.113 = (bf16[128,5120]{1,0:T(8,128)(2,1)S(1)}, bf16[128,5120]{1,0:T(8,128)(2,1)S(1)}) custom-call(bf16[2,8192,1792]{2,1,0:T(8,128)(2,1)} %frozen.3, bf16[256,1792]{1,0:T(8,128)(2,1)S(1)} %get-tuple-element.57.dgate, bf16[256,1792]{1,0:T(8,128)(2,1)S(1)} %get-tuple-element.43.dup), custom_call_target="tpu_custom_call" | custom-call | flops 9395240960 | bytes 36700160 | tf_op jit(solution)/shard_map/pallas_call | solution.py:520
  112.6 1.1 collective-permute-done.24
  113.9 1.4 shard_map.114
  115.8 1.4 collective-permute-done.26.side_far
  117.2 3.1 %shard_map.115 = (bf16[64,5120]{1,0:T(8,128)(2,1)S(1)}, bf16[64,5120]{1,0:T(8,128)(2,1)}) custom-call(s32[2]{0:T(128)S(1)} %pad_add_fusion.at, bf16[128,5120]{1,0:T(8,128)(2,1)S(1)} %get-tuple-element.49.near, bf16[128,5120]{1,0:T(8,128)(2,1)S(1)} %collective-permute-done.25.far, f32[128,512]{1,0:T(8,128)S(1)} %get-tuple-element.53.side, ...), custom_call_target="tpu_custom_call" | custom-call | flops 1310720 | bytes 3932160 | tf_op jit(solution)/shard_map/pallas_call | solution.py:562
  121.2 9.2 %shard_map.116 = (bf16[128,3072]{1,0:T(8,128)(2,1)S(1)}, bf16[128,3072]{1,0:T(8,128)(2,1)S(1)}) custom-call(bf16[2,8192,1792]{2,1,0:T(8,128)(2,1)} %frozen.3, bf16[256,1792]{1,0:T(8,128)(2,1)S(1)} %get-tuple-element.57.dgate, bf16[256,1792]{1,0:T(8,128)(2,1)S(1)} %get-tuple-element.43.dup), custom_call_target="tpu_custom_call" | custom-call | flops 5637144576 | bytes 22020096 | tf_op jit(solution)/shard_map/pallas_call | solution.py:520
  130.5 4.7 %shard_map.117 = f32[24,512,128]{2,1,0:T(8,128)} custom-call(bf16[256,512]{1,0:T(8,128)(2,1)S(1)} %copy-done.3, bf16[256,256]{1,0:T(8,128)(2,1)S(1)} %fusion.1.order, bf16[256,128]{1,0:T(8,128)(2,1)S(1)} %bitcast.41, s32[256,1]{1,0:T(8,128)S(1)} %copy.25.adapter), custom_call_target="tpu_custom_call" | custom-call | flops 805306368 | bytes 6291456 | tf_op jit(solution)/shard_map/pallas_call | solution.py:448
  135.2 2.2 %collective-permute-done.27 = bf16[64,5120]{1,0:T(8,128)(2,1)} collective-permute-done((bf16[64,5120]{1,0:T(8,128)(2,1)}, bf16[64,5120]{1,0:T(8,128)(2,1)}, u32[]{:S(2)}, u32[]{:S(2)}) %collective-permute-start.27) | collective-permute-done | bytes 655392 | tf_op jit(solution)/shard_map/ppermute | solution.py:67
  137.4 1.2 add_convert_fusion
  138.6 1.0 collective-permute-done.29.far
  139.7 1.2 shard_map.118
  141.7 3.1 %collective-permute-start.32 = (bf16[16,5120]{1,0:T(8,128)(2,1)S(1)}, bf16[16,5120]{1,0:T(8,128)(2,1)S(1)}, u32[]{:S(2)}, u32[]{:S(2)}) collective-permute-start(bf16[16,5120]{1,0:T(8,128)(2,1)S(1)} %get-tuple-element.73), channel_id=1, source_target_pairs={{0,12},{1,13},{2,14},{3,15},{4,0},{5,1},{6,2},{7,3},{8,4},{9,5},{1... | collective-permute-start | bytes 491528 | tf_op jit(solution)/shard_map/ppermute | solution.py:67
  144.9 1.2 collective-permute-start.28
  146.0 4.6 %shard_map.119 = f32[24,128,1792]{2,1,0:T(8,128)} custom-call(bf16[256,1792]{1,0:T(8,128)(2,1)S(1)} %get-tuple-element.57.dgate, bf16[256,1792]{1,0:T(8,128)(2,1)S(1)} %get-tuple-element.43.dup, bf16[256,256]{1,0:T(8,128)(2,1)S(1)} %fusion.1.order, bf16[256,128]{1,0:T(8,128)(2,1)S(1)} %bitcast.39, ...), custom_call_target="tpu_custom_call", output_to_operand_aliasing={{}: (5, {})} | custom-call | flops 1207959552 | bytes 9437184 | tf_op jit(solution)/shard_map/pallas_call | solution.py:404
  150.6 1.5 collective-permute-done.30
  152.2 3.1 %collective-permute-start.35 = (bf16[16,3072]{1,0:T(8,128)(2,1)S(1)}, bf16[16,3072]{1,0:T(8,128)(2,1)S(1)}, u32[]{:S(2)}, u32[]{:S(2)}) collective-permute-start(bf16[16,3072]{1,0:T(8,128)(2,1)S(1)} %get-tuple-element.78), channel_id=1, source_target_pairs={{0,12},{1,13},{2,14},{3,15},{4,0},{5,1},{6,2},{7,3},{8,4},{9,5},{1... | collective-permute-start | bytes 294920 | tf_op jit(solution)/shard_map/ppermute | solution.py:67
  155.3 1.2 collective-permute-start.33
  156.5 7.6 %collective-permute-done.31 = bf16[16,5120]{1,0:T(8,128)(2,1)S(1)} collective-permute-done((bf16[16,5120]{1,0:T(8,128)(2,1)S(1)}, bf16[16,5120]{1,0:T(8,128)(2,1)S(1)}, u32[]{:S(2)}, u32[]{:S(2)}) %collective-permute-start.31) | collective-permute-done | bytes 163872 | tf_op jit(solution)/shard_map/ppermute | solution.py:67
  164.1 3.5 %collective-permute-done.34 = bf16[16,3072]{1,0:T(8,128)(2,1)S(1)} collective-permute-done((bf16[16,3072]{1,0:T(8,128)(2,1)S(1)}, bf16[16,3072]{1,0:T(8,128)(2,1)S(1)}, u32[]{:S(2)}, u32[]{:S(2)}) %collective-permute-start.34) | collective-permute-done | bytes 98336 | tf_op jit(solution)/shard_map/ppermute | solution.py:67
  (118 shorter events, 16.3 us)
Async XLA Ops:
  1.5 9.7 %collective-permute-start.2 = (bf16[16,3072]{1,0:T(8,128)(2,1)S(1)}, bf16[16,3072]{1,0:T(8,128)(2,1)S(1)}, u32[]{:S(2)}, u32[]{:S(2)}) collective-permute-start(bf16[16,3072]{1,0:T(8,128)(2,1)S(1)} %get-tuple-element.81), channel_id=1, source_target_pairs={{0,4},{1,5},{2,6},{3,7},{4,8},{5,9},{6,10},{7,11},{8,12},{9,13},{1... | collective-permute-start | bytes 294920 | tf_op jit(solution)/shard_map/ppermute | solution.py:67
  4.6 9.2 %collective-permute-start.1 = (bf16[16,3072]{1,0:T(8,128)(2,1)S(1)}, bf16[16,3072]{1,0:T(8,128)(2,1)S(1)}, u32[]{:S(2)}, u32[]{:S(2)}) collective-permute-start(bf16[16,3072]{1,0:T(8,128)(2,1)S(1)} %get-tuple-element.81), channel_id=1, source_target_pairs={{0,8},{1,9},{2,10},{3,11},{4,12},{5,13},{6,14},{7,15},{8,0},{9,1},... | collective-permute-start | bytes 294920 | tf_op jit(solution)/shard_map/ppermute | solution.py:67
  7.2 6.6 %collective-permute-start = (bf16[16,3072]{1,0:T(8,128)(2,1)S(1)}, bf16[16,3072]{1,0:T(8,128)(2,1)S(1)}, u32[]{:S(2)}, u32[]{:S(2)}) collective-permute-start(bf16[16,3072]{1,0:T(8,128)(2,1)S(1)} %get-tuple-element.81), channel_id=1, source_target_pairs={{0,12},{1,13},{2,14},{3,15},{4,0},{5,1},{6,2},{7,3},{8,4},{9,5},{1... | collective-permute-start | bytes 294920 | tf_op jit(solution)/shard_map/ppermute | solution.py:67
  13.9 9.1 %collective-permute-start.5 = (bf16[16,5120]{1,0:T(8,128)(2,1)S(1)}, bf16[16,5120]{1,0:T(8,128)(2,1)S(1)}, u32[]{:S(2)}, u32[]{:S(2)}) collective-permute-start(bf16[16,5120]{1,0:T(8,128)(2,1)S(1)} %slice.60), channel_id=1, source_target_pairs={{0,4},{1,5},{2,6},{3,7},{4,8},{5,9},{6,10},{7,11},{8,12},{9,13},{1... | collective-permute-start | bytes 491528 | tf_op jit(solution)/shard_map/ppermute | solution.py:67
  16.5 12.4 %collective-permute-start.4 = (bf16[16,5120]{1,0:T(8,128)(2,1)S(1)}, bf16[16,5120]{1,0:T(8,128)(2,1)S(1)}, u32[]{:S(2)}, u32[]{:S(2)}) collective-permute-start(bf16[16,5120]{1,0:T(8,128)(2,1)S(1)} %slice.60), channel_id=1, source_target_pairs={{0,8},{1,9},{2,10},{3,11},{4,12},{5,13},{6,14},{7,15},{8,0},{9,1},... | collective-permute-start | bytes 491528 | tf_op jit(solution)/shard_map/ppermute | solution.py:67
  18.1 10.8 %collective-permute-start.3 = (bf16[16,5120]{1,0:T(8,128)(2,1)S(1)}, bf16[16,5120]{1,0:T(8,128)(2,1)S(1)}, u32[]{:S(2)}, u32[]{:S(2)}) collective-permute-start(bf16[16,5120]{1,0:T(8,128)(2,1)S(1)} %slice.60), channel_id=1, source_target_pairs={{0,12},{1,13},{2,14},{3,15},{4,0},{5,1},{6,2},{7,3},{8,4},{9,5},{1... | collective-permute-start | bytes 491528 | tf_op jit(solution)/shard_map/ppermute | solution.py:67
  20.0 10.5 %collective-permute-start.8 = (bf16[64,3072]{1,0:T(8,128)(2,1)S(1)}, bf16[64,3072]{1,0:T(8,128)(2,1)S(1)}, u32[]{:S(2)}, u32[]{:S(2)}) collective-permute-start(bf16[64,3072]{1,0:T(8,128)(2,1)S(1)} %bitcast.32), channel_id=1, source_target_pairs={{0,2},{1,3},{2,0},{3,1},{4,6},{5,7},{6,4},{7,5},{8,10},{9,11},{10,... | collective-permute-start | bytes 1179656 | tf_op jit(solution)/shard_map/ppermute | solution.py:67
  21.5 10.8 %collective-permute-start.9 = (bf16[64,3072]{1,0:T(8,128)(2,1)S(1)}, bf16[64,3072]{1,0:T(8,128)(2,1)S(1)}, u32[]{:S(2)}, u32[]{:S(2)}) collective-permute-start(bf16[64,3072]{1,0:T(8,128)(2,1)S(1)} %bitcast.33), channel_id=1, source_target_pairs={{0,1},{1,0},{2,3},{3,2},{4,5},{5,4},{6,7},{7,6},{8,9},{9,8},{10,11... | collective-permute-start | bytes 1179656 | tf_op jit(solution)/shard_map/ppermute | solution.py:67
  30.4 1.9 %collective-permute-start.10 = (bf16[64,3072]{1,0:T(8,128)(2,1)S(1)}, bf16[64,3072]{1,0:T(8,128)(2,1)S(1)}, u32[]{:S(2)}, u32[]{:S(2)}) collective-permute-start(bf16[64,3072]{1,0:T(8,128)(2,1)S(1)} %collective-permute-done.8.rest_1_.rest_9_), channel_id=1, source_target_pairs={{0,1},{1,0},{2,3},{3,2},{4,5},{5,4},{6,7},{7,6},{8,9},{9,8},{10,11... | collective-permute-start | bytes 1179656 | tf_op jit(solution)/shard_map/ppermute | solution.py:67
  30.5 11.4 %copy-start.5 = (s32[24]{0:T(128)S(1)}, s32[24]{0:T(128)}, u32[]{:S(2)}) copy-start(s32[24]{0:T(128)} %param.15) | copy-start | bytes 292
  30.5 11.1 %collective-permute-start.7 = (bf16[64,2560]{1,0:T(8,128)(2,1)S(1)}, bf16[64,2560]{1,0:T(8,128)(2,1)S(1)}, u32[]{:S(2)}, u32[]{:S(2)}) collective-permute-start(bf16[64,2560]{1,0:T(8,128)(2,1)S(1)} %get-tuple-element.75.rest_0_.rest_12_), channel_id=1, source_target_pairs={{0,2},{1,3},{2,0},{3,1},{4,6},{5,7},{6,4},{7,5},{8,10},{9,11},{10,... | collective-permute-start | bytes 983048 | tf_op jit(solution)/shard_map/ppermute | solution.py:67
  32.1 11.4 %collective-permute-start.11 = (bf16[64,2560]{1,0:T(8,128)(2,1)S(1)}, bf16[64,2560]{1,0:T(8,128)(2,1)S(1)}, u32[]{:S(2)}, u32[]{:S(2)}) collective-permute-start(bf16[64,2560]{1,0:T(8,128)(2,1)S(1)} %get-tuple-element.75.rest_0_.rest_12_), channel_id=1, source_target_pairs={{0,1},{1,0},{2,3},{3,2},{4,5},{5,4},{6,7},{7,6},{8,9},{9,8},{10,11... | collective-permute-start | bytes 983048 | tf_op jit(solution)/shard_map/ppermute | solution.py:67
  41.6 1.9 %collective-permute-start.12 = (bf16[64,2560]{1,0:T(8,128)(2,1)S(1)}, bf16[64,2560]{1,0:T(8,128)(2,1)S(1)}, u32[]{:S(2)}, u32[]{:S(2)}) collective-permute-start(bf16[64,2560]{1,0:T(8,128)(2,1)S(1)} %collective-permute-done.7.rest_1_.rest_13_), channel_id=1, source_target_pairs={{0,1},{1,0},{2,3},{3,2},{4,5},{5,4},{6,7},{7,6},{8,9},{9,8},{10,11... | collective-permute-start | bytes 983048 | tf_op jit(solution)/shard_map/ppermute | solution.py:67
  42.1 11.6 %copy-start = (bf16[24,512,128]{2,1,0:T(8,128)(2,1)S(1)}, bf16[24,512,128]{2,1,0:T(8,128)(2,1)}, u32[]{:S(2)}) copy-start(bf16[24,512,128]{2,1,0:T(8,128)(2,1)} %rest_7_.3) | copy-start | bytes 9437188
  42.1 11.6 %copy-start.4 = (s32[1,8]{1,0:T(1,128)S(1)}, s32[1,8]{1,0:T(1,128)}, u32[]{:S(2)}) copy-start(s32[1,8]{1,0:T(1,128)} %param.13) | copy-start | bytes 100
  42.1 9.9 %collective-permute-start.6 = (bf16[64,2560]{1,0:T(8,128)(2,1)S(1)}, bf16[64,2560]{1,0:T(8,128)(2,1)S(1)}, u32[]{:S(2)}, u32[]{:S(2)}) collective-permute-start(bf16[64,2560]{1,0:T(8,128)(2,1)S(1)} %get-tuple-element.76.rest_0_.rest_16_), channel_id=1, source_target_pairs={{0,2},{1,3},{2,0},{3,1},{4,6},{5,7},{6,4},{7,5},{8,10},{9,11},{10,... | collective-permute-start | bytes 983048 | tf_op jit(solution)/shard_map/ppermute | solution.py:67
  43.4 9.2 %collective-permute-start.13 = (bf16[64,2560]{1,0:T(8,128)(2,1)S(1)}, bf16[64,2560]{1,0:T(8,128)(2,1)S(1)}, u32[]{:S(2)}, u32[]{:S(2)}) collective-permute-start(bf16[64,2560]{1,0:T(8,128)(2,1)S(1)} %get-tuple-element.76.rest_0_.rest_16_), channel_id=1, source_target_pairs={{0,1},{1,0},{2,3},{3,2},{4,5},{5,4},{6,7},{7,6},{8,9},{9,8},{10,11... | collective-permute-start | bytes 983048 | tf_op jit(solution)/shard_map/ppermute | solution.py:67
  52.0 1.7 collective-permute-start.14
  55.3 2.8 %copy-start.2 = (bf16[256,512]{1,0:T(8,128)(2,1)}, bf16[256,512]{1,0:T(8,128)(2,1)S(1)}, u32[]{:S(2)}) copy-start(bf16[256,512]{1,0:T(8,128)(2,1)S(1)} %get-tuple-element.60.columns) | copy-start | bytes 786436
  55.3 1.3 collective-permute-start.15
  56.7 4.4 %collective-permute-start.16 = (f32[128,128]{1,0:T(8,128)S(1)}, f32[128,128]{1,0:T(8,128)S(1)}, u32[]{:S(2)}, u32[]{:S(2)}) collective-permute-start(f32[128,128]{1,0:T(8,128)S(1)} %slice_add_fusion.1), channel_id=1, source_target_pairs={{0,2},{1,3},{2,0},{3,1},{4,6},{5,7},{6,4},{7,5},{8,10},{9,11},{10,... | collective-permute-start | bytes 196616 | tf_op jit(solution)/shard_map/ppermute | solution.py:94
  61.1 6.3 %collective-permute-start.17 = (f32[128,128]{1,0:T(8,128)S(1)}, f32[128,128]{1,0:T(8,128)S(1)}, u32[]{:S(2)}, u32[]{:S(2)}) collective-permute-start(f32[128,128]{1,0:T(8,128)S(1)} %add.292), channel_id=1, source_target_pairs={{0,4},{1,5},{2,6},{3,7},{4,0},{5,1},{6,2},{7,3},{8,12},{9,13},{10,... | collective-permute-start | bytes 196616 | tf_op jit(solution)/shard_map/ppermute | solution.py:94
  67.4 5.9 %collective-permute-start.18 = (f32[128,128]{1,0:T(8,128)S(1)}, f32[128,128]{1,0:T(8,128)S(1)}, u32[]{:S(2)}, u32[]{:S(2)}) collective-permute-start(f32[128,128]{1,0:T(8,128)S(1)} %add.293), channel_id=1, source_target_pairs={{0,8},{1,9},{2,10},{3,11},{4,12},{5,13},{6,14},{7,15},{8,0},{9,1},... | collective-permute-start | bytes 196616 | tf_op jit(solution)/shard_map/ppermute | solution.py:94
  73.4 4.1 %slice-start = ((s8[11010048]{0:T(1024)(128)(4,1)}), s8[4194304]{0:T(1024)(128)(4,1)S(1)}, s32[]{:S(2)}) async-start(s8[11010048]{0:T(1024)(128)(4,1)} %bitcast.30), calls=%async_computation | async-start | bytes 8388608
  73.5 5.0 %slice-start.1 = ((s8[11010048]{0:T(1024)(128)(4,1)}), s8[4194304]{0:T(1024)(128)(4,1)S(1)}, s32[]{:S(2)}) async-start(s8[11010048]{0:T(1024)(128)(4,1)} %bitcast.30), calls=%async_computation.1 | async-start | bytes 8388608
  73.5 5.8 %slice-start.2 = ((s8[11010048]{0:T(1024)(128)(4,1)}), s8[2621440]{0:T(1024)(128)(4,1)S(1)}, s32[]{:S(2)}) async-start(s8[11010048]{0:T(1024)(128)(4,1)} %bitcast.30), calls=%async_computation.2 | async-start | bytes 5242880
  73.5 5.9 %copy-start.1 = (bf16[256,1792]{1,0:T(8,128)(2,1)S(1)}, bf16[256,1792]{1,0:T(8,128)(2,1)}, u32[]{:S(2)}) copy-start(bf16[256,1792]{1,0:T(8,128)(2,1)} %dhidden.1) | copy-start | bytes 2752516
  73.5 3.9 %collective-permute-start.19 = (bf16[128,128]{1,0:T(8,128)(2,1)S(1)}, bf16[128,128]{1,0:T(8,128)(2,1)S(1)}, u32[]{:S(2)}, u32[]{:S(2)}) collective-permute-start(bf16[128,128]{1,0:T(8,128)(2,1)S(1)} %fusion.2), channel_id=1, source_target_pairs={{0,1},{1,0},{2,3},{3,2},{4,5},{5,4},{6,7},{7,6},{8,9},{9,8},{10,11... | collective-permute-start | bytes 98312 | tf_op jit(solution)/shard_map/ppermute | solution.py:67
  86.9 1.3 collective-permute-start.20
  88.3 4.9 %collective-permute-start.21 = (f32[128,128]{1,0:T(8,128)S(1)}, f32[128,128]{1,0:T(8,128)S(1)}, u32[]{:S(2)}, u32[]{:S(2)}) collective-permute-start(f32[128,128]{1,0:T(8,128)S(1)} %slice_add_fusion), channel_id=1, source_target_pairs={{0,2},{1,3},{2,0},{3,1},{4,6},{5,7},{6,4},{7,5},{8,10},{9,11},{10,... | collective-permute-start | bytes 196616 | tf_op jit(solution)/shard_map/ppermute | solution.py:94
  93.2 4.3 %collective-permute-start.22 = (f32[128,128]{1,0:T(8,128)S(1)}, f32[128,128]{1,0:T(8,128)S(1)}, u32[]{:S(2)}, u32[]{:S(2)}) collective-permute-start(f32[128,128]{1,0:T(8,128)S(1)} %add.303), channel_id=1, source_target_pairs={{0,4},{1,5},{2,6},{3,7},{4,0},{5,1},{6,2},{7,3},{8,12},{9,13},{10,... | collective-permute-start | bytes 196616 | tf_op jit(solution)/shard_map/ppermute | solution.py:94
  97.6 14.7 %collective-permute-start.23 = (f32[128,128]{1,0:T(8,128)S(1)}, f32[128,128]{1,0:T(8,128)S(1)}, u32[]{:S(2)}, u32[]{:S(2)}) collective-permute-start(f32[128,128]{1,0:T(8,128)S(1)} %add.304), channel_id=1, source_target_pairs={{0,8},{1,9},{2,10},{3,11},{4,12},{5,13},{6,14},{7,15},{8,0},{9,1},... | collective-permute-start | bytes 196616 | tf_op jit(solution)/shard_map/ppermute | solution.py:94
  112.4 1.3 collective-permute-start.24
  113.7 3.5 %collective-permute-start.25 = (bf16[128,5120]{1,0:T(8,128)(2,1)S(1)}, bf16[128,5120]{1,0:T(8,128)(2,1)S(1)}, u32[]{:S(2)}, u32[]{:S(2)}) collective-permute-start(bf16[128,5120]{1,0:T(8,128)(2,1)S(1)} %get-tuple-element.52), channel_id=1, source_target_pairs={{0,1},{1,0},{2,3},{3,2},{4,5},{5,4},{6,7},{7,6},{8,9},{9,8},{10,11... | collective-permute-start | bytes 3932168 | tf_op jit(solution)/shard_map/ppermute | solution.py:67
  115.2 1.9 %collective-permute-start.26 = (f32[128,512]{1,0:T(8,128)S(1)}, f32[128,512]{1,0:T(8,128)S(1)}, u32[]{:S(2)}, u32[]{:S(2)}) collective-permute-start(f32[128,512]{1,0:T(8,128)S(1)} %get-tuple-element.54), channel_id=1, source_target_pairs={{0,1},{1,0},{2,3},{3,2},{4,5},{5,4},{6,7},{7,6},{8,9},{9,8},{10,11... | collective-permute-start | bytes 786440 | tf_op jit(solution)/shard_map/ppermute | solution.py:67
  120.3 17.1 %collective-permute-start.27 = (bf16[64,5120]{1,0:T(8,128)(2,1)}, bf16[64,5120]{1,0:T(8,128)(2,1)}, u32[]{:S(2)}, u32[]{:S(2)}) collective-permute-start(bf16[64,5120]{1,0:T(8,128)(2,1)} %get-tuple-element.56), channel_id=1, source_target_pairs={{0,2},{1,3},{2,0},{3,1},{4,6},{5,7},{6,4},{7,5},{8,10},{9,11},{10,... | collective-permute-start | bytes 1966088 | tf_op jit(solution)/shard_map/ppermute | solution.py:67
  121.2 9.3 %copy-start.3 = (bf16[256,512]{1,0:T(8,128)(2,1)S(1)}, bf16[256,512]{1,0:T(8,128)(2,1)}, u32[]{:S(2)}) copy-start(bf16[256,512]{1,0:T(8,128)(2,1)} %copy-done.2) | copy-start | bytes 786436
  137.4 2.3 %collective-permute-start.29 = (bf16[128,3072]{1,0:T(8,128)(2,1)S(1)}, bf16[128,3072]{1,0:T(8,128)(2,1)S(1)}, u32[]{:S(2)}, u32[]{:S(2)}) collective-permute-start(bf16[128,3072]{1,0:T(8,128)(2,1)S(1)} %get-tuple-element.62), channel_id=1, source_target_pairs={{0,1},{1,0},{2,3},{3,2},{4,5},{5,4},{6,7},{7,6},{8,9},{9,8},{10,11... | collective-permute-start | bytes 2359304 | tf_op jit(solution)/shard_map/ppermute | solution.py:67
  140.8 11.2 %collective-permute-start.30 = (bf16[64,3072]{1,0:T(8,128)(2,1)S(1)}, bf16[64,3072]{1,0:T(8,128)(2,1)S(1)}, u32[]{:S(2)}, u32[]{:S(2)}) collective-permute-start(bf16[64,3072]{1,0:T(8,128)(2,1)S(1)} %get-tuple-element.63), channel_id=1, source_target_pairs={{0,2},{1,3},{2,0},{3,1},{4,6},{5,7},{6,4},{7,5},{8,10},{9,11},{10,... | collective-permute-start | bytes 1179656 | tf_op jit(solution)/shard_map/ppermute | solution.py:67
  141.7 13.6 %collective-permute-start.32 = (bf16[16,5120]{1,0:T(8,128)(2,1)S(1)}, bf16[16,5120]{1,0:T(8,128)(2,1)S(1)}, u32[]{:S(2)}, u32[]{:S(2)}) collective-permute-start(bf16[16,5120]{1,0:T(8,128)(2,1)S(1)} %get-tuple-element.73), channel_id=1, source_target_pairs={{0,12},{1,13},{2,14},{3,15},{4,0},{5,1},{6,2},{7,3},{8,4},{9,5},{1... | collective-permute-start | bytes 491528 | tf_op jit(solution)/shard_map/ppermute | solution.py:67
  144.9 19.2 %collective-permute-start.31 = (bf16[16,5120]{1,0:T(8,128)(2,1)S(1)}, bf16[16,5120]{1,0:T(8,128)(2,1)S(1)}, u32[]{:S(2)}, u32[]{:S(2)}) collective-permute-start(bf16[16,5120]{1,0:T(8,128)(2,1)S(1)} %get-tuple-element.74), channel_id=1, source_target_pairs={{0,8},{1,9},{2,10},{3,11},{4,12},{5,13},{6,14},{7,15},{8,0},{9,1},... | collective-permute-start | bytes 491528 | tf_op jit(solution)/shard_map/ppermute | solution.py:67
  144.9 19.2 %collective-permute-start.28 = (bf16[16,5120]{1,0:T(8,128)(2,1)S(1)}, bf16[16,5120]{1,0:T(8,128)(2,1)S(1)}, u32[]{:S(2)}, u32[]{:S(2)}) collective-permute-start(bf16[16,5120]{1,0:T(8,128)(2,1)S(1)} %get-tuple-element.72), channel_id=1, source_target_pairs={{0,4},{1,5},{2,6},{3,7},{4,8},{5,9},{6,10},{7,11},{8,12},{9,13},{1... | collective-permute-start | bytes 491528 | tf_op jit(solution)/shard_map/ppermute | solution.py:67
  152.2 11.9 %collective-permute-start.35 = (bf16[16,3072]{1,0:T(8,128)(2,1)S(1)}, bf16[16,3072]{1,0:T(8,128)(2,1)S(1)}, u32[]{:S(2)}, u32[]{:S(2)}) collective-permute-start(bf16[16,3072]{1,0:T(8,128)(2,1)S(1)} %get-tuple-element.78), channel_id=1, source_target_pairs={{0,12},{1,13},{2,14},{3,15},{4,0},{5,1},{6,2},{7,3},{8,4},{9,5},{1... | collective-permute-start | bytes 294920 | tf_op jit(solution)/shard_map/ppermute | solution.py:67
  155.3 12.3 %collective-permute-start.34 = (bf16[16,3072]{1,0:T(8,128)(2,1)S(1)}, bf16[16,3072]{1,0:T(8,128)(2,1)S(1)}, u32[]{:S(2)}, u32[]{:S(2)}) collective-permute-start(bf16[16,3072]{1,0:T(8,128)(2,1)S(1)} %get-tuple-element.79), channel_id=1, source_target_pairs={{0,8},{1,9},{2,10},{3,11},{4,12},{5,13},{6,14},{7,15},{8,0},{9,1},... | collective-permute-start | bytes 294920 | tf_op jit(solution)/shard_map/ppermute | solution.py:67
  155.3 12.3 %collective-permute-start.33 = (bf16[16,3072]{1,0:T(8,128)(2,1)S(1)}, bf16[16,3072]{1,0:T(8,128)(2,1)S(1)}, u32[]{:S(2)}, u32[]{:S(2)}) collective-permute-start(bf16[16,3072]{1,0:T(8,128)(2,1)S(1)} %get-tuple-element.77), channel_id=1, source_target_pairs={{0,4},{1,5},{2,6},{3,7},{4,8},{5,9},{6,10},{7,11},{8,12},{9,13},{1... | collective-permute-start | bytes 294920 | tf_op jit(solution)/shard_map/ppermute | solution.py:67

commit v13 on v12

--- a/solution.py
+++ b/solution.py
@@ -347,7 +347,7 @@
             jax.ShapeDtypeStruct((tokens, hidden), BF16),
             jax.ShapeDtypeStruct((tokens, wide), F32),
         ],
-        compiler_params=params(20),
+        compiler_params=params(44),
         cost_estimate=cost(
             4 * tokens * hidden * segments * wide, hidden * (tokens * 14 + segments * wide * 2)
         ),

time: 169 us -> 168 us (level)
  local copies, waits for them, and re-layouts: 4.84 us -> 2.9 us
    unnamed x18 -> x12, local copies, waits for them, and re-layouts: 1.99 us -> 0.04 us
where the time goes in v13:
time: 168 us
  Pallas kernels  86.9 us (52%)
  starting transfers between devices  37.1 us (22%)
  waiting for transfers between devices  34.3 us (20%)
  other arithmetic  5.25 us (3%)
  local copies, waits for them, and re-layouts  2.9 us (2%)
    ppermute x30, waiting for transfers between devices, move(): return lax.ppermute(x, 'tensor', pairs)  32.6 us
    pallas_call x6, Pallas kernels, forward_chunk(): pl.pallas_call(functools.partial(forward_kernel, len(pieces), low, count,...  31.4 us
    ppermute x30, starting transfers between devices, move(): return lax.ppermute(x, 'tensor', pairs)  29.4 us
    pallas_call x2, Pallas kernels, backward_chunk(): pl.pallas_call(functools.partial(backward_kernel, count, first), grid=(co...  23.1 us
    pallas_call x3, Pallas kernels, grad_b_of(): pl.pallas_call(functools.partial(grad_b_kernel, first, last - first), gri...  11.9 us
    pallas_call x1, Pallas kernels, middle(): pl.pallas_call(functools.partial(middle_kernel, rows), grid_spec=pltpu.Pr...  8.64 us
    ppermute x6, starting transfers between devices, exchange_sum(): x = x + lax.ppermute(x, 'tensor', pairs)  7.69 us
    pallas_call x1, Pallas kernels, grad_a_of(): pl.pallas_call(grad_a_kernel, grid=(adapters // per,), in_specs=[full(col...  4.68 us
  transfers between devices with their start and end apart: 36, of which 18 were waited for; matrix products, arithmetic and copies ran while one was open for 4% of the time, Pallas kernels for 43%

profile of v13, /device:TPU:0, one launch (start us, length us, event | category | flops | bytes accessed | tf_op | source)
XLA Modules:
  0.0 167.5 jit_solution(14631337284625479182)
XLA Ops:
  0.6 0.9 slice_bitcast_fusion
  1.5 3.1 %collective-permute-start.2 = (bf16[16,3072]{1,0:T(8,128)(2,1)S(1)}, bf16[16,3072]{1,0:T(8,128)(2,1)S(1)}, u32[]{:S(2)}, u32[]{:S(2)}) collective-permute-start(bf16[16,3072]{1,0:T(8,128)(2,1)S(1)} %get-tuple-element.81), channel_id=1, source_target_pairs={{0,4},{1,5},{2,6},{3,7},{4,8},{5,9},{6,10},{7,11},{8,12},{9,13},{1... | collective-permute-start | bytes 294920 | tf_op jit(solution)/shard_map/ppermute | solution.py:67
  4.6 2.6 %collective-permute-start.1 = (bf16[16,3072]{1,0:T(8,128)(2,1)S(1)}, bf16[16,3072]{1,0:T(8,128)(2,1)S(1)}, u32[]{:S(2)}, u32[]{:S(2)}) collective-permute-start(bf16[16,3072]{1,0:T(8,128)(2,1)S(1)} %get-tuple-element.81), channel_id=1, source_target_pairs={{0,8},{1,9},{2,10},{3,11},{4,12},{5,13},{6,14},{7,15},{8,0},{9,1},... | collective-permute-start | bytes 294920 | tf_op jit(solution)/shard_map/ppermute | solution.py:67
  7.2 1.3 collective-permute-start
  8.6 0.9 slice.60
  11.3 2.5 %collective-permute-done.1 = bf16[16,3072]{1,0:T(8,128)(2,1)S(1)} collective-permute-done((bf16[16,3072]{1,0:T(8,128)(2,1)S(1)}, bf16[16,3072]{1,0:T(8,128)(2,1)S(1)}, u32[]{:S(2)}, u32[]{:S(2)}) %collective-permute-start.1) | collective-permute-done | bytes 98336 | tf_op jit(solution)/shard_map/ppermute | solution.py:67
  13.9 2.6 %collective-permute-start.5 = (bf16[16,5120]{1,0:T(8,128)(2,1)S(1)}, bf16[16,5120]{1,0:T(8,128)(2,1)S(1)}, u32[]{:S(2)}, u32[]{:S(2)}) collective-permute-start(bf16[16,5120]{1,0:T(8,128)(2,1)S(1)} %slice.60), channel_id=1, source_target_pairs={{0,4},{1,5},{2,6},{3,7},{4,8},{5,9},{6,10},{7,11},{8,12},{9,13},{1... | collective-permute-start | bytes 491528 | tf_op jit(solution)/shard_map/ppermute | solution.py:67
  16.5 1.6 collective-permute-start.4
  20.0 1.5 collective-permute-start.8
  21.5 1.5 collective-permute-done.5
  23.0 5.9 %collective-permute-done.4 = bf16[16,5120]{1,0:T(8,128)(2,1)S(1)} collective-permute-done((bf16[16,5120]{1,0:T(8,128)(2,1)S(1)}, bf16[16,5120]{1,0:T(8,128)(2,1)S(1)}, u32[]{:S(2)}, u32[]{:S(2)}) %collective-permute-start.4) | collective-permute-done | bytes 163872 | tf_op jit(solution)/shard_map/ppermute | solution.py:67
  29.0 1.5 collective-permute-done.8.rest_1_.rest_9_
  30.5 1.6 collective-permute-start.7
  32.3 9.2 %shard_map.103.rest_5_ = f32[2,256,1792]{2,1,0:T(8,128)S(1)} custom-call(bf16[64,3072]{1,0:T(8,128)(2,1)S(1)} %bitcast.32, bf16[64,3072]{1,0:T(8,128)(2,1)S(1)} %collective-permute-done.8.rest_1_.rest_9_, bf16[64,3072]{1,0:T(8,128)(2,1)S(1)} %collective-permute-done.9.rest_2_.rest_10_, bf16[64,3072]{1,0:T(8,128)(2,1)S(1)} %collective-permute-done.10.rest_3_.rest_11_, ...), custom_call_target="tpu_custom_call" | custom-call | flops 5637144576 | bytes 22020096 | tf_op jit(solution)/shard_map/pallas_call | solution.py:181
  42.1 1.3 collective-permute-start.6
  43.5 8.4 %shard_map.104.rest_5_ = f32[2,256,1792]{2,1,0:T(8,128)S(1)} custom-call(bf16[64,2560]{1,0:T(8,128)(2,1)S(1)} %get-tuple-element.75.rest_0_.rest_12_, bf16[64,2560]{1,0:T(8,128)(2,1)S(1)} %collective-permute-done.7.rest_1_.rest_13_, bf16[64,2560]{1,0:T(8,128)(2,1)S(1)} %collective-permute-done.11.rest_2_.rest_14_, ...), custom_call_target="tpu_custom_call", output_to_operand_aliasing={{}: (5, {})} | custom-call | flops 4697620480 | bytes 18350080 | tf_op jit(solution)/shard_map/pallas_call | solution.py:181
  52.7 1.1 collective-permute-done.14.rest_3_.rest_19_
  53.7 1.5 shard_map.109
  56.6 1.4 collective-permute-start.16
  58.0 2.7 %shard_map.105.rest_5_ = f32[2,256,1792]{2,1,0:T(8,128)S(1)} custom-call(bf16[64,2560]{1,0:T(8,128)(2,1)S(1)} %get-tuple-element.76.rest_0_.rest_16_, bf16[64,2560]{1,0:T(8,128)(2,1)S(1)} %collective-permute-done.6.rest_1_.rest_17_, bf16[64,2560]{1,0:T(8,128)(2,1)S(1)} %collective-permute-done.13.rest_2_.rest_18_, ...), custom_call_target="tpu_custom_call", output_to_operand_aliasing={{}: (5, {})} | custom-call | flops 671088640 | bytes 2621440 | tf_op jit(solution)/shard_map/pallas_call | solution.py:181
  61.1 2.6 %collective-permute-start.17 = (f32[128,128]{1,0:T(8,128)S(1)}, f32[128,128]{1,0:T(8,128)S(1)}, u32[]{:S(2)}, u32[]{:S(2)}) collective-permute-start(f32[128,128]{1,0:T(8,128)S(1)} %add.292), channel_id=1, source_target_pairs={{0,4},{1,5},{2,6},{3,7},{4,0},{5,1},{6,2},{7,3},{8,12},{9,13},{10,... | collective-permute-start | bytes 196616 | tf_op jit(solution)/shard_map/ppermute | solution.py:94
  63.7 3.7 %shard_map.106.rest_5_ = f32[2,256,1792]{2,1,0:T(8,128)S(1)} custom-call(bf16[64,2560]{1,0:T(8,128)(2,1)S(1)} %get-tuple-element.76.rest_0_.rest_16_, bf16[64,2560]{1,0:T(8,128)(2,1)S(1)} %collective-permute-done.6.rest_1_.rest_17_, bf16[64,2560]{1,0:T(8,128)(2,1)S(1)} %collective-permute-done.13.rest_2_.rest_18_, ...), custom_call_target="tpu_custom_call", output_to_operand_aliasing={{}: (5, {})} | custom-call | flops 1342177280 | bytes 5242880 | tf_op jit(solution)/shard_map/pallas_call | solution.py:181
  67.4 1.5 collective-permute-start.18
  68.9 3.7 %shard_map.107.rest_5_ = f32[2,256,1792]{2,1,0:T(8,128)S(1)} custom-call(bf16[64,2560]{1,0:T(8,128)(2,1)S(1)} %get-tuple-element.76.rest_0_.rest_16_, bf16[64,2560]{1,0:T(8,128)(2,1)S(1)} %collective-permute-done.6.rest_1_.rest_17_, bf16[64,2560]{1,0:T(8,128)(2,1)S(1)} %collective-permute-done.13.rest_2_.rest_18_, ...), custom_call_target="tpu_custom_call", output_to_operand_aliasing={{}: (5, {})} | custom-call | flops 1342177280 | bytes 5242880 | tf_op jit(solution)/shard_map/pallas_call | solution.py:181
  73.5 3.8 %shard_map.108.base = f32[2,256,1792]{2,1,0:T(8,128)S(1)} custom-call(bf16[64,2560]{1,0:T(8,128)(2,1)S(1)} %get-tuple-element.76.rest_0_.rest_16_, bf16[64,2560]{1,0:T(8,128)(2,1)S(1)} %collective-permute-done.6.rest_1_.rest_17_, bf16[64,2560]{1,0:T(8,128)(2,1)S(1)} %collective-permute-done.13.rest_2_.rest_18_, ...), custom_call_target="tpu_custom_call", output_to_operand_aliasing={{}: (5, {})} | custom-call | flops 1342177280 | bytes 5242880 | tf_op jit(solution)/shard_map/pallas_call | solution.py:181
  77.3 8.6 %shard_map.110 = (bf16[256,1792]{1,0:T(8,128)(2,1)S(1)}, bf16[256,1792]{1,0:T(8,128)(2,1)S(1)}, f32[256,128]{1,0:T(8,128)S(1)}) custom-call(s32[8]{0:T(128)S(1)} %bitcast.46, s32[16]{0:T(128)S(1)} %get-tuple-element.70.places, f32[2,256,1792]{2,1,0:T(8,128)S(1)} %shard_map.108.base, bf16[256,1792]{1,0:T(8,128)(2,1)S(1)} %copy-done.1, ...), custom_call_target="tpu_custom_call" | custom-call | flops 1879048192 | bytes 10092544 | tf_op jit(solution)/shard_map/pallas_call | solution.py:329
  87.4 1.3 collective-permute-start.21
  88.7 3.6 %shard_map.111.rest_0_ = f32[24,128,1792]{2,1,0:T(8,128)} custom-call(bf16[256,1792]{1,0:T(8,128)(2,1)S(1)} %get-tuple-element.57.dgate, bf16[256,1792]{1,0:T(8,128)(2,1)S(1)} %get-tuple-element.43.dup, bf16[256,256]{1,0:T(8,128)(2,1)S(1)} %fusion.1.order, bf16[256,128]{1,0:T(8,128)(2,1)S(1)} %bitcast.35, s32[1,256]{1,0:T(1,128)S(1)} %bitcast.40), custom_call_target="tpu_custom_call" | custom-call | flops 805306368 | bytes 6291456 | tf_op jit(solution)/shard_map/pallas_call | solution.py:404
  92.4 3.7 %shard_map.112.rest_0_ = f32[24,128,1792]{2,1,0:T(8,128)} custom-call(bf16[256,1792]{1,0:T(8,128)(2,1)S(1)} %get-tuple-element.57.dgate, bf16[256,1792]{1,0:T(8,128)(2,1)S(1)} %get-tuple-element.43.dup, bf16[256,256]{1,0:T(8,128)(2,1)S(1)} %fusion.1.order, bf16[256,128]{1,0:T(8,128)(2,1)S(1)} %bitcast.36, ...), custom_call_target="tpu_custom_call", output_to_operand_aliasing={{}: (5, {})} | custom-call | flops 805306368 | bytes 6291456 | tf_op jit(solution)/shard_map/pallas_call | solution.py:404
  97.5 13.9 %shard_map.113 = (bf16[128,5120]{1,0:T(8,128)(2,1)S(1)}, bf16[128,5120]{1,0:T(8,128)(2,1)S(1)}) custom-call(bf16[2,8192,1792]{2,1,0:T(8,128)(2,1)} %frozen.3, bf16[256,1792]{1,0:T(8,128)(2,1)S(1)} %get-tuple-element.57.dgate, bf16[256,1792]{1,0:T(8,128)(2,1)S(1)} %get-tuple-element.43.dup), custom_call_target="tpu_custom_call" | custom-call | flops 9395240960 | bytes 36700160 | tf_op jit(solution)/shard_map/pallas_call | solution.py:520
  111.7 1.1 collective-permute-done.24
  113.0 1.4 shard_map.114
  114.9 1.4 collective-permute-done.26.side_far
  116.3 3.1 %shard_map.115 = (bf16[64,5120]{1,0:T(8,128)(2,1)S(1)}, bf16[64,5120]{1,0:T(8,128)(2,1)}) custom-call(s32[2]{0:T(128)S(1)} %pad_add_fusion.at, bf16[128,5120]{1,0:T(8,128)(2,1)S(1)} %get-tuple-element.49.near, bf16[128,5120]{1,0:T(8,128)(2,1)S(1)} %collective-permute-done.25.far, f32[128,512]{1,0:T(8,128)S(1)} %get-tuple-element.53.side, ...), custom_call_target="tpu_custom_call" | custom-call | flops 1310720 | bytes 3932160 | tf_op jit(solution)/shard_map/pallas_call | solution.py:562
  120.3 9.2 %shard_map.116 = (bf16[128,3072]{1,0:T(8,128)(2,1)S(1)}, bf16[128,3072]{1,0:T(8,128)(2,1)S(1)}) custom-call(bf16[2,8192,1792]{2,1,0:T(8,128)(2,1)} %frozen.3, bf16[256,1792]{1,0:T(8,128)(2,1)S(1)} %get-tuple-element.57.dgate, bf16[256,1792]{1,0:T(8,128)(2,1)S(1)} %get-tuple-element.43.dup), custom_call_target="tpu_custom_call" | custom-call | flops 5637144576 | bytes 22020096 | tf_op jit(solution)/shard_map/pallas_call | solution.py:520
  129.6 4.7 %shard_map.117 = f32[24,512,128]{2,1,0:T(8,128)} custom-call(bf16[256,512]{1,0:T(8,128)(2,1)S(1)} %copy-done.3, bf16[256,256]{1,0:T(8,128)(2,1)S(1)} %fusion.1.order, bf16[256,128]{1,0:T(8,128)(2,1)S(1)} %bitcast.39, s32[256,1]{1,0:T(8,128)S(1)} %copy.25.adapter), custom_call_target="tpu_custom_call" | custom-call | flops 805306368 | bytes 6291456 | tf_op jit(solution)/shard_map/pallas_call | solution.py:448
  134.3 2.2 %collective-permute-done.27 = bf16[64,5120]{1,0:T(8,128)(2,1)} collective-permute-done((bf16[64,5120]{1,0:T(8,128)(2,1)}, bf16[64,5120]{1,0:T(8,128)(2,1)}, u32[]{:S(2)}, u32[]{:S(2)}) %collective-permute-start.27) | collective-permute-done | bytes 655392 | tf_op jit(solution)/shard_map/ppermute | solution.py:67
  136.5 1.2 add_convert_fusion
  137.7 1.0 collective-permute-done.29.far
  138.8 1.2 shard_map.118
  140.8 3.1 %collective-permute-start.32 = (bf16[16,5120]{1,0:T(8,128)(2,1)S(1)}, bf16[16,5120]{1,0:T(8,128)(2,1)S(1)}, u32[]{:S(2)}, u32[]{:S(2)}) collective-permute-start(bf16[16,5120]{1,0:T(8,128)(2,1)S(1)} %get-tuple-element.73), channel_id=1, source_target_pairs={{0,12},{1,13},{2,14},{3,15},{4,0},{5,1},{6,2},{7,3},{8,4},{9,5},{1... | collective-permute-start | bytes 491528 | tf_op jit(solution)/shard_map/ppermute | solution.py:67
  144.0 1.2 collective-permute-start.28
  145.1 4.6 %shard_map.119 = f32[24,128,1792]{2,1,0:T(8,128)} custom-call(bf16[256,1792]{1,0:T(8,128)(2,1)S(1)} %get-tuple-element.57.dgate, bf16[256,1792]{1,0:T(8,128)(2,1)S(1)} %get-tuple-element.43.dup, bf16[256,256]{1,0:T(8,128)(2,1)S(1)} %fusion.1.order, bf16[256,128]{1,0:T(8,128)(2,1)S(1)} %bitcast.37, ...), custom_call_target="tpu_custom_call", output_to_operand_aliasing={{}: (5, {})} | custom-call | flops 1207959552 | bytes 9437184 | tf_op jit(solution)/shard_map/pallas_call | solution.py:404
  149.7 1.5 collective-permute-done.30
  151.3 3.1 %collective-permute-start.35 = (bf16[16,3072]{1,0:T(8,128)(2,1)S(1)}, bf16[16,3072]{1,0:T(8,128)(2,1)S(1)}, u32[]{:S(2)}, u32[]{:S(2)}) collective-permute-start(bf16[16,3072]{1,0:T(8,128)(2,1)S(1)} %get-tuple-element.78), channel_id=1, source_target_pairs={{0,12},{1,13},{2,14},{3,15},{4,0},{5,1},{6,2},{7,3},{8,4},{9,5},{1... | collective-permute-start | bytes 294920 | tf_op jit(solution)/shard_map/ppermute | solution.py:67
  154.4 1.2 collective-permute-start.33
  155.6 7.6 %collective-permute-done.31 = bf16[16,5120]{1,0:T(8,128)(2,1)S(1)} collective-permute-done((bf16[16,5120]{1,0:T(8,128)(2,1)S(1)}, bf16[16,5120]{1,0:T(8,128)(2,1)S(1)}, u32[]{:S(2)}, u32[]{:S(2)}) %collective-permute-start.31) | collective-permute-done | bytes 163872 | tf_op jit(solution)/shard_map/ppermute | solution.py:67
  163.2 3.5 %collective-permute-done.34 = bf16[16,3072]{1,0:T(8,128)(2,1)S(1)} collective-permute-done((bf16[16,3072]{1,0:T(8,128)(2,1)S(1)}, bf16[16,3072]{1,0:T(8,128)(2,1)S(1)}, u32[]{:S(2)}, u32[]{:S(2)}) %collective-permute-start.34) | collective-permute-done | bytes 98336 | tf_op jit(solution)/shard_map/ppermute | solution.py:67
  (111 shorter events, 14.8 us)
Async XLA Ops:
  1.5 9.7 %collective-permute-start.2 = (bf16[16,3072]{1,0:T(8,128)(2,1)S(1)}, bf16[16,3072]{1,0:T(8,128)(2,1)S(1)}, u32[]{:S(2)}, u32[]{:S(2)}) collective-permute-start(bf16[16,3072]{1,0:T(8,128)(2,1)S(1)} %get-tuple-element.81), channel_id=1, source_target_pairs={{0,4},{1,5},{2,6},{3,7},{4,8},{5,9},{6,10},{7,11},{8,12},{9,13},{1... | collective-permute-start | bytes 294920 | tf_op jit(solution)/shard_map/ppermute | solution.py:67
  4.6 9.2 %collective-permute-start.1 = (bf16[16,3072]{1,0:T(8,128)(2,1)S(1)}, bf16[16,3072]{1,0:T(8,128)(2,1)S(1)}, u32[]{:S(2)}, u32[]{:S(2)}) collective-permute-start(bf16[16,3072]{1,0:T(8,128)(2,1)S(1)} %get-tuple-element.81), channel_id=1, source_target_pairs={{0,8},{1,9},{2,10},{3,11},{4,12},{5,13},{6,14},{7,15},{8,0},{9,1},... | collective-permute-start | bytes 294920 | tf_op jit(solution)/shard_map/ppermute | solution.py:67
  7.2 6.6 %collective-permute-start = (bf16[16,3072]{1,0:T(8,128)(2,1)S(1)}, bf16[16,3072]{1,0:T(8,128)(2,1)S(1)}, u32[]{:S(2)}, u32[]{:S(2)}) collective-permute-start(bf16[16,3072]{1,0:T(8,128)(2,1)S(1)} %get-tuple-element.81), channel_id=1, source_target_pairs={{0,12},{1,13},{2,14},{3,15},{4,0},{5,1},{6,2},{7,3},{8,4},{9,5},{1... | collective-permute-start | bytes 294920 | tf_op jit(solution)/shard_map/ppermute | solution.py:67
  13.9 9.1 %collective-permute-start.5 = (bf16[16,5120]{1,0:T(8,128)(2,1)S(1)}, bf16[16,5120]{1,0:T(8,128)(2,1)S(1)}, u32[]{:S(2)}, u32[]{:S(2)}) collective-permute-start(bf16[16,5120]{1,0:T(8,128)(2,1)S(1)} %slice.60), channel_id=1, source_target_pairs={{0,4},{1,5},{2,6},{3,7},{4,8},{5,9},{6,10},{7,11},{8,12},{9,13},{1... | collective-permute-start | bytes 491528 | tf_op jit(solution)/shard_map/ppermute | solution.py:67
  16.5 12.4 %collective-permute-start.4 = (bf16[16,5120]{1,0:T(8,128)(2,1)S(1)}, bf16[16,5120]{1,0:T(8,128)(2,1)S(1)}, u32[]{:S(2)}, u32[]{:S(2)}) collective-permute-start(bf16[16,5120]{1,0:T(8,128)(2,1)S(1)} %slice.60), channel_id=1, source_target_pairs={{0,8},{1,9},{2,10},{3,11},{4,12},{5,13},{6,14},{7,15},{8,0},{9,1},... | collective-permute-start | bytes 491528 | tf_op jit(solution)/shard_map/ppermute | solution.py:67
  18.1 10.8 %collective-permute-start.3 = (bf16[16,5120]{1,0:T(8,128)(2,1)S(1)}, bf16[16,5120]{1,0:T(8,128)(2,1)S(1)}, u32[]{:S(2)}, u32[]{:S(2)}) collective-permute-start(bf16[16,5120]{1,0:T(8,128)(2,1)S(1)} %slice.60), channel_id=1, source_target_pairs={{0,12},{1,13},{2,14},{3,15},{4,0},{5,1},{6,2},{7,3},{8,4},{9,5},{1... | collective-permute-start | bytes 491528 | tf_op jit(solution)/shard_map/ppermute | solution.py:67
  20.0 10.5 %collective-permute-start.8 = (bf16[64,3072]{1,0:T(8,128)(2,1)S(1)}, bf16[64,3072]{1,0:T(8,128)(2,1)S(1)}, u32[]{:S(2)}, u32[]{:S(2)}) collective-permute-start(bf16[64,3072]{1,0:T(8,128)(2,1)S(1)} %bitcast.30), channel_id=1, source_target_pairs={{0,2},{1,3},{2,0},{3,1},{4,6},{5,7},{6,4},{7,5},{8,10},{9,11},{10,... | collective-permute-start | bytes 1179656 | tf_op jit(solution)/shard_map/ppermute | solution.py:67
  21.5 10.8 %collective-permute-start.9 = (bf16[64,3072]{1,0:T(8,128)(2,1)S(1)}, bf16[64,3072]{1,0:T(8,128)(2,1)S(1)}, u32[]{:S(2)}, u32[]{:S(2)}) collective-permute-start(bf16[64,3072]{1,0:T(8,128)(2,1)S(1)} %bitcast.31), channel_id=1, source_target_pairs={{0,1},{1,0},{2,3},{3,2},{4,5},{5,4},{6,7},{7,6},{8,9},{9,8},{10,11... | collective-permute-start | bytes 1179656 | tf_op jit(solution)/shard_map/ppermute | solution.py:67
  30.4 1.9 %collective-permute-start.10 = (bf16[64,3072]{1,0:T(8,128)(2,1)S(1)}, bf16[64,3072]{1,0:T(8,128)(2,1)S(1)}, u32[]{:S(2)}, u32[]{:S(2)}) collective-permute-start(bf16[64,3072]{1,0:T(8,128)(2,1)S(1)} %collective-permute-done.8.rest_1_.rest_9_), channel_id=1, source_target_pairs={{0,1},{1,0},{2,3},{3,2},{4,5},{5,4},{6,7},{7,6},{8,9},{9,8},{10,11... | collective-permute-start | bytes 1179656 | tf_op jit(solution)/shard_map/ppermute | solution.py:67
  30.5 11.4 %copy-start.5 = (s32[24]{0:T(128)S(1)}, s32[24]{0:T(128)}, u32[]{:S(2)}) copy-start(s32[24]{0:T(128)} %param.15) | copy-start | bytes 292
  30.5 11.1 %collective-permute-start.7 = (bf16[64,2560]{1,0:T(8,128)(2,1)S(1)}, bf16[64,2560]{1,0:T(8,128)(2,1)S(1)}, u32[]{:S(2)}, u32[]{:S(2)}) collective-permute-start(bf16[64,2560]{1,0:T(8,128)(2,1)S(1)} %get-tuple-element.75.rest_0_.rest_12_), channel_id=1, source_target_pairs={{0,2},{1,3},{2,0},{3,1},{4,6},{5,7},{6,4},{7,5},{8,10},{9,11},{10,... | collective-permute-start | bytes 983048 | tf_op jit(solution)/shard_map/ppermute | solution.py:67
  32.1 11.4 %collective-permute-start.11 = (bf16[64,2560]{1,0:T(8,128)(2,1)S(1)}, bf16[64,2560]{1,0:T(8,128)(2,1)S(1)}, u32[]{:S(2)}, u32[]{:S(2)}) collective-permute-start(bf16[64,2560]{1,0:T(8,128)(2,1)S(1)} %get-tuple-element.75.rest_0_.rest_12_), channel_id=1, source_target_pairs={{0,1},{1,0},{2,3},{3,2},{4,5},{5,4},{6,7},{7,6},{8,9},{9,8},{10,11... | collective-permute-start | bytes 983048 | tf_op jit(solution)/shard_map/ppermute | solution.py:67
  41.6 1.9 %collective-permute-start.12 = (bf16[64,2560]{1,0:T(8,128)(2,1)S(1)}, bf16[64,2560]{1,0:T(8,128)(2,1)S(1)}, u32[]{:S(2)}, u32[]{:S(2)}) collective-permute-start(bf16[64,2560]{1,0:T(8,128)(2,1)S(1)} %collective-permute-done.7.rest_1_.rest_13_), channel_id=1, source_target_pairs={{0,1},{1,0},{2,3},{3,2},{4,5},{5,4},{6,7},{7,6},{8,9},{9,8},{10,11... | collective-permute-start | bytes 983048 | tf_op jit(solution)/shard_map/ppermute | solution.py:67
  42.1 11.6 %copy-start = (bf16[24,512,128]{2,1,0:T(8,128)(2,1)S(1)}, bf16[24,512,128]{2,1,0:T(8,128)(2,1)}, u32[]{:S(2)}) copy-start(bf16[24,512,128]{2,1,0:T(8,128)(2,1)} %rest_7_.3) | copy-start | bytes 9437188
  42.1 11.6 %copy-start.4 = (s32[1,8]{1,0:T(1,128)S(1)}, s32[1,8]{1,0:T(1,128)}, u32[]{:S(2)}) copy-start(s32[1,8]{1,0:T(1,128)} %param.13) | copy-start | bytes 100
  42.1 9.9 %collective-permute-start.6 = (bf16[64,2560]{1,0:T(8,128)(2,1)S(1)}, bf16[64,2560]{1,0:T(8,128)(2,1)S(1)}, u32[]{:S(2)}, u32[]{:S(2)}) collective-permute-start(bf16[64,2560]{1,0:T(8,128)(2,1)S(1)} %get-tuple-element.76.rest_0_.rest_16_), channel_id=1, source_target_pairs={{0,2},{1,3},{2,0},{3,1},{4,6},{5,7},{6,4},{7,5},{8,10},{9,11},{10,... | collective-permute-start | bytes 983048 | tf_op jit(solution)/shard_map/ppermute | solution.py:67
  43.4 9.2 %collective-permute-start.13 = (bf16[64,2560]{1,0:T(8,128)(2,1)S(1)}, bf16[64,2560]{1,0:T(8,128)(2,1)S(1)}, u32[]{:S(2)}, u32[]{:S(2)}) collective-permute-start(bf16[64,2560]{1,0:T(8,128)(2,1)S(1)} %get-tuple-element.76.rest_0_.rest_16_), channel_id=1, source_target_pairs={{0,1},{1,0},{2,3},{3,2},{4,5},{5,4},{6,7},{7,6},{8,9},{9,8},{10,11... | collective-permute-start | bytes 983048 | tf_op jit(solution)/shard_map/ppermute | solution.py:67
  52.0 1.7 collective-permute-start.14
  55.2 5.4 %copy-start.2 = (bf16[256,512]{1,0:T(8,128)(2,1)}, bf16[256,512]{1,0:T(8,128)(2,1)S(1)}, u32[]{:S(2)}) copy-start(bf16[256,512]{1,0:T(8,128)(2,1)S(1)} %get-tuple-element.60.columns) | copy-start | bytes 786436
  55.3 1.3 collective-permute-start.15
  56.6 4.4 %collective-permute-start.16 = (f32[128,128]{1,0:T(8,128)S(1)}, f32[128,128]{1,0:T(8,128)S(1)}, u32[]{:S(2)}, u32[]{:S(2)}) collective-permute-start(f32[128,128]{1,0:T(8,128)S(1)} %slice_add_fusion.1), channel_id=1, source_target_pairs={{0,2},{1,3},{2,0},{3,1},{4,6},{5,7},{6,4},{7,5},{8,10},{9,11},{10,... | collective-permute-start | bytes 196616 | tf_op jit(solution)/shard_map/ppermute | solution.py:94
  61.1 6.3 %collective-permute-start.17 = (f32[128,128]{1,0:T(8,128)S(1)}, f32[128,128]{1,0:T(8,128)S(1)}, u32[]{:S(2)}, u32[]{:S(2)}) collective-permute-start(f32[128,128]{1,0:T(8,128)S(1)} %add.292), channel_id=1, source_target_pairs={{0,4},{1,5},{2,6},{3,7},{4,0},{5,1},{6,2},{7,3},{8,12},{9,13},{10,... | collective-permute-start | bytes 196616 | tf_op jit(solution)/shard_map/ppermute | solution.py:94
  67.4 5.9 %collective-permute-start.18 = (f32[128,128]{1,0:T(8,128)S(1)}, f32[128,128]{1,0:T(8,128)S(1)}, u32[]{:S(2)}, u32[]{:S(2)}) collective-permute-start(f32[128,128]{1,0:T(8,128)S(1)} %add.293), channel_id=1, source_target_pairs={{0,8},{1,9},{2,10},{3,11},{4,12},{5,13},{6,14},{7,15},{8,0},{9,1},... | collective-permute-start | bytes 196616 | tf_op jit(solution)/shard_map/ppermute | solution.py:94
  73.4 3.9 %copy-start.1 = (bf16[256,1792]{1,0:T(8,128)(2,1)S(1)}, bf16[256,1792]{1,0:T(8,128)(2,1)}, u32[]{:S(2)}) copy-start(bf16[256,1792]{1,0:T(8,128)(2,1)} %dhidden.1) | copy-start | bytes 2752516
  73.4 3.9 %collective-permute-start.19 = (bf16[128,128]{1,0:T(8,128)(2,1)S(1)}, bf16[128,128]{1,0:T(8,128)(2,1)S(1)}, u32[]{:S(2)}, u32[]{:S(2)}) collective-permute-start(bf16[128,128]{1,0:T(8,128)(2,1)S(1)} %fusion.2), channel_id=1, source_target_pairs={{0,1},{1,0},{2,3},{3,2},{4,5},{5,4},{6,7},{7,6},{8,9},{9,8},{10,11... | collective-permute-start | bytes 98312 | tf_op jit(solution)/shard_map/ppermute | solution.py:67
  86.0 1.4 collective-permute-start.20
  87.4 4.9 %collective-permute-start.21 = (f32[128,128]{1,0:T(8,128)S(1)}, f32[128,128]{1,0:T(8,128)S(1)}, u32[]{:S(2)}, u32[]{:S(2)}) collective-permute-start(f32[128,128]{1,0:T(8,128)S(1)} %slice_add_fusion), channel_id=1, source_target_pairs={{0,2},{1,3},{2,0},{3,1},{4,6},{5,7},{6,4},{7,5},{8,10},{9,11},{10,... | collective-permute-start | bytes 196616 | tf_op jit(solution)/shard_map/ppermute | solution.py:94
  92.3 4.3 %collective-permute-start.22 = (f32[128,128]{1,0:T(8,128)S(1)}, f32[128,128]{1,0:T(8,128)S(1)}, u32[]{:S(2)}, u32[]{:S(2)}) collective-permute-start(f32[128,128]{1,0:T(8,128)S(1)} %add.303), channel_id=1, source_target_pairs={{0,4},{1,5},{2,6},{3,7},{4,0},{5,1},{6,2},{7,3},{8,12},{9,13},{10,... | collective-permute-start | bytes 196616 | tf_op jit(solution)/shard_map/ppermute | solution.py:94
  96.7 14.7 %collective-permute-start.23 = (f32[128,128]{1,0:T(8,128)S(1)}, f32[128,128]{1,0:T(8,128)S(1)}, u32[]{:S(2)}, u32[]{:S(2)}) collective-permute-start(f32[128,128]{1,0:T(8,128)S(1)} %add.304), channel_id=1, source_target_pairs={{0,8},{1,9},{2,10},{3,11},{4,12},{5,13},{6,14},{7,15},{8,0},{9,1},... | collective-permute-start | bytes 196616 | tf_op jit(solution)/shard_map/ppermute | solution.py:94
  111.5 1.3 collective-permute-start.24
  112.8 3.5 %collective-permute-start.25 = (bf16[128,5120]{1,0:T(8,128)(2,1)S(1)}, bf16[128,5120]{1,0:T(8,128)(2,1)S(1)}, u32[]{:S(2)}, u32[]{:S(2)}) collective-permute-start(bf16[128,5120]{1,0:T(8,128)(2,1)S(1)} %get-tuple-element.52), channel_id=1, source_target_pairs={{0,1},{1,0},{2,3},{3,2},{4,5},{5,4},{6,7},{7,6},{8,9},{9,8},{10,11... | collective-permute-start | bytes 3932168 | tf_op jit(solution)/shard_map/ppermute | solution.py:67
  114.3 1.9 %collective-permute-start.26 = (f32[128,512]{1,0:T(8,128)S(1)}, f32[128,512]{1,0:T(8,128)S(1)}, u32[]{:S(2)}, u32[]{:S(2)}) collective-permute-start(f32[128,512]{1,0:T(8,128)S(1)} %get-tuple-element.54), channel_id=1, source_target_pairs={{0,1},{1,0},{2,3},{3,2},{4,5},{5,4},{6,7},{7,6},{8,9},{9,8},{10,11... | collective-permute-start | bytes 786440 | tf_op jit(solution)/shard_map/ppermute | solution.py:67
  119.4 17.1 %collective-permute-start.27 = (bf16[64,5120]{1,0:T(8,128)(2,1)}, bf16[64,5120]{1,0:T(8,128)(2,1)}, u32[]{:S(2)}, u32[]{:S(2)}) collective-permute-start(bf16[64,5120]{1,0:T(8,128)(2,1)} %get-tuple-element.56), channel_id=1, source_target_pairs={{0,2},{1,3},{2,0},{3,1},{4,6},{5,7},{6,4},{7,5},{8,10},{9,11},{10,... | collective-permute-start | bytes 1966088 | tf_op jit(solution)/shard_map/ppermute | solution.py:67
  120.3 9.3 %copy-start.3 = (bf16[256,512]{1,0:T(8,128)(2,1)S(1)}, bf16[256,512]{1,0:T(8,128)(2,1)}, u32[]{:S(2)}) copy-start(bf16[256,512]{1,0:T(8,128)(2,1)} %copy-done.2) | copy-start | bytes 786436
  136.5 2.3 %collective-permute-start.29 = (bf16[128,3072]{1,0:T(8,128)(2,1)S(1)}, bf16[128,3072]{1,0:T(8,128)(2,1)S(1)}, u32[]{:S(2)}, u32[]{:S(2)}) collective-permute-start(bf16[128,3072]{1,0:T(8,128)(2,1)S(1)} %get-tuple-element.62), channel_id=1, source_target_pairs={{0,1},{1,0},{2,3},{3,2},{4,5},{5,4},{6,7},{7,6},{8,9},{9,8},{10,11... | collective-permute-start | bytes 2359304 | tf_op jit(solution)/shard_map/ppermute | solution.py:67
  139.9 11.2 %collective-permute-start.30 = (bf16[64,3072]{1,0:T(8,128)(2,1)S(1)}, bf16[64,3072]{1,0:T(8,128)(2,1)S(1)}, u32[]{:S(2)}, u32[]{:S(2)}) collective-permute-start(bf16[64,3072]{1,0:T(8,128)(2,1)S(1)} %get-tuple-element.63), channel_id=1, source_target_pairs={{0,2},{1,3},{2,0},{3,1},{4,6},{5,7},{6,4},{7,5},{8,10},{9,11},{10,... | collective-permute-start | bytes 1179656 | tf_op jit(solution)/shard_map/ppermute | solution.py:67
  140.8 13.6 %collective-permute-start.32 = (bf16[16,5120]{1,0:T(8,128)(2,1)S(1)}, bf16[16,5120]{1,0:T(8,128)(2,1)S(1)}, u32[]{:S(2)}, u32[]{:S(2)}) collective-permute-start(bf16[16,5120]{1,0:T(8,128)(2,1)S(1)} %get-tuple-element.73), channel_id=1, source_target_pairs={{0,12},{1,13},{2,14},{3,15},{4,0},{5,1},{6,2},{7,3},{8,4},{9,5},{1... | collective-permute-start | bytes 491528 | tf_op jit(solution)/shard_map/ppermute | solution.py:67
  143.9 19.2 %collective-permute-start.31 = (bf16[16,5120]{1,0:T(8,128)(2,1)S(1)}, bf16[16,5120]{1,0:T(8,128)(2,1)S(1)}, u32[]{:S(2)}, u32[]{:S(2)}) collective-permute-start(bf16[16,5120]{1,0:T(8,128)(2,1)S(1)} %get-tuple-element.74), channel_id=1, source_target_pairs={{0,8},{1,9},{2,10},{3,11},{4,12},{5,13},{6,14},{7,15},{8,0},{9,1},... | collective-permute-start | bytes 491528 | tf_op jit(solution)/shard_map/ppermute | solution.py:67
  144.0 19.2 %collective-permute-start.28 = (bf16[16,5120]{1,0:T(8,128)(2,1)S(1)}, bf16[16,5120]{1,0:T(8,128)(2,1)S(1)}, u32[]{:S(2)}, u32[]{:S(2)}) collective-permute-start(bf16[16,5120]{1,0:T(8,128)(2,1)S(1)} %get-tuple-element.72), channel_id=1, source_target_pairs={{0,4},{1,5},{2,6},{3,7},{4,8},{5,9},{6,10},{7,11},{8,12},{9,13},{1... | collective-permute-start | bytes 491528 | tf_op jit(solution)/shard_map/ppermute | solution.py:67
  151.3 11.9 %collective-permute-start.35 = (bf16[16,3072]{1,0:T(8,128)(2,1)S(1)}, bf16[16,3072]{1,0:T(8,128)(2,1)S(1)}, u32[]{:S(2)}, u32[]{:S(2)}) collective-permute-start(bf16[16,3072]{1,0:T(8,128)(2,1)S(1)} %get-tuple-element.78), channel_id=1, source_target_pairs={{0,12},{1,13},{2,14},{3,15},{4,0},{5,1},{6,2},{7,3},{8,4},{9,5},{1... | collective-permute-start | bytes 294920 | tf_op jit(solution)/shard_map/ppermute | solution.py:67
  154.4 12.3 %collective-permute-start.34 = (bf16[16,3072]{1,0:T(8,128)(2,1)S(1)}, bf16[16,3072]{1,0:T(8,128)(2,1)S(1)}, u32[]{:S(2)}, u32[]{:S(2)}) collective-permute-start(bf16[16,3072]{1,0:T(8,128)(2,1)S(1)} %get-tuple-element.79), channel_id=1, source_target_pairs={{0,8},{1,9},{2,10},{3,11},{4,12},{5,13},{6,14},{7,15},{8,0},{9,1},... | collective-permute-start | bytes 294920 | tf_op jit(solution)/shard_map/ppermute | solution.py:67
  154.4 12.3 %collective-permute-start.33 = (bf16[16,3072]{1,0:T(8,128)(2,1)S(1)}, bf16[16,3072]{1,0:T(8,128)(2,1)S(1)}, u32[]{:S(2)}, u32[]{:S(2)}) collective-permute-start(bf16[16,3072]{1,0:T(8,128)(2,1)S(1)} %get-tuple-element.77), channel_id=1, source_target_pairs={{0,4},{1,5},{2,6},{3,7},{4,8},{5,9},{6,10},{7,11},{8,12},{9,13},{1... | collective-permute-start | bytes 294920 | tf_op jit(solution)/shard_map/ppermute | solution.py:67

commit v14 on v13

--- a/solution.py
+++ b/solution.py
@@ -458,7 +458,7 @@
             pltpu.SemaphoreType.DMA((SLOTS,)),
         ],
         compiler_params=params(16),
-        cost_estimate=cost(2 * tokens * shard * adapters * wide, 4 * shard * adapters * wide),
+        cost_estimate=cost(tokens * shard * wide, shard * wide),
     )(columns, order, low, adapter)
 
 
@@ -709,7 +709,7 @@
                     columns, order, after(low_out, near), adapter[:, None], adapter_list
                 )
                 ahead = ahead + [grad_a]
-            far = lax.optimization_barrier((far, *ahead))[0]
+            near = lax.optimization_barrier((near, *ahead))[0]
         far = torus.move(far, 2, 1)
         sums.append(core_sum(near, far, side, side_far, at, first, b))
         inner_moves.append([torus.move(sums[q][k], 1, k) for k in range(1, b)])

time: 168 us -> 166 us (0.988)
  waiting for transfers between devices: 34.3 us -> 32.4 us
    ppermute x30, waiting for transfers between devices: 32.6 us -> 30.7 us  [move(): return lax.ppermute(x, 'tensor', pairs)]
  transfers between devices with their start and end apart: 36 -> 36, of which waited for: 18 -> 17; matrix products, arithmetic and copies ran while one was open for 4% -> 4% of each run, Pallas kernels for 43% -> 44%
where the time goes in v14:
time: 166 us
  Pallas kernels  86.9 us (52%)
  starting transfers between devices  37.2 us (22%)
  waiting for transfers between devices  32.4 us (20%)
  other arithmetic  5.25 us (3%)
  local copies, waits for them, and re-layouts  2.9 us (2%)
    pallas_call x6, Pallas kernels, forward_chunk(): pl.pallas_call(functools.partial(forward_kernel, len(pieces), low, count,...  31.4 us
    ppermute x30, waiting for transfers between devices, move(): return lax.ppermute(x, 'tensor', pairs)  30.7 us
    ppermute x30, starting transfers between devices, move(): return lax.ppermute(x, 'tensor', pairs)  29.5 us
    pallas_call x2, Pallas kernels, backward_chunk(): pl.pallas_call(functools.partial(backward_kernel, count, first), grid=(co...  23.1 us
    pallas_call x3, Pallas kernels, grad_b_of(): pl.pallas_call(functools.partial(grad_b_kernel, first, last - first), gri...  11.9 us
    pallas_call x1, Pallas kernels, middle(): pl.pallas_call(functools.partial(middle_kernel, rows), grid_spec=pltpu.Pr...  8.64 us
    ppermute x6, starting transfers between devices, exchange_sum(): x = x + lax.ppermute(x, 'tensor', pairs)  7.69 us
    pallas_call x1, Pallas kernels, grad_a_of(): pl.pallas_call(grad_a_kernel, grid=(adapters // per,), in_specs=[full(col...  4.67 us
  transfers between devices with their start and end apart: 36, of which 17 were waited for; matrix products, arithmetic and copies ran while one was open for 4% of the time, Pallas kernels for 44%

profile of v14, /device:TPU:0, one launch (start us, length us, event | category | flops | bytes accessed | tf_op | source)
XLA Modules:
  0.0 165.8 jit_solution(18418678121538314479)
XLA Ops:
  0.6 0.9 slice_bitcast_fusion
  1.5 3.1 %collective-permute-start.2 = (bf16[16,3072]{1,0:T(8,128)(2,1)S(1)}, bf16[16,3072]{1,0:T(8,128)(2,1)S(1)}, u32[]{:S(2)}, u32[]{:S(2)}) collective-permute-start(bf16[16,3072]{1,0:T(8,128)(2,1)S(1)} %get-tuple-element.81), channel_id=1, source_target_pairs={{0,4},{1,5},{2,6},{3,7},{4,8},{5,9},{6,10},{7,11},{8,12},{9,13},{1... | collective-permute-start | bytes 294920 | tf_op jit(solution)/shard_map/ppermute | solution.py:67
  4.6 2.6 %collective-permute-start.1 = (bf16[16,3072]{1,0:T(8,128)(2,1)S(1)}, bf16[16,3072]{1,0:T(8,128)(2,1)S(1)}, u32[]{:S(2)}, u32[]{:S(2)}) collective-permute-start(bf16[16,3072]{1,0:T(8,128)(2,1)S(1)} %get-tuple-element.81), channel_id=1, source_target_pairs={{0,8},{1,9},{2,10},{3,11},{4,12},{5,13},{6,14},{7,15},{8,0},{9,1},... | collective-permute-start | bytes 294920 | tf_op jit(solution)/shard_map/ppermute | solution.py:67
  7.2 1.3 collective-permute-start
  8.6 0.9 slice.60
  11.3 2.5 %collective-permute-done.1 = bf16[16,3072]{1,0:T(8,128)(2,1)S(1)} collective-permute-done((bf16[16,3072]{1,0:T(8,128)(2,1)S(1)}, bf16[16,3072]{1,0:T(8,128)(2,1)S(1)}, u32[]{:S(2)}, u32[]{:S(2)}) %collective-permute-start.1) | collective-permute-done | bytes 98336 | tf_op jit(solution)/shard_map/ppermute | solution.py:67
  13.9 2.6 %collective-permute-start.5 = (bf16[16,5120]{1,0:T(8,128)(2,1)S(1)}, bf16[16,5120]{1,0:T(8,128)(2,1)S(1)}, u32[]{:S(2)}, u32[]{:S(2)}) collective-permute-start(bf16[16,5120]{1,0:T(8,128)(2,1)S(1)} %slice.60), channel_id=1, source_target_pairs={{0,4},{1,5},{2,6},{3,7},{4,8},{5,9},{6,10},{7,11},{8,12},{9,13},{1... | collective-permute-start | bytes 491528 | tf_op jit(solution)/shard_map/ppermute | solution.py:67
  16.5 1.6 collective-permute-start.4
  20.0 1.5 collective-permute-start.8
  21.5 1.5 collective-permute-done.5
  23.0 5.9 %collective-permute-done.4 = bf16[16,5120]{1,0:T(8,128)(2,1)S(1)} collective-permute-done((bf16[16,5120]{1,0:T(8,128)(2,1)S(1)}, bf16[16,5120]{1,0:T(8,128)(2,1)S(1)}, u32[]{:S(2)}, u32[]{:S(2)}) %collective-permute-start.4) | collective-permute-done | bytes 163872 | tf_op jit(solution)/shard_map/ppermute | solution.py:67
  29.0 1.5 collective-permute-done.8.rest_1_.rest_9_
  30.5 1.6 collective-permute-start.7
  32.3 9.2 %shard_map.103.rest_5_ = f32[2,256,1792]{2,1,0:T(8,128)S(1)} custom-call(bf16[64,3072]{1,0:T(8,128)(2,1)S(1)} %bitcast.32, bf16[64,3072]{1,0:T(8,128)(2,1)S(1)} %collective-permute-done.8.rest_1_.rest_9_, bf16[64,3072]{1,0:T(8,128)(2,1)S(1)} %collective-permute-done.9.rest_2_.rest_10_, bf16[64,3072]{1,0:T(8,128)(2,1)S(1)} %collective-permute-done.10.rest_3_.rest_11_, ...), custom_call_target="tpu_custom_call" | custom-call | flops 5637144576 | bytes 22020096 | tf_op jit(solution)/shard_map/pallas_call | solution.py:181
  42.1 1.3 collective-permute-start.6
  43.5 8.4 %shard_map.104.rest_5_ = f32[2,256,1792]{2,1,0:T(8,128)S(1)} custom-call(bf16[64,2560]{1,0:T(8,128)(2,1)S(1)} %get-tuple-element.75.rest_0_.rest_12_, bf16[64,2560]{1,0:T(8,128)(2,1)S(1)} %collective-permute-done.7.rest_1_.rest_13_, bf16[64,2560]{1,0:T(8,128)(2,1)S(1)} %collective-permute-done.11.rest_2_.rest_14_, ...), custom_call_target="tpu_custom_call", output_to_operand_aliasing={{}: (5, {})} | custom-call | flops 4697620480 | bytes 18350080 | tf_op jit(solution)/shard_map/pallas_call | solution.py:181
  52.7 1.1 collective-permute-done.14.rest_3_.rest_19_
  53.7 1.5 shard_map.109
  55.7 0.9 collective-permute-done.15
  56.6 1.4 collective-permute-start.16
  58.0 2.7 %shard_map.105.rest_5_ = f32[2,256,1792]{2,1,0:T(8,128)S(1)} custom-call(bf16[64,2560]{1,0:T(8,128)(2,1)S(1)} %get-tuple-element.76.rest_0_.rest_16_, bf16[64,2560]{1,0:T(8,128)(2,1)S(1)} %collective-permute-done.6.rest_1_.rest_17_, bf16[64,2560]{1,0:T(8,128)(2,1)S(1)} %collective-permute-done.13.rest_2_.rest_18_, ...), custom_call_target="tpu_custom_call", output_to_operand_aliasing={{}: (5, {})} | custom-call | flops 671088640 | bytes 2621440 | tf_op jit(solution)/shard_map/pallas_call | solution.py:181
  61.1 2.6 %collective-permute-start.17 = (f32[128,128]{1,0:T(8,128)S(1)}, f32[128,128]{1,0:T(8,128)S(1)}, u32[]{:S(2)}, u32[]{:S(2)}) collective-permute-start(f32[128,128]{1,0:T(8,128)S(1)} %add.292), channel_id=1, source_target_pairs={{0,4},{1,5},{2,6},{3,7},{4,0},{5,1},{6,2},{7,3},{8,12},{9,13},{10,... | collective-permute-start | bytes 196616 | tf_op jit(solution)/shard_map/ppermute | solution.py:94
  63.7 3.7 %shard_map.106.rest_5_ = f32[2,256,1792]{2,1,0:T(8,128)S(1)} custom-call(bf16[64,2560]{1,0:T(8,128)(2,1)S(1)} %get-tuple-element.76.rest_0_.rest_16_, bf16[64,2560]{1,0:T(8,128)(2,1)S(1)} %collective-permute-done.6.rest_1_.rest_17_, bf16[64,2560]{1,0:T(8,128)(2,1)S(1)} %collective-permute-done.13.rest_2_.rest_18_, ...), custom_call_target="tpu_custom_call", output_to_operand_aliasing={{}: (5, {})} | custom-call | flops 1342177280 | bytes 5242880 | tf_op jit(solution)/shard_map/pallas_call | solution.py:181
  67.4 1.5 collective-permute-start.18
  68.9 3.7 %shard_map.107.rest_5_ = f32[2,256,1792]{2,1,0:T(8,128)S(1)} custom-call(bf16[64,2560]{1,0:T(8,128)(2,1)S(1)} %get-tuple-element.76.rest_0_.rest_16_, bf16[64,2560]{1,0:T(8,128)(2,1)S(1)} %collective-permute-done.6.rest_1_.rest_17_, bf16[64,2560]{1,0:T(8,128)(2,1)S(1)} %collective-permute-done.13.rest_2_.rest_18_, ...), custom_call_target="tpu_custom_call", output_to_operand_aliasing={{}: (5, {})} | custom-call | flops 1342177280 | bytes 5242880 | tf_op jit(solution)/shard_map/pallas_call | solution.py:181
  73.5 3.8 %shard_map.108.base = f32[2,256,1792]{2,1,0:T(8,128)S(1)} custom-call(bf16[64,2560]{1,0:T(8,128)(2,1)S(1)} %get-tuple-element.76.rest_0_.rest_16_, bf16[64,2560]{1,0:T(8,128)(2,1)S(1)} %collective-permute-done.6.rest_1_.rest_17_, bf16[64,2560]{1,0:T(8,128)(2,1)S(1)} %collective-permute-done.13.rest_2_.rest_18_, ...), custom_call_target="tpu_custom_call", output_to_operand_aliasing={{}: (5, {})} | custom-call | flops 1342177280 | bytes 5242880 | tf_op jit(solution)/shard_map/pallas_call | solution.py:181
  77.3 8.6 %shard_map.110 = (bf16[256,1792]{1,0:T(8,128)(2,1)S(1)}, bf16[256,1792]{1,0:T(8,128)(2,1)S(1)}, f32[256,128]{1,0:T(8,128)S(1)}) custom-call(s32[8]{0:T(128)S(1)} %bitcast.46, s32[16]{0:T(128)S(1)} %get-tuple-element.70.places, f32[2,256,1792]{2,1,0:T(8,128)S(1)} %shard_map.108.base, bf16[256,1792]{1,0:T(8,128)(2,1)S(1)} %copy-done.1, ...), custom_call_target="tpu_custom_call" | custom-call | flops 1879048192 | bytes 10092544 | tf_op jit(solution)/shard_map/pallas_call | solution.py:329
  87.4 1.3 collective-permute-start.21
  88.7 3.6 %shard_map.111.rest_0_ = f32[24,128,1792]{2,1,0:T(8,128)} custom-call(bf16[256,1792]{1,0:T(8,128)(2,1)S(1)} %get-tuple-element.57.dgate, bf16[256,1792]{1,0:T(8,128)(2,1)S(1)} %get-tuple-element.43.dup, bf16[256,256]{1,0:T(8,128)(2,1)S(1)} %fusion.1.order, bf16[256,128]{1,0:T(8,128)(2,1)S(1)} %bitcast.35, s32[1,256]{1,0:T(1,128)S(1)} %bitcast.40), custom_call_target="tpu_custom_call" | custom-call | flops 805306368 | bytes 6291456 | tf_op jit(solution)/shard_map/pallas_call | solution.py:404
  92.4 3.7 %shard_map.112.rest_0_ = f32[24,128,1792]{2,1,0:T(8,128)} custom-call(bf16[256,1792]{1,0:T(8,128)(2,1)S(1)} %get-tuple-element.57.dgate, bf16[256,1792]{1,0:T(8,128)(2,1)S(1)} %get-tuple-element.43.dup, bf16[256,256]{1,0:T(8,128)(2,1)S(1)} %fusion.1.order, bf16[256,128]{1,0:T(8,128)(2,1)S(1)} %bitcast.36, ...), custom_call_target="tpu_custom_call", output_to_operand_aliasing={{}: (5, {})} | custom-call | flops 805306368 | bytes 6291456 | tf_op jit(solution)/shard_map/pallas_call | solution.py:404
  97.5 13.9 %shard_map.113 = (bf16[128,5120]{1,0:T(8,128)(2,1)S(1)}, bf16[128,5120]{1,0:T(8,128)(2,1)S(1)}) custom-call(bf16[2,8192,1792]{2,1,0:T(8,128)(2,1)} %frozen.3, bf16[256,1792]{1,0:T(8,128)(2,1)S(1)} %get-tuple-element.57.dgate, bf16[256,1792]{1,0:T(8,128)(2,1)S(1)} %get-tuple-element.43.dup), custom_call_target="tpu_custom_call" | custom-call | flops 9395240960 | bytes 36700160 | tf_op jit(solution)/shard_map/pallas_call | solution.py:520
  111.7 1.1 collective-permute-done.24
  113.0 1.4 shard_map.114
  114.9 1.4 collective-permute-done.26.side_far
  116.3 3.1 %shard_map.115 = (bf16[64,5120]{1,0:T(8,128)(2,1)S(1)}, bf16[64,5120]{1,0:T(8,128)(2,1)}) custom-call(s32[2]{0:T(128)S(1)} %pad_add_fusion.at, bf16[128,5120]{1,0:T(8,128)(2,1)S(1)} %get-tuple-element.49.near, bf16[128,5120]{1,0:T(8,128)(2,1)S(1)} %collective-permute-done.25.far, f32[128,512]{1,0:T(8,128)S(1)} %get-tuple-element.53.side, ...), custom_call_target="tpu_custom_call" | custom-call | flops 1310720 | bytes 3932160 | tf_op jit(solution)/shard_map/pallas_call | solution.py:562
  120.3 9.2 %shard_map.116 = (bf16[128,3072]{1,0:T(8,128)(2,1)S(1)}, bf16[128,3072]{1,0:T(8,128)(2,1)S(1)}) custom-call(bf16[2,8192,1792]{2,1,0:T(8,128)(2,1)} %frozen.3, bf16[256,1792]{1,0:T(8,128)(2,1)S(1)} %get-tuple-element.57.dgate, bf16[256,1792]{1,0:T(8,128)(2,1)S(1)} %get-tuple-element.43.dup), custom_call_target="tpu_custom_call" | custom-call | flops 5637144576 | bytes 22020096 | tf_op jit(solution)/shard_map/pallas_call | solution.py:520
  129.6 4.7 %shard_map.117 = f32[24,512,128]{2,1,0:T(8,128)} custom-call(bf16[256,512]{1,0:T(8,128)(2,1)S(1)} %copy-done.3, bf16[256,256]{1,0:T(8,128)(2,1)S(1)} %fusion.1.order, bf16[256,128]{1,0:T(8,128)(2,1)S(1)} %bitcast.39, s32[256,1]{1,0:T(8,128)S(1)} %copy.25.adapter), custom_call_target="tpu_custom_call" | custom-call | flops 16777216 | bytes 65536 | tf_op jit(solution)/shard_map/pallas_call | solution.py:448
  134.3 2.1 %collective-permute-done.27 = bf16[64,5120]{1,0:T(8,128)(2,1)} collective-permute-done((bf16[64,5120]{1,0:T(8,128)(2,1)}, bf16[64,5120]{1,0:T(8,128)(2,1)}, u32[]{:S(2)}, u32[]{:S(2)}) %collective-permute-start.27) | collective-permute-done | bytes 655392 | tf_op jit(solution)/shard_map/ppermute | solution.py:67
  136.5 1.2 add_convert_fusion
  137.7 1.2 shard_map.118
  138.9 0.9 collective-permute-start.30
  139.8 3.1 %collective-permute-start.32 = (bf16[16,5120]{1,0:T(8,128)(2,1)S(1)}, bf16[16,5120]{1,0:T(8,128)(2,1)S(1)}, u32[]{:S(2)}, u32[]{:S(2)}) collective-permute-start(bf16[16,5120]{1,0:T(8,128)(2,1)S(1)} %get-tuple-element.73), channel_id=1, source_target_pairs={{0,12},{1,13},{2,14},{3,15},{4,0},{5,1},{6,2},{7,3},{8,4},{9,5},{1... | collective-permute-start | bytes 491528 | tf_op jit(solution)/shard_map/ppermute | solution.py:67
  142.9 1.2 collective-permute-start.28
  144.1 4.6 %shard_map.119 = f32[24,128,1792]{2,1,0:T(8,128)} custom-call(bf16[256,1792]{1,0:T(8,128)(2,1)S(1)} %get-tuple-element.57.dgate, bf16[256,1792]{1,0:T(8,128)(2,1)S(1)} %get-tuple-element.43.dup, bf16[256,256]{1,0:T(8,128)(2,1)S(1)} %fusion.1.order, bf16[256,128]{1,0:T(8,128)(2,1)S(1)} %bitcast.37, ...), custom_call_target="tpu_custom_call", output_to_operand_aliasing={{}: (5, {})} | custom-call | flops 1207959552 | bytes 9437184 | tf_op jit(solution)/shard_map/pallas_call | solution.py:404
  149.4 3.1 %collective-permute-start.35 = (bf16[16,3072]{1,0:T(8,128)(2,1)S(1)}, bf16[16,3072]{1,0:T(8,128)(2,1)S(1)}, u32[]{:S(2)}, u32[]{:S(2)}) collective-permute-start(bf16[16,3072]{1,0:T(8,128)(2,1)S(1)} %get-tuple-element.78), channel_id=1, source_target_pairs={{0,12},{1,13},{2,14},{3,15},{4,0},{5,1},{6,2},{7,3},{8,4},{9,5},{1... | collective-permute-start | bytes 294920 | tf_op jit(solution)/shard_map/ppermute | solution.py:67
  152.7 1.1 collective-permute-start.33
  153.7 8.1 %collective-permute-done.31 = bf16[16,5120]{1,0:T(8,128)(2,1)S(1)} collective-permute-done((bf16[16,5120]{1,0:T(8,128)(2,1)S(1)}, bf16[16,5120]{1,0:T(8,128)(2,1)S(1)}, u32[]{:S(2)}, u32[]{:S(2)}) %collective-permute-start.31) | collective-permute-done | bytes 163872 | tf_op jit(solution)/shard_map/ppermute | solution.py:67
  162.0 3.0 %collective-permute-done.34 = bf16[16,3072]{1,0:T(8,128)(2,1)S(1)} collective-permute-done((bf16[16,3072]{1,0:T(8,128)(2,1)S(1)}, bf16[16,3072]{1,0:T(8,128)(2,1)S(1)}, u32[]{:S(2)}, u32[]{:S(2)}) %collective-permute-start.34) | collective-permute-done | bytes 98336 | tf_op jit(solution)/shard_map/ppermute | solution.py:67
  (111 shorter events, 13.9 us)
Async XLA Ops:
  1.5 9.7 %collective-permute-start.2 = (bf16[16,3072]{1,0:T(8,128)(2,1)S(1)}, bf16[16,3072]{1,0:T(8,128)(2,1)S(1)}, u32[]{:S(2)}, u32[]{:S(2)}) collective-permute-start(bf16[16,3072]{1,0:T(8,128)(2,1)S(1)} %get-tuple-element.81), channel_id=1, source_target_pairs={{0,4},{1,5},{2,6},{3,7},{4,8},{5,9},{6,10},{7,11},{8,12},{9,13},{1... | collective-permute-start | bytes 294920 | tf_op jit(solution)/shard_map/ppermute | solution.py:67
  4.6 9.2 %collective-permute-start.1 = (bf16[16,3072]{1,0:T(8,128)(2,1)S(1)}, bf16[16,3072]{1,0:T(8,128)(2,1)S(1)}, u32[]{:S(2)}, u32[]{:S(2)}) collective-permute-start(bf16[16,3072]{1,0:T(8,128)(2,1)S(1)} %get-tuple-element.81), channel_id=1, source_target_pairs={{0,8},{1,9},{2,10},{3,11},{4,12},{5,13},{6,14},{7,15},{8,0},{9,1},... | collective-permute-start | bytes 294920 | tf_op jit(solution)/shard_map/ppermute | solution.py:67
  7.2 6.6 %collective-permute-start = (bf16[16,3072]{1,0:T(8,128)(2,1)S(1)}, bf16[16,3072]{1,0:T(8,128)(2,1)S(1)}, u32[]{:S(2)}, u32[]{:S(2)}) collective-permute-start(bf16[16,3072]{1,0:T(8,128)(2,1)S(1)} %get-tuple-element.81), channel_id=1, source_target_pairs={{0,12},{1,13},{2,14},{3,15},{4,0},{5,1},{6,2},{7,3},{8,4},{9,5},{1... | collective-permute-start | bytes 294920 | tf_op jit(solution)/shard_map/ppermute | solution.py:67
  13.9 9.1 %collective-permute-start.5 = (bf16[16,5120]{1,0:T(8,128)(2,1)S(1)}, bf16[16,5120]{1,0:T(8,128)(2,1)S(1)}, u32[]{:S(2)}, u32[]{:S(2)}) collective-permute-start(bf16[16,5120]{1,0:T(8,128)(2,1)S(1)} %slice.60), channel_id=1, source_target_pairs={{0,4},{1,5},{2,6},{3,7},{4,8},{5,9},{6,10},{7,11},{8,12},{9,13},{1... | collective-permute-start | bytes 491528 | tf_op jit(solution)/shard_map/ppermute | solution.py:67
  16.5 12.4 %collective-permute-start.4 = (bf16[16,5120]{1,0:T(8,128)(2,1)S(1)}, bf16[16,5120]{1,0:T(8,128)(2,1)S(1)}, u32[]{:S(2)}, u32[]{:S(2)}) collective-permute-start(bf16[16,5120]{1,0:T(8,128)(2,1)S(1)} %slice.60), channel_id=1, source_target_pairs={{0,8},{1,9},{2,10},{3,11},{4,12},{5,13},{6,14},{7,15},{8,0},{9,1},... | collective-permute-start | bytes 491528 | tf_op jit(solution)/shard_map/ppermute | solution.py:67
  18.1 10.8 %collective-permute-start.3 = (bf16[16,5120]{1,0:T(8,128)(2,1)S(1)}, bf16[16,5120]{1,0:T(8,128)(2,1)S(1)}, u32[]{:S(2)}, u32[]{:S(2)}) collective-permute-start(bf16[16,5120]{1,0:T(8,128)(2,1)S(1)} %slice.60), channel_id=1, source_target_pairs={{0,12},{1,13},{2,14},{3,15},{4,0},{5,1},{6,2},{7,3},{8,4},{9,5},{1... | collective-permute-start | bytes 491528 | tf_op jit(solution)/shard_map/ppermute | solution.py:67
  20.0 10.5 %collective-permute-start.8 = (bf16[64,3072]{1,0:T(8,128)(2,1)S(1)}, bf16[64,3072]{1,0:T(8,128)(2,1)S(1)}, u32[]{:S(2)}, u32[]{:S(2)}) collective-permute-start(bf16[64,3072]{1,0:T(8,128)(2,1)S(1)} %bitcast.30), channel_id=1, source_target_pairs={{0,2},{1,3},{2,0},{3,1},{4,6},{5,7},{6,4},{7,5},{8,10},{9,11},{10,... | collective-permute-start | bytes 1179656 | tf_op jit(solution)/shard_map/ppermute | solution.py:67
  21.5 10.8 %collective-permute-start.9 = (bf16[64,3072]{1,0:T(8,128)(2,1)S(1)}, bf16[64,3072]{1,0:T(8,128)(2,1)S(1)}, u32[]{:S(2)}, u32[]{:S(2)}) collective-permute-start(bf16[64,3072]{1,0:T(8,128)(2,1)S(1)} %bitcast.31), channel_id=1, source_target_pairs={{0,1},{1,0},{2,3},{3,2},{4,5},{5,4},{6,7},{7,6},{8,9},{9,8},{10,11... | collective-permute-start | bytes 1179656 | tf_op jit(solution)/shard_map/ppermute | solution.py:67
  30.4 1.9 %collective-permute-start.10 = (bf16[64,3072]{1,0:T(8,128)(2,1)S(1)}, bf16[64,3072]{1,0:T(8,128)(2,1)S(1)}, u32[]{:S(2)}, u32[]{:S(2)}) collective-permute-start(bf16[64,3072]{1,0:T(8,128)(2,1)S(1)} %collective-permute-done.8.rest_1_.rest_9_), channel_id=1, source_target_pairs={{0,1},{1,0},{2,3},{3,2},{4,5},{5,4},{6,7},{7,6},{8,9},{9,8},{10,11... | collective-permute-start | bytes 1179656 | tf_op jit(solution)/shard_map/ppermute | solution.py:67
  30.5 11.4 %copy-start.5 = (s32[24]{0:T(128)S(1)}, s32[24]{0:T(128)}, u32[]{:S(2)}) copy-start(s32[24]{0:T(128)} %param.15) | copy-start | bytes 292
  30.5 11.1 %collective-permute-start.7 = (bf16[64,2560]{1,0:T(8,128)(2,1)S(1)}, bf16[64,2560]{1,0:T(8,128)(2,1)S(1)}, u32[]{:S(2)}, u32[]{:S(2)}) collective-permute-start(bf16[64,2560]{1,0:T(8,128)(2,1)S(1)} %get-tuple-element.75.rest_0_.rest_12_), channel_id=1, source_target_pairs={{0,2},{1,3},{2,0},{3,1},{4,6},{5,7},{6,4},{7,5},{8,10},{9,11},{10,... | collective-permute-start | bytes 983048 | tf_op jit(solution)/shard_map/ppermute | solution.py:67
  32.1 11.4 %collective-permute-start.11 = (bf16[64,2560]{1,0:T(8,128)(2,1)S(1)}, bf16[64,2560]{1,0:T(8,128)(2,1)S(1)}, u32[]{:S(2)}, u32[]{:S(2)}) collective-permute-start(bf16[64,2560]{1,0:T(8,128)(2,1)S(1)} %get-tuple-element.75.rest_0_.rest_12_), channel_id=1, source_target_pairs={{0,1},{1,0},{2,3},{3,2},{4,5},{5,4},{6,7},{7,6},{8,9},{9,8},{10,11... | collective-permute-start | bytes 983048 | tf_op jit(solution)/shard_map/ppermute | solution.py:67
  41.6 1.9 %collective-permute-start.12 = (bf16[64,2560]{1,0:T(8,128)(2,1)S(1)}, bf16[64,2560]{1,0:T(8,128)(2,1)S(1)}, u32[]{:S(2)}, u32[]{:S(2)}) collective-permute-start(bf16[64,2560]{1,0:T(8,128)(2,1)S(1)} %collective-permute-done.7.rest_1_.rest_13_), channel_id=1, source_target_pairs={{0,1},{1,0},{2,3},{3,2},{4,5},{5,4},{6,7},{7,6},{8,9},{9,8},{10,11... | collective-permute-start | bytes 983048 | tf_op jit(solution)/shard_map/ppermute | solution.py:67
  42.1 11.6 %copy-start = (bf16[24,512,128]{2,1,0:T(8,128)(2,1)S(1)}, bf16[24,512,128]{2,1,0:T(8,128)(2,1)}, u32[]{:S(2)}) copy-start(bf16[24,512,128]{2,1,0:T(8,128)(2,1)} %rest_7_.3) | copy-start | bytes 9437188
  42.1 11.6 %copy-start.4 = (s32[1,8]{1,0:T(1,128)S(1)}, s32[1,8]{1,0:T(1,128)}, u32[]{:S(2)}) copy-start(s32[1,8]{1,0:T(1,128)} %param.13) | copy-start | bytes 100
  42.1 9.9 %collective-permute-start.6 = (bf16[64,2560]{1,0:T(8,128)(2,1)S(1)}, bf16[64,2560]{1,0:T(8,128)(2,1)S(1)}, u32[]{:S(2)}, u32[]{:S(2)}) collective-permute-start(bf16[64,2560]{1,0:T(8,128)(2,1)S(1)} %get-tuple-element.76.rest_0_.rest_16_), channel_id=1, source_target_pairs={{0,2},{1,3},{2,0},{3,1},{4,6},{5,7},{6,4},{7,5},{8,10},{9,11},{10,... | collective-permute-start | bytes 983048 | tf_op jit(solution)/shard_map/ppermute | solution.py:67
  43.4 9.2 %collective-permute-start.13 = (bf16[64,2560]{1,0:T(8,128)(2,1)S(1)}, bf16[64,2560]{1,0:T(8,128)(2,1)S(1)}, u32[]{:S(2)}, u32[]{:S(2)}) collective-permute-start(bf16[64,2560]{1,0:T(8,128)(2,1)S(1)} %get-tuple-element.76.rest_0_.rest_16_), channel_id=1, source_target_pairs={{0,1},{1,0},{2,3},{3,2},{4,5},{5,4},{6,7},{7,6},{8,9},{9,8},{10,11... | collective-permute-start | bytes 983048 | tf_op jit(solution)/shard_map/ppermute | solution.py:67
  52.0 1.7 %collective-permute-start.14 = (bf16[64,2560]{1,0:T(8,128)(2,1)S(1)}, bf16[64,2560]{1,0:T(8,128)(2,1)S(1)}, u32[]{:S(2)}, u32[]{:S(2)}) collective-permute-start(bf16[64,2560]{1,0:T(8,128)(2,1)S(1)} %collective-permute-done.6.rest_1_.rest_17_), channel_id=1, source_target_pairs={{0,1},{1,0},{2,3},{3,2},{4,5},{5,4},{6,7},{7,6},{8,9},{9,8},{10,11... | collective-permute-start | bytes 983048 | tf_op jit(solution)/shard_map/ppermute | solution.py:67
  55.2 5.4 %copy-start.2 = (bf16[256,512]{1,0:T(8,128)(2,1)}, bf16[256,512]{1,0:T(8,128)(2,1)S(1)}, u32[]{:S(2)}) copy-start(bf16[256,512]{1,0:T(8,128)(2,1)S(1)} %get-tuple-element.59.columns) | copy-start | bytes 786436
  55.3 1.3 collective-permute-start.15
  56.6 4.4 %collective-permute-start.16 = (f32[128,128]{1,0:T(8,128)S(1)}, f32[128,128]{1,0:T(8,128)S(1)}, u32[]{:S(2)}, u32[]{:S(2)}) collective-permute-start(f32[128,128]{1,0:T(8,128)S(1)} %slice_add_fusion.1), channel_id=1, source_target_pairs={{0,2},{1,3},{2,0},{3,1},{4,6},{5,7},{6,4},{7,5},{8,10},{9,11},{10,... | collective-permute-start | bytes 196616 | tf_op jit(solution)/shard_map/ppermute | solution.py:94
  61.1 6.3 %collective-permute-start.17 = (f32[128,128]{1,0:T(8,128)S(1)}, f32[128,128]{1,0:T(8,128)S(1)}, u32[]{:S(2)}, u32[]{:S(2)}) collective-permute-start(f32[128,128]{1,0:T(8,128)S(1)} %add.292), channel_id=1, source_target_pairs={{0,4},{1,5},{2,6},{3,7},{4,0},{5,1},{6,2},{7,3},{8,12},{9,13},{10,... | collective-permute-start | bytes 196616 | tf_op jit(solution)/shard_map/ppermute | solution.py:94
  67.4 5.9 %collective-permute-start.18 = (f32[128,128]{1,0:T(8,128)S(1)}, f32[128,128]{1,0:T(8,128)S(1)}, u32[]{:S(2)}, u32[]{:S(2)}) collective-permute-start(f32[128,128]{1,0:T(8,128)S(1)} %add.293), channel_id=1, source_target_pairs={{0,8},{1,9},{2,10},{3,11},{4,12},{5,13},{6,14},{7,15},{8,0},{9,1},... | collective-permute-start | bytes 196616 | tf_op jit(solution)/shard_map/ppermute | solution.py:94
  73.4 3.9 %copy-start.1 = (bf16[256,1792]{1,0:T(8,128)(2,1)S(1)}, bf16[256,1792]{1,0:T(8,128)(2,1)}, u32[]{:S(2)}) copy-start(bf16[256,1792]{1,0:T(8,128)(2,1)} %dhidden.1) | copy-start | bytes 2752516
  73.4 3.9 %collective-permute-start.19 = (bf16[128,128]{1,0:T(8,128)(2,1)S(1)}, bf16[128,128]{1,0:T(8,128)(2,1)S(1)}, u32[]{:S(2)}, u32[]{:S(2)}) collective-permute-start(bf16[128,128]{1,0:T(8,128)(2,1)S(1)} %fusion.2), channel_id=1, source_target_pairs={{0,1},{1,0},{2,3},{3,2},{4,5},{5,4},{6,7},{7,6},{8,9},{9,8},{10,11... | collective-permute-start | bytes 98312 | tf_op jit(solution)/shard_map/ppermute | solution.py:67
  86.0 1.4 collective-permute-start.20
  87.4 4.9 %collective-permute-start.21 = (f32[128,128]{1,0:T(8,128)S(1)}, f32[128,128]{1,0:T(8,128)S(1)}, u32[]{:S(2)}, u32[]{:S(2)}) collective-permute-start(f32[128,128]{1,0:T(8,128)S(1)} %slice_add_fusion), channel_id=1, source_target_pairs={{0,2},{1,3},{2,0},{3,1},{4,6},{5,7},{6,4},{7,5},{8,10},{9,11},{10,... | collective-permute-start | bytes 196616 | tf_op jit(solution)/shard_map/ppermute | solution.py:94
  92.3 4.3 %collective-permute-start.22 = (f32[128,128]{1,0:T(8,128)S(1)}, f32[128,128]{1,0:T(8,128)S(1)}, u32[]{:S(2)}, u32[]{:S(2)}) collective-permute-start(f32[128,128]{1,0:T(8,128)S(1)} %add.303), channel_id=1, source_target_pairs={{0,4},{1,5},{2,6},{3,7},{4,0},{5,1},{6,2},{7,3},{8,12},{9,13},{10,... | collective-permute-start | bytes 196616 | tf_op jit(solution)/shard_map/ppermute | solution.py:94
  96.7 14.7 %collective-permute-start.23 = (f32[128,128]{1,0:T(8,128)S(1)}, f32[128,128]{1,0:T(8,128)S(1)}, u32[]{:S(2)}, u32[]{:S(2)}) collective-permute-start(f32[128,128]{1,0:T(8,128)S(1)} %add.304), channel_id=1, source_target_pairs={{0,8},{1,9},{2,10},{3,11},{4,12},{5,13},{6,14},{7,15},{8,0},{9,1},... | collective-permute-start | bytes 196616 | tf_op jit(solution)/shard_map/ppermute | solution.py:94
  111.5 1.3 collective-permute-start.24
  112.8 3.5 %collective-permute-start.25 = (bf16[128,5120]{1,0:T(8,128)(2,1)S(1)}, bf16[128,5120]{1,0:T(8,128)(2,1)S(1)}, u32[]{:S(2)}, u32[]{:S(2)}) collective-permute-start(bf16[128,5120]{1,0:T(8,128)(2,1)S(1)} %get-tuple-element.52), channel_id=1, source_target_pairs={{0,1},{1,0},{2,3},{3,2},{4,5},{5,4},{6,7},{7,6},{8,9},{9,8},{10,11... | collective-permute-start | bytes 3932168 | tf_op jit(solution)/shard_map/ppermute | solution.py:67
  114.3 1.9 %collective-permute-start.26 = (f32[128,512]{1,0:T(8,128)S(1)}, f32[128,512]{1,0:T(8,128)S(1)}, u32[]{:S(2)}, u32[]{:S(2)}) collective-permute-start(f32[128,512]{1,0:T(8,128)S(1)} %get-tuple-element.54), channel_id=1, source_target_pairs={{0,1},{1,0},{2,3},{3,2},{4,5},{5,4},{6,7},{7,6},{8,9},{9,8},{10,11... | collective-permute-start | bytes 786440 | tf_op jit(solution)/shard_map/ppermute | solution.py:67
  119.4 17.1 %collective-permute-start.27 = (bf16[64,5120]{1,0:T(8,128)(2,1)}, bf16[64,5120]{1,0:T(8,128)(2,1)}, u32[]{:S(2)}, u32[]{:S(2)}) collective-permute-start(bf16[64,5120]{1,0:T(8,128)(2,1)} %get-tuple-element.56), channel_id=1, source_target_pairs={{0,2},{1,3},{2,0},{3,1},{4,6},{5,7},{6,4},{7,5},{8,10},{9,11},{10,... | collective-permute-start | bytes 1966088 | tf_op jit(solution)/shard_map/ppermute | solution.py:67
  120.3 9.3 %copy-start.3 = (bf16[256,512]{1,0:T(8,128)(2,1)S(1)}, bf16[256,512]{1,0:T(8,128)(2,1)}, u32[]{:S(2)}) copy-start(bf16[256,512]{1,0:T(8,128)(2,1)} %copy-done.2) | copy-start | bytes 786436
  129.6 8.1 %collective-permute-start.29 = (bf16[128,3072]{1,0:T(8,128)(2,1)S(1)}, bf16[128,3072]{1,0:T(8,128)(2,1)S(1)}, u32[]{:S(2)}, u32[]{:S(2)}) collective-permute-start(bf16[128,3072]{1,0:T(8,128)(2,1)S(1)} %get-tuple-element.62), channel_id=1, source_target_pairs={{0,1},{1,0},{2,3},{3,2},{4,5},{5,4},{6,7},{7,6},{8,9},{9,8},{10,11... | collective-permute-start | bytes 2359304 | tf_op jit(solution)/shard_map/ppermute | solution.py:67
  138.9 10.4 %collective-permute-start.30 = (bf16[64,3072]{1,0:T(8,128)(2,1)S(1)}, bf16[64,3072]{1,0:T(8,128)(2,1)S(1)}, u32[]{:S(2)}, u32[]{:S(2)}) collective-permute-start(bf16[64,3072]{1,0:T(8,128)(2,1)S(1)} %get-tuple-element.63), channel_id=1, source_target_pairs={{0,2},{1,3},{2,0},{3,1},{4,6},{5,7},{6,4},{7,5},{8,10},{9,11},{10,... | collective-permute-start | bytes 1179656 | tf_op jit(solution)/shard_map/ppermute | solution.py:67
  139.8 12.9 %collective-permute-start.32 = (bf16[16,5120]{1,0:T(8,128)(2,1)S(1)}, bf16[16,5120]{1,0:T(8,128)(2,1)S(1)}, u32[]{:S(2)}, u32[]{:S(2)}) collective-permute-start(bf16[16,5120]{1,0:T(8,128)(2,1)S(1)} %get-tuple-element.73), channel_id=1, source_target_pairs={{0,12},{1,13},{2,14},{3,15},{4,0},{5,1},{6,2},{7,3},{8,4},{9,5},{1... | collective-permute-start | bytes 491528 | tf_op jit(solution)/shard_map/ppermute | solution.py:67
  142.9 19.0 %collective-permute-start.31 = (bf16[16,5120]{1,0:T(8,128)(2,1)S(1)}, bf16[16,5120]{1,0:T(8,128)(2,1)S(1)}, u32[]{:S(2)}, u32[]{:S(2)}) collective-permute-start(bf16[16,5120]{1,0:T(8,128)(2,1)S(1)} %get-tuple-element.74), channel_id=1, source_target_pairs={{0,8},{1,9},{2,10},{3,11},{4,12},{5,13},{6,14},{7,15},{8,0},{9,1},... | collective-permute-start | bytes 491528 | tf_op jit(solution)/shard_map/ppermute | solution.py:67
  142.9 19.0 %collective-permute-start.28 = (bf16[16,5120]{1,0:T(8,128)(2,1)S(1)}, bf16[16,5120]{1,0:T(8,128)(2,1)S(1)}, u32[]{:S(2)}, u32[]{:S(2)}) collective-permute-start(bf16[16,5120]{1,0:T(8,128)(2,1)S(1)} %get-tuple-element.72), channel_id=1, source_target_pairs={{0,4},{1,5},{2,6},{3,7},{4,8},{5,9},{6,10},{7,11},{8,12},{9,13},{1... | collective-permute-start | bytes 491528 | tf_op jit(solution)/shard_map/ppermute | solution.py:67
  149.4 12.5 %collective-permute-start.35 = (bf16[16,3072]{1,0:T(8,128)(2,1)S(1)}, bf16[16,3072]{1,0:T(8,128)(2,1)S(1)}, u32[]{:S(2)}, u32[]{:S(2)}) collective-permute-start(bf16[16,3072]{1,0:T(8,128)(2,1)S(1)} %get-tuple-element.78), channel_id=1, source_target_pairs={{0,12},{1,13},{2,14},{3,15},{4,0},{5,1},{6,2},{7,3},{8,4},{9,5},{1... | collective-permute-start | bytes 294920 | tf_op jit(solution)/shard_map/ppermute | solution.py:67
  152.5 12.5 %collective-permute-start.34 = (bf16[16,3072]{1,0:T(8,128)(2,1)S(1)}, bf16[16,3072]{1,0:T(8,128)(2,1)S(1)}, u32[]{:S(2)}, u32[]{:S(2)}) collective-permute-start(bf16[16,3072]{1,0:T(8,128)(2,1)S(1)} %get-tuple-element.79), channel_id=1, source_target_pairs={{0,8},{1,9},{2,10},{3,11},{4,12},{5,13},{6,14},{7,15},{8,0},{9,1},... | collective-permute-start | bytes 294920 | tf_op jit(solution)/shard_map/ppermute | solution.py:67
  152.7 12.3 %collective-permute-start.33 = (bf16[16,3072]{1,0:T(8,128)(2,1)S(1)}, bf16[16,3072]{1,0:T(8,128)(2,1)S(1)}, u32[]{:S(2)}, u32[]{:S(2)}) collective-permute-start(bf16[16,3072]{1,0:T(8,128)(2,1)S(1)} %get-tuple-element.77), channel_id=1, source_target_pairs={{0,4},{1,5},{2,6},{3,7},{4,8},{5,9},{6,10},{7,11},{8,12},{9,13},{1... | collective-permute-start | bytes 294920 | tf_op jit(solution)/shard_map/ppermute | solution.py:67
